TPU v7x, 32 devices: a whole 2x2x4 slice. The times are simulated.
32 devices in a mesh: gx: 8 (over z, x), trait: 4 (over y, core).
Axes of the slice: x: 2, y: 2, z: 4, core: 2. Of those that a mesh axis runs over, the one named last changes fastest.
Arguments:
- initial: float32 [64, 128, 1024], P('gx', None, 'trait'), may hold values from 0.2 to 2
- section_one: float32 [64, 128, 1024], P('gx', None, 'trait'), may hold values from 0.2 to 2
- section_two: float32 [64, 128, 1024], P('gx', None, 'trait'), may hold values from 0.2 to 2
- kernels: bfloat16 [2, 1024, 1024], P(None, None, 'trait'), may hold values from -0.1875 to 0.1875
- growth: float32 [1024], P('trait'), may hold values from -3 to 3
- death_rate: float32 [1024], P('trait'), may hold values from 0.5 to 8
Outputs:
- new_one: float32 [64, 128, 1024], P('gx', None, 'trait')
- new_two: float32 [64, 128, 1024], P('gx', None, 'trait')
All inputs are finite; a program needn't handle non-finite values.
Results may differ from a plain program's by a relative error of at most 0.002.
Values may be sent and summed in bfloat16 or wider, within the bound.
No kernel may reach another device: no remote copies, remote signals or barrier semaphores. Data moves between devices by JAX's collectives and lax.ppermute only.
A program may use at most 64 MiB of HBM per device.

v0:
```python
import jax
import jax.numpy as jnp
from jax import lax
from jax.experimental import pallas as pl
from jax.experimental.pallas import tpu as pltpu
from jax.sharding import PartitionSpec as P

DIFFUSION = 0.25
STEP_SIZE = 0.5
FIRST = STEP_SIZE / 3.0
SECOND = 2.0 * STEP_SIZE / 3.0
F32 = jnp.float32
BF16 = jnp.bfloat16
VMEM_LIMIT = 20 * 1024 * 1024
SPEC = pl.BlockSpec(memory_space=pltpu.VMEM)
ANYWHERE = pl.BlockSpec(memory_space=pl.ANY)
FROM_HBM = pl.BlockSpec(memory_space=pltpu.HBM)


def chunks_of(xcount):
    last = max(1, 3 * xcount // 8)
    start = (xcount - last + 1) // 2
    middle = list(range(start, start + last))
    return [x for x in range(xcount) if x not in middle], middle


def after(value, *others):
    return lax.optimization_barrier((value, *others))[0]


def call(body, name, args, outs, scratch=(), specs=None, out_specs=None, gflop=0.0, alias=None):
    specs = specs or [SPEC] * len(args)
    space = {id(SPEC): pltpu.VMEM, id(FROM_HBM): pltpu.HBM}
    args = [
        pltpu.with_memory_space_constraint(a, space[id(s)]) if id(s) in space else a for a, s in zip(args, specs)
    ]
    return pl.pallas_call(
        body,
        out_shape=outs,
        in_specs=specs,
        out_specs=out_specs or [SPEC] * len(outs),
        scratch_shapes=list(scratch),
        compiler_params=pltpu.CompilerParams(vmem_limit_bytes=VMEM_LIMIT),
        cost_estimate=pl.CostEstimate(flops=int(gflop * 1e9), bytes_accessed=0, transcendentals=0),
        input_output_aliases=alias or {},
        name=name,
    )(*args)


def round_chunk(fields, cells, with_faces):
    xcount, ycount, owned = fields[0].shape
    count = len(fields)

    def body(*refs):
        field_refs = refs[:count]
        out = refs[count]
        held, sems = refs[-2:]
        copies = []
        for f in range(count):
            for i, x in enumerate(cells):
                copies.append(pltpu.make_async_copy(field_refs[f].at[x], held.at[f, i], sems.at[f, i]))
                copies[-1].start()
        for f in range(count):
            for i, x in enumerate(cells):
                copies[f * len(cells) + i].wait()
                value = held[f, i].astype(BF16)
                out[f, i * ycount:(i + 1) * ycount, :] = value
                if with_faces and x == 0:
                    refs[count + 1][f] = value
                if with_faces and x == xcount - 1:
                    refs[count + 2][f] = value

    outs = [pltpu.VMEM((count, len(cells) * ycount, owned), BF16)]
    if with_faces:
        outs += [pltpu.VMEM((count, ycount, owned), BF16)] * 2
    return call(
        body, "round_chunk", fields, outs,
        scratch=[pltpu.VMEM((count, len(cells), ycount, owned), F32), pltpu.SemaphoreType.DMA((count, len(cells)))],
        specs=[FROM_HBM] * count, gflop=0.0,
    )


def blocks_dot(blocks, kernels_ref, k, owners):
    depth = blocks[0].shape[-1]
    lhs = jnp.concatenate(blocks, axis=-1)
    rhs = jnp.concatenate(
        [kernels_ref[k, pl.ds(pl.multiple_of(o * depth, depth), depth), :] for o in owners], axis=0
    )
    return jnp.dot(lhs, rhs, preferred_element_type=F32)


def along_y(core):
    return DIFFUSION * (pltpu.roll(core, 1, 0) + pltpu.roll(core, core.shape[0] - 1, 0)) - 2.0 * core


def before_first(one, two, lo, hi, growth, chunks):
    xcount, ycount, owned = one.shape

    def body(one_ref, two_ref, lo_ref, hi_ref, g_ref, *outs):
        growth = g_ref[...]
        for cells, base_ref in zip(chunks, outs):
            for f, ref in enumerate((one_ref, two_ref)):
                for i, x in enumerate(cells):
                    core = ref[x]
                    before = ref[x - 1] if x > 0 else lo_ref[f].astype(F32)
                    behind = ref[x + 1] if x < xcount - 1 else hi_ref[f].astype(F32)
                    base_ref[f, i] = DIFFUSION * (before + behind) + along_y(core) + core * growth

    outs = [pltpu.VMEM((2, len(cells), ycount, owned), F32) for cells in chunks]
    return call(body, "before_first", [one, two, lo, hi, growth], outs)


def early_part(blocks, kernels):
    rows, owned = blocks[0].shape[0] * blocks[0].shape[1], blocks[0].shape[2]
    count = len(blocks)

    def body(*refs):
        block_refs, k_ref, part_ref = refs[:count], refs[count], refs[count + 1]
        me = lax.axis_index("trait")
        values = [r[...].reshape(rows, owned) for r in block_refs]
        for k in range(2):
            part_ref[k] = blocks_dot(values, k_ref, k, [me ^ j for j in range(count)])

    return call(body, "early_part", [*blocks, kernels], [pltpu.VMEM((2, rows, owned), F32)], gflop=20.0)[0]


def first_node(part, last, base, one, two, initial, kernels, death, cells, with_faces):
    xcount, ycount, owned = one.shape
    rows = len(cells) * ycount

    def body(part_ref, last_ref, base_ref, one_ref, two_ref, init_ref, k_ref, d_ref, *refs):
        new_ref, rounded_ref, rest_ref = refs[:3]
        sums = refs[-1]
        me = lax.axis_index("trait")
        for k in range(2):
            far_part = blocks_dot([last_ref[...].reshape(2 * rows, owned)], k_ref, k, [me ^ 3])
            sums[k] = (part_ref[k] + far_part).astype(BF16)
        death = d_ref[...]
        inv_one = 1.0 / (1.0 + FIRST * death)
        inv_two = 1.0 / (1.0 + SECOND * death)
        for i, x in enumerate(cells):
            cores = (one_ref[x], two_ref[x])
            e = []
            for f in range(2):
                at = pl.ds(f * rows + i * ycount, ycount)
                e.append(base_ref[f, i] - cores[f] * sums[0, at, :].astype(F32) + sums[1, at, :].astype(F32))
            full_one = e[0] - death * cores[0]
            full_two = e[1] - death * cores[1]
            new = (
                init_ref[x]
                + FIRST * death * cores[0]
                + STEP_SIZE * (5.0 / 12.0 * full_one - 1.0 / 12.0 * full_two)
            ) * inv_one
            new_ref[i] = new
            rounded = new.astype(BF16)
            rounded_ref[0, i * ycount:(i + 1) * ycount, :] = rounded
            if with_faces and x == 0:
                refs[3][0] = rounded
            if with_faces and x == xcount - 1:
                refs[4][0] = rounded
            rest_ref[i] = (
                new - SECOND * e[0] + SECOND * death * cores[1] + STEP_SIZE / 3.0 * (full_one + full_two)
            ) * inv_two

    outs = [
        pltpu.VMEM((len(cells), ycount, owned), F32),
        pltpu.VMEM((1, rows, owned), BF16),
        pltpu.VMEM((len(cells), ycount, owned), F32),
    ]
    if with_faces:
        outs += [pltpu.VMEM((1, ycount, owned), BF16)] * 2
    args = [part, last, base, one, two, initial, kernels, death]
    return call(
        body, "first_node", args, outs, scratch=[pltpu.VMEM((2, 2 * rows, owned), BF16)],
        gflop=0.0,
    )


def before_second(news, rests, growth, death, chunks):
    _, ycount, owned = news[0].shape
    xcount = sum(len(cells) for cells in chunks)
    count = len(chunks)
    place = {x: (c, i) for c, cells in enumerate(chunks) for i, x in enumerate(cells)}

    def body(*refs):
        new_refs, rest_refs = refs[:count], refs[count:2 * count]
        g_ref, d_ref, whole_ref = refs[2 * count:2 * count + 3]
        base_refs, sems = refs[2 * count + 3:-1], refs[-1]
        copies = [
            pltpu.make_async_copy(new_refs[c].at[i], whole_ref.at[x], sems.at[x]) for x, (c, i) in place.items()
        ]
        for copy in copies:
            copy.start()
        growth = g_ref[...]
        factor = SECOND / (1.0 + SECOND * d_ref[...])
        for x, (c, i) in place.items():
            core = new_refs[c][i]
            e = along_y(core) + core * growth
            for near in (x - 1, x + 1):
                if near in place:
                    e = e + DIFFUSION * new_refs[place[near][0]][place[near][1]]
            base_refs[c][i] = rest_refs[c][i] + factor * e
        for copy in copies:
            copy.wait()

    outs = [jax.ShapeDtypeStruct((xcount, ycount, owned), F32)]
    outs += [pltpu.VMEM((len(cells), ycount, owned), F32) for cells in chunks]
    return call(
        body, "before_second", [*news, *rests, growth, death], outs, scratch=[pltpu.SemaphoreType.DMA((xcount,))],
        out_specs=[ANYWHERE] + [SPEC] * count, gflop=20.0,
    )


def whole_sums(blocks, kernels):
    rows, owned = blocks[0].shape[1:]
    count = len(blocks)

    def body(*refs):
        block_refs, k_ref, sums_ref = refs[:count], refs[count], refs[count + 1]
        me = lax.axis_index("trait")
        values = [r[...].reshape(rows, owned) for r in block_refs]
        for k in range(2):
            sums_ref[k] = blocks_dot(values, k_ref, k, [me ^ j for j in range(count)]).astype(BF16)

    return call(body, "whole_sums", [*blocks, kernels], [pltpu.VMEM((2, rows, owned), BF16)])[0]


def finish(cells, ycount, sums, base_ref, new_ref, factor, faces, held, out_ref, sems):
    copies = []
    for i, x in enumerate(cells):
        at = pl.ds(i * ycount, ycount)
        e = sums[1, at, :].astype(F32) - new_ref[i] * sums[0, at, :].astype(F32)
        if x in faces:
            e = e + DIFFUSION * faces[x][0].astype(F32)
        held[i] = base_ref[i] + factor * e
        copies.append(pltpu.make_async_copy(held.at[i], out_ref.at[x], sems.at[i]))
        copies[-1].start()
    return copies


def second_first(sums, base, new, death, lo, hi, blocks, kernels, cells, xcount):
    _, ycount, owned = new.shape
    rows = blocks[0].shape[1]
    count = len(blocks)

    def body(sums_ref, base_ref, new_ref, d_ref, lo_ref, hi_ref, k_ref, *refs):
        block_refs = refs[:count]
        out_ref, part_ref, held, sems = refs[count:]
        factor = SECOND / (1.0 + SECOND * d_ref[...])
        faces = {0: lo_ref, xcount - 1: hi_ref}
        copies = finish(cells, ycount, sums_ref, base_ref, new_ref, factor, faces, held, out_ref, sems)
        me = lax.axis_index("trait")
        values = [r[...].reshape(rows, owned) for r in block_refs]
        for k in range(2):
            part_ref[k] = blocks_dot(values, k_ref, k, [me ^ j for j in range(count)])
        for copy in copies:
            copy.wait()

    return call(
        body, "second_first", [sums, base, new, death, lo, hi, kernels, *blocks],
        [jax.ShapeDtypeStruct((xcount, ycount, owned), F32), pltpu.VMEM((2, rows, owned), F32)],
        scratch=[pltpu.VMEM((len(cells), ycount, owned), F32), pltpu.SemaphoreType.DMA((len(cells),))],
        out_specs=[ANYWHERE, SPEC],
    )


def second_last(part, last, base, new, death, kernels, begun, cells, xcount):
    _, ycount, owned = new.shape
    rows = len(cells) * ycount

    def body(part_ref, last_ref, base_ref, new_ref, d_ref, k_ref, begun_ref, out_ref, sums, held, sems):
        me = lax.axis_index("trait")
        for k in range(2):
            sums[k] = (part_ref[k] + blocks_dot([last_ref[...].reshape(rows, owned)], k_ref, k, [me ^ 3])).astype(BF16)
        factor = SECOND / (1.0 + SECOND * d_ref[...])
        for copy in finish(cells, ycount, sums, base_ref, new_ref, factor, {}, held, out_ref, sems):
            copy.wait()

    return call(
        body, "second_last", [part, last, base, new, death, kernels, begun],
        [jax.ShapeDtypeStruct((xcount, ycount, owned), F32)],
        scratch=[
            pltpu.VMEM((2, rows, owned), BF16),
            pltpu.VMEM((len(cells), ycount, owned), F32),
            pltpu.SemaphoreType.DMA((len(cells),)),
        ],
        specs=[SPEC] * 6 + [FROM_HBM], out_specs=[ANYWHERE], alias={6: 0},
    )[0]


def local(initial, section_one, section_two, kernels, growth, death_rate):
    xcount, ycount, owned = section_one.shape
    traits = lax.axis_size("trait")
    gcount = lax.axis_size("gx")
    growth = growth.reshape(1, owned)
    death = death_rate.reshape(1, owned)
    chunks = chunks_of(xcount)

    def to_sibling(v):
        return lax.ppermute(v, "trait", [(i, i ^ 1) for i in range(traits)])

    def to_far(v):
        return lax.ppermute(v, "trait", [(i, i ^ 2) for i in range(traits)])

    def faces(head, tail):
        lo = lax.ppermute(tail, "gx", [(i, (i + 1) % gcount) for i in range(gcount)])
        hi = lax.ppermute(head, "gx", [((i + 1) % gcount, i) for i in range(gcount)])
        return lo, hi

    own_a, head, tail = round_chunk((section_one, section_two), chunks[0], True)
    far_a = to_far(own_a)
    own_b = round_chunk((after(section_one, own_a), section_two), chunks[1], False)[0]
    far_b = to_far(own_b)
    head, tail, kernels = lax.optimization_barrier((head, tail, kernels, own_b))[:3]
    lo, hi = faces(head, tail)
    base_a, base_b = before_first(section_one, section_two, lo, hi, growth, chunks)
    sib_a = to_sibling(after(own_a, own_b))
    sib_b = to_sibling(own_b)
    far_a = after(far_a, base_a)
    farsib_a = to_sibling(far_a)
    part_a = early_part([own_a, sib_a, far_a], kernels)
    new_a, rounded_a, rest_a, new_head, new_tail = first_node(
        part_a, farsib_a, base_a, section_one, section_two, initial, kernels, death, chunks[0], True
    )
    nfar_a = to_far(rounded_a)
    nsib_a = to_sibling(rounded_a)

    far_b = after(far_b, rounded_a)
    farsib_b = to_sibling(far_b)
    part_b = early_part([own_b, sib_b, far_b], kernels)
    new_b, rounded_b, rest_b = first_node(
        part_b, farsib_b, base_b, section_one, section_two, initial, kernels, death, chunks[1], False
    )
    nfar_b = to_far(rounded_b)
    nsib_b = to_sibling(rounded_b)
    new_lo, new_hi = faces(*lax.optimization_barrier((new_head, new_tail, rounded_b))[:2])
    nfar_a = after(nfar_a, rounded_b)
    nfarsib_a = to_sibling(nfar_a)
    new_one, nbase_a, nbase_b = before_second((new_a, new_b), (rest_a, rest_b), growth, death, chunks)
    sums_a = whole_sums([rounded_a, nsib_a, nfar_a, nfarsib_a], after(kernels, nbase_a))
    nfar_b = after(nfar_b, sums_a, new_lo, new_hi)
    nfarsib_b = to_sibling(nfar_b)
    begun, npart_b = second_first(
        sums_a, nbase_a, new_a, death, new_lo, new_hi, [rounded_b, nsib_b, nfar_b], kernels, chunks[0], xcount
    )
    new_two = second_last(npart_b, nfarsib_b, nbase_b, new_b, death, kernels, begun, chunks[1], xcount)
    return new_one, new_two


def solution(mesh):
    in_specs = (
        P("gx", None, "trait"),
        P("gx", None, "trait"),
        P("gx", None, "trait"),
        P(None, None, "trait"),
        P("trait"),
        P("trait"),
    )
    out_specs = (P("gx", None, "trait"), P("gx", None, "trait"))
    return jax.shard_map(local, mesh=mesh, in_specs=in_specs, out_specs=out_specs, check_vma=False)
```

profile of v0, /device:TPU:0, one launch (start us, length us, event | category | flops | bytes accessed | tf_op | source)
XLA Modules:
  0.0 43.5 jit_solution(17200246201131040127)
XLA Ops:
  0.6 1.5 %round_chunk.2 = (bf16[2,640,256]{2,1,0:T(8,128)(2,1)S(1)}, bf16[2,128,256]{2,1,0:T(8,128)(2,1)S(1)}, bf16[2,128,256]{2,1,0:T(8,128)(2,1)S(1)}) custom-call(f32[8,128,256]{2,1,0:T(8,128)} %one_ref.5, f32[8,128,256]{2,1,0:T(8,128)} %two_ref.5), custom_call_target="tpu_custom_call" | custom-call | tf_op jit(solution)/shard_map/round_chunk/pallas_call | solution.py:37
  2.1 0.0 copy-start
  2.1 0.0 copy-start.1
  2.1 0.0 copy-start.5
  2.1 3.0 %collective-permute-start.1 = (bf16[2,640,256]{2,1,0:T(8,128)(2,1)S(1)}, bf16[2,640,256]{2,1,0:T(8,128)(2,1)S(1)}, u32[]{:S(2)}, u32[]{:S(2)}) collective-permute-start(bf16[2,640,256]{2,1,0:T(8,128)(2,1)S(1)} %get-tuple-element.34.refs_0_), channel_id=1, source_target_pairs={{0,2},{1,3},{2,0},{3,1},{4,6},{5,7},{6,4},{7,5},{8,10},{9,11},{10,... | collective-permute-start | bytes 1966088 | tf_op jit(solution)/shard_map/ppermute | solution.py:303
  5.2 1.3 %round_chunk.3.refs_0_ = bf16[2,384,256]{2,1,0:T(8,128)(2,1)S(1)} custom-call(f32[8,128,256]{2,1,0:T(8,128)} %one_ref.5, f32[8,128,256]{2,1,0:T(8,128)} %two_ref.5), custom_call_target="tpu_custom_call" | custom-call | tf_op jit(solution)/shard_map/round_chunk/pallas_call | solution.py:37
  6.4 0.0 copy-start.2
  6.4 0.1 collective-permute-start
  6.5 1.5 %collective-permute-start.2 = (bf16[2,128,256]{2,1,0:T(8,128)(2,1)S(1)}, bf16[2,128,256]{2,1,0:T(8,128)(2,1)S(1)}, u32[]{:S(2)}, u32[]{:S(2)}) collective-permute-start(bf16[2,128,256]{2,1,0:T(8,128)(2,1)S(1)} %get-tuple-element.37), channel_id=1, source_target_pairs={{0,4},{4,8},{8,12},{12,16},{16,20},{20,24},{24,28},{28,0},{1,5},{5... | collective-permute-start | bytes 393224 | tf_op jit(solution)/shard_map/ppermute | solution.py:306
  8.1 3.2 %collective-permute-start.3 = (bf16[2,128,256]{2,1,0:T(8,128)(2,1)S(1)}, bf16[2,128,256]{2,1,0:T(8,128)(2,1)S(1)}, u32[]{:S(2)}, u32[]{:S(2)}) collective-permute-start(bf16[2,128,256]{2,1,0:T(8,128)(2,1)S(1)} %get-tuple-element.38), channel_id=1, source_target_pairs={{4,0},{8,4},{12,8},{16,12},{20,16},{24,20},{28,24},{0,28},{5,1},{9... | collective-permute-start | bytes 393224 | tf_op jit(solution)/shard_map/ppermute | solution.py:307
  11.3 0.4 collective-permute-start.6
  11.7 3.6 %collective-permute-done.2.lo_ref = bf16[2,128,256]{2,1,0:T(8,128)(2,1)S(1)} collective-permute-done((bf16[2,128,256]{2,1,0:T(8,128)(2,1)S(1)}, bf16[2,128,256]{2,1,0:T(8,128)(2,1)S(1)}, u32[]{:S(2)}, u32[]{:S(2)}) %collective-permute-start.2) | collective-permute-done | bytes 131104 | tf_op jit(solution)/shard_map/ppermute | solution.py:306
  15.3 0.0 collective-permute-start.5
  15.3 1.1 %collective-permute-done.3.hi_ref = bf16[2,128,256]{2,1,0:T(8,128)(2,1)S(1)} collective-permute-done((bf16[2,128,256]{2,1,0:T(8,128)(2,1)S(1)}, bf16[2,128,256]{2,1,0:T(8,128)(2,1)S(1)}, u32[]{:S(2)}, u32[]{:S(2)}) %collective-permute-start.3) | collective-permute-done | bytes 131104 | tf_op jit(solution)/shard_map/ppermute | solution.py:307
  16.4 0.0 copy-done.1
  16.5 0.9 %before_first.1 = (f32[2,5,128,256]{3,2,1,0:T(8,128)S(1)}, f32[2,3,128,256]{3,2,1,0:T(8,128)S(1)}) custom-call(f32[8,128,256]{2,1,0:T(8,128)S(1)} %copy-done, f32[8,128,256]{2,1,0:T(8,128)S(1)} %copy-done.1, bf16[2,128,256]{2,1,0:T(8,128)(2,1)S(1)} %collective-permute-done.2.lo_ref, bf16[2,128,256]{2,1,0:T(8,128)(2,1)S(1)} %collective-permute-done.3.hi_ref, ...), custom_call_target="tpu_custom_call" | custom-call | tf_op jit(solution)/shard_map/before_first/pallas_call | solution.py:37
  17.4 3.4 %collective-permute-done.1.refs_2_ = bf16[2,640,256]{2,1,0:T(8,128)(2,1)S(1)} collective-permute-done((bf16[2,640,256]{2,1,0:T(8,128)(2,1)S(1)}, bf16[2,640,256]{2,1,0:T(8,128)(2,1)S(1)}, u32[]{:S(2)}, u32[]{:S(2)}) %collective-permute-start.1) | collective-permute-done | bytes 655392 | tf_op jit(solution)/shard_map/ppermute | solution.py:303
  20.7 0.0 collective-permute-start.4
  20.7 0.0 collective-permute-done.refs_1_
  20.8 1.2 %early_part.2.part_ref = f32[2,1280,256]{2,1,0:T(8,128)S(1)} custom-call(bf16[2,640,256]{2,1,0:T(8,128)(2,1)S(1)} %get-tuple-element.34.refs_0_, bf16[2,640,256]{2,1,0:T(8,128)(2,1)S(1)} %collective-permute-done.refs_1_, bf16[2,640,256]{2,1,0:T(8,128)(2,1)S(1)} %collective-permute-done.1.refs_2_, bf16[2,1024,256]{2,1,0:T(8,128)(2,1)S(1)} %copy-done.2), custom_call_target="tpu_custom_call" | custom-call | flops 20000000000 | tf_op jit(solution)/shard_map/early_part/pallas_call | solution.py:37
  21.9 0.9 %collective-permute-done.4.last_ref = bf16[2,640,256]{2,1,0:T(8,128)(2,1)S(1)} collective-permute-done((bf16[2,640,256]{2,1,0:T(8,128)(2,1)S(1)}, bf16[2,640,256]{2,1,0:T(8,128)(2,1)S(1)}, u32[]{:S(2)}, u32[]{:S(2)}) %collective-permute-start.4) | collective-permute-done | bytes 655392 | tf_op jit(solution)/shard_map/ppermute | solution.py:300
  22.8 1.0 %first_node.2 = (f32[5,128,256]{2,1,0:T(8,128)S(1)}, bf16[1,640,256]{2,1,0:T(8,128)(2,1)S(1)}, f32[5,128,256]{2,1,0:T(8,128)S(1)}, bf16[1,128,256]{2,1,0:T(8,128)(2,1)S(1)}, bf16[1,128,256]{2,1,0:T(8,128)(2,1)S(1)}) custom-call(f32[2,1280,256]{2,1,0:T(8,128)S(1)} %early_part.2.part_ref, bf16[2,640,256]{2,1,0:T(8,128)(2,1)S(1)} %collective-permute-done.4.last_ref, ...), custom_call_target="tpu_custom_call" | custom-call | tf_op jit(solution)/shard_map/first_node/pallas_call | solution.py:37
  23.9 2.1 %collective-permute-start.9 = (bf16[1,640,256]{2,1,0:T(8,128)(2,1)S(1)}, bf16[1,640,256]{2,1,0:T(8,128)(2,1)S(1)}, u32[]{:S(2)}, u32[]{:S(2)}) collective-permute-start(bf16[1,640,256]{2,1,0:T(8,128)(2,1)S(1)} %get-tuple-element.43.refs_0_), channel_id=1, source_target_pairs={{0,2},{1,3},{2,0},{3,1},{4,6},{5,7},{6,4},{7,5},{8,10},{9,11},{10,... | collective-permute-start | bytes 983048 | tf_op jit(solution)/shard_map/ppermute | solution.py:303
  26.0 0.0 collective-permute-start.8
  26.0 3.2 %collective-permute-done.6.refs_2_ = bf16[2,384,256]{2,1,0:T(8,128)(2,1)S(1)} collective-permute-done((bf16[2,384,256]{2,1,0:T(8,128)(2,1)S(1)}, bf16[2,384,256]{2,1,0:T(8,128)(2,1)S(1)}, u32[]{:S(2)}, u32[]{:S(2)}) %collective-permute-start.6) | collective-permute-done | bytes 393248 | tf_op jit(solution)/shard_map/ppermute | solution.py:303
  29.2 0.0 collective-permute-start.7
  29.2 0.0 collective-permute-done.5.refs_1_
  29.2 0.8 %early_part.3.part_ref = f32[2,768,256]{2,1,0:T(8,128)S(1)} custom-call(bf16[2,384,256]{2,1,0:T(8,128)(2,1)S(1)} %round_chunk.3.refs_0_, bf16[2,384,256]{2,1,0:T(8,128)(2,1)S(1)} %collective-permute-done.5.refs_1_, bf16[2,384,256]{2,1,0:T(8,128)(2,1)S(1)} %collective-permute-done.6.refs_2_, bf16[2,1024,256]{2,1,0:T(8,128)(2,1)S(1)} %copy-done.2), custom_call_target="tpu_custom_call" | custom-call | flops 20000000000 | tf_op jit(solution)/shard_map/early_part/pallas_call | solution.py:37
  29.9 0.9 %collective-permute-done.7.last_ref = bf16[2,384,256]{2,1,0:T(8,128)(2,1)S(1)} collective-permute-done((bf16[2,384,256]{2,1,0:T(8,128)(2,1)S(1)}, bf16[2,384,256]{2,1,0:T(8,128)(2,1)S(1)}, u32[]{:S(2)}, u32[]{:S(2)}) %collective-permute-start.7) | collective-permute-done | bytes 393248 | tf_op jit(solution)/shard_map/ppermute | solution.py:300
  30.9 0.7 %first_node.3 = (f32[3,128,256]{2,1,0:T(8,128)S(1)}, bf16[1,384,256]{2,1,0:T(8,128)(2,1)S(1)}, f32[3,128,256]{2,1,0:T(8,128)S(1)}) custom-call(f32[2,768,256]{2,1,0:T(8,128)S(1)} %early_part.3.part_ref, bf16[2,384,256]{2,1,0:T(8,128)(2,1)S(1)} %collective-permute-done.7.last_ref, f32[2,3,128,256]{3,2,1,0:T(8,128)S(1)} %get-tuple-element.45.base_ref, ...), custom_call_target="tpu_custom_call" | custom-call | tf_op jit(solution)/shard_map/first_node/pallas_call | solution.py:37
  31.6 2.1 %collective-permute-start.14 = (bf16[1,384,256]{2,1,0:T(8,128)(2,1)S(1)}, bf16[1,384,256]{2,1,0:T(8,128)(2,1)S(1)}, u32[]{:S(2)}, u32[]{:S(2)}) collective-permute-start(bf16[1,384,256]{2,1,0:T(8,128)(2,1)S(1)} %get-tuple-element.50.refs_0_), channel_id=1, source_target_pairs={{0,2},{1,3},{2,0},{3,1},{4,6},{5,7},{6,4},{7,5},{8,10},{9,11},{10,... | collective-permute-start | bytes 589832 | tf_op jit(solution)/shard_map/ppermute | solution.py:303
  33.7 1.5 %collective-permute-start.11 = (bf16[1,128,256]{2,1,0:T(8,128)(2,1)S(1)}, bf16[1,128,256]{2,1,0:T(8,128)(2,1)S(1)}, u32[]{:S(2)}, u32[]{:S(2)}) collective-permute-start(bf16[1,128,256]{2,1,0:T(8,128)(2,1)S(1)} %get-tuple-element.56), channel_id=1, source_target_pairs={{0,4},{4,8},{8,12},{12,16},{16,20},{20,24},{24,28},{28,0},{1,5},{5... | collective-permute-start | bytes 196616 | tf_op jit(solution)/shard_map/ppermute | solution.py:306
  35.2 3.2 %collective-permute-start.12 = (bf16[1,128,256]{2,1,0:T(8,128)(2,1)S(1)}, bf16[1,128,256]{2,1,0:T(8,128)(2,1)S(1)}, u32[]{:S(2)}, u32[]{:S(2)}) collective-permute-start(bf16[1,128,256]{2,1,0:T(8,128)(2,1)S(1)} %get-tuple-element.57), channel_id=1, source_target_pairs={{4,0},{8,4},{12,8},{16,12},{20,16},{24,20},{28,24},{0,28},{5,1},{9... | collective-permute-start | bytes 196616 | tf_op jit(solution)/shard_map/ppermute | solution.py:307
  38.4 0.0 collective-permute-done.9.refs_2_
  38.4 0.0 collective-permute-start.10
  38.4 1.0 %before_second.1 = (f32[8,128,256]{2,1,0:T(8,128)}, f32[5,128,256]{2,1,0:T(8,128)S(1)}, f32[3,128,256]{2,1,0:T(8,128)S(1)}) custom-call(f32[5,128,256]{2,1,0:T(8,128)S(1)} %get-tuple-element.42.refs_0_.new_ref, f32[3,128,256]{2,1,0:T(8,128)S(1)} %get-tuple-element.46.refs_1_.new_ref, f32[5,128,256]{2,1,0:T(8,128)S(1)} %get-tuple-element.47.refs_2_, ...), custom_call_target="tpu_custom_call" | custom-call | flops 20000000000 | tf_op jit(solution)/shard_map/before_second/pallas_call | solution.py:37
  39.5 0.0 collective-permute-done.8.refs_1_
  39.5 0.6 %collective-permute-start.13 = (bf16[1,384,256]{2,1,0:T(8,128)(2,1)S(1)}, bf16[1,384,256]{2,1,0:T(8,128)(2,1)S(1)}, u32[]{:S(2)}, u32[]{:S(2)}) collective-permute-start(bf16[1,384,256]{2,1,0:T(8,128)(2,1)S(1)} %get-tuple-element.50.refs_0_), channel_id=1, source_target_pairs={{0,1},{1,0},{2,3},{3,2},{4,5},{5,4},{6,7},{7,6},{8,9},{9,8},{10,11... | collective-permute-start | bytes 589832 | tf_op jit(solution)/shard_map/ppermute | solution.py:300
  40.0 0.0 collective-permute-done.10.refs_3_
  40.0 0.8 %whole_sums.1.sums_ref = bf16[2,640,256]{2,1,0:T(8,128)(2,1)S(1)} custom-call(bf16[1,640,256]{2,1,0:T(8,128)(2,1)S(1)} %get-tuple-element.43.refs_0_, bf16[1,640,256]{2,1,0:T(8,128)(2,1)S(1)} %collective-permute-done.8.refs_1_, bf16[1,640,256]{2,1,0:T(8,128)(2,1)S(1)} %collective-permute-done.9.refs_2_, ...), custom_call_target="tpu_custom_call" | custom-call | tf_op jit(solution)/shard_map/whole_sums/pallas_call | solution.py:37
  40.9 0.0 collective-permute-done.11.lo_ref
  40.9 0.0 collective-permute-done.12.hi_ref
  40.9 0.0 collective-permute-done.14.refs_2_
  40.9 0.2 collective-permute-start.15
  41.1 0.0 collective-permute-done.13.refs_1_
  41.1 1.3 %second_first.1 = (f32[8,128,256]{2,1,0:T(8,128)}, f32[2,384,256]{2,1,0:T(8,128)S(1)}) custom-call(bf16[2,640,256]{2,1,0:T(8,128)(2,1)S(1)} %whole_sums.1.sums_ref, f32[5,128,256]{2,1,0:T(8,128)S(1)} %get-tuple-element.52.base_ref, f32[5,128,256]{2,1,0:T(8,128)S(1)} %get-tuple-element.42.refs_0_.new_ref, f32[1,256]{1,0:T(1,128)S(1)} %bitcast.5, ...), custom_call_target="tpu_custom_call" | custom-call | tf_op jit(solution)/shard_map/second_first/pallas_call | solution.py:37
  42.5 0.0 collective-permute-done.15.last_ref
  42.5 1.0 %second_last.1 = f32[8,128,256]{2,1,0:T(8,128)} custom-call(f32[2,384,256]{2,1,0:T(8,128)S(1)} %get-tuple-element.59.part_ref, bf16[1,384,256]{2,1,0:T(8,128)(2,1)S(1)} %collective-permute-done.15.last_ref, f32[3,128,256]{2,1,0:T(8,128)S(1)} %get-tuple-element.60.base_ref, ...), custom_call_target="tpu_custom_call", output_to_operand_aliasing={{}: (6, {})} | custom-call | tf_op jit(solution)/shard_map/second_last/pallas_call | solution.py:37
  (7 shorter events, 0.0 us)
Async XLA Ops:
  2.1 14.3 %copy-start = (f32[8,128,256]{2,1,0:T(8,128)S(1)}, f32[8,128,256]{2,1,0:T(8,128)}, u32[]{:S(2)}) copy-start(f32[8,128,256]{2,1,0:T(8,128)} %one_ref.5) | copy-start | bytes 3145732
  2.1 14.3 %copy-start.1 = (f32[8,128,256]{2,1,0:T(8,128)S(1)}, f32[8,128,256]{2,1,0:T(8,128)}, u32[]{:S(2)}) copy-start(f32[8,128,256]{2,1,0:T(8,128)} %two_ref.5) | copy-start | bytes 3145732
  2.1 14.3 %copy-start.5 = (f32[256]{0:T(256)S(1)}, f32[256]{0:T(256)}, u32[]{:S(2)}) copy-start(f32[256]{0:T(256)} %param.10) | copy-start | bytes 3076
  2.1 18.6 %collective-permute-start.1 = (bf16[2,640,256]{2,1,0:T(8,128)(2,1)S(1)}, bf16[2,640,256]{2,1,0:T(8,128)(2,1)S(1)}, u32[]{:S(2)}, u32[]{:S(2)}) collective-permute-start(bf16[2,640,256]{2,1,0:T(8,128)(2,1)S(1)} %get-tuple-element.34.refs_0_), channel_id=1, source_target_pairs={{0,2},{1,3},{2,0},{3,1},{4,6},{5,7},{6,4},{7,5},{8,10},{9,11},{10,... | collective-permute-start | bytes 1966088 | tf_op jit(solution)/shard_map/ppermute | solution.py:303
  6.4 14.3 %copy-start.2 = (bf16[2,1024,256]{2,1,0:T(8,128)(2,1)S(1)}, bf16[2,1024,256]{2,1,0:T(8,128)(2,1)}, u32[]{:S(2)}) copy-start(bf16[2,1024,256]{2,1,0:T(8,128)(2,1)} %k_ref.3) | copy-start | bytes 3145732
  6.4 14.3 %collective-permute-start = (bf16[2,640,256]{2,1,0:T(8,128)(2,1)S(1)}, bf16[2,640,256]{2,1,0:T(8,128)(2,1)S(1)}, u32[]{:S(2)}, u32[]{:S(2)}) collective-permute-start(bf16[2,640,256]{2,1,0:T(8,128)(2,1)S(1)} %get-tuple-element.34.refs_0_), channel_id=1, source_target_pairs={{0,1},{1,0},{2,3},{3,2},{4,5},{5,4},{6,7},{7,6},{8,9},{9,8},{10,11... | collective-permute-start | bytes 1966088 | tf_op jit(solution)/shard_map/ppermute | solution.py:300
  6.5 8.8 %collective-permute-start.2 = (bf16[2,128,256]{2,1,0:T(8,128)(2,1)S(1)}, bf16[2,128,256]{2,1,0:T(8,128)(2,1)S(1)}, u32[]{:S(2)}, u32[]{:S(2)}) collective-permute-start(bf16[2,128,256]{2,1,0:T(8,128)(2,1)S(1)} %get-tuple-element.37), channel_id=1, source_target_pairs={{0,4},{4,8},{8,12},{12,16},{16,20},{20,24},{24,28},{28,0},{1,5},{5... | collective-permute-start | bytes 393224 | tf_op jit(solution)/shard_map/ppermute | solution.py:306
  8.1 8.4 %collective-permute-start.3 = (bf16[2,128,256]{2,1,0:T(8,128)(2,1)S(1)}, bf16[2,128,256]{2,1,0:T(8,128)(2,1)S(1)}, u32[]{:S(2)}, u32[]{:S(2)}) collective-permute-start(bf16[2,128,256]{2,1,0:T(8,128)(2,1)S(1)} %get-tuple-element.38), channel_id=1, source_target_pairs={{4,0},{8,4},{12,8},{16,12},{20,16},{24,20},{28,24},{0,28},{5,1},{9... | collective-permute-start | bytes 393224 | tf_op jit(solution)/shard_map/ppermute | solution.py:307
  11.3 17.9 %collective-permute-start.6 = (bf16[2,384,256]{2,1,0:T(8,128)(2,1)S(1)}, bf16[2,384,256]{2,1,0:T(8,128)(2,1)S(1)}, u32[]{:S(2)}, u32[]{:S(2)}) collective-permute-start(bf16[2,384,256]{2,1,0:T(8,128)(2,1)S(1)} %round_chunk.3.refs_0_), channel_id=1, source_target_pairs={{0,2},{1,3},{2,0},{3,1},{4,6},{5,7},{6,4},{7,5},{8,10},{9,11},{10,... | collective-permute-start | bytes 1179656 | tf_op jit(solution)/shard_map/ppermute | solution.py:303
  15.3 13.8 %collective-permute-start.5 = (bf16[2,384,256]{2,1,0:T(8,128)(2,1)S(1)}, bf16[2,384,256]{2,1,0:T(8,128)(2,1)S(1)}, u32[]{:S(2)}, u32[]{:S(2)}) collective-permute-start(bf16[2,384,256]{2,1,0:T(8,128)(2,1)S(1)} %round_chunk.3.refs_0_), channel_id=1, source_target_pairs={{0,1},{1,0},{2,3},{3,2},{4,5},{5,4},{6,7},{7,6},{8,9},{9,8},{10,11... | collective-permute-start | bytes 1179656 | tf_op jit(solution)/shard_map/ppermute | solution.py:300
  20.7 2.1 %copy-start.3 = (f32[8,128,256]{2,1,0:T(8,128)S(1)}, f32[8,128,256]{2,1,0:T(8,128)}, u32[]{:S(2)}) copy-start(f32[8,128,256]{2,1,0:T(8,128)} %init_ref.3) | copy-start | bytes 3145732
  20.7 2.1 %copy-start.4 = (f32[256]{0:T(256)S(1)}, f32[256]{0:T(256)}, u32[]{:S(2)}) copy-start(f32[256]{0:T(256)} %param.11) | copy-start | bytes 3076
  20.7 2.1 %collective-permute-start.4 = (bf16[2,640,256]{2,1,0:T(8,128)(2,1)S(1)}, bf16[2,640,256]{2,1,0:T(8,128)(2,1)S(1)}, u32[]{:S(2)}, u32[]{:S(2)}) collective-permute-start(bf16[2,640,256]{2,1,0:T(8,128)(2,1)S(1)} %collective-permute-done.1.refs_2_), channel_id=1, source_target_pairs={{0,1},{1,0},{2,3},{3,2},{4,5},{5,4},{6,7},{7,6},{8,9},{9,8},{10,11... | collective-permute-start | bytes 1966088 | tf_op jit(solution)/shard_map/ppermute | solution.py:300
  23.9 14.6 %collective-permute-start.9 = (bf16[1,640,256]{2,1,0:T(8,128)(2,1)S(1)}, bf16[1,640,256]{2,1,0:T(8,128)(2,1)S(1)}, u32[]{:S(2)}, u32[]{:S(2)}) collective-permute-start(bf16[1,640,256]{2,1,0:T(8,128)(2,1)S(1)} %get-tuple-element.43.refs_0_), channel_id=1, source_target_pairs={{0,2},{1,3},{2,0},{3,1},{4,6},{5,7},{6,4},{7,5},{8,10},{9,11},{10,... | collective-permute-start | bytes 983048 | tf_op jit(solution)/shard_map/ppermute | solution.py:303
  26.0 13.5 %collective-permute-start.8 = (bf16[1,640,256]{2,1,0:T(8,128)(2,1)S(1)}, bf16[1,640,256]{2,1,0:T(8,128)(2,1)S(1)}, u32[]{:S(2)}, u32[]{:S(2)}) collective-permute-start(bf16[1,640,256]{2,1,0:T(8,128)(2,1)S(1)} %get-tuple-element.43.refs_0_), channel_id=1, source_target_pairs={{0,1},{1,0},{2,3},{3,2},{4,5},{5,4},{6,7},{7,6},{8,9},{9,8},{10,11... | collective-permute-start | bytes 983048 | tf_op jit(solution)/shard_map/ppermute | solution.py:300
  29.2 1.7 %collective-permute-start.7 = (bf16[2,384,256]{2,1,0:T(8,128)(2,1)S(1)}, bf16[2,384,256]{2,1,0:T(8,128)(2,1)S(1)}, u32[]{:S(2)}, u32[]{:S(2)}) collective-permute-start(bf16[2,384,256]{2,1,0:T(8,128)(2,1)S(1)} %collective-permute-done.6.refs_2_), channel_id=1, source_target_pairs={{0,1},{1,0},{2,3},{3,2},{4,5},{5,4},{6,7},{7,6},{8,9},{9,8},{10,11... | collective-permute-start | bytes 1179656 | tf_op jit(solution)/shard_map/ppermute | solution.py:300
  31.6 9.4 %collective-permute-start.14 = (bf16[1,384,256]{2,1,0:T(8,128)(2,1)S(1)}, bf16[1,384,256]{2,1,0:T(8,128)(2,1)S(1)}, u32[]{:S(2)}, u32[]{:S(2)}) collective-permute-start(bf16[1,384,256]{2,1,0:T(8,128)(2,1)S(1)} %get-tuple-element.50.refs_0_), channel_id=1, source_target_pairs={{0,2},{1,3},{2,0},{3,1},{4,6},{5,7},{6,4},{7,5},{8,10},{9,11},{10,... | collective-permute-start | bytes 589832 | tf_op jit(solution)/shard_map/ppermute | solution.py:303
  33.7 7.2 %collective-permute-start.11 = (bf16[1,128,256]{2,1,0:T(8,128)(2,1)S(1)}, bf16[1,128,256]{2,1,0:T(8,128)(2,1)S(1)}, u32[]{:S(2)}, u32[]{:S(2)}) collective-permute-start(bf16[1,128,256]{2,1,0:T(8,128)(2,1)S(1)} %get-tuple-element.56), channel_id=1, source_target_pairs={{0,4},{4,8},{8,12},{12,16},{16,20},{20,24},{24,28},{28,0},{1,5},{5... | collective-permute-start | bytes 196616 | tf_op jit(solution)/shard_map/ppermute | solution.py:306
  35.2 5.7 %collective-permute-start.12 = (bf16[1,128,256]{2,1,0:T(8,128)(2,1)S(1)}, bf16[1,128,256]{2,1,0:T(8,128)(2,1)S(1)}, u32[]{:S(2)}, u32[]{:S(2)}) collective-permute-start(bf16[1,128,256]{2,1,0:T(8,128)(2,1)S(1)} %get-tuple-element.57), channel_id=1, source_target_pairs={{4,0},{8,4},{12,8},{16,12},{20,16},{24,20},{28,24},{0,28},{5,1},{9... | collective-permute-start | bytes 196616 | tf_op jit(solution)/shard_map/ppermute | solution.py:307
  38.4 1.6 %collective-permute-start.10 = (bf16[1,640,256]{2,1,0:T(8,128)(2,1)S(1)}, bf16[1,640,256]{2,1,0:T(8,128)(2,1)S(1)}, u32[]{:S(2)}, u32[]{:S(2)}) collective-permute-start(bf16[1,640,256]{2,1,0:T(8,128)(2,1)S(1)} %collective-permute-done.9.refs_2_), channel_id=1, source_target_pairs={{0,1},{1,0},{2,3},{3,2},{4,5},{5,4},{6,7},{7,6},{8,9},{9,8},{10,11... | collective-permute-start | bytes 983048 | tf_op jit(solution)/shard_map/ppermute | solution.py:300
  39.5 1.7 %collective-permute-start.13 = (bf16[1,384,256]{2,1,0:T(8,128)(2,1)S(1)}, bf16[1,384,256]{2,1,0:T(8,128)(2,1)S(1)}, u32[]{:S(2)}, u32[]{:S(2)}) collective-permute-start(bf16[1,384,256]{2,1,0:T(8,128)(2,1)S(1)} %get-tuple-element.50.refs_0_), channel_id=1, source_target_pairs={{0,1},{1,0},{2,3},{3,2},{4,5},{5,4},{6,7},{7,6},{8,9},{9,8},{10,11... | collective-permute-start | bytes 589832 | tf_op jit(solution)/shard_map/ppermute | solution.py:300
  40.9 1.5 %collective-permute-start.15 = (bf16[1,384,256]{2,1,0:T(8,128)(2,1)S(1)}, bf16[1,384,256]{2,1,0:T(8,128)(2,1)S(1)}, u32[]{:S(2)}, u32[]{:S(2)}) collective-permute-start(bf16[1,384,256]{2,1,0:T(8,128)(2,1)S(1)} %collective-permute-done.14.refs_2_), channel_id=1, source_target_pairs={{0,1},{1,0},{2,3},{3,2},{4,5},{5,4},{6,7},{7,6},{8,9},{9,8},{10,11... | collective-permute-start | bytes 589832 | tf_op jit(solution)/shard_map/ppermute | solution.py:300
where the time goes:
time: 43.6 us; the launch traced here: 43.5 us
  starting transfers between devices  18.1 us (42%)
  waiting for transfers between devices  13.1 us (30%)
  Pallas kernels  11.5 us (26%)
  between operations  0.81 us (2%)
    pallas_call x11, Pallas kernels, call(): pl.pallas_call(body, out_shape=outs, in_specs=specs, out_specs=out_specs...  11.5 us
    ppermute x4, starting transfers between devices, to_far(): return lax.ppermute(v, 'trait', [(i, i ^ 2) for i in range(traits)])  7.71 us
    ppermute x4, waiting for transfers between devices, to_far(): return lax.ppermute(v, 'trait', [(i, i ^ 2) for i in range(traits)])  6.52 us
    ppermute x2, starting transfers between devices, faces(): lax.ppermute(head, 'gx', [((i + 1) % gcount, i) for i in range(gcount)])  6.47 us
    ppermute x2, waiting for transfers between devices, faces(): lax.ppermute(tail, 'gx', [(i, (i + 1) % gcount) for i in range(gcount)])  3.58 us
    ppermute x2, starting transfers between devices, faces(): lax.ppermute(tail, 'gx', [(i, (i + 1) % gcount) for i in range(gcount)])  3.03 us
    ppermute x8, waiting for transfers between devices, to_sibling(): return lax.ppermute(v, 'trait', [(i, i ^ 1) for i in range(traits)])  1.84 us
    ppermute x2, waiting for transfers between devices, faces(): lax.ppermute(head, 'gx', [((i + 1) % gcount, i) for i in range(gcount)])  1.13 us
  transfers between devices with their start and end apart: 16, of which 6 were waited for; matrix products, arithmetic and copies ran while one was open for 0% of the time, Pallas kernels for 21%

commit v1 on v0

--- a/solution.py
+++ b/solution.py
@@ -18,7 +18,7 @@
 
 
 def chunks_of(xcount):
-    last = max(1, 3 * xcount // 8)
+    last = max(1, xcount // 4)
     start = (xcount - last + 1) // 2
     middle = list(range(start, start + last))
     return [x for x in range(xcount) if x not in middle], middle
@@ -47,6 +47,10 @@
     )(*args)
 
 
+def side_of(low_value, high_value):
+    return jnp.where(lax.axis_index("gx") % 2 == 0, low_value, high_value)
+
+
 def round_chunk(fields, cells, with_faces):
     xcount, ycount, owned = fields[0].shape
     count = len(fields)
@@ -56,6 +60,7 @@
         out = refs[count]
         held, sems = refs[-2:]
         copies = []
+        ends = {}
         for f in range(count):
             for i, x in enumerate(cells):
                 copies.append(pltpu.make_async_copy(field_refs[f].at[x], held.at[f, i], sems.at[f, i]))
@@ -65,10 +70,11 @@
                 copies[f * len(cells) + i].wait()
                 value = held[f, i].astype(BF16)
                 out[f, i * ycount:(i + 1) * ycount, :] = value
-                if with_faces and x == 0:
-                    refs[count + 1][f] = value
-                if with_faces and x == xcount - 1:
-                    refs[count + 2][f] = value
+                ends[x, f] = value
+        if with_faces:
+            for f in range(count):
+                refs[count + 1][f] = side_of(ends[xcount - 1, f], ends[0, f])
+                refs[count + 2][f] = side_of(ends[0, f], ends[xcount - 1, f])
 
     outs = [pltpu.VMEM((count, len(cells) * ycount, owned), BF16)]
     if with_faces:
@@ -93,35 +99,53 @@
     return DIFFUSION * (pltpu.roll(core, 1, 0) + pltpu.roll(core, core.shape[0] - 1, 0)) - 2.0 * core
 
 
-def before_first(one, two, lo, hi, growth, chunks):
+def before_first(one, two, near, beyond, growth, chunks):
     xcount, ycount, owned = one.shape
 
-    def body(one_ref, two_ref, lo_ref, hi_ref, g_ref, *outs):
+    def body(one_ref, two_ref, near_ref, beyond_ref, g_ref, *outs):
         growth = g_ref[...]
         for cells, base_ref in zip(chunks, outs):
             for f, ref in enumerate((one_ref, two_ref)):
                 for i, x in enumerate(cells):
                     core = ref[x]
-                    before = ref[x - 1] if x > 0 else lo_ref[f].astype(F32)
-                    behind = ref[x + 1] if x < xcount - 1 else hi_ref[f].astype(F32)
+                    before = ref[x - 1] if x > 0 else side_of(beyond_ref[f], near_ref[f]).astype(F32)
+                    behind = ref[x + 1] if x < xcount - 1 else side_of(near_ref[f], beyond_ref[f]).astype(F32)
                     base_ref[f, i] = DIFFUSION * (before + behind) + along_y(core) + core * growth
 
     outs = [pltpu.VMEM((2, len(cells), ycount, owned), F32) for cells in chunks]
-    return call(body, "before_first", [one, two, lo, hi, growth], outs)
-
-
-def early_part(blocks, kernels):
+    return call(body, "before_first", [one, two, near, beyond, growth], outs)
+
+
+def early_part(blocks, kernels, new=None, cells=(), xcount=0):
     rows, owned = blocks[0].shape[0] * blocks[0].shape[1], blocks[0].shape[2]
     count = len(blocks)
 
     def body(*refs):
-        block_refs, k_ref, part_ref = refs[:count], refs[count], refs[count + 1]
+        block_refs, k_ref = refs[:count], refs[count]
+        copies = []
+        if new is None:
+            part_ref = refs[-1]
+        else:
+            new_ref, part_ref, whole_ref, sems = refs[count + 1:]
+            copies = [pltpu.make_async_copy(new_ref.at[i], whole_ref.at[x], sems.at[i]) for i, x in enumerate(cells)]
+        for copy in copies:
+            copy.start()
         me = lax.axis_index("trait")
         values = [r[...].reshape(rows, owned) for r in block_refs]
         for k in range(2):
             part_ref[k] = blocks_dot(values, k_ref, k, [me ^ j for j in range(count)])
-
-    return call(body, "early_part", [*blocks, kernels], [pltpu.VMEM((2, rows, owned), F32)], gflop=20.0)[0]
+        for copy in copies:
+            copy.wait()
+
+    args = [*blocks, kernels]
+    outs = [pltpu.VMEM((2, rows, owned), F32)]
+    if new is None:
+        return call(body, "early_part", args, outs, gflop=20.0)[0]
+    outs.append(jax.ShapeDtypeStruct((xcount, *new.shape[1:]), F32))
+    return call(
+        body, "early_part", [*args, new], outs, scratch=[pltpu.SemaphoreType.DMA((len(cells),))],
+        out_specs=[SPEC, ANYWHERE], gflop=20.0,
+    )
 
 
 def first_node(part, last, base, one, two, initial, kernels, death, cells, with_faces):
@@ -138,6 +162,7 @@
         death = d_ref[...]
         inv_one = 1.0 / (1.0 + FIRST * death)
         inv_two = 1.0 / (1.0 + SECOND * death)
+        ends = {}
         for i, x in enumerate(cells):
             cores = (one_ref[x], two_ref[x])
             e = []
@@ -154,13 +179,13 @@
             new_ref[i] = new
             rounded = new.astype(BF16)
             rounded_ref[0, i * ycount:(i + 1) * ycount, :] = rounded
-            if with_faces and x == 0:
-                refs[3][0] = rounded
-            if with_faces and x == xcount - 1:
-                refs[4][0] = rounded
+            ends[x] = rounded
             rest_ref[i] = (
                 new - SECOND * e[0] + SECOND * death * cores[1] + STEP_SIZE / 3.0 * (full_one + full_two)
             ) * inv_two
+        if with_faces:
+            refs[3][0] = side_of(ends[xcount - 1], ends[0])
+            refs[4][0] = side_of(ends[0], ends[xcount - 1])
 
     outs = [
         pltpu.VMEM((len(cells), ycount, owned), F32),
@@ -176,7 +201,7 @@
     )
 
 
-def before_second(news, rests, growth, death, chunks):
+def before_second(news, rests, growth, death, begun, chunks):
     _, ycount, owned = news[0].shape
     xcount = sum(len(cells) for cells in chunks)
     count = len(chunks)
@@ -184,10 +209,10 @@
 
     def body(*refs):
         new_refs, rest_refs = refs[:count], refs[count:2 * count]
-        g_ref, d_ref, whole_ref = refs[2 * count:2 * count + 3]
-        base_refs, sems = refs[2 * count + 3:-1], refs[-1]
+        g_ref, d_ref, _, whole_ref = refs[2 * count:2 * count + 4]
+        base_refs, sems = refs[2 * count + 4:-1], refs[-1]
         copies = [
-            pltpu.make_async_copy(new_refs[c].at[i], whole_ref.at[x], sems.at[x]) for x, (c, i) in place.items()
+            pltpu.make_async_copy(new_refs[-1].at[i], whole_ref.at[x], sems.at[i]) for i, x in enumerate(chunks[-1])
         ]
         for copy in copies:
             copy.start()
@@ -205,50 +230,85 @@
 
     outs = [jax.ShapeDtypeStruct((xcount, ycount, owned), F32)]
     outs += [pltpu.VMEM((len(cells), ycount, owned), F32) for cells in chunks]
-    return call(
-        body, "before_second", [*news, *rests, growth, death], outs, scratch=[pltpu.SemaphoreType.DMA((xcount,))],
-        out_specs=[ANYWHERE] + [SPEC] * count, gflop=20.0,
-    )
-
-
-def whole_sums(blocks, kernels):
-    rows, owned = blocks[0].shape[1:]
+    args = [*news, *rests, growth, death, begun]
+    return call(
+        body, "before_second", args, outs, scratch=[pltpu.SemaphoreType.DMA((len(chunks[-1]),))],
+        specs=[SPEC] * (len(args) - 1) + [FROM_HBM], out_specs=[ANYWHERE] + [SPEC] * count, gflop=20.0,
+        alias={len(args) - 1: 0},
+    )
+
+
+def finish(cells, sums_at, base_ref, new_ref, factor, faces, held, out_ref, sems):
+    copies = []
+    for j, (i, x) in enumerate(cells):
+        e = sums_at(1, j) - new_ref[i] * sums_at(0, j)
+        if x in faces:
+            e = e + DIFFUSION * faces[x].astype(F32)
+        held[j] = base_ref[i] + factor * e
+        copies.append(pltpu.make_async_copy(held.at[j], out_ref.at[x], sems.at[j]))
+        copies[-1].start()
+    return copies
+
+
+def split_cells(cells, xcount):
+    placed = list(enumerate(cells))
+    return [p for p in placed if p[1] in (0, xcount - 1)], [p for p in placed if p[1] not in (0, xcount - 1)]
+
+
+def second_inner(blocks, base, new, death, kernels, cells, xcount):
+    _, ycount, owned = new.shape
+    rows = blocks[0].shape[1]
     count = len(blocks)
+    outer, inner = split_cells(cells, xcount)
 
     def body(*refs):
-        block_refs, k_ref, sums_ref = refs[:count], refs[count], refs[count + 1]
+        block_refs = refs[:count]
+        base_ref, new_ref, d_ref, k_ref, out_ref, sums_ref, sums, held, sems = refs[count:]
         me = lax.axis_index("trait")
         values = [r[...].reshape(rows, owned) for r in block_refs]
         for k in range(2):
-            sums_ref[k] = blocks_dot(values, k_ref, k, [me ^ j for j in range(count)]).astype(BF16)
-
-    return call(body, "whole_sums", [*blocks, kernels], [pltpu.VMEM((2, rows, owned), BF16)])[0]
-
-
-def finish(cells, ycount, sums, base_ref, new_ref, factor, faces, held, out_ref, sems):
-    copies = []
-    for i, x in enumerate(cells):
-        at = pl.ds(i * ycount, ycount)
-        e = sums[1, at, :].astype(F32) - new_ref[i] * sums[0, at, :].astype(F32)
-        if x in faces:
-            e = e + DIFFUSION * faces[x][0].astype(F32)
-        held[i] = base_ref[i] + factor * e
-        copies.append(pltpu.make_async_copy(held.at[i], out_ref.at[x], sems.at[i]))
-        copies[-1].start()
-    return copies
-
-
-def second_first(sums, base, new, death, lo, hi, blocks, kernels, cells, xcount):
+            sums[k] = blocks_dot(values, k_ref, k, [me ^ j for j in range(count)]).astype(BF16)
+        factor = SECOND / (1.0 + SECOND * d_ref[...])
+
+        def sums_at(k, j):
+            return sums[k, pl.ds(inner[j][0] * ycount, ycount), :].astype(F32)
+
+        copies = finish(inner, sums_at, base_ref, new_ref, factor, {}, held, out_ref, sems)
+        for j, (i, _) in enumerate(outer):
+            for k in range(2):
+                sums_ref[k, j] = sums[k, pl.ds(i * ycount, ycount), :]
+        for copy in copies:
+            copy.wait()
+
+    return call(
+        body, "second_inner", [*blocks, base, new, death, kernels],
+        [jax.ShapeDtypeStruct((xcount, ycount, owned), F32), pltpu.VMEM((2, len(outer), ycount, owned), BF16)],
+        scratch=[
+            pltpu.VMEM((2, rows, owned), BF16),
+            pltpu.VMEM((len(inner), ycount, owned), F32),
+            pltpu.SemaphoreType.DMA((len(inner),)),
+        ],
+        out_specs=[ANYWHERE, SPEC],
+    )
+
+
+def second_outer(sums, base, new, death, near, beyond, kernels, blocks, begun, cells, xcount):
     _, ycount, owned = new.shape
     rows = blocks[0].shape[1]
     count = len(blocks)
-
-    def body(sums_ref, base_ref, new_ref, d_ref, lo_ref, hi_ref, k_ref, *refs):
+    outer, _ = split_cells(cells, xcount)
+
+    def body(sums_ref, base_ref, new_ref, d_ref, near_ref, beyond_ref, k_ref, *refs):
         block_refs = refs[:count]
-        out_ref, part_ref, held, sems = refs[count:]
+        _, out_ref, part_ref, held, sems = refs[count:]
         factor = SECOND / (1.0 + SECOND * d_ref[...])
-        faces = {0: lo_ref, xcount - 1: hi_ref}
-        copies = finish(cells, ycount, sums_ref, base_ref, new_ref, factor, faces, held, out_ref, sems)
+        faces = {
+            0: side_of(beyond_ref[0], near_ref[0]),
+            xcount - 1: side_of(near_ref[0], beyond_ref[0]),
+        }
+        copies = finish(
+            outer, lambda k, j: sums_ref[k, j].astype(F32), base_ref, new_ref, factor, faces, held, out_ref, sems
+        )
         me = lax.axis_index("trait")
         values = [r[...].reshape(rows, owned) for r in block_refs]
         for k in range(2):
@@ -256,11 +316,12 @@
         for copy in copies:
             copy.wait()
 
-    return call(
-        body, "second_first", [sums, base, new, death, lo, hi, kernels, *blocks],
+    args = [sums, base, new, death, near, beyond, kernels, *blocks, begun]
+    return call(
+        body, "second_outer", args,
         [jax.ShapeDtypeStruct((xcount, ycount, owned), F32), pltpu.VMEM((2, rows, owned), F32)],
-        scratch=[pltpu.VMEM((len(cells), ycount, owned), F32), pltpu.SemaphoreType.DMA((len(cells),))],
-        out_specs=[ANYWHERE, SPEC],
+        scratch=[pltpu.VMEM((len(outer), ycount, owned), F32), pltpu.SemaphoreType.DMA((len(outer),))],
+        specs=[SPEC] * (len(args) - 1) + [FROM_HBM], out_specs=[ANYWHERE, SPEC], alias={len(args) - 1: 0},
     )
 
 
@@ -273,7 +334,11 @@
         for k in range(2):
             sums[k] = (part_ref[k] + blocks_dot([last_ref[...].reshape(rows, owned)], k_ref, k, [me ^ 3])).astype(BF16)
         factor = SECOND / (1.0 + SECOND * d_ref[...])
-        for copy in finish(cells, ycount, sums, base_ref, new_ref, factor, {}, held, out_ref, sems):
+
+        def sums_at(k, j):
+            return sums[k, pl.ds(j * ycount, ycount), :].astype(F32)
+
+        for copy in finish(list(enumerate(cells)), sums_at, base_ref, new_ref, factor, {}, held, out_ref, sems):
             copy.wait()
 
     return call(
@@ -302,24 +367,25 @@
     def to_far(v):
         return lax.ppermute(v, "trait", [(i, i ^ 2) for i in range(traits)])
 
-    def faces(head, tail):
-        lo = lax.ppermute(tail, "gx", [(i, (i + 1) % gcount) for i in range(gcount)])
-        hi = lax.ppermute(head, "gx", [((i + 1) % gcount, i) for i in range(gcount)])
-        return lo, hi
-
-    own_a, head, tail = round_chunk((section_one, section_two), chunks[0], True)
+    def to_near(v):
+        return lax.ppermute(v, "gx", [(i, i ^ 1) for i in range(gcount)])
+
+    def to_beyond(v):
+        return lax.ppermute(v, "gx", [(i, (i + 1 - 2 * (i % 2 == 0)) % gcount) for i in range(gcount)])
+
+    own_a, near, beyond = round_chunk((section_one, section_two), chunks[0], True)
     far_a = to_far(own_a)
     own_b = round_chunk((after(section_one, own_a), section_two), chunks[1], False)[0]
     far_b = to_far(own_b)
-    head, tail, kernels = lax.optimization_barrier((head, tail, kernels, own_b))[:3]
-    lo, hi = faces(head, tail)
-    base_a, base_b = before_first(section_one, section_two, lo, hi, growth, chunks)
+    near, beyond, kernels = lax.optimization_barrier((near, beyond, kernels, own_b))[:3]
+    near, beyond = to_near(near), to_beyond(beyond)
+    base_a, base_b = before_first(section_one, section_two, near, beyond, growth, chunks)
     sib_a = to_sibling(after(own_a, own_b))
     sib_b = to_sibling(own_b)
     far_a = after(far_a, base_a)
     farsib_a = to_sibling(far_a)
     part_a = early_part([own_a, sib_a, far_a], kernels)
-    new_a, rounded_a, rest_a, new_head, new_tail = first_node(
+    new_a, rounded_a, rest_a, new_near, new_beyond = first_node(
         part_a, farsib_a, base_a, section_one, section_two, initial, kernels, death, chunks[0], True
     )
     nfar_a = to_far(rounded_a)
@@ -327,21 +393,25 @@
 
     far_b = after(far_b, rounded_a)
     farsib_b = to_sibling(far_b)
-    part_b = early_part([own_b, sib_b, far_b], kernels)
+    part_b, new_one = early_part([own_b, sib_b, far_b], kernels, new_a, chunks[0], xcount)
     new_b, rounded_b, rest_b = first_node(
         part_b, farsib_b, base_b, section_one, section_two, initial, kernels, death, chunks[1], False
     )
     nfar_b = to_far(rounded_b)
     nsib_b = to_sibling(rounded_b)
-    new_lo, new_hi = faces(*lax.optimization_barrier((new_head, new_tail, rounded_b))[:2])
+    new_near, new_beyond = lax.optimization_barrier((new_near, new_beyond, rounded_b))[:2]
+    new_near, new_beyond = to_near(new_near), to_beyond(new_beyond)
     nfar_a = after(nfar_a, rounded_b)
     nfarsib_a = to_sibling(nfar_a)
-    new_one, nbase_a, nbase_b = before_second((new_a, new_b), (rest_a, rest_b), growth, death, chunks)
-    sums_a = whole_sums([rounded_a, nsib_a, nfar_a, nfarsib_a], after(kernels, nbase_a))
-    nfar_b = after(nfar_b, sums_a, new_lo, new_hi)
+    new_one, nbase_a, nbase_b = before_second((new_a, new_b), (rest_a, rest_b), growth, death, new_one, chunks)
+    begun, sums_a = second_inner(
+        [rounded_a, nsib_a, nfar_a, nfarsib_a], nbase_a, new_a, death, kernels, chunks[0], xcount
+    )
+    nfar_b = after(nfar_b, sums_a, new_near, new_beyond)
     nfarsib_b = to_sibling(nfar_b)
-    begun, npart_b = second_first(
-        sums_a, nbase_a, new_a, death, new_lo, new_hi, [rounded_b, nsib_b, nfar_b], kernels, chunks[0], xcount
+    begun, npart_b = second_outer(
+        sums_a, nbase_a, new_a, death, new_near, new_beyond, kernels, [rounded_b, nsib_b, nfar_b], begun, chunks[0],
+        xcount,
     )
     new_two = second_last(npart_b, nfarsib_b, nbase_b, new_b, death, kernels, begun, chunks[1], xcount)
     return new_one, new_two

time: 43.6 us -> 45.3 us (1.039)
  waiting for transfers between devices: 13.1 us -> 14.3 us
  Pallas kernels: 11.5 us -> 12.2 us
    ppermute x4, starting transfers between devices: 7.71 us -> 6.06 us  [to_far(): return lax.ppermute(v, 'trait', [(i, i ^ 2) for i in range(traits)])]
    ppermute x4, waiting for transfers between devices: 6.52 us -> 8.06 us  [to_far(): return lax.ppermute(v, 'trait', [(i, i ^ 2) for i in range(traits)])]
    ppermute x4, starting transfers between devices: 9.5 us -> 10.4 us  [the longest x2 7.14 us: to_beyond(): lax.ppermute(v, 'gx', [(i, (i + 1 - 2 * (i % 2 == 0)) % gcount) for i in...]
    pallas_call x11, Pallas kernels: 11.5 us -> 12.2 us  [call(): pl.pallas_call(body, out_shape=outs, in_specs=specs, out_specs=out_specs...]
    ppermute x4, waiting for transfers between devices: 4.71 us -> 4.19 us  [the longest x2 2.1 us: to_near(): return lax.ppermute(v, 'gx', [(i, i ^ 1) for i in range(gcount)])]
    ppermute x8, starting transfers between devices: 0.86 us -> 1.36 us  [to_sibling(): return lax.ppermute(v, 'trait', [(i, i ^ 1) for i in range(traits)])]
  transfers between devices with their start and end apart: 16 -> 16, of which waited for: 6 -> 8; matrix products, arithmetic and copies ran while one was open for 0% -> 0% of each run, Pallas kernels for 21% -> 21%
where the time goes in v1:
time: 45.3 us; the launch traced here: 45.1 us
  starting transfers between devices  17.8 us (39%)
  waiting for transfers between devices  14.3 us (32%)
  Pallas kernels  12.2 us (27%)
  between operations  0.8 us (2%)
    pallas_call x11, Pallas kernels, call(): pl.pallas_call(body, out_shape=outs, in_specs=specs, out_specs=out_specs...  12.2 us
    ppermute x4, waiting for transfers between devices, to_far(): return lax.ppermute(v, 'trait', [(i, i ^ 2) for i in range(traits)])  8.06 us
    ppermute x2, starting transfers between devices, to_beyond(): lax.ppermute(v, 'gx', [(i, (i + 1 - 2 * (i % 2 == 0)) % gcount) for i in...  7.14 us
    ppermute x4, starting transfers between devices, to_far(): return lax.ppermute(v, 'trait', [(i, i ^ 2) for i in range(traits)])  6.06 us
    ppermute x2, starting transfers between devices, to_near(): return lax.ppermute(v, 'gx', [(i, i ^ 1) for i in range(gcount)])  3.22 us
    ppermute x2, waiting for transfers between devices, to_near(): return lax.ppermute(v, 'gx', [(i, i ^ 1) for i in range(gcount)])  2.1 us
    ppermute x2, waiting for transfers between devices, to_beyond(): lax.ppermute(v, 'gx', [(i, (i + 1 - 2 * (i % 2 == 0)) % gcount) for i in...  2.09 us
    ppermute x8, waiting for transfers between devices, to_sibling(): return lax.ppermute(v, 'trait', [(i, i ^ 1) for i in range(traits)])  2.04 us
  transfers between devices with their start and end apart: 16, of which 8 were waited for; matrix products, arithmetic and copies ran while one was open for 0% of the time, Pallas kernels for 21%

profile of v1, /device:TPU:0, one launch (start us, length us, event | category | flops | bytes accessed | tf_op | source)
XLA Modules:
  0.0 45.1 jit_solution(257411513878453154)
XLA Ops:
  0.6 0.0 copy-start.1
  0.6 0.0 copy-start.2
  0.7 0.0 copy-start
  0.7 1.7 %round_chunk.2 = (bf16[2,768,256]{2,1,0:T(8,128)(2,1)S(1)}, bf16[2,128,256]{2,1,0:T(8,128)(2,1)S(1)}, bf16[2,128,256]{2,1,0:T(8,128)(2,1)S(1)}) custom-call(f32[8,128,256]{2,1,0:T(8,128)} %one_ref.5, f32[8,128,256]{2,1,0:T(8,128)} %two_ref.5), custom_call_target="tpu_custom_call" | custom-call | tf_op jit(solution)/shard_map/round_chunk/pallas_call | solution.py:37
  2.4 3.0 %collective-permute-start.1 = (bf16[2,768,256]{2,1,0:T(8,128)(2,1)S(1)}, bf16[2,768,256]{2,1,0:T(8,128)(2,1)S(1)}, u32[]{:S(2)}, u32[]{:S(2)}) collective-permute-start(bf16[2,768,256]{2,1,0:T(8,128)(2,1)S(1)} %get-tuple-element.37.refs_0_), channel_id=1, source_target_pairs={{0,2},{1,3},{2,0},{3,1},{4,6},{5,7},{6,4},{7,5},{8,10},{9,11},{10,... | collective-permute-start | bytes 2359304 | tf_op jit(solution)/shard_map/ppermute | solution.py:368
  5.4 1.1 %round_chunk.3.refs_0_ = bf16[2,256,256]{2,1,0:T(8,128)(2,1)S(1)} custom-call(f32[8,128,256]{2,1,0:T(8,128)} %one_ref.5, f32[8,128,256]{2,1,0:T(8,128)} %two_ref.5), custom_call_target="tpu_custom_call" | custom-call | tf_op jit(solution)/shard_map/round_chunk/pallas_call | solution.py:37
  6.6 0.1 collective-permute-start
  6.7 1.6 %collective-permute-start.2 = (bf16[2,128,256]{2,1,0:T(8,128)(2,1)S(1)}, bf16[2,128,256]{2,1,0:T(8,128)(2,1)S(1)}, u32[]{:S(2)}, u32[]{:S(2)}) collective-permute-start(bf16[2,128,256]{2,1,0:T(8,128)(2,1)S(1)} %get-tuple-element.40), channel_id=1, source_target_pairs={{0,4},{4,0},{8,12},{12,8},{16,20},{20,16},{24,28},{28,24},{1,5},{5... | collective-permute-start | bytes 393224 | tf_op jit(solution)/shard_map/ppermute | solution.py:371
  8.2 3.6 %collective-permute-start.3 = (bf16[2,128,256]{2,1,0:T(8,128)(2,1)S(1)}, bf16[2,128,256]{2,1,0:T(8,128)(2,1)S(1)}, u32[]{:S(2)}, u32[]{:S(2)}) collective-permute-start(bf16[2,128,256]{2,1,0:T(8,128)(2,1)S(1)} %get-tuple-element.41), channel_id=1, source_target_pairs={{0,28},{4,8},{8,4},{12,16},{16,12},{20,24},{24,20},{28,0},{1,29},{... | collective-permute-start | bytes 393224 | tf_op jit(solution)/shard_map/ppermute | solution.py:374
  11.8 0.5 %collective-permute-start.6 = (bf16[2,256,256]{2,1,0:T(8,128)(2,1)S(1)}, bf16[2,256,256]{2,1,0:T(8,128)(2,1)S(1)}, u32[]{:S(2)}, u32[]{:S(2)}) collective-permute-start(bf16[2,256,256]{2,1,0:T(8,128)(2,1)S(1)} %round_chunk.3.refs_0_), channel_id=1, source_target_pairs={{0,2},{1,3},{2,0},{3,1},{4,6},{5,7},{6,4},{7,5},{8,10},{9,11},{10,... | collective-permute-start | bytes 786440 | tf_op jit(solution)/shard_map/ppermute | solution.py:368
  12.3 2.1 %collective-permute-done.2.near_ref = bf16[2,128,256]{2,1,0:T(8,128)(2,1)S(1)} collective-permute-done((bf16[2,128,256]{2,1,0:T(8,128)(2,1)S(1)}, bf16[2,128,256]{2,1,0:T(8,128)(2,1)S(1)}, u32[]{:S(2)}, u32[]{:S(2)}) %collective-permute-start.2) | collective-permute-done | bytes 131104 | tf_op jit(solution)/shard_map/ppermute | solution.py:371
  14.4 0.0 collective-permute-start.5
  14.4 2.1 %collective-permute-done.3.beyond_ref = bf16[2,128,256]{2,1,0:T(8,128)(2,1)S(1)} collective-permute-done((bf16[2,128,256]{2,1,0:T(8,128)(2,1)S(1)}, bf16[2,128,256]{2,1,0:T(8,128)(2,1)S(1)}, u32[]{:S(2)}, u32[]{:S(2)}) %collective-permute-start.3) | collective-permute-done | bytes 131104 | tf_op jit(solution)/shard_map/ppermute | solution.py:374
  16.5 0.9 %before_first.1 = (f32[2,6,128,256]{3,2,1,0:T(8,128)S(1)}, f32[2,2,128,256]{3,2,1,0:T(8,128)S(1)}) custom-call(f32[8,128,256]{2,1,0:T(8,128)S(1)} %copy-done.1, f32[8,128,256]{2,1,0:T(8,128)S(1)} %copy-done.2, bf16[2,128,256]{2,1,0:T(8,128)(2,1)S(1)} %collective-permute-done.2.near_ref, bf16[2,128,256]{2,1,0:T(8,128)(2,1)S(1)} %collective-permute-done.3.beyond_ref, ...), custom_call_target="tpu_custom_call" | custom-call | tf_op jit(solution)/shard_map/before_first/pallas_call | solution.py:37
  17.4 6.4 %collective-permute-done.1.refs_2_ = bf16[2,768,256]{2,1,0:T(8,128)(2,1)S(1)} collective-permute-done((bf16[2,768,256]{2,1,0:T(8,128)(2,1)S(1)}, bf16[2,768,256]{2,1,0:T(8,128)(2,1)S(1)}, u32[]{:S(2)}, u32[]{:S(2)}) %collective-permute-start.1) | collective-permute-done | bytes 786464 | tf_op jit(solution)/shard_map/ppermute | solution.py:368
  23.8 0.0 collective-permute-start.4
  23.8 0.0 collective-permute-done.refs_1_
  23.8 0.0 copy-done
  23.8 1.4 %early_part.2.part_ref = f32[2,1536,256]{2,1,0:T(8,128)S(1)} custom-call(bf16[2,768,256]{2,1,0:T(8,128)(2,1)S(1)} %get-tuple-element.37.refs_0_, bf16[2,768,256]{2,1,0:T(8,128)(2,1)S(1)} %collective-permute-done.refs_1_, bf16[2,768,256]{2,1,0:T(8,128)(2,1)S(1)} %collective-permute-done.1.refs_2_, bf16[2,1024,256]{2,1,0:T(8,128)(2,1)S(1)} %copy-done), custom_call_target="tpu_custom_call" | custom-call | flops 20000000000 | tf_op jit(solution)/shard_map/early_part/pallas_call | solution.py:37
  25.2 0.9 %collective-permute-done.4.last_ref = bf16[2,768,256]{2,1,0:T(8,128)(2,1)S(1)} collective-permute-done((bf16[2,768,256]{2,1,0:T(8,128)(2,1)S(1)}, bf16[2,768,256]{2,1,0:T(8,128)(2,1)S(1)}, u32[]{:S(2)}, u32[]{:S(2)}) %collective-permute-start.4) | collective-permute-done | bytes 786464 | tf_op jit(solution)/shard_map/ppermute | solution.py:365
  26.1 0.0 copy-done.3
  26.1 1.2 %first_node.2 = (f32[6,128,256]{2,1,0:T(8,128)S(1)}, bf16[1,768,256]{2,1,0:T(8,128)(2,1)S(1)}, f32[6,128,256]{2,1,0:T(8,128)S(1)}, bf16[1,128,256]{2,1,0:T(8,128)(2,1)S(1)}, bf16[1,128,256]{2,1,0:T(8,128)(2,1)S(1)}) custom-call(f32[2,1536,256]{2,1,0:T(8,128)S(1)} %early_part.2.part_ref, bf16[2,768,256]{2,1,0:T(8,128)(2,1)S(1)} %collective-permute-done.4.last_ref, ...), custom_call_target="tpu_custom_call" | custom-call | tf_op jit(solution)/shard_map/first_node/pallas_call | solution.py:37
  27.3 2.1 %collective-permute-start.9 = (bf16[1,768,256]{2,1,0:T(8,128)(2,1)S(1)}, bf16[1,768,256]{2,1,0:T(8,128)(2,1)S(1)}, u32[]{:S(2)}, u32[]{:S(2)}) collective-permute-start(bf16[1,768,256]{2,1,0:T(8,128)(2,1)S(1)} %get-tuple-element.46.refs_0_), channel_id=1, source_target_pairs={{0,2},{1,3},{2,0},{3,1},{4,6},{5,7},{6,4},{7,5},{8,10},{9,11},{10,... | collective-permute-start | bytes 1179656 | tf_op jit(solution)/shard_map/ppermute | solution.py:368
  29.4 0.0 collective-permute-start.8
  29.4 0.0 collective-permute-done.6.refs_2_
  29.4 0.5 %collective-permute-start.7 = (bf16[2,256,256]{2,1,0:T(8,128)(2,1)S(1)}, bf16[2,256,256]{2,1,0:T(8,128)(2,1)S(1)}, u32[]{:S(2)}, u32[]{:S(2)}) collective-permute-start(bf16[2,256,256]{2,1,0:T(8,128)(2,1)S(1)} %collective-permute-done.6.refs_2_), channel_id=1, source_target_pairs={{0,1},{1,0},{2,3},{3,2},{4,5},{5,4},{6,7},{7,6},{8,9},{9,8},{10,11... | collective-permute-start | bytes 786440 | tf_op jit(solution)/shard_map/ppermute | solution.py:365
  29.9 0.0 collective-permute-done.5.refs_1_
  30.0 0.9 %early_part.3 = (f32[2,512,256]{2,1,0:T(8,128)S(1)}, f32[8,128,256]{2,1,0:T(8,128)}) custom-call(bf16[2,256,256]{2,1,0:T(8,128)(2,1)S(1)} %round_chunk.3.refs_0_, bf16[2,256,256]{2,1,0:T(8,128)(2,1)S(1)} %collective-permute-done.5.refs_1_, bf16[2,256,256]{2,1,0:T(8,128)(2,1)S(1)} %collective-permute-done.6.refs_2_, bf16[2,1024,256]{2,1,0:T(8,128)(2,1)S(1)} %copy-done, ...), custom_call_target="tpu_custom_call" | custom-call | flops 20000000000 | tf_op jit(solution)/shard_map/early_part/pallas_call | solution.py:37
  30.9 0.6 %collective-permute-done.7.last_ref = bf16[2,256,256]{2,1,0:T(8,128)(2,1)S(1)} collective-permute-done((bf16[2,256,256]{2,1,0:T(8,128)(2,1)S(1)}, bf16[2,256,256]{2,1,0:T(8,128)(2,1)S(1)}, u32[]{:S(2)}, u32[]{:S(2)}) %collective-permute-start.7) | collective-permute-done | bytes 262176 | tf_op jit(solution)/shard_map/ppermute | solution.py:365
  31.5 0.5 %first_node.3 = (f32[2,128,256]{2,1,0:T(8,128)S(1)}, bf16[1,256,256]{2,1,0:T(8,128)(2,1)S(1)}, f32[2,128,256]{2,1,0:T(8,128)S(1)}) custom-call(f32[2,512,256]{2,1,0:T(8,128)S(1)} %get-tuple-element.48.part_ref, bf16[2,256,256]{2,1,0:T(8,128)(2,1)S(1)} %collective-permute-done.7.last_ref, f32[2,2,128,256]{3,2,1,0:T(8,128)S(1)} %get-tuple-element.49.base_ref, ...), custom_call_target="tpu_custom_call" | custom-call | tf_op jit(solution)/shard_map/first_node/pallas_call | solution.py:37
  32.0 0.4 collective-permute-start.14
  32.4 1.7 %collective-permute-start.11 = (bf16[1,128,256]{2,1,0:T(8,128)(2,1)S(1)}, bf16[1,128,256]{2,1,0:T(8,128)(2,1)S(1)}, u32[]{:S(2)}, u32[]{:S(2)}) collective-permute-start(bf16[1,128,256]{2,1,0:T(8,128)(2,1)S(1)} %get-tuple-element.61), channel_id=1, source_target_pairs={{0,4},{4,0},{8,12},{12,8},{16,20},{20,16},{24,28},{28,24},{1,5},{5... | collective-permute-start | bytes 196616 | tf_op jit(solution)/shard_map/ppermute | solution.py:371
  34.1 3.6 %collective-permute-start.12 = (bf16[1,128,256]{2,1,0:T(8,128)(2,1)S(1)}, bf16[1,128,256]{2,1,0:T(8,128)(2,1)S(1)}, u32[]{:S(2)}, u32[]{:S(2)}) collective-permute-start(bf16[1,128,256]{2,1,0:T(8,128)(2,1)S(1)} %get-tuple-element.62), channel_id=1, source_target_pairs={{0,28},{4,8},{8,4},{12,16},{16,12},{20,24},{24,20},{28,0},{1,29},{... | collective-permute-start | bytes 196616 | tf_op jit(solution)/shard_map/ppermute | solution.py:374
  37.7 1.7 %collective-permute-done.9.refs_2_ = bf16[1,768,256]{2,1,0:T(8,128)(2,1)S(1)} collective-permute-done((bf16[1,768,256]{2,1,0:T(8,128)(2,1)S(1)}, bf16[1,768,256]{2,1,0:T(8,128)(2,1)S(1)}, u32[]{:S(2)}, u32[]{:S(2)}) %collective-permute-start.9) | collective-permute-done | bytes 393248 | tf_op jit(solution)/shard_map/ppermute | solution.py:368
  39.3 0.0 collective-permute-start.10
  39.3 0.7 %before_second.1 = (f32[8,128,256]{2,1,0:T(8,128)}, f32[6,128,256]{2,1,0:T(8,128)S(1)}, f32[2,128,256]{2,1,0:T(8,128)S(1)}) custom-call(f32[6,128,256]{2,1,0:T(8,128)S(1)} %get-tuple-element.45.refs_4_.refs_0_.refs_5_.new_ref, f32[2,128,256]{2,1,0:T(8,128)S(1)} %get-tuple-element.50.refs_1_.new_ref, ...), custom_call_target="tpu_custom_call", output_to_operand_aliasing={{0}: (6, {})} | custom-call | flops 20000000000 | tf_op jit(solution)/shard_map/before_second/pallas_call | solution.py:37
  40.1 0.0 collective-permute-done.8.refs_1_
  40.1 0.6 %collective-permute-start.13 = (bf16[1,256,256]{2,1,0:T(8,128)(2,1)S(1)}, bf16[1,256,256]{2,1,0:T(8,128)(2,1)S(1)}, u32[]{:S(2)}, u32[]{:S(2)}) collective-permute-start(bf16[1,256,256]{2,1,0:T(8,128)(2,1)S(1)} %get-tuple-element.55.refs_0_), channel_id=1, source_target_pairs={{0,1},{1,0},{2,3},{3,2},{4,5},{5,4},{6,7},{7,6},{8,9},{9,8},{10,11... | collective-permute-start | bytes 393224 | tf_op jit(solution)/shard_map/ppermute | solution.py:365
  40.6 0.4 collective-permute-done.10.refs_3_
  41.1 1.7 %second_inner.1 = (f32[8,128,256]{2,1,0:T(8,128)}, bf16[2,2,128,256]{3,2,1,0:T(8,128)(2,1)S(1)}) custom-call(bf16[1,768,256]{2,1,0:T(8,128)(2,1)S(1)} %get-tuple-element.46.refs_0_, bf16[1,768,256]{2,1,0:T(8,128)(2,1)S(1)} %collective-permute-done.8.refs_1_, bf16[1,768,256]{2,1,0:T(8,128)(2,1)S(1)} %collective-permute-done.9.refs_2_, ...), custom_call_target="tpu_custom_call" | custom-call | tf_op jit(solution)/shard_map/second_inner/pallas_call | solution.py:37
  42.7 0.0 collective-permute-done.11.near_ref
  42.7 0.0 collective-permute-done.12.beyond_ref
  42.8 0.0 collective-permute-done.14.refs_2_
  42.8 0.2 collective-permute-start.15
  43.0 0.0 collective-permute-done.13.refs_1_
  43.0 1.1 %second_outer.1 = (f32[8,128,256]{2,1,0:T(8,128)}, f32[2,256,256]{2,1,0:T(8,128)S(1)}) custom-call(bf16[2,2,128,256]{3,2,1,0:T(8,128)(2,1)S(1)} %get-tuple-element.58.sums_ref, f32[6,128,256]{2,1,0:T(8,128)S(1)} %get-tuple-element.57.refs_4_.base_ref, ...), custom_call_target="tpu_custom_call", output_to_operand_aliasing={{0}: (10, {})} | custom-call | tf_op jit(solution)/shard_map/second_outer/pallas_call | solution.py:37
  44.1 0.1 collective-permute-done.15.last_ref
  44.2 0.9 %second_last.1 = f32[8,128,256]{2,1,0:T(8,128)} custom-call(f32[2,256,256]{2,1,0:T(8,128)S(1)} %get-tuple-element.65.part_ref, bf16[1,256,256]{2,1,0:T(8,128)(2,1)S(1)} %collective-permute-done.15.last_ref, f32[2,128,256]{2,1,0:T(8,128)S(1)} %get-tuple-element.66.base_ref, ...), custom_call_target="tpu_custom_call", output_to_operand_aliasing={{}: (6, {})} | custom-call | tf_op jit(solution)/shard_map/second_last/pallas_call | solution.py:37
  (7 shorter events, 0.0 us)
Async XLA Ops:
  0.6 15.9 %copy-start.1 = (f32[8,128,256]{2,1,0:T(8,128)S(1)}, f32[8,128,256]{2,1,0:T(8,128)}, u32[]{:S(2)}) copy-start(f32[8,128,256]{2,1,0:T(8,128)} %one_ref.5) | copy-start | bytes 3145732
  0.6 15.8 %copy-start.2 = (f32[8,128,256]{2,1,0:T(8,128)S(1)}, f32[8,128,256]{2,1,0:T(8,128)}, u32[]{:S(2)}) copy-start(f32[8,128,256]{2,1,0:T(8,128)} %two_ref.5) | copy-start | bytes 3145732
  0.7 23.2 %copy-start = (bf16[2,1024,256]{2,1,0:T(8,128)(2,1)S(1)}, bf16[2,1024,256]{2,1,0:T(8,128)(2,1)}, u32[]{:S(2)}) copy-start(bf16[2,1024,256]{2,1,0:T(8,128)(2,1)} %k_ref.3) | copy-start | bytes 3145732
  0.7 15.8 %copy-start.5 = (f32[256]{0:T(256)S(1)}, f32[256]{0:T(256)}, u32[]{:S(2)}) copy-start(f32[256]{0:T(256)} %param.10) | copy-start | bytes 3076
  2.4 21.4 %collective-permute-start.1 = (bf16[2,768,256]{2,1,0:T(8,128)(2,1)S(1)}, bf16[2,768,256]{2,1,0:T(8,128)(2,1)S(1)}, u32[]{:S(2)}, u32[]{:S(2)}) collective-permute-start(bf16[2,768,256]{2,1,0:T(8,128)(2,1)S(1)} %get-tuple-element.37.refs_0_), channel_id=1, source_target_pairs={{0,2},{1,3},{2,0},{3,1},{4,6},{5,7},{6,4},{7,5},{8,10},{9,11},{10,... | collective-permute-start | bytes 2359304 | tf_op jit(solution)/shard_map/ppermute | solution.py:368
  6.6 17.2 %collective-permute-start = (bf16[2,768,256]{2,1,0:T(8,128)(2,1)S(1)}, bf16[2,768,256]{2,1,0:T(8,128)(2,1)S(1)}, u32[]{:S(2)}, u32[]{:S(2)}) collective-permute-start(bf16[2,768,256]{2,1,0:T(8,128)(2,1)S(1)} %get-tuple-element.37.refs_0_), channel_id=1, source_target_pairs={{0,1},{1,0},{2,3},{3,2},{4,5},{5,4},{6,7},{7,6},{8,9},{9,8},{10,11... | collective-permute-start | bytes 2359304 | tf_op jit(solution)/shard_map/ppermute | solution.py:365
  6.7 7.7 %collective-permute-start.2 = (bf16[2,128,256]{2,1,0:T(8,128)(2,1)S(1)}, bf16[2,128,256]{2,1,0:T(8,128)(2,1)S(1)}, u32[]{:S(2)}, u32[]{:S(2)}) collective-permute-start(bf16[2,128,256]{2,1,0:T(8,128)(2,1)S(1)} %get-tuple-element.40), channel_id=1, source_target_pairs={{0,4},{4,0},{8,12},{12,8},{16,20},{20,16},{24,28},{28,24},{1,5},{5... | collective-permute-start | bytes 393224 | tf_op jit(solution)/shard_map/ppermute | solution.py:371
  8.2 8.3 %collective-permute-start.3 = (bf16[2,128,256]{2,1,0:T(8,128)(2,1)S(1)}, bf16[2,128,256]{2,1,0:T(8,128)(2,1)S(1)}, u32[]{:S(2)}, u32[]{:S(2)}) collective-permute-start(bf16[2,128,256]{2,1,0:T(8,128)(2,1)S(1)} %get-tuple-element.41), channel_id=1, source_target_pairs={{0,28},{4,8},{8,4},{12,16},{16,12},{20,24},{24,20},{28,0},{1,29},{... | collective-permute-start | bytes 393224 | tf_op jit(solution)/shard_map/ppermute | solution.py:374
  11.8 17.7 %collective-permute-start.6 = (bf16[2,256,256]{2,1,0:T(8,128)(2,1)S(1)}, bf16[2,256,256]{2,1,0:T(8,128)(2,1)S(1)}, u32[]{:S(2)}, u32[]{:S(2)}) collective-permute-start(bf16[2,256,256]{2,1,0:T(8,128)(2,1)S(1)} %round_chunk.3.refs_0_), channel_id=1, source_target_pairs={{0,2},{1,3},{2,0},{3,1},{4,6},{5,7},{6,4},{7,5},{8,10},{9,11},{10,... | collective-permute-start | bytes 786440 | tf_op jit(solution)/shard_map/ppermute | solution.py:368
  14.4 15.6 %collective-permute-start.5 = (bf16[2,256,256]{2,1,0:T(8,128)(2,1)S(1)}, bf16[2,256,256]{2,1,0:T(8,128)(2,1)S(1)}, u32[]{:S(2)}, u32[]{:S(2)}) collective-permute-start(bf16[2,256,256]{2,1,0:T(8,128)(2,1)S(1)} %round_chunk.3.refs_0_), channel_id=1, source_target_pairs={{0,1},{1,0},{2,3},{3,2},{4,5},{5,4},{6,7},{7,6},{8,9},{9,8},{10,11... | collective-permute-start | bytes 786440 | tf_op jit(solution)/shard_map/ppermute | solution.py:365
  23.8 2.3 %copy-start.3 = (f32[8,128,256]{2,1,0:T(8,128)S(1)}, f32[8,128,256]{2,1,0:T(8,128)}, u32[]{:S(2)}) copy-start(f32[8,128,256]{2,1,0:T(8,128)} %init_ref.3) | copy-start | bytes 3145732
  23.8 2.3 %copy-start.4 = (f32[256]{0:T(256)S(1)}, f32[256]{0:T(256)}, u32[]{:S(2)}) copy-start(f32[256]{0:T(256)} %param.11) | copy-start | bytes 3076
  23.8 2.3 %collective-permute-start.4 = (bf16[2,768,256]{2,1,0:T(8,128)(2,1)S(1)}, bf16[2,768,256]{2,1,0:T(8,128)(2,1)S(1)}, u32[]{:S(2)}, u32[]{:S(2)}) collective-permute-start(bf16[2,768,256]{2,1,0:T(8,128)(2,1)S(1)} %collective-permute-done.1.refs_2_), channel_id=1, source_target_pairs={{0,1},{1,0},{2,3},{3,2},{4,5},{5,4},{6,7},{7,6},{8,9},{9,8},{10,11... | collective-permute-start | bytes 2359304 | tf_op jit(solution)/shard_map/ppermute | solution.py:365
  27.3 12.0 %collective-permute-start.9 = (bf16[1,768,256]{2,1,0:T(8,128)(2,1)S(1)}, bf16[1,768,256]{2,1,0:T(8,128)(2,1)S(1)}, u32[]{:S(2)}, u32[]{:S(2)}) collective-permute-start(bf16[1,768,256]{2,1,0:T(8,128)(2,1)S(1)} %get-tuple-element.46.refs_0_), channel_id=1, source_target_pairs={{0,2},{1,3},{2,0},{3,1},{4,6},{5,7},{6,4},{7,5},{8,10},{9,11},{10,... | collective-permute-start | bytes 1179656 | tf_op jit(solution)/shard_map/ppermute | solution.py:368
  29.4 10.6 %collective-permute-start.8 = (bf16[1,768,256]{2,1,0:T(8,128)(2,1)S(1)}, bf16[1,768,256]{2,1,0:T(8,128)(2,1)S(1)}, u32[]{:S(2)}, u32[]{:S(2)}) collective-permute-start(bf16[1,768,256]{2,1,0:T(8,128)(2,1)S(1)} %get-tuple-element.46.refs_0_), channel_id=1, source_target_pairs={{0,1},{1,0},{2,3},{3,2},{4,5},{5,4},{6,7},{7,6},{8,9},{9,8},{10,11... | collective-permute-start | bytes 1179656 | tf_op jit(solution)/shard_map/ppermute | solution.py:365
  29.4 2.1 %collective-permute-start.7 = (bf16[2,256,256]{2,1,0:T(8,128)(2,1)S(1)}, bf16[2,256,256]{2,1,0:T(8,128)(2,1)S(1)}, u32[]{:S(2)}, u32[]{:S(2)}) collective-permute-start(bf16[2,256,256]{2,1,0:T(8,128)(2,1)S(1)} %collective-permute-done.6.refs_2_), channel_id=1, source_target_pairs={{0,1},{1,0},{2,3},{3,2},{4,5},{5,4},{6,7},{7,6},{8,9},{9,8},{10,11... | collective-permute-start | bytes 786440 | tf_op jit(solution)/shard_map/ppermute | solution.py:365
  32.0 10.7 %collective-permute-start.14 = (bf16[1,256,256]{2,1,0:T(8,128)(2,1)S(1)}, bf16[1,256,256]{2,1,0:T(8,128)(2,1)S(1)}, u32[]{:S(2)}, u32[]{:S(2)}) collective-permute-start(bf16[1,256,256]{2,1,0:T(8,128)(2,1)S(1)} %get-tuple-element.55.refs_0_), channel_id=1, source_target_pairs={{0,2},{1,3},{2,0},{3,1},{4,6},{5,7},{6,4},{7,5},{8,10},{9,11},{10,... | collective-permute-start | bytes 393224 | tf_op jit(solution)/shard_map/ppermute | solution.py:368
  32.4 10.3 %collective-permute-start.11 = (bf16[1,128,256]{2,1,0:T(8,128)(2,1)S(1)}, bf16[1,128,256]{2,1,0:T(8,128)(2,1)S(1)}, u32[]{:S(2)}, u32[]{:S(2)}) collective-permute-start(bf16[1,128,256]{2,1,0:T(8,128)(2,1)S(1)} %get-tuple-element.61), channel_id=1, source_target_pairs={{0,4},{4,0},{8,12},{12,8},{16,20},{20,16},{24,28},{28,24},{1,5},{5... | collective-permute-start | bytes 196616 | tf_op jit(solution)/shard_map/ppermute | solution.py:371
  34.1 8.7 %collective-permute-start.12 = (bf16[1,128,256]{2,1,0:T(8,128)(2,1)S(1)}, bf16[1,128,256]{2,1,0:T(8,128)(2,1)S(1)}, u32[]{:S(2)}, u32[]{:S(2)}) collective-permute-start(bf16[1,128,256]{2,1,0:T(8,128)(2,1)S(1)} %get-tuple-element.62), channel_id=1, source_target_pairs={{0,28},{4,8},{8,4},{12,16},{16,12},{20,24},{24,20},{28,0},{1,29},{... | collective-permute-start | bytes 196616 | tf_op jit(solution)/shard_map/ppermute | solution.py:374
  39.3 1.7 %collective-permute-start.10 = (bf16[1,768,256]{2,1,0:T(8,128)(2,1)S(1)}, bf16[1,768,256]{2,1,0:T(8,128)(2,1)S(1)}, u32[]{:S(2)}, u32[]{:S(2)}) collective-permute-start(bf16[1,768,256]{2,1,0:T(8,128)(2,1)S(1)} %collective-permute-done.9.refs_2_), channel_id=1, source_target_pairs={{0,1},{1,0},{2,3},{3,2},{4,5},{5,4},{6,7},{7,6},{8,9},{9,8},{10,11... | collective-permute-start | bytes 1179656 | tf_op jit(solution)/shard_map/ppermute | solution.py:365
  40.1 2.9 %collective-permute-start.13 = (bf16[1,256,256]{2,1,0:T(8,128)(2,1)S(1)}, bf16[1,256,256]{2,1,0:T(8,128)(2,1)S(1)}, u32[]{:S(2)}, u32[]{:S(2)}) collective-permute-start(bf16[1,256,256]{2,1,0:T(8,128)(2,1)S(1)} %get-tuple-element.55.refs_0_), channel_id=1, source_target_pairs={{0,1},{1,0},{2,3},{3,2},{4,5},{5,4},{6,7},{7,6},{8,9},{9,8},{10,11... | collective-permute-start | bytes 393224 | tf_op jit(solution)/shard_map/ppermute | solution.py:365
  42.8 1.4 %collective-permute-start.15 = (bf16[1,256,256]{2,1,0:T(8,128)(2,1)S(1)}, bf16[1,256,256]{2,1,0:T(8,128)(2,1)S(1)}, u32[]{:S(2)}, u32[]{:S(2)}) collective-permute-start(bf16[1,256,256]{2,1,0:T(8,128)(2,1)S(1)} %collective-permute-done.14.refs_2_), channel_id=1, source_target_pairs={{0,1},{1,0},{2,3},{3,2},{4,5},{5,4},{6,7},{7,6},{8,9},{9,8},{10,11... | collective-permute-start | bytes 393224 | tf_op jit(solution)/shard_map/ppermute | solution.py:365

commit v2 on v0

--- a/solution.py
+++ b/solution.py
@@ -47,37 +47,62 @@
     )(*args)
 
 
-def round_chunk(fields, cells, with_faces):
+def round_field(field, cells):
+    _, ycount, owned = field.shape
+
+    def body(field_ref, out_ref, held, sems):
+        copies = [pltpu.make_async_copy(field_ref.at[x], held.at[i], sems.at[i]) for i, x in enumerate(cells)]
+        for copy in copies:
+            copy.start()
+        for i, copy in enumerate(copies):
+            copy.wait()
+            out_ref[0, pl.ds(i * ycount, ycount), :] = held[i].astype(BF16)
+
+    return call(
+        body, "round_field", [field], [pltpu.VMEM((1, len(cells) * ycount, owned), BF16)],
+        scratch=[pltpu.VMEM((len(cells), ycount, owned), F32), pltpu.SemaphoreType.DMA((len(cells),))],
+        specs=[FROM_HBM],
+    )[0]
+
+
+def round_rest(fields, chunks):
     xcount, ycount, owned = fields[0].shape
     count = len(fields)
+    cells = chunks[-1]
+    ends = (0, xcount - 1)
+    wanted = [(f, x) for f in range(count) for x in (*cells, *ends)]
 
     def body(*refs):
         field_refs = refs[:count]
-        out = refs[count]
-        held, sems = refs[-2:]
-        copies = []
-        for f in range(count):
-            for i, x in enumerate(cells):
-                copies.append(pltpu.make_async_copy(field_refs[f].at[x], held.at[f, i], sems.at[f, i]))
-                copies[-1].start()
-        for f in range(count):
-            for i, x in enumerate(cells):
-                copies[f * len(cells) + i].wait()
-                value = held[f, i].astype(BF16)
-                out[f, i * ycount:(i + 1) * ycount, :] = value
-                if with_faces and x == 0:
-                    refs[count + 1][f] = value
-                if with_faces and x == xcount - 1:
-                    refs[count + 2][f] = value
-
-    outs = [pltpu.VMEM((count, len(cells) * ycount, owned), BF16)]
-    if with_faces:
-        outs += [pltpu.VMEM((count, ycount, owned), BF16)] * 2
-    return call(
-        body, "round_chunk", fields, outs,
-        scratch=[pltpu.VMEM((count, len(cells), ycount, owned), F32), pltpu.SemaphoreType.DMA((count, len(cells)))],
-        specs=[FROM_HBM] * count, gflop=0.0,
-    )
+        out_ref, head_ref, tail_ref, held, sems = refs[count:]
+        copies = [
+            pltpu.make_async_copy(field_refs[f].at[x], held.at[j], sems.at[j]) for j, (f, x) in enumerate(wanted)
+        ]
+        for copy in copies:
+            copy.start()
+        for j, (f, x) in enumerate(wanted):
+            copies[j].wait()
+            value = held[j].astype(BF16)
+            if x in cells:
+                i = cells.index(x)
+                out_ref[f, pl.ds(i * ycount, ycount), :] = value
+            else:
+                (head_ref if x == 0 else tail_ref)[f] = value
+
+    outs = [
+        pltpu.VMEM((count, len(cells) * ycount, owned), BF16),
+        pltpu.VMEM((count, ycount, owned), BF16),
+        pltpu.VMEM((count, ycount, owned), BF16),
+    ]
+    return call(
+        body, "round_rest", fields, outs,
+        scratch=[pltpu.VMEM((len(wanted), ycount, owned), F32), pltpu.SemaphoreType.DMA((len(wanted),))],
+        specs=[FROM_HBM] * count,
+    )
+
+
+def rows_of(refs):
+    return jnp.concatenate([r[...].reshape(-1, r.shape[-1]) for r in refs], axis=0)
 
 
 def blocks_dot(blocks, kernels_ref, k, owners):
@@ -110,30 +135,54 @@
     return call(body, "before_first", [one, two, lo, hi, growth], outs)
 
 
-def early_part(blocks, kernels):
-    rows, owned = blocks[0].shape[0] * blocks[0].shape[1], blocks[0].shape[2]
-    count = len(blocks)
+def early_part(own, sib, far, kernels, new=None, cells=(), xcount=0):
+    owned = own[0].shape[-1]
+    rows = len(own) * own[0].shape[0] * own[0].shape[1]
+    count = len(own)
 
     def body(*refs):
-        block_refs, k_ref, part_ref = refs[:count], refs[count], refs[count + 1]
-        me = lax.axis_index("trait")
-        values = [r[...].reshape(rows, owned) for r in block_refs]
-        for k in range(2):
-            part_ref[k] = blocks_dot(values, k_ref, k, [me ^ j for j in range(count)])
-
-    return call(body, "early_part", [*blocks, kernels], [pltpu.VMEM((2, rows, owned), F32)], gflop=20.0)[0]
+        blocks = [refs[j * count:(j + 1) * count] for j in range(3)]
+        k_ref = refs[3 * count]
+        copies = []
+        if new is None:
+            part_ref = refs[-1]
+        else:
+            new_ref, part_ref, whole_ref, sems = refs[3 * count + 1:]
+            copies = [pltpu.make_async_copy(new_ref.at[i], whole_ref.at[x], sems.at[i]) for i, x in enumerate(cells)]
+        for copy in copies:
+            copy.start()
+        me = lax.axis_index("trait")
+        values = [rows_of(block) for block in blocks]
+        for k in range(2):
+            part_ref[k] = blocks_dot(values, k_ref, k, [me, me ^ 1, me ^ 2])
+        for copy in copies:
+            copy.wait()
+
+    args = [*own, *sib, *far, kernels]
+    outs = [pltpu.VMEM((2, rows, owned), F32)]
+    if new is None:
+        return call(body, "early_part", args, outs, gflop=20.0)[0]
+    outs.append(jax.ShapeDtypeStruct((xcount, *new.shape[1:]), F32))
+    return call(
+        body, "early_part", [*args, new], outs, scratch=[pltpu.SemaphoreType.DMA((len(cells),))],
+        out_specs=[SPEC, ANYWHERE], gflop=20.0,
+    )
 
 
 def first_node(part, last, base, one, two, initial, kernels, death, cells, with_faces):
     xcount, ycount, owned = one.shape
     rows = len(cells) * ycount
-
-    def body(part_ref, last_ref, base_ref, one_ref, two_ref, init_ref, k_ref, d_ref, *refs):
+    count = len(last)
+
+    def body(*refs):
+        last_refs = refs[:count]
+        part_ref, base_ref, one_ref, two_ref, init_ref, k_ref, d_ref = refs[count:count + 7]
+        refs = refs[count + 7:]
         new_ref, rounded_ref, rest_ref = refs[:3]
         sums = refs[-1]
         me = lax.axis_index("trait")
         for k in range(2):
-            far_part = blocks_dot([last_ref[...].reshape(2 * rows, owned)], k_ref, k, [me ^ 3])
+            far_part = blocks_dot([rows_of(last_refs)], k_ref, k, [me ^ 3])
             sums[k] = (part_ref[k] + far_part).astype(BF16)
         death = d_ref[...]
         inv_one = 1.0 / (1.0 + FIRST * death)
@@ -169,28 +218,34 @@
     ]
     if with_faces:
         outs += [pltpu.VMEM((1, ycount, owned), BF16)] * 2
-    args = [part, last, base, one, two, initial, kernels, death]
+    args = [*last, part, base, one, two, initial, kernels, death]
     return call(
         body, "first_node", args, outs, scratch=[pltpu.VMEM((2, 2 * rows, owned), BF16)],
         gflop=0.0,
     )
 
 
-def before_second(news, rests, growth, death, chunks):
+def before_second(news, rests, growth, death, begun, blocks, kernels, chunks):
     _, ycount, owned = news[0].shape
+    rows = blocks[0].shape[1]
     xcount = sum(len(cells) for cells in chunks)
     count = len(chunks)
+    size = len(blocks)
     place = {x: (c, i) for c, cells in enumerate(chunks) for i, x in enumerate(cells)}
 
     def body(*refs):
-        new_refs, rest_refs = refs[:count], refs[count:2 * count]
-        g_ref, d_ref, whole_ref = refs[2 * count:2 * count + 3]
-        base_refs, sems = refs[2 * count + 3:-1], refs[-1]
+        new_refs, rest_refs, block_refs = refs[:count], refs[count:2 * count], refs[2 * count:2 * count + size]
+        k_ref, g_ref, d_ref, _, whole_ref, part_ref = refs[2 * count + size:2 * count + size + 6]
+        base_refs, sems = refs[2 * count + size + 6:-1], refs[-1]
         copies = [
-            pltpu.make_async_copy(new_refs[c].at[i], whole_ref.at[x], sems.at[x]) for x, (c, i) in place.items()
+            pltpu.make_async_copy(new_refs[-1].at[i], whole_ref.at[x], sems.at[i]) for i, x in enumerate(chunks[-1])
         ]
         for copy in copies:
             copy.start()
+        me = lax.axis_index("trait")
+        values = [r[...].reshape(rows, owned) for r in block_refs]
+        for k in range(2):
+            part_ref[k] = blocks_dot(values, k_ref, k, [me ^ j for j in range(size)])
         growth = g_ref[...]
         factor = SECOND / (1.0 + SECOND * d_ref[...])
         for x, (c, i) in place.items():
@@ -203,26 +258,26 @@
         for copy in copies:
             copy.wait()
 
-    outs = [jax.ShapeDtypeStruct((xcount, ycount, owned), F32)]
+    outs = [jax.ShapeDtypeStruct((xcount, ycount, owned), F32), pltpu.VMEM((2, rows, owned), F32)]
     outs += [pltpu.VMEM((len(cells), ycount, owned), F32) for cells in chunks]
-    return call(
-        body, "before_second", [*news, *rests, growth, death], outs, scratch=[pltpu.SemaphoreType.DMA((xcount,))],
-        out_specs=[ANYWHERE] + [SPEC] * count, gflop=20.0,
-    )
-
-
-def whole_sums(blocks, kernels):
+    args = [*news, *rests, *blocks, kernels, growth, death, begun]
+    return call(
+        body, "before_second", args, outs, scratch=[pltpu.SemaphoreType.DMA((len(chunks[-1]),))],
+        specs=[SPEC] * (len(args) - 1) + [FROM_HBM], out_specs=[ANYWHERE] + [SPEC] * (len(outs) - 1), gflop=20.0,
+        alias={len(args) - 1: 0},
+    )
+
+
+def whole_sums(part, blocks, kernels):
     rows, owned = blocks[0].shape[1:]
-    count = len(blocks)
-
-    def body(*refs):
-        block_refs, k_ref, sums_ref = refs[:count], refs[count], refs[count + 1]
-        me = lax.axis_index("trait")
-        values = [r[...].reshape(rows, owned) for r in block_refs]
-        for k in range(2):
-            sums_ref[k] = blocks_dot(values, k_ref, k, [me ^ j for j in range(count)]).astype(BF16)
-
-    return call(body, "whole_sums", [*blocks, kernels], [pltpu.VMEM((2, rows, owned), BF16)])[0]
+
+    def body(part_ref, sib_ref, far_ref, farsib_ref, k_ref, sums_ref):
+        me = lax.axis_index("trait")
+        values = [r[...].reshape(rows, owned) for r in (sib_ref, far_ref, farsib_ref)]
+        for k in range(2):
+            sums_ref[k] = (part_ref[k] + blocks_dot(values, k_ref, k, [me ^ 1, me ^ 2, me ^ 3])).astype(BF16)
+
+    return call(body, "whole_sums", [part, *blocks, kernels], [pltpu.VMEM((2, rows, owned), BF16)])[0]
 
 
 def finish(cells, ycount, sums, base_ref, new_ref, factor, faces, held, out_ref, sems):
@@ -307,18 +362,20 @@
         hi = lax.ppermute(head, "gx", [((i + 1) % gcount, i) for i in range(gcount)])
         return lo, hi
 
-    own_a, head, tail = round_chunk((section_one, section_two), chunks[0], True)
-    far_a = to_far(own_a)
-    own_b = round_chunk((after(section_one, own_a), section_two), chunks[1], False)[0]
+    own_a = [round_field(section_one, chunks[0])]
+    far_a = [to_far(own_a[0])]
+    own_a.append(round_field(after(section_two, own_a[0]), chunks[0]))
+    far_a.append(to_far(own_a[1]))
+    own_b, head, tail = round_rest((after(section_one, own_a[1]), section_two), chunks)
     far_b = to_far(own_b)
-    head, tail, kernels = lax.optimization_barrier((head, tail, kernels, own_b))[:3]
+    kernels = after(kernels, own_b)
     lo, hi = faces(head, tail)
     base_a, base_b = before_first(section_one, section_two, lo, hi, growth, chunks)
-    sib_a = to_sibling(after(own_a, own_b))
+    sib_a = [to_sibling(v) for v in lax.optimization_barrier((*own_a, own_b))[:-1]]
     sib_b = to_sibling(own_b)
-    far_a = after(far_a, base_a)
-    farsib_a = to_sibling(far_a)
-    part_a = early_part([own_a, sib_a, far_a], kernels)
+    far_a = list(lax.optimization_barrier((*far_a, base_a))[:-1])
+    farsib_a = [to_sibling(v) for v in far_a]
+    part_a = early_part(own_a, sib_a, far_a, kernels)
     new_a, rounded_a, rest_a, new_head, new_tail = first_node(
         part_a, farsib_a, base_a, section_one, section_two, initial, kernels, death, chunks[0], True
     )
@@ -327,17 +384,19 @@
 
     far_b = after(far_b, rounded_a)
     farsib_b = to_sibling(far_b)
-    part_b = early_part([own_b, sib_b, far_b], kernels)
+    part_b, new_one = early_part([own_b], [sib_b], [far_b], kernels, new_a, chunks[0], xcount)
     new_b, rounded_b, rest_b = first_node(
-        part_b, farsib_b, base_b, section_one, section_two, initial, kernels, death, chunks[1], False
+        part_b, [farsib_b], base_b, section_one, section_two, initial, kernels, death, chunks[1], False
     )
     nfar_b = to_far(rounded_b)
     nsib_b = to_sibling(rounded_b)
     new_lo, new_hi = faces(*lax.optimization_barrier((new_head, new_tail, rounded_b))[:2])
     nfar_a = after(nfar_a, rounded_b)
     nfarsib_a = to_sibling(nfar_a)
-    new_one, nbase_a, nbase_b = before_second((new_a, new_b), (rest_a, rest_b), growth, death, chunks)
-    sums_a = whole_sums([rounded_a, nsib_a, nfar_a, nfarsib_a], after(kernels, nbase_a))
+    new_one, npart_a, nbase_a, nbase_b = before_second(
+        (new_a, new_b), (rest_a, rest_b), growth, death, new_one, [rounded_a], kernels, chunks
+    )
+    sums_a = whole_sums(npart_a, [nsib_a, nfar_a, nfarsib_a], after(kernels, nbase_a))
     nfar_b = after(nfar_b, sums_a, new_lo, new_hi)
     nfarsib_b = to_sibling(nfar_b)
     begun, npart_b = second_first(

time: 43.6 us -> 46.2 us (1.060)
  waiting for transfers between devices: 13.1 us -> 14.7 us
  Pallas kernels: 11.5 us -> 12.7 us
    ppermute x4 -> x5, waiting for transfers between devices: 6.52 us -> 3.02 us  [to_far(): return lax.ppermute(v, 'trait', [(i, i ^ 2) for i in range(traits)])]
    ppermute x2, waiting for transfers between devices: 3.58 us -> 6.78 us  [faces(): lax.ppermute(tail, 'gx', [(i, (i + 1) % gcount) for i in range(gcount)])]
    ppermute x2, waiting for transfers between devices: 1.13 us -> 3.23 us  [faces(): lax.ppermute(head, 'gx', [((i + 1) % gcount, i) for i in range(gcount)])]
    pallas_call x11 -> x12, Pallas kernels: 11.5 us -> 12.7 us  [call(): pl.pallas_call(body, out_shape=outs, in_specs=specs, out_specs=out_specs...]
    ppermute x8 -> x10, starting transfers between devices: 0.86 us -> 2 us  [to_sibling(): return lax.ppermute(v, 'trait', [(i, i ^ 1) for i in range(traits)])]
    ppermute x2, starting transfers between devices: 3.03 us -> 2.04 us  [faces(): lax.ppermute(tail, 'gx', [(i, (i + 1) % gcount) for i in range(gcount)])]
    ppermute x4 -> x5, starting transfers between devices: 7.71 us -> 7.38 us  [to_far(): return lax.ppermute(v, 'trait', [(i, i ^ 2) for i in range(traits)])]
    ppermute x8 -> x10, waiting for transfers between devices: 1.84 us -> 1.66 us  [to_sibling(): return lax.ppermute(v, 'trait', [(i, i ^ 1) for i in range(traits)])]
  transfers between devices with their start and end apart: 16 -> 19, of which waited for: 6 -> 8; matrix products, arithmetic and copies ran while one was open for 0% -> 0% of each run, Pallas kernels for 21% -> 23%
where the time goes in v2:
time: 46.2 us; the launch traced here: 46 us
  starting transfers between devices  17.7 us (38%)
  waiting for transfers between devices  14.7 us (32%)
  Pallas kernels  12.7 us (27%)
  between operations  0.85 us (2%)
    pallas_call x12, Pallas kernels, call(): pl.pallas_call(body, out_shape=outs, in_specs=specs, out_specs=out_specs...  12.7 us
    ppermute x5, starting transfers between devices, to_far(): return lax.ppermute(v, 'trait', [(i, i ^ 2) for i in range(traits)])  7.38 us
    ppermute x2, waiting for transfers between devices, faces(): lax.ppermute(tail, 'gx', [(i, (i + 1) % gcount) for i in range(gcount)])  6.78 us
    ppermute x2, starting transfers between devices, faces(): lax.ppermute(head, 'gx', [((i + 1) % gcount, i) for i in range(gcount)])  6.32 us
    ppermute x2, waiting for transfers between devices, faces(): lax.ppermute(head, 'gx', [((i + 1) % gcount, i) for i in range(gcount)])  3.23 us
    ppermute x5, waiting for transfers between devices, to_far(): return lax.ppermute(v, 'trait', [(i, i ^ 2) for i in range(traits)])  3.02 us
    ppermute x2, starting transfers between devices, faces(): lax.ppermute(tail, 'gx', [(i, (i + 1) % gcount) for i in range(gcount)])  2.04 us
    ppermute x10, starting transfers between devices, to_sibling(): return lax.ppermute(v, 'trait', [(i, i ^ 1) for i in range(traits)])  2 us
  transfers between devices with their start and end apart: 19, of which 8 were waited for; matrix products, arithmetic and copies ran while one was open for 0% of the time, Pallas kernels for 23%

profile of v2, /device:TPU:0, one launch (start us, length us, event | category | flops | bytes accessed | tf_op | source)
XLA Modules:
  0.0 46.0 jit_solution(8600385937274695180)
XLA Ops:
  0.6 1.2 %round_field.2.refs_0_ = bf16[1,640,256]{2,1,0:T(8,128)(2,1)S(1)} custom-call(f32[8,128,256]{2,1,0:T(8,128)} %refs_3_.2), custom_call_target="tpu_custom_call" | custom-call | tf_op jit(solution)/shard_map/round_field/pallas_call | solution.py:37
  1.9 0.0 copy-start
  1.9 0.0 copy-start.1
  1.9 0.0 copy-start.5
  1.9 3.0 %collective-permute-start = (bf16[1,640,256]{2,1,0:T(8,128)(2,1)S(1)}, bf16[1,640,256]{2,1,0:T(8,128)(2,1)S(1)}, u32[]{:S(2)}, u32[]{:S(2)}) collective-permute-start(bf16[1,640,256]{2,1,0:T(8,128)(2,1)S(1)} %round_field.2.refs_0_), channel_id=1, source_target_pairs={{0,2},{1,3},{2,0},{3,1},{4,6},{5,7},{6,4},{7,5},{8,10},{9,11},{10,... | collective-permute-start | bytes 983048 | tf_op jit(solution)/shard_map/ppermute | solution.py:358
  4.9 1.2 %round_field.3.refs_1_ = bf16[1,640,256]{2,1,0:T(8,128)(2,1)S(1)} custom-call(f32[8,128,256]{2,1,0:T(8,128)} %refs_4_.3), custom_call_target="tpu_custom_call" | custom-call | tf_op jit(solution)/shard_map/round_field/pallas_call | solution.py:37
  6.1 0.2 collective-permute-start.1
  6.3 1.5 %round_rest.1 = (bf16[2,384,256]{2,1,0:T(8,128)(2,1)S(1)}, bf16[2,128,256]{2,1,0:T(8,128)(2,1)S(1)}, bf16[2,128,256]{2,1,0:T(8,128)(2,1)S(1)}) custom-call(f32[8,128,256]{2,1,0:T(8,128)} %refs_3_.2, f32[8,128,256]{2,1,0:T(8,128)} %refs_4_.3), custom_call_target="tpu_custom_call" | custom-call | tf_op jit(solution)/shard_map/round_rest/pallas_call | solution.py:37
  7.8 0.0 copy-start.2
  7.8 0.1 collective-permute-start.6
  7.9 0.5 %collective-permute-start.7 = (bf16[1,640,256]{2,1,0:T(8,128)(2,1)S(1)}, bf16[1,640,256]{2,1,0:T(8,128)(2,1)S(1)}, u32[]{:S(2)}, u32[]{:S(2)}) collective-permute-start(bf16[1,640,256]{2,1,0:T(8,128)(2,1)S(1)} %round_field.3.refs_1_), channel_id=1, source_target_pairs={{0,1},{1,0},{2,3},{3,2},{4,5},{5,4},{6,7},{7,6},{8,9},{9,8},{10,11... | collective-permute-start | bytes 983048 | tf_op jit(solution)/shard_map/ppermute | solution.py:355
  8.4 1.9 %collective-permute-start.2 = (bf16[2,128,256]{2,1,0:T(8,128)(2,1)S(1)}, bf16[2,128,256]{2,1,0:T(8,128)(2,1)S(1)}, u32[]{:S(2)}, u32[]{:S(2)}) collective-permute-start(bf16[2,128,256]{2,1,0:T(8,128)(2,1)S(1)} %get-tuple-element.38), channel_id=1, source_target_pairs={{0,4},{4,8},{8,12},{12,16},{16,20},{20,24},{24,28},{28,0},{1,5},{5... | collective-permute-start | bytes 393224 | tf_op jit(solution)/shard_map/ppermute | solution.py:361
  10.3 6.8 %collective-permute-done.2.lo_ref = bf16[2,128,256]{2,1,0:T(8,128)(2,1)S(1)} collective-permute-done((bf16[2,128,256]{2,1,0:T(8,128)(2,1)S(1)}, bf16[2,128,256]{2,1,0:T(8,128)(2,1)S(1)}, u32[]{:S(2)}, u32[]{:S(2)}) %collective-permute-start.2) | collective-permute-done | bytes 131104 | tf_op jit(solution)/shard_map/ppermute | solution.py:361
  17.1 1.7 %collective-permute-start.3 = (bf16[2,128,256]{2,1,0:T(8,128)(2,1)S(1)}, bf16[2,128,256]{2,1,0:T(8,128)(2,1)S(1)}, u32[]{:S(2)}, u32[]{:S(2)}) collective-permute-start(bf16[2,128,256]{2,1,0:T(8,128)(2,1)S(1)} %get-tuple-element.39), channel_id=1, source_target_pairs={{4,0},{8,4},{12,8},{16,12},{20,16},{24,20},{28,24},{0,28},{5,1},{9... | collective-permute-start | bytes 393224 | tf_op jit(solution)/shard_map/ppermute | solution.py:362
  18.8 3.2 %collective-permute-done.3.hi_ref = bf16[2,128,256]{2,1,0:T(8,128)(2,1)S(1)} collective-permute-done((bf16[2,128,256]{2,1,0:T(8,128)(2,1)S(1)}, bf16[2,128,256]{2,1,0:T(8,128)(2,1)S(1)}, u32[]{:S(2)}, u32[]{:S(2)}) %collective-permute-start.3) | collective-permute-done | bytes 131104 | tf_op jit(solution)/shard_map/ppermute | solution.py:362
  22.0 1.5 %collective-permute-start.8 = (bf16[2,384,256]{2,1,0:T(8,128)(2,1)S(1)}, bf16[2,384,256]{2,1,0:T(8,128)(2,1)S(1)}, u32[]{:S(2)}, u32[]{:S(2)}) collective-permute-start(bf16[2,384,256]{2,1,0:T(8,128)(2,1)S(1)} %get-tuple-element.43.refs_0_), channel_id=1, source_target_pairs={{0,2},{1,3},{2,0},{3,1},{4,6},{5,7},{6,4},{7,5},{8,10},{9,11},{10,... | collective-permute-start | bytes 1179656 | tf_op jit(solution)/shard_map/ppermute | solution.py:358
  23.5 0.9 %before_first.1 = (f32[2,5,128,256]{3,2,1,0:T(8,128)S(1)}, f32[2,3,128,256]{3,2,1,0:T(8,128)S(1)}) custom-call(f32[8,128,256]{2,1,0:T(8,128)S(1)} %copy-done, f32[8,128,256]{2,1,0:T(8,128)S(1)} %copy-done.1, bf16[2,128,256]{2,1,0:T(8,128)(2,1)S(1)} %collective-permute-done.2.lo_ref, bf16[2,128,256]{2,1,0:T(8,128)(2,1)S(1)} %collective-permute-done.3.hi_ref, ...), custom_call_target="tpu_custom_call" | custom-call | tf_op jit(solution)/shard_map/before_first/pallas_call | solution.py:37
  24.4 0.0 collective-permute-done.1.refs_5_
  24.4 0.1 collective-permute-start.10
  24.5 0.0 collective-permute-done.refs_4_
  24.5 0.0 copy-start.3
  24.6 0.0 copy-start.4
  24.6 0.5 %collective-permute-start.4 = (bf16[1,640,256]{2,1,0:T(8,128)(2,1)S(1)}, bf16[1,640,256]{2,1,0:T(8,128)(2,1)S(1)}, u32[]{:S(2)}, u32[]{:S(2)}) collective-permute-start(bf16[1,640,256]{2,1,0:T(8,128)(2,1)S(1)} %collective-permute-done.refs_4_), channel_id=1, source_target_pairs={{0,1},{1,0},{2,3},{3,2},{4,5},{5,4},{6,7},{7,6},{8,9},{9,8},{10,11... | collective-permute-start | bytes 983048 | tf_op jit(solution)/shard_map/ppermute | solution.py:355
  25.0 0.0 collective-permute-done.6.refs_2_
  25.0 0.1 collective-permute-start.5
  25.1 1.2 %early_part.2.refs_2_ = f32[2,1280,256]{2,1,0:T(8,128)S(1)} custom-call(bf16[1,640,256]{2,1,0:T(8,128)(2,1)S(1)} %round_field.2.refs_0_, bf16[1,640,256]{2,1,0:T(8,128)(2,1)S(1)} %round_field.3.refs_1_, bf16[1,640,256]{2,1,0:T(8,128)(2,1)S(1)} %collective-permute-done.6.refs_2_, bf16[1,640,256]{2,1,0:T(8,128)(2,1)S(1)} %collective-permute-done.7.refs_3_, ...), custom_call_target="tpu_custom_call" | custom-call | flops 20000000000 | tf_op jit(solution)/shard_map/early_part/pallas_call | solution.py:37
  26.3 0.4 collective-permute-done.4.refs_0_
  26.7 0.5 %collective-permute-done.5.refs_1_ = bf16[1,640,256]{2,1,0:T(8,128)(2,1)S(1)} collective-permute-done((bf16[1,640,256]{2,1,0:T(8,128)(2,1)S(1)}, bf16[1,640,256]{2,1,0:T(8,128)(2,1)S(1)}, u32[]{:S(2)}, u32[]{:S(2)}) %collective-permute-start.5) | collective-permute-done | bytes 327712 | tf_op jit(solution)/shard_map/ppermute | solution.py:355
  27.2 1.0 %first_node.2 = (f32[5,128,256]{2,1,0:T(8,128)S(1)}, bf16[1,640,256]{2,1,0:T(8,128)(2,1)S(1)}, f32[5,128,256]{2,1,0:T(8,128)S(1)}, bf16[1,128,256]{2,1,0:T(8,128)(2,1)S(1)}, bf16[1,128,256]{2,1,0:T(8,128)(2,1)S(1)}) custom-call(bf16[1,640,256]{2,1,0:T(8,128)(2,1)S(1)} %collective-permute-done.4.refs_0_, ...), custom_call_target="tpu_custom_call" | custom-call | tf_op jit(solution)/shard_map/first_node/pallas_call | solution.py:37
  28.2 0.6 %collective-permute-start.12 = (bf16[1,640,256]{2,1,0:T(8,128)(2,1)S(1)}, bf16[1,640,256]{2,1,0:T(8,128)(2,1)S(1)}, u32[]{:S(2)}, u32[]{:S(2)}) collective-permute-start(bf16[1,640,256]{2,1,0:T(8,128)(2,1)S(1)} %get-tuple-element.48.refs_4_), channel_id=1, source_target_pairs={{0,2},{1,3},{2,0},{3,1},{4,6},{5,7},{6,4},{7,5},{8,10},{9,11},{10,... | collective-permute-start | bytes 983048 | tf_op jit(solution)/shard_map/ppermute | solution.py:358
  28.8 0.0 collective-permute-start.11
  28.8 3.0 %collective-permute-done.8.refs_2_ = bf16[2,384,256]{2,1,0:T(8,128)(2,1)S(1)} collective-permute-done((bf16[2,384,256]{2,1,0:T(8,128)(2,1)S(1)}, bf16[2,384,256]{2,1,0:T(8,128)(2,1)S(1)}, u32[]{:S(2)}, u32[]{:S(2)}) %collective-permute-start.8) | collective-permute-done | bytes 393248 | tf_op jit(solution)/shard_map/ppermute | solution.py:358
  31.8 0.0 collective-permute-start.9
  31.8 0.0 collective-permute-done.10.refs_1_
  31.8 1.0 %early_part.3 = (f32[2,768,256]{2,1,0:T(8,128)S(1)}, f32[8,128,256]{2,1,0:T(8,128)}) custom-call(bf16[2,384,256]{2,1,0:T(8,128)(2,1)S(1)} %get-tuple-element.43.refs_0_, bf16[2,384,256]{2,1,0:T(8,128)(2,1)S(1)} %collective-permute-done.10.refs_1_, bf16[2,384,256]{2,1,0:T(8,128)(2,1)S(1)} %collective-permute-done.8.refs_2_, ...), custom_call_target="tpu_custom_call" | custom-call | flops 20000000000 | tf_op jit(solution)/shard_map/early_part/pallas_call | solution.py:37
  32.9 0.7 %collective-permute-done.9.refs_0_ = bf16[2,384,256]{2,1,0:T(8,128)(2,1)S(1)} collective-permute-done((bf16[2,384,256]{2,1,0:T(8,128)(2,1)S(1)}, bf16[2,384,256]{2,1,0:T(8,128)(2,1)S(1)}, u32[]{:S(2)}, u32[]{:S(2)}) %collective-permute-start.9) | collective-permute-done | bytes 393248 | tf_op jit(solution)/shard_map/ppermute | solution.py:355
  33.6 0.7 %first_node.3 = (f32[3,128,256]{2,1,0:T(8,128)S(1)}, bf16[1,384,256]{2,1,0:T(8,128)(2,1)S(1)}, f32[3,128,256]{2,1,0:T(8,128)S(1)}) custom-call(bf16[2,384,256]{2,1,0:T(8,128)(2,1)S(1)} %collective-permute-done.9.refs_0_, f32[2,768,256]{2,1,0:T(8,128)S(1)} %get-tuple-element.50.refs_1_, f32[2,3,128,256]{3,2,1,0:T(8,128)S(1)} %get-tuple-element.51.refs_2_, ...), custom_call_target="tpu_custom_call" | custom-call | tf_op jit(solution)/shard_map/first_node/pallas_call | solution.py:37
  34.3 2.1 %collective-permute-start.17 = (bf16[1,384,256]{2,1,0:T(8,128)(2,1)S(1)}, bf16[1,384,256]{2,1,0:T(8,128)(2,1)S(1)}, u32[]{:S(2)}, u32[]{:S(2)}) collective-permute-start(bf16[1,384,256]{2,1,0:T(8,128)(2,1)S(1)} %get-tuple-element.58.refs_0_), channel_id=1, source_target_pairs={{0,2},{1,3},{2,0},{3,1},{4,6},{5,7},{6,4},{7,5},{8,10},{9,11},{10,... | collective-permute-start | bytes 589832 | tf_op jit(solution)/shard_map/ppermute | solution.py:358
  36.3 0.1 collective-permute-start.14
  36.5 4.6 %collective-permute-start.15 = (bf16[1,128,256]{2,1,0:T(8,128)(2,1)S(1)}, bf16[1,128,256]{2,1,0:T(8,128)(2,1)S(1)}, u32[]{:S(2)}, u32[]{:S(2)}) collective-permute-start(bf16[1,128,256]{2,1,0:T(8,128)(2,1)S(1)} %get-tuple-element.65), channel_id=1, source_target_pairs={{4,0},{8,4},{12,8},{16,12},{20,16},{24,20},{28,24},{0,28},{5,1},{9... | collective-permute-start | bytes 196616 | tf_op jit(solution)/shard_map/ppermute | solution.py:362
  41.0 1.0 %before_second.1 = (f32[8,128,256]{2,1,0:T(8,128)}, f32[2,640,256]{2,1,0:T(8,128)S(1)}, f32[5,128,256]{2,1,0:T(8,128)S(1)}, f32[3,128,256]{2,1,0:T(8,128)S(1)}) custom-call(f32[5,128,256]{2,1,0:T(8,128)S(1)} %get-tuple-element.47.refs_4_.refs_0_.new_ref, f32[3,128,256]{2,1,0:T(8,128)S(1)} %get-tuple-element.52.refs_1_.new_ref, ...), custom_call_target="tpu_custom_call", output_to_operand_aliasing={{0}: (8, {})} | custom-call | flops 20000000000 | tf_op jit(solution)/shard_map/before_second/pallas_call | solution.py:37
  42.0 0.6 %collective-permute-start.16 = (bf16[1,384,256]{2,1,0:T(8,128)(2,1)S(1)}, bf16[1,384,256]{2,1,0:T(8,128)(2,1)S(1)}, u32[]{:S(2)}, u32[]{:S(2)}) collective-permute-start(bf16[1,384,256]{2,1,0:T(8,128)(2,1)S(1)} %get-tuple-element.58.refs_0_), channel_id=1, source_target_pairs={{0,1},{1,0},{2,3},{3,2},{4,5},{5,4},{6,7},{7,6},{8,9},{9,8},{10,11... | collective-permute-start | bytes 589832 | tf_op jit(solution)/shard_map/ppermute | solution.py:355
  42.6 0.1 collective-permute-done.13.farsib_ref
  42.7 0.7 %whole_sums.1.sums_ref = bf16[2,640,256]{2,1,0:T(8,128)(2,1)S(1)} custom-call(f32[2,640,256]{2,1,0:T(8,128)S(1)} %get-tuple-element.57.part_ref, bf16[1,640,256]{2,1,0:T(8,128)(2,1)S(1)} %collective-permute-done.11.sib_ref, bf16[1,640,256]{2,1,0:T(8,128)(2,1)S(1)} %collective-permute-done.12.far_ref, ...), custom_call_target="tpu_custom_call" | custom-call | tf_op jit(solution)/shard_map/whole_sums/pallas_call | solution.py:37
  43.4 0.2 collective-permute-start.18
  43.6 0.1 collective-permute-done.16.refs_1_
  43.7 1.3 %second_first.1 = (f32[8,128,256]{2,1,0:T(8,128)}, f32[2,384,256]{2,1,0:T(8,128)S(1)}) custom-call(bf16[2,640,256]{2,1,0:T(8,128)(2,1)S(1)} %whole_sums.1.sums_ref, f32[5,128,256]{2,1,0:T(8,128)S(1)} %get-tuple-element.60.base_ref, f32[5,128,256]{2,1,0:T(8,128)S(1)} %get-tuple-element.47.refs_4_.refs_0_.new_ref, f32[1,256]{1,0:T(1,128)S(1)} %bitcast.5, ...), custom_call_target="tpu_custom_call" | custom-call | tf_op jit(solution)/shard_map/second_first/pallas_call | solution.py:37
  45.0 1.0 %second_last.1 = f32[8,128,256]{2,1,0:T(8,128)} custom-call(f32[2,384,256]{2,1,0:T(8,128)S(1)} %get-tuple-element.67.part_ref, bf16[1,384,256]{2,1,0:T(8,128)(2,1)S(1)} %collective-permute-done.18.last_ref, f32[3,128,256]{2,1,0:T(8,128)S(1)} %get-tuple-element.68.base_ref, ...), custom_call_target="tpu_custom_call", output_to_operand_aliasing={{}: (6, {})} | custom-call | tf_op jit(solution)/shard_map/second_last/pallas_call | solution.py:37
  (14 shorter events, 0.0 us)
Async XLA Ops:
  1.9 21.7 %copy-start = (f32[8,128,256]{2,1,0:T(8,128)S(1)}, f32[8,128,256]{2,1,0:T(8,128)}, u32[]{:S(2)}) copy-start(f32[8,128,256]{2,1,0:T(8,128)} %refs_3_.2) | copy-start | bytes 3145732
  1.9 21.7 %copy-start.1 = (f32[8,128,256]{2,1,0:T(8,128)S(1)}, f32[8,128,256]{2,1,0:T(8,128)}, u32[]{:S(2)}) copy-start(f32[8,128,256]{2,1,0:T(8,128)} %refs_4_.3) | copy-start | bytes 3145732
  1.9 21.6 %copy-start.5 = (f32[256]{0:T(256)S(1)}, f32[256]{0:T(256)}, u32[]{:S(2)}) copy-start(f32[256]{0:T(256)} %param.10) | copy-start | bytes 3076
  1.9 22.6 %collective-permute-start = (bf16[1,640,256]{2,1,0:T(8,128)(2,1)S(1)}, bf16[1,640,256]{2,1,0:T(8,128)(2,1)S(1)}, u32[]{:S(2)}, u32[]{:S(2)}) collective-permute-start(bf16[1,640,256]{2,1,0:T(8,128)(2,1)S(1)} %round_field.2.refs_0_), channel_id=1, source_target_pairs={{0,2},{1,3},{2,0},{3,1},{4,6},{5,7},{6,4},{7,5},{8,10},{9,11},{10,... | collective-permute-start | bytes 983048 | tf_op jit(solution)/shard_map/ppermute | solution.py:358
  6.1 18.3 %collective-permute-start.1 = (bf16[1,640,256]{2,1,0:T(8,128)(2,1)S(1)}, bf16[1,640,256]{2,1,0:T(8,128)(2,1)S(1)}, u32[]{:S(2)}, u32[]{:S(2)}) collective-permute-start(bf16[1,640,256]{2,1,0:T(8,128)(2,1)S(1)} %round_field.3.refs_1_), channel_id=1, source_target_pairs={{0,2},{1,3},{2,0},{3,1},{4,6},{5,7},{6,4},{7,5},{8,10},{9,11},{10,... | collective-permute-start | bytes 983048 | tf_op jit(solution)/shard_map/ppermute | solution.py:358
  7.8 17.3 %copy-start.2 = (bf16[2,1024,256]{2,1,0:T(8,128)(2,1)S(1)}, bf16[2,1024,256]{2,1,0:T(8,128)(2,1)}, u32[]{:S(2)}) copy-start(bf16[2,1024,256]{2,1,0:T(8,128)(2,1)} %k_ref.2) | copy-start | bytes 3145732
  7.8 17.2 %collective-permute-start.6 = (bf16[1,640,256]{2,1,0:T(8,128)(2,1)S(1)}, bf16[1,640,256]{2,1,0:T(8,128)(2,1)S(1)}, u32[]{:S(2)}, u32[]{:S(2)}) collective-permute-start(bf16[1,640,256]{2,1,0:T(8,128)(2,1)S(1)} %round_field.2.refs_0_), channel_id=1, source_target_pairs={{0,1},{1,0},{2,3},{3,2},{4,5},{5,4},{6,7},{7,6},{8,9},{9,8},{10,11... | collective-permute-start | bytes 983048 | tf_op jit(solution)/shard_map/ppermute | solution.py:355
  7.9 17.2 %collective-permute-start.7 = (bf16[1,640,256]{2,1,0:T(8,128)(2,1)S(1)}, bf16[1,640,256]{2,1,0:T(8,128)(2,1)S(1)}, u32[]{:S(2)}, u32[]{:S(2)}) collective-permute-start(bf16[1,640,256]{2,1,0:T(8,128)(2,1)S(1)} %round_field.3.refs_1_), channel_id=1, source_target_pairs={{0,1},{1,0},{2,3},{3,2},{4,5},{5,4},{6,7},{7,6},{8,9},{9,8},{10,11... | collective-permute-start | bytes 983048 | tf_op jit(solution)/shard_map/ppermute | solution.py:355
  8.4 8.7 %collective-permute-start.2 = (bf16[2,128,256]{2,1,0:T(8,128)(2,1)S(1)}, bf16[2,128,256]{2,1,0:T(8,128)(2,1)S(1)}, u32[]{:S(2)}, u32[]{:S(2)}) collective-permute-start(bf16[2,128,256]{2,1,0:T(8,128)(2,1)S(1)} %get-tuple-element.38), channel_id=1, source_target_pairs={{0,4},{4,8},{8,12},{12,16},{16,20},{20,24},{24,28},{28,0},{1,5},{5... | collective-permute-start | bytes 393224 | tf_op jit(solution)/shard_map/ppermute | solution.py:361
  17.1 5.0 %collective-permute-start.3 = (bf16[2,128,256]{2,1,0:T(8,128)(2,1)S(1)}, bf16[2,128,256]{2,1,0:T(8,128)(2,1)S(1)}, u32[]{:S(2)}, u32[]{:S(2)}) collective-permute-start(bf16[2,128,256]{2,1,0:T(8,128)(2,1)S(1)} %get-tuple-element.39), channel_id=1, source_target_pairs={{4,0},{8,4},{12,8},{16,12},{20,16},{24,20},{28,24},{0,28},{5,1},{9... | collective-permute-start | bytes 393224 | tf_op jit(solution)/shard_map/ppermute | solution.py:362
  22.0 9.8 %collective-permute-start.8 = (bf16[2,384,256]{2,1,0:T(8,128)(2,1)S(1)}, bf16[2,384,256]{2,1,0:T(8,128)(2,1)S(1)}, u32[]{:S(2)}, u32[]{:S(2)}) collective-permute-start(bf16[2,384,256]{2,1,0:T(8,128)(2,1)S(1)} %get-tuple-element.43.refs_0_), channel_id=1, source_target_pairs={{0,2},{1,3},{2,0},{3,1},{4,6},{5,7},{6,4},{7,5},{8,10},{9,11},{10,... | collective-permute-start | bytes 1179656 | tf_op jit(solution)/shard_map/ppermute | solution.py:358
  24.4 7.4 %collective-permute-start.10 = (bf16[2,384,256]{2,1,0:T(8,128)(2,1)S(1)}, bf16[2,384,256]{2,1,0:T(8,128)(2,1)S(1)}, u32[]{:S(2)}, u32[]{:S(2)}) collective-permute-start(bf16[2,384,256]{2,1,0:T(8,128)(2,1)S(1)} %get-tuple-element.43.refs_0_), channel_id=1, source_target_pairs={{0,1},{1,0},{2,3},{3,2},{4,5},{5,4},{6,7},{7,6},{8,9},{9,8},{10,11... | collective-permute-start | bytes 1179656 | tf_op jit(solution)/shard_map/ppermute | solution.py:355
  24.5 2.6 %copy-start.3 = (f32[8,128,256]{2,1,0:T(8,128)S(1)}, f32[8,128,256]{2,1,0:T(8,128)}, u32[]{:S(2)}) copy-start(f32[8,128,256]{2,1,0:T(8,128)} %refs_5_.3) | copy-start | bytes 3145732
  24.6 2.6 %copy-start.4 = (f32[256]{0:T(256)S(1)}, f32[256]{0:T(256)}, u32[]{:S(2)}) copy-start(f32[256]{0:T(256)} %param.11) | copy-start | bytes 3076
  24.6 2.1 %collective-permute-start.4 = (bf16[1,640,256]{2,1,0:T(8,128)(2,1)S(1)}, bf16[1,640,256]{2,1,0:T(8,128)(2,1)S(1)}, u32[]{:S(2)}, u32[]{:S(2)}) collective-permute-start(bf16[1,640,256]{2,1,0:T(8,128)(2,1)S(1)} %collective-permute-done.refs_4_), channel_id=1, source_target_pairs={{0,1},{1,0},{2,3},{3,2},{4,5},{5,4},{6,7},{7,6},{8,9},{9,8},{10,11... | collective-permute-start | bytes 983048 | tf_op jit(solution)/shard_map/ppermute | solution.py:355
  25.0 2.1 %collective-permute-start.5 = (bf16[1,640,256]{2,1,0:T(8,128)(2,1)S(1)}, bf16[1,640,256]{2,1,0:T(8,128)(2,1)S(1)}, u32[]{:S(2)}, u32[]{:S(2)}) collective-permute-start(bf16[1,640,256]{2,1,0:T(8,128)(2,1)S(1)} %collective-permute-done.1.refs_5_), channel_id=1, source_target_pairs={{0,1},{1,0},{2,3},{3,2},{4,5},{5,4},{6,7},{7,6},{8,9},{9,8},{10,11... | collective-permute-start | bytes 983048 | tf_op jit(solution)/shard_map/ppermute | solution.py:355
  28.2 12.8 %collective-permute-start.12 = (bf16[1,640,256]{2,1,0:T(8,128)(2,1)S(1)}, bf16[1,640,256]{2,1,0:T(8,128)(2,1)S(1)}, u32[]{:S(2)}, u32[]{:S(2)}) collective-permute-start(bf16[1,640,256]{2,1,0:T(8,128)(2,1)S(1)} %get-tuple-element.48.refs_4_), channel_id=1, source_target_pairs={{0,2},{1,3},{2,0},{3,1},{4,6},{5,7},{6,4},{7,5},{8,10},{9,11},{10,... | collective-permute-start | bytes 983048 | tf_op jit(solution)/shard_map/ppermute | solution.py:358
  28.8 13.2 %collective-permute-start.11 = (bf16[1,640,256]{2,1,0:T(8,128)(2,1)S(1)}, bf16[1,640,256]{2,1,0:T(8,128)(2,1)S(1)}, u32[]{:S(2)}, u32[]{:S(2)}) collective-permute-start(bf16[1,640,256]{2,1,0:T(8,128)(2,1)S(1)} %get-tuple-element.48.refs_4_), channel_id=1, source_target_pairs={{0,1},{1,0},{2,3},{3,2},{4,5},{5,4},{6,7},{7,6},{8,9},{9,8},{10,11... | collective-permute-start | bytes 983048 | tf_op jit(solution)/shard_map/ppermute | solution.py:355
  31.8 1.7 %collective-permute-start.9 = (bf16[2,384,256]{2,1,0:T(8,128)(2,1)S(1)}, bf16[2,384,256]{2,1,0:T(8,128)(2,1)S(1)}, u32[]{:S(2)}, u32[]{:S(2)}) collective-permute-start(bf16[2,384,256]{2,1,0:T(8,128)(2,1)S(1)} %collective-permute-done.8.refs_2_), channel_id=1, source_target_pairs={{0,1},{1,0},{2,3},{3,2},{4,5},{5,4},{6,7},{7,6},{8,9},{9,8},{10,11... | collective-permute-start | bytes 1179656 | tf_op jit(solution)/shard_map/ppermute | solution.py:355
  34.3 9.1 %collective-permute-start.17 = (bf16[1,384,256]{2,1,0:T(8,128)(2,1)S(1)}, bf16[1,384,256]{2,1,0:T(8,128)(2,1)S(1)}, u32[]{:S(2)}, u32[]{:S(2)}) collective-permute-start(bf16[1,384,256]{2,1,0:T(8,128)(2,1)S(1)} %get-tuple-element.58.refs_0_), channel_id=1, source_target_pairs={{0,2},{1,3},{2,0},{3,1},{4,6},{5,7},{6,4},{7,5},{8,10},{9,11},{10,... | collective-permute-start | bytes 589832 | tf_op jit(solution)/shard_map/ppermute | solution.py:358
  36.3 7.0 %collective-permute-start.14 = (bf16[1,128,256]{2,1,0:T(8,128)(2,1)S(1)}, bf16[1,128,256]{2,1,0:T(8,128)(2,1)S(1)}, u32[]{:S(2)}, u32[]{:S(2)}) collective-permute-start(bf16[1,128,256]{2,1,0:T(8,128)(2,1)S(1)} %get-tuple-element.64), channel_id=1, source_target_pairs={{0,4},{4,8},{8,12},{12,16},{16,20},{20,24},{24,28},{28,0},{1,5},{5... | collective-permute-start | bytes 196616 | tf_op jit(solution)/shard_map/ppermute | solution.py:361
  36.5 6.9 %collective-permute-start.15 = (bf16[1,128,256]{2,1,0:T(8,128)(2,1)S(1)}, bf16[1,128,256]{2,1,0:T(8,128)(2,1)S(1)}, u32[]{:S(2)}, u32[]{:S(2)}) collective-permute-start(bf16[1,128,256]{2,1,0:T(8,128)(2,1)S(1)} %get-tuple-element.65), channel_id=1, source_target_pairs={{4,0},{8,4},{12,8},{16,12},{20,16},{24,20},{28,24},{0,28},{5,1},{9... | collective-permute-start | bytes 196616 | tf_op jit(solution)/shard_map/ppermute | solution.py:362
  41.0 1.6 %collective-permute-start.13 = (bf16[1,640,256]{2,1,0:T(8,128)(2,1)S(1)}, bf16[1,640,256]{2,1,0:T(8,128)(2,1)S(1)}, u32[]{:S(2)}, u32[]{:S(2)}) collective-permute-start(bf16[1,640,256]{2,1,0:T(8,128)(2,1)S(1)} %collective-permute-done.12.far_ref), channel_id=1, source_target_pairs={{0,1},{1,0},{2,3},{3,2},{4,5},{5,4},{6,7},{7,6},{8,9},{9,8},{10,11... | collective-permute-start | bytes 983048 | tf_op jit(solution)/shard_map/ppermute | solution.py:355
  42.0 1.6 %collective-permute-start.16 = (bf16[1,384,256]{2,1,0:T(8,128)(2,1)S(1)}, bf16[1,384,256]{2,1,0:T(8,128)(2,1)S(1)}, u32[]{:S(2)}, u32[]{:S(2)}) collective-permute-start(bf16[1,384,256]{2,1,0:T(8,128)(2,1)S(1)} %get-tuple-element.58.refs_0_), channel_id=1, source_target_pairs={{0,1},{1,0},{2,3},{3,2},{4,5},{5,4},{6,7},{7,6},{8,9},{9,8},{10,11... | collective-permute-start | bytes 589832 | tf_op jit(solution)/shard_map/ppermute | solution.py:355
  43.4 1.6 %collective-permute-start.18 = (bf16[1,384,256]{2,1,0:T(8,128)(2,1)S(1)}, bf16[1,384,256]{2,1,0:T(8,128)(2,1)S(1)}, u32[]{:S(2)}, u32[]{:S(2)}) collective-permute-start(bf16[1,384,256]{2,1,0:T(8,128)(2,1)S(1)} %collective-permute-done.17.refs_2_), channel_id=1, source_target_pairs={{0,1},{1,0},{2,3},{3,2},{4,5},{5,4},{6,7},{7,6},{8,9},{9,8},{10,11... | collective-permute-start | bytes 589832 | tf_op jit(solution)/shard_map/ppermute | solution.py:355

commit v3 on v0

--- a/solution.py
+++ b/solution.py
@@ -47,36 +47,35 @@
     )(*args)
 
 
-def round_chunk(fields, cells, with_faces):
+def load_chunk(fields, cells, with_faces):
     xcount, ycount, owned = fields[0].shape
     count = len(fields)
 
     def body(*refs):
-        field_refs = refs[:count]
-        out = refs[count]
-        held, sems = refs[-2:]
+        field_refs, held_refs, out_ref = refs[:count], refs[count:2 * count], refs[2 * count]
+        sems = refs[-1]
         copies = []
         for f in range(count):
             for i, x in enumerate(cells):
-                copies.append(pltpu.make_async_copy(field_refs[f].at[x], held.at[f, i], sems.at[f, i]))
+                copies.append(pltpu.make_async_copy(field_refs[f].at[x], held_refs[f].at[i], sems.at[f, i]))
                 copies[-1].start()
         for f in range(count):
             for i, x in enumerate(cells):
                 copies[f * len(cells) + i].wait()
-                value = held[f, i].astype(BF16)
-                out[f, i * ycount:(i + 1) * ycount, :] = value
+                value = held_refs[f][i].astype(BF16)
+                out_ref[f, i * ycount:(i + 1) * ycount, :] = value
                 if with_faces and x == 0:
-                    refs[count + 1][f] = value
+                    refs[2 * count + 1][f] = value
                 if with_faces and x == xcount - 1:
-                    refs[count + 2][f] = value
-
-    outs = [pltpu.VMEM((count, len(cells) * ycount, owned), BF16)]
+                    refs[2 * count + 2][f] = value
+
+    outs = [pltpu.VMEM((len(cells), ycount, owned), F32)] * count
+    outs.append(pltpu.VMEM((count, len(cells) * ycount, owned), BF16))
     if with_faces:
         outs += [pltpu.VMEM((count, ycount, owned), BF16)] * 2
     return call(
-        body, "round_chunk", fields, outs,
-        scratch=[pltpu.VMEM((count, len(cells), ycount, owned), F32), pltpu.SemaphoreType.DMA((count, len(cells)))],
-        specs=[FROM_HBM] * count, gflop=0.0,
+        body, "load_chunk", fields, outs, scratch=[pltpu.SemaphoreType.DMA((count, len(cells)))],
+        specs=[FROM_HBM] * count,
     )
 
 
@@ -93,39 +92,65 @@
     return DIFFUSION * (pltpu.roll(core, 1, 0) + pltpu.roll(core, core.shape[0] - 1, 0)) - 2.0 * core
 
 
-def before_first(one, two, lo, hi, growth, chunks):
-    xcount, ycount, owned = one.shape
-
-    def body(one_ref, two_ref, lo_ref, hi_ref, g_ref, *outs):
+def before_first(ones, twos, lo, hi, growth, chunks):
+    _, ycount, owned = ones[0].shape
+    xcount = sum(len(cells) for cells in chunks)
+    count = len(chunks)
+    place = {x: (c, i) for c, cells in enumerate(chunks) for i, x in enumerate(cells)}
+
+    def body(*refs):
+        lo_ref, hi_ref, g_ref, *outs = refs[2 * count:]
         growth = g_ref[...]
-        for cells, base_ref in zip(chunks, outs):
-            for f, ref in enumerate((one_ref, two_ref)):
-                for i, x in enumerate(cells):
-                    core = ref[x]
-                    before = ref[x - 1] if x > 0 else lo_ref[f].astype(F32)
-                    behind = ref[x + 1] if x < xcount - 1 else hi_ref[f].astype(F32)
-                    base_ref[f, i] = DIFFUSION * (before + behind) + along_y(core) + core * growth
+        for f in range(2):
+
+            def get(x):
+                c, i = place[x]
+                return refs[f * count + c][i]
+
+            for x, (c, i) in place.items():
+                core = get(x)
+                before = get(x - 1) if x > 0 else lo_ref[f].astype(F32)
+                behind = get(x + 1) if x < xcount - 1 else hi_ref[f].astype(F32)
+                outs[c][f, i] = DIFFUSION * (before + behind) + along_y(core) + core * growth
 
     outs = [pltpu.VMEM((2, len(cells), ycount, owned), F32) for cells in chunks]
-    return call(body, "before_first", [one, two, lo, hi, growth], outs)
-
-
-def early_part(blocks, kernels):
+    return call(body, "before_first", [*ones, *twos, lo, hi, growth], outs)
+
+
+def early_part(blocks, kernels, new=None, cells=(), xcount=0):
     rows, owned = blocks[0].shape[0] * blocks[0].shape[1], blocks[0].shape[2]
     count = len(blocks)
 
     def body(*refs):
-        block_refs, k_ref, part_ref = refs[:count], refs[count], refs[count + 1]
+        block_refs, k_ref = refs[:count], refs[count]
+        copies = []
+        if new is None:
+            part_ref = refs[-1]
+        else:
+            new_ref, part_ref, whole_ref, sems = refs[count + 1:]
+            copies = [pltpu.make_async_copy(new_ref.at[i], whole_ref.at[x], sems.at[i]) for i, x in enumerate(cells)]
+        for copy in copies:
+            copy.start()
         me = lax.axis_index("trait")
         values = [r[...].reshape(rows, owned) for r in block_refs]
         for k in range(2):
             part_ref[k] = blocks_dot(values, k_ref, k, [me ^ j for j in range(count)])
-
-    return call(body, "early_part", [*blocks, kernels], [pltpu.VMEM((2, rows, owned), F32)], gflop=20.0)[0]
+        for copy in copies:
+            copy.wait()
+
+    args = [*blocks, kernels]
+    outs = [pltpu.VMEM((2, rows, owned), F32)]
+    if new is None:
+        return call(body, "early_part", args, outs, gflop=20.0)[0]
+    outs.append(jax.ShapeDtypeStruct((xcount, *new.shape[1:]), F32))
+    return call(
+        body, "early_part", [*args, new], outs, scratch=[pltpu.SemaphoreType.DMA((len(cells),))],
+        out_specs=[SPEC, ANYWHERE], gflop=20.0,
+    )
 
 
 def first_node(part, last, base, one, two, initial, kernels, death, cells, with_faces):
-    xcount, ycount, owned = one.shape
+    xcount, ycount, owned = initial.shape
     rows = len(cells) * ycount
 
     def body(part_ref, last_ref, base_ref, one_ref, two_ref, init_ref, k_ref, d_ref, *refs):
@@ -139,7 +164,7 @@
         inv_one = 1.0 / (1.0 + FIRST * death)
         inv_two = 1.0 / (1.0 + SECOND * death)
         for i, x in enumerate(cells):
-            cores = (one_ref[x], two_ref[x])
+            cores = (one_ref[i], two_ref[i])
             e = []
             for f in range(2):
                 at = pl.ds(f * rows + i * ycount, ycount)
@@ -176,21 +201,27 @@
     )
 
 
-def before_second(news, rests, growth, death, chunks):
+def before_second(news, rests, growth, death, begun, blocks, kernels, chunks):
     _, ycount, owned = news[0].shape
+    rows = blocks[0].shape[1]
     xcount = sum(len(cells) for cells in chunks)
     count = len(chunks)
+    size = len(blocks)
     place = {x: (c, i) for c, cells in enumerate(chunks) for i, x in enumerate(cells)}
 
     def body(*refs):
-        new_refs, rest_refs = refs[:count], refs[count:2 * count]
-        g_ref, d_ref, whole_ref = refs[2 * count:2 * count + 3]
-        base_refs, sems = refs[2 * count + 3:-1], refs[-1]
+        new_refs, rest_refs, block_refs = refs[:count], refs[count:2 * count], refs[2 * count:2 * count + size]
+        k_ref, g_ref, d_ref, _, whole_ref, part_ref = refs[2 * count + size:2 * count + size + 6]
+        base_refs, sems = refs[2 * count + size + 6:-1], refs[-1]
         copies = [
-            pltpu.make_async_copy(new_refs[c].at[i], whole_ref.at[x], sems.at[x]) for x, (c, i) in place.items()
+            pltpu.make_async_copy(new_refs[-1].at[i], whole_ref.at[x], sems.at[i]) for i, x in enumerate(chunks[-1])
         ]
         for copy in copies:
             copy.start()
+        me = lax.axis_index("trait")
+        values = [r[...].reshape(rows, owned) for r in block_refs]
+        for k in range(2):
+            part_ref[k] = blocks_dot(values, k_ref, k, [me ^ j for j in range(size)])
         growth = g_ref[...]
         factor = SECOND / (1.0 + SECOND * d_ref[...])
         for x, (c, i) in place.items():
@@ -203,26 +234,26 @@
         for copy in copies:
             copy.wait()
 
-    outs = [jax.ShapeDtypeStruct((xcount, ycount, owned), F32)]
+    outs = [jax.ShapeDtypeStruct((xcount, ycount, owned), F32), pltpu.VMEM((2, rows, owned), F32)]
     outs += [pltpu.VMEM((len(cells), ycount, owned), F32) for cells in chunks]
-    return call(
-        body, "before_second", [*news, *rests, growth, death], outs, scratch=[pltpu.SemaphoreType.DMA((xcount,))],
-        out_specs=[ANYWHERE] + [SPEC] * count, gflop=20.0,
-    )
-
-
-def whole_sums(blocks, kernels):
+    args = [*news, *rests, *blocks, kernels, growth, death, begun]
+    return call(
+        body, "before_second", args, outs, scratch=[pltpu.SemaphoreType.DMA((len(chunks[-1]),))],
+        specs=[SPEC] * (len(args) - 1) + [FROM_HBM], out_specs=[ANYWHERE] + [SPEC] * (len(outs) - 1), gflop=20.0,
+        alias={len(args) - 1: 0},
+    )
+
+
+def whole_sums(part, blocks, kernels):
     rows, owned = blocks[0].shape[1:]
-    count = len(blocks)
-
-    def body(*refs):
-        block_refs, k_ref, sums_ref = refs[:count], refs[count], refs[count + 1]
-        me = lax.axis_index("trait")
-        values = [r[...].reshape(rows, owned) for r in block_refs]
-        for k in range(2):
-            sums_ref[k] = blocks_dot(values, k_ref, k, [me ^ j for j in range(count)]).astype(BF16)
-
-    return call(body, "whole_sums", [*blocks, kernels], [pltpu.VMEM((2, rows, owned), BF16)])[0]
+
+    def body(part_ref, sib_ref, far_ref, farsib_ref, k_ref, sums_ref):
+        me = lax.axis_index("trait")
+        values = [r[...].reshape(rows, owned) for r in (sib_ref, far_ref, farsib_ref)]
+        for k in range(2):
+            sums_ref[k] = (part_ref[k] + blocks_dot(values, k_ref, k, [me ^ 1, me ^ 2, me ^ 3])).astype(BF16)
+
+    return call(body, "whole_sums", [part, *blocks, kernels], [pltpu.VMEM((2, rows, owned), BF16)])[0]
 
 
 def finish(cells, ycount, sums, base_ref, new_ref, factor, faces, held, out_ref, sems):
@@ -307,37 +338,39 @@
         hi = lax.ppermute(head, "gx", [((i + 1) % gcount, i) for i in range(gcount)])
         return lo, hi
 
-    own_a, head, tail = round_chunk((section_one, section_two), chunks[0], True)
+    one_a, two_a, own_a, head, tail = load_chunk((section_one, section_two), chunks[0], True)
     far_a = to_far(own_a)
-    own_b = round_chunk((after(section_one, own_a), section_two), chunks[1], False)[0]
+    one_b, two_b, own_b = load_chunk((after(section_one, own_a), section_two), chunks[1], False)
     far_b = to_far(own_b)
     head, tail, kernels = lax.optimization_barrier((head, tail, kernels, own_b))[:3]
     lo, hi = faces(head, tail)
-    base_a, base_b = before_first(section_one, section_two, lo, hi, growth, chunks)
+    base_a, base_b = before_first((one_a, one_b), (two_a, two_b), lo, hi, growth, chunks)
     sib_a = to_sibling(after(own_a, own_b))
     sib_b = to_sibling(own_b)
     far_a = after(far_a, base_a)
     farsib_a = to_sibling(far_a)
     part_a = early_part([own_a, sib_a, far_a], kernels)
     new_a, rounded_a, rest_a, new_head, new_tail = first_node(
-        part_a, farsib_a, base_a, section_one, section_two, initial, kernels, death, chunks[0], True
+        part_a, farsib_a, base_a, one_a, two_a, initial, kernels, death, chunks[0], True
     )
     nfar_a = to_far(rounded_a)
     nsib_a = to_sibling(rounded_a)
 
     far_b = after(far_b, rounded_a)
     farsib_b = to_sibling(far_b)
-    part_b = early_part([own_b, sib_b, far_b], kernels)
+    part_b, new_one = early_part([own_b, sib_b, far_b], kernels, new_a, chunks[0], xcount)
     new_b, rounded_b, rest_b = first_node(
-        part_b, farsib_b, base_b, section_one, section_two, initial, kernels, death, chunks[1], False
+        part_b, farsib_b, base_b, one_b, two_b, initial, kernels, death, chunks[1], False
     )
     nfar_b = to_far(rounded_b)
     nsib_b = to_sibling(rounded_b)
     new_lo, new_hi = faces(*lax.optimization_barrier((new_head, new_tail, rounded_b))[:2])
     nfar_a = after(nfar_a, rounded_b)
     nfarsib_a = to_sibling(nfar_a)
-    new_one, nbase_a, nbase_b = before_second((new_a, new_b), (rest_a, rest_b), growth, death, chunks)
-    sums_a = whole_sums([rounded_a, nsib_a, nfar_a, nfarsib_a], after(kernels, nbase_a))
+    new_one, npart_a, nbase_a, nbase_b = before_second(
+        (new_a, new_b), (rest_a, rest_b), growth, death, new_one, [rounded_a], kernels, chunks
+    )
+    sums_a = whole_sums(npart_a, [nsib_a, nfar_a, nfarsib_a], after(kernels, nbase_a))
     nfar_b = after(nfar_b, sums_a, new_lo, new_hi)
     nfarsib_b = to_sibling(nfar_b)
     begun, npart_b = second_first(

time: 43.6 us -> 43.5 us (level)
  transfers between devices with their start and end apart: 16 -> 16, of which waited for: 6 -> 9; matrix products, arithmetic and copies ran while one was open for 0% -> 0% of each run, Pallas kernels for 21% -> 21%
where the time goes in v3:
time: 43.5 us; the launch traced here: 43.4 us
  starting transfers between devices  17.9 us (41%)
  waiting for transfers between devices  13.1 us (30%)
  Pallas kernels  11.5 us (26%)
  between operations  0.78 us (2%)
    pallas_call x11, Pallas kernels, call(): pl.pallas_call(body, out_shape=outs, in_specs=specs, out_specs=out_specs...  11.5 us
    ppermute x4, starting transfers between devices, to_far(): return lax.ppermute(v, 'trait', [(i, i ^ 2) for i in range(traits)])  7.68 us
    ppermute x4, waiting for transfers between devices, to_far(): return lax.ppermute(v, 'trait', [(i, i ^ 2) for i in range(traits)])  6.53 us
    ppermute x2, starting transfers between devices, faces(): lax.ppermute(head, 'gx', [((i + 1) % gcount, i) for i in range(gcount)])  6.46 us
    ppermute x2, waiting for transfers between devices, faces(): lax.ppermute(tail, 'gx', [(i, (i + 1) % gcount) for i in range(gcount)])  3.62 us
    ppermute x2, starting transfers between devices, faces(): lax.ppermute(tail, 'gx', [(i, (i + 1) % gcount) for i in range(gcount)])  3.03 us
    ppermute x8, waiting for transfers between devices, to_sibling(): return lax.ppermute(v, 'trait', [(i, i ^ 1) for i in range(traits)])  1.7 us
    ppermute x2, waiting for transfers between devices, faces(): lax.ppermute(head, 'gx', [((i + 1) % gcount, i) for i in range(gcount)])  1.23 us
  transfers between devices with their start and end apart: 16, of which 9 were waited for; matrix products, arithmetic and copies ran while one was open for 0% of the time, Pallas kernels for 21%

profile of v3, /device:TPU:0, one launch (start us, length us, event | category | flops | bytes accessed | tf_op | source)
XLA Modules:
  0.0 43.4 jit_solution(2338045943132896893)
XLA Ops:
  0.6 1.5 %load_chunk.2 = (f32[5,128,256]{2,1,0:T(8,128)S(1)}, f32[5,128,256]{2,1,0:T(8,128)S(1)}, bf16[2,640,256]{2,1,0:T(8,128)(2,1)S(1)}, bf16[2,128,256]{2,1,0:T(8,128)(2,1)S(1)}, bf16[2,128,256]{2,1,0:T(8,128)(2,1)S(1)}) custom-call(f32[8,128,256]{2,1,0:T(8,128)} %refs_0_.2, f32[8,128,256]{2,1,0:T(8,128)} %refs_1_.3), custom_call_target="tpu_custom_call" | custom-call | tf_op jit(solution)/shard_map/load_chunk/pallas_call | solution.py:37
  2.1 0.0 copy-start.3
  2.1 3.0 %collective-permute-start.1 = (bf16[2,640,256]{2,1,0:T(8,128)(2,1)S(1)}, bf16[2,640,256]{2,1,0:T(8,128)(2,1)S(1)}, u32[]{:S(2)}, u32[]{:S(2)}) collective-permute-start(bf16[2,640,256]{2,1,0:T(8,128)(2,1)S(1)} %get-tuple-element.43.refs_0_), channel_id=1, source_target_pairs={{0,2},{1,3},{2,0},{3,1},{4,6},{5,7},{6,4},{7,5},{8,10},{9,11},{10,... | collective-permute-start | bytes 1966088 | tf_op jit(solution)/shard_map/ppermute | solution.py:334
  5.1 1.3 %load_chunk.3 = (f32[3,128,256]{2,1,0:T(8,128)S(1)}, f32[3,128,256]{2,1,0:T(8,128)S(1)}, bf16[2,384,256]{2,1,0:T(8,128)(2,1)S(1)}) custom-call(f32[8,128,256]{2,1,0:T(8,128)} %refs_0_.2, f32[8,128,256]{2,1,0:T(8,128)} %refs_1_.3), custom_call_target="tpu_custom_call" | custom-call | tf_op jit(solution)/shard_map/load_chunk/pallas_call | solution.py:37
  6.4 0.0 copy-start
  6.4 0.1 collective-permute-start
  6.5 1.5 %collective-permute-start.2 = (bf16[2,128,256]{2,1,0:T(8,128)(2,1)S(1)}, bf16[2,128,256]{2,1,0:T(8,128)(2,1)S(1)}, u32[]{:S(2)}, u32[]{:S(2)}) collective-permute-start(bf16[2,128,256]{2,1,0:T(8,128)(2,1)S(1)} %get-tuple-element.50), channel_id=1, source_target_pairs={{0,4},{4,8},{8,12},{12,16},{16,20},{20,24},{24,28},{28,0},{1,5},{5... | collective-permute-start | bytes 393224 | tf_op jit(solution)/shard_map/ppermute | solution.py:337
  8.0 3.2 %collective-permute-start.3 = (bf16[2,128,256]{2,1,0:T(8,128)(2,1)S(1)}, bf16[2,128,256]{2,1,0:T(8,128)(2,1)S(1)}, u32[]{:S(2)}, u32[]{:S(2)}) collective-permute-start(bf16[2,128,256]{2,1,0:T(8,128)(2,1)S(1)} %get-tuple-element.51), channel_id=1, source_target_pairs={{4,0},{8,4},{12,8},{16,12},{20,16},{24,20},{28,24},{0,28},{5,1},{9... | collective-permute-start | bytes 393224 | tf_op jit(solution)/shard_map/ppermute | solution.py:338
  11.3 0.4 collective-permute-start.6
  11.7 3.6 %collective-permute-done.2.refs_4_ = bf16[2,128,256]{2,1,0:T(8,128)(2,1)S(1)} collective-permute-done((bf16[2,128,256]{2,1,0:T(8,128)(2,1)S(1)}, bf16[2,128,256]{2,1,0:T(8,128)(2,1)S(1)}, u32[]{:S(2)}, u32[]{:S(2)}) %collective-permute-start.2) | collective-permute-done | bytes 131104 | tf_op jit(solution)/shard_map/ppermute | solution.py:337
  15.3 0.0 collective-permute-start.5
  15.3 1.1 %collective-permute-done.3.refs_5_ = bf16[2,128,256]{2,1,0:T(8,128)(2,1)S(1)} collective-permute-done((bf16[2,128,256]{2,1,0:T(8,128)(2,1)S(1)}, bf16[2,128,256]{2,1,0:T(8,128)(2,1)S(1)}, u32[]{:S(2)}, u32[]{:S(2)}) %collective-permute-start.3) | collective-permute-done | bytes 131104 | tf_op jit(solution)/shard_map/ppermute | solution.py:338
  16.4 0.0 copy-done.3
  16.4 0.9 %before_first.1 = (f32[2,5,128,256]{3,2,1,0:T(8,128)S(1)}, f32[2,3,128,256]{3,2,1,0:T(8,128)S(1)}) custom-call(f32[5,128,256]{2,1,0:T(8,128)S(1)} %get-tuple-element.44.refs_0_.one_ref, f32[3,128,256]{2,1,0:T(8,128)S(1)} %get-tuple-element.45.refs_1_.one_ref, f32[5,128,256]{2,1,0:T(8,128)S(1)} %get-tuple-element.46.refs_2_.two_ref, ...), custom_call_target="tpu_custom_call" | custom-call | tf_op jit(solution)/shard_map/before_first/pallas_call | solution.py:37
  17.3 3.4 %collective-permute-done.1.refs_2_ = bf16[2,640,256]{2,1,0:T(8,128)(2,1)S(1)} collective-permute-done((bf16[2,640,256]{2,1,0:T(8,128)(2,1)S(1)}, bf16[2,640,256]{2,1,0:T(8,128)(2,1)S(1)}, u32[]{:S(2)}, u32[]{:S(2)}) %collective-permute-start.1) | collective-permute-done | bytes 655392 | tf_op jit(solution)/shard_map/ppermute | solution.py:334
  20.7 0.0 collective-permute-start.4
  20.7 0.0 collective-permute-done.refs_1_
  20.7 0.0 copy-done
  20.7 1.2 %early_part.2.part_ref = f32[2,1280,256]{2,1,0:T(8,128)S(1)} custom-call(bf16[2,640,256]{2,1,0:T(8,128)(2,1)S(1)} %get-tuple-element.43.refs_0_, bf16[2,640,256]{2,1,0:T(8,128)(2,1)S(1)} %collective-permute-done.refs_1_, bf16[2,640,256]{2,1,0:T(8,128)(2,1)S(1)} %collective-permute-done.1.refs_2_, bf16[2,1024,256]{2,1,0:T(8,128)(2,1)S(1)} %copy-done), custom_call_target="tpu_custom_call" | custom-call | flops 20000000000 | tf_op jit(solution)/shard_map/early_part/pallas_call | solution.py:37
  21.9 0.9 %collective-permute-done.4.last_ref = bf16[2,640,256]{2,1,0:T(8,128)(2,1)S(1)} collective-permute-done((bf16[2,640,256]{2,1,0:T(8,128)(2,1)S(1)}, bf16[2,640,256]{2,1,0:T(8,128)(2,1)S(1)}, u32[]{:S(2)}, u32[]{:S(2)}) %collective-permute-start.4) | collective-permute-done | bytes 655392 | tf_op jit(solution)/shard_map/ppermute | solution.py:331
  22.8 0.0 copy-done.1
  22.8 1.0 %first_node.2 = (f32[5,128,256]{2,1,0:T(8,128)S(1)}, bf16[1,640,256]{2,1,0:T(8,128)(2,1)S(1)}, f32[5,128,256]{2,1,0:T(8,128)S(1)}, bf16[1,128,256]{2,1,0:T(8,128)(2,1)S(1)}, bf16[1,128,256]{2,1,0:T(8,128)(2,1)S(1)}) custom-call(f32[2,1280,256]{2,1,0:T(8,128)S(1)} %early_part.2.part_ref, bf16[2,640,256]{2,1,0:T(8,128)(2,1)S(1)} %collective-permute-done.4.last_ref, ...), custom_call_target="tpu_custom_call" | custom-call | tf_op jit(solution)/shard_map/first_node/pallas_call | solution.py:37
  23.8 2.1 %collective-permute-start.9 = (bf16[1,640,256]{2,1,0:T(8,128)(2,1)S(1)}, bf16[1,640,256]{2,1,0:T(8,128)(2,1)S(1)}, u32[]{:S(2)}, u32[]{:S(2)}) collective-permute-start(bf16[1,640,256]{2,1,0:T(8,128)(2,1)S(1)} %get-tuple-element.56.refs_4_), channel_id=1, source_target_pairs={{0,2},{1,3},{2,0},{3,1},{4,6},{5,7},{6,4},{7,5},{8,10},{9,11},{10,... | collective-permute-start | bytes 983048 | tf_op jit(solution)/shard_map/ppermute | solution.py:334
  26.0 0.0 collective-permute-start.8
  26.0 3.2 %collective-permute-done.6.refs_2_ = bf16[2,384,256]{2,1,0:T(8,128)(2,1)S(1)} collective-permute-done((bf16[2,384,256]{2,1,0:T(8,128)(2,1)S(1)}, bf16[2,384,256]{2,1,0:T(8,128)(2,1)S(1)}, u32[]{:S(2)}, u32[]{:S(2)}) %collective-permute-start.6) | collective-permute-done | bytes 393248 | tf_op jit(solution)/shard_map/ppermute | solution.py:334
  29.1 0.0 collective-permute-start.7
  29.1 0.0 collective-permute-done.5.refs_1_
  29.1 1.0 %early_part.3 = (f32[2,768,256]{2,1,0:T(8,128)S(1)}, f32[8,128,256]{2,1,0:T(8,128)}) custom-call(bf16[2,384,256]{2,1,0:T(8,128)(2,1)S(1)} %get-tuple-element.42.refs_0_, bf16[2,384,256]{2,1,0:T(8,128)(2,1)S(1)} %collective-permute-done.5.refs_1_, bf16[2,384,256]{2,1,0:T(8,128)(2,1)S(1)} %collective-permute-done.6.refs_2_, bf16[2,1024,256]{2,1,0:T(8,128)(2,1)S(1)} %copy-done, ...), custom_call_target="tpu_custom_call" | custom-call | flops 20000000000 | tf_op jit(solution)/shard_map/early_part/pallas_call | solution.py:37
  30.2 0.7 %collective-permute-done.7.last_ref = bf16[2,384,256]{2,1,0:T(8,128)(2,1)S(1)} collective-permute-done((bf16[2,384,256]{2,1,0:T(8,128)(2,1)S(1)}, bf16[2,384,256]{2,1,0:T(8,128)(2,1)S(1)}, u32[]{:S(2)}, u32[]{:S(2)}) %collective-permute-start.7) | collective-permute-done | bytes 393248 | tf_op jit(solution)/shard_map/ppermute | solution.py:331
  30.9 0.7 %first_node.3 = (f32[3,128,256]{2,1,0:T(8,128)S(1)}, bf16[1,384,256]{2,1,0:T(8,128)(2,1)S(1)}, f32[3,128,256]{2,1,0:T(8,128)S(1)}) custom-call(f32[2,768,256]{2,1,0:T(8,128)S(1)} %get-tuple-element.58.part_ref, bf16[2,384,256]{2,1,0:T(8,128)(2,1)S(1)} %collective-permute-done.7.last_ref, f32[2,3,128,256]{3,2,1,0:T(8,128)S(1)} %get-tuple-element.59.base_ref, ...), custom_call_target="tpu_custom_call" | custom-call | tf_op jit(solution)/shard_map/first_node/pallas_call | solution.py:37
  31.6 2.1 %collective-permute-start.14 = (bf16[1,384,256]{2,1,0:T(8,128)(2,1)S(1)}, bf16[1,384,256]{2,1,0:T(8,128)(2,1)S(1)}, u32[]{:S(2)}, u32[]{:S(2)}) collective-permute-start(bf16[1,384,256]{2,1,0:T(8,128)(2,1)S(1)} %get-tuple-element.66.refs_0_), channel_id=1, source_target_pairs={{0,2},{1,3},{2,0},{3,1},{4,6},{5,7},{6,4},{7,5},{8,10},{9,11},{10,... | collective-permute-start | bytes 589832 | tf_op jit(solution)/shard_map/ppermute | solution.py:334
  33.7 1.5 %collective-permute-start.11 = (bf16[1,128,256]{2,1,0:T(8,128)(2,1)S(1)}, bf16[1,128,256]{2,1,0:T(8,128)(2,1)S(1)}, u32[]{:S(2)}, u32[]{:S(2)}) collective-permute-start(bf16[1,128,256]{2,1,0:T(8,128)(2,1)S(1)} %get-tuple-element.72), channel_id=1, source_target_pairs={{0,4},{4,8},{8,12},{12,16},{16,20},{20,24},{24,28},{28,0},{1,5},{5... | collective-permute-start | bytes 196616 | tf_op jit(solution)/shard_map/ppermute | solution.py:337
  35.2 3.2 %collective-permute-start.12 = (bf16[1,128,256]{2,1,0:T(8,128)(2,1)S(1)}, bf16[1,128,256]{2,1,0:T(8,128)(2,1)S(1)}, u32[]{:S(2)}, u32[]{:S(2)}) collective-permute-start(bf16[1,128,256]{2,1,0:T(8,128)(2,1)S(1)} %get-tuple-element.73), channel_id=1, source_target_pairs={{4,0},{8,4},{12,8},{16,12},{20,16},{24,20},{28,24},{0,28},{5,1},{9... | collective-permute-start | bytes 196616 | tf_op jit(solution)/shard_map/ppermute | solution.py:338
  38.4 0.0 collective-permute-done.9.far_ref
  38.4 0.0 collective-permute-start.10
  38.4 1.0 %before_second.1 = (f32[8,128,256]{2,1,0:T(8,128)}, f32[2,640,256]{2,1,0:T(8,128)S(1)}, f32[5,128,256]{2,1,0:T(8,128)S(1)}, f32[3,128,256]{2,1,0:T(8,128)S(1)}) custom-call(f32[5,128,256]{2,1,0:T(8,128)S(1)} %get-tuple-element.55.refs_4_.refs_0_.new_ref, f32[3,128,256]{2,1,0:T(8,128)S(1)} %get-tuple-element.60.refs_1_.new_ref, ...), custom_call_target="tpu_custom_call", output_to_operand_aliasing={{0}: (8, {})} | custom-call | flops 20000000000 | tf_op jit(solution)/shard_map/before_second/pallas_call | solution.py:37
  39.4 0.0 collective-permute-done.8.sib_ref
  39.4 0.6 %collective-permute-start.13 = (bf16[1,384,256]{2,1,0:T(8,128)(2,1)S(1)}, bf16[1,384,256]{2,1,0:T(8,128)(2,1)S(1)}, u32[]{:S(2)}, u32[]{:S(2)}) collective-permute-start(bf16[1,384,256]{2,1,0:T(8,128)(2,1)S(1)} %get-tuple-element.66.refs_0_), channel_id=1, source_target_pairs={{0,1},{1,0},{2,3},{3,2},{4,5},{5,4},{6,7},{7,6},{8,9},{9,8},{10,11... | collective-permute-start | bytes 589832 | tf_op jit(solution)/shard_map/ppermute | solution.py:331
  40.0 0.1 collective-permute-done.10.farsib_ref
  40.0 0.7 %whole_sums.1.sums_ref = bf16[2,640,256]{2,1,0:T(8,128)(2,1)S(1)} custom-call(f32[2,640,256]{2,1,0:T(8,128)S(1)} %get-tuple-element.65.part_ref, bf16[1,640,256]{2,1,0:T(8,128)(2,1)S(1)} %collective-permute-done.8.sib_ref, bf16[1,640,256]{2,1,0:T(8,128)(2,1)S(1)} %collective-permute-done.9.far_ref, ...), custom_call_target="tpu_custom_call" | custom-call | tf_op jit(solution)/shard_map/whole_sums/pallas_call | solution.py:37
  40.7 0.0 collective-permute-done.11.lo_ref
  40.7 0.1 collective-permute-done.12.hi_ref
  40.8 0.0 collective-permute-done.14.refs_2_
  40.8 0.1 collective-permute-start.15
  41.0 0.1 collective-permute-done.13.refs_1_
  41.0 1.3 %second_first.1 = (f32[8,128,256]{2,1,0:T(8,128)}, f32[2,384,256]{2,1,0:T(8,128)S(1)}) custom-call(bf16[2,640,256]{2,1,0:T(8,128)(2,1)S(1)} %whole_sums.1.sums_ref, f32[5,128,256]{2,1,0:T(8,128)S(1)} %get-tuple-element.68.base_ref, f32[5,128,256]{2,1,0:T(8,128)S(1)} %get-tuple-element.55.refs_4_.refs_0_.new_ref, f32[1,256]{1,0:T(1,128)S(1)} %bitcast.5, ...), custom_call_target="tpu_custom_call" | custom-call | tf_op jit(solution)/shard_map/second_first/pallas_call | solution.py:37
  42.3 0.0 collective-permute-done.15.last_ref
  42.4 1.0 %second_last.1 = f32[8,128,256]{2,1,0:T(8,128)} custom-call(f32[2,384,256]{2,1,0:T(8,128)S(1)} %get-tuple-element.75.part_ref, bf16[1,384,256]{2,1,0:T(8,128)(2,1)S(1)} %collective-permute-done.15.last_ref, f32[3,128,256]{2,1,0:T(8,128)S(1)} %get-tuple-element.76.base_ref, ...), custom_call_target="tpu_custom_call", output_to_operand_aliasing={{}: (6, {})} | custom-call | tf_op jit(solution)/shard_map/second_last/pallas_call | solution.py:37
  (3 shorter events, 0.0 us)
Async XLA Ops:
  2.1 14.3 %copy-start.3 = (f32[256]{0:T(256)S(1)}, f32[256]{0:T(256)}, u32[]{:S(2)}) copy-start(f32[256]{0:T(256)} %param.10) | copy-start | bytes 3076
  2.1 18.6 %collective-permute-start.1 = (bf16[2,640,256]{2,1,0:T(8,128)(2,1)S(1)}, bf16[2,640,256]{2,1,0:T(8,128)(2,1)S(1)}, u32[]{:S(2)}, u32[]{:S(2)}) collective-permute-start(bf16[2,640,256]{2,1,0:T(8,128)(2,1)S(1)} %get-tuple-element.43.refs_0_), channel_id=1, source_target_pairs={{0,2},{1,3},{2,0},{3,1},{4,6},{5,7},{6,4},{7,5},{8,10},{9,11},{10,... | collective-permute-start | bytes 1966088 | tf_op jit(solution)/shard_map/ppermute | solution.py:334
  6.4 14.3 %copy-start = (bf16[2,1024,256]{2,1,0:T(8,128)(2,1)S(1)}, bf16[2,1024,256]{2,1,0:T(8,128)(2,1)}, u32[]{:S(2)}) copy-start(bf16[2,1024,256]{2,1,0:T(8,128)(2,1)} %k_ref.4) | copy-start | bytes 3145732
  6.4 14.3 %collective-permute-start = (bf16[2,640,256]{2,1,0:T(8,128)(2,1)S(1)}, bf16[2,640,256]{2,1,0:T(8,128)(2,1)S(1)}, u32[]{:S(2)}, u32[]{:S(2)}) collective-permute-start(bf16[2,640,256]{2,1,0:T(8,128)(2,1)S(1)} %get-tuple-element.43.refs_0_), channel_id=1, source_target_pairs={{0,1},{1,0},{2,3},{3,2},{4,5},{5,4},{6,7},{7,6},{8,9},{9,8},{10,11... | collective-permute-start | bytes 1966088 | tf_op jit(solution)/shard_map/ppermute | solution.py:331
  6.5 8.8 %collective-permute-start.2 = (bf16[2,128,256]{2,1,0:T(8,128)(2,1)S(1)}, bf16[2,128,256]{2,1,0:T(8,128)(2,1)S(1)}, u32[]{:S(2)}, u32[]{:S(2)}) collective-permute-start(bf16[2,128,256]{2,1,0:T(8,128)(2,1)S(1)} %get-tuple-element.50), channel_id=1, source_target_pairs={{0,4},{4,8},{8,12},{12,16},{16,20},{20,24},{24,28},{28,0},{1,5},{5... | collective-permute-start | bytes 393224 | tf_op jit(solution)/shard_map/ppermute | solution.py:337
  8.0 8.4 %collective-permute-start.3 = (bf16[2,128,256]{2,1,0:T(8,128)(2,1)S(1)}, bf16[2,128,256]{2,1,0:T(8,128)(2,1)S(1)}, u32[]{:S(2)}, u32[]{:S(2)}) collective-permute-start(bf16[2,128,256]{2,1,0:T(8,128)(2,1)S(1)} %get-tuple-element.51), channel_id=1, source_target_pairs={{4,0},{8,4},{12,8},{16,12},{20,16},{24,20},{28,24},{0,28},{5,1},{9... | collective-permute-start | bytes 393224 | tf_op jit(solution)/shard_map/ppermute | solution.py:338
  11.3 17.9 %collective-permute-start.6 = (bf16[2,384,256]{2,1,0:T(8,128)(2,1)S(1)}, bf16[2,384,256]{2,1,0:T(8,128)(2,1)S(1)}, u32[]{:S(2)}, u32[]{:S(2)}) collective-permute-start(bf16[2,384,256]{2,1,0:T(8,128)(2,1)S(1)} %get-tuple-element.42.refs_0_), channel_id=1, source_target_pairs={{0,2},{1,3},{2,0},{3,1},{4,6},{5,7},{6,4},{7,5},{8,10},{9,11},{10,... | collective-permute-start | bytes 1179656 | tf_op jit(solution)/shard_map/ppermute | solution.py:334
  15.3 13.8 %collective-permute-start.5 = (bf16[2,384,256]{2,1,0:T(8,128)(2,1)S(1)}, bf16[2,384,256]{2,1,0:T(8,128)(2,1)S(1)}, u32[]{:S(2)}, u32[]{:S(2)}) collective-permute-start(bf16[2,384,256]{2,1,0:T(8,128)(2,1)S(1)} %get-tuple-element.42.refs_0_), channel_id=1, source_target_pairs={{0,1},{1,0},{2,3},{3,2},{4,5},{5,4},{6,7},{7,6},{8,9},{9,8},{10,11... | collective-permute-start | bytes 1179656 | tf_op jit(solution)/shard_map/ppermute | solution.py:331
  20.7 2.1 %copy-start.1 = (f32[8,128,256]{2,1,0:T(8,128)S(1)}, f32[8,128,256]{2,1,0:T(8,128)}, u32[]{:S(2)}) copy-start(f32[8,128,256]{2,1,0:T(8,128)} %init_ref.3) | copy-start | bytes 3145732
  20.7 2.1 %copy-start.2 = (f32[256]{0:T(256)S(1)}, f32[256]{0:T(256)}, u32[]{:S(2)}) copy-start(f32[256]{0:T(256)} %param.11) | copy-start | bytes 3076
  20.7 2.1 %collective-permute-start.4 = (bf16[2,640,256]{2,1,0:T(8,128)(2,1)S(1)}, bf16[2,640,256]{2,1,0:T(8,128)(2,1)S(1)}, u32[]{:S(2)}, u32[]{:S(2)}) collective-permute-start(bf16[2,640,256]{2,1,0:T(8,128)(2,1)S(1)} %collective-permute-done.1.refs_2_), channel_id=1, source_target_pairs={{0,1},{1,0},{2,3},{3,2},{4,5},{5,4},{6,7},{7,6},{8,9},{9,8},{10,11... | collective-permute-start | bytes 1966088 | tf_op jit(solution)/shard_map/ppermute | solution.py:331
  23.8 14.6 %collective-permute-start.9 = (bf16[1,640,256]{2,1,0:T(8,128)(2,1)S(1)}, bf16[1,640,256]{2,1,0:T(8,128)(2,1)S(1)}, u32[]{:S(2)}, u32[]{:S(2)}) collective-permute-start(bf16[1,640,256]{2,1,0:T(8,128)(2,1)S(1)} %get-tuple-element.56.refs_4_), channel_id=1, source_target_pairs={{0,2},{1,3},{2,0},{3,1},{4,6},{5,7},{6,4},{7,5},{8,10},{9,11},{10,... | collective-permute-start | bytes 983048 | tf_op jit(solution)/shard_map/ppermute | solution.py:334
  26.0 13.4 %collective-permute-start.8 = (bf16[1,640,256]{2,1,0:T(8,128)(2,1)S(1)}, bf16[1,640,256]{2,1,0:T(8,128)(2,1)S(1)}, u32[]{:S(2)}, u32[]{:S(2)}) collective-permute-start(bf16[1,640,256]{2,1,0:T(8,128)(2,1)S(1)} %get-tuple-element.56.refs_4_), channel_id=1, source_target_pairs={{0,1},{1,0},{2,3},{3,2},{4,5},{5,4},{6,7},{7,6},{8,9},{9,8},{10,11... | collective-permute-start | bytes 983048 | tf_op jit(solution)/shard_map/ppermute | solution.py:331
  29.1 1.7 %collective-permute-start.7 = (bf16[2,384,256]{2,1,0:T(8,128)(2,1)S(1)}, bf16[2,384,256]{2,1,0:T(8,128)(2,1)S(1)}, u32[]{:S(2)}, u32[]{:S(2)}) collective-permute-start(bf16[2,384,256]{2,1,0:T(8,128)(2,1)S(1)} %collective-permute-done.6.refs_2_), channel_id=1, source_target_pairs={{0,1},{1,0},{2,3},{3,2},{4,5},{5,4},{6,7},{7,6},{8,9},{9,8},{10,11... | collective-permute-start | bytes 1179656 | tf_op jit(solution)/shard_map/ppermute | solution.py:331
  31.6 9.3 %collective-permute-start.14 = (bf16[1,384,256]{2,1,0:T(8,128)(2,1)S(1)}, bf16[1,384,256]{2,1,0:T(8,128)(2,1)S(1)}, u32[]{:S(2)}, u32[]{:S(2)}) collective-permute-start(bf16[1,384,256]{2,1,0:T(8,128)(2,1)S(1)} %get-tuple-element.66.refs_0_), channel_id=1, source_target_pairs={{0,2},{1,3},{2,0},{3,1},{4,6},{5,7},{6,4},{7,5},{8,10},{9,11},{10,... | collective-permute-start | bytes 589832 | tf_op jit(solution)/shard_map/ppermute | solution.py:334
  33.7 7.0 %collective-permute-start.11 = (bf16[1,128,256]{2,1,0:T(8,128)(2,1)S(1)}, bf16[1,128,256]{2,1,0:T(8,128)(2,1)S(1)}, u32[]{:S(2)}, u32[]{:S(2)}) collective-permute-start(bf16[1,128,256]{2,1,0:T(8,128)(2,1)S(1)} %get-tuple-element.72), channel_id=1, source_target_pairs={{0,4},{4,8},{8,12},{12,16},{16,20},{20,24},{24,28},{28,0},{1,5},{5... | collective-permute-start | bytes 196616 | tf_op jit(solution)/shard_map/ppermute | solution.py:337
  35.2 5.7 %collective-permute-start.12 = (bf16[1,128,256]{2,1,0:T(8,128)(2,1)S(1)}, bf16[1,128,256]{2,1,0:T(8,128)(2,1)S(1)}, u32[]{:S(2)}, u32[]{:S(2)}) collective-permute-start(bf16[1,128,256]{2,1,0:T(8,128)(2,1)S(1)} %get-tuple-element.73), channel_id=1, source_target_pairs={{4,0},{8,4},{12,8},{16,12},{20,16},{24,20},{28,24},{0,28},{5,1},{9... | collective-permute-start | bytes 196616 | tf_op jit(solution)/shard_map/ppermute | solution.py:338
  38.4 1.6 %collective-permute-start.10 = (bf16[1,640,256]{2,1,0:T(8,128)(2,1)S(1)}, bf16[1,640,256]{2,1,0:T(8,128)(2,1)S(1)}, u32[]{:S(2)}, u32[]{:S(2)}) collective-permute-start(bf16[1,640,256]{2,1,0:T(8,128)(2,1)S(1)} %collective-permute-done.9.far_ref), channel_id=1, source_target_pairs={{0,1},{1,0},{2,3},{3,2},{4,5},{5,4},{6,7},{7,6},{8,9},{9,8},{10,11... | collective-permute-start | bytes 983048 | tf_op jit(solution)/shard_map/ppermute | solution.py:331
  39.4 1.6 %collective-permute-start.13 = (bf16[1,384,256]{2,1,0:T(8,128)(2,1)S(1)}, bf16[1,384,256]{2,1,0:T(8,128)(2,1)S(1)}, u32[]{:S(2)}, u32[]{:S(2)}) collective-permute-start(bf16[1,384,256]{2,1,0:T(8,128)(2,1)S(1)} %get-tuple-element.66.refs_0_), channel_id=1, source_target_pairs={{0,1},{1,0},{2,3},{3,2},{4,5},{5,4},{6,7},{7,6},{8,9},{9,8},{10,11... | collective-permute-start | bytes 589832 | tf_op jit(solution)/shard_map/ppermute | solution.py:331
  40.8 1.5 %collective-permute-start.15 = (bf16[1,384,256]{2,1,0:T(8,128)(2,1)S(1)}, bf16[1,384,256]{2,1,0:T(8,128)(2,1)S(1)}, u32[]{:S(2)}, u32[]{:S(2)}) collective-permute-start(bf16[1,384,256]{2,1,0:T(8,128)(2,1)S(1)} %collective-permute-done.14.refs_2_), channel_id=1, source_target_pairs={{0,1},{1,0},{2,3},{3,2},{4,5},{5,4},{6,7},{7,6},{8,9},{9,8},{10,11... | collective-permute-start | bytes 589832 | tf_op jit(solution)/shard_map/ppermute | solution.py:331

commit v4 on v3

--- a/solution.py
+++ b/solution.py
@@ -19,9 +19,8 @@
 
 def chunks_of(xcount):
     last = max(1, 3 * xcount // 8)
-    start = (xcount - last + 1) // 2
-    middle = list(range(start, start + last))
-    return [x for x in range(xcount) if x not in middle], middle
+    inner = list(range(1, xcount - 1))
+    return [0, xcount - 1], inner[:-last], inner[-last:]
 
 
 def after(value, *others):
@@ -47,34 +46,36 @@
     )(*args)
 
 
-def load_chunk(fields, cells, with_faces):
+def load_cells(fields, groups, with_faces):
     xcount, ycount, owned = fields[0].shape
     count = len(fields)
+    size = count + 1
 
     def body(*refs):
-        field_refs, held_refs, out_ref = refs[:count], refs[count:2 * count], refs[2 * count]
-        sems = refs[-1]
-        copies = []
-        for f in range(count):
-            for i, x in enumerate(cells):
-                copies.append(pltpu.make_async_copy(field_refs[f].at[x], held_refs[f].at[i], sems.at[f, i]))
-                copies[-1].start()
-        for f in range(count):
-            for i, x in enumerate(cells):
-                copies[f * len(cells) + i].wait()
-                value = held_refs[f][i].astype(BF16)
-                out_ref[f, i * ycount:(i + 1) * ycount, :] = value
-                if with_faces and x == 0:
-                    refs[2 * count + 1][f] = value
-                if with_faces and x == xcount - 1:
-                    refs[2 * count + 2][f] = value
-
-    outs = [pltpu.VMEM((len(cells), ycount, owned), F32)] * count
-    outs.append(pltpu.VMEM((count, len(cells) * ycount, owned), BF16))
+        field_refs, outs, sems = refs[:count], refs[count:-1], refs[-1]
+        copies = {}
+        for g, cells in enumerate(groups):
+            for f in range(count):
+                for i, x in enumerate(cells):
+                    copies[f, x] = pltpu.make_async_copy(field_refs[f].at[x], outs[size * g + f].at[i], sems.at[f, x])
+                    copies[f, x].start()
+        for g, cells in enumerate(groups):
+            for f in range(count):
+                for i, x in enumerate(cells):
+                    copies[f, x].wait()
+                    value = outs[size * g + f][i].astype(BF16)
+                    outs[size * g + count][f, pl.ds(i * ycount, ycount), :] = value
+                    if with_faces and x in (0, xcount - 1):
+                        outs[-2 if x == 0 else -1][f] = value
+
+    outs = []
+    for cells in groups:
+        outs += [pltpu.VMEM((len(cells), ycount, owned), F32)] * count
+        outs.append(pltpu.VMEM((count, len(cells) * ycount, owned), BF16))
     if with_faces:
         outs += [pltpu.VMEM((count, ycount, owned), BF16)] * 2
     return call(
-        body, "load_chunk", fields, outs, scratch=[pltpu.SemaphoreType.DMA((count, len(cells)))],
+        body, "load_cells", fields, outs, scratch=[pltpu.SemaphoreType.DMA((count, xcount))],
         specs=[FROM_HBM] * count,
     )
 
@@ -117,28 +118,27 @@
     return call(body, "before_first", [*ones, *twos, lo, hi, growth], outs)
 
 
-def early_part(blocks, kernels, new=None, cells=(), xcount=0):
-    rows, owned = blocks[0].shape[0] * blocks[0].shape[1], blocks[0].shape[2]
-    count = len(blocks)
-
-    def body(*refs):
-        block_refs, k_ref = refs[:count], refs[count]
+def early_part(own, sib, far, kernels, new=None, cells=(), xcount=0):
+    fields, size, owned = own.shape
+    rows = fields * size
+
+    def body(own_ref, sib_ref, far_ref, k_ref, *refs):
         copies = []
         if new is None:
-            part_ref = refs[-1]
+            (part_ref,) = refs
         else:
-            new_ref, part_ref, whole_ref, sems = refs[count + 1:]
+            new_ref, part_ref, whole_ref, sems = refs
             copies = [pltpu.make_async_copy(new_ref.at[i], whole_ref.at[x], sems.at[i]) for i, x in enumerate(cells)]
         for copy in copies:
             copy.start()
         me = lax.axis_index("trait")
-        values = [r[...].reshape(rows, owned) for r in block_refs]
-        for k in range(2):
-            part_ref[k] = blocks_dot(values, k_ref, k, [me ^ j for j in range(count)])
+        values = [r[...].reshape(rows, owned) for r in (own_ref, sib_ref, far_ref)]
+        for k in range(2):
+            part_ref[k] = blocks_dot(values, k_ref, k, [me, me ^ 1, me ^ 2])
         for copy in copies:
             copy.wait()
 
-    args = [*blocks, kernels]
+    args = [own, sib, far, kernels]
     outs = [pltpu.VMEM((2, rows, owned), F32)]
     if new is None:
         return call(body, "early_part", args, outs, gflop=20.0)[0]
@@ -149,17 +149,22 @@
     )
 
 
-def first_node(part, last, base, one, two, initial, kernels, death, cells, with_faces):
+def first_node(part, last, base, one, two, initial, kernels, death, cells, with_faces, begun=()):
     xcount, ycount, owned = initial.shape
     rows = len(cells) * ycount
+    count = len(begun)
+    ahead = begun[0].shape[0] if begun else 0
 
     def body(part_ref, last_ref, base_ref, one_ref, two_ref, init_ref, k_ref, d_ref, *refs):
-        new_ref, rounded_ref, rest_ref = refs[:3]
-        sums = refs[-1]
+        begun_refs, (new_ref, rounded_ref, rest_ref, *face_refs, sums) = refs[:count], refs[count:]
         me = lax.axis_index("trait")
         for k in range(2):
             far_part = blocks_dot([last_ref[...].reshape(2 * rows, owned)], k_ref, k, [me ^ 3])
             sums[k] = (part_ref[k] + far_part).astype(BF16)
+        if begun:
+            new_ref[pl.ds(0, ahead)] = begun_refs[0][...]
+            rounded_ref[:, pl.ds(0, ahead * ycount), :] = begun_refs[1][...]
+            rest_ref[pl.ds(0, ahead)] = begun_refs[2][...]
         death = d_ref[...]
         inv_one = 1.0 / (1.0 + FIRST * death)
         inv_two = 1.0 / (1.0 + SECOND * death)
@@ -176,28 +181,26 @@
                 + FIRST * death * cores[0]
                 + STEP_SIZE * (5.0 / 12.0 * full_one - 1.0 / 12.0 * full_two)
             ) * inv_one
-            new_ref[i] = new
+            new_ref[ahead + i] = new
             rounded = new.astype(BF16)
-            rounded_ref[0, i * ycount:(i + 1) * ycount, :] = rounded
-            if with_faces and x == 0:
-                refs[3][0] = rounded
-            if with_faces and x == xcount - 1:
-                refs[4][0] = rounded
-            rest_ref[i] = (
+            rounded_ref[0, pl.ds((ahead + i) * ycount, ycount), :] = rounded
+            if with_faces and x in (0, xcount - 1):
+                face_refs[x != 0][0] = rounded
+            rest_ref[ahead + i] = (
                 new - SECOND * e[0] + SECOND * death * cores[1] + STEP_SIZE / 3.0 * (full_one + full_two)
             ) * inv_two
 
+    size = ahead + len(cells)
     outs = [
-        pltpu.VMEM((len(cells), ycount, owned), F32),
-        pltpu.VMEM((1, rows, owned), BF16),
-        pltpu.VMEM((len(cells), ycount, owned), F32),
+        pltpu.VMEM((size, ycount, owned), F32),
+        pltpu.VMEM((1, size * ycount, owned), BF16),
+        pltpu.VMEM((size, ycount, owned), F32),
     ]
     if with_faces:
         outs += [pltpu.VMEM((1, ycount, owned), BF16)] * 2
-    args = [part, last, base, one, two, initial, kernels, death]
-    return call(
-        body, "first_node", args, outs, scratch=[pltpu.VMEM((2, 2 * rows, owned), BF16)],
-        gflop=0.0,
+    return call(
+        body, "first_node", [part, last, base, one, two, initial, kernels, death, *begun], outs,
+        scratch=[pltpu.VMEM((2, 2 * rows, owned), BF16)],
     )
 
 
@@ -338,40 +341,53 @@
         hi = lax.ppermute(head, "gx", [((i + 1) % gcount, i) for i in range(gcount)])
         return lo, hi
 
-    one_a, two_a, own_a, head, tail = load_chunk((section_one, section_two), chunks[0], True)
+    inputs = (section_one, section_two)
+    outer, inner, ending = chunks
+    one_e, two_e, own_e, head, tail = load_cells(inputs, [outer], True)
+    far_e = to_far(own_e)
+    one_a, two_a, own_a, one_b, two_b, own_b = load_cells((after(section_one, own_e), section_two), [inner, ending], False)
     far_a = to_far(own_a)
-    one_b, two_b, own_b = load_chunk((after(section_one, own_a), section_two), chunks[1], False)
     far_b = to_far(own_b)
     head, tail, kernels = lax.optimization_barrier((head, tail, kernels, own_b))[:3]
     lo, hi = faces(head, tail)
-    base_a, base_b = before_first((one_a, one_b), (two_a, two_b), lo, hi, growth, chunks)
-    sib_a = to_sibling(after(own_a, own_b))
+    sib_e = to_sibling(after(own_e, own_b))
+    sib_a = to_sibling(own_a)
     sib_b = to_sibling(own_b)
-    far_a = after(far_a, base_a)
+    base_e, base_a, base_b = before_first((one_e, one_a, one_b), (two_e, two_a, two_b), lo, hi, growth, chunks)
+
+    far_e = after(far_e, base_e)
+    farsib_e = to_sibling(far_e)
+    part_e = early_part(own_e, sib_e, far_e, kernels)
+    *begun, new_head, new_tail = first_node(
+        part_e, farsib_e, base_e, one_e, two_e, initial, kernels, death, outer, True
+    )
+    new_lo, new_hi = faces(new_head, new_tail)
+
+    far_a = after(far_a, new_lo, new_hi)
     farsib_a = to_sibling(far_a)
-    part_a = early_part([own_a, sib_a, far_a], kernels)
-    new_a, rounded_a, rest_a, new_head, new_tail = first_node(
-        part_a, farsib_a, base_a, one_a, two_a, initial, kernels, death, chunks[0], True
-    )
+    part_a = early_part(own_a, sib_a, far_a, kernels)
+    new_a, rounded_a, rest_a = first_node(
+        part_a, farsib_a, base_a, one_a, two_a, initial, kernels, death, inner, False, begun
+    )
+    chunks = (outer + inner, ending)
     nfar_a = to_far(rounded_a)
     nsib_a = to_sibling(rounded_a)
 
     far_b = after(far_b, rounded_a)
     farsib_b = to_sibling(far_b)
-    part_b, new_one = early_part([own_b, sib_b, far_b], kernels, new_a, chunks[0], xcount)
+    part_b, new_one = early_part(own_b, sib_b, far_b, kernels, new_a, chunks[0], xcount)
     new_b, rounded_b, rest_b = first_node(
         part_b, farsib_b, base_b, one_b, two_b, initial, kernels, death, chunks[1], False
     )
     nfar_b = to_far(rounded_b)
     nsib_b = to_sibling(rounded_b)
-    new_lo, new_hi = faces(*lax.optimization_barrier((new_head, new_tail, rounded_b))[:2])
     nfar_a = after(nfar_a, rounded_b)
     nfarsib_a = to_sibling(nfar_a)
     new_one, npart_a, nbase_a, nbase_b = before_second(
         (new_a, new_b), (rest_a, rest_b), growth, death, new_one, [rounded_a], kernels, chunks
     )
     sums_a = whole_sums(npart_a, [nsib_a, nfar_a, nfarsib_a], after(kernels, nbase_a))
-    nfar_b = after(nfar_b, sums_a, new_lo, new_hi)
+    nfar_b = after(nfar_b, sums_a)
     nfarsib_b = to_sibling(nfar_b)
     begun, npart_b = second_first(
         sums_a, nbase_a, new_a, death, new_lo, new_hi, [rounded_b, nsib_b, nfar_b], kernels, chunks[0], xcount

time: 43.5 us -> 48.8 us (1.12)
  waiting for transfers between devices: 13.1 us -> 21 us
  starting transfers between devices: 17.9 us -> 14.8 us
  Pallas kernels: 11.5 us -> 12 us
    ppermute x4 -> x5, waiting for transfers between devices: 6.53 us -> 11.3 us  [to_far(): return lax.ppermute(v, 'trait', [(i, i ^ 2) for i in range(traits)])]
    ppermute x4 -> x5, starting transfers between devices: 7.68 us -> 5.08 us  [to_far(): return lax.ppermute(v, 'trait', [(i, i ^ 2) for i in range(traits)])]
    ppermute x2, waiting for transfers between devices: 3.62 us -> 5.34 us  [faces(): lax.ppermute(tail, 'gx', [(i, (i + 1) % gcount) for i in range(gcount)])]
    ppermute x8 -> x10, waiting for transfers between devices: 1.7 us -> 3.28 us  [to_sibling(): return lax.ppermute(v, 'trait', [(i, i ^ 1) for i in range(traits)])]
    ppermute x2, starting transfers between devices: 6.46 us -> 7.52 us  [faces(): lax.ppermute(head, 'gx', [((i + 1) % gcount, i) for i in range(gcount)])]
    ppermute x2, starting transfers between devices: 3.03 us -> 2.03 us  [faces(): lax.ppermute(tail, 'gx', [(i, (i + 1) % gcount) for i in range(gcount)])]
    ppermute x8 -> x10, starting transfers between devices: 0.76 us -> 0.16 us  [to_sibling(): return lax.ppermute(v, 'trait', [(i, i ^ 1) for i in range(traits)])]
    pallas_call x11 -> x13, Pallas kernels: 11.5 us -> 12 us  [call(): pl.pallas_call(body, out_shape=outs, in_specs=specs, out_specs=out_specs...]
  transfers between devices with their start and end apart: 16 -> 19, of which waited for: 9 -> 11; matrix products, arithmetic and copies ran while one was open for 0% -> 0% of each run, Pallas kernels for 21% -> 20%
where the time goes in v4:
time: 48.8 us; the launch traced here: 48.6 us
  waiting for transfers between devices  21 us (43%)
  starting transfers between devices  14.8 us (30%)
  Pallas kernels  12 us (25%)
  between operations  0.81 us (2%)
    pallas_call x13, Pallas kernels, call(): pl.pallas_call(body, out_shape=outs, in_specs=specs, out_specs=out_specs...  12 us
    ppermute x5, waiting for transfers between devices, to_far(): return lax.ppermute(v, 'trait', [(i, i ^ 2) for i in range(traits)])  11.3 us
    ppermute x2, starting transfers between devices, faces(): lax.ppermute(head, 'gx', [((i + 1) % gcount, i) for i in range(gcount)])  7.52 us
    ppermute x2, waiting for transfers between devices, faces(): lax.ppermute(tail, 'gx', [(i, (i + 1) % gcount) for i in range(gcount)])  5.34 us
    ppermute x5, starting transfers between devices, to_far(): return lax.ppermute(v, 'trait', [(i, i ^ 2) for i in range(traits)])  5.08 us
    ppermute x10, waiting for transfers between devices, to_sibling(): return lax.ppermute(v, 'trait', [(i, i ^ 1) for i in range(traits)])  3.28 us
    ppermute x2, starting transfers between devices, faces(): lax.ppermute(tail, 'gx', [(i, (i + 1) % gcount) for i in range(gcount)])  2.03 us
    ppermute x2, waiting for transfers between devices, faces(): lax.ppermute(head, 'gx', [((i + 1) % gcount, i) for i in range(gcount)])  1.13 us
  transfers between devices with their start and end apart: 19, of which 11 were waited for; matrix products, arithmetic and copies ran while one was open for 0% of the time, Pallas kernels for 20%

profile of v4, /device:TPU:0, one launch (start us, length us, event | category | flops | bytes accessed | tf_op | source)
XLA Modules:
  0.0 48.6 jit_solution(973742770325356022)
XLA Ops:
  0.6 1.2 %load_cells.2 = (f32[2,128,256]{2,1,0:T(8,128)S(1)}, f32[2,128,256]{2,1,0:T(8,128)S(1)}, bf16[2,256,256]{2,1,0:T(8,128)(2,1)S(1)}, bf16[2,128,256]{2,1,0:T(8,128)(2,1)S(1)}, bf16[2,128,256]{2,1,0:T(8,128)(2,1)S(1)}) custom-call(f32[8,128,256]{2,1,0:T(8,128)} %refs_0_.2, f32[8,128,256]{2,1,0:T(8,128)} %refs_1_.3), custom_call_target="tpu_custom_call" | custom-call | tf_op jit(solution)/shard_map/load_cells/pallas_call | solution.py:36
  1.9 0.0 copy-start.3
  1.9 3.0 %collective-permute-start.3 = (bf16[2,256,256]{2,1,0:T(8,128)(2,1)S(1)}, bf16[2,256,256]{2,1,0:T(8,128)(2,1)S(1)}, u32[]{:S(2)}, u32[]{:S(2)}) collective-permute-start(bf16[2,256,256]{2,1,0:T(8,128)(2,1)S(1)} %get-tuple-element.50.own_ref), channel_id=1, source_target_pairs={{0,2},{1,3},{2,0},{3,1},{4,6},{5,7},{6,4},{7,5},{8,10},{9,11},{10,... | collective-permute-start | bytes 786440 | tf_op jit(solution)/shard_map/ppermute | solution.py:337
  4.9 1.6 %load_cells.3 = (f32[3,128,256]{2,1,0:T(8,128)S(1)}, f32[3,128,256]{2,1,0:T(8,128)S(1)}, bf16[2,384,256]{2,1,0:T(8,128)(2,1)S(1)}, f32[3,128,256]{2,1,0:T(8,128)...) custom-call(f32[8,128,256]{2,1,0:T(8,128)} %refs_0_.2, f32[8,128,256]{2,1,0:T(8,128)} %refs_1_.3), custom_call_target="tpu_custom_call" | custom-call | tf_op jit(solution)/shard_map/load_cells/pallas_call | solution.py:36
  6.5 0.0 copy-start
  6.5 0.1 collective-permute-start.2
  6.6 1.5 %collective-permute-start.4 = (bf16[2,128,256]{2,1,0:T(8,128)(2,1)S(1)}, bf16[2,128,256]{2,1,0:T(8,128)(2,1)S(1)}, u32[]{:S(2)}, u32[]{:S(2)}) collective-permute-start(bf16[2,128,256]{2,1,0:T(8,128)(2,1)S(1)} %get-tuple-element.59), channel_id=1, source_target_pairs={{0,4},{4,8},{8,12},{12,16},{16,20},{20,24},{24,28},{28,0},{1,5},{5... | collective-permute-start | bytes 393224 | tf_op jit(solution)/shard_map/ppermute | solution.py:340
  8.2 3.2 %collective-permute-start.5 = (bf16[2,128,256]{2,1,0:T(8,128)(2,1)S(1)}, bf16[2,128,256]{2,1,0:T(8,128)(2,1)S(1)}, u32[]{:S(2)}, u32[]{:S(2)}) collective-permute-start(bf16[2,128,256]{2,1,0:T(8,128)(2,1)S(1)} %get-tuple-element.60), channel_id=1, source_target_pairs={{4,0},{8,4},{12,8},{16,12},{20,16},{24,20},{28,24},{0,28},{5,1},{9... | collective-permute-start | bytes 393224 | tf_op jit(solution)/shard_map/ppermute | solution.py:341
  11.4 0.4 collective-permute-start.1
  11.8 3.6 %collective-permute-done.4.refs_6_ = bf16[2,128,256]{2,1,0:T(8,128)(2,1)S(1)} collective-permute-done((bf16[2,128,256]{2,1,0:T(8,128)(2,1)S(1)}, bf16[2,128,256]{2,1,0:T(8,128)(2,1)S(1)}, u32[]{:S(2)}, u32[]{:S(2)}) %collective-permute-start.4) | collective-permute-done | bytes 131104 | tf_op jit(solution)/shard_map/ppermute | solution.py:340
  15.4 0.0 collective-permute-start
  15.4 1.1 %collective-permute-done.5.refs_7_ = bf16[2,128,256]{2,1,0:T(8,128)(2,1)S(1)} collective-permute-done((bf16[2,128,256]{2,1,0:T(8,128)(2,1)S(1)}, bf16[2,128,256]{2,1,0:T(8,128)(2,1)S(1)}, u32[]{:S(2)}, u32[]{:S(2)}) %collective-permute-start.5) | collective-permute-done | bytes 131104 | tf_op jit(solution)/shard_map/ppermute | solution.py:341
  16.5 0.9 %before_first.1 = (f32[2,2,128,256]{3,2,1,0:T(8,128)S(1)}, f32[2,3,128,256]{3,2,1,0:T(8,128)S(1)}, f32[2,3,128,256]{3,2,1,0:T(8,128)S(1)}) custom-call(f32[2,128,256]{2,1,0:T(8,128)S(1)} %get-tuple-element.51.refs_0_.one_ref, f32[3,128,256]{2,1,0:T(8,128)S(1)} %get-tuple-element.52.refs_1_.one_ref, f32[3,128,256]{2,1,0:T(8,128)S(1)} %get-tuple-element.53.refs_2_.one_ref, ...), custom_call_target="tpu_custom_call" | custom-call | tf_op jit(solution)/shard_map/before_first/pallas_call | solution.py:36
  17.4 0.0 collective-permute-done.3.far_ref
  17.5 0.0 copy-start.1
  17.5 0.0 copy-start.2
  17.5 0.1 collective-permute-start.6
  17.6 0.0 collective-permute-done.2.sib_ref
  17.6 0.6 %early_part.3.part_ref = f32[2,512,256]{2,1,0:T(8,128)S(1)} custom-call(bf16[2,256,256]{2,1,0:T(8,128)(2,1)S(1)} %get-tuple-element.50.own_ref, bf16[2,256,256]{2,1,0:T(8,128)(2,1)S(1)} %collective-permute-done.2.sib_ref, bf16[2,256,256]{2,1,0:T(8,128)(2,1)S(1)} %collective-permute-done.3.far_ref, bf16[2,1024,256]{2,1,0:T(8,128)(2,1)S(1)} %copy-done), custom_call_target="tpu_custom_call" | custom-call | flops 20000000000 | tf_op jit(solution)/shard_map/early_part/pallas_call | solution.py:36
  18.2 0.9 %collective-permute-done.6.last_ref = bf16[2,256,256]{2,1,0:T(8,128)(2,1)S(1)} collective-permute-done((bf16[2,256,256]{2,1,0:T(8,128)(2,1)S(1)}, bf16[2,256,256]{2,1,0:T(8,128)(2,1)S(1)}, u32[]{:S(2)}, u32[]{:S(2)}) %collective-permute-start.6) | collective-permute-done | bytes 262176 | tf_op jit(solution)/shard_map/ppermute | solution.py:334
  19.1 0.5 %first_node.3 = (f32[2,128,256]{2,1,0:T(8,128)S(1)}, bf16[1,256,256]{2,1,0:T(8,128)(2,1)S(1)}, f32[2,128,256]{2,1,0:T(8,128)S(1)}, bf16[1,128,256]{2,1,0:T(8,128)(2,1)S(1)}, bf16[1,128,256]{2,1,0:T(8,128)(2,1)S(1)}) custom-call(f32[2,512,256]{2,1,0:T(8,128)S(1)} %early_part.3.part_ref, bf16[2,256,256]{2,1,0:T(8,128)(2,1)S(1)} %collective-permute-done.6.last_ref, ...), custom_call_target="tpu_custom_call" | custom-call | tf_op jit(solution)/shard_map/first_node/pallas_call | solution.py:36
  19.6 0.5 collective-permute-start.7
  20.1 4.3 %collective-permute-start.8 = (bf16[1,128,256]{2,1,0:T(8,128)(2,1)S(1)}, bf16[1,128,256]{2,1,0:T(8,128)(2,1)S(1)}, u32[]{:S(2)}, u32[]{:S(2)}) collective-permute-start(bf16[1,128,256]{2,1,0:T(8,128)(2,1)S(1)} %get-tuple-element.65), channel_id=1, source_target_pairs={{4,0},{8,4},{12,8},{16,12},{20,16},{24,20},{28,24},{0,28},{5,1},{9... | collective-permute-start | bytes 196616 | tf_op jit(solution)/shard_map/ppermute | solution.py:341
  24.4 0.5 %collective-permute-start.11 = (bf16[2,384,256]{2,1,0:T(8,128)(2,1)S(1)}, bf16[2,384,256]{2,1,0:T(8,128)(2,1)S(1)}, u32[]{:S(2)}, u32[]{:S(2)}) collective-permute-start(bf16[2,384,256]{2,1,0:T(8,128)(2,1)S(1)} %get-tuple-element.49.own_ref), channel_id=1, source_target_pairs={{0,2},{1,3},{2,0},{3,1},{4,6},{5,7},{6,4},{7,5},{8,10},{9,11},{10,... | collective-permute-start | bytes 1179656 | tf_op jit(solution)/shard_map/ppermute | solution.py:337
  24.9 0.0 collective-permute-done.1.far_ref
  24.9 0.0 collective-permute-start.10
  24.9 1.7 %collective-permute-done.7.lo_ref = bf16[1,128,256]{2,1,0:T(8,128)(2,1)S(1)} collective-permute-done((bf16[1,128,256]{2,1,0:T(8,128)(2,1)S(1)}, bf16[1,128,256]{2,1,0:T(8,128)(2,1)S(1)}, u32[]{:S(2)}, u32[]{:S(2)}) %collective-permute-start.7) | collective-permute-done | bytes 65568 | tf_op jit(solution)/shard_map/ppermute | solution.py:340
  26.6 0.8 %early_part.4.part_ref = f32[2,768,256]{2,1,0:T(8,128)S(1)} custom-call(bf16[2,384,256]{2,1,0:T(8,128)(2,1)S(1)} %get-tuple-element.48.own_ref, bf16[2,384,256]{2,1,0:T(8,128)(2,1)S(1)} %collective-permute-done.sib_ref, bf16[2,384,256]{2,1,0:T(8,128)(2,1)S(1)} %collective-permute-done.1.far_ref, bf16[2,1024,256]{2,1,0:T(8,128)(2,1)S(1)} %copy-done), custom_call_target="tpu_custom_call" | custom-call | flops 20000000000 | tf_op jit(solution)/shard_map/early_part/pallas_call | solution.py:36
  27.4 0.9 %collective-permute-done.9.last_ref = bf16[2,384,256]{2,1,0:T(8,128)(2,1)S(1)} collective-permute-done((bf16[2,384,256]{2,1,0:T(8,128)(2,1)S(1)}, bf16[2,384,256]{2,1,0:T(8,128)(2,1)S(1)}, u32[]{:S(2)}, u32[]{:S(2)}) %collective-permute-start.9) | collective-permute-done | bytes 393248 | tf_op jit(solution)/shard_map/ppermute | solution.py:334
  28.3 0.7 %first_node.4 = (f32[5,128,256]{2,1,0:T(8,128)S(1)}, bf16[1,640,256]{2,1,0:T(8,128)(2,1)S(1)}, f32[5,128,256]{2,1,0:T(8,128)S(1)}) custom-call(f32[2,768,256]{2,1,0:T(8,128)S(1)} %early_part.4.part_ref, bf16[2,384,256]{2,1,0:T(8,128)(2,1)S(1)} %collective-permute-done.9.last_ref, f32[2,3,128,256]{3,2,1,0:T(8,128)S(1)} %get-tuple-element.67.base_ref, ...), custom_call_target="tpu_custom_call" | custom-call | tf_op jit(solution)/shard_map/first_node/pallas_call | solution.py:36
  29.0 0.6 %collective-permute-start.14 = (bf16[1,640,256]{2,1,0:T(8,128)(2,1)S(1)}, bf16[1,640,256]{2,1,0:T(8,128)(2,1)S(1)}, u32[]{:S(2)}, u32[]{:S(2)}) collective-permute-start(bf16[1,640,256]{2,1,0:T(8,128)(2,1)S(1)} %get-tuple-element.72.refs_4_), channel_id=1, source_target_pairs={{0,2},{1,3},{2,0},{3,1},{4,6},{5,7},{6,4},{7,5},{8,10},{9,11},{10,... | collective-permute-start | bytes 983048 | tf_op jit(solution)/shard_map/ppermute | solution.py:337
  29.6 0.0 collective-permute-start.13
  29.6 6.8 %collective-permute-done.11.far_ref = bf16[2,384,256]{2,1,0:T(8,128)(2,1)S(1)} collective-permute-done((bf16[2,384,256]{2,1,0:T(8,128)(2,1)S(1)}, bf16[2,384,256]{2,1,0:T(8,128)(2,1)S(1)}, u32[]{:S(2)}, u32[]{:S(2)}) %collective-permute-start.11) | collective-permute-done | bytes 393248 | tf_op jit(solution)/shard_map/ppermute | solution.py:337
  36.4 0.0 collective-permute-start.12
  36.4 0.0 collective-permute-done.10.sib_ref
  36.4 1.0 %early_part.5 = (f32[2,768,256]{2,1,0:T(8,128)S(1)}, f32[8,128,256]{2,1,0:T(8,128)}) custom-call(bf16[2,384,256]{2,1,0:T(8,128)(2,1)S(1)} %get-tuple-element.49.own_ref, bf16[2,384,256]{2,1,0:T(8,128)(2,1)S(1)} %collective-permute-done.10.sib_ref, bf16[2,384,256]{2,1,0:T(8,128)(2,1)S(1)} %collective-permute-done.11.far_ref, ...), custom_call_target="tpu_custom_call" | custom-call | flops 20000000000 | tf_op jit(solution)/shard_map/early_part/pallas_call | solution.py:36
  37.5 0.7 %collective-permute-done.12.last_ref = bf16[2,384,256]{2,1,0:T(8,128)(2,1)S(1)} collective-permute-done((bf16[2,384,256]{2,1,0:T(8,128)(2,1)S(1)}, bf16[2,384,256]{2,1,0:T(8,128)(2,1)S(1)}, u32[]{:S(2)}, u32[]{:S(2)}) %collective-permute-start.12) | collective-permute-done | bytes 393248 | tf_op jit(solution)/shard_map/ppermute | solution.py:334
  38.1 0.7 %first_node.5 = (f32[3,128,256]{2,1,0:T(8,128)S(1)}, bf16[1,384,256]{2,1,0:T(8,128)(2,1)S(1)}, f32[3,128,256]{2,1,0:T(8,128)S(1)}) custom-call(f32[2,768,256]{2,1,0:T(8,128)S(1)} %get-tuple-element.74.part_ref, bf16[2,384,256]{2,1,0:T(8,128)(2,1)S(1)} %collective-permute-done.12.last_ref, f32[2,3,128,256]{3,2,1,0:T(8,128)S(1)} %get-tuple-element.75.base_ref, ...), custom_call_target="tpu_custom_call" | custom-call | tf_op jit(solution)/shard_map/first_node/pallas_call | solution.py:36
  38.8 0.6 %collective-permute-start.17 = (bf16[1,384,256]{2,1,0:T(8,128)(2,1)S(1)}, bf16[1,384,256]{2,1,0:T(8,128)(2,1)S(1)}, u32[]{:S(2)}, u32[]{:S(2)}) collective-permute-start(bf16[1,384,256]{2,1,0:T(8,128)(2,1)S(1)} %get-tuple-element.82.refs_0_), channel_id=1, source_target_pairs={{0,2},{1,3},{2,0},{3,1},{4,6},{5,7},{6,4},{7,5},{8,10},{9,11},{10,... | collective-permute-start | bytes 589832 | tf_op jit(solution)/shard_map/ppermute | solution.py:337
  39.4 2.9 %collective-permute-done.14.far_ref = bf16[1,640,256]{2,1,0:T(8,128)(2,1)S(1)} collective-permute-done((bf16[1,640,256]{2,1,0:T(8,128)(2,1)S(1)}, bf16[1,640,256]{2,1,0:T(8,128)(2,1)S(1)}, u32[]{:S(2)}, u32[]{:S(2)}) %collective-permute-start.14) | collective-permute-done | bytes 327712 | tf_op jit(solution)/shard_map/ppermute | solution.py:337
  42.3 0.0 collective-permute-start.15
  42.3 0.9 %before_second.1 = (f32[8,128,256]{2,1,0:T(8,128)}, f32[2,640,256]{2,1,0:T(8,128)S(1)}, f32[5,128,256]{2,1,0:T(8,128)S(1)}, f32[3,128,256]{2,1,0:T(8,128)S(1)}) custom-call(f32[5,128,256]{2,1,0:T(8,128)S(1)} %get-tuple-element.71.refs_0_.new_ref, f32[3,128,256]{2,1,0:T(8,128)S(1)} %get-tuple-element.76.refs_1_.new_ref, ...), custom_call_target="tpu_custom_call", output_to_operand_aliasing={{0}: (8, {})} | custom-call | flops 20000000000 | tf_op jit(solution)/shard_map/before_second/pallas_call | solution.py:36
  43.3 0.7 %collective-permute-done.15.farsib_ref = bf16[1,640,256]{2,1,0:T(8,128)(2,1)S(1)} collective-permute-done((bf16[1,640,256]{2,1,0:T(8,128)(2,1)S(1)}, bf16[1,640,256]{2,1,0:T(8,128)(2,1)S(1)}, u32[]{:S(2)}, u32[]{:S(2)}) %collective-permute-start.15) | collective-permute-done | bytes 327712 | tf_op jit(solution)/shard_map/ppermute | solution.py:334
  43.9 0.7 %whole_sums.1.sums_ref = bf16[2,640,256]{2,1,0:T(8,128)(2,1)S(1)} custom-call(f32[2,640,256]{2,1,0:T(8,128)S(1)} %get-tuple-element.81.part_ref, bf16[1,640,256]{2,1,0:T(8,128)(2,1)S(1)} %collective-permute-done.13.sib_ref, bf16[1,640,256]{2,1,0:T(8,128)(2,1)S(1)} %collective-permute-done.14.far_ref, ...), custom_call_target="tpu_custom_call" | custom-call | tf_op jit(solution)/shard_map/whole_sums/pallas_call | solution.py:36
  44.6 1.6 %collective-permute-done.17.refs_2_ = bf16[1,384,256]{2,1,0:T(8,128)(2,1)S(1)} collective-permute-done((bf16[1,384,256]{2,1,0:T(8,128)(2,1)S(1)}, bf16[1,384,256]{2,1,0:T(8,128)(2,1)S(1)}, u32[]{:S(2)}, u32[]{:S(2)}) %collective-permute-start.17) | collective-permute-done | bytes 196640 | tf_op jit(solution)/shard_map/ppermute | solution.py:337
  46.2 1.3 %second_first.1 = (f32[8,128,256]{2,1,0:T(8,128)}, f32[2,384,256]{2,1,0:T(8,128)S(1)}) custom-call(bf16[2,640,256]{2,1,0:T(8,128)(2,1)S(1)} %whole_sums.1.sums_ref, f32[5,128,256]{2,1,0:T(8,128)S(1)} %get-tuple-element.84.base_ref, f32[5,128,256]{2,1,0:T(8,128)S(1)} %get-tuple-element.71.refs_0_.new_ref, f32[1,256]{1,0:T(1,128)S(1)} %bitcast.6, ...), custom_call_target="tpu_custom_call" | custom-call | tf_op jit(solution)/shard_map/second_first/pallas_call | solution.py:36
  47.5 0.1 collective-permute-done.18.last_ref
  47.7 1.0 %second_last.1 = f32[8,128,256]{2,1,0:T(8,128)} custom-call(f32[2,384,256]{2,1,0:T(8,128)S(1)} %get-tuple-element.87.part_ref, bf16[1,384,256]{2,1,0:T(8,128)(2,1)S(1)} %collective-permute-done.18.last_ref, f32[3,128,256]{2,1,0:T(8,128)S(1)} %get-tuple-element.88.base_ref, ...), custom_call_target="tpu_custom_call", output_to_operand_aliasing={{}: (6, {})} | custom-call | tf_op jit(solution)/shard_map/second_last/pallas_call | solution.py:36
  (11 shorter events, 0.0 us)
Async XLA Ops:
  1.9 14.6 %copy-start.3 = (f32[256]{0:T(256)S(1)}, f32[256]{0:T(256)}, u32[]{:S(2)}) copy-start(f32[256]{0:T(256)} %param.10) | copy-start | bytes 3076
  1.9 15.6 %collective-permute-start.3 = (bf16[2,256,256]{2,1,0:T(8,128)(2,1)S(1)}, bf16[2,256,256]{2,1,0:T(8,128)(2,1)S(1)}, u32[]{:S(2)}, u32[]{:S(2)}) collective-permute-start(bf16[2,256,256]{2,1,0:T(8,128)(2,1)S(1)} %get-tuple-element.50.own_ref), channel_id=1, source_target_pairs={{0,2},{1,3},{2,0},{3,1},{4,6},{5,7},{6,4},{7,5},{8,10},{9,11},{10,... | collective-permute-start | bytes 786440 | tf_op jit(solution)/shard_map/ppermute | solution.py:337
  6.5 11.1 %copy-start = (bf16[2,1024,256]{2,1,0:T(8,128)(2,1)S(1)}, bf16[2,1024,256]{2,1,0:T(8,128)(2,1)}, u32[]{:S(2)}) copy-start(bf16[2,1024,256]{2,1,0:T(8,128)(2,1)} %k_ref.8) | copy-start | bytes 3145732
  6.5 11.0 %collective-permute-start.2 = (bf16[2,256,256]{2,1,0:T(8,128)(2,1)S(1)}, bf16[2,256,256]{2,1,0:T(8,128)(2,1)S(1)}, u32[]{:S(2)}, u32[]{:S(2)}) collective-permute-start(bf16[2,256,256]{2,1,0:T(8,128)(2,1)S(1)} %get-tuple-element.50.own_ref), channel_id=1, source_target_pairs={{0,1},{1,0},{2,3},{3,2},{4,5},{5,4},{6,7},{7,6},{8,9},{9,8},{10,11... | collective-permute-start | bytes 786440 | tf_op jit(solution)/shard_map/ppermute | solution.py:334
  6.6 8.8 %collective-permute-start.4 = (bf16[2,128,256]{2,1,0:T(8,128)(2,1)S(1)}, bf16[2,128,256]{2,1,0:T(8,128)(2,1)S(1)}, u32[]{:S(2)}, u32[]{:S(2)}) collective-permute-start(bf16[2,128,256]{2,1,0:T(8,128)(2,1)S(1)} %get-tuple-element.59), channel_id=1, source_target_pairs={{0,4},{4,8},{8,12},{12,16},{16,20},{20,24},{24,28},{28,0},{1,5},{5... | collective-permute-start | bytes 393224 | tf_op jit(solution)/shard_map/ppermute | solution.py:340
  8.2 8.4 %collective-permute-start.5 = (bf16[2,128,256]{2,1,0:T(8,128)(2,1)S(1)}, bf16[2,128,256]{2,1,0:T(8,128)(2,1)S(1)}, u32[]{:S(2)}, u32[]{:S(2)}) collective-permute-start(bf16[2,128,256]{2,1,0:T(8,128)(2,1)S(1)} %get-tuple-element.60), channel_id=1, source_target_pairs={{4,0},{8,4},{12,8},{16,12},{20,16},{24,20},{28,24},{0,28},{5,1},{9... | collective-permute-start | bytes 393224 | tf_op jit(solution)/shard_map/ppermute | solution.py:341
  11.4 13.5 %collective-permute-start.1 = (bf16[2,384,256]{2,1,0:T(8,128)(2,1)S(1)}, bf16[2,384,256]{2,1,0:T(8,128)(2,1)S(1)}, u32[]{:S(2)}, u32[]{:S(2)}) collective-permute-start(bf16[2,384,256]{2,1,0:T(8,128)(2,1)S(1)} %get-tuple-element.48.own_ref), channel_id=1, source_target_pairs={{0,2},{1,3},{2,0},{3,1},{4,6},{5,7},{6,4},{7,5},{8,10},{9,11},{10,... | collective-permute-start | bytes 1179656 | tf_op jit(solution)/shard_map/ppermute | solution.py:337
  15.4 11.2 %collective-permute-start = (bf16[2,384,256]{2,1,0:T(8,128)(2,1)S(1)}, bf16[2,384,256]{2,1,0:T(8,128)(2,1)S(1)}, u32[]{:S(2)}, u32[]{:S(2)}) collective-permute-start(bf16[2,384,256]{2,1,0:T(8,128)(2,1)S(1)} %get-tuple-element.48.own_ref), channel_id=1, source_target_pairs={{0,1},{1,0},{2,3},{3,2},{4,5},{5,4},{6,7},{7,6},{8,9},{9,8},{10,11... | collective-permute-start | bytes 1179656 | tf_op jit(solution)/shard_map/ppermute | solution.py:334
  17.5 1.6 %copy-start.1 = (f32[8,128,256]{2,1,0:T(8,128)S(1)}, f32[8,128,256]{2,1,0:T(8,128)}, u32[]{:S(2)}) copy-start(f32[8,128,256]{2,1,0:T(8,128)} %init_ref.5) | copy-start | bytes 3145732
  17.5 1.6 %copy-start.2 = (f32[256]{0:T(256)S(1)}, f32[256]{0:T(256)}, u32[]{:S(2)}) copy-start(f32[256]{0:T(256)} %param.11) | copy-start | bytes 3076
  17.5 1.6 %collective-permute-start.6 = (bf16[2,256,256]{2,1,0:T(8,128)(2,1)S(1)}, bf16[2,256,256]{2,1,0:T(8,128)(2,1)S(1)}, u32[]{:S(2)}, u32[]{:S(2)}) collective-permute-start(bf16[2,256,256]{2,1,0:T(8,128)(2,1)S(1)} %collective-permute-done.3.far_ref), channel_id=1, source_target_pairs={{0,1},{1,0},{2,3},{3,2},{4,5},{5,4},{6,7},{7,6},{8,9},{9,8},{10,11... | collective-permute-start | bytes 786440 | tf_op jit(solution)/shard_map/ppermute | solution.py:334
  19.6 7.0 %collective-permute-start.7 = (bf16[1,128,256]{2,1,0:T(8,128)(2,1)S(1)}, bf16[1,128,256]{2,1,0:T(8,128)(2,1)S(1)}, u32[]{:S(2)}, u32[]{:S(2)}) collective-permute-start(bf16[1,128,256]{2,1,0:T(8,128)(2,1)S(1)} %get-tuple-element.64), channel_id=1, source_target_pairs={{0,4},{4,8},{8,12},{12,16},{16,20},{20,24},{24,28},{28,0},{1,5},{5... | collective-permute-start | bytes 196616 | tf_op jit(solution)/shard_map/ppermute | solution.py:340
  20.1 6.5 %collective-permute-start.8 = (bf16[1,128,256]{2,1,0:T(8,128)(2,1)S(1)}, bf16[1,128,256]{2,1,0:T(8,128)(2,1)S(1)}, u32[]{:S(2)}, u32[]{:S(2)}) collective-permute-start(bf16[1,128,256]{2,1,0:T(8,128)(2,1)S(1)} %get-tuple-element.65), channel_id=1, source_target_pairs={{4,0},{8,4},{12,8},{16,12},{20,16},{24,20},{28,24},{0,28},{5,1},{9... | collective-permute-start | bytes 196616 | tf_op jit(solution)/shard_map/ppermute | solution.py:341
  24.4 12.0 %collective-permute-start.11 = (bf16[2,384,256]{2,1,0:T(8,128)(2,1)S(1)}, bf16[2,384,256]{2,1,0:T(8,128)(2,1)S(1)}, u32[]{:S(2)}, u32[]{:S(2)}) collective-permute-start(bf16[2,384,256]{2,1,0:T(8,128)(2,1)S(1)} %get-tuple-element.49.own_ref), channel_id=1, source_target_pairs={{0,2},{1,3},{2,0},{3,1},{4,6},{5,7},{6,4},{7,5},{8,10},{9,11},{10,... | collective-permute-start | bytes 1179656 | tf_op jit(solution)/shard_map/ppermute | solution.py:337
  24.9 11.5 %collective-permute-start.10 = (bf16[2,384,256]{2,1,0:T(8,128)(2,1)S(1)}, bf16[2,384,256]{2,1,0:T(8,128)(2,1)S(1)}, u32[]{:S(2)}, u32[]{:S(2)}) collective-permute-start(bf16[2,384,256]{2,1,0:T(8,128)(2,1)S(1)} %get-tuple-element.49.own_ref), channel_id=1, source_target_pairs={{0,1},{1,0},{2,3},{3,2},{4,5},{5,4},{6,7},{7,6},{8,9},{9,8},{10,11... | collective-permute-start | bytes 1179656 | tf_op jit(solution)/shard_map/ppermute | solution.py:334
  26.6 1.7 %collective-permute-start.9 = (bf16[2,384,256]{2,1,0:T(8,128)(2,1)S(1)}, bf16[2,384,256]{2,1,0:T(8,128)(2,1)S(1)}, u32[]{:S(2)}, u32[]{:S(2)}) collective-permute-start(bf16[2,384,256]{2,1,0:T(8,128)(2,1)S(1)} %collective-permute-done.1.far_ref), channel_id=1, source_target_pairs={{0,1},{1,0},{2,3},{3,2},{4,5},{5,4},{6,7},{7,6},{8,9},{9,8},{10,11... | collective-permute-start | bytes 1179656 | tf_op jit(solution)/shard_map/ppermute | solution.py:334
  29.0 13.2 %collective-permute-start.14 = (bf16[1,640,256]{2,1,0:T(8,128)(2,1)S(1)}, bf16[1,640,256]{2,1,0:T(8,128)(2,1)S(1)}, u32[]{:S(2)}, u32[]{:S(2)}) collective-permute-start(bf16[1,640,256]{2,1,0:T(8,128)(2,1)S(1)} %get-tuple-element.72.refs_4_), channel_id=1, source_target_pairs={{0,2},{1,3},{2,0},{3,1},{4,6},{5,7},{6,4},{7,5},{8,10},{9,11},{10,... | collective-permute-start | bytes 983048 | tf_op jit(solution)/shard_map/ppermute | solution.py:337
  29.6 13.6 %collective-permute-start.13 = (bf16[1,640,256]{2,1,0:T(8,128)(2,1)S(1)}, bf16[1,640,256]{2,1,0:T(8,128)(2,1)S(1)}, u32[]{:S(2)}, u32[]{:S(2)}) collective-permute-start(bf16[1,640,256]{2,1,0:T(8,128)(2,1)S(1)} %get-tuple-element.72.refs_4_), channel_id=1, source_target_pairs={{0,1},{1,0},{2,3},{3,2},{4,5},{5,4},{6,7},{7,6},{8,9},{9,8},{10,11... | collective-permute-start | bytes 983048 | tf_op jit(solution)/shard_map/ppermute | solution.py:334
  36.4 1.7 %collective-permute-start.12 = (bf16[2,384,256]{2,1,0:T(8,128)(2,1)S(1)}, bf16[2,384,256]{2,1,0:T(8,128)(2,1)S(1)}, u32[]{:S(2)}, u32[]{:S(2)}) collective-permute-start(bf16[2,384,256]{2,1,0:T(8,128)(2,1)S(1)} %collective-permute-done.11.far_ref), channel_id=1, source_target_pairs={{0,1},{1,0},{2,3},{3,2},{4,5},{5,4},{6,7},{7,6},{8,9},{9,8},{10,11... | collective-permute-start | bytes 1179656 | tf_op jit(solution)/shard_map/ppermute | solution.py:334
  38.8 7.4 %collective-permute-start.17 = (bf16[1,384,256]{2,1,0:T(8,128)(2,1)S(1)}, bf16[1,384,256]{2,1,0:T(8,128)(2,1)S(1)}, u32[]{:S(2)}, u32[]{:S(2)}) collective-permute-start(bf16[1,384,256]{2,1,0:T(8,128)(2,1)S(1)} %get-tuple-element.82.refs_0_), channel_id=1, source_target_pairs={{0,2},{1,3},{2,0},{3,1},{4,6},{5,7},{6,4},{7,5},{8,10},{9,11},{10,... | collective-permute-start | bytes 589832 | tf_op jit(solution)/shard_map/ppermute | solution.py:337
  39.4 6.8 %collective-permute-start.16 = (bf16[1,384,256]{2,1,0:T(8,128)(2,1)S(1)}, bf16[1,384,256]{2,1,0:T(8,128)(2,1)S(1)}, u32[]{:S(2)}, u32[]{:S(2)}) collective-permute-start(bf16[1,384,256]{2,1,0:T(8,128)(2,1)S(1)} %get-tuple-element.82.refs_0_), channel_id=1, source_target_pairs={{0,1},{1,0},{2,3},{3,2},{4,5},{5,4},{6,7},{7,6},{8,9},{9,8},{10,11... | collective-permute-start | bytes 589832 | tf_op jit(solution)/shard_map/ppermute | solution.py:334
  42.3 1.6 %collective-permute-start.15 = (bf16[1,640,256]{2,1,0:T(8,128)(2,1)S(1)}, bf16[1,640,256]{2,1,0:T(8,128)(2,1)S(1)}, u32[]{:S(2)}, u32[]{:S(2)}) collective-permute-start(bf16[1,640,256]{2,1,0:T(8,128)(2,1)S(1)} %collective-permute-done.14.far_ref), channel_id=1, source_target_pairs={{0,1},{1,0},{2,3},{3,2},{4,5},{5,4},{6,7},{7,6},{8,9},{9,8},{10,11... | collective-permute-start | bytes 983048 | tf_op jit(solution)/shard_map/ppermute | solution.py:334
  46.2 1.4 %collective-permute-start.18 = (bf16[1,384,256]{2,1,0:T(8,128)(2,1)S(1)}, bf16[1,384,256]{2,1,0:T(8,128)(2,1)S(1)}, u32[]{:S(2)}, u32[]{:S(2)}) collective-permute-start(bf16[1,384,256]{2,1,0:T(8,128)(2,1)S(1)} %collective-permute-done.17.refs_2_), channel_id=1, source_target_pairs={{0,1},{1,0},{2,3},{3,2},{4,5},{5,4},{6,7},{7,6},{8,9},{9,8},{10,11... | collective-permute-start | bytes 589832 | tf_op jit(solution)/shard_map/ppermute | solution.py:334

commit v5 on v3

--- a/solution.py
+++ b/solution.py
@@ -333,17 +333,18 @@
     def to_far(v):
         return lax.ppermute(v, "trait", [(i, i ^ 2) for i in range(traits)])
 
-    def faces(head, tail):
-        lo = lax.ppermute(tail, "gx", [(i, (i + 1) % gcount) for i in range(gcount)])
-        hi = lax.ppermute(head, "gx", [((i + 1) % gcount, i) for i in range(gcount)])
-        return lo, hi
+    def from_below(tail):
+        return lax.ppermute(tail, "gx", [(i, (i + 1) % gcount) for i in range(gcount)])
+
+    def from_above(head):
+        return lax.ppermute(head, "gx", [((i + 1) % gcount, i) for i in range(gcount)])
 
     one_a, two_a, own_a, head, tail = load_chunk((section_one, section_two), chunks[0], True)
     far_a = to_far(own_a)
     one_b, two_b, own_b = load_chunk((after(section_one, own_a), section_two), chunks[1], False)
     far_b = to_far(own_b)
     head, tail, kernels = lax.optimization_barrier((head, tail, kernels, own_b))[:3]
-    lo, hi = faces(head, tail)
+    lo, hi = from_below(tail), from_above(head)
     base_a, base_b = before_first((one_a, one_b), (two_a, two_b), lo, hi, growth, chunks)
     sib_a = to_sibling(after(own_a, own_b))
     sib_b = to_sibling(own_b)
@@ -356,7 +357,8 @@
     nfar_a = to_far(rounded_a)
     nsib_a = to_sibling(rounded_a)
 
-    far_b = after(far_b, rounded_a)
+    new_hi = from_above(new_head)
+    far_b = after(far_b, rounded_a, new_hi)
     farsib_b = to_sibling(far_b)
     part_b, new_one = early_part([own_b, sib_b, far_b], kernels, new_a, chunks[0], xcount)
     new_b, rounded_b, rest_b = first_node(
@@ -364,14 +366,14 @@
     )
     nfar_b = to_far(rounded_b)
     nsib_b = to_sibling(rounded_b)
-    new_lo, new_hi = faces(*lax.optimization_barrier((new_head, new_tail, rounded_b))[:2])
+    new_lo = from_below(after(new_tail, rounded_b))
     nfar_a = after(nfar_a, rounded_b)
     nfarsib_a = to_sibling(nfar_a)
     new_one, npart_a, nbase_a, nbase_b = before_second(
         (new_a, new_b), (rest_a, rest_b), growth, death, new_one, [rounded_a], kernels, chunks
     )
     sums_a = whole_sums(npart_a, [nsib_a, nfar_a, nfarsib_a], after(kernels, nbase_a))
-    nfar_b = after(nfar_b, sums_a, new_lo, new_hi)
+    nfar_b = after(nfar_b, sums_a, new_lo)
     nfarsib_b = to_sibling(nfar_b)
     begun, npart_b = second_first(
         sums_a, nbase_a, new_a, death, new_lo, new_hi, [rounded_b, nsib_b, nfar_b], kernels, chunks[0], xcount

time: 43.5 us -> 45.3 us (1.041)
  waiting for transfers between devices: 13.1 us -> 16 us
  starting transfers between devices: 17.9 us -> 16.8 us
    ppermute x4, waiting for transfers between devices: 6.53 us -> 7.83 us  [to_far(): return lax.ppermute(v, 'trait', [(i, i ^ 2) for i in range(traits)])]
    ppermute x4, starting transfers between devices: 7.68 us -> 6.45 us  [to_far(): return lax.ppermute(v, 'trait', [(i, i ^ 2) for i in range(traits)])]
    ppermute x4, waiting for transfers between devices: 4.85 us -> 5.95 us  [the longest x2 4.44 us: from_below(): lax.ppermute(tail, 'gx', [(i, (i + 1) % gcount) for i in range(gcount)])]
    ppermute x4, starting transfers between devices: 9.5 us -> 10.1 us  [the longest x2 8.35 us: from_above(): lax.ppermute(head, 'gx', [((i + 1) % gcount, i) for i in range(gcount)])]
    ppermute x8, waiting for transfers between devices: 1.7 us -> 2.26 us  [to_sibling(): return lax.ppermute(v, 'trait', [(i, i ^ 1) for i in range(traits)])]
    ppermute x8, starting transfers between devices: 0.76 us -> 0.22 us  [to_sibling(): return lax.ppermute(v, 'trait', [(i, i ^ 1) for i in range(traits)])]
  transfers between devices with their start and end apart: 16 -> 16, of which waited for: 9 -> 10; matrix products, arithmetic and copies ran while one was open for 0% -> 0% of each run, Pallas kernels for 21% -> 20%
where the time goes in v5:
time: 45.3 us; the launch traced here: 45.2 us
  starting transfers between devices  16.8 us (37%)
  waiting for transfers between devices  16 us (35%)
  Pallas kernels  11.5 us (25%)
  between operations  0.77 us (2%)
    pallas_call x11, Pallas kernels, call(): pl.pallas_call(body, out_shape=outs, in_specs=specs, out_specs=out_specs...  11.5 us
    ppermute x2, starting transfers between devices, from_above(): lax.ppermute(head, 'gx', [((i + 1) % gcount, i) for i in range(gcount)])  8.35 us
    ppermute x4, waiting for transfers between devices, to_far(): return lax.ppermute(v, 'trait', [(i, i ^ 2) for i in range(traits)])  7.83 us
    ppermute x4, starting transfers between devices, to_far(): return lax.ppermute(v, 'trait', [(i, i ^ 2) for i in range(traits)])  6.45 us
    ppermute x2, waiting for transfers between devices, from_below(): lax.ppermute(tail, 'gx', [(i, (i + 1) % gcount) for i in range(gcount)])  4.44 us
    ppermute x8, waiting for transfers between devices, to_sibling(): return lax.ppermute(v, 'trait', [(i, i ^ 1) for i in range(traits)])  2.26 us
    ppermute x2, starting transfers between devices, from_below(): lax.ppermute(tail, 'gx', [(i, (i + 1) % gcount) for i in range(gcount)])  1.76 us
    ppermute x2, waiting for transfers between devices, from_above(): lax.ppermute(head, 'gx', [((i + 1) % gcount, i) for i in range(gcount)])  1.51 us
  transfers between devices with their start and end apart: 16, of which 10 were waited for; matrix products, arithmetic and copies ran while one was open for 0% of the time, Pallas kernels for 20%

profile of v5, /device:TPU:0, one launch (start us, length us, event | category | flops | bytes accessed | tf_op | source)
XLA Modules:
  0.0 45.2 jit_solution(6543720539822943762)
XLA Ops:
  0.6 1.5 %load_chunk.2 = (f32[5,128,256]{2,1,0:T(8,128)S(1)}, f32[5,128,256]{2,1,0:T(8,128)S(1)}, bf16[2,640,256]{2,1,0:T(8,128)(2,1)S(1)}, bf16[2,128,256]{2,1,0:T(8,128)(2,1)S(1)}, bf16[2,128,256]{2,1,0:T(8,128)(2,1)S(1)}) custom-call(f32[8,128,256]{2,1,0:T(8,128)} %refs_0_.2, f32[8,128,256]{2,1,0:T(8,128)} %refs_1_.3), custom_call_target="tpu_custom_call" | custom-call | tf_op jit(solution)/shard_map/load_chunk/pallas_call | solution.py:37
  2.1 0.0 copy-start.3
  2.1 3.0 %collective-permute-start.1 = (bf16[2,640,256]{2,1,0:T(8,128)(2,1)S(1)}, bf16[2,640,256]{2,1,0:T(8,128)(2,1)S(1)}, u32[]{:S(2)}, u32[]{:S(2)}) collective-permute-start(bf16[2,640,256]{2,1,0:T(8,128)(2,1)S(1)} %get-tuple-element.42.refs_0_), channel_id=1, source_target_pairs={{0,2},{1,3},{2,0},{3,1},{4,6},{5,7},{6,4},{7,5},{8,10},{9,11},{10,... | collective-permute-start | bytes 1966088 | tf_op jit(solution)/shard_map/ppermute | solution.py:334
  5.1 1.3 %load_chunk.3 = (f32[3,128,256]{2,1,0:T(8,128)S(1)}, f32[3,128,256]{2,1,0:T(8,128)S(1)}, bf16[2,384,256]{2,1,0:T(8,128)(2,1)S(1)}) custom-call(f32[8,128,256]{2,1,0:T(8,128)} %refs_0_.2, f32[8,128,256]{2,1,0:T(8,128)} %refs_1_.3), custom_call_target="tpu_custom_call" | custom-call | tf_op jit(solution)/shard_map/load_chunk/pallas_call | solution.py:37
  6.4 0.0 copy-start
  6.4 0.1 collective-permute-start
  6.5 1.5 %collective-permute-start.2 = (bf16[2,128,256]{2,1,0:T(8,128)(2,1)S(1)}, bf16[2,128,256]{2,1,0:T(8,128)(2,1)S(1)}, u32[]{:S(2)}, u32[]{:S(2)}) collective-permute-start(bf16[2,128,256]{2,1,0:T(8,128)(2,1)S(1)} %get-tuple-element.49), channel_id=1, source_target_pairs={{0,4},{4,8},{8,12},{12,16},{16,20},{20,24},{24,28},{28,0},{1,5},{5... | collective-permute-start | bytes 393224 | tf_op jit(solution)/shard_map/ppermute | solution.py:337
  8.0 3.2 %collective-permute-start.3 = (bf16[2,128,256]{2,1,0:T(8,128)(2,1)S(1)}, bf16[2,128,256]{2,1,0:T(8,128)(2,1)S(1)}, u32[]{:S(2)}, u32[]{:S(2)}) collective-permute-start(bf16[2,128,256]{2,1,0:T(8,128)(2,1)S(1)} %get-tuple-element.50), channel_id=1, source_target_pairs={{4,0},{8,4},{12,8},{16,12},{20,16},{24,20},{28,24},{0,28},{5,1},{9... | collective-permute-start | bytes 393224 | tf_op jit(solution)/shard_map/ppermute | solution.py:340
  11.3 0.4 collective-permute-start.6
  11.7 3.6 %collective-permute-done.2.refs_4_ = bf16[2,128,256]{2,1,0:T(8,128)(2,1)S(1)} collective-permute-done((bf16[2,128,256]{2,1,0:T(8,128)(2,1)S(1)}, bf16[2,128,256]{2,1,0:T(8,128)(2,1)S(1)}, u32[]{:S(2)}, u32[]{:S(2)}) %collective-permute-start.2) | collective-permute-done | bytes 131104 | tf_op jit(solution)/shard_map/ppermute | solution.py:337
  15.3 0.0 collective-permute-start.5
  15.3 1.1 %collective-permute-done.3.refs_5_ = bf16[2,128,256]{2,1,0:T(8,128)(2,1)S(1)} collective-permute-done((bf16[2,128,256]{2,1,0:T(8,128)(2,1)S(1)}, bf16[2,128,256]{2,1,0:T(8,128)(2,1)S(1)}, u32[]{:S(2)}, u32[]{:S(2)}) %collective-permute-start.3) | collective-permute-done | bytes 131104 | tf_op jit(solution)/shard_map/ppermute | solution.py:340
  16.4 0.0 copy-done.3
  16.4 0.9 %before_first.1 = (f32[2,5,128,256]{3,2,1,0:T(8,128)S(1)}, f32[2,3,128,256]{3,2,1,0:T(8,128)S(1)}) custom-call(f32[5,128,256]{2,1,0:T(8,128)S(1)} %get-tuple-element.43.refs_0_.one_ref, f32[3,128,256]{2,1,0:T(8,128)S(1)} %get-tuple-element.44.refs_1_.one_ref, f32[5,128,256]{2,1,0:T(8,128)S(1)} %get-tuple-element.45.refs_2_.two_ref, ...), custom_call_target="tpu_custom_call" | custom-call | tf_op jit(solution)/shard_map/before_first/pallas_call | solution.py:37
  17.3 3.4 %collective-permute-done.1.refs_2_ = bf16[2,640,256]{2,1,0:T(8,128)(2,1)S(1)} collective-permute-done((bf16[2,640,256]{2,1,0:T(8,128)(2,1)S(1)}, bf16[2,640,256]{2,1,0:T(8,128)(2,1)S(1)}, u32[]{:S(2)}, u32[]{:S(2)}) %collective-permute-start.1) | collective-permute-done | bytes 655392 | tf_op jit(solution)/shard_map/ppermute | solution.py:334
  20.7 0.0 collective-permute-start.4
  20.7 0.0 collective-permute-done.refs_1_
  20.7 0.0 copy-done
  20.7 1.2 %early_part.2.part_ref = f32[2,1280,256]{2,1,0:T(8,128)S(1)} custom-call(bf16[2,640,256]{2,1,0:T(8,128)(2,1)S(1)} %get-tuple-element.42.refs_0_, bf16[2,640,256]{2,1,0:T(8,128)(2,1)S(1)} %collective-permute-done.refs_1_, bf16[2,640,256]{2,1,0:T(8,128)(2,1)S(1)} %collective-permute-done.1.refs_2_, bf16[2,1024,256]{2,1,0:T(8,128)(2,1)S(1)} %copy-done), custom_call_target="tpu_custom_call" | custom-call | flops 20000000000 | tf_op jit(solution)/shard_map/early_part/pallas_call | solution.py:37
  21.9 0.9 %collective-permute-done.4.last_ref = bf16[2,640,256]{2,1,0:T(8,128)(2,1)S(1)} collective-permute-done((bf16[2,640,256]{2,1,0:T(8,128)(2,1)S(1)}, bf16[2,640,256]{2,1,0:T(8,128)(2,1)S(1)}, u32[]{:S(2)}, u32[]{:S(2)}) %collective-permute-start.4) | collective-permute-done | bytes 655392 | tf_op jit(solution)/shard_map/ppermute | solution.py:331
  22.8 0.0 copy-done.2
  22.8 1.0 %first_node.2 = (f32[5,128,256]{2,1,0:T(8,128)S(1)}, bf16[1,640,256]{2,1,0:T(8,128)(2,1)S(1)}, f32[5,128,256]{2,1,0:T(8,128)S(1)}, bf16[1,128,256]{2,1,0:T(8,128)(2,1)S(1)}, bf16[1,128,256]{2,1,0:T(8,128)(2,1)S(1)}) custom-call(f32[2,1280,256]{2,1,0:T(8,128)S(1)} %early_part.2.part_ref, bf16[2,640,256]{2,1,0:T(8,128)(2,1)S(1)} %collective-permute-done.4.last_ref, ...), custom_call_target="tpu_custom_call" | custom-call | tf_op jit(solution)/shard_map/first_node/pallas_call | solution.py:37
  23.8 5.1 %collective-permute-start.7 = (bf16[1,128,256]{2,1,0:T(8,128)(2,1)S(1)}, bf16[1,128,256]{2,1,0:T(8,128)(2,1)S(1)}, u32[]{:S(2)}, u32[]{:S(2)}) collective-permute-start(bf16[1,128,256]{2,1,0:T(8,128)(2,1)S(1)} %get-tuple-element.56), channel_id=1, source_target_pairs={{4,0},{8,4},{12,8},{16,12},{20,16},{24,20},{28,24},{0,28},{5,1},{9... | collective-permute-start | bytes 196616 | tf_op jit(solution)/shard_map/ppermute | solution.py:340
  29.0 1.5 %collective-permute-start.10 = (bf16[1,640,256]{2,1,0:T(8,128)(2,1)S(1)}, bf16[1,640,256]{2,1,0:T(8,128)(2,1)S(1)}, u32[]{:S(2)}, u32[]{:S(2)}) collective-permute-start(bf16[1,640,256]{2,1,0:T(8,128)(2,1)S(1)} %get-tuple-element.55.refs_4_), channel_id=1, source_target_pairs={{0,2},{1,3},{2,0},{3,1},{4,6},{5,7},{6,4},{7,5},{8,10},{9,11},{10,... | collective-permute-start | bytes 983048 | tf_op jit(solution)/shard_map/ppermute | solution.py:334
  30.5 0.0 collective-permute-start.9
  30.5 0.0 collective-permute-done.6.refs_2_
  30.5 0.4 collective-permute-done.7.hi_ref
  30.9 0.1 collective-permute-start.8
  31.0 0.0 collective-permute-done.5.refs_1_
  31.0 1.1 %early_part.3 = (f32[2,768,256]{2,1,0:T(8,128)S(1)}, f32[8,128,256]{2,1,0:T(8,128)}) custom-call(bf16[2,384,256]{2,1,0:T(8,128)(2,1)S(1)} %get-tuple-element.41.refs_0_, bf16[2,384,256]{2,1,0:T(8,128)(2,1)S(1)} %collective-permute-done.5.refs_1_, bf16[2,384,256]{2,1,0:T(8,128)(2,1)S(1)} %collective-permute-done.6.refs_2_, bf16[2,1024,256]{2,1,0:T(8,128)(2,1)S(1)} %copy-done, ...), custom_call_target="tpu_custom_call" | custom-call | flops 20000000000 | tf_op jit(solution)/shard_map/early_part/pallas_call | solution.py:37
  32.1 0.6 %collective-permute-done.8.last_ref = bf16[2,384,256]{2,1,0:T(8,128)(2,1)S(1)} collective-permute-done((bf16[2,384,256]{2,1,0:T(8,128)(2,1)S(1)}, bf16[2,384,256]{2,1,0:T(8,128)(2,1)S(1)}, u32[]{:S(2)}, u32[]{:S(2)}) %collective-permute-start.8) | collective-permute-done | bytes 393248 | tf_op jit(solution)/shard_map/ppermute | solution.py:331
  32.7 0.7 %first_node.3 = (f32[3,128,256]{2,1,0:T(8,128)S(1)}, bf16[1,384,256]{2,1,0:T(8,128)(2,1)S(1)}, f32[3,128,256]{2,1,0:T(8,128)S(1)}) custom-call(f32[2,768,256]{2,1,0:T(8,128)S(1)} %get-tuple-element.58.part_ref, bf16[2,384,256]{2,1,0:T(8,128)(2,1)S(1)} %collective-permute-done.8.last_ref, f32[2,3,128,256]{3,2,1,0:T(8,128)S(1)} %get-tuple-element.59.base_ref, ...), custom_call_target="tpu_custom_call" | custom-call | tf_op jit(solution)/shard_map/first_node/pallas_call | solution.py:37
  33.4 1.5 %collective-permute-start.14 = (bf16[1,384,256]{2,1,0:T(8,128)(2,1)S(1)}, bf16[1,384,256]{2,1,0:T(8,128)(2,1)S(1)}, u32[]{:S(2)}, u32[]{:S(2)}) collective-permute-start(bf16[1,384,256]{2,1,0:T(8,128)(2,1)S(1)} %get-tuple-element.66.refs_0_), channel_id=1, source_target_pairs={{0,2},{1,3},{2,0},{3,1},{4,6},{5,7},{6,4},{7,5},{8,10},{9,11},{10,... | collective-permute-start | bytes 589832 | tf_op jit(solution)/shard_map/ppermute | solution.py:334
  34.9 0.0 collective-permute-start.13
  34.9 0.2 collective-permute-start.12
  35.1 4.5 %collective-permute-done.10.far_ref = bf16[1,640,256]{2,1,0:T(8,128)(2,1)S(1)} collective-permute-done((bf16[1,640,256]{2,1,0:T(8,128)(2,1)S(1)}, bf16[1,640,256]{2,1,0:T(8,128)(2,1)S(1)}, u32[]{:S(2)}, u32[]{:S(2)}) %collective-permute-start.10) | collective-permute-done | bytes 327712 | tf_op jit(solution)/shard_map/ppermute | solution.py:334
  39.6 0.0 collective-permute-start.11
  39.6 0.9 %before_second.1 = (f32[8,128,256]{2,1,0:T(8,128)}, f32[2,640,256]{2,1,0:T(8,128)S(1)}, f32[5,128,256]{2,1,0:T(8,128)S(1)}, f32[3,128,256]{2,1,0:T(8,128)S(1)}) custom-call(f32[5,128,256]{2,1,0:T(8,128)S(1)} %get-tuple-element.54.refs_4_.refs_0_.new_ref, f32[3,128,256]{2,1,0:T(8,128)S(1)} %get-tuple-element.60.refs_1_.new_ref, ...), custom_call_target="tpu_custom_call", output_to_operand_aliasing={{0}: (8, {})} | custom-call | flops 20000000000 | tf_op jit(solution)/shard_map/before_second/pallas_call | solution.py:37
  40.5 0.0 collective-permute-done.9.sib_ref
  40.5 0.7 %collective-permute-done.11.farsib_ref = bf16[1,640,256]{2,1,0:T(8,128)(2,1)S(1)} collective-permute-done((bf16[1,640,256]{2,1,0:T(8,128)(2,1)S(1)}, bf16[1,640,256]{2,1,0:T(8,128)(2,1)S(1)}, u32[]{:S(2)}, u32[]{:S(2)}) %collective-permute-start.11) | collective-permute-done | bytes 327712 | tf_op jit(solution)/shard_map/ppermute | solution.py:331
  41.2 0.7 %whole_sums.1.sums_ref = bf16[2,640,256]{2,1,0:T(8,128)(2,1)S(1)} custom-call(f32[2,640,256]{2,1,0:T(8,128)S(1)} %get-tuple-element.65.part_ref, bf16[1,640,256]{2,1,0:T(8,128)(2,1)S(1)} %collective-permute-done.9.sib_ref, bf16[1,640,256]{2,1,0:T(8,128)(2,1)S(1)} %collective-permute-done.10.far_ref, ...), custom_call_target="tpu_custom_call" | custom-call | tf_op jit(solution)/shard_map/whole_sums/pallas_call | solution.py:37
  41.9 0.8 %collective-permute-done.12.lo_ref = bf16[1,128,256]{2,1,0:T(8,128)(2,1)S(1)} collective-permute-done((bf16[1,128,256]{2,1,0:T(8,128)(2,1)S(1)}, bf16[1,128,256]{2,1,0:T(8,128)(2,1)S(1)}, u32[]{:S(2)}, u32[]{:S(2)}) %collective-permute-start.12) | collective-permute-done | bytes 65568 | tf_op jit(solution)/shard_map/ppermute | solution.py:337
  42.7 0.0 collective-permute-done.14.refs_2_
  42.7 0.0 collective-permute-start.15
  42.7 0.0 collective-permute-done.13.refs_1_
  42.7 1.3 %second_first.1 = (f32[8,128,256]{2,1,0:T(8,128)}, f32[2,384,256]{2,1,0:T(8,128)S(1)}) custom-call(bf16[2,640,256]{2,1,0:T(8,128)(2,1)S(1)} %whole_sums.1.sums_ref, f32[5,128,256]{2,1,0:T(8,128)S(1)} %get-tuple-element.68.base_ref, f32[5,128,256]{2,1,0:T(8,128)S(1)} %get-tuple-element.54.refs_4_.refs_0_.new_ref, f32[1,256]{1,0:T(1,128)S(1)} %bitcast.5, ...), custom_call_target="tpu_custom_call" | custom-call | tf_op jit(solution)/shard_map/second_first/pallas_call | solution.py:37
  44.1 0.1 collective-permute-done.15.last_ref
  44.2 1.0 %second_last.1 = f32[8,128,256]{2,1,0:T(8,128)} custom-call(f32[2,384,256]{2,1,0:T(8,128)S(1)} %get-tuple-element.73.part_ref, bf16[1,384,256]{2,1,0:T(8,128)(2,1)S(1)} %collective-permute-done.15.last_ref, f32[3,128,256]{2,1,0:T(8,128)S(1)} %get-tuple-element.74.base_ref, ...), custom_call_target="tpu_custom_call", output_to_operand_aliasing={{}: (6, {})} | custom-call | tf_op jit(solution)/shard_map/second_last/pallas_call | solution.py:37
  (3 shorter events, 0.0 us)
Async XLA Ops:
  2.1 14.3 %copy-start.3 = (f32[256]{0:T(256)S(1)}, f32[256]{0:T(256)}, u32[]{:S(2)}) copy-start(f32[256]{0:T(256)} %param.10) | copy-start | bytes 3076
  2.1 18.6 %collective-permute-start.1 = (bf16[2,640,256]{2,1,0:T(8,128)(2,1)S(1)}, bf16[2,640,256]{2,1,0:T(8,128)(2,1)S(1)}, u32[]{:S(2)}, u32[]{:S(2)}) collective-permute-start(bf16[2,640,256]{2,1,0:T(8,128)(2,1)S(1)} %get-tuple-element.42.refs_0_), channel_id=1, source_target_pairs={{0,2},{1,3},{2,0},{3,1},{4,6},{5,7},{6,4},{7,5},{8,10},{9,11},{10,... | collective-permute-start | bytes 1966088 | tf_op jit(solution)/shard_map/ppermute | solution.py:334
  6.4 14.3 %copy-start = (bf16[2,1024,256]{2,1,0:T(8,128)(2,1)S(1)}, bf16[2,1024,256]{2,1,0:T(8,128)(2,1)}, u32[]{:S(2)}) copy-start(bf16[2,1024,256]{2,1,0:T(8,128)(2,1)} %k_ref.4) | copy-start | bytes 3145732
  6.4 14.3 %collective-permute-start = (bf16[2,640,256]{2,1,0:T(8,128)(2,1)S(1)}, bf16[2,640,256]{2,1,0:T(8,128)(2,1)S(1)}, u32[]{:S(2)}, u32[]{:S(2)}) collective-permute-start(bf16[2,640,256]{2,1,0:T(8,128)(2,1)S(1)} %get-tuple-element.42.refs_0_), channel_id=1, source_target_pairs={{0,1},{1,0},{2,3},{3,2},{4,5},{5,4},{6,7},{7,6},{8,9},{9,8},{10,11... | collective-permute-start | bytes 1966088 | tf_op jit(solution)/shard_map/ppermute | solution.py:331
  6.5 8.8 %collective-permute-start.2 = (bf16[2,128,256]{2,1,0:T(8,128)(2,1)S(1)}, bf16[2,128,256]{2,1,0:T(8,128)(2,1)S(1)}, u32[]{:S(2)}, u32[]{:S(2)}) collective-permute-start(bf16[2,128,256]{2,1,0:T(8,128)(2,1)S(1)} %get-tuple-element.49), channel_id=1, source_target_pairs={{0,4},{4,8},{8,12},{12,16},{16,20},{20,24},{24,28},{28,0},{1,5},{5... | collective-permute-start | bytes 393224 | tf_op jit(solution)/shard_map/ppermute | solution.py:337
  8.0 8.4 %collective-permute-start.3 = (bf16[2,128,256]{2,1,0:T(8,128)(2,1)S(1)}, bf16[2,128,256]{2,1,0:T(8,128)(2,1)S(1)}, u32[]{:S(2)}, u32[]{:S(2)}) collective-permute-start(bf16[2,128,256]{2,1,0:T(8,128)(2,1)S(1)} %get-tuple-element.50), channel_id=1, source_target_pairs={{4,0},{8,4},{12,8},{16,12},{20,16},{24,20},{28,24},{0,28},{5,1},{9... | collective-permute-start | bytes 393224 | tf_op jit(solution)/shard_map/ppermute | solution.py:340
  11.3 19.2 %collective-permute-start.6 = (bf16[2,384,256]{2,1,0:T(8,128)(2,1)S(1)}, bf16[2,384,256]{2,1,0:T(8,128)(2,1)S(1)}, u32[]{:S(2)}, u32[]{:S(2)}) collective-permute-start(bf16[2,384,256]{2,1,0:T(8,128)(2,1)S(1)} %get-tuple-element.41.refs_0_), channel_id=1, source_target_pairs={{0,2},{1,3},{2,0},{3,1},{4,6},{5,7},{6,4},{7,5},{8,10},{9,11},{10,... | collective-permute-start | bytes 1179656 | tf_op jit(solution)/shard_map/ppermute | solution.py:334
  15.3 15.7 %collective-permute-start.5 = (bf16[2,384,256]{2,1,0:T(8,128)(2,1)S(1)}, bf16[2,384,256]{2,1,0:T(8,128)(2,1)S(1)}, u32[]{:S(2)}, u32[]{:S(2)}) collective-permute-start(bf16[2,384,256]{2,1,0:T(8,128)(2,1)S(1)} %get-tuple-element.41.refs_0_), channel_id=1, source_target_pairs={{0,1},{1,0},{2,3},{3,2},{4,5},{5,4},{6,7},{7,6},{8,9},{9,8},{10,11... | collective-permute-start | bytes 1179656 | tf_op jit(solution)/shard_map/ppermute | solution.py:331
  20.7 2.1 %copy-start.1 = (f32[8,128,256]{2,1,0:T(8,128)S(1)}, f32[8,128,256]{2,1,0:T(8,128)}, u32[]{:S(2)}) copy-start(f32[8,128,256]{2,1,0:T(8,128)} %init_ref.3) | copy-start | bytes 3145732
  20.7 2.1 %copy-start.2 = (f32[256]{0:T(256)S(1)}, f32[256]{0:T(256)}, u32[]{:S(2)}) copy-start(f32[256]{0:T(256)} %param.11) | copy-start | bytes 3076
  20.7 2.1 %collective-permute-start.4 = (bf16[2,640,256]{2,1,0:T(8,128)(2,1)S(1)}, bf16[2,640,256]{2,1,0:T(8,128)(2,1)S(1)}, u32[]{:S(2)}, u32[]{:S(2)}) collective-permute-start(bf16[2,640,256]{2,1,0:T(8,128)(2,1)S(1)} %collective-permute-done.1.refs_2_), channel_id=1, source_target_pairs={{0,1},{1,0},{2,3},{3,2},{4,5},{5,4},{6,7},{7,6},{8,9},{9,8},{10,11... | collective-permute-start | bytes 1966088 | tf_op jit(solution)/shard_map/ppermute | solution.py:331
  23.8 7.0 %collective-permute-start.7 = (bf16[1,128,256]{2,1,0:T(8,128)(2,1)S(1)}, bf16[1,128,256]{2,1,0:T(8,128)(2,1)S(1)}, u32[]{:S(2)}, u32[]{:S(2)}) collective-permute-start(bf16[1,128,256]{2,1,0:T(8,128)(2,1)S(1)} %get-tuple-element.56), channel_id=1, source_target_pairs={{4,0},{8,4},{12,8},{16,12},{20,16},{24,20},{28,24},{0,28},{5,1},{9... | collective-permute-start | bytes 196616 | tf_op jit(solution)/shard_map/ppermute | solution.py:340
  29.0 10.6 %collective-permute-start.10 = (bf16[1,640,256]{2,1,0:T(8,128)(2,1)S(1)}, bf16[1,640,256]{2,1,0:T(8,128)(2,1)S(1)}, u32[]{:S(2)}, u32[]{:S(2)}) collective-permute-start(bf16[1,640,256]{2,1,0:T(8,128)(2,1)S(1)} %get-tuple-element.55.refs_4_), channel_id=1, source_target_pairs={{0,2},{1,3},{2,0},{3,1},{4,6},{5,7},{6,4},{7,5},{8,10},{9,11},{10,... | collective-permute-start | bytes 983048 | tf_op jit(solution)/shard_map/ppermute | solution.py:334
  30.5 10.0 %collective-permute-start.9 = (bf16[1,640,256]{2,1,0:T(8,128)(2,1)S(1)}, bf16[1,640,256]{2,1,0:T(8,128)(2,1)S(1)}, u32[]{:S(2)}, u32[]{:S(2)}) collective-permute-start(bf16[1,640,256]{2,1,0:T(8,128)(2,1)S(1)} %get-tuple-element.55.refs_4_), channel_id=1, source_target_pairs={{0,1},{1,0},{2,3},{3,2},{4,5},{5,4},{6,7},{7,6},{8,9},{9,8},{10,11... | collective-permute-start | bytes 983048 | tf_op jit(solution)/shard_map/ppermute | solution.py:331
  30.9 1.8 %collective-permute-start.8 = (bf16[2,384,256]{2,1,0:T(8,128)(2,1)S(1)}, bf16[2,384,256]{2,1,0:T(8,128)(2,1)S(1)}, u32[]{:S(2)}, u32[]{:S(2)}) collective-permute-start(bf16[2,384,256]{2,1,0:T(8,128)(2,1)S(1)} %collective-permute-done.6.refs_2_), channel_id=1, source_target_pairs={{0,1},{1,0},{2,3},{3,2},{4,5},{5,4},{6,7},{7,6},{8,9},{9,8},{10,11... | collective-permute-start | bytes 1179656 | tf_op jit(solution)/shard_map/ppermute | solution.py:331
  33.4 9.3 %collective-permute-start.14 = (bf16[1,384,256]{2,1,0:T(8,128)(2,1)S(1)}, bf16[1,384,256]{2,1,0:T(8,128)(2,1)S(1)}, u32[]{:S(2)}, u32[]{:S(2)}) collective-permute-start(bf16[1,384,256]{2,1,0:T(8,128)(2,1)S(1)} %get-tuple-element.66.refs_0_), channel_id=1, source_target_pairs={{0,2},{1,3},{2,0},{3,1},{4,6},{5,7},{6,4},{7,5},{8,10},{9,11},{10,... | collective-permute-start | bytes 589832 | tf_op jit(solution)/shard_map/ppermute | solution.py:334
  34.9 7.8 %collective-permute-start.13 = (bf16[1,384,256]{2,1,0:T(8,128)(2,1)S(1)}, bf16[1,384,256]{2,1,0:T(8,128)(2,1)S(1)}, u32[]{:S(2)}, u32[]{:S(2)}) collective-permute-start(bf16[1,384,256]{2,1,0:T(8,128)(2,1)S(1)} %get-tuple-element.66.refs_0_), channel_id=1, source_target_pairs={{0,1},{1,0},{2,3},{3,2},{4,5},{5,4},{6,7},{7,6},{8,9},{9,8},{10,11... | collective-permute-start | bytes 589832 | tf_op jit(solution)/shard_map/ppermute | solution.py:331
  34.9 7.8 %collective-permute-start.12 = (bf16[1,128,256]{2,1,0:T(8,128)(2,1)S(1)}, bf16[1,128,256]{2,1,0:T(8,128)(2,1)S(1)}, u32[]{:S(2)}, u32[]{:S(2)}) collective-permute-start(bf16[1,128,256]{2,1,0:T(8,128)(2,1)S(1)} %get-tuple-element.71), channel_id=1, source_target_pairs={{0,4},{4,8},{8,12},{12,16},{16,20},{20,24},{24,28},{28,0},{1,5},{5... | collective-permute-start | bytes 196616 | tf_op jit(solution)/shard_map/ppermute | solution.py:337
  39.6 1.6 %collective-permute-start.11 = (bf16[1,640,256]{2,1,0:T(8,128)(2,1)S(1)}, bf16[1,640,256]{2,1,0:T(8,128)(2,1)S(1)}, u32[]{:S(2)}, u32[]{:S(2)}) collective-permute-start(bf16[1,640,256]{2,1,0:T(8,128)(2,1)S(1)} %collective-permute-done.10.far_ref), channel_id=1, source_target_pairs={{0,1},{1,0},{2,3},{3,2},{4,5},{5,4},{6,7},{7,6},{8,9},{9,8},{10,11... | collective-permute-start | bytes 983048 | tf_op jit(solution)/shard_map/ppermute | solution.py:331
  42.7 1.4 %collective-permute-start.15 = (bf16[1,384,256]{2,1,0:T(8,128)(2,1)S(1)}, bf16[1,384,256]{2,1,0:T(8,128)(2,1)S(1)}, u32[]{:S(2)}, u32[]{:S(2)}) collective-permute-start(bf16[1,384,256]{2,1,0:T(8,128)(2,1)S(1)} %collective-permute-done.14.refs_2_), channel_id=1, source_target_pairs={{0,1},{1,0},{2,3},{3,2},{4,5},{5,4},{6,7},{7,6},{8,9},{9,8},{10,11... | collective-permute-start | bytes 589832 | tf_op jit(solution)/shard_map/ppermute | solution.py:331

commit v6 on v5

--- a/solution.py
+++ b/solution.py
@@ -357,8 +357,8 @@
     nfar_a = to_far(rounded_a)
     nsib_a = to_sibling(rounded_a)
 
-    new_hi = from_above(new_head)
-    far_b = after(far_b, rounded_a, new_hi)
+    new_lo = from_below(new_tail)
+    far_b = after(far_b, rounded_a, new_lo)
     farsib_b = to_sibling(far_b)
     part_b, new_one = early_part([own_b, sib_b, far_b], kernels, new_a, chunks[0], xcount)
     new_b, rounded_b, rest_b = first_node(
@@ -366,14 +366,14 @@
     )
     nfar_b = to_far(rounded_b)
     nsib_b = to_sibling(rounded_b)
-    new_lo = from_below(after(new_tail, rounded_b))
+    new_hi = from_above(after(new_head, rounded_b))
     nfar_a = after(nfar_a, rounded_b)
     nfarsib_a = to_sibling(nfar_a)
     new_one, npart_a, nbase_a, nbase_b = before_second(
         (new_a, new_b), (rest_a, rest_b), growth, death, new_one, [rounded_a], kernels, chunks
     )
     sums_a = whole_sums(npart_a, [nsib_a, nfar_a, nfarsib_a], after(kernels, nbase_a))
-    nfar_b = after(nfar_b, sums_a, new_lo)
+    nfar_b = after(nfar_b, sums_a, new_hi)
     nfarsib_b = to_sibling(nfar_b)
     begun, npart_b = second_first(
         sums_a, nbase_a, new_a, death, new_lo, new_hi, [rounded_b, nsib_b, nfar_b], kernels, chunks[0], xcount

time: 45.3 us -> 43.4 us (0.958)
  waiting for transfers between devices: 16 us -> 14.3 us
    ppermute x4, waiting for transfers between devices: 7.83 us -> 4.47 us  [to_far(): return lax.ppermute(v, 'trait', [(i, i ^ 2) for i in range(traits)])]
    ppermute x2, starting transfers between devices: 8.35 us -> 6.03 us  [from_above(): lax.ppermute(head, 'gx', [((i + 1) % gcount, i) for i in range(gcount)])]
    ppermute x2, waiting for transfers between devices: 4.44 us -> 6.67 us  [from_below(): lax.ppermute(tail, 'gx', [(i, (i + 1) % gcount) for i in range(gcount)])]
    ppermute x2, starting transfers between devices: 1.76 us -> 3.62 us  [from_below(): lax.ppermute(tail, 'gx', [(i, (i + 1) % gcount) for i in range(gcount)])]
  transfers between devices with their start and end apart: 16 -> 16, of which waited for: 10 -> 10; matrix products, arithmetic and copies ran while one was open for 0% -> 0% of each run, Pallas kernels for 20% -> 21%
where the time goes in v6:
time: 43.4 us; the launch traced here: 43.2 us
  starting transfers between devices  16.6 us (38%)
  waiting for transfers between devices  14.3 us (33%)
  Pallas kernels  11.5 us (26%)
  between operations  0.77 us (2%)
    pallas_call x11, Pallas kernels, call(): pl.pallas_call(body, out_shape=outs, in_specs=specs, out_specs=out_specs...  11.5 us
    ppermute x2, waiting for transfers between devices, from_below(): lax.ppermute(tail, 'gx', [(i, (i + 1) % gcount) for i in range(gcount)])  6.67 us
    ppermute x4, starting transfers between devices, to_far(): return lax.ppermute(v, 'trait', [(i, i ^ 2) for i in range(traits)])  6.57 us
    ppermute x2, starting transfers between devices, from_above(): lax.ppermute(head, 'gx', [((i + 1) % gcount, i) for i in range(gcount)])  6.03 us
    ppermute x4, waiting for transfers between devices, to_far(): return lax.ppermute(v, 'trait', [(i, i ^ 2) for i in range(traits)])  4.47 us
    ppermute x2, starting transfers between devices, from_below(): lax.ppermute(tail, 'gx', [(i, (i + 1) % gcount) for i in range(gcount)])  3.62 us
    ppermute x8, waiting for transfers between devices, to_sibling(): return lax.ppermute(v, 'trait', [(i, i ^ 1) for i in range(traits)])  2.04 us
    ppermute x2, waiting for transfers between devices, from_above(): lax.ppermute(head, 'gx', [((i + 1) % gcount, i) for i in range(gcount)])  1.13 us
  transfers between devices with their start and end apart: 16, of which 10 were waited for; matrix products, arithmetic and copies ran while one was open for 0% of the time, Pallas kernels for 21%

profile of v6, /device:TPU:0, one launch (start us, length us, event | category | flops | bytes accessed | tf_op | source)
XLA Modules:
  0.0 43.2 jit_solution(17545968137008727077)
XLA Ops:
  0.6 1.5 %load_chunk.2 = (f32[5,128,256]{2,1,0:T(8,128)S(1)}, f32[5,128,256]{2,1,0:T(8,128)S(1)}, bf16[2,640,256]{2,1,0:T(8,128)(2,1)S(1)}, bf16[2,128,256]{2,1,0:T(8,128)(2,1)S(1)}, bf16[2,128,256]{2,1,0:T(8,128)(2,1)S(1)}) custom-call(f32[8,128,256]{2,1,0:T(8,128)} %refs_0_.2, f32[8,128,256]{2,1,0:T(8,128)} %refs_1_.3), custom_call_target="tpu_custom_call" | custom-call | tf_op jit(solution)/shard_map/load_chunk/pallas_call | solution.py:37
  2.1 0.0 copy-start.3
  2.1 3.0 %collective-permute-start.1 = (bf16[2,640,256]{2,1,0:T(8,128)(2,1)S(1)}, bf16[2,640,256]{2,1,0:T(8,128)(2,1)S(1)}, u32[]{:S(2)}, u32[]{:S(2)}) collective-permute-start(bf16[2,640,256]{2,1,0:T(8,128)(2,1)S(1)} %get-tuple-element.42.refs_0_), channel_id=1, source_target_pairs={{0,2},{1,3},{2,0},{3,1},{4,6},{5,7},{6,4},{7,5},{8,10},{9,11},{10,... | collective-permute-start | bytes 1966088 | tf_op jit(solution)/shard_map/ppermute | solution.py:334
  5.1 1.3 %load_chunk.3 = (f32[3,128,256]{2,1,0:T(8,128)S(1)}, f32[3,128,256]{2,1,0:T(8,128)S(1)}, bf16[2,384,256]{2,1,0:T(8,128)(2,1)S(1)}) custom-call(f32[8,128,256]{2,1,0:T(8,128)} %refs_0_.2, f32[8,128,256]{2,1,0:T(8,128)} %refs_1_.3), custom_call_target="tpu_custom_call" | custom-call | tf_op jit(solution)/shard_map/load_chunk/pallas_call | solution.py:37
  6.4 0.0 copy-start
  6.4 0.1 collective-permute-start
  6.5 1.5 %collective-permute-start.2 = (bf16[2,128,256]{2,1,0:T(8,128)(2,1)S(1)}, bf16[2,128,256]{2,1,0:T(8,128)(2,1)S(1)}, u32[]{:S(2)}, u32[]{:S(2)}) collective-permute-start(bf16[2,128,256]{2,1,0:T(8,128)(2,1)S(1)} %get-tuple-element.49), channel_id=1, source_target_pairs={{0,4},{4,8},{8,12},{12,16},{16,20},{20,24},{24,28},{28,0},{1,5},{5... | collective-permute-start | bytes 393224 | tf_op jit(solution)/shard_map/ppermute | solution.py:337
  8.0 3.2 %collective-permute-start.3 = (bf16[2,128,256]{2,1,0:T(8,128)(2,1)S(1)}, bf16[2,128,256]{2,1,0:T(8,128)(2,1)S(1)}, u32[]{:S(2)}, u32[]{:S(2)}) collective-permute-start(bf16[2,128,256]{2,1,0:T(8,128)(2,1)S(1)} %get-tuple-element.50), channel_id=1, source_target_pairs={{4,0},{8,4},{12,8},{16,12},{20,16},{24,20},{28,24},{0,28},{5,1},{9... | collective-permute-start | bytes 393224 | tf_op jit(solution)/shard_map/ppermute | solution.py:340
  11.3 0.4 collective-permute-start.6
  11.7 3.6 %collective-permute-done.2.refs_4_ = bf16[2,128,256]{2,1,0:T(8,128)(2,1)S(1)} collective-permute-done((bf16[2,128,256]{2,1,0:T(8,128)(2,1)S(1)}, bf16[2,128,256]{2,1,0:T(8,128)(2,1)S(1)}, u32[]{:S(2)}, u32[]{:S(2)}) %collective-permute-start.2) | collective-permute-done | bytes 131104 | tf_op jit(solution)/shard_map/ppermute | solution.py:337
  15.3 0.0 collective-permute-start.5
  15.3 1.1 %collective-permute-done.3.refs_5_ = bf16[2,128,256]{2,1,0:T(8,128)(2,1)S(1)} collective-permute-done((bf16[2,128,256]{2,1,0:T(8,128)(2,1)S(1)}, bf16[2,128,256]{2,1,0:T(8,128)(2,1)S(1)}, u32[]{:S(2)}, u32[]{:S(2)}) %collective-permute-start.3) | collective-permute-done | bytes 131104 | tf_op jit(solution)/shard_map/ppermute | solution.py:340
  16.4 0.0 copy-done.3
  16.4 0.9 %before_first.1 = (f32[2,5,128,256]{3,2,1,0:T(8,128)S(1)}, f32[2,3,128,256]{3,2,1,0:T(8,128)S(1)}) custom-call(f32[5,128,256]{2,1,0:T(8,128)S(1)} %get-tuple-element.43.refs_0_.one_ref, f32[3,128,256]{2,1,0:T(8,128)S(1)} %get-tuple-element.44.refs_1_.one_ref, f32[5,128,256]{2,1,0:T(8,128)S(1)} %get-tuple-element.45.refs_2_.two_ref, ...), custom_call_target="tpu_custom_call" | custom-call | tf_op jit(solution)/shard_map/before_first/pallas_call | solution.py:37
  17.3 3.4 %collective-permute-done.1.refs_2_ = bf16[2,640,256]{2,1,0:T(8,128)(2,1)S(1)} collective-permute-done((bf16[2,640,256]{2,1,0:T(8,128)(2,1)S(1)}, bf16[2,640,256]{2,1,0:T(8,128)(2,1)S(1)}, u32[]{:S(2)}, u32[]{:S(2)}) %collective-permute-start.1) | collective-permute-done | bytes 655392 | tf_op jit(solution)/shard_map/ppermute | solution.py:334
  20.7 0.0 collective-permute-start.4
  20.7 0.0 collective-permute-done.refs_1_
  20.7 0.0 copy-done
  20.7 1.2 %early_part.2.part_ref = f32[2,1280,256]{2,1,0:T(8,128)S(1)} custom-call(bf16[2,640,256]{2,1,0:T(8,128)(2,1)S(1)} %get-tuple-element.42.refs_0_, bf16[2,640,256]{2,1,0:T(8,128)(2,1)S(1)} %collective-permute-done.refs_1_, bf16[2,640,256]{2,1,0:T(8,128)(2,1)S(1)} %collective-permute-done.1.refs_2_, bf16[2,1024,256]{2,1,0:T(8,128)(2,1)S(1)} %copy-done), custom_call_target="tpu_custom_call" | custom-call | flops 20000000000 | tf_op jit(solution)/shard_map/early_part/pallas_call | solution.py:37
  21.9 0.9 %collective-permute-done.4.last_ref = bf16[2,640,256]{2,1,0:T(8,128)(2,1)S(1)} collective-permute-done((bf16[2,640,256]{2,1,0:T(8,128)(2,1)S(1)}, bf16[2,640,256]{2,1,0:T(8,128)(2,1)S(1)}, u32[]{:S(2)}, u32[]{:S(2)}) %collective-permute-start.4) | collective-permute-done | bytes 655392 | tf_op jit(solution)/shard_map/ppermute | solution.py:331
  22.8 0.0 copy-done.2
  22.8 1.0 %first_node.2 = (f32[5,128,256]{2,1,0:T(8,128)S(1)}, bf16[1,640,256]{2,1,0:T(8,128)(2,1)S(1)}, f32[5,128,256]{2,1,0:T(8,128)S(1)}, bf16[1,128,256]{2,1,0:T(8,128)(2,1)S(1)}, bf16[1,128,256]{2,1,0:T(8,128)(2,1)S(1)}) custom-call(f32[2,1280,256]{2,1,0:T(8,128)S(1)} %early_part.2.part_ref, bf16[2,640,256]{2,1,0:T(8,128)(2,1)S(1)} %collective-permute-done.4.last_ref, ...), custom_call_target="tpu_custom_call" | custom-call | tf_op jit(solution)/shard_map/first_node/pallas_call | solution.py:37
  23.8 2.1 %collective-permute-start.7 = (bf16[1,128,256]{2,1,0:T(8,128)(2,1)S(1)}, bf16[1,128,256]{2,1,0:T(8,128)(2,1)S(1)}, u32[]{:S(2)}, u32[]{:S(2)}) collective-permute-start(bf16[1,128,256]{2,1,0:T(8,128)(2,1)S(1)} %get-tuple-element.56), channel_id=1, source_target_pairs={{0,4},{4,8},{8,12},{12,16},{16,20},{20,24},{24,28},{28,0},{1,5},{5... | collective-permute-start | bytes 196616 | tf_op jit(solution)/shard_map/ppermute | solution.py:337
  25.9 1.5 %collective-permute-start.10 = (bf16[1,640,256]{2,1,0:T(8,128)(2,1)S(1)}, bf16[1,640,256]{2,1,0:T(8,128)(2,1)S(1)}, u32[]{:S(2)}, u32[]{:S(2)}) collective-permute-start(bf16[1,640,256]{2,1,0:T(8,128)(2,1)S(1)} %get-tuple-element.55.refs_4_), channel_id=1, source_target_pairs={{0,2},{1,3},{2,0},{3,1},{4,6},{5,7},{6,4},{7,5},{8,10},{9,11},{10,... | collective-permute-start | bytes 983048 | tf_op jit(solution)/shard_map/ppermute | solution.py:334
  27.4 0.0 collective-permute-start.9
  27.5 0.8 %collective-permute-done.6.refs_2_ = bf16[2,384,256]{2,1,0:T(8,128)(2,1)S(1)} collective-permute-done((bf16[2,384,256]{2,1,0:T(8,128)(2,1)S(1)}, bf16[2,384,256]{2,1,0:T(8,128)(2,1)S(1)}, u32[]{:S(2)}, u32[]{:S(2)}) %collective-permute-start.6) | collective-permute-done | bytes 393248 | tf_op jit(solution)/shard_map/ppermute | solution.py:334
  28.3 3.1 %collective-permute-done.7.lo_ref = bf16[1,128,256]{2,1,0:T(8,128)(2,1)S(1)} collective-permute-done((bf16[1,128,256]{2,1,0:T(8,128)(2,1)S(1)}, bf16[1,128,256]{2,1,0:T(8,128)(2,1)S(1)}, u32[]{:S(2)}, u32[]{:S(2)}) %collective-permute-start.7) | collective-permute-done | bytes 65568 | tf_op jit(solution)/shard_map/ppermute | solution.py:337
  31.4 0.0 collective-permute-start.8
  31.4 0.0 collective-permute-done.5.refs_1_
  31.4 1.0 %early_part.3 = (f32[2,768,256]{2,1,0:T(8,128)S(1)}, f32[8,128,256]{2,1,0:T(8,128)}) custom-call(bf16[2,384,256]{2,1,0:T(8,128)(2,1)S(1)} %get-tuple-element.41.refs_0_, bf16[2,384,256]{2,1,0:T(8,128)(2,1)S(1)} %collective-permute-done.5.refs_1_, bf16[2,384,256]{2,1,0:T(8,128)(2,1)S(1)} %collective-permute-done.6.refs_2_, bf16[2,1024,256]{2,1,0:T(8,128)(2,1)S(1)} %copy-done, ...), custom_call_target="tpu_custom_call" | custom-call | flops 20000000000 | tf_op jit(solution)/shard_map/early_part/pallas_call | solution.py:37
  32.4 0.7 %collective-permute-done.8.last_ref = bf16[2,384,256]{2,1,0:T(8,128)(2,1)S(1)} collective-permute-done((bf16[2,384,256]{2,1,0:T(8,128)(2,1)S(1)}, bf16[2,384,256]{2,1,0:T(8,128)(2,1)S(1)}, u32[]{:S(2)}, u32[]{:S(2)}) %collective-permute-start.8) | collective-permute-done | bytes 393248 | tf_op jit(solution)/shard_map/ppermute | solution.py:331
  33.1 0.7 %first_node.3 = (f32[3,128,256]{2,1,0:T(8,128)S(1)}, bf16[1,384,256]{2,1,0:T(8,128)(2,1)S(1)}, f32[3,128,256]{2,1,0:T(8,128)S(1)}) custom-call(f32[2,768,256]{2,1,0:T(8,128)S(1)} %get-tuple-element.58.part_ref, bf16[2,384,256]{2,1,0:T(8,128)(2,1)S(1)} %collective-permute-done.8.last_ref, f32[2,3,128,256]{3,2,1,0:T(8,128)S(1)} %get-tuple-element.59.base_ref, ...), custom_call_target="tpu_custom_call" | custom-call | tf_op jit(solution)/shard_map/first_node/pallas_call | solution.py:37
  33.8 1.6 %collective-permute-start.14 = (bf16[1,384,256]{2,1,0:T(8,128)(2,1)S(1)}, bf16[1,384,256]{2,1,0:T(8,128)(2,1)S(1)}, u32[]{:S(2)}, u32[]{:S(2)}) collective-permute-start(bf16[1,384,256]{2,1,0:T(8,128)(2,1)S(1)} %get-tuple-element.66.refs_0_), channel_id=1, source_target_pairs={{0,2},{1,3},{2,0},{3,1},{4,6},{5,7},{6,4},{7,5},{8,10},{9,11},{10,... | collective-permute-start | bytes 589832 | tf_op jit(solution)/shard_map/ppermute | solution.py:334
  35.4 0.0 collective-permute-start.13
  35.4 2.8 %collective-permute-start.12 = (bf16[1,128,256]{2,1,0:T(8,128)(2,1)S(1)}, bf16[1,128,256]{2,1,0:T(8,128)(2,1)S(1)}, u32[]{:S(2)}, u32[]{:S(2)}) collective-permute-start(bf16[1,128,256]{2,1,0:T(8,128)(2,1)S(1)} %get-tuple-element.71), channel_id=1, source_target_pairs={{4,0},{8,4},{12,8},{16,12},{20,16},{24,20},{28,24},{0,28},{5,1},{9... | collective-permute-start | bytes 196616 | tf_op jit(solution)/shard_map/ppermute | solution.py:340
  38.2 0.0 collective-permute-done.10.far_ref
  38.2 0.2 collective-permute-start.11
  38.4 1.0 %before_second.1 = (f32[8,128,256]{2,1,0:T(8,128)}, f32[2,640,256]{2,1,0:T(8,128)S(1)}, f32[5,128,256]{2,1,0:T(8,128)S(1)}, f32[3,128,256]{2,1,0:T(8,128)S(1)}) custom-call(f32[5,128,256]{2,1,0:T(8,128)S(1)} %get-tuple-element.54.refs_4_.refs_0_.new_ref, f32[3,128,256]{2,1,0:T(8,128)S(1)} %get-tuple-element.60.refs_1_.new_ref, ...), custom_call_target="tpu_custom_call", output_to_operand_aliasing={{0}: (8, {})} | custom-call | flops 20000000000 | tf_op jit(solution)/shard_map/before_second/pallas_call | solution.py:37
  39.4 0.0 collective-permute-done.9.sib_ref
  39.4 0.4 collective-permute-done.11.farsib_ref
  39.9 0.7 %whole_sums.1.sums_ref = bf16[2,640,256]{2,1,0:T(8,128)(2,1)S(1)} custom-call(f32[2,640,256]{2,1,0:T(8,128)S(1)} %get-tuple-element.65.part_ref, bf16[1,640,256]{2,1,0:T(8,128)(2,1)S(1)} %collective-permute-done.9.sib_ref, bf16[1,640,256]{2,1,0:T(8,128)(2,1)S(1)} %collective-permute-done.10.far_ref, ...), custom_call_target="tpu_custom_call" | custom-call | tf_op jit(solution)/shard_map/whole_sums/pallas_call | solution.py:37
  40.5 0.0 collective-permute-done.12.hi_ref
  40.5 0.2 collective-permute-done.14.refs_2_
  40.8 0.1 collective-permute-start.15
  40.9 0.0 collective-permute-done.13.refs_1_
  40.9 1.3 %second_first.1 = (f32[8,128,256]{2,1,0:T(8,128)}, f32[2,384,256]{2,1,0:T(8,128)S(1)}) custom-call(bf16[2,640,256]{2,1,0:T(8,128)(2,1)S(1)} %whole_sums.1.sums_ref, f32[5,128,256]{2,1,0:T(8,128)S(1)} %get-tuple-element.68.base_ref, f32[5,128,256]{2,1,0:T(8,128)S(1)} %get-tuple-element.54.refs_4_.refs_0_.new_ref, f32[1,256]{1,0:T(1,128)S(1)} %bitcast.5, ...), custom_call_target="tpu_custom_call" | custom-call | tf_op jit(solution)/shard_map/second_first/pallas_call | solution.py:37
  42.2 0.1 collective-permute-done.15.last_ref
  42.2 1.0 %second_last.1 = f32[8,128,256]{2,1,0:T(8,128)} custom-call(f32[2,384,256]{2,1,0:T(8,128)S(1)} %get-tuple-element.73.part_ref, bf16[1,384,256]{2,1,0:T(8,128)(2,1)S(1)} %collective-permute-done.15.last_ref, f32[3,128,256]{2,1,0:T(8,128)S(1)} %get-tuple-element.74.base_ref, ...), custom_call_target="tpu_custom_call", output_to_operand_aliasing={{}: (6, {})} | custom-call | tf_op jit(solution)/shard_map/second_last/pallas_call | solution.py:37
  (3 shorter events, 0.0 us)
Async XLA Ops:
  2.1 14.3 %copy-start.3 = (f32[256]{0:T(256)S(1)}, f32[256]{0:T(256)}, u32[]{:S(2)}) copy-start(f32[256]{0:T(256)} %param.10) | copy-start | bytes 3076
  2.1 18.6 %collective-permute-start.1 = (bf16[2,640,256]{2,1,0:T(8,128)(2,1)S(1)}, bf16[2,640,256]{2,1,0:T(8,128)(2,1)S(1)}, u32[]{:S(2)}, u32[]{:S(2)}) collective-permute-start(bf16[2,640,256]{2,1,0:T(8,128)(2,1)S(1)} %get-tuple-element.42.refs_0_), channel_id=1, source_target_pairs={{0,2},{1,3},{2,0},{3,1},{4,6},{5,7},{6,4},{7,5},{8,10},{9,11},{10,... | collective-permute-start | bytes 1966088 | tf_op jit(solution)/shard_map/ppermute | solution.py:334
  6.4 14.3 %copy-start = (bf16[2,1024,256]{2,1,0:T(8,128)(2,1)S(1)}, bf16[2,1024,256]{2,1,0:T(8,128)(2,1)}, u32[]{:S(2)}) copy-start(bf16[2,1024,256]{2,1,0:T(8,128)(2,1)} %k_ref.4) | copy-start | bytes 3145732
  6.4 14.3 %collective-permute-start = (bf16[2,640,256]{2,1,0:T(8,128)(2,1)S(1)}, bf16[2,640,256]{2,1,0:T(8,128)(2,1)S(1)}, u32[]{:S(2)}, u32[]{:S(2)}) collective-permute-start(bf16[2,640,256]{2,1,0:T(8,128)(2,1)S(1)} %get-tuple-element.42.refs_0_), channel_id=1, source_target_pairs={{0,1},{1,0},{2,3},{3,2},{4,5},{5,4},{6,7},{7,6},{8,9},{9,8},{10,11... | collective-permute-start | bytes 1966088 | tf_op jit(solution)/shard_map/ppermute | solution.py:331
  6.5 8.8 %collective-permute-start.2 = (bf16[2,128,256]{2,1,0:T(8,128)(2,1)S(1)}, bf16[2,128,256]{2,1,0:T(8,128)(2,1)S(1)}, u32[]{:S(2)}, u32[]{:S(2)}) collective-permute-start(bf16[2,128,256]{2,1,0:T(8,128)(2,1)S(1)} %get-tuple-element.49), channel_id=1, source_target_pairs={{0,4},{4,8},{8,12},{12,16},{16,20},{20,24},{24,28},{28,0},{1,5},{5... | collective-permute-start | bytes 393224 | tf_op jit(solution)/shard_map/ppermute | solution.py:337
  8.0 8.4 %collective-permute-start.3 = (bf16[2,128,256]{2,1,0:T(8,128)(2,1)S(1)}, bf16[2,128,256]{2,1,0:T(8,128)(2,1)S(1)}, u32[]{:S(2)}, u32[]{:S(2)}) collective-permute-start(bf16[2,128,256]{2,1,0:T(8,128)(2,1)S(1)} %get-tuple-element.50), channel_id=1, source_target_pairs={{4,0},{8,4},{12,8},{16,12},{20,16},{24,20},{28,24},{0,28},{5,1},{9... | collective-permute-start | bytes 393224 | tf_op jit(solution)/shard_map/ppermute | solution.py:340
  11.3 17.0 %collective-permute-start.6 = (bf16[2,384,256]{2,1,0:T(8,128)(2,1)S(1)}, bf16[2,384,256]{2,1,0:T(8,128)(2,1)S(1)}, u32[]{:S(2)}, u32[]{:S(2)}) collective-permute-start(bf16[2,384,256]{2,1,0:T(8,128)(2,1)S(1)} %get-tuple-element.41.refs_0_), channel_id=1, source_target_pairs={{0,2},{1,3},{2,0},{3,1},{4,6},{5,7},{6,4},{7,5},{8,10},{9,11},{10,... | collective-permute-start | bytes 1179656 | tf_op jit(solution)/shard_map/ppermute | solution.py:334
  15.3 16.1 %collective-permute-start.5 = (bf16[2,384,256]{2,1,0:T(8,128)(2,1)S(1)}, bf16[2,384,256]{2,1,0:T(8,128)(2,1)S(1)}, u32[]{:S(2)}, u32[]{:S(2)}) collective-permute-start(bf16[2,384,256]{2,1,0:T(8,128)(2,1)S(1)} %get-tuple-element.41.refs_0_), channel_id=1, source_target_pairs={{0,1},{1,0},{2,3},{3,2},{4,5},{5,4},{6,7},{7,6},{8,9},{9,8},{10,11... | collective-permute-start | bytes 1179656 | tf_op jit(solution)/shard_map/ppermute | solution.py:331
  20.7 2.1 %copy-start.1 = (f32[8,128,256]{2,1,0:T(8,128)S(1)}, f32[8,128,256]{2,1,0:T(8,128)}, u32[]{:S(2)}) copy-start(f32[8,128,256]{2,1,0:T(8,128)} %init_ref.3) | copy-start | bytes 3145732
  20.7 2.1 %copy-start.2 = (f32[256]{0:T(256)S(1)}, f32[256]{0:T(256)}, u32[]{:S(2)}) copy-start(f32[256]{0:T(256)} %param.11) | copy-start | bytes 3076
  20.7 2.1 %collective-permute-start.4 = (bf16[2,640,256]{2,1,0:T(8,128)(2,1)S(1)}, bf16[2,640,256]{2,1,0:T(8,128)(2,1)S(1)}, u32[]{:S(2)}, u32[]{:S(2)}) collective-permute-start(bf16[2,640,256]{2,1,0:T(8,128)(2,1)S(1)} %collective-permute-done.1.refs_2_), channel_id=1, source_target_pairs={{0,1},{1,0},{2,3},{3,2},{4,5},{5,4},{6,7},{7,6},{8,9},{9,8},{10,11... | collective-permute-start | bytes 1966088 | tf_op jit(solution)/shard_map/ppermute | solution.py:331
  23.8 7.5 %collective-permute-start.7 = (bf16[1,128,256]{2,1,0:T(8,128)(2,1)S(1)}, bf16[1,128,256]{2,1,0:T(8,128)(2,1)S(1)}, u32[]{:S(2)}, u32[]{:S(2)}) collective-permute-start(bf16[1,128,256]{2,1,0:T(8,128)(2,1)S(1)} %get-tuple-element.56), channel_id=1, source_target_pairs={{0,4},{4,8},{8,12},{12,16},{16,20},{20,24},{24,28},{28,0},{1,5},{5... | collective-permute-start | bytes 196616 | tf_op jit(solution)/shard_map/ppermute | solution.py:337
  25.9 12.3 %collective-permute-start.10 = (bf16[1,640,256]{2,1,0:T(8,128)(2,1)S(1)}, bf16[1,640,256]{2,1,0:T(8,128)(2,1)S(1)}, u32[]{:S(2)}, u32[]{:S(2)}) collective-permute-start(bf16[1,640,256]{2,1,0:T(8,128)(2,1)S(1)} %get-tuple-element.55.refs_4_), channel_id=1, source_target_pairs={{0,2},{1,3},{2,0},{3,1},{4,6},{5,7},{6,4},{7,5},{8,10},{9,11},{10,... | collective-permute-start | bytes 983048 | tf_op jit(solution)/shard_map/ppermute | solution.py:334
  27.4 12.0 %collective-permute-start.9 = (bf16[1,640,256]{2,1,0:T(8,128)(2,1)S(1)}, bf16[1,640,256]{2,1,0:T(8,128)(2,1)S(1)}, u32[]{:S(2)}, u32[]{:S(2)}) collective-permute-start(bf16[1,640,256]{2,1,0:T(8,128)(2,1)S(1)} %get-tuple-element.55.refs_4_), channel_id=1, source_target_pairs={{0,1},{1,0},{2,3},{3,2},{4,5},{5,4},{6,7},{7,6},{8,9},{9,8},{10,11... | collective-permute-start | bytes 983048 | tf_op jit(solution)/shard_map/ppermute | solution.py:331
  31.4 1.7 %collective-permute-start.8 = (bf16[2,384,256]{2,1,0:T(8,128)(2,1)S(1)}, bf16[2,384,256]{2,1,0:T(8,128)(2,1)S(1)}, u32[]{:S(2)}, u32[]{:S(2)}) collective-permute-start(bf16[2,384,256]{2,1,0:T(8,128)(2,1)S(1)} %collective-permute-done.6.refs_2_), channel_id=1, source_target_pairs={{0,1},{1,0},{2,3},{3,2},{4,5},{5,4},{6,7},{7,6},{8,9},{9,8},{10,11... | collective-permute-start | bytes 1179656 | tf_op jit(solution)/shard_map/ppermute | solution.py:331
  33.8 7.0 %collective-permute-start.14 = (bf16[1,384,256]{2,1,0:T(8,128)(2,1)S(1)}, bf16[1,384,256]{2,1,0:T(8,128)(2,1)S(1)}, u32[]{:S(2)}, u32[]{:S(2)}) collective-permute-start(bf16[1,384,256]{2,1,0:T(8,128)(2,1)S(1)} %get-tuple-element.66.refs_0_), channel_id=1, source_target_pairs={{0,2},{1,3},{2,0},{3,1},{4,6},{5,7},{6,4},{7,5},{8,10},{9,11},{10,... | collective-permute-start | bytes 589832 | tf_op jit(solution)/shard_map/ppermute | solution.py:334
  35.4 5.4 %collective-permute-start.13 = (bf16[1,384,256]{2,1,0:T(8,128)(2,1)S(1)}, bf16[1,384,256]{2,1,0:T(8,128)(2,1)S(1)}, u32[]{:S(2)}, u32[]{:S(2)}) collective-permute-start(bf16[1,384,256]{2,1,0:T(8,128)(2,1)S(1)} %get-tuple-element.66.refs_0_), channel_id=1, source_target_pairs={{0,1},{1,0},{2,3},{3,2},{4,5},{5,4},{6,7},{7,6},{8,9},{9,8},{10,11... | collective-permute-start | bytes 589832 | tf_op jit(solution)/shard_map/ppermute | solution.py:331
  35.4 5.1 %collective-permute-start.12 = (bf16[1,128,256]{2,1,0:T(8,128)(2,1)S(1)}, bf16[1,128,256]{2,1,0:T(8,128)(2,1)S(1)}, u32[]{:S(2)}, u32[]{:S(2)}) collective-permute-start(bf16[1,128,256]{2,1,0:T(8,128)(2,1)S(1)} %get-tuple-element.71), channel_id=1, source_target_pairs={{4,0},{8,4},{12,8},{16,12},{20,16},{24,20},{28,24},{0,28},{5,1},{9... | collective-permute-start | bytes 196616 | tf_op jit(solution)/shard_map/ppermute | solution.py:340
  38.2 1.6 %collective-permute-start.11 = (bf16[1,640,256]{2,1,0:T(8,128)(2,1)S(1)}, bf16[1,640,256]{2,1,0:T(8,128)(2,1)S(1)}, u32[]{:S(2)}, u32[]{:S(2)}) collective-permute-start(bf16[1,640,256]{2,1,0:T(8,128)(2,1)S(1)} %collective-permute-done.10.far_ref), channel_id=1, source_target_pairs={{0,1},{1,0},{2,3},{3,2},{4,5},{5,4},{6,7},{7,6},{8,9},{9,8},{10,11... | collective-permute-start | bytes 983048 | tf_op jit(solution)/shard_map/ppermute | solution.py:331
  40.8 1.4 %collective-permute-start.15 = (bf16[1,384,256]{2,1,0:T(8,128)(2,1)S(1)}, bf16[1,384,256]{2,1,0:T(8,128)(2,1)S(1)}, u32[]{:S(2)}, u32[]{:S(2)}) collective-permute-start(bf16[1,384,256]{2,1,0:T(8,128)(2,1)S(1)} %collective-permute-done.14.refs_2_), channel_id=1, source_target_pairs={{0,1},{1,0},{2,3},{3,2},{4,5},{5,4},{6,7},{7,6},{8,9},{9,8},{10,11... | collective-permute-start | bytes 589832 | tf_op jit(solution)/shard_map/ppermute | solution.py:331

commit v7 on v6

--- a/solution.py
+++ b/solution.py
@@ -47,34 +47,48 @@
     )(*args)
 
 
+def runs_of(cells):
+    runs = []
+    for i, x in enumerate(cells):
+        if runs and x == sum(runs[-1][1:]):
+            runs[-1][2] += 1
+        else:
+            runs.append([i, x, 1])
+    return runs
+
+
 def load_chunk(fields, cells, with_faces):
     xcount, ycount, owned = fields[0].shape
     count = len(fields)
+    runs = runs_of(cells)
 
     def body(*refs):
         field_refs, held_refs, out_ref = refs[:count], refs[count:2 * count], refs[2 * count]
         sems = refs[-1]
-        copies = []
+        copies = {}
         for f in range(count):
-            for i, x in enumerate(cells):
-                copies.append(pltpu.make_async_copy(field_refs[f].at[x], held_refs[f].at[i], sems.at[f, i]))
-                copies[-1].start()
+            for r, (i, x, size) in enumerate(runs):
+                copies[f, r] = pltpu.make_async_copy(
+                    field_refs[f].at[pl.ds(x, size)], held_refs[f].at[pl.ds(i, size)], sems.at[f, r]
+                )
+                copies[f, r].start()
         for f in range(count):
-            for i, x in enumerate(cells):
-                copies[f * len(cells) + i].wait()
-                value = held_refs[f][i].astype(BF16)
-                out_ref[f, i * ycount:(i + 1) * ycount, :] = value
-                if with_faces and x == 0:
-                    refs[2 * count + 1][f] = value
-                if with_faces and x == xcount - 1:
-                    refs[2 * count + 2][f] = value
+            for r, (start, _, size) in enumerate(runs):
+                copies[f, r].wait()
+                for i in range(start, start + size):
+                    value = held_refs[f][i].astype(BF16)
+                    out_ref[f, i * ycount:(i + 1) * ycount, :] = value
+                    if with_faces and cells[i] == 0:
+                        refs[2 * count + 1][f] = value
+                    if with_faces and cells[i] == xcount - 1:
+                        refs[2 * count + 2][f] = value
 
     outs = [pltpu.VMEM((len(cells), ycount, owned), F32)] * count
     outs.append(pltpu.VMEM((count, len(cells) * ycount, owned), BF16))
     if with_faces:
         outs += [pltpu.VMEM((count, ycount, owned), BF16)] * 2
     return call(
-        body, "load_chunk", fields, outs, scratch=[pltpu.SemaphoreType.DMA((count, len(cells)))],
+        body, "load_chunk", fields, outs, scratch=[pltpu.SemaphoreType.DMA((count, len(runs)))],
         specs=[FROM_HBM] * count,
     )
 

time: 43.4 us -> 43.3 us (level)
  no operation moved by 1% of the time
where the time goes in v7:
time: 43.3 us; the launch traced here: 43.1 us
  starting transfers between devices  16.6 us (38%)
  waiting for transfers between devices  14.4 us (33%)
  Pallas kernels  11.3 us (26%)
  between operations  0.77 us (2%)
    pallas_call x11, Pallas kernels, call(): pl.pallas_call(body, out_shape=outs, in_specs=specs, out_specs=out_specs...  11.3 us
    ppermute x2, waiting for transfers between devices, from_below(): lax.ppermute(tail, 'gx', [(i, (i + 1) % gcount) for i in range(gcount)])  6.68 us
    ppermute x4, starting transfers between devices, to_far(): return lax.ppermute(v, 'trait', [(i, i ^ 2) for i in range(traits)])  6.57 us
    ppermute x2, starting transfers between devices, from_above(): lax.ppermute(head, 'gx', [((i + 1) % gcount, i) for i in range(gcount)])  6.03 us
    ppermute x4, waiting for transfers between devices, to_far(): return lax.ppermute(v, 'trait', [(i, i ^ 2) for i in range(traits)])  4.58 us
    ppermute x2, starting transfers between devices, from_below(): lax.ppermute(tail, 'gx', [(i, (i + 1) % gcount) for i in range(gcount)])  3.63 us
    ppermute x8, waiting for transfers between devices, to_sibling(): return lax.ppermute(v, 'trait', [(i, i ^ 1) for i in range(traits)])  2.05 us
    ppermute x2, waiting for transfers between devices, from_above(): lax.ppermute(head, 'gx', [((i + 1) % gcount, i) for i in range(gcount)])  1.13 us
  transfers between devices with their start and end apart: 16, of which 10 were waited for; matrix products, arithmetic and copies ran while one was open for 0% of the time, Pallas kernels for 21%

profile of v7, /device:TPU:0, one launch (start us, length us, event | category | flops | bytes accessed | tf_op | source)
XLA Modules:
  0.0 43.1 jit_solution(6053993604966844287)
XLA Ops:
  0.6 1.3 %load_chunk.2 = (f32[5,128,256]{2,1,0:T(8,128)S(1)}, f32[5,128,256]{2,1,0:T(8,128)S(1)}, bf16[2,640,256]{2,1,0:T(8,128)(2,1)S(1)}, bf16[2,128,256]{2,1,0:T(8,128)(2,1)S(1)}, bf16[2,128,256]{2,1,0:T(8,128)(2,1)S(1)}) custom-call(f32[8,128,256]{2,1,0:T(8,128)} %refs_0_.2, f32[8,128,256]{2,1,0:T(8,128)} %refs_1_.3), custom_call_target="tpu_custom_call" | custom-call | tf_op jit(solution)/shard_map/load_chunk/pallas_call | solution.py:37
  2.0 0.0 copy-start.3
  2.0 3.0 %collective-permute-start.1 = (bf16[2,640,256]{2,1,0:T(8,128)(2,1)S(1)}, bf16[2,640,256]{2,1,0:T(8,128)(2,1)S(1)}, u32[]{:S(2)}, u32[]{:S(2)}) collective-permute-start(bf16[2,640,256]{2,1,0:T(8,128)(2,1)S(1)} %get-tuple-element.42.refs_0_), channel_id=1, source_target_pairs={{0,2},{1,3},{2,0},{3,1},{4,6},{5,7},{6,4},{7,5},{8,10},{9,11},{10,... | collective-permute-start | bytes 1966088 | tf_op jit(solution)/shard_map/ppermute | solution.py:348
  5.0 1.1 %load_chunk.3 = (f32[3,128,256]{2,1,0:T(8,128)S(1)}, f32[3,128,256]{2,1,0:T(8,128)S(1)}, bf16[2,384,256]{2,1,0:T(8,128)(2,1)S(1)}) custom-call(f32[8,128,256]{2,1,0:T(8,128)} %refs_0_.2, f32[8,128,256]{2,1,0:T(8,128)} %refs_1_.3), custom_call_target="tpu_custom_call" | custom-call | tf_op jit(solution)/shard_map/load_chunk/pallas_call | solution.py:37
  6.2 0.0 copy-start
  6.2 0.1 collective-permute-start
  6.3 1.5 %collective-permute-start.2 = (bf16[2,128,256]{2,1,0:T(8,128)(2,1)S(1)}, bf16[2,128,256]{2,1,0:T(8,128)(2,1)S(1)}, u32[]{:S(2)}, u32[]{:S(2)}) collective-permute-start(bf16[2,128,256]{2,1,0:T(8,128)(2,1)S(1)} %get-tuple-element.49), channel_id=1, source_target_pairs={{0,4},{4,8},{8,12},{12,16},{16,20},{20,24},{24,28},{28,0},{1,5},{5... | collective-permute-start | bytes 393224 | tf_op jit(solution)/shard_map/ppermute | solution.py:351
  7.8 3.2 %collective-permute-start.3 = (bf16[2,128,256]{2,1,0:T(8,128)(2,1)S(1)}, bf16[2,128,256]{2,1,0:T(8,128)(2,1)S(1)}, u32[]{:S(2)}, u32[]{:S(2)}) collective-permute-start(bf16[2,128,256]{2,1,0:T(8,128)(2,1)S(1)} %get-tuple-element.50), channel_id=1, source_target_pairs={{4,0},{8,4},{12,8},{16,12},{20,16},{24,20},{28,24},{0,28},{5,1},{9... | collective-permute-start | bytes 393224 | tf_op jit(solution)/shard_map/ppermute | solution.py:354
  11.0 0.4 collective-permute-start.6
  11.4 3.6 %collective-permute-done.2.refs_4_ = bf16[2,128,256]{2,1,0:T(8,128)(2,1)S(1)} collective-permute-done((bf16[2,128,256]{2,1,0:T(8,128)(2,1)S(1)}, bf16[2,128,256]{2,1,0:T(8,128)(2,1)S(1)}, u32[]{:S(2)}, u32[]{:S(2)}) %collective-permute-start.2) | collective-permute-done | bytes 131104 | tf_op jit(solution)/shard_map/ppermute | solution.py:351
  15.0 0.0 collective-permute-start.5
  15.0 1.1 %collective-permute-done.3.refs_5_ = bf16[2,128,256]{2,1,0:T(8,128)(2,1)S(1)} collective-permute-done((bf16[2,128,256]{2,1,0:T(8,128)(2,1)S(1)}, bf16[2,128,256]{2,1,0:T(8,128)(2,1)S(1)}, u32[]{:S(2)}, u32[]{:S(2)}) %collective-permute-start.3) | collective-permute-done | bytes 131104 | tf_op jit(solution)/shard_map/ppermute | solution.py:354
  16.2 0.0 copy-done.3
  16.2 0.9 %before_first.1 = (f32[2,5,128,256]{3,2,1,0:T(8,128)S(1)}, f32[2,3,128,256]{3,2,1,0:T(8,128)S(1)}) custom-call(f32[5,128,256]{2,1,0:T(8,128)S(1)} %get-tuple-element.43.refs_0_.one_ref, f32[3,128,256]{2,1,0:T(8,128)S(1)} %get-tuple-element.44.refs_1_.one_ref, f32[5,128,256]{2,1,0:T(8,128)S(1)} %get-tuple-element.45.refs_2_.two_ref, ...), custom_call_target="tpu_custom_call" | custom-call | tf_op jit(solution)/shard_map/before_first/pallas_call | solution.py:37
  17.1 3.5 %collective-permute-done.1.refs_2_ = bf16[2,640,256]{2,1,0:T(8,128)(2,1)S(1)} collective-permute-done((bf16[2,640,256]{2,1,0:T(8,128)(2,1)S(1)}, bf16[2,640,256]{2,1,0:T(8,128)(2,1)S(1)}, u32[]{:S(2)}, u32[]{:S(2)}) %collective-permute-start.1) | collective-permute-done | bytes 655392 | tf_op jit(solution)/shard_map/ppermute | solution.py:348
  20.6 0.0 collective-permute-start.4
  20.6 0.0 collective-permute-done.refs_1_
  20.6 0.0 copy-done
  20.6 1.2 %early_part.2.part_ref = f32[2,1280,256]{2,1,0:T(8,128)S(1)} custom-call(bf16[2,640,256]{2,1,0:T(8,128)(2,1)S(1)} %get-tuple-element.42.refs_0_, bf16[2,640,256]{2,1,0:T(8,128)(2,1)S(1)} %collective-permute-done.refs_1_, bf16[2,640,256]{2,1,0:T(8,128)(2,1)S(1)} %collective-permute-done.1.refs_2_, bf16[2,1024,256]{2,1,0:T(8,128)(2,1)S(1)} %copy-done), custom_call_target="tpu_custom_call" | custom-call | flops 20000000000 | tf_op jit(solution)/shard_map/early_part/pallas_call | solution.py:37
  21.8 0.9 %collective-permute-done.4.last_ref = bf16[2,640,256]{2,1,0:T(8,128)(2,1)S(1)} collective-permute-done((bf16[2,640,256]{2,1,0:T(8,128)(2,1)S(1)}, bf16[2,640,256]{2,1,0:T(8,128)(2,1)S(1)}, u32[]{:S(2)}, u32[]{:S(2)}) %collective-permute-start.4) | collective-permute-done | bytes 655392 | tf_op jit(solution)/shard_map/ppermute | solution.py:345
  22.7 0.0 copy-done.1
  22.7 1.0 %first_node.2 = (f32[5,128,256]{2,1,0:T(8,128)S(1)}, bf16[1,640,256]{2,1,0:T(8,128)(2,1)S(1)}, f32[5,128,256]{2,1,0:T(8,128)S(1)}, bf16[1,128,256]{2,1,0:T(8,128)(2,1)S(1)}, bf16[1,128,256]{2,1,0:T(8,128)(2,1)S(1)}) custom-call(f32[2,1280,256]{2,1,0:T(8,128)S(1)} %early_part.2.part_ref, bf16[2,640,256]{2,1,0:T(8,128)(2,1)S(1)} %collective-permute-done.4.last_ref, ...), custom_call_target="tpu_custom_call" | custom-call | tf_op jit(solution)/shard_map/first_node/pallas_call | solution.py:37
  23.7 2.1 %collective-permute-start.7 = (bf16[1,128,256]{2,1,0:T(8,128)(2,1)S(1)}, bf16[1,128,256]{2,1,0:T(8,128)(2,1)S(1)}, u32[]{:S(2)}, u32[]{:S(2)}) collective-permute-start(bf16[1,128,256]{2,1,0:T(8,128)(2,1)S(1)} %get-tuple-element.56), channel_id=1, source_target_pairs={{0,4},{4,8},{8,12},{12,16},{16,20},{20,24},{24,28},{28,0},{1,5},{5... | collective-permute-start | bytes 196616 | tf_op jit(solution)/shard_map/ppermute | solution.py:351
  25.8 1.5 %collective-permute-start.10 = (bf16[1,640,256]{2,1,0:T(8,128)(2,1)S(1)}, bf16[1,640,256]{2,1,0:T(8,128)(2,1)S(1)}, u32[]{:S(2)}, u32[]{:S(2)}) collective-permute-start(bf16[1,640,256]{2,1,0:T(8,128)(2,1)S(1)} %get-tuple-element.55.refs_4_), channel_id=1, source_target_pairs={{0,2},{1,3},{2,0},{3,1},{4,6},{5,7},{6,4},{7,5},{8,10},{9,11},{10,... | collective-permute-start | bytes 983048 | tf_op jit(solution)/shard_map/ppermute | solution.py:348
  27.3 0.0 collective-permute-start.9
  27.3 0.8 %collective-permute-done.6.refs_2_ = bf16[2,384,256]{2,1,0:T(8,128)(2,1)S(1)} collective-permute-done((bf16[2,384,256]{2,1,0:T(8,128)(2,1)S(1)}, bf16[2,384,256]{2,1,0:T(8,128)(2,1)S(1)}, u32[]{:S(2)}, u32[]{:S(2)}) %collective-permute-start.6) | collective-permute-done | bytes 393248 | tf_op jit(solution)/shard_map/ppermute | solution.py:348
  28.2 3.1 %collective-permute-done.7.lo_ref = bf16[1,128,256]{2,1,0:T(8,128)(2,1)S(1)} collective-permute-done((bf16[1,128,256]{2,1,0:T(8,128)(2,1)S(1)}, bf16[1,128,256]{2,1,0:T(8,128)(2,1)S(1)}, u32[]{:S(2)}, u32[]{:S(2)}) %collective-permute-start.7) | collective-permute-done | bytes 65568 | tf_op jit(solution)/shard_map/ppermute | solution.py:351
  31.2 0.0 collective-permute-start.8
  31.2 0.0 collective-permute-done.5.refs_1_
  31.2 1.1 %early_part.3 = (f32[2,768,256]{2,1,0:T(8,128)S(1)}, f32[8,128,256]{2,1,0:T(8,128)}) custom-call(bf16[2,384,256]{2,1,0:T(8,128)(2,1)S(1)} %get-tuple-element.41.refs_0_, bf16[2,384,256]{2,1,0:T(8,128)(2,1)S(1)} %collective-permute-done.5.refs_1_, bf16[2,384,256]{2,1,0:T(8,128)(2,1)S(1)} %collective-permute-done.6.refs_2_, bf16[2,1024,256]{2,1,0:T(8,128)(2,1)S(1)} %copy-done, ...), custom_call_target="tpu_custom_call" | custom-call | flops 20000000000 | tf_op jit(solution)/shard_map/early_part/pallas_call | solution.py:37
  32.3 0.7 %collective-permute-done.8.last_ref = bf16[2,384,256]{2,1,0:T(8,128)(2,1)S(1)} collective-permute-done((bf16[2,384,256]{2,1,0:T(8,128)(2,1)S(1)}, bf16[2,384,256]{2,1,0:T(8,128)(2,1)S(1)}, u32[]{:S(2)}, u32[]{:S(2)}) %collective-permute-start.8) | collective-permute-done | bytes 393248 | tf_op jit(solution)/shard_map/ppermute | solution.py:345
  32.9 0.7 %first_node.3 = (f32[3,128,256]{2,1,0:T(8,128)S(1)}, bf16[1,384,256]{2,1,0:T(8,128)(2,1)S(1)}, f32[3,128,256]{2,1,0:T(8,128)S(1)}) custom-call(f32[2,768,256]{2,1,0:T(8,128)S(1)} %get-tuple-element.58.part_ref, bf16[2,384,256]{2,1,0:T(8,128)(2,1)S(1)} %collective-permute-done.8.last_ref, f32[2,3,128,256]{3,2,1,0:T(8,128)S(1)} %get-tuple-element.59.base_ref, ...), custom_call_target="tpu_custom_call" | custom-call | tf_op jit(solution)/shard_map/first_node/pallas_call | solution.py:37
  33.7 1.6 %collective-permute-start.14 = (bf16[1,384,256]{2,1,0:T(8,128)(2,1)S(1)}, bf16[1,384,256]{2,1,0:T(8,128)(2,1)S(1)}, u32[]{:S(2)}, u32[]{:S(2)}) collective-permute-start(bf16[1,384,256]{2,1,0:T(8,128)(2,1)S(1)} %get-tuple-element.66.refs_0_), channel_id=1, source_target_pairs={{0,2},{1,3},{2,0},{3,1},{4,6},{5,7},{6,4},{7,5},{8,10},{9,11},{10,... | collective-permute-start | bytes 589832 | tf_op jit(solution)/shard_map/ppermute | solution.py:348
  35.3 0.0 collective-permute-start.13
  35.3 2.8 %collective-permute-start.12 = (bf16[1,128,256]{2,1,0:T(8,128)(2,1)S(1)}, bf16[1,128,256]{2,1,0:T(8,128)(2,1)S(1)}, u32[]{:S(2)}, u32[]{:S(2)}) collective-permute-start(bf16[1,128,256]{2,1,0:T(8,128)(2,1)S(1)} %get-tuple-element.71), channel_id=1, source_target_pairs={{4,0},{8,4},{12,8},{16,12},{20,16},{24,20},{28,24},{0,28},{5,1},{9... | collective-permute-start | bytes 196616 | tf_op jit(solution)/shard_map/ppermute | solution.py:354
  38.1 0.0 collective-permute-done.10.far_ref
  38.1 0.2 collective-permute-start.11
  38.3 0.9 %before_second.1 = (f32[8,128,256]{2,1,0:T(8,128)}, f32[2,640,256]{2,1,0:T(8,128)S(1)}, f32[5,128,256]{2,1,0:T(8,128)S(1)}, f32[3,128,256]{2,1,0:T(8,128)S(1)}) custom-call(f32[5,128,256]{2,1,0:T(8,128)S(1)} %get-tuple-element.54.refs_4_.refs_0_.new_ref, f32[3,128,256]{2,1,0:T(8,128)S(1)} %get-tuple-element.60.refs_1_.new_ref, ...), custom_call_target="tpu_custom_call", output_to_operand_aliasing={{0}: (8, {})} | custom-call | flops 20000000000 | tf_op jit(solution)/shard_map/before_second/pallas_call | solution.py:37
  39.3 0.0 collective-permute-done.9.sib_ref
  39.3 0.4 %collective-permute-done.11.farsib_ref = bf16[1,640,256]{2,1,0:T(8,128)(2,1)S(1)} collective-permute-done((bf16[1,640,256]{2,1,0:T(8,128)(2,1)S(1)}, bf16[1,640,256]{2,1,0:T(8,128)(2,1)S(1)}, u32[]{:S(2)}, u32[]{:S(2)}) %collective-permute-start.11) | collective-permute-done | bytes 327712 | tf_op jit(solution)/shard_map/ppermute | solution.py:345
  39.7 0.7 %whole_sums.1.sums_ref = bf16[2,640,256]{2,1,0:T(8,128)(2,1)S(1)} custom-call(f32[2,640,256]{2,1,0:T(8,128)S(1)} %get-tuple-element.65.part_ref, bf16[1,640,256]{2,1,0:T(8,128)(2,1)S(1)} %collective-permute-done.9.sib_ref, bf16[1,640,256]{2,1,0:T(8,128)(2,1)S(1)} %collective-permute-done.10.far_ref, ...), custom_call_target="tpu_custom_call" | custom-call | tf_op jit(solution)/shard_map/whole_sums/pallas_call | solution.py:37
  40.4 0.0 collective-permute-done.12.hi_ref
  40.4 0.3 collective-permute-done.14.refs_2_
  40.7 0.1 collective-permute-start.15
  40.7 0.0 collective-permute-done.13.refs_1_
  40.7 1.3 %second_first.1 = (f32[8,128,256]{2,1,0:T(8,128)}, f32[2,384,256]{2,1,0:T(8,128)S(1)}) custom-call(bf16[2,640,256]{2,1,0:T(8,128)(2,1)S(1)} %whole_sums.1.sums_ref, f32[5,128,256]{2,1,0:T(8,128)S(1)} %get-tuple-element.68.base_ref, f32[5,128,256]{2,1,0:T(8,128)S(1)} %get-tuple-element.54.refs_4_.refs_0_.new_ref, f32[1,256]{1,0:T(1,128)S(1)} %bitcast.5, ...), custom_call_target="tpu_custom_call" | custom-call | tf_op jit(solution)/shard_map/second_first/pallas_call | solution.py:37
  42.0 0.1 collective-permute-done.15.last_ref
  42.1 1.0 %second_last.1 = f32[8,128,256]{2,1,0:T(8,128)} custom-call(f32[2,384,256]{2,1,0:T(8,128)S(1)} %get-tuple-element.73.part_ref, bf16[1,384,256]{2,1,0:T(8,128)(2,1)S(1)} %collective-permute-done.15.last_ref, f32[3,128,256]{2,1,0:T(8,128)S(1)} %get-tuple-element.74.base_ref, ...), custom_call_target="tpu_custom_call", output_to_operand_aliasing={{}: (6, {})} | custom-call | tf_op jit(solution)/shard_map/second_last/pallas_call | solution.py:37
  (3 shorter events, 0.0 us)
Async XLA Ops:
  2.0 14.2 %copy-start.3 = (f32[256]{0:T(256)S(1)}, f32[256]{0:T(256)}, u32[]{:S(2)}) copy-start(f32[256]{0:T(256)} %param.10) | copy-start | bytes 3076
  2.0 18.6 %collective-permute-start.1 = (bf16[2,640,256]{2,1,0:T(8,128)(2,1)S(1)}, bf16[2,640,256]{2,1,0:T(8,128)(2,1)S(1)}, u32[]{:S(2)}, u32[]{:S(2)}) collective-permute-start(bf16[2,640,256]{2,1,0:T(8,128)(2,1)S(1)} %get-tuple-element.42.refs_0_), channel_id=1, source_target_pairs={{0,2},{1,3},{2,0},{3,1},{4,6},{5,7},{6,4},{7,5},{8,10},{9,11},{10,... | collective-permute-start | bytes 1966088 | tf_op jit(solution)/shard_map/ppermute | solution.py:348
  6.2 14.4 %copy-start = (bf16[2,1024,256]{2,1,0:T(8,128)(2,1)S(1)}, bf16[2,1024,256]{2,1,0:T(8,128)(2,1)}, u32[]{:S(2)}) copy-start(bf16[2,1024,256]{2,1,0:T(8,128)(2,1)} %k_ref.4) | copy-start | bytes 3145732
  6.2 14.4 %collective-permute-start = (bf16[2,640,256]{2,1,0:T(8,128)(2,1)S(1)}, bf16[2,640,256]{2,1,0:T(8,128)(2,1)S(1)}, u32[]{:S(2)}, u32[]{:S(2)}) collective-permute-start(bf16[2,640,256]{2,1,0:T(8,128)(2,1)S(1)} %get-tuple-element.42.refs_0_), channel_id=1, source_target_pairs={{0,1},{1,0},{2,3},{3,2},{4,5},{5,4},{6,7},{7,6},{8,9},{9,8},{10,11... | collective-permute-start | bytes 1966088 | tf_op jit(solution)/shard_map/ppermute | solution.py:345
  6.3 8.8 %collective-permute-start.2 = (bf16[2,128,256]{2,1,0:T(8,128)(2,1)S(1)}, bf16[2,128,256]{2,1,0:T(8,128)(2,1)S(1)}, u32[]{:S(2)}, u32[]{:S(2)}) collective-permute-start(bf16[2,128,256]{2,1,0:T(8,128)(2,1)S(1)} %get-tuple-element.49), channel_id=1, source_target_pairs={{0,4},{4,8},{8,12},{12,16},{16,20},{20,24},{24,28},{28,0},{1,5},{5... | collective-permute-start | bytes 393224 | tf_op jit(solution)/shard_map/ppermute | solution.py:351
  7.8 8.4 %collective-permute-start.3 = (bf16[2,128,256]{2,1,0:T(8,128)(2,1)S(1)}, bf16[2,128,256]{2,1,0:T(8,128)(2,1)S(1)}, u32[]{:S(2)}, u32[]{:S(2)}) collective-permute-start(bf16[2,128,256]{2,1,0:T(8,128)(2,1)S(1)} %get-tuple-element.50), channel_id=1, source_target_pairs={{4,0},{8,4},{12,8},{16,12},{20,16},{24,20},{28,24},{0,28},{5,1},{9... | collective-permute-start | bytes 393224 | tf_op jit(solution)/shard_map/ppermute | solution.py:354
  11.0 17.1 %collective-permute-start.6 = (bf16[2,384,256]{2,1,0:T(8,128)(2,1)S(1)}, bf16[2,384,256]{2,1,0:T(8,128)(2,1)S(1)}, u32[]{:S(2)}, u32[]{:S(2)}) collective-permute-start(bf16[2,384,256]{2,1,0:T(8,128)(2,1)S(1)} %get-tuple-element.41.refs_0_), channel_id=1, source_target_pairs={{0,2},{1,3},{2,0},{3,1},{4,6},{5,7},{6,4},{7,5},{8,10},{9,11},{10,... | collective-permute-start | bytes 1179656 | tf_op jit(solution)/shard_map/ppermute | solution.py:348
  15.0 16.2 %collective-permute-start.5 = (bf16[2,384,256]{2,1,0:T(8,128)(2,1)S(1)}, bf16[2,384,256]{2,1,0:T(8,128)(2,1)S(1)}, u32[]{:S(2)}, u32[]{:S(2)}) collective-permute-start(bf16[2,384,256]{2,1,0:T(8,128)(2,1)S(1)} %get-tuple-element.41.refs_0_), channel_id=1, source_target_pairs={{0,1},{1,0},{2,3},{3,2},{4,5},{5,4},{6,7},{7,6},{8,9},{9,8},{10,11... | collective-permute-start | bytes 1179656 | tf_op jit(solution)/shard_map/ppermute | solution.py:345
  20.6 2.1 %copy-start.1 = (f32[8,128,256]{2,1,0:T(8,128)S(1)}, f32[8,128,256]{2,1,0:T(8,128)}, u32[]{:S(2)}) copy-start(f32[8,128,256]{2,1,0:T(8,128)} %init_ref.3) | copy-start | bytes 3145732
  20.6 2.1 %copy-start.2 = (f32[256]{0:T(256)S(1)}, f32[256]{0:T(256)}, u32[]{:S(2)}) copy-start(f32[256]{0:T(256)} %param.11) | copy-start | bytes 3076
  20.6 2.1 %collective-permute-start.4 = (bf16[2,640,256]{2,1,0:T(8,128)(2,1)S(1)}, bf16[2,640,256]{2,1,0:T(8,128)(2,1)S(1)}, u32[]{:S(2)}, u32[]{:S(2)}) collective-permute-start(bf16[2,640,256]{2,1,0:T(8,128)(2,1)S(1)} %collective-permute-done.1.refs_2_), channel_id=1, source_target_pairs={{0,1},{1,0},{2,3},{3,2},{4,5},{5,4},{6,7},{7,6},{8,9},{9,8},{10,11... | collective-permute-start | bytes 1966088 | tf_op jit(solution)/shard_map/ppermute | solution.py:345
  23.7 7.5 %collective-permute-start.7 = (bf16[1,128,256]{2,1,0:T(8,128)(2,1)S(1)}, bf16[1,128,256]{2,1,0:T(8,128)(2,1)S(1)}, u32[]{:S(2)}, u32[]{:S(2)}) collective-permute-start(bf16[1,128,256]{2,1,0:T(8,128)(2,1)S(1)} %get-tuple-element.56), channel_id=1, source_target_pairs={{0,4},{4,8},{8,12},{12,16},{16,20},{20,24},{24,28},{28,0},{1,5},{5... | collective-permute-start | bytes 196616 | tf_op jit(solution)/shard_map/ppermute | solution.py:351
  25.8 12.3 %collective-permute-start.10 = (bf16[1,640,256]{2,1,0:T(8,128)(2,1)S(1)}, bf16[1,640,256]{2,1,0:T(8,128)(2,1)S(1)}, u32[]{:S(2)}, u32[]{:S(2)}) collective-permute-start(bf16[1,640,256]{2,1,0:T(8,128)(2,1)S(1)} %get-tuple-element.55.refs_4_), channel_id=1, source_target_pairs={{0,2},{1,3},{2,0},{3,1},{4,6},{5,7},{6,4},{7,5},{8,10},{9,11},{10,... | collective-permute-start | bytes 983048 | tf_op jit(solution)/shard_map/ppermute | solution.py:348
  27.3 12.0 %collective-permute-start.9 = (bf16[1,640,256]{2,1,0:T(8,128)(2,1)S(1)}, bf16[1,640,256]{2,1,0:T(8,128)(2,1)S(1)}, u32[]{:S(2)}, u32[]{:S(2)}) collective-permute-start(bf16[1,640,256]{2,1,0:T(8,128)(2,1)S(1)} %get-tuple-element.55.refs_4_), channel_id=1, source_target_pairs={{0,1},{1,0},{2,3},{3,2},{4,5},{5,4},{6,7},{7,6},{8,9},{9,8},{10,11... | collective-permute-start | bytes 983048 | tf_op jit(solution)/shard_map/ppermute | solution.py:345
  31.2 1.7 %collective-permute-start.8 = (bf16[2,384,256]{2,1,0:T(8,128)(2,1)S(1)}, bf16[2,384,256]{2,1,0:T(8,128)(2,1)S(1)}, u32[]{:S(2)}, u32[]{:S(2)}) collective-permute-start(bf16[2,384,256]{2,1,0:T(8,128)(2,1)S(1)} %collective-permute-done.6.refs_2_), channel_id=1, source_target_pairs={{0,1},{1,0},{2,3},{3,2},{4,5},{5,4},{6,7},{7,6},{8,9},{9,8},{10,11... | collective-permute-start | bytes 1179656 | tf_op jit(solution)/shard_map/ppermute | solution.py:345
  33.7 7.0 %collective-permute-start.14 = (bf16[1,384,256]{2,1,0:T(8,128)(2,1)S(1)}, bf16[1,384,256]{2,1,0:T(8,128)(2,1)S(1)}, u32[]{:S(2)}, u32[]{:S(2)}) collective-permute-start(bf16[1,384,256]{2,1,0:T(8,128)(2,1)S(1)} %get-tuple-element.66.refs_0_), channel_id=1, source_target_pairs={{0,2},{1,3},{2,0},{3,1},{4,6},{5,7},{6,4},{7,5},{8,10},{9,11},{10,... | collective-permute-start | bytes 589832 | tf_op jit(solution)/shard_map/ppermute | solution.py:348
  35.3 5.4 %collective-permute-start.13 = (bf16[1,384,256]{2,1,0:T(8,128)(2,1)S(1)}, bf16[1,384,256]{2,1,0:T(8,128)(2,1)S(1)}, u32[]{:S(2)}, u32[]{:S(2)}) collective-permute-start(bf16[1,384,256]{2,1,0:T(8,128)(2,1)S(1)} %get-tuple-element.66.refs_0_), channel_id=1, source_target_pairs={{0,1},{1,0},{2,3},{3,2},{4,5},{5,4},{6,7},{7,6},{8,9},{9,8},{10,11... | collective-permute-start | bytes 589832 | tf_op jit(solution)/shard_map/ppermute | solution.py:345
  35.3 5.1 %collective-permute-start.12 = (bf16[1,128,256]{2,1,0:T(8,128)(2,1)S(1)}, bf16[1,128,256]{2,1,0:T(8,128)(2,1)S(1)}, u32[]{:S(2)}, u32[]{:S(2)}) collective-permute-start(bf16[1,128,256]{2,1,0:T(8,128)(2,1)S(1)} %get-tuple-element.71), channel_id=1, source_target_pairs={{4,0},{8,4},{12,8},{16,12},{20,16},{24,20},{28,24},{0,28},{5,1},{9... | collective-permute-start | bytes 196616 | tf_op jit(solution)/shard_map/ppermute | solution.py:354
  38.1 1.6 %collective-permute-start.11 = (bf16[1,640,256]{2,1,0:T(8,128)(2,1)S(1)}, bf16[1,640,256]{2,1,0:T(8,128)(2,1)S(1)}, u32[]{:S(2)}, u32[]{:S(2)}) collective-permute-start(bf16[1,640,256]{2,1,0:T(8,128)(2,1)S(1)} %collective-permute-done.10.far_ref), channel_id=1, source_target_pairs={{0,1},{1,0},{2,3},{3,2},{4,5},{5,4},{6,7},{7,6},{8,9},{9,8},{10,11... | collective-permute-start | bytes 983048 | tf_op jit(solution)/shard_map/ppermute | solution.py:345
  40.7 1.4 %collective-permute-start.15 = (bf16[1,384,256]{2,1,0:T(8,128)(2,1)S(1)}, bf16[1,384,256]{2,1,0:T(8,128)(2,1)S(1)}, u32[]{:S(2)}, u32[]{:S(2)}) collective-permute-start(bf16[1,384,256]{2,1,0:T(8,128)(2,1)S(1)} %collective-permute-done.14.refs_2_), channel_id=1, source_target_pairs={{0,1},{1,0},{2,3},{3,2},{4,5},{5,4},{6,7},{7,6},{8,9},{9,8},{10,11... | collective-permute-start | bytes 589832 | tf_op jit(solution)/shard_map/ppermute | solution.py:345

commit v8 on v7

--- a/solution.py
+++ b/solution.py
@@ -215,27 +215,25 @@
     )
 
 
-def before_second(news, rests, growth, death, begun, blocks, kernels, chunks):
+def before_second(news, rests, growth, death, begun, owns, kernels, chunks):
     _, ycount, owned = news[0].shape
-    rows = blocks[0].shape[1]
     xcount = sum(len(cells) for cells in chunks)
     count = len(chunks)
-    size = len(blocks)
     place = {x: (c, i) for c, cells in enumerate(chunks) for i, x in enumerate(cells)}
 
     def body(*refs):
-        new_refs, rest_refs, block_refs = refs[:count], refs[count:2 * count], refs[2 * count:2 * count + size]
-        k_ref, g_ref, d_ref, _, whole_ref, part_ref = refs[2 * count + size:2 * count + size + 6]
-        base_refs, sems = refs[2 * count + size + 6:-1], refs[-1]
+        new_refs, rest_refs = refs[:count], refs[count:2 * count]
+        own_refs, (k_ref, g_ref, d_ref, _, whole_ref) = refs[2 * count:3 * count], refs[3 * count:3 * count + 5]
+        part_refs, base_refs, sems = refs[3 * count + 5:4 * count + 5], refs[4 * count + 5:-1], refs[-1]
         copies = [
             pltpu.make_async_copy(new_refs[-1].at[i], whole_ref.at[x], sems.at[i]) for i, x in enumerate(chunks[-1])
         ]
         for copy in copies:
             copy.start()
         me = lax.axis_index("trait")
-        values = [r[...].reshape(rows, owned) for r in block_refs]
-        for k in range(2):
-            part_ref[k] = blocks_dot(values, k_ref, k, [me ^ j for j in range(size)])
+        for part_ref, own_ref in zip(part_refs, own_refs):
+            for k in range(2):
+                part_ref[k] = blocks_dot([own_ref[...].reshape(-1, owned)], k_ref, k, [me])
         growth = g_ref[...]
         factor = SECOND / (1.0 + SECOND * d_ref[...])
         for x, (c, i) in place.items():
@@ -248,9 +246,10 @@
         for copy in copies:
             copy.wait()
 
-    outs = [jax.ShapeDtypeStruct((xcount, ycount, owned), F32), pltpu.VMEM((2, rows, owned), F32)]
+    outs = [jax.ShapeDtypeStruct((xcount, ycount, owned), F32)]
+    outs += [pltpu.VMEM((2, len(cells) * ycount, owned), F32) for cells in chunks]
     outs += [pltpu.VMEM((len(cells), ycount, owned), F32) for cells in chunks]
-    args = [*news, *rests, *blocks, kernels, growth, death, begun]
+    args = [*news, *rests, *owns, kernels, growth, death, begun]
     return call(
         body, "before_second", args, outs, scratch=[pltpu.SemaphoreType.DMA((len(chunks[-1]),))],
         specs=[SPEC] * (len(args) - 1) + [FROM_HBM], out_specs=[ANYWHERE] + [SPEC] * (len(outs) - 1), gflop=20.0,
@@ -270,66 +269,64 @@
     return call(body, "whole_sums", [part, *blocks, kernels], [pltpu.VMEM((2, rows, owned), BF16)])[0]
 
 
-def finish(cells, ycount, sums, base_ref, new_ref, factor, faces, held, out_ref, sems):
-    copies = []
-    for i, x in enumerate(cells):
-        at = pl.ds(i * ycount, ycount)
-        e = sums[1, at, :].astype(F32) - new_ref[i] * sums[0, at, :].astype(F32)
-        if x in faces:
-            e = e + DIFFUSION * faces[x][0].astype(F32)
-        held[i] = base_ref[i] + factor * e
-        copies.append(pltpu.make_async_copy(held.at[i], out_ref.at[x], sems.at[i]))
-        copies[-1].start()
-    return copies
-
-
-def second_first(sums, base, new, death, lo, hi, blocks, kernels, cells, xcount):
+def second_first(sums, base, new, death, lo, hi, cells, part, sib, far, base_b, new_b, kernels, xcount):
     _, ycount, owned = new.shape
-    rows = blocks[0].shape[1]
-    count = len(blocks)
-
-    def body(sums_ref, base_ref, new_ref, d_ref, lo_ref, hi_ref, k_ref, *refs):
-        block_refs = refs[:count]
-        out_ref, part_ref, held, sems = refs[count:]
+    rows = far.shape[1]
+
+    def body(sums_ref, base_ref, new_ref, d_ref, lo_ref, hi_ref, part_ref, sib_ref, far_ref, base_b_ref, new_b_ref, *refs):
+        k_ref, out_ref, base_out_ref, held, sems = refs
         factor = SECOND / (1.0 + SECOND * d_ref[...])
         faces = {0: lo_ref, xcount - 1: hi_ref}
-        copies = finish(cells, ycount, sums_ref, base_ref, new_ref, factor, faces, held, out_ref, sems)
-        me = lax.axis_index("trait")
-        values = [r[...].reshape(rows, owned) for r in block_refs]
-        for k in range(2):
-            part_ref[k] = blocks_dot(values, k_ref, k, [me ^ j for j in range(count)])
+        copies = []
+        for i, x in enumerate(cells):
+            at = pl.ds(i * ycount, ycount)
+            e = sums_ref[1, at, :].astype(F32) - new_ref[i] * sums_ref[0, at, :].astype(F32)
+            if x in faces:
+                e = e + DIFFUSION * faces[x][0].astype(F32)
+            held[i] = base_ref[i] + factor * e
+            copies.append(pltpu.make_async_copy(held.at[i], out_ref.at[x], sems.at[i]))
+            copies[-1].start()
+        me = lax.axis_index("trait")
+        values = [r[...].reshape(rows, owned) for r in (sib_ref, far_ref)]
+        compete, mutate = (part_ref[k] + blocks_dot(values, k_ref, k, [me ^ 1, me ^ 2]) for k in range(2))
+        for i in range(rows // ycount):
+            at = slice(i * ycount, (i + 1) * ycount)
+            base_out_ref[i] = base_b_ref[i] + factor * (mutate[at] - new_b_ref[i] * compete[at])
         for copy in copies:
             copy.wait()
 
     return call(
-        body, "second_first", [sums, base, new, death, lo, hi, kernels, *blocks],
-        [jax.ShapeDtypeStruct((xcount, ycount, owned), F32), pltpu.VMEM((2, rows, owned), F32)],
+        body, "second_first", [sums, base, new, death, lo, hi, part, sib, far, base_b, new_b, kernels],
+        [jax.ShapeDtypeStruct((xcount, ycount, owned), F32), pltpu.VMEM(base_b.shape, F32)],
         scratch=[pltpu.VMEM((len(cells), ycount, owned), F32), pltpu.SemaphoreType.DMA((len(cells),))],
         out_specs=[ANYWHERE, SPEC],
     )
 
 
-def second_last(part, last, base, new, death, kernels, begun, cells, xcount):
+def second_last(last, base, new, death, kernels, begun, cells, xcount):
     _, ycount, owned = new.shape
     rows = len(cells) * ycount
 
-    def body(part_ref, last_ref, base_ref, new_ref, d_ref, k_ref, begun_ref, out_ref, sums, held, sems):
-        me = lax.axis_index("trait")
-        for k in range(2):
-            sums[k] = (part_ref[k] + blocks_dot([last_ref[...].reshape(rows, owned)], k_ref, k, [me ^ 3])).astype(BF16)
+    def body(last_ref, base_ref, new_ref, d_ref, k_ref, begun_ref, out_ref, held, sems):
+        me = lax.axis_index("trait")
+        compete, mutate = (
+            blocks_dot([last_ref[...].reshape(rows, owned)], k_ref, k, [me ^ 3]) for k in range(2)
+        )
         factor = SECOND / (1.0 + SECOND * d_ref[...])
-        for copy in finish(cells, ycount, sums, base_ref, new_ref, factor, {}, held, out_ref, sems):
+        copies = []
+        for i, x in enumerate(cells):
+            at = slice(i * ycount, (i + 1) * ycount)
+            held[i] = base_ref[i] + factor * (mutate[at] - new_ref[i] * compete[at])
+            copies.append(pltpu.make_async_copy(held.at[i], out_ref.at[x], sems.at[i]))
+            copies[-1].start()
+        for copy in copies:
             copy.wait()
 
     return call(
-        body, "second_last", [part, last, base, new, death, kernels, begun],
+        body, "second_last", [last, base, new, death, kernels, begun],
         [jax.ShapeDtypeStruct((xcount, ycount, owned), F32)],
-        scratch=[
-            pltpu.VMEM((2, rows, owned), BF16),
-            pltpu.VMEM((len(cells), ycount, owned), F32),
-            pltpu.SemaphoreType.DMA((len(cells),)),
-        ],
-        specs=[SPEC] * 6 + [FROM_HBM], out_specs=[ANYWHERE], alias={6: 0},
+        scratch=[pltpu.VMEM((len(cells), ycount, owned), F32), pltpu.SemaphoreType.DMA((len(cells),))],
+        specs=[SPEC] * 5 + [FROM_HBM], out_specs=[ANYWHERE], alias={5: 0},
     )[0]
 
 
@@ -383,16 +380,17 @@
     new_hi = from_above(after(new_head, rounded_b))
     nfar_a = after(nfar_a, rounded_b)
     nfarsib_a = to_sibling(nfar_a)
-    new_one, npart_a, nbase_a, nbase_b = before_second(
-        (new_a, new_b), (rest_a, rest_b), growth, death, new_one, [rounded_a], kernels, chunks
+    new_one, npart_a, npart_b, nbase_a, nbase_b = before_second(
+        (new_a, new_b), (rest_a, rest_b), growth, death, new_one, (rounded_a, rounded_b), kernels, chunks
     )
     sums_a = whole_sums(npart_a, [nsib_a, nfar_a, nfarsib_a], after(kernels, nbase_a))
     nfar_b = after(nfar_b, sums_a, new_hi)
     nfarsib_b = to_sibling(nfar_b)
-    begun, npart_b = second_first(
-        sums_a, nbase_a, new_a, death, new_lo, new_hi, [rounded_b, nsib_b, nfar_b], kernels, chunks[0], xcount
-    )
-    new_two = second_last(npart_b, nfarsib_b, nbase_b, new_b, death, kernels, begun, chunks[1], xcount)
+    begun, nbase_b = second_first(
+        sums_a, nbase_a, new_a, death, new_lo, new_hi, chunks[0], npart_b, nsib_b, nfar_b, nbase_b, new_b,
+        kernels, xcount,
+    )
+    new_two = second_last(nfarsib_b, nbase_b, new_b, death, kernels, begun, chunks[1], xcount)
     return new_one, new_two
 
 

time: 43.3 us -> 43.2 us (level)
  no operation moved by 1% of the time
where the time goes in v8:
time: 43.2 us; the launch traced here: 43.1 us
  starting transfers between devices  16.6 us (38%)
  waiting for transfers between devices  14.3 us (33%)
  Pallas kernels  11.4 us (26%)
  between operations  0.77 us (2%)
    pallas_call x11, Pallas kernels, call(): pl.pallas_call(body, out_shape=outs, in_specs=specs, out_specs=out_specs...  11.4 us
    ppermute x2, waiting for transfers between devices, from_below(): lax.ppermute(tail, 'gx', [(i, (i + 1) % gcount) for i in range(gcount)])  6.68 us
    ppermute x4, starting transfers between devices, to_far(): return lax.ppermute(v, 'trait', [(i, i ^ 2) for i in range(traits)])  6.57 us
    ppermute x2, starting transfers between devices, from_above(): lax.ppermute(head, 'gx', [((i + 1) % gcount, i) for i in range(gcount)])  6.03 us
    ppermute x4, waiting for transfers between devices, to_far(): return lax.ppermute(v, 'trait', [(i, i ^ 2) for i in range(traits)])  4.58 us
    ppermute x2, starting transfers between devices, from_below(): lax.ppermute(tail, 'gx', [(i, (i + 1) % gcount) for i in range(gcount)])  3.63 us
    ppermute x8, waiting for transfers between devices, to_sibling(): return lax.ppermute(v, 'trait', [(i, i ^ 1) for i in range(traits)])  1.95 us
    ppermute x2, waiting for transfers between devices, from_above(): lax.ppermute(head, 'gx', [((i + 1) % gcount, i) for i in range(gcount)])  1.13 us
  transfers between devices with their start and end apart: 16, of which 10 were waited for; matrix products, arithmetic and copies ran while one was open for 0% of the time, Pallas kernels for 21%

profile of v8, /device:TPU:0, one launch (start us, length us, event | category | flops | bytes accessed | tf_op | source)
XLA Modules:
  0.0 43.1 jit_solution(5803477145230411394)
XLA Ops:
  0.6 1.3 %load_chunk.2 = (f32[5,128,256]{2,1,0:T(8,128)S(1)}, f32[5,128,256]{2,1,0:T(8,128)S(1)}, bf16[2,640,256]{2,1,0:T(8,128)(2,1)S(1)}, bf16[2,128,256]{2,1,0:T(8,128)(2,1)S(1)}, bf16[2,128,256]{2,1,0:T(8,128)(2,1)S(1)}) custom-call(f32[8,128,256]{2,1,0:T(8,128)} %refs_0_.2, f32[8,128,256]{2,1,0:T(8,128)} %refs_1_.3), custom_call_target="tpu_custom_call" | custom-call | tf_op jit(solution)/shard_map/load_chunk/pallas_call | solution.py:37
  2.0 0.0 copy-start.3
  2.0 3.0 %collective-permute-start.1 = (bf16[2,640,256]{2,1,0:T(8,128)(2,1)S(1)}, bf16[2,640,256]{2,1,0:T(8,128)(2,1)S(1)}, u32[]{:S(2)}, u32[]{:S(2)}) collective-permute-start(bf16[2,640,256]{2,1,0:T(8,128)(2,1)S(1)} %get-tuple-element.43.refs_0_), channel_id=1, source_target_pairs={{0,2},{1,3},{2,0},{3,1},{4,6},{5,7},{6,4},{7,5},{8,10},{9,11},{10,... | collective-permute-start | bytes 1966088 | tf_op jit(solution)/shard_map/ppermute | solution.py:345
  5.0 1.1 %load_chunk.3 = (f32[3,128,256]{2,1,0:T(8,128)S(1)}, f32[3,128,256]{2,1,0:T(8,128)S(1)}, bf16[2,384,256]{2,1,0:T(8,128)(2,1)S(1)}) custom-call(f32[8,128,256]{2,1,0:T(8,128)} %refs_0_.2, f32[8,128,256]{2,1,0:T(8,128)} %refs_1_.3), custom_call_target="tpu_custom_call" | custom-call | tf_op jit(solution)/shard_map/load_chunk/pallas_call | solution.py:37
  6.2 0.0 copy-start
  6.2 0.1 collective-permute-start
  6.3 1.5 %collective-permute-start.2 = (bf16[2,128,256]{2,1,0:T(8,128)(2,1)S(1)}, bf16[2,128,256]{2,1,0:T(8,128)(2,1)S(1)}, u32[]{:S(2)}, u32[]{:S(2)}) collective-permute-start(bf16[2,128,256]{2,1,0:T(8,128)(2,1)S(1)} %get-tuple-element.50), channel_id=1, source_target_pairs={{0,4},{4,8},{8,12},{12,16},{16,20},{20,24},{24,28},{28,0},{1,5},{5... | collective-permute-start | bytes 393224 | tf_op jit(solution)/shard_map/ppermute | solution.py:348
  7.8 3.2 %collective-permute-start.3 = (bf16[2,128,256]{2,1,0:T(8,128)(2,1)S(1)}, bf16[2,128,256]{2,1,0:T(8,128)(2,1)S(1)}, u32[]{:S(2)}, u32[]{:S(2)}) collective-permute-start(bf16[2,128,256]{2,1,0:T(8,128)(2,1)S(1)} %get-tuple-element.51), channel_id=1, source_target_pairs={{4,0},{8,4},{12,8},{16,12},{20,16},{24,20},{28,24},{0,28},{5,1},{9... | collective-permute-start | bytes 393224 | tf_op jit(solution)/shard_map/ppermute | solution.py:351
  11.0 0.4 collective-permute-start.6
  11.4 3.6 %collective-permute-done.2.refs_4_ = bf16[2,128,256]{2,1,0:T(8,128)(2,1)S(1)} collective-permute-done((bf16[2,128,256]{2,1,0:T(8,128)(2,1)S(1)}, bf16[2,128,256]{2,1,0:T(8,128)(2,1)S(1)}, u32[]{:S(2)}, u32[]{:S(2)}) %collective-permute-start.2) | collective-permute-done | bytes 131104 | tf_op jit(solution)/shard_map/ppermute | solution.py:348
  15.0 0.0 collective-permute-start.5
  15.0 1.1 %collective-permute-done.3.refs_5_ = bf16[2,128,256]{2,1,0:T(8,128)(2,1)S(1)} collective-permute-done((bf16[2,128,256]{2,1,0:T(8,128)(2,1)S(1)}, bf16[2,128,256]{2,1,0:T(8,128)(2,1)S(1)}, u32[]{:S(2)}, u32[]{:S(2)}) %collective-permute-start.3) | collective-permute-done | bytes 131104 | tf_op jit(solution)/shard_map/ppermute | solution.py:351
  16.2 0.0 copy-done.3
  16.2 0.9 %before_first.1 = (f32[2,5,128,256]{3,2,1,0:T(8,128)S(1)}, f32[2,3,128,256]{3,2,1,0:T(8,128)S(1)}) custom-call(f32[5,128,256]{2,1,0:T(8,128)S(1)} %get-tuple-element.44.refs_0_.one_ref, f32[3,128,256]{2,1,0:T(8,128)S(1)} %get-tuple-element.45.refs_1_.one_ref, f32[5,128,256]{2,1,0:T(8,128)S(1)} %get-tuple-element.46.refs_2_.two_ref, ...), custom_call_target="tpu_custom_call" | custom-call | tf_op jit(solution)/shard_map/before_first/pallas_call | solution.py:37
  17.1 3.5 %collective-permute-done.1.refs_2_ = bf16[2,640,256]{2,1,0:T(8,128)(2,1)S(1)} collective-permute-done((bf16[2,640,256]{2,1,0:T(8,128)(2,1)S(1)}, bf16[2,640,256]{2,1,0:T(8,128)(2,1)S(1)}, u32[]{:S(2)}, u32[]{:S(2)}) %collective-permute-start.1) | collective-permute-done | bytes 655392 | tf_op jit(solution)/shard_map/ppermute | solution.py:345
  20.6 0.0 collective-permute-start.4
  20.6 0.0 collective-permute-done.refs_1_
  20.6 0.0 copy-done
  20.6 1.2 %early_part.2.part_ref = f32[2,1280,256]{2,1,0:T(8,128)S(1)} custom-call(bf16[2,640,256]{2,1,0:T(8,128)(2,1)S(1)} %get-tuple-element.43.refs_0_, bf16[2,640,256]{2,1,0:T(8,128)(2,1)S(1)} %collective-permute-done.refs_1_, bf16[2,640,256]{2,1,0:T(8,128)(2,1)S(1)} %collective-permute-done.1.refs_2_, bf16[2,1024,256]{2,1,0:T(8,128)(2,1)S(1)} %copy-done), custom_call_target="tpu_custom_call" | custom-call | flops 20000000000 | tf_op jit(solution)/shard_map/early_part/pallas_call | solution.py:37
  21.8 0.9 %collective-permute-done.4.last_ref = bf16[2,640,256]{2,1,0:T(8,128)(2,1)S(1)} collective-permute-done((bf16[2,640,256]{2,1,0:T(8,128)(2,1)S(1)}, bf16[2,640,256]{2,1,0:T(8,128)(2,1)S(1)}, u32[]{:S(2)}, u32[]{:S(2)}) %collective-permute-start.4) | collective-permute-done | bytes 655392 | tf_op jit(solution)/shard_map/ppermute | solution.py:342
  22.7 0.0 copy-done.1
  22.7 1.0 %first_node.2 = (f32[5,128,256]{2,1,0:T(8,128)S(1)}, bf16[1,640,256]{2,1,0:T(8,128)(2,1)S(1)}, f32[5,128,256]{2,1,0:T(8,128)S(1)}, bf16[1,128,256]{2,1,0:T(8,128)(2,1)S(1)}, bf16[1,128,256]{2,1,0:T(8,128)(2,1)S(1)}) custom-call(f32[2,1280,256]{2,1,0:T(8,128)S(1)} %early_part.2.part_ref, bf16[2,640,256]{2,1,0:T(8,128)(2,1)S(1)} %collective-permute-done.4.last_ref, ...), custom_call_target="tpu_custom_call" | custom-call | tf_op jit(solution)/shard_map/first_node/pallas_call | solution.py:37
  23.7 2.1 %collective-permute-start.7 = (bf16[1,128,256]{2,1,0:T(8,128)(2,1)S(1)}, bf16[1,128,256]{2,1,0:T(8,128)(2,1)S(1)}, u32[]{:S(2)}, u32[]{:S(2)}) collective-permute-start(bf16[1,128,256]{2,1,0:T(8,128)(2,1)S(1)} %get-tuple-element.57), channel_id=1, source_target_pairs={{0,4},{4,8},{8,12},{12,16},{16,20},{20,24},{24,28},{28,0},{1,5},{5... | collective-permute-start | bytes 196616 | tf_op jit(solution)/shard_map/ppermute | solution.py:348
  25.8 1.5 %collective-permute-start.11 = (bf16[1,640,256]{2,1,0:T(8,128)(2,1)S(1)}, bf16[1,640,256]{2,1,0:T(8,128)(2,1)S(1)}, u32[]{:S(2)}, u32[]{:S(2)}) collective-permute-start(bf16[1,640,256]{2,1,0:T(8,128)(2,1)S(1)} %get-tuple-element.56.refs_4_), channel_id=1, source_target_pairs={{0,2},{1,3},{2,0},{3,1},{4,6},{5,7},{6,4},{7,5},{8,10},{9,11},{10,... | collective-permute-start | bytes 983048 | tf_op jit(solution)/shard_map/ppermute | solution.py:345
  27.3 0.0 collective-permute-start.10
  27.3 0.8 %collective-permute-done.6.refs_2_ = bf16[2,384,256]{2,1,0:T(8,128)(2,1)S(1)} collective-permute-done((bf16[2,384,256]{2,1,0:T(8,128)(2,1)S(1)}, bf16[2,384,256]{2,1,0:T(8,128)(2,1)S(1)}, u32[]{:S(2)}, u32[]{:S(2)}) %collective-permute-start.6) | collective-permute-done | bytes 393248 | tf_op jit(solution)/shard_map/ppermute | solution.py:345
  28.2 3.1 %collective-permute-done.7.lo_ref = bf16[1,128,256]{2,1,0:T(8,128)(2,1)S(1)} collective-permute-done((bf16[1,128,256]{2,1,0:T(8,128)(2,1)S(1)}, bf16[1,128,256]{2,1,0:T(8,128)(2,1)S(1)}, u32[]{:S(2)}, u32[]{:S(2)}) %collective-permute-start.7) | collective-permute-done | bytes 65568 | tf_op jit(solution)/shard_map/ppermute | solution.py:348
  31.2 0.0 collective-permute-start.8
  31.2 0.0 collective-permute-done.5.refs_1_
  31.2 1.0 %early_part.3 = (f32[2,768,256]{2,1,0:T(8,128)S(1)}, f32[8,128,256]{2,1,0:T(8,128)}) custom-call(bf16[2,384,256]{2,1,0:T(8,128)(2,1)S(1)} %get-tuple-element.42.refs_0_, bf16[2,384,256]{2,1,0:T(8,128)(2,1)S(1)} %collective-permute-done.5.refs_1_, bf16[2,384,256]{2,1,0:T(8,128)(2,1)S(1)} %collective-permute-done.6.refs_2_, bf16[2,1024,256]{2,1,0:T(8,128)(2,1)S(1)} %copy-done, ...), custom_call_target="tpu_custom_call" | custom-call | flops 20000000000 | tf_op jit(solution)/shard_map/early_part/pallas_call | solution.py:37
  32.3 0.7 %collective-permute-done.8.last_ref = bf16[2,384,256]{2,1,0:T(8,128)(2,1)S(1)} collective-permute-done((bf16[2,384,256]{2,1,0:T(8,128)(2,1)S(1)}, bf16[2,384,256]{2,1,0:T(8,128)(2,1)S(1)}, u32[]{:S(2)}, u32[]{:S(2)}) %collective-permute-start.8) | collective-permute-done | bytes 393248 | tf_op jit(solution)/shard_map/ppermute | solution.py:342
  32.9 0.7 %first_node.3 = (f32[3,128,256]{2,1,0:T(8,128)S(1)}, bf16[1,384,256]{2,1,0:T(8,128)(2,1)S(1)}, f32[3,128,256]{2,1,0:T(8,128)S(1)}) custom-call(f32[2,768,256]{2,1,0:T(8,128)S(1)} %get-tuple-element.59.part_ref, bf16[2,384,256]{2,1,0:T(8,128)(2,1)S(1)} %collective-permute-done.8.last_ref, f32[2,3,128,256]{3,2,1,0:T(8,128)S(1)} %get-tuple-element.60.base_ref, ...), custom_call_target="tpu_custom_call" | custom-call | tf_op jit(solution)/shard_map/first_node/pallas_call | solution.py:37
  33.6 1.6 %collective-permute-start.9 = (bf16[1,384,256]{2,1,0:T(8,128)(2,1)S(1)}, bf16[1,384,256]{2,1,0:T(8,128)(2,1)S(1)}, u32[]{:S(2)}, u32[]{:S(2)}) collective-permute-start(bf16[1,384,256]{2,1,0:T(8,128)(2,1)S(1)} %get-tuple-element.64.refs_5_), channel_id=1, source_target_pairs={{0,2},{1,3},{2,0},{3,1},{4,6},{5,7},{6,4},{7,5},{8,10},{9,11},{10,... | collective-permute-start | bytes 589832 | tf_op jit(solution)/shard_map/ppermute | solution.py:345
  35.3 0.0 collective-permute-start.15
  35.3 2.8 %collective-permute-start.13 = (bf16[1,128,256]{2,1,0:T(8,128)(2,1)S(1)}, bf16[1,128,256]{2,1,0:T(8,128)(2,1)S(1)}, u32[]{:S(2)}, u32[]{:S(2)}) collective-permute-start(bf16[1,128,256]{2,1,0:T(8,128)(2,1)S(1)} %get-tuple-element.72), channel_id=1, source_target_pairs={{4,0},{8,4},{12,8},{16,12},{20,16},{24,20},{28,24},{0,28},{5,1},{9... | collective-permute-start | bytes 196616 | tf_op jit(solution)/shard_map/ppermute | solution.py:351
  38.1 0.0 collective-permute-done.11.far_ref
  38.1 0.2 collective-permute-start.12
  38.3 1.0 %before_second.1 = (f32[8,128,256]{2,1,0:T(8,128)}, f32[2,640,256]{2,1,0:T(8,128)S(1)}, f32[2,384,256]{2,1,0:T(8,128)S(1)}, f32[5,128,256]{2,1,0:T(8,128)S(1)}, f32[3,128,256]{2,1,0:T(8,128)S(1)}) custom-call(f32[5,128,256]{2,1,0:T(8,128)S(1)} %get-tuple-element.55.refs_4_.refs_0_.new_ref, ...), custom_call_target="tpu_custom_call", output_to_operand_aliasing={{0}: (9, {})} | custom-call | flops 20000000000 | tf_op jit(solution)/shard_map/before_second/pallas_call | solution.py:37
  39.4 0.0 collective-permute-done.10.sib_ref
  39.4 0.3 collective-permute-done.12.farsib_ref
  39.7 0.7 %whole_sums.1.sums_ref = bf16[2,640,256]{2,1,0:T(8,128)(2,1)S(1)} custom-call(f32[2,640,256]{2,1,0:T(8,128)S(1)} %get-tuple-element.67.part_ref, bf16[1,640,256]{2,1,0:T(8,128)(2,1)S(1)} %collective-permute-done.10.sib_ref, bf16[1,640,256]{2,1,0:T(8,128)(2,1)S(1)} %collective-permute-done.11.far_ref, ...), custom_call_target="tpu_custom_call" | custom-call | tf_op jit(solution)/shard_map/whole_sums/pallas_call | solution.py:37
  40.4 0.0 collective-permute-done.13.hi_ref
  40.4 0.3 collective-permute-done.9.far_ref
  40.7 0.1 collective-permute-start.14
  40.7 0.0 collective-permute-done.15.sib_ref
  40.7 1.3 %second_first.1 = (f32[8,128,256]{2,1,0:T(8,128)}, f32[3,128,256]{2,1,0:T(8,128)S(1)}) custom-call(bf16[2,640,256]{2,1,0:T(8,128)(2,1)S(1)} %whole_sums.1.sums_ref, f32[5,128,256]{2,1,0:T(8,128)S(1)} %get-tuple-element.69.base_ref, f32[5,128,256]{2,1,0:T(8,128)S(1)} %get-tuple-element.55.refs_4_.refs_0_.new_ref, f32[1,256]{1,0:T(1,128)S(1)} %bitcast.5, ...), custom_call_target="tpu_custom_call" | custom-call | tf_op jit(solution)/shard_map/second_first/pallas_call | solution.py:37
  42.0 0.1 collective-permute-done.14.last_ref
  42.1 1.0 %second_last.1 = f32[8,128,256]{2,1,0:T(8,128)} custom-call(bf16[1,384,256]{2,1,0:T(8,128)(2,1)S(1)} %collective-permute-done.14.last_ref, f32[3,128,256]{2,1,0:T(8,128)S(1)} %get-tuple-element.76.base_ref, f32[3,128,256]{2,1,0:T(8,128)S(1)} %get-tuple-element.61.refs_1_.new_b_ref.new_ref, f32[1,256]{1,0:T(1,128)S(1)} %bitcast.6, ...), custom_call_target="tpu_custom_call", output_to_operand_aliasing={{}: (5, {})} | custom-call | tf_op jit(solution)/shard_map/second_last/pallas_call | solution.py:37
  (3 shorter events, 0.0 us)
Async XLA Ops:
  2.0 14.2 %copy-start.3 = (f32[256]{0:T(256)S(1)}, f32[256]{0:T(256)}, u32[]{:S(2)}) copy-start(f32[256]{0:T(256)} %param.10) | copy-start | bytes 3076
  2.0 18.6 %collective-permute-start.1 = (bf16[2,640,256]{2,1,0:T(8,128)(2,1)S(1)}, bf16[2,640,256]{2,1,0:T(8,128)(2,1)S(1)}, u32[]{:S(2)}, u32[]{:S(2)}) collective-permute-start(bf16[2,640,256]{2,1,0:T(8,128)(2,1)S(1)} %get-tuple-element.43.refs_0_), channel_id=1, source_target_pairs={{0,2},{1,3},{2,0},{3,1},{4,6},{5,7},{6,4},{7,5},{8,10},{9,11},{10,... | collective-permute-start | bytes 1966088 | tf_op jit(solution)/shard_map/ppermute | solution.py:345
  6.2 14.4 %copy-start = (bf16[2,1024,256]{2,1,0:T(8,128)(2,1)S(1)}, bf16[2,1024,256]{2,1,0:T(8,128)(2,1)}, u32[]{:S(2)}) copy-start(bf16[2,1024,256]{2,1,0:T(8,128)(2,1)} %k_ref.3) | copy-start | bytes 3145732
  6.2 14.4 %collective-permute-start = (bf16[2,640,256]{2,1,0:T(8,128)(2,1)S(1)}, bf16[2,640,256]{2,1,0:T(8,128)(2,1)S(1)}, u32[]{:S(2)}, u32[]{:S(2)}) collective-permute-start(bf16[2,640,256]{2,1,0:T(8,128)(2,1)S(1)} %get-tuple-element.43.refs_0_), channel_id=1, source_target_pairs={{0,1},{1,0},{2,3},{3,2},{4,5},{5,4},{6,7},{7,6},{8,9},{9,8},{10,11... | collective-permute-start | bytes 1966088 | tf_op jit(solution)/shard_map/ppermute | solution.py:342
  6.3 8.8 %collective-permute-start.2 = (bf16[2,128,256]{2,1,0:T(8,128)(2,1)S(1)}, bf16[2,128,256]{2,1,0:T(8,128)(2,1)S(1)}, u32[]{:S(2)}, u32[]{:S(2)}) collective-permute-start(bf16[2,128,256]{2,1,0:T(8,128)(2,1)S(1)} %get-tuple-element.50), channel_id=1, source_target_pairs={{0,4},{4,8},{8,12},{12,16},{16,20},{20,24},{24,28},{28,0},{1,5},{5... | collective-permute-start | bytes 393224 | tf_op jit(solution)/shard_map/ppermute | solution.py:348
  7.8 8.4 %collective-permute-start.3 = (bf16[2,128,256]{2,1,0:T(8,128)(2,1)S(1)}, bf16[2,128,256]{2,1,0:T(8,128)(2,1)S(1)}, u32[]{:S(2)}, u32[]{:S(2)}) collective-permute-start(bf16[2,128,256]{2,1,0:T(8,128)(2,1)S(1)} %get-tuple-element.51), channel_id=1, source_target_pairs={{4,0},{8,4},{12,8},{16,12},{20,16},{24,20},{28,24},{0,28},{5,1},{9... | collective-permute-start | bytes 393224 | tf_op jit(solution)/shard_map/ppermute | solution.py:351
  11.0 17.1 %collective-permute-start.6 = (bf16[2,384,256]{2,1,0:T(8,128)(2,1)S(1)}, bf16[2,384,256]{2,1,0:T(8,128)(2,1)S(1)}, u32[]{:S(2)}, u32[]{:S(2)}) collective-permute-start(bf16[2,384,256]{2,1,0:T(8,128)(2,1)S(1)} %get-tuple-element.42.refs_0_), channel_id=1, source_target_pairs={{0,2},{1,3},{2,0},{3,1},{4,6},{5,7},{6,4},{7,5},{8,10},{9,11},{10,... | collective-permute-start | bytes 1179656 | tf_op jit(solution)/shard_map/ppermute | solution.py:345
  15.0 16.2 %collective-permute-start.5 = (bf16[2,384,256]{2,1,0:T(8,128)(2,1)S(1)}, bf16[2,384,256]{2,1,0:T(8,128)(2,1)S(1)}, u32[]{:S(2)}, u32[]{:S(2)}) collective-permute-start(bf16[2,384,256]{2,1,0:T(8,128)(2,1)S(1)} %get-tuple-element.42.refs_0_), channel_id=1, source_target_pairs={{0,1},{1,0},{2,3},{3,2},{4,5},{5,4},{6,7},{7,6},{8,9},{9,8},{10,11... | collective-permute-start | bytes 1179656 | tf_op jit(solution)/shard_map/ppermute | solution.py:342
  20.6 2.1 %copy-start.1 = (f32[8,128,256]{2,1,0:T(8,128)S(1)}, f32[8,128,256]{2,1,0:T(8,128)}, u32[]{:S(2)}) copy-start(f32[8,128,256]{2,1,0:T(8,128)} %init_ref.3) | copy-start | bytes 3145732
  20.6 2.1 %copy-start.2 = (f32[256]{0:T(256)S(1)}, f32[256]{0:T(256)}, u32[]{:S(2)}) copy-start(f32[256]{0:T(256)} %param.11) | copy-start | bytes 3076
  20.6 2.1 %collective-permute-start.4 = (bf16[2,640,256]{2,1,0:T(8,128)(2,1)S(1)}, bf16[2,640,256]{2,1,0:T(8,128)(2,1)S(1)}, u32[]{:S(2)}, u32[]{:S(2)}) collective-permute-start(bf16[2,640,256]{2,1,0:T(8,128)(2,1)S(1)} %collective-permute-done.1.refs_2_), channel_id=1, source_target_pairs={{0,1},{1,0},{2,3},{3,2},{4,5},{5,4},{6,7},{7,6},{8,9},{9,8},{10,11... | collective-permute-start | bytes 1966088 | tf_op jit(solution)/shard_map/ppermute | solution.py:342
  23.7 7.5 %collective-permute-start.7 = (bf16[1,128,256]{2,1,0:T(8,128)(2,1)S(1)}, bf16[1,128,256]{2,1,0:T(8,128)(2,1)S(1)}, u32[]{:S(2)}, u32[]{:S(2)}) collective-permute-start(bf16[1,128,256]{2,1,0:T(8,128)(2,1)S(1)} %get-tuple-element.57), channel_id=1, source_target_pairs={{0,4},{4,8},{8,12},{12,16},{16,20},{20,24},{24,28},{28,0},{1,5},{5... | collective-permute-start | bytes 196616 | tf_op jit(solution)/shard_map/ppermute | solution.py:348
  25.8 12.3 %collective-permute-start.11 = (bf16[1,640,256]{2,1,0:T(8,128)(2,1)S(1)}, bf16[1,640,256]{2,1,0:T(8,128)(2,1)S(1)}, u32[]{:S(2)}, u32[]{:S(2)}) collective-permute-start(bf16[1,640,256]{2,1,0:T(8,128)(2,1)S(1)} %get-tuple-element.56.refs_4_), channel_id=1, source_target_pairs={{0,2},{1,3},{2,0},{3,1},{4,6},{5,7},{6,4},{7,5},{8,10},{9,11},{10,... | collective-permute-start | bytes 983048 | tf_op jit(solution)/shard_map/ppermute | solution.py:345
  27.3 12.1 %collective-permute-start.10 = (bf16[1,640,256]{2,1,0:T(8,128)(2,1)S(1)}, bf16[1,640,256]{2,1,0:T(8,128)(2,1)S(1)}, u32[]{:S(2)}, u32[]{:S(2)}) collective-permute-start(bf16[1,640,256]{2,1,0:T(8,128)(2,1)S(1)} %get-tuple-element.56.refs_4_), channel_id=1, source_target_pairs={{0,1},{1,0},{2,3},{3,2},{4,5},{5,4},{6,7},{7,6},{8,9},{9,8},{10,11... | collective-permute-start | bytes 983048 | tf_op jit(solution)/shard_map/ppermute | solution.py:342
  31.2 1.7 %collective-permute-start.8 = (bf16[2,384,256]{2,1,0:T(8,128)(2,1)S(1)}, bf16[2,384,256]{2,1,0:T(8,128)(2,1)S(1)}, u32[]{:S(2)}, u32[]{:S(2)}) collective-permute-start(bf16[2,384,256]{2,1,0:T(8,128)(2,1)S(1)} %collective-permute-done.6.refs_2_), channel_id=1, source_target_pairs={{0,1},{1,0},{2,3},{3,2},{4,5},{5,4},{6,7},{7,6},{8,9},{9,8},{10,11... | collective-permute-start | bytes 1179656 | tf_op jit(solution)/shard_map/ppermute | solution.py:342
  33.6 7.0 %collective-permute-start.9 = (bf16[1,384,256]{2,1,0:T(8,128)(2,1)S(1)}, bf16[1,384,256]{2,1,0:T(8,128)(2,1)S(1)}, u32[]{:S(2)}, u32[]{:S(2)}) collective-permute-start(bf16[1,384,256]{2,1,0:T(8,128)(2,1)S(1)} %get-tuple-element.64.refs_5_), channel_id=1, source_target_pairs={{0,2},{1,3},{2,0},{3,1},{4,6},{5,7},{6,4},{7,5},{8,10},{9,11},{10,... | collective-permute-start | bytes 589832 | tf_op jit(solution)/shard_map/ppermute | solution.py:345
  35.3 5.4 %collective-permute-start.15 = (bf16[1,384,256]{2,1,0:T(8,128)(2,1)S(1)}, bf16[1,384,256]{2,1,0:T(8,128)(2,1)S(1)}, u32[]{:S(2)}, u32[]{:S(2)}) collective-permute-start(bf16[1,384,256]{2,1,0:T(8,128)(2,1)S(1)} %get-tuple-element.64.refs_5_), channel_id=1, source_target_pairs={{0,1},{1,0},{2,3},{3,2},{4,5},{5,4},{6,7},{7,6},{8,9},{9,8},{10,11... | collective-permute-start | bytes 589832 | tf_op jit(solution)/shard_map/ppermute | solution.py:342
  35.3 5.1 %collective-permute-start.13 = (bf16[1,128,256]{2,1,0:T(8,128)(2,1)S(1)}, bf16[1,128,256]{2,1,0:T(8,128)(2,1)S(1)}, u32[]{:S(2)}, u32[]{:S(2)}) collective-permute-start(bf16[1,128,256]{2,1,0:T(8,128)(2,1)S(1)} %get-tuple-element.72), channel_id=1, source_target_pairs={{4,0},{8,4},{12,8},{16,12},{20,16},{24,20},{28,24},{0,28},{5,1},{9... | collective-permute-start | bytes 196616 | tf_op jit(solution)/shard_map/ppermute | solution.py:351
  38.1 1.6 %collective-permute-start.12 = (bf16[1,640,256]{2,1,0:T(8,128)(2,1)S(1)}, bf16[1,640,256]{2,1,0:T(8,128)(2,1)S(1)}, u32[]{:S(2)}, u32[]{:S(2)}) collective-permute-start(bf16[1,640,256]{2,1,0:T(8,128)(2,1)S(1)} %collective-permute-done.11.far_ref), channel_id=1, source_target_pairs={{0,1},{1,0},{2,3},{3,2},{4,5},{5,4},{6,7},{7,6},{8,9},{9,8},{10,11... | collective-permute-start | bytes 983048 | tf_op jit(solution)/shard_map/ppermute | solution.py:342
  40.7 1.4 %collective-permute-start.14 = (bf16[1,384,256]{2,1,0:T(8,128)(2,1)S(1)}, bf16[1,384,256]{2,1,0:T(8,128)(2,1)S(1)}, u32[]{:S(2)}, u32[]{:S(2)}) collective-permute-start(bf16[1,384,256]{2,1,0:T(8,128)(2,1)S(1)} %collective-permute-done.9.far_ref), channel_id=1, source_target_pairs={{0,1},{1,0},{2,3},{3,2},{4,5},{5,4},{6,7},{7,6},{8,9},{9,8},{10,11... | collective-permute-start | bytes 589832 | tf_op jit(solution)/shard_map/ppermute | solution.py:342

commit v9 on v7

--- a/solution.py
+++ b/solution.py
@@ -142,7 +142,10 @@
             part_ref = refs[-1]
         else:
             new_ref, part_ref, whole_ref, sems = refs[count + 1:]
-            copies = [pltpu.make_async_copy(new_ref.at[i], whole_ref.at[x], sems.at[i]) for i, x in enumerate(cells)]
+            copies = [
+                pltpu.make_async_copy(new_ref.at[pl.ds(i, size)], whole_ref.at[pl.ds(x, size)], sems.at[r])
+                for r, (i, x, size) in enumerate(runs_of(cells))
+            ]
         for copy in copies:
             copy.start()
         me = lax.axis_index("trait")
@@ -158,7 +161,7 @@
         return call(body, "early_part", args, outs, gflop=20.0)[0]
     outs.append(jax.ShapeDtypeStruct((xcount, *new.shape[1:]), F32))
     return call(
-        body, "early_part", [*args, new], outs, scratch=[pltpu.SemaphoreType.DMA((len(cells),))],
+        body, "early_part", [*args, new], outs, scratch=[pltpu.SemaphoreType.DMA((len(runs_of(cells)),))],
         out_specs=[SPEC, ANYWHERE], gflop=20.0,
     )
 
@@ -228,7 +231,8 @@
         k_ref, g_ref, d_ref, _, whole_ref, part_ref = refs[2 * count + size:2 * count + size + 6]
         base_refs, sems = refs[2 * count + size + 6:-1], refs[-1]
         copies = [
-            pltpu.make_async_copy(new_refs[-1].at[i], whole_ref.at[x], sems.at[i]) for i, x in enumerate(chunks[-1])
+            pltpu.make_async_copy(new_refs[-1].at[pl.ds(i, size)], whole_ref.at[pl.ds(x, size)], sems.at[r])
+            for r, (i, x, size) in enumerate(runs_of(chunks[-1]))
         ]
         for copy in copies:
             copy.start()
@@ -252,7 +256,7 @@
     outs += [pltpu.VMEM((len(cells), ycount, owned), F32) for cells in chunks]
     args = [*news, *rests, *blocks, kernels, growth, death, begun]
     return call(
-        body, "before_second", args, outs, scratch=[pltpu.SemaphoreType.DMA((len(chunks[-1]),))],
+        body, "before_second", args, outs, scratch=[pltpu.SemaphoreType.DMA((len(runs_of(chunks[-1])),))],
         specs=[SPEC] * (len(args) - 1) + [FROM_HBM], out_specs=[ANYWHERE] + [SPEC] * (len(outs) - 1), gflop=20.0,
         alias={len(args) - 1: 0},
     )
@@ -270,15 +274,18 @@
     return call(body, "whole_sums", [part, *blocks, kernels], [pltpu.VMEM((2, rows, owned), BF16)])[0]
 
 
-def finish(cells, ycount, sums, base_ref, new_ref, factor, faces, held, out_ref, sems):
+def finish(cells, runs, ycount, sums, base_ref, new_ref, factor, faces, held, out_ref, sems):
     copies = []
-    for i, x in enumerate(cells):
-        at = pl.ds(i * ycount, ycount)
-        e = sums[1, at, :].astype(F32) - new_ref[i] * sums[0, at, :].astype(F32)
-        if x in faces:
-            e = e + DIFFUSION * faces[x][0].astype(F32)
-        held[i] = base_ref[i] + factor * e
-        copies.append(pltpu.make_async_copy(held.at[i], out_ref.at[x], sems.at[i]))
+    for r, (start, place, size) in enumerate(runs):
+        for i in range(start, start + size):
+            at = pl.ds(i * ycount, ycount)
+            e = sums[1, at, :].astype(F32) - new_ref[i] * sums[0, at, :].astype(F32)
+            if cells[i] in faces:
+                e = e + DIFFUSION * faces[cells[i]][0].astype(F32)
+            held[i] = base_ref[i] + factor * e
+        copies.append(
+            pltpu.make_async_copy(held.at[pl.ds(start, size)], out_ref.at[pl.ds(place, size)], sems.at[r])
+        )
         copies[-1].start()
     return copies
 
@@ -293,7 +300,7 @@
         out_ref, part_ref, held, sems = refs[count:]
         factor = SECOND / (1.0 + SECOND * d_ref[...])
         faces = {0: lo_ref, xcount - 1: hi_ref}
-        copies = finish(cells, ycount, sums_ref, base_ref, new_ref, factor, faces, held, out_ref, sems)
+        copies = finish(cells, runs_of(cells), ycount, sums_ref, base_ref, new_ref, factor, faces, held, out_ref, sems)
         me = lax.axis_index("trait")
         values = [r[...].reshape(rows, owned) for r in block_refs]
         for k in range(2):
@@ -304,7 +311,7 @@
     return call(
         body, "second_first", [sums, base, new, death, lo, hi, kernels, *blocks],
         [jax.ShapeDtypeStruct((xcount, ycount, owned), F32), pltpu.VMEM((2, rows, owned), F32)],
-        scratch=[pltpu.VMEM((len(cells), ycount, owned), F32), pltpu.SemaphoreType.DMA((len(cells),))],
+        scratch=[pltpu.VMEM((len(cells), ycount, owned), F32), pltpu.SemaphoreType.DMA((len(runs_of(cells)),))],
         out_specs=[ANYWHERE, SPEC],
     )
 
@@ -312,13 +319,14 @@
 def second_last(part, last, base, new, death, kernels, begun, cells, xcount):
     _, ycount, owned = new.shape
     rows = len(cells) * ycount
+    runs = runs_of(cells[:-1]) + [[len(cells) - 1, cells[-1], 1]]
 
     def body(part_ref, last_ref, base_ref, new_ref, d_ref, k_ref, begun_ref, out_ref, sums, held, sems):
         me = lax.axis_index("trait")
         for k in range(2):
             sums[k] = (part_ref[k] + blocks_dot([last_ref[...].reshape(rows, owned)], k_ref, k, [me ^ 3])).astype(BF16)
         factor = SECOND / (1.0 + SECOND * d_ref[...])
-        for copy in finish(cells, ycount, sums, base_ref, new_ref, factor, {}, held, out_ref, sems):
+        for copy in finish(cells, runs, ycount, sums, base_ref, new_ref, factor, {}, held, out_ref, sems):
             copy.wait()
 
     return call(
@@ -327,7 +335,7 @@
         scratch=[
             pltpu.VMEM((2, rows, owned), BF16),
             pltpu.VMEM((len(cells), ycount, owned), F32),
-            pltpu.SemaphoreType.DMA((len(cells),)),
+            pltpu.SemaphoreType.DMA((len(runs),)),
         ],
         specs=[SPEC] * 6 + [FROM_HBM], out_specs=[ANYWHERE], alias={6: 0},
     )[0]

time: 43.3 us -> 43.3 us (level)
  transfers between devices with their start and end apart: 16 -> 16, of which waited for: 10 -> 9; matrix products, arithmetic and copies ran while one was open for 0% -> 0% of each run, Pallas kernels for 21% -> 21%
where the time goes in v9:
time: 43.3 us; the launch traced here: 43.1 us
  starting transfers between devices  16.6 us (38%)
  waiting for transfers between devices  14.4 us (33%)
  Pallas kernels  11.3 us (26%)
  between operations  0.77 us (2%)
    pallas_call x11, Pallas kernels, call(): pl.pallas_call(body, out_shape=outs, in_specs=specs, out_specs=out_specs...  11.3 us
    ppermute x2, waiting for transfers between devices, from_below(): lax.ppermute(tail, 'gx', [(i, (i + 1) % gcount) for i in range(gcount)])  6.68 us
    ppermute x4, starting transfers between devices, to_far(): return lax.ppermute(v, 'trait', [(i, i ^ 2) for i in range(traits)])  6.57 us
    ppermute x2, starting transfers between devices, from_above(): lax.ppermute(head, 'gx', [((i + 1) % gcount, i) for i in range(gcount)])  6.03 us
    ppermute x4, waiting for transfers between devices, to_far(): return lax.ppermute(v, 'trait', [(i, i ^ 2) for i in range(traits)])  4.58 us
    ppermute x2, starting transfers between devices, from_below(): lax.ppermute(tail, 'gx', [(i, (i + 1) % gcount) for i in range(gcount)])  3.63 us
    ppermute x8, waiting for transfers between devices, to_sibling(): return lax.ppermute(v, 'trait', [(i, i ^ 1) for i in range(traits)])  2.02 us
    ppermute x2, waiting for transfers between devices, from_above(): lax.ppermute(head, 'gx', [((i + 1) % gcount, i) for i in range(gcount)])  1.13 us
  transfers between devices with their start and end apart: 16, of which 9 were waited for; matrix products, arithmetic and copies ran while one was open for 0% of the time, Pallas kernels for 21%

profile of v9, /device:TPU:0, one launch (start us, length us, event | category | flops | bytes accessed | tf_op | source)
XLA Modules:
  0.0 43.1 jit_solution(6242609251992309068)
XLA Ops:
  0.6 1.3 %load_chunk.2 = (f32[5,128,256]{2,1,0:T(8,128)S(1)}, f32[5,128,256]{2,1,0:T(8,128)S(1)}, bf16[2,640,256]{2,1,0:T(8,128)(2,1)S(1)}, bf16[2,128,256]{2,1,0:T(8,128)(2,1)S(1)}, bf16[2,128,256]{2,1,0:T(8,128)(2,1)S(1)}) custom-call(f32[8,128,256]{2,1,0:T(8,128)} %refs_0_.2, f32[8,128,256]{2,1,0:T(8,128)} %refs_1_.3), custom_call_target="tpu_custom_call" | custom-call | tf_op jit(solution)/shard_map/load_chunk/pallas_call | solution.py:37
  2.0 0.0 copy-start.3
  2.0 3.0 %collective-permute-start.1 = (bf16[2,640,256]{2,1,0:T(8,128)(2,1)S(1)}, bf16[2,640,256]{2,1,0:T(8,128)(2,1)S(1)}, u32[]{:S(2)}, u32[]{:S(2)}) collective-permute-start(bf16[2,640,256]{2,1,0:T(8,128)(2,1)S(1)} %get-tuple-element.42.refs_0_), channel_id=1, source_target_pairs={{0,2},{1,3},{2,0},{3,1},{4,6},{5,7},{6,4},{7,5},{8,10},{9,11},{10,... | collective-permute-start | bytes 1966088 | tf_op jit(solution)/shard_map/ppermute | solution.py:356
  5.0 1.1 %load_chunk.3 = (f32[3,128,256]{2,1,0:T(8,128)S(1)}, f32[3,128,256]{2,1,0:T(8,128)S(1)}, bf16[2,384,256]{2,1,0:T(8,128)(2,1)S(1)}) custom-call(f32[8,128,256]{2,1,0:T(8,128)} %refs_0_.2, f32[8,128,256]{2,1,0:T(8,128)} %refs_1_.3), custom_call_target="tpu_custom_call" | custom-call | tf_op jit(solution)/shard_map/load_chunk/pallas_call | solution.py:37
  6.2 0.0 copy-start
  6.2 0.1 collective-permute-start
  6.3 1.5 %collective-permute-start.2 = (bf16[2,128,256]{2,1,0:T(8,128)(2,1)S(1)}, bf16[2,128,256]{2,1,0:T(8,128)(2,1)S(1)}, u32[]{:S(2)}, u32[]{:S(2)}) collective-permute-start(bf16[2,128,256]{2,1,0:T(8,128)(2,1)S(1)} %get-tuple-element.49), channel_id=1, source_target_pairs={{0,4},{4,8},{8,12},{12,16},{16,20},{20,24},{24,28},{28,0},{1,5},{5... | collective-permute-start | bytes 393224 | tf_op jit(solution)/shard_map/ppermute | solution.py:359
  7.8 3.2 %collective-permute-start.3 = (bf16[2,128,256]{2,1,0:T(8,128)(2,1)S(1)}, bf16[2,128,256]{2,1,0:T(8,128)(2,1)S(1)}, u32[]{:S(2)}, u32[]{:S(2)}) collective-permute-start(bf16[2,128,256]{2,1,0:T(8,128)(2,1)S(1)} %get-tuple-element.50), channel_id=1, source_target_pairs={{4,0},{8,4},{12,8},{16,12},{20,16},{24,20},{28,24},{0,28},{5,1},{9... | collective-permute-start | bytes 393224 | tf_op jit(solution)/shard_map/ppermute | solution.py:362
  11.0 0.4 collective-permute-start.6
  11.4 3.6 %collective-permute-done.2.refs_4_ = bf16[2,128,256]{2,1,0:T(8,128)(2,1)S(1)} collective-permute-done((bf16[2,128,256]{2,1,0:T(8,128)(2,1)S(1)}, bf16[2,128,256]{2,1,0:T(8,128)(2,1)S(1)}, u32[]{:S(2)}, u32[]{:S(2)}) %collective-permute-start.2) | collective-permute-done | bytes 131104 | tf_op jit(solution)/shard_map/ppermute | solution.py:359
  15.0 0.0 collective-permute-start.5
  15.0 1.1 %collective-permute-done.3.refs_5_ = bf16[2,128,256]{2,1,0:T(8,128)(2,1)S(1)} collective-permute-done((bf16[2,128,256]{2,1,0:T(8,128)(2,1)S(1)}, bf16[2,128,256]{2,1,0:T(8,128)(2,1)S(1)}, u32[]{:S(2)}, u32[]{:S(2)}) %collective-permute-start.3) | collective-permute-done | bytes 131104 | tf_op jit(solution)/shard_map/ppermute | solution.py:362
  16.2 0.0 copy-done.3
  16.2 0.9 %before_first.1 = (f32[2,5,128,256]{3,2,1,0:T(8,128)S(1)}, f32[2,3,128,256]{3,2,1,0:T(8,128)S(1)}) custom-call(f32[5,128,256]{2,1,0:T(8,128)S(1)} %get-tuple-element.43.refs_0_.one_ref, f32[3,128,256]{2,1,0:T(8,128)S(1)} %get-tuple-element.44.refs_1_.one_ref, f32[5,128,256]{2,1,0:T(8,128)S(1)} %get-tuple-element.45.refs_2_.two_ref, ...), custom_call_target="tpu_custom_call" | custom-call | tf_op jit(solution)/shard_map/before_first/pallas_call | solution.py:37
  17.1 3.5 %collective-permute-done.1.refs_2_ = bf16[2,640,256]{2,1,0:T(8,128)(2,1)S(1)} collective-permute-done((bf16[2,640,256]{2,1,0:T(8,128)(2,1)S(1)}, bf16[2,640,256]{2,1,0:T(8,128)(2,1)S(1)}, u32[]{:S(2)}, u32[]{:S(2)}) %collective-permute-start.1) | collective-permute-done | bytes 655392 | tf_op jit(solution)/shard_map/ppermute | solution.py:356
  20.6 0.0 collective-permute-start.4
  20.6 0.0 collective-permute-done.refs_1_
  20.6 0.0 copy-done
  20.6 1.2 %early_part.2.part_ref = f32[2,1280,256]{2,1,0:T(8,128)S(1)} custom-call(bf16[2,640,256]{2,1,0:T(8,128)(2,1)S(1)} %get-tuple-element.42.refs_0_, bf16[2,640,256]{2,1,0:T(8,128)(2,1)S(1)} %collective-permute-done.refs_1_, bf16[2,640,256]{2,1,0:T(8,128)(2,1)S(1)} %collective-permute-done.1.refs_2_, bf16[2,1024,256]{2,1,0:T(8,128)(2,1)S(1)} %copy-done), custom_call_target="tpu_custom_call" | custom-call | flops 20000000000 | tf_op jit(solution)/shard_map/early_part/pallas_call | solution.py:37
  21.8 0.9 %collective-permute-done.4.last_ref = bf16[2,640,256]{2,1,0:T(8,128)(2,1)S(1)} collective-permute-done((bf16[2,640,256]{2,1,0:T(8,128)(2,1)S(1)}, bf16[2,640,256]{2,1,0:T(8,128)(2,1)S(1)}, u32[]{:S(2)}, u32[]{:S(2)}) %collective-permute-start.4) | collective-permute-done | bytes 655392 | tf_op jit(solution)/shard_map/ppermute | solution.py:353
  22.7 0.0 copy-done.2
  22.7 1.0 %first_node.2 = (f32[5,128,256]{2,1,0:T(8,128)S(1)}, bf16[1,640,256]{2,1,0:T(8,128)(2,1)S(1)}, f32[5,128,256]{2,1,0:T(8,128)S(1)}, bf16[1,128,256]{2,1,0:T(8,128)(2,1)S(1)}, bf16[1,128,256]{2,1,0:T(8,128)(2,1)S(1)}) custom-call(f32[2,1280,256]{2,1,0:T(8,128)S(1)} %early_part.2.part_ref, bf16[2,640,256]{2,1,0:T(8,128)(2,1)S(1)} %collective-permute-done.4.last_ref, ...), custom_call_target="tpu_custom_call" | custom-call | tf_op jit(solution)/shard_map/first_node/pallas_call | solution.py:37
  23.7 2.1 %collective-permute-start.7 = (bf16[1,128,256]{2,1,0:T(8,128)(2,1)S(1)}, bf16[1,128,256]{2,1,0:T(8,128)(2,1)S(1)}, u32[]{:S(2)}, u32[]{:S(2)}) collective-permute-start(bf16[1,128,256]{2,1,0:T(8,128)(2,1)S(1)} %get-tuple-element.56), channel_id=1, source_target_pairs={{0,4},{4,8},{8,12},{12,16},{16,20},{20,24},{24,28},{28,0},{1,5},{5... | collective-permute-start | bytes 196616 | tf_op jit(solution)/shard_map/ppermute | solution.py:359
  25.8 1.5 %collective-permute-start.10 = (bf16[1,640,256]{2,1,0:T(8,128)(2,1)S(1)}, bf16[1,640,256]{2,1,0:T(8,128)(2,1)S(1)}, u32[]{:S(2)}, u32[]{:S(2)}) collective-permute-start(bf16[1,640,256]{2,1,0:T(8,128)(2,1)S(1)} %get-tuple-element.55.refs_4_), channel_id=1, source_target_pairs={{0,2},{1,3},{2,0},{3,1},{4,6},{5,7},{6,4},{7,5},{8,10},{9,11},{10,... | collective-permute-start | bytes 983048 | tf_op jit(solution)/shard_map/ppermute | solution.py:356
  27.3 0.0 collective-permute-start.9
  27.3 0.8 %collective-permute-done.6.refs_2_ = bf16[2,384,256]{2,1,0:T(8,128)(2,1)S(1)} collective-permute-done((bf16[2,384,256]{2,1,0:T(8,128)(2,1)S(1)}, bf16[2,384,256]{2,1,0:T(8,128)(2,1)S(1)}, u32[]{:S(2)}, u32[]{:S(2)}) %collective-permute-start.6) | collective-permute-done | bytes 393248 | tf_op jit(solution)/shard_map/ppermute | solution.py:356
  28.2 3.1 %collective-permute-done.7.lo_ref = bf16[1,128,256]{2,1,0:T(8,128)(2,1)S(1)} collective-permute-done((bf16[1,128,256]{2,1,0:T(8,128)(2,1)S(1)}, bf16[1,128,256]{2,1,0:T(8,128)(2,1)S(1)}, u32[]{:S(2)}, u32[]{:S(2)}) %collective-permute-start.7) | collective-permute-done | bytes 65568 | tf_op jit(solution)/shard_map/ppermute | solution.py:359
  31.2 0.0 collective-permute-start.8
  31.2 0.0 collective-permute-done.5.refs_1_
  31.2 1.0 %early_part.3 = (f32[2,768,256]{2,1,0:T(8,128)S(1)}, f32[8,128,256]{2,1,0:T(8,128)}) custom-call(bf16[2,384,256]{2,1,0:T(8,128)(2,1)S(1)} %get-tuple-element.41.refs_0_, bf16[2,384,256]{2,1,0:T(8,128)(2,1)S(1)} %collective-permute-done.5.refs_1_, bf16[2,384,256]{2,1,0:T(8,128)(2,1)S(1)} %collective-permute-done.6.refs_2_, bf16[2,1024,256]{2,1,0:T(8,128)(2,1)S(1)} %copy-done, ...), custom_call_target="tpu_custom_call" | custom-call | flops 20000000000 | tf_op jit(solution)/shard_map/early_part/pallas_call | solution.py:37
  32.3 0.7 %collective-permute-done.8.last_ref = bf16[2,384,256]{2,1,0:T(8,128)(2,1)S(1)} collective-permute-done((bf16[2,384,256]{2,1,0:T(8,128)(2,1)S(1)}, bf16[2,384,256]{2,1,0:T(8,128)(2,1)S(1)}, u32[]{:S(2)}, u32[]{:S(2)}) %collective-permute-start.8) | collective-permute-done | bytes 393248 | tf_op jit(solution)/shard_map/ppermute | solution.py:353
  32.9 0.7 %first_node.3 = (f32[3,128,256]{2,1,0:T(8,128)S(1)}, bf16[1,384,256]{2,1,0:T(8,128)(2,1)S(1)}, f32[3,128,256]{2,1,0:T(8,128)S(1)}) custom-call(f32[2,768,256]{2,1,0:T(8,128)S(1)} %get-tuple-element.58.part_ref, bf16[2,384,256]{2,1,0:T(8,128)(2,1)S(1)} %collective-permute-done.8.last_ref, f32[2,3,128,256]{3,2,1,0:T(8,128)S(1)} %get-tuple-element.59.base_ref, ...), custom_call_target="tpu_custom_call" | custom-call | tf_op jit(solution)/shard_map/first_node/pallas_call | solution.py:37
  33.7 1.6 %collective-permute-start.14 = (bf16[1,384,256]{2,1,0:T(8,128)(2,1)S(1)}, bf16[1,384,256]{2,1,0:T(8,128)(2,1)S(1)}, u32[]{:S(2)}, u32[]{:S(2)}) collective-permute-start(bf16[1,384,256]{2,1,0:T(8,128)(2,1)S(1)} %get-tuple-element.66.refs_0_), channel_id=1, source_target_pairs={{0,2},{1,3},{2,0},{3,1},{4,6},{5,7},{6,4},{7,5},{8,10},{9,11},{10,... | collective-permute-start | bytes 589832 | tf_op jit(solution)/shard_map/ppermute | solution.py:356
  35.3 0.0 collective-permute-start.13
  35.3 2.8 %collective-permute-start.12 = (bf16[1,128,256]{2,1,0:T(8,128)(2,1)S(1)}, bf16[1,128,256]{2,1,0:T(8,128)(2,1)S(1)}, u32[]{:S(2)}, u32[]{:S(2)}) collective-permute-start(bf16[1,128,256]{2,1,0:T(8,128)(2,1)S(1)} %get-tuple-element.71), channel_id=1, source_target_pairs={{4,0},{8,4},{12,8},{16,12},{20,16},{24,20},{28,24},{0,28},{5,1},{9... | collective-permute-start | bytes 196616 | tf_op jit(solution)/shard_map/ppermute | solution.py:362
  38.1 0.0 collective-permute-done.10.far_ref
  38.1 0.2 collective-permute-start.11
  38.3 0.9 %before_second.1 = (f32[8,128,256]{2,1,0:T(8,128)}, f32[2,640,256]{2,1,0:T(8,128)S(1)}, f32[5,128,256]{2,1,0:T(8,128)S(1)}, f32[3,128,256]{2,1,0:T(8,128)S(1)}) custom-call(f32[5,128,256]{2,1,0:T(8,128)S(1)} %get-tuple-element.54.refs_4_.refs_0_.new_ref, f32[3,128,256]{2,1,0:T(8,128)S(1)} %get-tuple-element.60.refs_1_.new_ref, ...), custom_call_target="tpu_custom_call", output_to_operand_aliasing={{0}: (8, {})} | custom-call | flops 20000000000 | tf_op jit(solution)/shard_map/before_second/pallas_call | solution.py:37
  39.3 0.0 collective-permute-done.9.sib_ref
  39.3 0.4 %collective-permute-done.11.farsib_ref = bf16[1,640,256]{2,1,0:T(8,128)(2,1)S(1)} collective-permute-done((bf16[1,640,256]{2,1,0:T(8,128)(2,1)S(1)}, bf16[1,640,256]{2,1,0:T(8,128)(2,1)S(1)}, u32[]{:S(2)}, u32[]{:S(2)}) %collective-permute-start.11) | collective-permute-done | bytes 327712 | tf_op jit(solution)/shard_map/ppermute | solution.py:353
  39.7 0.7 %whole_sums.1.sums_ref = bf16[2,640,256]{2,1,0:T(8,128)(2,1)S(1)} custom-call(f32[2,640,256]{2,1,0:T(8,128)S(1)} %get-tuple-element.65.part_ref, bf16[1,640,256]{2,1,0:T(8,128)(2,1)S(1)} %collective-permute-done.9.sib_ref, bf16[1,640,256]{2,1,0:T(8,128)(2,1)S(1)} %collective-permute-done.10.far_ref, ...), custom_call_target="tpu_custom_call" | custom-call | tf_op jit(solution)/shard_map/whole_sums/pallas_call | solution.py:37
  40.4 0.0 collective-permute-done.12.hi_ref
  40.4 0.3 collective-permute-done.14.refs_2_
  40.7 0.1 collective-permute-start.15
  40.7 0.0 collective-permute-done.13.refs_1_
  40.7 1.4 %second_first.1 = (f32[8,128,256]{2,1,0:T(8,128)}, f32[2,384,256]{2,1,0:T(8,128)S(1)}) custom-call(bf16[2,640,256]{2,1,0:T(8,128)(2,1)S(1)} %whole_sums.1.sums_ref, f32[5,128,256]{2,1,0:T(8,128)S(1)} %get-tuple-element.68.base_ref, f32[5,128,256]{2,1,0:T(8,128)S(1)} %get-tuple-element.54.refs_4_.refs_0_.new_ref, f32[1,256]{1,0:T(1,128)S(1)} %bitcast.5, ...), custom_call_target="tpu_custom_call" | custom-call | tf_op jit(solution)/shard_map/second_first/pallas_call | solution.py:37
  42.1 0.0 collective-permute-done.15.last_ref
  42.1 1.0 %second_last.1 = f32[8,128,256]{2,1,0:T(8,128)} custom-call(f32[2,384,256]{2,1,0:T(8,128)S(1)} %get-tuple-element.73.part_ref, bf16[1,384,256]{2,1,0:T(8,128)(2,1)S(1)} %collective-permute-done.15.last_ref, f32[3,128,256]{2,1,0:T(8,128)S(1)} %get-tuple-element.74.base_ref, ...), custom_call_target="tpu_custom_call", output_to_operand_aliasing={{}: (6, {})} | custom-call | tf_op jit(solution)/shard_map/second_last/pallas_call | solution.py:37
  (3 shorter events, 0.0 us)
Async XLA Ops:
  2.0 14.2 %copy-start.3 = (f32[256]{0:T(256)S(1)}, f32[256]{0:T(256)}, u32[]{:S(2)}) copy-start(f32[256]{0:T(256)} %param.10) | copy-start | bytes 3076
  2.0 18.6 %collective-permute-start.1 = (bf16[2,640,256]{2,1,0:T(8,128)(2,1)S(1)}, bf16[2,640,256]{2,1,0:T(8,128)(2,1)S(1)}, u32[]{:S(2)}, u32[]{:S(2)}) collective-permute-start(bf16[2,640,256]{2,1,0:T(8,128)(2,1)S(1)} %get-tuple-element.42.refs_0_), channel_id=1, source_target_pairs={{0,2},{1,3},{2,0},{3,1},{4,6},{5,7},{6,4},{7,5},{8,10},{9,11},{10,... | collective-permute-start | bytes 1966088 | tf_op jit(solution)/shard_map/ppermute | solution.py:356
  6.2 14.4 %copy-start = (bf16[2,1024,256]{2,1,0:T(8,128)(2,1)S(1)}, bf16[2,1024,256]{2,1,0:T(8,128)(2,1)}, u32[]{:S(2)}) copy-start(bf16[2,1024,256]{2,1,0:T(8,128)(2,1)} %k_ref.4) | copy-start | bytes 3145732
  6.2 14.4 %collective-permute-start = (bf16[2,640,256]{2,1,0:T(8,128)(2,1)S(1)}, bf16[2,640,256]{2,1,0:T(8,128)(2,1)S(1)}, u32[]{:S(2)}, u32[]{:S(2)}) collective-permute-start(bf16[2,640,256]{2,1,0:T(8,128)(2,1)S(1)} %get-tuple-element.42.refs_0_), channel_id=1, source_target_pairs={{0,1},{1,0},{2,3},{3,2},{4,5},{5,4},{6,7},{7,6},{8,9},{9,8},{10,11... | collective-permute-start | bytes 1966088 | tf_op jit(solution)/shard_map/ppermute | solution.py:353
  6.3 8.8 %collective-permute-start.2 = (bf16[2,128,256]{2,1,0:T(8,128)(2,1)S(1)}, bf16[2,128,256]{2,1,0:T(8,128)(2,1)S(1)}, u32[]{:S(2)}, u32[]{:S(2)}) collective-permute-start(bf16[2,128,256]{2,1,0:T(8,128)(2,1)S(1)} %get-tuple-element.49), channel_id=1, source_target_pairs={{0,4},{4,8},{8,12},{12,16},{16,20},{20,24},{24,28},{28,0},{1,5},{5... | collective-permute-start | bytes 393224 | tf_op jit(solution)/shard_map/ppermute | solution.py:359
  7.8 8.4 %collective-permute-start.3 = (bf16[2,128,256]{2,1,0:T(8,128)(2,1)S(1)}, bf16[2,128,256]{2,1,0:T(8,128)(2,1)S(1)}, u32[]{:S(2)}, u32[]{:S(2)}) collective-permute-start(bf16[2,128,256]{2,1,0:T(8,128)(2,1)S(1)} %get-tuple-element.50), channel_id=1, source_target_pairs={{4,0},{8,4},{12,8},{16,12},{20,16},{24,20},{28,24},{0,28},{5,1},{9... | collective-permute-start | bytes 393224 | tf_op jit(solution)/shard_map/ppermute | solution.py:362
  11.0 17.1 %collective-permute-start.6 = (bf16[2,384,256]{2,1,0:T(8,128)(2,1)S(1)}, bf16[2,384,256]{2,1,0:T(8,128)(2,1)S(1)}, u32[]{:S(2)}, u32[]{:S(2)}) collective-permute-start(bf16[2,384,256]{2,1,0:T(8,128)(2,1)S(1)} %get-tuple-element.41.refs_0_), channel_id=1, source_target_pairs={{0,2},{1,3},{2,0},{3,1},{4,6},{5,7},{6,4},{7,5},{8,10},{9,11},{10,... | collective-permute-start | bytes 1179656 | tf_op jit(solution)/shard_map/ppermute | solution.py:356
  15.0 16.2 %collective-permute-start.5 = (bf16[2,384,256]{2,1,0:T(8,128)(2,1)S(1)}, bf16[2,384,256]{2,1,0:T(8,128)(2,1)S(1)}, u32[]{:S(2)}, u32[]{:S(2)}) collective-permute-start(bf16[2,384,256]{2,1,0:T(8,128)(2,1)S(1)} %get-tuple-element.41.refs_0_), channel_id=1, source_target_pairs={{0,1},{1,0},{2,3},{3,2},{4,5},{5,4},{6,7},{7,6},{8,9},{9,8},{10,11... | collective-permute-start | bytes 1179656 | tf_op jit(solution)/shard_map/ppermute | solution.py:353
  20.6 2.1 %copy-start.1 = (f32[8,128,256]{2,1,0:T(8,128)S(1)}, f32[8,128,256]{2,1,0:T(8,128)}, u32[]{:S(2)}) copy-start(f32[8,128,256]{2,1,0:T(8,128)} %init_ref.3) | copy-start | bytes 3145732
  20.6 2.1 %copy-start.2 = (f32[256]{0:T(256)S(1)}, f32[256]{0:T(256)}, u32[]{:S(2)}) copy-start(f32[256]{0:T(256)} %param.11) | copy-start | bytes 3076
  20.6 2.1 %collective-permute-start.4 = (bf16[2,640,256]{2,1,0:T(8,128)(2,1)S(1)}, bf16[2,640,256]{2,1,0:T(8,128)(2,1)S(1)}, u32[]{:S(2)}, u32[]{:S(2)}) collective-permute-start(bf16[2,640,256]{2,1,0:T(8,128)(2,1)S(1)} %collective-permute-done.1.refs_2_), channel_id=1, source_target_pairs={{0,1},{1,0},{2,3},{3,2},{4,5},{5,4},{6,7},{7,6},{8,9},{9,8},{10,11... | collective-permute-start | bytes 1966088 | tf_op jit(solution)/shard_map/ppermute | solution.py:353
  23.7 7.5 %collective-permute-start.7 = (bf16[1,128,256]{2,1,0:T(8,128)(2,1)S(1)}, bf16[1,128,256]{2,1,0:T(8,128)(2,1)S(1)}, u32[]{:S(2)}, u32[]{:S(2)}) collective-permute-start(bf16[1,128,256]{2,1,0:T(8,128)(2,1)S(1)} %get-tuple-element.56), channel_id=1, source_target_pairs={{0,4},{4,8},{8,12},{12,16},{16,20},{20,24},{24,28},{28,0},{1,5},{5... | collective-permute-start | bytes 196616 | tf_op jit(solution)/shard_map/ppermute | solution.py:359
  25.8 12.3 %collective-permute-start.10 = (bf16[1,640,256]{2,1,0:T(8,128)(2,1)S(1)}, bf16[1,640,256]{2,1,0:T(8,128)(2,1)S(1)}, u32[]{:S(2)}, u32[]{:S(2)}) collective-permute-start(bf16[1,640,256]{2,1,0:T(8,128)(2,1)S(1)} %get-tuple-element.55.refs_4_), channel_id=1, source_target_pairs={{0,2},{1,3},{2,0},{3,1},{4,6},{5,7},{6,4},{7,5},{8,10},{9,11},{10,... | collective-permute-start | bytes 983048 | tf_op jit(solution)/shard_map/ppermute | solution.py:356
  27.3 12.0 %collective-permute-start.9 = (bf16[1,640,256]{2,1,0:T(8,128)(2,1)S(1)}, bf16[1,640,256]{2,1,0:T(8,128)(2,1)S(1)}, u32[]{:S(2)}, u32[]{:S(2)}) collective-permute-start(bf16[1,640,256]{2,1,0:T(8,128)(2,1)S(1)} %get-tuple-element.55.refs_4_), channel_id=1, source_target_pairs={{0,1},{1,0},{2,3},{3,2},{4,5},{5,4},{6,7},{7,6},{8,9},{9,8},{10,11... | collective-permute-start | bytes 983048 | tf_op jit(solution)/shard_map/ppermute | solution.py:353
  31.2 1.7 %collective-permute-start.8 = (bf16[2,384,256]{2,1,0:T(8,128)(2,1)S(1)}, bf16[2,384,256]{2,1,0:T(8,128)(2,1)S(1)}, u32[]{:S(2)}, u32[]{:S(2)}) collective-permute-start(bf16[2,384,256]{2,1,0:T(8,128)(2,1)S(1)} %collective-permute-done.6.refs_2_), channel_id=1, source_target_pairs={{0,1},{1,0},{2,3},{3,2},{4,5},{5,4},{6,7},{7,6},{8,9},{9,8},{10,11... | collective-permute-start | bytes 1179656 | tf_op jit(solution)/shard_map/ppermute | solution.py:353
  33.7 7.0 %collective-permute-start.14 = (bf16[1,384,256]{2,1,0:T(8,128)(2,1)S(1)}, bf16[1,384,256]{2,1,0:T(8,128)(2,1)S(1)}, u32[]{:S(2)}, u32[]{:S(2)}) collective-permute-start(bf16[1,384,256]{2,1,0:T(8,128)(2,1)S(1)} %get-tuple-element.66.refs_0_), channel_id=1, source_target_pairs={{0,2},{1,3},{2,0},{3,1},{4,6},{5,7},{6,4},{7,5},{8,10},{9,11},{10,... | collective-permute-start | bytes 589832 | tf_op jit(solution)/shard_map/ppermute | solution.py:356
  35.3 5.4 %collective-permute-start.13 = (bf16[1,384,256]{2,1,0:T(8,128)(2,1)S(1)}, bf16[1,384,256]{2,1,0:T(8,128)(2,1)S(1)}, u32[]{:S(2)}, u32[]{:S(2)}) collective-permute-start(bf16[1,384,256]{2,1,0:T(8,128)(2,1)S(1)} %get-tuple-element.66.refs_0_), channel_id=1, source_target_pairs={{0,1},{1,0},{2,3},{3,2},{4,5},{5,4},{6,7},{7,6},{8,9},{9,8},{10,11... | collective-permute-start | bytes 589832 | tf_op jit(solution)/shard_map/ppermute | solution.py:353
  35.3 5.1 %collective-permute-start.12 = (bf16[1,128,256]{2,1,0:T(8,128)(2,1)S(1)}, bf16[1,128,256]{2,1,0:T(8,128)(2,1)S(1)}, u32[]{:S(2)}, u32[]{:S(2)}) collective-permute-start(bf16[1,128,256]{2,1,0:T(8,128)(2,1)S(1)} %get-tuple-element.71), channel_id=1, source_target_pairs={{4,0},{8,4},{12,8},{16,12},{20,16},{24,20},{28,24},{0,28},{5,1},{9... | collective-permute-start | bytes 196616 | tf_op jit(solution)/shard_map/ppermute | solution.py:362
  38.1 1.6 %collective-permute-start.11 = (bf16[1,640,256]{2,1,0:T(8,128)(2,1)S(1)}, bf16[1,640,256]{2,1,0:T(8,128)(2,1)S(1)}, u32[]{:S(2)}, u32[]{:S(2)}) collective-permute-start(bf16[1,640,256]{2,1,0:T(8,128)(2,1)S(1)} %collective-permute-done.10.far_ref), channel_id=1, source_target_pairs={{0,1},{1,0},{2,3},{3,2},{4,5},{5,4},{6,7},{7,6},{8,9},{9,8},{10,11... | collective-permute-start | bytes 983048 | tf_op jit(solution)/shard_map/ppermute | solution.py:353
  40.7 1.4 %collective-permute-start.15 = (bf16[1,384,256]{2,1,0:T(8,128)(2,1)S(1)}, bf16[1,384,256]{2,1,0:T(8,128)(2,1)S(1)}, u32[]{:S(2)}, u32[]{:S(2)}) collective-permute-start(bf16[1,384,256]{2,1,0:T(8,128)(2,1)S(1)} %collective-permute-done.14.refs_2_), channel_id=1, source_target_pairs={{0,1},{1,0},{2,3},{3,2},{4,5},{5,4},{6,7},{7,6},{8,9},{9,8},{10,11... | collective-permute-start | bytes 589832 | tf_op jit(solution)/shard_map/ppermute | solution.py:353

commit v10 on v9

--- a/solution.py
+++ b/solution.py
@@ -274,19 +274,21 @@
     return call(body, "whole_sums", [part, *blocks, kernels], [pltpu.VMEM((2, rows, owned), BF16)])[0]
 
 
-def finish(cells, runs, ycount, sums, base_ref, new_ref, factor, faces, held, out_ref, sems):
+def finish(cells, pieces, ycount, sums, base_ref, new_ref, factor, faces, held, out_ref, sems):
     copies = []
-    for r, (start, place, size) in enumerate(runs):
-        for i in range(start, start + size):
-            at = pl.ds(i * ycount, ycount)
-            e = sums[1, at, :].astype(F32) - new_ref[i] * sums[0, at, :].astype(F32)
-            if cells[i] in faces:
-                e = e + DIFFUSION * faces[cells[i]][0].astype(F32)
-            held[i] = base_ref[i] + factor * e
-        copies.append(
-            pltpu.make_async_copy(held.at[pl.ds(start, size)], out_ref.at[pl.ds(place, size)], sems.at[r])
-        )
-        copies[-1].start()
+    size = ycount // pieces
+    for i, x in enumerate(cells):
+        for p in range(pieces):
+            rows = pl.ds(p * size, size)
+            at = pl.ds(i * ycount + p * size, size)
+            e = sums[1, at, :].astype(F32) - new_ref[i, rows, :] * sums[0, at, :].astype(F32)
+            if x in faces:
+                e = e + DIFFUSION * faces[x][0, rows, :].astype(F32)
+            held[i, rows, :] = base_ref[i, rows, :] + factor * e
+            copies.append(
+                pltpu.make_async_copy(held.at[i, rows], out_ref.at[x, rows], sems.at[i * pieces + p])
+            )
+            copies[-1].start()
     return copies
 
 
@@ -300,7 +302,7 @@
         out_ref, part_ref, held, sems = refs[count:]
         factor = SECOND / (1.0 + SECOND * d_ref[...])
         faces = {0: lo_ref, xcount - 1: hi_ref}
-        copies = finish(cells, runs_of(cells), ycount, sums_ref, base_ref, new_ref, factor, faces, held, out_ref, sems)
+        copies = finish(cells, 1, ycount, sums_ref, base_ref, new_ref, factor, faces, held, out_ref, sems)
         me = lax.axis_index("trait")
         values = [r[...].reshape(rows, owned) for r in block_refs]
         for k in range(2):
@@ -311,7 +313,7 @@
     return call(
         body, "second_first", [sums, base, new, death, lo, hi, kernels, *blocks],
         [jax.ShapeDtypeStruct((xcount, ycount, owned), F32), pltpu.VMEM((2, rows, owned), F32)],
-        scratch=[pltpu.VMEM((len(cells), ycount, owned), F32), pltpu.SemaphoreType.DMA((len(runs_of(cells)),))],
+        scratch=[pltpu.VMEM((len(cells), ycount, owned), F32), pltpu.SemaphoreType.DMA((len(cells),))],
         out_specs=[ANYWHERE, SPEC],
     )
 
@@ -319,14 +321,13 @@
 def second_last(part, last, base, new, death, kernels, begun, cells, xcount):
     _, ycount, owned = new.shape
     rows = len(cells) * ycount
-    runs = runs_of(cells[:-1]) + [[len(cells) - 1, cells[-1], 1]]
 
     def body(part_ref, last_ref, base_ref, new_ref, d_ref, k_ref, begun_ref, out_ref, sums, held, sems):
         me = lax.axis_index("trait")
         for k in range(2):
             sums[k] = (part_ref[k] + blocks_dot([last_ref[...].reshape(rows, owned)], k_ref, k, [me ^ 3])).astype(BF16)
         factor = SECOND / (1.0 + SECOND * d_ref[...])
-        for copy in finish(cells, runs, ycount, sums, base_ref, new_ref, factor, {}, held, out_ref, sems):
+        for copy in finish(cells, 2, ycount, sums, base_ref, new_ref, factor, {}, held, out_ref, sems):
             copy.wait()
 
     return call(
@@ -335,7 +336,7 @@
         scratch=[
             pltpu.VMEM((2, rows, owned), BF16),
             pltpu.VMEM((len(cells), ycount, owned), F32),
-            pltpu.SemaphoreType.DMA((len(runs),)),
+            pltpu.SemaphoreType.DMA((2 * len(cells),)),
         ],
         specs=[SPEC] * 6 + [FROM_HBM], out_specs=[ANYWHERE], alias={6: 0},
     )[0]

time: 43.3 us -> 43.3 us (level)
  transfers between devices with their start and end apart: 16 -> 16, of which waited for: 9 -> 10; matrix products, arithmetic and copies ran while one was open for 0% -> 0% of each run, Pallas kernels for 21% -> 21%
where the time goes in v10:
time: 43.3 us; the launch traced here: 43.1 us
  starting transfers between devices  16.6 us (38%)
  waiting for transfers between devices  14.5 us (33%)
  Pallas kernels  11.2 us (26%)
  between operations  0.77 us (2%)
    pallas_call x11, Pallas kernels, call(): pl.pallas_call(body, out_shape=outs, in_specs=specs, out_specs=out_specs...  11.2 us
    ppermute x2, waiting for transfers between devices, from_below(): lax.ppermute(tail, 'gx', [(i, (i + 1) % gcount) for i in range(gcount)])  6.68 us
    ppermute x4, starting transfers between devices, to_far(): return lax.ppermute(v, 'trait', [(i, i ^ 2) for i in range(traits)])  6.57 us
    ppermute x2, starting transfers between devices, from_above(): lax.ppermute(head, 'gx', [((i + 1) % gcount, i) for i in range(gcount)])  6.03 us
    ppermute x4, waiting for transfers between devices, to_far(): return lax.ppermute(v, 'trait', [(i, i ^ 2) for i in range(traits)])  4.58 us
    ppermute x2, starting transfers between devices, from_below(): lax.ppermute(tail, 'gx', [(i, (i + 1) % gcount) for i in range(gcount)])  3.63 us
    ppermute x8, waiting for transfers between devices, to_sibling(): return lax.ppermute(v, 'trait', [(i, i ^ 1) for i in range(traits)])  2.08 us
    ppermute x2, waiting for transfers between devices, from_above(): lax.ppermute(head, 'gx', [((i + 1) % gcount, i) for i in range(gcount)])  1.13 us
  transfers between devices with their start and end apart: 16, of which 10 were waited for; matrix products, arithmetic and copies ran while one was open for 0% of the time, Pallas kernels for 21%

profile of v10, /device:TPU:0, one launch (start us, length us, event | category | flops | bytes accessed | tf_op | source)
XLA Modules:
  0.0 43.1 jit_solution(272997514759290715)
XLA Ops:
  0.6 1.3 %load_chunk.2 = (f32[5,128,256]{2,1,0:T(8,128)S(1)}, f32[5,128,256]{2,1,0:T(8,128)S(1)}, bf16[2,640,256]{2,1,0:T(8,128)(2,1)S(1)}, bf16[2,128,256]{2,1,0:T(8,128)(2,1)S(1)}, bf16[2,128,256]{2,1,0:T(8,128)(2,1)S(1)}) custom-call(f32[8,128,256]{2,1,0:T(8,128)} %refs_0_.2, f32[8,128,256]{2,1,0:T(8,128)} %refs_1_.3), custom_call_target="tpu_custom_call" | custom-call | tf_op jit(solution)/shard_map/load_chunk/pallas_call | solution.py:37
  2.0 0.0 copy-start.3
  2.0 3.0 %collective-permute-start.1 = (bf16[2,640,256]{2,1,0:T(8,128)(2,1)S(1)}, bf16[2,640,256]{2,1,0:T(8,128)(2,1)S(1)}, u32[]{:S(2)}, u32[]{:S(2)}) collective-permute-start(bf16[2,640,256]{2,1,0:T(8,128)(2,1)S(1)} %get-tuple-element.42.refs_0_), channel_id=1, source_target_pairs={{0,2},{1,3},{2,0},{3,1},{4,6},{5,7},{6,4},{7,5},{8,10},{9,11},{10,... | collective-permute-start | bytes 1966088 | tf_op jit(solution)/shard_map/ppermute | solution.py:357
  5.0 1.1 %load_chunk.3 = (f32[3,128,256]{2,1,0:T(8,128)S(1)}, f32[3,128,256]{2,1,0:T(8,128)S(1)}, bf16[2,384,256]{2,1,0:T(8,128)(2,1)S(1)}) custom-call(f32[8,128,256]{2,1,0:T(8,128)} %refs_0_.2, f32[8,128,256]{2,1,0:T(8,128)} %refs_1_.3), custom_call_target="tpu_custom_call" | custom-call | tf_op jit(solution)/shard_map/load_chunk/pallas_call | solution.py:37
  6.2 0.0 copy-start
  6.2 0.1 collective-permute-start
  6.3 1.5 %collective-permute-start.2 = (bf16[2,128,256]{2,1,0:T(8,128)(2,1)S(1)}, bf16[2,128,256]{2,1,0:T(8,128)(2,1)S(1)}, u32[]{:S(2)}, u32[]{:S(2)}) collective-permute-start(bf16[2,128,256]{2,1,0:T(8,128)(2,1)S(1)} %get-tuple-element.49), channel_id=1, source_target_pairs={{0,4},{4,8},{8,12},{12,16},{16,20},{20,24},{24,28},{28,0},{1,5},{5... | collective-permute-start | bytes 393224 | tf_op jit(solution)/shard_map/ppermute | solution.py:360
  7.8 3.2 %collective-permute-start.3 = (bf16[2,128,256]{2,1,0:T(8,128)(2,1)S(1)}, bf16[2,128,256]{2,1,0:T(8,128)(2,1)S(1)}, u32[]{:S(2)}, u32[]{:S(2)}) collective-permute-start(bf16[2,128,256]{2,1,0:T(8,128)(2,1)S(1)} %get-tuple-element.50), channel_id=1, source_target_pairs={{4,0},{8,4},{12,8},{16,12},{20,16},{24,20},{28,24},{0,28},{5,1},{9... | collective-permute-start | bytes 393224 | tf_op jit(solution)/shard_map/ppermute | solution.py:363
  11.0 0.4 collective-permute-start.6
  11.4 3.6 %collective-permute-done.2.refs_4_ = bf16[2,128,256]{2,1,0:T(8,128)(2,1)S(1)} collective-permute-done((bf16[2,128,256]{2,1,0:T(8,128)(2,1)S(1)}, bf16[2,128,256]{2,1,0:T(8,128)(2,1)S(1)}, u32[]{:S(2)}, u32[]{:S(2)}) %collective-permute-start.2) | collective-permute-done | bytes 131104 | tf_op jit(solution)/shard_map/ppermute | solution.py:360
  15.0 0.0 collective-permute-start.5
  15.0 1.1 %collective-permute-done.3.refs_5_ = bf16[2,128,256]{2,1,0:T(8,128)(2,1)S(1)} collective-permute-done((bf16[2,128,256]{2,1,0:T(8,128)(2,1)S(1)}, bf16[2,128,256]{2,1,0:T(8,128)(2,1)S(1)}, u32[]{:S(2)}, u32[]{:S(2)}) %collective-permute-start.3) | collective-permute-done | bytes 131104 | tf_op jit(solution)/shard_map/ppermute | solution.py:363
  16.2 0.0 copy-done.3
  16.2 0.9 %before_first.1 = (f32[2,5,128,256]{3,2,1,0:T(8,128)S(1)}, f32[2,3,128,256]{3,2,1,0:T(8,128)S(1)}) custom-call(f32[5,128,256]{2,1,0:T(8,128)S(1)} %get-tuple-element.43.refs_0_.one_ref, f32[3,128,256]{2,1,0:T(8,128)S(1)} %get-tuple-element.44.refs_1_.one_ref, f32[5,128,256]{2,1,0:T(8,128)S(1)} %get-tuple-element.45.refs_2_.two_ref, ...), custom_call_target="tpu_custom_call" | custom-call | tf_op jit(solution)/shard_map/before_first/pallas_call | solution.py:37
  17.1 3.5 %collective-permute-done.1.refs_2_ = bf16[2,640,256]{2,1,0:T(8,128)(2,1)S(1)} collective-permute-done((bf16[2,640,256]{2,1,0:T(8,128)(2,1)S(1)}, bf16[2,640,256]{2,1,0:T(8,128)(2,1)S(1)}, u32[]{:S(2)}, u32[]{:S(2)}) %collective-permute-start.1) | collective-permute-done | bytes 655392 | tf_op jit(solution)/shard_map/ppermute | solution.py:357
  20.6 0.0 collective-permute-start.4
  20.6 0.0 collective-permute-done.refs_1_
  20.6 0.0 copy-done
  20.6 1.2 %early_part.2.part_ref = f32[2,1280,256]{2,1,0:T(8,128)S(1)} custom-call(bf16[2,640,256]{2,1,0:T(8,128)(2,1)S(1)} %get-tuple-element.42.refs_0_, bf16[2,640,256]{2,1,0:T(8,128)(2,1)S(1)} %collective-permute-done.refs_1_, bf16[2,640,256]{2,1,0:T(8,128)(2,1)S(1)} %collective-permute-done.1.refs_2_, bf16[2,1024,256]{2,1,0:T(8,128)(2,1)S(1)} %copy-done), custom_call_target="tpu_custom_call" | custom-call | flops 20000000000 | tf_op jit(solution)/shard_map/early_part/pallas_call | solution.py:37
  21.8 0.9 %collective-permute-done.4.last_ref = bf16[2,640,256]{2,1,0:T(8,128)(2,1)S(1)} collective-permute-done((bf16[2,640,256]{2,1,0:T(8,128)(2,1)S(1)}, bf16[2,640,256]{2,1,0:T(8,128)(2,1)S(1)}, u32[]{:S(2)}, u32[]{:S(2)}) %collective-permute-start.4) | collective-permute-done | bytes 655392 | tf_op jit(solution)/shard_map/ppermute | solution.py:354
  22.7 0.0 copy-done.1
  22.7 1.0 %first_node.2 = (f32[5,128,256]{2,1,0:T(8,128)S(1)}, bf16[1,640,256]{2,1,0:T(8,128)(2,1)S(1)}, f32[5,128,256]{2,1,0:T(8,128)S(1)}, bf16[1,128,256]{2,1,0:T(8,128)(2,1)S(1)}, bf16[1,128,256]{2,1,0:T(8,128)(2,1)S(1)}) custom-call(f32[2,1280,256]{2,1,0:T(8,128)S(1)} %early_part.2.part_ref, bf16[2,640,256]{2,1,0:T(8,128)(2,1)S(1)} %collective-permute-done.4.last_ref, ...), custom_call_target="tpu_custom_call" | custom-call | tf_op jit(solution)/shard_map/first_node/pallas_call | solution.py:37
  23.7 2.1 %collective-permute-start.7 = (bf16[1,128,256]{2,1,0:T(8,128)(2,1)S(1)}, bf16[1,128,256]{2,1,0:T(8,128)(2,1)S(1)}, u32[]{:S(2)}, u32[]{:S(2)}) collective-permute-start(bf16[1,128,256]{2,1,0:T(8,128)(2,1)S(1)} %get-tuple-element.56), channel_id=1, source_target_pairs={{0,4},{4,8},{8,12},{12,16},{16,20},{20,24},{24,28},{28,0},{1,5},{5... | collective-permute-start | bytes 196616 | tf_op jit(solution)/shard_map/ppermute | solution.py:360
  25.8 1.5 %collective-permute-start.10 = (bf16[1,640,256]{2,1,0:T(8,128)(2,1)S(1)}, bf16[1,640,256]{2,1,0:T(8,128)(2,1)S(1)}, u32[]{:S(2)}, u32[]{:S(2)}) collective-permute-start(bf16[1,640,256]{2,1,0:T(8,128)(2,1)S(1)} %get-tuple-element.55.refs_4_), channel_id=1, source_target_pairs={{0,2},{1,3},{2,0},{3,1},{4,6},{5,7},{6,4},{7,5},{8,10},{9,11},{10,... | collective-permute-start | bytes 983048 | tf_op jit(solution)/shard_map/ppermute | solution.py:357
  27.3 0.0 collective-permute-start.9
  27.3 0.8 %collective-permute-done.6.refs_2_ = bf16[2,384,256]{2,1,0:T(8,128)(2,1)S(1)} collective-permute-done((bf16[2,384,256]{2,1,0:T(8,128)(2,1)S(1)}, bf16[2,384,256]{2,1,0:T(8,128)(2,1)S(1)}, u32[]{:S(2)}, u32[]{:S(2)}) %collective-permute-start.6) | collective-permute-done | bytes 393248 | tf_op jit(solution)/shard_map/ppermute | solution.py:357
  28.2 3.1 %collective-permute-done.7.lo_ref = bf16[1,128,256]{2,1,0:T(8,128)(2,1)S(1)} collective-permute-done((bf16[1,128,256]{2,1,0:T(8,128)(2,1)S(1)}, bf16[1,128,256]{2,1,0:T(8,128)(2,1)S(1)}, u32[]{:S(2)}, u32[]{:S(2)}) %collective-permute-start.7) | collective-permute-done | bytes 65568 | tf_op jit(solution)/shard_map/ppermute | solution.py:360
  31.2 0.0 collective-permute-start.8
  31.2 0.0 collective-permute-done.5.refs_1_
  31.2 1.0 %early_part.3 = (f32[2,768,256]{2,1,0:T(8,128)S(1)}, f32[8,128,256]{2,1,0:T(8,128)}) custom-call(bf16[2,384,256]{2,1,0:T(8,128)(2,1)S(1)} %get-tuple-element.41.refs_0_, bf16[2,384,256]{2,1,0:T(8,128)(2,1)S(1)} %collective-permute-done.5.refs_1_, bf16[2,384,256]{2,1,0:T(8,128)(2,1)S(1)} %collective-permute-done.6.refs_2_, bf16[2,1024,256]{2,1,0:T(8,128)(2,1)S(1)} %copy-done, ...), custom_call_target="tpu_custom_call" | custom-call | flops 20000000000 | tf_op jit(solution)/shard_map/early_part/pallas_call | solution.py:37
  32.3 0.7 %collective-permute-done.8.last_ref = bf16[2,384,256]{2,1,0:T(8,128)(2,1)S(1)} collective-permute-done((bf16[2,384,256]{2,1,0:T(8,128)(2,1)S(1)}, bf16[2,384,256]{2,1,0:T(8,128)(2,1)S(1)}, u32[]{:S(2)}, u32[]{:S(2)}) %collective-permute-start.8) | collective-permute-done | bytes 393248 | tf_op jit(solution)/shard_map/ppermute | solution.py:354
  32.9 0.7 %first_node.3 = (f32[3,128,256]{2,1,0:T(8,128)S(1)}, bf16[1,384,256]{2,1,0:T(8,128)(2,1)S(1)}, f32[3,128,256]{2,1,0:T(8,128)S(1)}) custom-call(f32[2,768,256]{2,1,0:T(8,128)S(1)} %get-tuple-element.58.part_ref, bf16[2,384,256]{2,1,0:T(8,128)(2,1)S(1)} %collective-permute-done.8.last_ref, f32[2,3,128,256]{3,2,1,0:T(8,128)S(1)} %get-tuple-element.59.base_ref, ...), custom_call_target="tpu_custom_call" | custom-call | tf_op jit(solution)/shard_map/first_node/pallas_call | solution.py:37
  33.7 1.6 %collective-permute-start.14 = (bf16[1,384,256]{2,1,0:T(8,128)(2,1)S(1)}, bf16[1,384,256]{2,1,0:T(8,128)(2,1)S(1)}, u32[]{:S(2)}, u32[]{:S(2)}) collective-permute-start(bf16[1,384,256]{2,1,0:T(8,128)(2,1)S(1)} %get-tuple-element.66.refs_0_), channel_id=1, source_target_pairs={{0,2},{1,3},{2,0},{3,1},{4,6},{5,7},{6,4},{7,5},{8,10},{9,11},{10,... | collective-permute-start | bytes 589832 | tf_op jit(solution)/shard_map/ppermute | solution.py:357
  35.3 0.0 collective-permute-start.13
  35.3 2.8 %collective-permute-start.12 = (bf16[1,128,256]{2,1,0:T(8,128)(2,1)S(1)}, bf16[1,128,256]{2,1,0:T(8,128)(2,1)S(1)}, u32[]{:S(2)}, u32[]{:S(2)}) collective-permute-start(bf16[1,128,256]{2,1,0:T(8,128)(2,1)S(1)} %get-tuple-element.71), channel_id=1, source_target_pairs={{4,0},{8,4},{12,8},{16,12},{20,16},{24,20},{28,24},{0,28},{5,1},{9... | collective-permute-start | bytes 196616 | tf_op jit(solution)/shard_map/ppermute | solution.py:363
  38.1 0.0 collective-permute-done.10.far_ref
  38.1 0.2 collective-permute-start.11
  38.3 0.9 %before_second.1 = (f32[8,128,256]{2,1,0:T(8,128)}, f32[2,640,256]{2,1,0:T(8,128)S(1)}, f32[5,128,256]{2,1,0:T(8,128)S(1)}, f32[3,128,256]{2,1,0:T(8,128)S(1)}) custom-call(f32[5,128,256]{2,1,0:T(8,128)S(1)} %get-tuple-element.54.refs_4_.refs_0_.new_ref, f32[3,128,256]{2,1,0:T(8,128)S(1)} %get-tuple-element.60.refs_1_.new_ref, ...), custom_call_target="tpu_custom_call", output_to_operand_aliasing={{0}: (8, {})} | custom-call | flops 20000000000 | tf_op jit(solution)/shard_map/before_second/pallas_call | solution.py:37
  39.3 0.0 collective-permute-done.9.sib_ref
  39.3 0.4 %collective-permute-done.11.farsib_ref = bf16[1,640,256]{2,1,0:T(8,128)(2,1)S(1)} collective-permute-done((bf16[1,640,256]{2,1,0:T(8,128)(2,1)S(1)}, bf16[1,640,256]{2,1,0:T(8,128)(2,1)S(1)}, u32[]{:S(2)}, u32[]{:S(2)}) %collective-permute-start.11) | collective-permute-done | bytes 327712 | tf_op jit(solution)/shard_map/ppermute | solution.py:354
  39.7 0.7 %whole_sums.1.sums_ref = bf16[2,640,256]{2,1,0:T(8,128)(2,1)S(1)} custom-call(f32[2,640,256]{2,1,0:T(8,128)S(1)} %get-tuple-element.65.part_ref, bf16[1,640,256]{2,1,0:T(8,128)(2,1)S(1)} %collective-permute-done.9.sib_ref, bf16[1,640,256]{2,1,0:T(8,128)(2,1)S(1)} %collective-permute-done.10.far_ref, ...), custom_call_target="tpu_custom_call" | custom-call | tf_op jit(solution)/shard_map/whole_sums/pallas_call | solution.py:37
  40.4 0.0 collective-permute-done.12.hi_ref
  40.4 0.3 collective-permute-done.14.refs_2_
  40.7 0.1 collective-permute-start.15
  40.7 0.0 collective-permute-done.13.refs_1_
  40.7 1.3 %second_first.1 = (f32[8,128,256]{2,1,0:T(8,128)}, f32[2,384,256]{2,1,0:T(8,128)S(1)}) custom-call(bf16[2,640,256]{2,1,0:T(8,128)(2,1)S(1)} %whole_sums.1.sums_ref, f32[5,128,256]{2,1,0:T(8,128)S(1)} %get-tuple-element.68.base_ref, f32[5,128,256]{2,1,0:T(8,128)S(1)} %get-tuple-element.54.refs_4_.refs_0_.new_ref, f32[1,256]{1,0:T(1,128)S(1)} %bitcast.5, ...), custom_call_target="tpu_custom_call" | custom-call | tf_op jit(solution)/shard_map/second_first/pallas_call | solution.py:37
  42.0 0.1 collective-permute-done.15.last_ref
  42.1 1.0 %second_last.1 = f32[8,128,256]{2,1,0:T(8,128)} custom-call(f32[2,384,256]{2,1,0:T(8,128)S(1)} %get-tuple-element.73.part_ref, bf16[1,384,256]{2,1,0:T(8,128)(2,1)S(1)} %collective-permute-done.15.last_ref, f32[3,128,256]{2,1,0:T(8,128)S(1)} %get-tuple-element.74.base_ref, ...), custom_call_target="tpu_custom_call", output_to_operand_aliasing={{}: (6, {})} | custom-call | tf_op jit(solution)/shard_map/second_last/pallas_call | solution.py:37
  (3 shorter events, 0.0 us)
Async XLA Ops:
  2.0 14.2 %copy-start.3 = (f32[256]{0:T(256)S(1)}, f32[256]{0:T(256)}, u32[]{:S(2)}) copy-start(f32[256]{0:T(256)} %param.10) | copy-start | bytes 3076
  2.0 18.6 %collective-permute-start.1 = (bf16[2,640,256]{2,1,0:T(8,128)(2,1)S(1)}, bf16[2,640,256]{2,1,0:T(8,128)(2,1)S(1)}, u32[]{:S(2)}, u32[]{:S(2)}) collective-permute-start(bf16[2,640,256]{2,1,0:T(8,128)(2,1)S(1)} %get-tuple-element.42.refs_0_), channel_id=1, source_target_pairs={{0,2},{1,3},{2,0},{3,1},{4,6},{5,7},{6,4},{7,5},{8,10},{9,11},{10,... | collective-permute-start | bytes 1966088 | tf_op jit(solution)/shard_map/ppermute | solution.py:357
  6.2 14.4 %copy-start = (bf16[2,1024,256]{2,1,0:T(8,128)(2,1)S(1)}, bf16[2,1024,256]{2,1,0:T(8,128)(2,1)}, u32[]{:S(2)}) copy-start(bf16[2,1024,256]{2,1,0:T(8,128)(2,1)} %k_ref.4) | copy-start | bytes 3145732
  6.2 14.4 %collective-permute-start = (bf16[2,640,256]{2,1,0:T(8,128)(2,1)S(1)}, bf16[2,640,256]{2,1,0:T(8,128)(2,1)S(1)}, u32[]{:S(2)}, u32[]{:S(2)}) collective-permute-start(bf16[2,640,256]{2,1,0:T(8,128)(2,1)S(1)} %get-tuple-element.42.refs_0_), channel_id=1, source_target_pairs={{0,1},{1,0},{2,3},{3,2},{4,5},{5,4},{6,7},{7,6},{8,9},{9,8},{10,11... | collective-permute-start | bytes 1966088 | tf_op jit(solution)/shard_map/ppermute | solution.py:354
  6.3 8.8 %collective-permute-start.2 = (bf16[2,128,256]{2,1,0:T(8,128)(2,1)S(1)}, bf16[2,128,256]{2,1,0:T(8,128)(2,1)S(1)}, u32[]{:S(2)}, u32[]{:S(2)}) collective-permute-start(bf16[2,128,256]{2,1,0:T(8,128)(2,1)S(1)} %get-tuple-element.49), channel_id=1, source_target_pairs={{0,4},{4,8},{8,12},{12,16},{16,20},{20,24},{24,28},{28,0},{1,5},{5... | collective-permute-start | bytes 393224 | tf_op jit(solution)/shard_map/ppermute | solution.py:360
  7.8 8.4 %collective-permute-start.3 = (bf16[2,128,256]{2,1,0:T(8,128)(2,1)S(1)}, bf16[2,128,256]{2,1,0:T(8,128)(2,1)S(1)}, u32[]{:S(2)}, u32[]{:S(2)}) collective-permute-start(bf16[2,128,256]{2,1,0:T(8,128)(2,1)S(1)} %get-tuple-element.50), channel_id=1, source_target_pairs={{4,0},{8,4},{12,8},{16,12},{20,16},{24,20},{28,24},{0,28},{5,1},{9... | collective-permute-start | bytes 393224 | tf_op jit(solution)/shard_map/ppermute | solution.py:363
  11.0 17.1 %collective-permute-start.6 = (bf16[2,384,256]{2,1,0:T(8,128)(2,1)S(1)}, bf16[2,384,256]{2,1,0:T(8,128)(2,1)S(1)}, u32[]{:S(2)}, u32[]{:S(2)}) collective-permute-start(bf16[2,384,256]{2,1,0:T(8,128)(2,1)S(1)} %get-tuple-element.41.refs_0_), channel_id=1, source_target_pairs={{0,2},{1,3},{2,0},{3,1},{4,6},{5,7},{6,4},{7,5},{8,10},{9,11},{10,... | collective-permute-start | bytes 1179656 | tf_op jit(solution)/shard_map/ppermute | solution.py:357
  15.0 16.2 %collective-permute-start.5 = (bf16[2,384,256]{2,1,0:T(8,128)(2,1)S(1)}, bf16[2,384,256]{2,1,0:T(8,128)(2,1)S(1)}, u32[]{:S(2)}, u32[]{:S(2)}) collective-permute-start(bf16[2,384,256]{2,1,0:T(8,128)(2,1)S(1)} %get-tuple-element.41.refs_0_), channel_id=1, source_target_pairs={{0,1},{1,0},{2,3},{3,2},{4,5},{5,4},{6,7},{7,6},{8,9},{9,8},{10,11... | collective-permute-start | bytes 1179656 | tf_op jit(solution)/shard_map/ppermute | solution.py:354
  20.6 2.1 %copy-start.1 = (f32[8,128,256]{2,1,0:T(8,128)S(1)}, f32[8,128,256]{2,1,0:T(8,128)}, u32[]{:S(2)}) copy-start(f32[8,128,256]{2,1,0:T(8,128)} %init_ref.3) | copy-start | bytes 3145732
  20.6 2.1 %copy-start.2 = (f32[256]{0:T(256)S(1)}, f32[256]{0:T(256)}, u32[]{:S(2)}) copy-start(f32[256]{0:T(256)} %param.11) | copy-start | bytes 3076
  20.6 2.1 %collective-permute-start.4 = (bf16[2,640,256]{2,1,0:T(8,128)(2,1)S(1)}, bf16[2,640,256]{2,1,0:T(8,128)(2,1)S(1)}, u32[]{:S(2)}, u32[]{:S(2)}) collective-permute-start(bf16[2,640,256]{2,1,0:T(8,128)(2,1)S(1)} %collective-permute-done.1.refs_2_), channel_id=1, source_target_pairs={{0,1},{1,0},{2,3},{3,2},{4,5},{5,4},{6,7},{7,6},{8,9},{9,8},{10,11... | collective-permute-start | bytes 1966088 | tf_op jit(solution)/shard_map/ppermute | solution.py:354
  23.7 7.5 %collective-permute-start.7 = (bf16[1,128,256]{2,1,0:T(8,128)(2,1)S(1)}, bf16[1,128,256]{2,1,0:T(8,128)(2,1)S(1)}, u32[]{:S(2)}, u32[]{:S(2)}) collective-permute-start(bf16[1,128,256]{2,1,0:T(8,128)(2,1)S(1)} %get-tuple-element.56), channel_id=1, source_target_pairs={{0,4},{4,8},{8,12},{12,16},{16,20},{20,24},{24,28},{28,0},{1,5},{5... | collective-permute-start | bytes 196616 | tf_op jit(solution)/shard_map/ppermute | solution.py:360
  25.8 12.3 %collective-permute-start.10 = (bf16[1,640,256]{2,1,0:T(8,128)(2,1)S(1)}, bf16[1,640,256]{2,1,0:T(8,128)(2,1)S(1)}, u32[]{:S(2)}, u32[]{:S(2)}) collective-permute-start(bf16[1,640,256]{2,1,0:T(8,128)(2,1)S(1)} %get-tuple-element.55.refs_4_), channel_id=1, source_target_pairs={{0,2},{1,3},{2,0},{3,1},{4,6},{5,7},{6,4},{7,5},{8,10},{9,11},{10,... | collective-permute-start | bytes 983048 | tf_op jit(solution)/shard_map/ppermute | solution.py:357
  27.3 12.0 %collective-permute-start.9 = (bf16[1,640,256]{2,1,0:T(8,128)(2,1)S(1)}, bf16[1,640,256]{2,1,0:T(8,128)(2,1)S(1)}, u32[]{:S(2)}, u32[]{:S(2)}) collective-permute-start(bf16[1,640,256]{2,1,0:T(8,128)(2,1)S(1)} %get-tuple-element.55.refs_4_), channel_id=1, source_target_pairs={{0,1},{1,0},{2,3},{3,2},{4,5},{5,4},{6,7},{7,6},{8,9},{9,8},{10,11... | collective-permute-start | bytes 983048 | tf_op jit(solution)/shard_map/ppermute | solution.py:354
  31.2 1.7 %collective-permute-start.8 = (bf16[2,384,256]{2,1,0:T(8,128)(2,1)S(1)}, bf16[2,384,256]{2,1,0:T(8,128)(2,1)S(1)}, u32[]{:S(2)}, u32[]{:S(2)}) collective-permute-start(bf16[2,384,256]{2,1,0:T(8,128)(2,1)S(1)} %collective-permute-done.6.refs_2_), channel_id=1, source_target_pairs={{0,1},{1,0},{2,3},{3,2},{4,5},{5,4},{6,7},{7,6},{8,9},{9,8},{10,11... | collective-permute-start | bytes 1179656 | tf_op jit(solution)/shard_map/ppermute | solution.py:354
  33.7 7.0 %collective-permute-start.14 = (bf16[1,384,256]{2,1,0:T(8,128)(2,1)S(1)}, bf16[1,384,256]{2,1,0:T(8,128)(2,1)S(1)}, u32[]{:S(2)}, u32[]{:S(2)}) collective-permute-start(bf16[1,384,256]{2,1,0:T(8,128)(2,1)S(1)} %get-tuple-element.66.refs_0_), channel_id=1, source_target_pairs={{0,2},{1,3},{2,0},{3,1},{4,6},{5,7},{6,4},{7,5},{8,10},{9,11},{10,... | collective-permute-start | bytes 589832 | tf_op jit(solution)/shard_map/ppermute | solution.py:357
  35.3 5.4 %collective-permute-start.13 = (bf16[1,384,256]{2,1,0:T(8,128)(2,1)S(1)}, bf16[1,384,256]{2,1,0:T(8,128)(2,1)S(1)}, u32[]{:S(2)}, u32[]{:S(2)}) collective-permute-start(bf16[1,384,256]{2,1,0:T(8,128)(2,1)S(1)} %get-tuple-element.66.refs_0_), channel_id=1, source_target_pairs={{0,1},{1,0},{2,3},{3,2},{4,5},{5,4},{6,7},{7,6},{8,9},{9,8},{10,11... | collective-permute-start | bytes 589832 | tf_op jit(solution)/shard_map/ppermute | solution.py:354
  35.3 5.1 %collective-permute-start.12 = (bf16[1,128,256]{2,1,0:T(8,128)(2,1)S(1)}, bf16[1,128,256]{2,1,0:T(8,128)(2,1)S(1)}, u32[]{:S(2)}, u32[]{:S(2)}) collective-permute-start(bf16[1,128,256]{2,1,0:T(8,128)(2,1)S(1)} %get-tuple-element.71), channel_id=1, source_target_pairs={{4,0},{8,4},{12,8},{16,12},{20,16},{24,20},{28,24},{0,28},{5,1},{9... | collective-permute-start | bytes 196616 | tf_op jit(solution)/shard_map/ppermute | solution.py:363
  38.1 1.6 %collective-permute-start.11 = (bf16[1,640,256]{2,1,0:T(8,128)(2,1)S(1)}, bf16[1,640,256]{2,1,0:T(8,128)(2,1)S(1)}, u32[]{:S(2)}, u32[]{:S(2)}) collective-permute-start(bf16[1,640,256]{2,1,0:T(8,128)(2,1)S(1)} %collective-permute-done.10.far_ref), channel_id=1, source_target_pairs={{0,1},{1,0},{2,3},{3,2},{4,5},{5,4},{6,7},{7,6},{8,9},{9,8},{10,11... | collective-permute-start | bytes 983048 | tf_op jit(solution)/shard_map/ppermute | solution.py:354
  40.7 1.4 %collective-permute-start.15 = (bf16[1,384,256]{2,1,0:T(8,128)(2,1)S(1)}, bf16[1,384,256]{2,1,0:T(8,128)(2,1)S(1)}, u32[]{:S(2)}, u32[]{:S(2)}) collective-permute-start(bf16[1,384,256]{2,1,0:T(8,128)(2,1)S(1)} %collective-permute-done.14.refs_2_), channel_id=1, source_target_pairs={{0,1},{1,0},{2,3},{3,2},{4,5},{5,4},{6,7},{7,6},{8,9},{9,8},{10,11... | collective-permute-start | bytes 589832 | tf_op jit(solution)/shard_map/ppermute | solution.py:354

commit v11 on v10

--- a/solution.py
+++ b/solution.py
@@ -381,9 +381,9 @@
     nsib_a = to_sibling(rounded_a)
 
     new_lo = from_below(new_tail)
-    far_b = after(far_b, rounded_a, new_lo)
+    far_b = after(far_b, rounded_a)
     farsib_b = to_sibling(far_b)
-    part_b, new_one = early_part([own_b, sib_b, far_b], kernels, new_a, chunks[0], xcount)
+    part_b, new_one = early_part([own_b, sib_b, far_b], after(kernels, new_lo), new_a, chunks[0], xcount)
     new_b, rounded_b, rest_b = first_node(
         part_b, farsib_b, base_b, one_b, two_b, initial, kernels, death, chunks[1], False
     )

time: 43.3 us -> 43.2 us (level)
  waiting for transfers between devices: 14.5 us -> 13.5 us
  starting transfers between devices: 16.6 us -> 17.5 us
    ppermute x8, waiting for transfers between devices: 2.08 us -> 1.33 us  [to_sibling(): return lax.ppermute(v, 'trait', [(i, i ^ 1) for i in range(traits)])]
    ppermute x2, starting transfers between devices: 6.03 us -> 6.69 us  [from_above(): lax.ppermute(head, 'gx', [((i + 1) % gcount, i) for i in range(gcount)])]
  transfers between devices with their start and end apart: 16 -> 16, of which waited for: 10 -> 7; matrix products, arithmetic and copies ran while one was open for 0% -> 0% of each run, Pallas kernels for 21% -> 21%
where the time goes in v11:
time: 43.2 us; the launch traced here: 43 us
  starting transfers between devices  17.5 us (41%)
  waiting for transfers between devices  13.5 us (31%)
  Pallas kernels  11.3 us (26%)
  between operations  0.79 us (2%)
    pallas_call x11, Pallas kernels, call(): pl.pallas_call(body, out_shape=outs, in_specs=specs, out_specs=out_specs...  11.3 us
    ppermute x2, starting transfers between devices, from_above(): lax.ppermute(head, 'gx', [((i + 1) % gcount, i) for i in range(gcount)])  6.69 us
    ppermute x2, waiting for transfers between devices, from_below(): lax.ppermute(tail, 'gx', [(i, (i + 1) % gcount) for i in range(gcount)])  6.67 us
    ppermute x4, starting transfers between devices, to_far(): return lax.ppermute(v, 'trait', [(i, i ^ 2) for i in range(traits)])  6.57 us
    ppermute x4, waiting for transfers between devices, to_far(): return lax.ppermute(v, 'trait', [(i, i ^ 2) for i in range(traits)])  4.33 us
    ppermute x2, starting transfers between devices, from_below(): lax.ppermute(tail, 'gx', [(i, (i + 1) % gcount) for i in range(gcount)])  3.63 us
    ppermute x8, waiting for transfers between devices, to_sibling(): return lax.ppermute(v, 'trait', [(i, i ^ 1) for i in range(traits)])  1.33 us
    ppermute x2, waiting for transfers between devices, from_above(): lax.ppermute(head, 'gx', [((i + 1) % gcount, i) for i in range(gcount)])  1.13 us
  transfers between devices with their start and end apart: 16, of which 7 were waited for; matrix products, arithmetic and copies ran while one was open for 0% of the time, Pallas kernels for 21%

profile of v11, /device:TPU:0, one launch (start us, length us, event | category | flops | bytes accessed | tf_op | source)
XLA Modules:
  0.0 43.0 jit_solution(11470740108769436337)
XLA Ops:
  0.6 1.3 %load_chunk.2 = (f32[5,128,256]{2,1,0:T(8,128)S(1)}, f32[5,128,256]{2,1,0:T(8,128)S(1)}, bf16[2,640,256]{2,1,0:T(8,128)(2,1)S(1)}, bf16[2,128,256]{2,1,0:T(8,128)(2,1)S(1)}, bf16[2,128,256]{2,1,0:T(8,128)(2,1)S(1)}) custom-call(f32[8,128,256]{2,1,0:T(8,128)} %refs_0_.2, f32[8,128,256]{2,1,0:T(8,128)} %refs_1_.3), custom_call_target="tpu_custom_call" | custom-call | tf_op jit(solution)/shard_map/load_chunk/pallas_call | solution.py:37
  2.0 0.0 copy-start.3
  2.0 3.0 %collective-permute-start.1 = (bf16[2,640,256]{2,1,0:T(8,128)(2,1)S(1)}, bf16[2,640,256]{2,1,0:T(8,128)(2,1)S(1)}, u32[]{:S(2)}, u32[]{:S(2)}) collective-permute-start(bf16[2,640,256]{2,1,0:T(8,128)(2,1)S(1)} %get-tuple-element.43.refs_0_), channel_id=1, source_target_pairs={{0,2},{1,3},{2,0},{3,1},{4,6},{5,7},{6,4},{7,5},{8,10},{9,11},{10,... | collective-permute-start | bytes 1966088 | tf_op jit(solution)/shard_map/ppermute | solution.py:357
  5.0 1.1 %load_chunk.3 = (f32[3,128,256]{2,1,0:T(8,128)S(1)}, f32[3,128,256]{2,1,0:T(8,128)S(1)}, bf16[2,384,256]{2,1,0:T(8,128)(2,1)S(1)}) custom-call(f32[8,128,256]{2,1,0:T(8,128)} %refs_0_.2, f32[8,128,256]{2,1,0:T(8,128)} %refs_1_.3), custom_call_target="tpu_custom_call" | custom-call | tf_op jit(solution)/shard_map/load_chunk/pallas_call | solution.py:37
  6.2 0.0 copy-start
  6.2 0.1 collective-permute-start
  6.3 1.5 %collective-permute-start.2 = (bf16[2,128,256]{2,1,0:T(8,128)(2,1)S(1)}, bf16[2,128,256]{2,1,0:T(8,128)(2,1)S(1)}, u32[]{:S(2)}, u32[]{:S(2)}) collective-permute-start(bf16[2,128,256]{2,1,0:T(8,128)(2,1)S(1)} %get-tuple-element.50), channel_id=1, source_target_pairs={{0,4},{4,8},{8,12},{12,16},{16,20},{20,24},{24,28},{28,0},{1,5},{5... | collective-permute-start | bytes 393224 | tf_op jit(solution)/shard_map/ppermute | solution.py:360
  7.8 3.2 %collective-permute-start.3 = (bf16[2,128,256]{2,1,0:T(8,128)(2,1)S(1)}, bf16[2,128,256]{2,1,0:T(8,128)(2,1)S(1)}, u32[]{:S(2)}, u32[]{:S(2)}) collective-permute-start(bf16[2,128,256]{2,1,0:T(8,128)(2,1)S(1)} %get-tuple-element.51), channel_id=1, source_target_pairs={{4,0},{8,4},{12,8},{16,12},{20,16},{24,20},{28,24},{0,28},{5,1},{9... | collective-permute-start | bytes 393224 | tf_op jit(solution)/shard_map/ppermute | solution.py:363
  11.0 0.4 collective-permute-start.6
  11.4 3.6 %collective-permute-done.2.refs_4_ = bf16[2,128,256]{2,1,0:T(8,128)(2,1)S(1)} collective-permute-done((bf16[2,128,256]{2,1,0:T(8,128)(2,1)S(1)}, bf16[2,128,256]{2,1,0:T(8,128)(2,1)S(1)}, u32[]{:S(2)}, u32[]{:S(2)}) %collective-permute-start.2) | collective-permute-done | bytes 131104 | tf_op jit(solution)/shard_map/ppermute | solution.py:360
  15.0 0.0 collective-permute-start.5
  15.0 1.1 %collective-permute-done.3.refs_5_ = bf16[2,128,256]{2,1,0:T(8,128)(2,1)S(1)} collective-permute-done((bf16[2,128,256]{2,1,0:T(8,128)(2,1)S(1)}, bf16[2,128,256]{2,1,0:T(8,128)(2,1)S(1)}, u32[]{:S(2)}, u32[]{:S(2)}) %collective-permute-start.3) | collective-permute-done | bytes 131104 | tf_op jit(solution)/shard_map/ppermute | solution.py:363
  16.2 0.0 copy-done.3
  16.2 0.9 %before_first.1 = (f32[2,5,128,256]{3,2,1,0:T(8,128)S(1)}, f32[2,3,128,256]{3,2,1,0:T(8,128)S(1)}) custom-call(f32[5,128,256]{2,1,0:T(8,128)S(1)} %get-tuple-element.44.refs_0_.one_ref, f32[3,128,256]{2,1,0:T(8,128)S(1)} %get-tuple-element.45.refs_1_.one_ref, f32[5,128,256]{2,1,0:T(8,128)S(1)} %get-tuple-element.46.refs_2_.two_ref, ...), custom_call_target="tpu_custom_call" | custom-call | tf_op jit(solution)/shard_map/before_first/pallas_call | solution.py:37
  17.1 3.5 %collective-permute-done.1.refs_2_ = bf16[2,640,256]{2,1,0:T(8,128)(2,1)S(1)} collective-permute-done((bf16[2,640,256]{2,1,0:T(8,128)(2,1)S(1)}, bf16[2,640,256]{2,1,0:T(8,128)(2,1)S(1)}, u32[]{:S(2)}, u32[]{:S(2)}) %collective-permute-start.1) | collective-permute-done | bytes 655392 | tf_op jit(solution)/shard_map/ppermute | solution.py:357
  20.6 0.0 collective-permute-start.4
  20.6 0.0 collective-permute-done.refs_1_
  20.6 0.0 copy-done
  20.6 1.2 %early_part.2.part_ref = f32[2,1280,256]{2,1,0:T(8,128)S(1)} custom-call(bf16[2,640,256]{2,1,0:T(8,128)(2,1)S(1)} %get-tuple-element.43.refs_0_, bf16[2,640,256]{2,1,0:T(8,128)(2,1)S(1)} %collective-permute-done.refs_1_, bf16[2,640,256]{2,1,0:T(8,128)(2,1)S(1)} %collective-permute-done.1.refs_2_, bf16[2,1024,256]{2,1,0:T(8,128)(2,1)S(1)} %copy-done), custom_call_target="tpu_custom_call" | custom-call | flops 20000000000 | tf_op jit(solution)/shard_map/early_part/pallas_call | solution.py:37
  21.8 0.9 %collective-permute-done.4.last_ref = bf16[2,640,256]{2,1,0:T(8,128)(2,1)S(1)} collective-permute-done((bf16[2,640,256]{2,1,0:T(8,128)(2,1)S(1)}, bf16[2,640,256]{2,1,0:T(8,128)(2,1)S(1)}, u32[]{:S(2)}, u32[]{:S(2)}) %collective-permute-start.4) | collective-permute-done | bytes 655392 | tf_op jit(solution)/shard_map/ppermute | solution.py:354
  22.7 0.0 copy-done.1
  22.7 1.0 %first_node.2 = (f32[5,128,256]{2,1,0:T(8,128)S(1)}, bf16[1,640,256]{2,1,0:T(8,128)(2,1)S(1)}, f32[5,128,256]{2,1,0:T(8,128)S(1)}, bf16[1,128,256]{2,1,0:T(8,128)(2,1)S(1)}, bf16[1,128,256]{2,1,0:T(8,128)(2,1)S(1)}) custom-call(f32[2,1280,256]{2,1,0:T(8,128)S(1)} %early_part.2.part_ref, bf16[2,640,256]{2,1,0:T(8,128)(2,1)S(1)} %collective-permute-done.4.last_ref, ...), custom_call_target="tpu_custom_call" | custom-call | tf_op jit(solution)/shard_map/first_node/pallas_call | solution.py:37
  23.7 2.1 %collective-permute-start.7 = (bf16[1,128,256]{2,1,0:T(8,128)(2,1)S(1)}, bf16[1,128,256]{2,1,0:T(8,128)(2,1)S(1)}, u32[]{:S(2)}, u32[]{:S(2)}) collective-permute-start(bf16[1,128,256]{2,1,0:T(8,128)(2,1)S(1)} %get-tuple-element.58), channel_id=1, source_target_pairs={{0,4},{4,8},{8,12},{12,16},{16,20},{20,24},{24,28},{28,0},{1,5},{5... | collective-permute-start | bytes 196616 | tf_op jit(solution)/shard_map/ppermute | solution.py:360
  25.8 1.5 %collective-permute-start.10 = (bf16[1,640,256]{2,1,0:T(8,128)(2,1)S(1)}, bf16[1,640,256]{2,1,0:T(8,128)(2,1)S(1)}, u32[]{:S(2)}, u32[]{:S(2)}) collective-permute-start(bf16[1,640,256]{2,1,0:T(8,128)(2,1)S(1)} %get-tuple-element.56.refs_4_), channel_id=1, source_target_pairs={{0,2},{1,3},{2,0},{3,1},{4,6},{5,7},{6,4},{7,5},{8,10},{9,11},{10,... | collective-permute-start | bytes 983048 | tf_op jit(solution)/shard_map/ppermute | solution.py:357
  27.3 0.0 collective-permute-start.9
  27.3 0.8 %collective-permute-done.6.refs_2_ = bf16[2,384,256]{2,1,0:T(8,128)(2,1)S(1)} collective-permute-done((bf16[2,384,256]{2,1,0:T(8,128)(2,1)S(1)}, bf16[2,384,256]{2,1,0:T(8,128)(2,1)S(1)}, u32[]{:S(2)}, u32[]{:S(2)}) %collective-permute-start.6) | collective-permute-done | bytes 393248 | tf_op jit(solution)/shard_map/ppermute | solution.py:357
  28.2 0.0 collective-permute-start.8
  28.2 3.1 %collective-permute-done.7.lo_ref = bf16[1,128,256]{2,1,0:T(8,128)(2,1)S(1)} collective-permute-done((bf16[1,128,256]{2,1,0:T(8,128)(2,1)S(1)}, bf16[1,128,256]{2,1,0:T(8,128)(2,1)S(1)}, u32[]{:S(2)}, u32[]{:S(2)}) %collective-permute-start.7) | collective-permute-done | bytes 65568 | tf_op jit(solution)/shard_map/ppermute | solution.py:360
  31.2 0.0 collective-permute-done.5.refs_1_
  31.2 1.0 %early_part.3 = (f32[2,768,256]{2,1,0:T(8,128)S(1)}, f32[8,128,256]{2,1,0:T(8,128)}) custom-call(bf16[2,384,256]{2,1,0:T(8,128)(2,1)S(1)} %get-tuple-element.42.refs_0_, bf16[2,384,256]{2,1,0:T(8,128)(2,1)S(1)} %collective-permute-done.5.refs_1_, bf16[2,384,256]{2,1,0:T(8,128)(2,1)S(1)} %collective-permute-done.6.refs_2_, bf16[2,1024,256]{2,1,0:T(8,128)(2,1)S(1)} %copy-done, ...), custom_call_target="tpu_custom_call" | custom-call | flops 20000000000 | tf_op jit(solution)/shard_map/early_part/pallas_call | solution.py:37
  32.3 0.0 collective-permute-done.8.last_ref
  32.3 0.7 %first_node.3 = (f32[3,128,256]{2,1,0:T(8,128)S(1)}, bf16[1,384,256]{2,1,0:T(8,128)(2,1)S(1)}, f32[3,128,256]{2,1,0:T(8,128)S(1)}) custom-call(f32[2,768,256]{2,1,0:T(8,128)S(1)} %get-tuple-element.60.part_ref, bf16[2,384,256]{2,1,0:T(8,128)(2,1)S(1)} %collective-permute-done.8.last_ref, f32[2,3,128,256]{3,2,1,0:T(8,128)S(1)} %get-tuple-element.61.base_ref, ...), custom_call_target="tpu_custom_call" | custom-call | tf_op jit(solution)/shard_map/first_node/pallas_call | solution.py:37
  33.0 1.6 %collective-permute-start.14 = (bf16[1,384,256]{2,1,0:T(8,128)(2,1)S(1)}, bf16[1,384,256]{2,1,0:T(8,128)(2,1)S(1)}, u32[]{:S(2)}, u32[]{:S(2)}) collective-permute-start(bf16[1,384,256]{2,1,0:T(8,128)(2,1)S(1)} %get-tuple-element.68.refs_0_), channel_id=1, source_target_pairs={{0,2},{1,3},{2,0},{3,1},{4,6},{5,7},{6,4},{7,5},{8,10},{9,11},{10,... | collective-permute-start | bytes 589832 | tf_op jit(solution)/shard_map/ppermute | solution.py:357
  34.6 0.0 collective-permute-start.13
  34.6 3.5 %collective-permute-start.12 = (bf16[1,128,256]{2,1,0:T(8,128)(2,1)S(1)}, bf16[1,128,256]{2,1,0:T(8,128)(2,1)S(1)}, u32[]{:S(2)}, u32[]{:S(2)}) collective-permute-start(bf16[1,128,256]{2,1,0:T(8,128)(2,1)S(1)} %get-tuple-element.73), channel_id=1, source_target_pairs={{4,0},{8,4},{12,8},{16,12},{20,16},{24,20},{28,24},{0,28},{5,1},{9... | collective-permute-start | bytes 196616 | tf_op jit(solution)/shard_map/ppermute | solution.py:363
  38.1 0.0 collective-permute-done.10.far_ref
  38.1 0.2 collective-permute-start.11
  38.3 0.9 %before_second.1 = (f32[8,128,256]{2,1,0:T(8,128)}, f32[2,640,256]{2,1,0:T(8,128)S(1)}, f32[5,128,256]{2,1,0:T(8,128)S(1)}, f32[3,128,256]{2,1,0:T(8,128)S(1)}) custom-call(f32[5,128,256]{2,1,0:T(8,128)S(1)} %get-tuple-element.55.refs_4_.refs_0_.new_ref, f32[3,128,256]{2,1,0:T(8,128)S(1)} %get-tuple-element.62.refs_1_.new_ref, ...), custom_call_target="tpu_custom_call", output_to_operand_aliasing={{0}: (8, {})} | custom-call | flops 20000000000 | tf_op jit(solution)/shard_map/before_second/pallas_call | solution.py:37
  39.3 0.0 collective-permute-done.9.sib_ref
  39.3 0.4 %collective-permute-done.11.farsib_ref = bf16[1,640,256]{2,1,0:T(8,128)(2,1)S(1)} collective-permute-done((bf16[1,640,256]{2,1,0:T(8,128)(2,1)S(1)}, bf16[1,640,256]{2,1,0:T(8,128)(2,1)S(1)}, u32[]{:S(2)}, u32[]{:S(2)}) %collective-permute-start.11) | collective-permute-done | bytes 327712 | tf_op jit(solution)/shard_map/ppermute | solution.py:354
  39.7 0.7 %whole_sums.1.sums_ref = bf16[2,640,256]{2,1,0:T(8,128)(2,1)S(1)} custom-call(f32[2,640,256]{2,1,0:T(8,128)S(1)} %get-tuple-element.67.part_ref, bf16[1,640,256]{2,1,0:T(8,128)(2,1)S(1)} %collective-permute-done.9.sib_ref, bf16[1,640,256]{2,1,0:T(8,128)(2,1)S(1)} %collective-permute-done.10.far_ref, ...), custom_call_target="tpu_custom_call" | custom-call | tf_op jit(solution)/shard_map/whole_sums/pallas_call | solution.py:37
  40.4 0.0 collective-permute-done.12.hi_ref
  40.4 0.0 collective-permute-done.14.refs_2_
  40.4 0.3 collective-permute-start.15
  40.7 0.0 collective-permute-done.13.refs_1_
  40.7 1.3 %second_first.1 = (f32[8,128,256]{2,1,0:T(8,128)}, f32[2,384,256]{2,1,0:T(8,128)S(1)}) custom-call(bf16[2,640,256]{2,1,0:T(8,128)(2,1)S(1)} %whole_sums.1.sums_ref, f32[5,128,256]{2,1,0:T(8,128)S(1)} %get-tuple-element.70.base_ref, f32[5,128,256]{2,1,0:T(8,128)S(1)} %get-tuple-element.55.refs_4_.refs_0_.new_ref, f32[1,256]{1,0:T(1,128)S(1)} %bitcast.5, ...), custom_call_target="tpu_custom_call" | custom-call | tf_op jit(solution)/shard_map/second_first/pallas_call | solution.py:37
  42.0 0.0 collective-permute-done.15.last_ref
  42.0 1.0 %second_last.1 = f32[8,128,256]{2,1,0:T(8,128)} custom-call(f32[2,384,256]{2,1,0:T(8,128)S(1)} %get-tuple-element.75.part_ref, bf16[1,384,256]{2,1,0:T(8,128)(2,1)S(1)} %collective-permute-done.15.last_ref, f32[3,128,256]{2,1,0:T(8,128)S(1)} %get-tuple-element.76.base_ref, ...), custom_call_target="tpu_custom_call", output_to_operand_aliasing={{}: (6, {})} | custom-call | tf_op jit(solution)/shard_map/second_last/pallas_call | solution.py:37
  (3 shorter events, 0.0 us)
Async XLA Ops:
  2.0 14.2 %copy-start.3 = (f32[256]{0:T(256)S(1)}, f32[256]{0:T(256)}, u32[]{:S(2)}) copy-start(f32[256]{0:T(256)} %param.10) | copy-start | bytes 3076
  2.0 18.6 %collective-permute-start.1 = (bf16[2,640,256]{2,1,0:T(8,128)(2,1)S(1)}, bf16[2,640,256]{2,1,0:T(8,128)(2,1)S(1)}, u32[]{:S(2)}, u32[]{:S(2)}) collective-permute-start(bf16[2,640,256]{2,1,0:T(8,128)(2,1)S(1)} %get-tuple-element.43.refs_0_), channel_id=1, source_target_pairs={{0,2},{1,3},{2,0},{3,1},{4,6},{5,7},{6,4},{7,5},{8,10},{9,11},{10,... | collective-permute-start | bytes 1966088 | tf_op jit(solution)/shard_map/ppermute | solution.py:357
  6.2 14.4 %copy-start = (bf16[2,1024,256]{2,1,0:T(8,128)(2,1)S(1)}, bf16[2,1024,256]{2,1,0:T(8,128)(2,1)}, u32[]{:S(2)}) copy-start(bf16[2,1024,256]{2,1,0:T(8,128)(2,1)} %k_ref.4) | copy-start | bytes 3145732
  6.2 14.4 %collective-permute-start = (bf16[2,640,256]{2,1,0:T(8,128)(2,1)S(1)}, bf16[2,640,256]{2,1,0:T(8,128)(2,1)S(1)}, u32[]{:S(2)}, u32[]{:S(2)}) collective-permute-start(bf16[2,640,256]{2,1,0:T(8,128)(2,1)S(1)} %get-tuple-element.43.refs_0_), channel_id=1, source_target_pairs={{0,1},{1,0},{2,3},{3,2},{4,5},{5,4},{6,7},{7,6},{8,9},{9,8},{10,11... | collective-permute-start | bytes 1966088 | tf_op jit(solution)/shard_map/ppermute | solution.py:354
  6.3 8.8 %collective-permute-start.2 = (bf16[2,128,256]{2,1,0:T(8,128)(2,1)S(1)}, bf16[2,128,256]{2,1,0:T(8,128)(2,1)S(1)}, u32[]{:S(2)}, u32[]{:S(2)}) collective-permute-start(bf16[2,128,256]{2,1,0:T(8,128)(2,1)S(1)} %get-tuple-element.50), channel_id=1, source_target_pairs={{0,4},{4,8},{8,12},{12,16},{16,20},{20,24},{24,28},{28,0},{1,5},{5... | collective-permute-start | bytes 393224 | tf_op jit(solution)/shard_map/ppermute | solution.py:360
  7.8 8.4 %collective-permute-start.3 = (bf16[2,128,256]{2,1,0:T(8,128)(2,1)S(1)}, bf16[2,128,256]{2,1,0:T(8,128)(2,1)S(1)}, u32[]{:S(2)}, u32[]{:S(2)}) collective-permute-start(bf16[2,128,256]{2,1,0:T(8,128)(2,1)S(1)} %get-tuple-element.51), channel_id=1, source_target_pairs={{4,0},{8,4},{12,8},{16,12},{20,16},{24,20},{28,24},{0,28},{5,1},{9... | collective-permute-start | bytes 393224 | tf_op jit(solution)/shard_map/ppermute | solution.py:363
  11.0 17.1 %collective-permute-start.6 = (bf16[2,384,256]{2,1,0:T(8,128)(2,1)S(1)}, bf16[2,384,256]{2,1,0:T(8,128)(2,1)S(1)}, u32[]{:S(2)}, u32[]{:S(2)}) collective-permute-start(bf16[2,384,256]{2,1,0:T(8,128)(2,1)S(1)} %get-tuple-element.42.refs_0_), channel_id=1, source_target_pairs={{0,2},{1,3},{2,0},{3,1},{4,6},{5,7},{6,4},{7,5},{8,10},{9,11},{10,... | collective-permute-start | bytes 1179656 | tf_op jit(solution)/shard_map/ppermute | solution.py:357
  15.0 16.2 %collective-permute-start.5 = (bf16[2,384,256]{2,1,0:T(8,128)(2,1)S(1)}, bf16[2,384,256]{2,1,0:T(8,128)(2,1)S(1)}, u32[]{:S(2)}, u32[]{:S(2)}) collective-permute-start(bf16[2,384,256]{2,1,0:T(8,128)(2,1)S(1)} %get-tuple-element.42.refs_0_), channel_id=1, source_target_pairs={{0,1},{1,0},{2,3},{3,2},{4,5},{5,4},{6,7},{7,6},{8,9},{9,8},{10,11... | collective-permute-start | bytes 1179656 | tf_op jit(solution)/shard_map/ppermute | solution.py:354
  20.6 2.1 %copy-start.1 = (f32[8,128,256]{2,1,0:T(8,128)S(1)}, f32[8,128,256]{2,1,0:T(8,128)}, u32[]{:S(2)}) copy-start(f32[8,128,256]{2,1,0:T(8,128)} %init_ref.3) | copy-start | bytes 3145732
  20.6 2.1 %copy-start.2 = (f32[256]{0:T(256)S(1)}, f32[256]{0:T(256)}, u32[]{:S(2)}) copy-start(f32[256]{0:T(256)} %param.11) | copy-start | bytes 3076
  20.6 2.1 %collective-permute-start.4 = (bf16[2,640,256]{2,1,0:T(8,128)(2,1)S(1)}, bf16[2,640,256]{2,1,0:T(8,128)(2,1)S(1)}, u32[]{:S(2)}, u32[]{:S(2)}) collective-permute-start(bf16[2,640,256]{2,1,0:T(8,128)(2,1)S(1)} %collective-permute-done.1.refs_2_), channel_id=1, source_target_pairs={{0,1},{1,0},{2,3},{3,2},{4,5},{5,4},{6,7},{7,6},{8,9},{9,8},{10,11... | collective-permute-start | bytes 1966088 | tf_op jit(solution)/shard_map/ppermute | solution.py:354
  23.7 7.5 %collective-permute-start.7 = (bf16[1,128,256]{2,1,0:T(8,128)(2,1)S(1)}, bf16[1,128,256]{2,1,0:T(8,128)(2,1)S(1)}, u32[]{:S(2)}, u32[]{:S(2)}) collective-permute-start(bf16[1,128,256]{2,1,0:T(8,128)(2,1)S(1)} %get-tuple-element.58), channel_id=1, source_target_pairs={{0,4},{4,8},{8,12},{12,16},{16,20},{20,24},{24,28},{28,0},{1,5},{5... | collective-permute-start | bytes 196616 | tf_op jit(solution)/shard_map/ppermute | solution.py:360
  25.8 12.3 %collective-permute-start.10 = (bf16[1,640,256]{2,1,0:T(8,128)(2,1)S(1)}, bf16[1,640,256]{2,1,0:T(8,128)(2,1)S(1)}, u32[]{:S(2)}, u32[]{:S(2)}) collective-permute-start(bf16[1,640,256]{2,1,0:T(8,128)(2,1)S(1)} %get-tuple-element.56.refs_4_), channel_id=1, source_target_pairs={{0,2},{1,3},{2,0},{3,1},{4,6},{5,7},{6,4},{7,5},{8,10},{9,11},{10,... | collective-permute-start | bytes 983048 | tf_op jit(solution)/shard_map/ppermute | solution.py:357
  27.3 12.0 %collective-permute-start.9 = (bf16[1,640,256]{2,1,0:T(8,128)(2,1)S(1)}, bf16[1,640,256]{2,1,0:T(8,128)(2,1)S(1)}, u32[]{:S(2)}, u32[]{:S(2)}) collective-permute-start(bf16[1,640,256]{2,1,0:T(8,128)(2,1)S(1)} %get-tuple-element.56.refs_4_), channel_id=1, source_target_pairs={{0,1},{1,0},{2,3},{3,2},{4,5},{5,4},{6,7},{7,6},{8,9},{9,8},{10,11... | collective-permute-start | bytes 983048 | tf_op jit(solution)/shard_map/ppermute | solution.py:354
  28.2 4.1 %collective-permute-start.8 = (bf16[2,384,256]{2,1,0:T(8,128)(2,1)S(1)}, bf16[2,384,256]{2,1,0:T(8,128)(2,1)S(1)}, u32[]{:S(2)}, u32[]{:S(2)}) collective-permute-start(bf16[2,384,256]{2,1,0:T(8,128)(2,1)S(1)} %collective-permute-done.6.refs_2_), channel_id=1, source_target_pairs={{0,1},{1,0},{2,3},{3,2},{4,5},{5,4},{6,7},{7,6},{8,9},{9,8},{10,11... | collective-permute-start | bytes 1179656 | tf_op jit(solution)/shard_map/ppermute | solution.py:354
  33.0 7.4 %collective-permute-start.14 = (bf16[1,384,256]{2,1,0:T(8,128)(2,1)S(1)}, bf16[1,384,256]{2,1,0:T(8,128)(2,1)S(1)}, u32[]{:S(2)}, u32[]{:S(2)}) collective-permute-start(bf16[1,384,256]{2,1,0:T(8,128)(2,1)S(1)} %get-tuple-element.68.refs_0_), channel_id=1, source_target_pairs={{0,2},{1,3},{2,0},{3,1},{4,6},{5,7},{6,4},{7,5},{8,10},{9,11},{10,... | collective-permute-start | bytes 589832 | tf_op jit(solution)/shard_map/ppermute | solution.py:357
  34.6 6.1 %collective-permute-start.13 = (bf16[1,384,256]{2,1,0:T(8,128)(2,1)S(1)}, bf16[1,384,256]{2,1,0:T(8,128)(2,1)S(1)}, u32[]{:S(2)}, u32[]{:S(2)}) collective-permute-start(bf16[1,384,256]{2,1,0:T(8,128)(2,1)S(1)} %get-tuple-element.68.refs_0_), channel_id=1, source_target_pairs={{0,1},{1,0},{2,3},{3,2},{4,5},{5,4},{6,7},{7,6},{8,9},{9,8},{10,11... | collective-permute-start | bytes 589832 | tf_op jit(solution)/shard_map/ppermute | solution.py:354
  34.6 5.8 %collective-permute-start.12 = (bf16[1,128,256]{2,1,0:T(8,128)(2,1)S(1)}, bf16[1,128,256]{2,1,0:T(8,128)(2,1)S(1)}, u32[]{:S(2)}, u32[]{:S(2)}) collective-permute-start(bf16[1,128,256]{2,1,0:T(8,128)(2,1)S(1)} %get-tuple-element.73), channel_id=1, source_target_pairs={{4,0},{8,4},{12,8},{16,12},{20,16},{24,20},{28,24},{0,28},{5,1},{9... | collective-permute-start | bytes 196616 | tf_op jit(solution)/shard_map/ppermute | solution.py:363
  38.1 1.6 %collective-permute-start.11 = (bf16[1,640,256]{2,1,0:T(8,128)(2,1)S(1)}, bf16[1,640,256]{2,1,0:T(8,128)(2,1)S(1)}, u32[]{:S(2)}, u32[]{:S(2)}) collective-permute-start(bf16[1,640,256]{2,1,0:T(8,128)(2,1)S(1)} %collective-permute-done.10.far_ref), channel_id=1, source_target_pairs={{0,1},{1,0},{2,3},{3,2},{4,5},{5,4},{6,7},{7,6},{8,9},{9,8},{10,11... | collective-permute-start | bytes 983048 | tf_op jit(solution)/shard_map/ppermute | solution.py:354
  40.4 1.6 %collective-permute-start.15 = (bf16[1,384,256]{2,1,0:T(8,128)(2,1)S(1)}, bf16[1,384,256]{2,1,0:T(8,128)(2,1)S(1)}, u32[]{:S(2)}, u32[]{:S(2)}) collective-permute-start(bf16[1,384,256]{2,1,0:T(8,128)(2,1)S(1)} %collective-permute-done.14.refs_2_), channel_id=1, source_target_pairs={{0,1},{1,0},{2,3},{3,2},{4,5},{5,4},{6,7},{7,6},{8,9},{9,8},{10,11... | collective-permute-start | bytes 589832 | tf_op jit(solution)/shard_map/ppermute | solution.py:354

commit v12 on v11

--- a/solution.py
+++ b/solution.py
@@ -262,16 +262,16 @@
     )
 
 
-def whole_sums(part, blocks, kernels):
-    rows, owned = blocks[0].shape[1:]
-
-    def body(part_ref, sib_ref, far_ref, farsib_ref, k_ref, sums_ref):
-        me = lax.axis_index("trait")
-        values = [r[...].reshape(rows, owned) for r in (sib_ref, far_ref, farsib_ref)]
-        for k in range(2):
-            sums_ref[k] = (part_ref[k] + blocks_dot(values, k_ref, k, [me ^ 1, me ^ 2, me ^ 3])).astype(BF16)
-
-    return call(body, "whole_sums", [part, *blocks, kernels], [pltpu.VMEM((2, rows, owned), BF16)])[0]
+def whole_sums(part, last, kernels):
+    rows, owned = last.shape[1:]
+
+    def body(part_ref, last_ref, k_ref, sums_ref):
+        me = lax.axis_index("trait")
+        for k in range(2):
+            last_part = blocks_dot([last_ref[...].reshape(rows, owned)], k_ref, k, [me ^ 3])
+            sums_ref[k] = (part_ref[k] + last_part).astype(BF16)
+
+    return call(body, "whole_sums", [part, last, kernels], [pltpu.VMEM((2, rows, owned), BF16)])[0]
 
 
 def finish(cells, pieces, ycount, sums, base_ref, new_ref, factor, faces, held, out_ref, sems):
@@ -393,9 +393,9 @@
     nfar_a = after(nfar_a, rounded_b)
     nfarsib_a = to_sibling(nfar_a)
     new_one, npart_a, nbase_a, nbase_b = before_second(
-        (new_a, new_b), (rest_a, rest_b), growth, death, new_one, [rounded_a], kernels, chunks
-    )
-    sums_a = whole_sums(npart_a, [nsib_a, nfar_a, nfarsib_a], after(kernels, nbase_a))
+        (new_a, new_b), (rest_a, rest_b), growth, death, new_one, [rounded_a, nsib_a, nfar_a], kernels, chunks
+    )
+    sums_a = whole_sums(npart_a, nfarsib_a, after(kernels, nbase_a))
     nfar_b = after(nfar_b, sums_a, new_hi)
     nfarsib_b = to_sibling(nfar_b)
     begun, npart_b = second_first(

time: 43.2 us -> 42.9 us (level)
  transfers between devices with their start and end apart: 16 -> 16, of which waited for: 7 -> 8; matrix products, arithmetic and copies ran while one was open for 0% -> 0% of each run, Pallas kernels for 21% -> 21%
where the time goes in v12:
time: 42.9 us; the launch traced here: 42.7 us
  starting transfers between devices  17.5 us (41%)
  waiting for transfers between devices  13.2 us (31%)
  Pallas kernels  11.3 us (26%)
  between operations  0.77 us (2%)
    pallas_call x11, Pallas kernels, call(): pl.pallas_call(body, out_shape=outs, in_specs=specs, out_specs=out_specs...  11.3 us
    ppermute x2, starting transfers between devices, from_above(): lax.ppermute(head, 'gx', [((i + 1) % gcount, i) for i in range(gcount)])  6.69 us
    ppermute x2, waiting for transfers between devices, from_below(): lax.ppermute(tail, 'gx', [(i, (i + 1) % gcount) for i in range(gcount)])  6.67 us
    ppermute x4, starting transfers between devices, to_far(): return lax.ppermute(v, 'trait', [(i, i ^ 2) for i in range(traits)])  6.57 us
    ppermute x4, waiting for transfers between devices, to_far(): return lax.ppermute(v, 'trait', [(i, i ^ 2) for i in range(traits)])  4.33 us
    ppermute x2, starting transfers between devices, from_below(): lax.ppermute(tail, 'gx', [(i, (i + 1) % gcount) for i in range(gcount)])  3.63 us
    ppermute x2, waiting for transfers between devices, from_above(): lax.ppermute(head, 'gx', [((i + 1) % gcount, i) for i in range(gcount)])  1.18 us
    ppermute x8, waiting for transfers between devices, to_sibling(): return lax.ppermute(v, 'trait', [(i, i ^ 1) for i in range(traits)])  0.99 us
  transfers between devices with their start and end apart: 16, of which 8 were waited for; matrix products, arithmetic and copies ran while one was open for 0% of the time, Pallas kernels for 21%

profile of v12, /device:TPU:0, one launch (start us, length us, event | category | flops | bytes accessed | tf_op | source)
XLA Modules:
  0.0 42.7 jit_solution(9019776038361290554)
XLA Ops:
  0.6 1.3 %load_chunk.2 = (f32[5,128,256]{2,1,0:T(8,128)S(1)}, f32[5,128,256]{2,1,0:T(8,128)S(1)}, bf16[2,640,256]{2,1,0:T(8,128)(2,1)S(1)}, bf16[2,128,256]{2,1,0:T(8,128)(2,1)S(1)}, bf16[2,128,256]{2,1,0:T(8,128)(2,1)S(1)}) custom-call(f32[8,128,256]{2,1,0:T(8,128)} %refs_0_.2, f32[8,128,256]{2,1,0:T(8,128)} %refs_1_.3), custom_call_target="tpu_custom_call" | custom-call | tf_op jit(solution)/shard_map/load_chunk/pallas_call | solution.py:37
  2.0 0.0 copy-start.3
  2.0 3.0 %collective-permute-start.1 = (bf16[2,640,256]{2,1,0:T(8,128)(2,1)S(1)}, bf16[2,640,256]{2,1,0:T(8,128)(2,1)S(1)}, u32[]{:S(2)}, u32[]{:S(2)}) collective-permute-start(bf16[2,640,256]{2,1,0:T(8,128)(2,1)S(1)} %get-tuple-element.43.refs_0_), channel_id=1, source_target_pairs={{0,2},{1,3},{2,0},{3,1},{4,6},{5,7},{6,4},{7,5},{8,10},{9,11},{10,... | collective-permute-start | bytes 1966088 | tf_op jit(solution)/shard_map/ppermute | solution.py:357
  5.0 1.1 %load_chunk.3 = (f32[3,128,256]{2,1,0:T(8,128)S(1)}, f32[3,128,256]{2,1,0:T(8,128)S(1)}, bf16[2,384,256]{2,1,0:T(8,128)(2,1)S(1)}) custom-call(f32[8,128,256]{2,1,0:T(8,128)} %refs_0_.2, f32[8,128,256]{2,1,0:T(8,128)} %refs_1_.3), custom_call_target="tpu_custom_call" | custom-call | tf_op jit(solution)/shard_map/load_chunk/pallas_call | solution.py:37
  6.2 0.0 copy-start
  6.2 0.1 collective-permute-start
  6.3 1.5 %collective-permute-start.2 = (bf16[2,128,256]{2,1,0:T(8,128)(2,1)S(1)}, bf16[2,128,256]{2,1,0:T(8,128)(2,1)S(1)}, u32[]{:S(2)}, u32[]{:S(2)}) collective-permute-start(bf16[2,128,256]{2,1,0:T(8,128)(2,1)S(1)} %get-tuple-element.50), channel_id=1, source_target_pairs={{0,4},{4,8},{8,12},{12,16},{16,20},{20,24},{24,28},{28,0},{1,5},{5... | collective-permute-start | bytes 393224 | tf_op jit(solution)/shard_map/ppermute | solution.py:360
  7.8 3.2 %collective-permute-start.3 = (bf16[2,128,256]{2,1,0:T(8,128)(2,1)S(1)}, bf16[2,128,256]{2,1,0:T(8,128)(2,1)S(1)}, u32[]{:S(2)}, u32[]{:S(2)}) collective-permute-start(bf16[2,128,256]{2,1,0:T(8,128)(2,1)S(1)} %get-tuple-element.51), channel_id=1, source_target_pairs={{4,0},{8,4},{12,8},{16,12},{20,16},{24,20},{28,24},{0,28},{5,1},{9... | collective-permute-start | bytes 393224 | tf_op jit(solution)/shard_map/ppermute | solution.py:363
  11.0 0.4 collective-permute-start.6
  11.4 3.6 %collective-permute-done.2.refs_4_ = bf16[2,128,256]{2,1,0:T(8,128)(2,1)S(1)} collective-permute-done((bf16[2,128,256]{2,1,0:T(8,128)(2,1)S(1)}, bf16[2,128,256]{2,1,0:T(8,128)(2,1)S(1)}, u32[]{:S(2)}, u32[]{:S(2)}) %collective-permute-start.2) | collective-permute-done | bytes 131104 | tf_op jit(solution)/shard_map/ppermute | solution.py:360
  15.0 0.0 collective-permute-start.5
  15.0 1.1 %collective-permute-done.3.refs_5_ = bf16[2,128,256]{2,1,0:T(8,128)(2,1)S(1)} collective-permute-done((bf16[2,128,256]{2,1,0:T(8,128)(2,1)S(1)}, bf16[2,128,256]{2,1,0:T(8,128)(2,1)S(1)}, u32[]{:S(2)}, u32[]{:S(2)}) %collective-permute-start.3) | collective-permute-done | bytes 131104 | tf_op jit(solution)/shard_map/ppermute | solution.py:363
  16.2 0.0 copy-done.3
  16.2 0.9 %before_first.1 = (f32[2,5,128,256]{3,2,1,0:T(8,128)S(1)}, f32[2,3,128,256]{3,2,1,0:T(8,128)S(1)}) custom-call(f32[5,128,256]{2,1,0:T(8,128)S(1)} %get-tuple-element.44.refs_0_.one_ref, f32[3,128,256]{2,1,0:T(8,128)S(1)} %get-tuple-element.45.refs_1_.one_ref, f32[5,128,256]{2,1,0:T(8,128)S(1)} %get-tuple-element.46.refs_2_.two_ref, ...), custom_call_target="tpu_custom_call" | custom-call | tf_op jit(solution)/shard_map/before_first/pallas_call | solution.py:37
  17.1 3.5 %collective-permute-done.1.refs_2_ = bf16[2,640,256]{2,1,0:T(8,128)(2,1)S(1)} collective-permute-done((bf16[2,640,256]{2,1,0:T(8,128)(2,1)S(1)}, bf16[2,640,256]{2,1,0:T(8,128)(2,1)S(1)}, u32[]{:S(2)}, u32[]{:S(2)}) %collective-permute-start.1) | collective-permute-done | bytes 655392 | tf_op jit(solution)/shard_map/ppermute | solution.py:357
  20.6 0.0 collective-permute-start.4
  20.6 0.0 collective-permute-done.refs_1_
  20.6 0.0 copy-done
  20.6 1.2 %early_part.2.part_ref = f32[2,1280,256]{2,1,0:T(8,128)S(1)} custom-call(bf16[2,640,256]{2,1,0:T(8,128)(2,1)S(1)} %get-tuple-element.43.refs_0_, bf16[2,640,256]{2,1,0:T(8,128)(2,1)S(1)} %collective-permute-done.refs_1_, bf16[2,640,256]{2,1,0:T(8,128)(2,1)S(1)} %collective-permute-done.1.refs_2_, bf16[2,1024,256]{2,1,0:T(8,128)(2,1)S(1)} %copy-done), custom_call_target="tpu_custom_call" | custom-call | flops 20000000000 | tf_op jit(solution)/shard_map/early_part/pallas_call | solution.py:37
  21.8 0.9 %collective-permute-done.4.last_ref = bf16[2,640,256]{2,1,0:T(8,128)(2,1)S(1)} collective-permute-done((bf16[2,640,256]{2,1,0:T(8,128)(2,1)S(1)}, bf16[2,640,256]{2,1,0:T(8,128)(2,1)S(1)}, u32[]{:S(2)}, u32[]{:S(2)}) %collective-permute-start.4) | collective-permute-done | bytes 655392 | tf_op jit(solution)/shard_map/ppermute | solution.py:354
  22.7 0.0 copy-done.2
  22.7 1.0 %first_node.2 = (f32[5,128,256]{2,1,0:T(8,128)S(1)}, bf16[1,640,256]{2,1,0:T(8,128)(2,1)S(1)}, f32[5,128,256]{2,1,0:T(8,128)S(1)}, bf16[1,128,256]{2,1,0:T(8,128)(2,1)S(1)}, bf16[1,128,256]{2,1,0:T(8,128)(2,1)S(1)}) custom-call(f32[2,1280,256]{2,1,0:T(8,128)S(1)} %early_part.2.part_ref, bf16[2,640,256]{2,1,0:T(8,128)(2,1)S(1)} %collective-permute-done.4.last_ref, ...), custom_call_target="tpu_custom_call" | custom-call | tf_op jit(solution)/shard_map/first_node/pallas_call | solution.py:37
  23.7 2.1 %collective-permute-start.7 = (bf16[1,128,256]{2,1,0:T(8,128)(2,1)S(1)}, bf16[1,128,256]{2,1,0:T(8,128)(2,1)S(1)}, u32[]{:S(2)}, u32[]{:S(2)}) collective-permute-start(bf16[1,128,256]{2,1,0:T(8,128)(2,1)S(1)} %get-tuple-element.58), channel_id=1, source_target_pairs={{0,4},{4,8},{8,12},{12,16},{16,20},{20,24},{24,28},{28,0},{1,5},{5... | collective-permute-start | bytes 196616 | tf_op jit(solution)/shard_map/ppermute | solution.py:360
  25.8 1.5 %collective-permute-start.10 = (bf16[1,640,256]{2,1,0:T(8,128)(2,1)S(1)}, bf16[1,640,256]{2,1,0:T(8,128)(2,1)S(1)}, u32[]{:S(2)}, u32[]{:S(2)}) collective-permute-start(bf16[1,640,256]{2,1,0:T(8,128)(2,1)S(1)} %get-tuple-element.56.refs_4_), channel_id=1, source_target_pairs={{0,2},{1,3},{2,0},{3,1},{4,6},{5,7},{6,4},{7,5},{8,10},{9,11},{10,... | collective-permute-start | bytes 983048 | tf_op jit(solution)/shard_map/ppermute | solution.py:357
  27.3 0.0 collective-permute-start.9
  27.3 0.8 %collective-permute-done.6.refs_2_ = bf16[2,384,256]{2,1,0:T(8,128)(2,1)S(1)} collective-permute-done((bf16[2,384,256]{2,1,0:T(8,128)(2,1)S(1)}, bf16[2,384,256]{2,1,0:T(8,128)(2,1)S(1)}, u32[]{:S(2)}, u32[]{:S(2)}) %collective-permute-start.6) | collective-permute-done | bytes 393248 | tf_op jit(solution)/shard_map/ppermute | solution.py:357
  28.2 0.0 collective-permute-start.8
  28.2 3.1 %collective-permute-done.7.lo_ref = bf16[1,128,256]{2,1,0:T(8,128)(2,1)S(1)} collective-permute-done((bf16[1,128,256]{2,1,0:T(8,128)(2,1)S(1)}, bf16[1,128,256]{2,1,0:T(8,128)(2,1)S(1)}, u32[]{:S(2)}, u32[]{:S(2)}) %collective-permute-start.7) | collective-permute-done | bytes 65568 | tf_op jit(solution)/shard_map/ppermute | solution.py:360
  31.2 0.0 collective-permute-done.5.refs_1_
  31.2 1.0 %early_part.3 = (f32[2,768,256]{2,1,0:T(8,128)S(1)}, f32[8,128,256]{2,1,0:T(8,128)}) custom-call(bf16[2,384,256]{2,1,0:T(8,128)(2,1)S(1)} %get-tuple-element.42.refs_0_, bf16[2,384,256]{2,1,0:T(8,128)(2,1)S(1)} %collective-permute-done.5.refs_1_, bf16[2,384,256]{2,1,0:T(8,128)(2,1)S(1)} %collective-permute-done.6.refs_2_, bf16[2,1024,256]{2,1,0:T(8,128)(2,1)S(1)} %copy-done, ...), custom_call_target="tpu_custom_call" | custom-call | flops 20000000000 | tf_op jit(solution)/shard_map/early_part/pallas_call | solution.py:37
  32.3 0.0 collective-permute-done.8.last_ref
  32.3 0.7 %first_node.3 = (f32[3,128,256]{2,1,0:T(8,128)S(1)}, bf16[1,384,256]{2,1,0:T(8,128)(2,1)S(1)}, f32[3,128,256]{2,1,0:T(8,128)S(1)}) custom-call(f32[2,768,256]{2,1,0:T(8,128)S(1)} %get-tuple-element.60.part_ref, bf16[2,384,256]{2,1,0:T(8,128)(2,1)S(1)} %collective-permute-done.8.last_ref, f32[2,3,128,256]{3,2,1,0:T(8,128)S(1)} %get-tuple-element.61.base_ref, ...), custom_call_target="tpu_custom_call" | custom-call | tf_op jit(solution)/shard_map/first_node/pallas_call | solution.py:37
  33.0 1.6 %collective-permute-start.14 = (bf16[1,384,256]{2,1,0:T(8,128)(2,1)S(1)}, bf16[1,384,256]{2,1,0:T(8,128)(2,1)S(1)}, u32[]{:S(2)}, u32[]{:S(2)}) collective-permute-start(bf16[1,384,256]{2,1,0:T(8,128)(2,1)S(1)} %get-tuple-element.65.refs_0_), channel_id=1, source_target_pairs={{0,2},{1,3},{2,0},{3,1},{4,6},{5,7},{6,4},{7,5},{8,10},{9,11},{10,... | collective-permute-start | bytes 589832 | tf_op jit(solution)/shard_map/ppermute | solution.py:357
  34.6 0.0 collective-permute-start.13
  34.6 3.5 %collective-permute-start.12 = (bf16[1,128,256]{2,1,0:T(8,128)(2,1)S(1)}, bf16[1,128,256]{2,1,0:T(8,128)(2,1)S(1)}, u32[]{:S(2)}, u32[]{:S(2)}) collective-permute-start(bf16[1,128,256]{2,1,0:T(8,128)(2,1)S(1)} %get-tuple-element.73), channel_id=1, source_target_pairs={{4,0},{8,4},{12,8},{16,12},{20,16},{24,20},{28,24},{0,28},{5,1},{9... | collective-permute-start | bytes 196616 | tf_op jit(solution)/shard_map/ppermute | solution.py:363
  38.1 0.0 collective-permute-done.10.refs_6_
  38.1 0.2 collective-permute-start.11
  38.3 0.0 collective-permute-done.9.refs_5_
  38.3 1.3 %before_second.1 = (f32[8,128,256]{2,1,0:T(8,128)}, f32[2,640,256]{2,1,0:T(8,128)S(1)}, f32[5,128,256]{2,1,0:T(8,128)S(1)}, f32[3,128,256]{2,1,0:T(8,128)S(1)}) custom-call(f32[5,128,256]{2,1,0:T(8,128)S(1)} %get-tuple-element.55.refs_4_.refs_0_.new_ref, f32[3,128,256]{2,1,0:T(8,128)S(1)} %get-tuple-element.62.refs_1_.new_ref, ...), custom_call_target="tpu_custom_call", output_to_operand_aliasing={{0}: (10, {})} | custom-call | flops 20000000000 | tf_op jit(solution)/shard_map/before_second/pallas_call | solution.py:37
  39.6 0.1 collective-permute-done.11.last_ref
  39.7 0.3 whole_sums.1.sums_ref
  40.0 0.1 collective-permute-done.12.hi_ref
  40.1 0.0 collective-permute-done.14.refs_2_
  40.1 0.3 collective-permute-start.15
  40.4 0.0 collective-permute-done.13.refs_1_
  40.4 1.3 %second_first.1 = (f32[8,128,256]{2,1,0:T(8,128)}, f32[2,384,256]{2,1,0:T(8,128)S(1)}) custom-call(bf16[2,640,256]{2,1,0:T(8,128)(2,1)S(1)} %whole_sums.1.sums_ref, f32[5,128,256]{2,1,0:T(8,128)S(1)} %get-tuple-element.70.base_ref, f32[5,128,256]{2,1,0:T(8,128)S(1)} %get-tuple-element.55.refs_4_.refs_0_.new_ref, f32[1,256]{1,0:T(1,128)S(1)} %bitcast.5, ...), custom_call_target="tpu_custom_call" | custom-call | tf_op jit(solution)/shard_map/second_first/pallas_call | solution.py:37
  41.7 0.0 collective-permute-done.15.last_ref
  41.7 1.0 %second_last.1 = f32[8,128,256]{2,1,0:T(8,128)} custom-call(f32[2,384,256]{2,1,0:T(8,128)S(1)} %get-tuple-element.75.part_ref, bf16[1,384,256]{2,1,0:T(8,128)(2,1)S(1)} %collective-permute-done.15.last_ref, f32[3,128,256]{2,1,0:T(8,128)S(1)} %get-tuple-element.76.base_ref, ...), custom_call_target="tpu_custom_call", output_to_operand_aliasing={{}: (6, {})} | custom-call | tf_op jit(solution)/shard_map/second_last/pallas_call | solution.py:37
  (3 shorter events, 0.0 us)
Async XLA Ops:
  2.0 14.2 %copy-start.3 = (f32[256]{0:T(256)S(1)}, f32[256]{0:T(256)}, u32[]{:S(2)}) copy-start(f32[256]{0:T(256)} %param.10) | copy-start | bytes 3076
  2.0 18.6 %collective-permute-start.1 = (bf16[2,640,256]{2,1,0:T(8,128)(2,1)S(1)}, bf16[2,640,256]{2,1,0:T(8,128)(2,1)S(1)}, u32[]{:S(2)}, u32[]{:S(2)}) collective-permute-start(bf16[2,640,256]{2,1,0:T(8,128)(2,1)S(1)} %get-tuple-element.43.refs_0_), channel_id=1, source_target_pairs={{0,2},{1,3},{2,0},{3,1},{4,6},{5,7},{6,4},{7,5},{8,10},{9,11},{10,... | collective-permute-start | bytes 1966088 | tf_op jit(solution)/shard_map/ppermute | solution.py:357
  6.2 14.4 %copy-start = (bf16[2,1024,256]{2,1,0:T(8,128)(2,1)S(1)}, bf16[2,1024,256]{2,1,0:T(8,128)(2,1)}, u32[]{:S(2)}) copy-start(bf16[2,1024,256]{2,1,0:T(8,128)(2,1)} %k_ref.4) | copy-start | bytes 3145732
  6.2 14.4 %collective-permute-start = (bf16[2,640,256]{2,1,0:T(8,128)(2,1)S(1)}, bf16[2,640,256]{2,1,0:T(8,128)(2,1)S(1)}, u32[]{:S(2)}, u32[]{:S(2)}) collective-permute-start(bf16[2,640,256]{2,1,0:T(8,128)(2,1)S(1)} %get-tuple-element.43.refs_0_), channel_id=1, source_target_pairs={{0,1},{1,0},{2,3},{3,2},{4,5},{5,4},{6,7},{7,6},{8,9},{9,8},{10,11... | collective-permute-start | bytes 1966088 | tf_op jit(solution)/shard_map/ppermute | solution.py:354
  6.3 8.8 %collective-permute-start.2 = (bf16[2,128,256]{2,1,0:T(8,128)(2,1)S(1)}, bf16[2,128,256]{2,1,0:T(8,128)(2,1)S(1)}, u32[]{:S(2)}, u32[]{:S(2)}) collective-permute-start(bf16[2,128,256]{2,1,0:T(8,128)(2,1)S(1)} %get-tuple-element.50), channel_id=1, source_target_pairs={{0,4},{4,8},{8,12},{12,16},{16,20},{20,24},{24,28},{28,0},{1,5},{5... | collective-permute-start | bytes 393224 | tf_op jit(solution)/shard_map/ppermute | solution.py:360
  7.8 8.4 %collective-permute-start.3 = (bf16[2,128,256]{2,1,0:T(8,128)(2,1)S(1)}, bf16[2,128,256]{2,1,0:T(8,128)(2,1)S(1)}, u32[]{:S(2)}, u32[]{:S(2)}) collective-permute-start(bf16[2,128,256]{2,1,0:T(8,128)(2,1)S(1)} %get-tuple-element.51), channel_id=1, source_target_pairs={{4,0},{8,4},{12,8},{16,12},{20,16},{24,20},{28,24},{0,28},{5,1},{9... | collective-permute-start | bytes 393224 | tf_op jit(solution)/shard_map/ppermute | solution.py:363
  11.0 17.1 %collective-permute-start.6 = (bf16[2,384,256]{2,1,0:T(8,128)(2,1)S(1)}, bf16[2,384,256]{2,1,0:T(8,128)(2,1)S(1)}, u32[]{:S(2)}, u32[]{:S(2)}) collective-permute-start(bf16[2,384,256]{2,1,0:T(8,128)(2,1)S(1)} %get-tuple-element.42.refs_0_), channel_id=1, source_target_pairs={{0,2},{1,3},{2,0},{3,1},{4,6},{5,7},{6,4},{7,5},{8,10},{9,11},{10,... | collective-permute-start | bytes 1179656 | tf_op jit(solution)/shard_map/ppermute | solution.py:357
  15.0 16.2 %collective-permute-start.5 = (bf16[2,384,256]{2,1,0:T(8,128)(2,1)S(1)}, bf16[2,384,256]{2,1,0:T(8,128)(2,1)S(1)}, u32[]{:S(2)}, u32[]{:S(2)}) collective-permute-start(bf16[2,384,256]{2,1,0:T(8,128)(2,1)S(1)} %get-tuple-element.42.refs_0_), channel_id=1, source_target_pairs={{0,1},{1,0},{2,3},{3,2},{4,5},{5,4},{6,7},{7,6},{8,9},{9,8},{10,11... | collective-permute-start | bytes 1179656 | tf_op jit(solution)/shard_map/ppermute | solution.py:354
  20.6 2.1 %copy-start.1 = (f32[8,128,256]{2,1,0:T(8,128)S(1)}, f32[8,128,256]{2,1,0:T(8,128)}, u32[]{:S(2)}) copy-start(f32[8,128,256]{2,1,0:T(8,128)} %init_ref.3) | copy-start | bytes 3145732
  20.6 2.1 %copy-start.2 = (f32[256]{0:T(256)S(1)}, f32[256]{0:T(256)}, u32[]{:S(2)}) copy-start(f32[256]{0:T(256)} %param.11) | copy-start | bytes 3076
  20.6 2.1 %collective-permute-start.4 = (bf16[2,640,256]{2,1,0:T(8,128)(2,1)S(1)}, bf16[2,640,256]{2,1,0:T(8,128)(2,1)S(1)}, u32[]{:S(2)}, u32[]{:S(2)}) collective-permute-start(bf16[2,640,256]{2,1,0:T(8,128)(2,1)S(1)} %collective-permute-done.1.refs_2_), channel_id=1, source_target_pairs={{0,1},{1,0},{2,3},{3,2},{4,5},{5,4},{6,7},{7,6},{8,9},{9,8},{10,11... | collective-permute-start | bytes 1966088 | tf_op jit(solution)/shard_map/ppermute | solution.py:354
  23.7 7.5 %collective-permute-start.7 = (bf16[1,128,256]{2,1,0:T(8,128)(2,1)S(1)}, bf16[1,128,256]{2,1,0:T(8,128)(2,1)S(1)}, u32[]{:S(2)}, u32[]{:S(2)}) collective-permute-start(bf16[1,128,256]{2,1,0:T(8,128)(2,1)S(1)} %get-tuple-element.58), channel_id=1, source_target_pairs={{0,4},{4,8},{8,12},{12,16},{16,20},{20,24},{24,28},{28,0},{1,5},{5... | collective-permute-start | bytes 196616 | tf_op jit(solution)/shard_map/ppermute | solution.py:360
  25.8 12.3 %collective-permute-start.10 = (bf16[1,640,256]{2,1,0:T(8,128)(2,1)S(1)}, bf16[1,640,256]{2,1,0:T(8,128)(2,1)S(1)}, u32[]{:S(2)}, u32[]{:S(2)}) collective-permute-start(bf16[1,640,256]{2,1,0:T(8,128)(2,1)S(1)} %get-tuple-element.56.refs_4_), channel_id=1, source_target_pairs={{0,2},{1,3},{2,0},{3,1},{4,6},{5,7},{6,4},{7,5},{8,10},{9,11},{10,... | collective-permute-start | bytes 983048 | tf_op jit(solution)/shard_map/ppermute | solution.py:357
  27.3 11.0 %collective-permute-start.9 = (bf16[1,640,256]{2,1,0:T(8,128)(2,1)S(1)}, bf16[1,640,256]{2,1,0:T(8,128)(2,1)S(1)}, u32[]{:S(2)}, u32[]{:S(2)}) collective-permute-start(bf16[1,640,256]{2,1,0:T(8,128)(2,1)S(1)} %get-tuple-element.56.refs_4_), channel_id=1, source_target_pairs={{0,1},{1,0},{2,3},{3,2},{4,5},{5,4},{6,7},{7,6},{8,9},{9,8},{10,11... | collective-permute-start | bytes 983048 | tf_op jit(solution)/shard_map/ppermute | solution.py:354
  28.2 4.1 %collective-permute-start.8 = (bf16[2,384,256]{2,1,0:T(8,128)(2,1)S(1)}, bf16[2,384,256]{2,1,0:T(8,128)(2,1)S(1)}, u32[]{:S(2)}, u32[]{:S(2)}) collective-permute-start(bf16[2,384,256]{2,1,0:T(8,128)(2,1)S(1)} %collective-permute-done.6.refs_2_), channel_id=1, source_target_pairs={{0,1},{1,0},{2,3},{3,2},{4,5},{5,4},{6,7},{7,6},{8,9},{9,8},{10,11... | collective-permute-start | bytes 1179656 | tf_op jit(solution)/shard_map/ppermute | solution.py:354
  33.0 7.1 %collective-permute-start.14 = (bf16[1,384,256]{2,1,0:T(8,128)(2,1)S(1)}, bf16[1,384,256]{2,1,0:T(8,128)(2,1)S(1)}, u32[]{:S(2)}, u32[]{:S(2)}) collective-permute-start(bf16[1,384,256]{2,1,0:T(8,128)(2,1)S(1)} %get-tuple-element.65.refs_0_), channel_id=1, source_target_pairs={{0,2},{1,3},{2,0},{3,1},{4,6},{5,7},{6,4},{7,5},{8,10},{9,11},{10,... | collective-permute-start | bytes 589832 | tf_op jit(solution)/shard_map/ppermute | solution.py:357
  34.6 5.8 %collective-permute-start.13 = (bf16[1,384,256]{2,1,0:T(8,128)(2,1)S(1)}, bf16[1,384,256]{2,1,0:T(8,128)(2,1)S(1)}, u32[]{:S(2)}, u32[]{:S(2)}) collective-permute-start(bf16[1,384,256]{2,1,0:T(8,128)(2,1)S(1)} %get-tuple-element.65.refs_0_), channel_id=1, source_target_pairs={{0,1},{1,0},{2,3},{3,2},{4,5},{5,4},{6,7},{7,6},{8,9},{9,8},{10,11... | collective-permute-start | bytes 589832 | tf_op jit(solution)/shard_map/ppermute | solution.py:354
  34.6 5.5 %collective-permute-start.12 = (bf16[1,128,256]{2,1,0:T(8,128)(2,1)S(1)}, bf16[1,128,256]{2,1,0:T(8,128)(2,1)S(1)}, u32[]{:S(2)}, u32[]{:S(2)}) collective-permute-start(bf16[1,128,256]{2,1,0:T(8,128)(2,1)S(1)} %get-tuple-element.73), channel_id=1, source_target_pairs={{4,0},{8,4},{12,8},{16,12},{20,16},{24,20},{28,24},{0,28},{5,1},{9... | collective-permute-start | bytes 196616 | tf_op jit(solution)/shard_map/ppermute | solution.py:363
  38.1 1.6 %collective-permute-start.11 = (bf16[1,640,256]{2,1,0:T(8,128)(2,1)S(1)}, bf16[1,640,256]{2,1,0:T(8,128)(2,1)S(1)}, u32[]{:S(2)}, u32[]{:S(2)}) collective-permute-start(bf16[1,640,256]{2,1,0:T(8,128)(2,1)S(1)} %collective-permute-done.10.refs_6_), channel_id=1, source_target_pairs={{0,1},{1,0},{2,3},{3,2},{4,5},{5,4},{6,7},{7,6},{8,9},{9,8},{10,11... | collective-permute-start | bytes 983048 | tf_op jit(solution)/shard_map/ppermute | solution.py:354
  40.1 1.6 %collective-permute-start.15 = (bf16[1,384,256]{2,1,0:T(8,128)(2,1)S(1)}, bf16[1,384,256]{2,1,0:T(8,128)(2,1)S(1)}, u32[]{:S(2)}, u32[]{:S(2)}) collective-permute-start(bf16[1,384,256]{2,1,0:T(8,128)(2,1)S(1)} %collective-permute-done.14.refs_2_), channel_id=1, source_target_pairs={{0,1},{1,0},{2,3},{3,2},{4,5},{5,4},{6,7},{7,6},{8,9},{9,8},{10,11... | collective-permute-start | bytes 589832 | tf_op jit(solution)/shard_map/ppermute | solution.py:354

commit v13 on v12

--- a/solution.py
+++ b/solution.py
@@ -131,52 +131,27 @@
     return call(body, "before_first", [*ones, *twos, lo, hi, growth], outs)
 
 
-def early_part(blocks, kernels, new=None, cells=(), xcount=0):
-    rows, owned = blocks[0].shape[0] * blocks[0].shape[1], blocks[0].shape[2]
+def early_part(blocks, base, one, two, initial, kernels, death, cells, new=None, new_cells=()):
+    xcount, ycount, owned = initial.shape
+    rows = len(cells) * ycount
     count = len(blocks)
 
     def body(*refs):
-        block_refs, k_ref = refs[:count], refs[count]
+        block_refs = refs[:count]
+        base_ref, one_ref, two_ref, init_ref, k_ref, d_ref, *refs = refs[count:]
         copies = []
-        if new is None:
-            part_ref = refs[-1]
-        else:
-            new_ref, part_ref, whole_ref, sems = refs[count + 1:]
+        if new is not None:
+            new_ref, whole_ref, sems = refs[0], refs[-2], refs[-1]
             copies = [
                 pltpu.make_async_copy(new_ref.at[pl.ds(i, size)], whole_ref.at[pl.ds(x, size)], sems.at[r])
-                for r, (i, x, size) in enumerate(runs_of(cells))
+                for r, (i, x, size) in enumerate(runs_of(new_cells))
             ]
         for copy in copies:
             copy.start()
-        me = lax.axis_index("trait")
-        values = [r[...].reshape(rows, owned) for r in block_refs]
-        for k in range(2):
-            part_ref[k] = blocks_dot(values, k_ref, k, [me ^ j for j in range(count)])
-        for copy in copies:
-            copy.wait()
-
-    args = [*blocks, kernels]
-    outs = [pltpu.VMEM((2, rows, owned), F32)]
-    if new is None:
-        return call(body, "early_part", args, outs, gflop=20.0)[0]
-    outs.append(jax.ShapeDtypeStruct((xcount, *new.shape[1:]), F32))
-    return call(
-        body, "early_part", [*args, new], outs, scratch=[pltpu.SemaphoreType.DMA((len(runs_of(cells)),))],
-        out_specs=[SPEC, ANYWHERE], gflop=20.0,
-    )
-
-
-def first_node(part, last, base, one, two, initial, kernels, death, cells, with_faces):
-    xcount, ycount, owned = initial.shape
-    rows = len(cells) * ycount
-
-    def body(part_ref, last_ref, base_ref, one_ref, two_ref, init_ref, k_ref, d_ref, *refs):
-        new_ref, rounded_ref, rest_ref = refs[:3]
-        sums = refs[-1]
-        me = lax.axis_index("trait")
-        for k in range(2):
-            far_part = blocks_dot([last_ref[...].reshape(2 * rows, owned)], k_ref, k, [me ^ 3])
-            sums[k] = (part_ref[k] + far_part).astype(BF16)
+        first_ref, rest_ref = refs[:2] if new is None else refs[1:3]
+        me = lax.axis_index("trait")
+        values = [r[...].reshape(2 * rows, owned) for r in block_refs]
+        compete, mutate = (blocks_dot(values, k_ref, k, [me ^ j for j in range(count)]) for k in range(2))
         death = d_ref[...]
         inv_one = 1.0 / (1.0 + FIRST * death)
         inv_two = 1.0 / (1.0 + SECOND * death)
@@ -184,25 +159,58 @@
             cores = (one_ref[i], two_ref[i])
             e = []
             for f in range(2):
-                at = pl.ds(f * rows + i * ycount, ycount)
-                e.append(base_ref[f, i] - cores[f] * sums[0, at, :].astype(F32) + sums[1, at, :].astype(F32))
+                at = slice(f * rows + i * ycount, f * rows + (i + 1) * ycount)
+                e.append(base_ref[f, i] - cores[f] * compete[at] + mutate[at])
             full_one = e[0] - death * cores[0]
             full_two = e[1] - death * cores[1]
-            new = (
+            first = (
                 init_ref[x]
                 + FIRST * death * cores[0]
                 + STEP_SIZE * (5.0 / 12.0 * full_one - 1.0 / 12.0 * full_two)
             ) * inv_one
+            first_ref[i] = first
+            rest_ref[i] = (
+                first - SECOND * e[0] + SECOND * death * cores[1] + STEP_SIZE / 3.0 * (full_one + full_two)
+            ) * inv_two
+        for copy in copies:
+            copy.wait()
+
+    args = [*blocks, base, one, two, initial, kernels, death]
+    outs = [pltpu.VMEM((len(cells), ycount, owned), F32)] * 2
+    if new is None:
+        return call(body, "early_part", args, outs, gflop=20.0)
+    outs.append(jax.ShapeDtypeStruct((xcount, ycount, owned), F32))
+    return call(
+        body, "early_part", [*args, new], outs, scratch=[pltpu.SemaphoreType.DMA((len(runs_of(new_cells)),))],
+        out_specs=[SPEC, SPEC, ANYWHERE], gflop=20.0,
+    )
+
+
+def first_node(first, rest, last, one, two, kernels, death, cells, xcount, with_faces):
+    _, ycount, owned = one.shape
+    rows = len(cells) * ycount
+
+    def body(first_ref, begun_ref, last_ref, one_ref, two_ref, k_ref, d_ref, new_ref, rounded_ref, rest_ref, *face_refs):
+        me = lax.axis_index("trait")
+        values = [last_ref[...].reshape(2 * rows, owned)]
+        compete, mutate = (blocks_dot(values, k_ref, k, [me ^ 3]) for k in range(2))
+        inv_one = STEP_SIZE / (1.0 + FIRST * d_ref[...])
+        inv_two = 1.0 / (1.0 + SECOND * d_ref[...])
+        for i, x in enumerate(cells):
+            e = []
+            for f, ref in enumerate((one_ref, two_ref)):
+                at = slice(f * rows + i * ycount, f * rows + (i + 1) * ycount)
+                e.append(mutate[at] - ref[i] * compete[at])
+            more = (5.0 / 12.0 * e[0] - 1.0 / 12.0 * e[1]) * inv_one
+            new = first_ref[i] + more
             new_ref[i] = new
             rounded = new.astype(BF16)
             rounded_ref[0, i * ycount:(i + 1) * ycount, :] = rounded
             if with_faces and x == 0:
-                refs[3][0] = rounded
+                face_refs[0][0] = rounded
             if with_faces and x == xcount - 1:
-                refs[4][0] = rounded
-            rest_ref[i] = (
-                new - SECOND * e[0] + SECOND * death * cores[1] + STEP_SIZE / 3.0 * (full_one + full_two)
-            ) * inv_two
+                face_refs[1][0] = rounded
+            rest_ref[i] = begun_ref[i] + (more - SECOND * e[0] + STEP_SIZE / 3.0 * (e[0] + e[1])) * inv_two
 
     outs = [
         pltpu.VMEM((len(cells), ycount, owned), F32),
@@ -211,11 +219,7 @@
     ]
     if with_faces:
         outs += [pltpu.VMEM((1, ycount, owned), BF16)] * 2
-    args = [part, last, base, one, two, initial, kernels, death]
-    return call(
-        body, "first_node", args, outs, scratch=[pltpu.VMEM((2, 2 * rows, owned), BF16)],
-        gflop=0.0,
-    )
+    return call(body, "first_node", [first, rest, last, one, two, kernels, death], outs)
 
 
 def before_second(news, rests, growth, death, begun, blocks, kernels, chunks):
@@ -373,9 +377,9 @@
     sib_b = to_sibling(own_b)
     far_a = after(far_a, base_a)
     farsib_a = to_sibling(far_a)
-    part_a = early_part([own_a, sib_a, far_a], kernels)
+    first_a, rest_a = early_part([own_a, sib_a, far_a], base_a, one_a, two_a, initial, kernels, death, chunks[0])
     new_a, rounded_a, rest_a, new_head, new_tail = first_node(
-        part_a, farsib_a, base_a, one_a, two_a, initial, kernels, death, chunks[0], True
+        first_a, rest_a, farsib_a, one_a, two_a, kernels, death, chunks[0], xcount, True
     )
     nfar_a = to_far(rounded_a)
     nsib_a = to_sibling(rounded_a)
@@ -383,9 +387,11 @@
     new_lo = from_below(new_tail)
     far_b = after(far_b, rounded_a)
     farsib_b = to_sibling(far_b)
-    part_b, new_one = early_part([own_b, sib_b, far_b], after(kernels, new_lo), new_a, chunks[0], xcount)
+    first_b, rest_b, new_one = early_part(
+        [own_b, sib_b, far_b], base_b, one_b, two_b, initial, after(kernels, new_lo), death, chunks[1], new_a, chunks[0]
+    )
     new_b, rounded_b, rest_b = first_node(
-        part_b, farsib_b, base_b, one_b, two_b, initial, kernels, death, chunks[1], False
+        first_b, rest_b, farsib_b, one_b, two_b, kernels, death, chunks[1], xcount, False
     )
     nfar_b = to_far(rounded_b)
     nsib_b = to_sibling(rounded_b)

time: 42.9 us -> 42.6 us (level)
    ppermute x2, waiting for transfers between devices: 6.67 us -> 6.12 us  [from_below(): lax.ppermute(tail, 'gx', [(i, (i + 1) % gcount) for i in range(gcount)])]
    ppermute x4, waiting for transfers between devices: 4.33 us -> 4.86 us  [to_far(): return lax.ppermute(v, 'trait', [(i, i ^ 2) for i in range(traits)])]
where the time goes in v13:
time: 42.6 us; the launch traced here: 42.5 us
  starting transfers between devices  17.8 us (42%)
  waiting for transfers between devices  12.8 us (30%)
  Pallas kernels  11.1 us (26%)
  between operations  0.79 us (2%)
    pallas_call x11, Pallas kernels, call(): pl.pallas_call(body, out_shape=outs, in_specs=specs, out_specs=out_specs...  11.1 us
    ppermute x2, starting transfers between devices, from_above(): lax.ppermute(head, 'gx', [((i + 1) % gcount, i) for i in range(gcount)])  7.05 us
    ppermute x4, starting transfers between devices, to_far(): return lax.ppermute(v, 'trait', [(i, i ^ 2) for i in range(traits)])  6.58 us
    ppermute x2, waiting for transfers between devices, from_below(): lax.ppermute(tail, 'gx', [(i, (i + 1) % gcount) for i in range(gcount)])  6.12 us
    ppermute x4, waiting for transfers between devices, to_far(): return lax.ppermute(v, 'trait', [(i, i ^ 2) for i in range(traits)])  4.86 us
    ppermute x2, starting transfers between devices, from_below(): lax.ppermute(tail, 'gx', [(i, (i + 1) % gcount) for i in range(gcount)])  3.62 us
    ppermute x2, waiting for transfers between devices, from_above(): lax.ppermute(head, 'gx', [((i + 1) % gcount, i) for i in range(gcount)])  1.18 us
  transfers between devices with their start and end apart: 16, of which 8 were waited for; matrix products, arithmetic and copies ran while one was open for 0% of the time, Pallas kernels for 21%

profile of v13, /device:TPU:0, one launch (start us, length us, event | category | flops | bytes accessed | tf_op | source)
XLA Modules:
  0.0 42.5 jit_solution(14267947043158891362)
XLA Ops:
  0.6 1.3 %load_chunk.2 = (f32[5,128,256]{2,1,0:T(8,128)S(1)}, f32[5,128,256]{2,1,0:T(8,128)S(1)}, bf16[2,640,256]{2,1,0:T(8,128)(2,1)S(1)}, bf16[2,128,256]{2,1,0:T(8,128)(2,1)S(1)}, bf16[2,128,256]{2,1,0:T(8,128)(2,1)S(1)}) custom-call(f32[8,128,256]{2,1,0:T(8,128)} %refs_0_.2, f32[8,128,256]{2,1,0:T(8,128)} %refs_1_.3), custom_call_target="tpu_custom_call" | custom-call | tf_op jit(solution)/shard_map/load_chunk/pallas_call | solution.py:37
  2.0 0.0 copy-start.2
  2.0 3.0 %collective-permute-start.1 = (bf16[2,640,256]{2,1,0:T(8,128)(2,1)S(1)}, bf16[2,640,256]{2,1,0:T(8,128)(2,1)S(1)}, u32[]{:S(2)}, u32[]{:S(2)}) collective-permute-start(bf16[2,640,256]{2,1,0:T(8,128)(2,1)S(1)} %get-tuple-element.46.refs_0_), channel_id=1, source_target_pairs={{0,2},{1,3},{2,0},{3,1},{4,6},{5,7},{6,4},{7,5},{8,10},{9,11},{10,... | collective-permute-start | bytes 1966088 | tf_op jit(solution)/shard_map/ppermute | solution.py:361
  5.0 1.1 %load_chunk.3 = (f32[3,128,256]{2,1,0:T(8,128)S(1)}, f32[3,128,256]{2,1,0:T(8,128)S(1)}, bf16[2,384,256]{2,1,0:T(8,128)(2,1)S(1)}) custom-call(f32[8,128,256]{2,1,0:T(8,128)} %refs_0_.2, f32[8,128,256]{2,1,0:T(8,128)} %refs_1_.3), custom_call_target="tpu_custom_call" | custom-call | tf_op jit(solution)/shard_map/load_chunk/pallas_call | solution.py:37
  6.2 0.0 copy-start
  6.2 0.0 copy-start.1
  6.2 0.0 copy-start.3
  6.2 0.1 collective-permute-start
  6.3 1.5 %collective-permute-start.2 = (bf16[2,128,256]{2,1,0:T(8,128)(2,1)S(1)}, bf16[2,128,256]{2,1,0:T(8,128)(2,1)S(1)}, u32[]{:S(2)}, u32[]{:S(2)}) collective-permute-start(bf16[2,128,256]{2,1,0:T(8,128)(2,1)S(1)} %get-tuple-element.53), channel_id=1, source_target_pairs={{0,4},{4,8},{8,12},{12,16},{16,20},{20,24},{24,28},{28,0},{1,5},{5... | collective-permute-start | bytes 393224 | tf_op jit(solution)/shard_map/ppermute | solution.py:364
  7.8 3.2 %collective-permute-start.3 = (bf16[2,128,256]{2,1,0:T(8,128)(2,1)S(1)}, bf16[2,128,256]{2,1,0:T(8,128)(2,1)S(1)}, u32[]{:S(2)}, u32[]{:S(2)}) collective-permute-start(bf16[2,128,256]{2,1,0:T(8,128)(2,1)S(1)} %get-tuple-element.54), channel_id=1, source_target_pairs={{4,0},{8,4},{12,8},{16,12},{20,16},{24,20},{28,24},{0,28},{5,1},{9... | collective-permute-start | bytes 393224 | tf_op jit(solution)/shard_map/ppermute | solution.py:367
  11.1 0.4 collective-permute-start.6
  11.4 3.6 %collective-permute-done.2.refs_4_ = bf16[2,128,256]{2,1,0:T(8,128)(2,1)S(1)} collective-permute-done((bf16[2,128,256]{2,1,0:T(8,128)(2,1)S(1)}, bf16[2,128,256]{2,1,0:T(8,128)(2,1)S(1)}, u32[]{:S(2)}, u32[]{:S(2)}) %collective-permute-start.2) | collective-permute-done | bytes 131104 | tf_op jit(solution)/shard_map/ppermute | solution.py:364
  15.1 0.0 collective-permute-start.5
  15.1 1.1 %collective-permute-done.3.refs_5_ = bf16[2,128,256]{2,1,0:T(8,128)(2,1)S(1)} collective-permute-done((bf16[2,128,256]{2,1,0:T(8,128)(2,1)S(1)}, bf16[2,128,256]{2,1,0:T(8,128)(2,1)S(1)}, u32[]{:S(2)}, u32[]{:S(2)}) %collective-permute-start.3) | collective-permute-done | bytes 131104 | tf_op jit(solution)/shard_map/ppermute | solution.py:367
  16.2 0.0 copy-done.2
  16.2 0.9 %before_first.1 = (f32[2,5,128,256]{3,2,1,0:T(8,128)S(1)}, f32[2,3,128,256]{3,2,1,0:T(8,128)S(1)}) custom-call(f32[5,128,256]{2,1,0:T(8,128)S(1)} %get-tuple-element.47.refs_0_.refs_4_.one_ref, f32[3,128,256]{2,1,0:T(8,128)S(1)} %get-tuple-element.48.refs_1_.refs_4_.one_ref, f32[5,128,256]{2,1,0:T(8,128)S(1)} %get-tuple-element.49.refs_2_.refs_5_.two_ref, ...), custom_call_target="tpu_custom_call" | custom-call | tf_op jit(solution)/shard_map/before_first/pallas_call | solution.py:37
  17.1 3.4 %collective-permute-done.1.refs_2_ = bf16[2,640,256]{2,1,0:T(8,128)(2,1)S(1)} collective-permute-done((bf16[2,640,256]{2,1,0:T(8,128)(2,1)S(1)}, bf16[2,640,256]{2,1,0:T(8,128)(2,1)S(1)}, u32[]{:S(2)}, u32[]{:S(2)}) %collective-permute-start.1) | collective-permute-done | bytes 655392 | tf_op jit(solution)/shard_map/ppermute | solution.py:361
  20.6 0.0 collective-permute-start.4
  20.6 0.0 collective-permute-done.refs_1_
  20.6 1.6 %early_part.2 = (f32[5,128,256]{2,1,0:T(8,128)S(1)}, f32[5,128,256]{2,1,0:T(8,128)S(1)}) custom-call(bf16[2,640,256]{2,1,0:T(8,128)(2,1)S(1)} %get-tuple-element.46.refs_0_, bf16[2,640,256]{2,1,0:T(8,128)(2,1)S(1)} %collective-permute-done.refs_1_, bf16[2,640,256]{2,1,0:T(8,128)(2,1)S(1)} %collective-permute-done.1.refs_2_, ...), custom_call_target="tpu_custom_call" | custom-call | flops 20000000000 | tf_op jit(solution)/shard_map/early_part/pallas_call | solution.py:37
  22.2 0.5 %collective-permute-done.4.last_ref = bf16[2,640,256]{2,1,0:T(8,128)(2,1)S(1)} collective-permute-done((bf16[2,640,256]{2,1,0:T(8,128)(2,1)S(1)}, bf16[2,640,256]{2,1,0:T(8,128)(2,1)S(1)}, u32[]{:S(2)}, u32[]{:S(2)}) %collective-permute-start.4) | collective-permute-done | bytes 655392 | tf_op jit(solution)/shard_map/ppermute | solution.py:358
  22.7 0.7 %first_node.2 = (f32[5,128,256]{2,1,0:T(8,128)S(1)}, bf16[1,640,256]{2,1,0:T(8,128)(2,1)S(1)}, f32[5,128,256]{2,1,0:T(8,128)S(1)}, bf16[1,128,256]{2,1,0:T(8,128)(2,1)S(1)}, bf16[1,128,256]{2,1,0:T(8,128)(2,1)S(1)}) custom-call(f32[5,128,256]{2,1,0:T(8,128)S(1)} %get-tuple-element.58.first_ref, f32[5,128,256]{2,1,0:T(8,128)S(1)} %get-tuple-element.59.begun_ref, ...), custom_call_target="tpu_custom_call" | custom-call | tf_op jit(solution)/shard_map/first_node/pallas_call | solution.py:37
  23.4 2.1 %collective-permute-start.7 = (bf16[1,128,256]{2,1,0:T(8,128)(2,1)S(1)}, bf16[1,128,256]{2,1,0:T(8,128)(2,1)S(1)}, u32[]{:S(2)}, u32[]{:S(2)}) collective-permute-start(bf16[1,128,256]{2,1,0:T(8,128)(2,1)S(1)} %get-tuple-element.64), channel_id=1, source_target_pairs={{0,4},{4,8},{8,12},{12,16},{16,20},{20,24},{24,28},{28,0},{1,5},{5... | collective-permute-start | bytes 196616 | tf_op jit(solution)/shard_map/ppermute | solution.py:364
  25.4 1.5 %collective-permute-start.10 = (bf16[1,640,256]{2,1,0:T(8,128)(2,1)S(1)}, bf16[1,640,256]{2,1,0:T(8,128)(2,1)S(1)}, u32[]{:S(2)}, u32[]{:S(2)}) collective-permute-start(bf16[1,640,256]{2,1,0:T(8,128)(2,1)S(1)} %get-tuple-element.61.refs_4_), channel_id=1, source_target_pairs={{0,2},{1,3},{2,0},{3,1},{4,6},{5,7},{6,4},{7,5},{8,10},{9,11},{10,... | collective-permute-start | bytes 983048 | tf_op jit(solution)/shard_map/ppermute | solution.py:361
  27.0 0.0 collective-permute-start.9
  27.0 1.4 %collective-permute-done.6.refs_2_ = bf16[2,384,256]{2,1,0:T(8,128)(2,1)S(1)} collective-permute-done((bf16[2,384,256]{2,1,0:T(8,128)(2,1)S(1)}, bf16[2,384,256]{2,1,0:T(8,128)(2,1)S(1)}, u32[]{:S(2)}, u32[]{:S(2)}) %collective-permute-start.6) | collective-permute-done | bytes 393248 | tf_op jit(solution)/shard_map/ppermute | solution.py:361
  28.4 0.0 collective-permute-start.8
  28.4 2.5 %collective-permute-done.7.lo_ref = bf16[1,128,256]{2,1,0:T(8,128)(2,1)S(1)} collective-permute-done((bf16[1,128,256]{2,1,0:T(8,128)(2,1)S(1)}, bf16[1,128,256]{2,1,0:T(8,128)(2,1)S(1)}, u32[]{:S(2)}, u32[]{:S(2)}) %collective-permute-start.7) | collective-permute-done | bytes 65568 | tf_op jit(solution)/shard_map/ppermute | solution.py:364
  30.9 0.0 collective-permute-done.5.refs_1_
  30.9 1.0 %early_part.3 = (f32[3,128,256]{2,1,0:T(8,128)S(1)}, f32[3,128,256]{2,1,0:T(8,128)S(1)}, f32[8,128,256]{2,1,0:T(8,128)}) custom-call(bf16[2,384,256]{2,1,0:T(8,128)(2,1)S(1)} %get-tuple-element.45.refs_0_, bf16[2,384,256]{2,1,0:T(8,128)(2,1)S(1)} %collective-permute-done.5.refs_1_, bf16[2,384,256]{2,1,0:T(8,128)(2,1)S(1)} %collective-permute-done.6.refs_2_, ...), custom_call_target="tpu_custom_call" | custom-call | flops 20000000000 | tf_op jit(solution)/shard_map/early_part/pallas_call | solution.py:37
  31.9 0.0 collective-permute-done.8.last_ref
  31.9 0.5 %first_node.3 = (f32[3,128,256]{2,1,0:T(8,128)S(1)}, bf16[1,384,256]{2,1,0:T(8,128)(2,1)S(1)}, f32[3,128,256]{2,1,0:T(8,128)S(1)}) custom-call(f32[3,128,256]{2,1,0:T(8,128)S(1)} %get-tuple-element.66.first_ref, f32[3,128,256]{2,1,0:T(8,128)S(1)} %get-tuple-element.67.begun_ref, bf16[2,384,256]{2,1,0:T(8,128)(2,1)S(1)} %collective-permute-done.8.last_ref, ...), custom_call_target="tpu_custom_call" | custom-call | tf_op jit(solution)/shard_map/first_node/pallas_call | solution.py:37
  32.4 1.6 %collective-permute-start.14 = (bf16[1,384,256]{2,1,0:T(8,128)(2,1)S(1)}, bf16[1,384,256]{2,1,0:T(8,128)(2,1)S(1)}, u32[]{:S(2)}, u32[]{:S(2)}) collective-permute-start(bf16[1,384,256]{2,1,0:T(8,128)(2,1)S(1)} %get-tuple-element.71.refs_0_), channel_id=1, source_target_pairs={{0,2},{1,3},{2,0},{3,1},{4,6},{5,7},{6,4},{7,5},{8,10},{9,11},{10,... | collective-permute-start | bytes 589832 | tf_op jit(solution)/shard_map/ppermute | solution.py:361
  34.0 0.0 collective-permute-start.13
  34.0 3.8 %collective-permute-start.12 = (bf16[1,128,256]{2,1,0:T(8,128)(2,1)S(1)}, bf16[1,128,256]{2,1,0:T(8,128)(2,1)S(1)}, u32[]{:S(2)}, u32[]{:S(2)}) collective-permute-start(bf16[1,128,256]{2,1,0:T(8,128)(2,1)S(1)} %get-tuple-element.79), channel_id=1, source_target_pairs={{4,0},{8,4},{12,8},{16,12},{20,16},{24,20},{28,24},{0,28},{5,1},{9... | collective-permute-start | bytes 196616 | tf_op jit(solution)/shard_map/ppermute | solution.py:367
  37.8 0.0 collective-permute-done.10.refs_6_
  37.9 0.2 collective-permute-start.11
  38.1 0.0 collective-permute-done.9.refs_5_
  38.1 1.3 %before_second.1 = (f32[8,128,256]{2,1,0:T(8,128)}, f32[2,640,256]{2,1,0:T(8,128)S(1)}, f32[5,128,256]{2,1,0:T(8,128)S(1)}, f32[3,128,256]{2,1,0:T(8,128)S(1)}) custom-call(f32[5,128,256]{2,1,0:T(8,128)S(1)} %get-tuple-element.60.refs_9_.refs_0_.new_ref, f32[3,128,256]{2,1,0:T(8,128)S(1)} %get-tuple-element.68.refs_1_.new_ref, ...), custom_call_target="tpu_custom_call", output_to_operand_aliasing={{0}: (10, {})} | custom-call | flops 20000000000 | tf_op jit(solution)/shard_map/before_second/pallas_call | solution.py:37
  39.4 0.1 collective-permute-done.11.last_ref
  39.5 0.3 whole_sums.1.sums_ref
  39.8 0.1 collective-permute-done.12.hi_ref
  39.9 0.0 collective-permute-done.14.refs_2_
  39.9 0.3 collective-permute-start.15
  40.1 0.0 collective-permute-done.13.refs_1_
  40.1 1.3 %second_first.1 = (f32[8,128,256]{2,1,0:T(8,128)}, f32[2,384,256]{2,1,0:T(8,128)S(1)}) custom-call(bf16[2,640,256]{2,1,0:T(8,128)(2,1)S(1)} %whole_sums.1.sums_ref, f32[5,128,256]{2,1,0:T(8,128)S(1)} %get-tuple-element.76.base_ref, f32[5,128,256]{2,1,0:T(8,128)S(1)} %get-tuple-element.60.refs_9_.refs_0_.new_ref, f32[1,256]{1,0:T(1,128)S(1)} %bitcast.7, ...), custom_call_target="tpu_custom_call" | custom-call | tf_op jit(solution)/shard_map/second_first/pallas_call | solution.py:37
  41.5 0.0 collective-permute-done.15.last_ref
  41.5 1.0 %second_last.1 = f32[8,128,256]{2,1,0:T(8,128)} custom-call(f32[2,384,256]{2,1,0:T(8,128)S(1)} %get-tuple-element.81.part_ref, bf16[1,384,256]{2,1,0:T(8,128)(2,1)S(1)} %collective-permute-done.15.last_ref, f32[3,128,256]{2,1,0:T(8,128)S(1)} %get-tuple-element.82.base_ref, ...), custom_call_target="tpu_custom_call", output_to_operand_aliasing={{}: (6, {})} | custom-call | tf_op jit(solution)/shard_map/second_last/pallas_call | solution.py:37
  (3 shorter events, 0.0 us)
Async XLA Ops:
  2.0 14.2 %copy-start.2 = (f32[256]{0:T(256)S(1)}, f32[256]{0:T(256)}, u32[]{:S(2)}) copy-start(f32[256]{0:T(256)} %param.10) | copy-start | bytes 3076
  2.0 18.6 %collective-permute-start.1 = (bf16[2,640,256]{2,1,0:T(8,128)(2,1)S(1)}, bf16[2,640,256]{2,1,0:T(8,128)(2,1)S(1)}, u32[]{:S(2)}, u32[]{:S(2)}) collective-permute-start(bf16[2,640,256]{2,1,0:T(8,128)(2,1)S(1)} %get-tuple-element.46.refs_0_), channel_id=1, source_target_pairs={{0,2},{1,3},{2,0},{3,1},{4,6},{5,7},{6,4},{7,5},{8,10},{9,11},{10,... | collective-permute-start | bytes 1966088 | tf_op jit(solution)/shard_map/ppermute | solution.py:361
  6.2 14.4 %copy-start = (bf16[2,1024,256]{2,1,0:T(8,128)(2,1)S(1)}, bf16[2,1024,256]{2,1,0:T(8,128)(2,1)}, u32[]{:S(2)}) copy-start(bf16[2,1024,256]{2,1,0:T(8,128)(2,1)} %k_ref.4) | copy-start | bytes 3145732
  6.2 14.4 %copy-start.1 = (f32[256]{0:T(256)S(1)}, f32[256]{0:T(256)}, u32[]{:S(2)}) copy-start(f32[256]{0:T(256)} %param.11) | copy-start | bytes 3076
  6.2 14.4 %copy-start.3 = (f32[8,128,256]{2,1,0:T(8,128)S(1)}, f32[8,128,256]{2,1,0:T(8,128)}, u32[]{:S(2)}) copy-start(f32[8,128,256]{2,1,0:T(8,128)} %refs_6_.3) | copy-start | bytes 3145732
  6.2 14.4 %collective-permute-start = (bf16[2,640,256]{2,1,0:T(8,128)(2,1)S(1)}, bf16[2,640,256]{2,1,0:T(8,128)(2,1)S(1)}, u32[]{:S(2)}, u32[]{:S(2)}) collective-permute-start(bf16[2,640,256]{2,1,0:T(8,128)(2,1)S(1)} %get-tuple-element.46.refs_0_), channel_id=1, source_target_pairs={{0,1},{1,0},{2,3},{3,2},{4,5},{5,4},{6,7},{7,6},{8,9},{9,8},{10,11... | collective-permute-start | bytes 1966088 | tf_op jit(solution)/shard_map/ppermute | solution.py:358
  6.3 8.8 %collective-permute-start.2 = (bf16[2,128,256]{2,1,0:T(8,128)(2,1)S(1)}, bf16[2,128,256]{2,1,0:T(8,128)(2,1)S(1)}, u32[]{:S(2)}, u32[]{:S(2)}) collective-permute-start(bf16[2,128,256]{2,1,0:T(8,128)(2,1)S(1)} %get-tuple-element.53), channel_id=1, source_target_pairs={{0,4},{4,8},{8,12},{12,16},{16,20},{20,24},{24,28},{28,0},{1,5},{5... | collective-permute-start | bytes 393224 | tf_op jit(solution)/shard_map/ppermute | solution.py:364
  7.8 8.4 %collective-permute-start.3 = (bf16[2,128,256]{2,1,0:T(8,128)(2,1)S(1)}, bf16[2,128,256]{2,1,0:T(8,128)(2,1)S(1)}, u32[]{:S(2)}, u32[]{:S(2)}) collective-permute-start(bf16[2,128,256]{2,1,0:T(8,128)(2,1)S(1)} %get-tuple-element.54), channel_id=1, source_target_pairs={{4,0},{8,4},{12,8},{16,12},{20,16},{24,20},{28,24},{0,28},{5,1},{9... | collective-permute-start | bytes 393224 | tf_op jit(solution)/shard_map/ppermute | solution.py:367
  11.1 17.3 %collective-permute-start.6 = (bf16[2,384,256]{2,1,0:T(8,128)(2,1)S(1)}, bf16[2,384,256]{2,1,0:T(8,128)(2,1)S(1)}, u32[]{:S(2)}, u32[]{:S(2)}) collective-permute-start(bf16[2,384,256]{2,1,0:T(8,128)(2,1)S(1)} %get-tuple-element.45.refs_0_), channel_id=1, source_target_pairs={{0,2},{1,3},{2,0},{3,1},{4,6},{5,7},{6,4},{7,5},{8,10},{9,11},{10,... | collective-permute-start | bytes 1179656 | tf_op jit(solution)/shard_map/ppermute | solution.py:361
  15.1 15.8 %collective-permute-start.5 = (bf16[2,384,256]{2,1,0:T(8,128)(2,1)S(1)}, bf16[2,384,256]{2,1,0:T(8,128)(2,1)S(1)}, u32[]{:S(2)}, u32[]{:S(2)}) collective-permute-start(bf16[2,384,256]{2,1,0:T(8,128)(2,1)S(1)} %get-tuple-element.45.refs_0_), channel_id=1, source_target_pairs={{0,1},{1,0},{2,3},{3,2},{4,5},{5,4},{6,7},{7,6},{8,9},{9,8},{10,11... | collective-permute-start | bytes 1179656 | tf_op jit(solution)/shard_map/ppermute | solution.py:358
  20.6 2.1 %collective-permute-start.4 = (bf16[2,640,256]{2,1,0:T(8,128)(2,1)S(1)}, bf16[2,640,256]{2,1,0:T(8,128)(2,1)S(1)}, u32[]{:S(2)}, u32[]{:S(2)}) collective-permute-start(bf16[2,640,256]{2,1,0:T(8,128)(2,1)S(1)} %collective-permute-done.1.refs_2_), channel_id=1, source_target_pairs={{0,1},{1,0},{2,3},{3,2},{4,5},{5,4},{6,7},{7,6},{8,9},{9,8},{10,11... | collective-permute-start | bytes 1966088 | tf_op jit(solution)/shard_map/ppermute | solution.py:358
  23.4 7.5 %collective-permute-start.7 = (bf16[1,128,256]{2,1,0:T(8,128)(2,1)S(1)}, bf16[1,128,256]{2,1,0:T(8,128)(2,1)S(1)}, u32[]{:S(2)}, u32[]{:S(2)}) collective-permute-start(bf16[1,128,256]{2,1,0:T(8,128)(2,1)S(1)} %get-tuple-element.64), channel_id=1, source_target_pairs={{0,4},{4,8},{8,12},{12,16},{16,20},{20,24},{24,28},{28,0},{1,5},{5... | collective-permute-start | bytes 196616 | tf_op jit(solution)/shard_map/ppermute | solution.py:364
  25.4 12.4 %collective-permute-start.10 = (bf16[1,640,256]{2,1,0:T(8,128)(2,1)S(1)}, bf16[1,640,256]{2,1,0:T(8,128)(2,1)S(1)}, u32[]{:S(2)}, u32[]{:S(2)}) collective-permute-start(bf16[1,640,256]{2,1,0:T(8,128)(2,1)S(1)} %get-tuple-element.61.refs_4_), channel_id=1, source_target_pairs={{0,2},{1,3},{2,0},{3,1},{4,6},{5,7},{6,4},{7,5},{8,10},{9,11},{10,... | collective-permute-start | bytes 983048 | tf_op jit(solution)/shard_map/ppermute | solution.py:361
  27.0 11.1 %collective-permute-start.9 = (bf16[1,640,256]{2,1,0:T(8,128)(2,1)S(1)}, bf16[1,640,256]{2,1,0:T(8,128)(2,1)S(1)}, u32[]{:S(2)}, u32[]{:S(2)}) collective-permute-start(bf16[1,640,256]{2,1,0:T(8,128)(2,1)S(1)} %get-tuple-element.61.refs_4_), channel_id=1, source_target_pairs={{0,1},{1,0},{2,3},{3,2},{4,5},{5,4},{6,7},{7,6},{8,9},{9,8},{10,11... | collective-permute-start | bytes 983048 | tf_op jit(solution)/shard_map/ppermute | solution.py:358
  28.4 3.5 %collective-permute-start.8 = (bf16[2,384,256]{2,1,0:T(8,128)(2,1)S(1)}, bf16[2,384,256]{2,1,0:T(8,128)(2,1)S(1)}, u32[]{:S(2)}, u32[]{:S(2)}) collective-permute-start(bf16[2,384,256]{2,1,0:T(8,128)(2,1)S(1)} %collective-permute-done.6.refs_2_), channel_id=1, source_target_pairs={{0,1},{1,0},{2,3},{3,2},{4,5},{5,4},{6,7},{7,6},{8,9},{9,8},{10,11... | collective-permute-start | bytes 1179656 | tf_op jit(solution)/shard_map/ppermute | solution.py:358
  32.4 7.5 %collective-permute-start.14 = (bf16[1,384,256]{2,1,0:T(8,128)(2,1)S(1)}, bf16[1,384,256]{2,1,0:T(8,128)(2,1)S(1)}, u32[]{:S(2)}, u32[]{:S(2)}) collective-permute-start(bf16[1,384,256]{2,1,0:T(8,128)(2,1)S(1)} %get-tuple-element.71.refs_0_), channel_id=1, source_target_pairs={{0,2},{1,3},{2,0},{3,1},{4,6},{5,7},{6,4},{7,5},{8,10},{9,11},{10,... | collective-permute-start | bytes 589832 | tf_op jit(solution)/shard_map/ppermute | solution.py:361
  34.0 6.1 %collective-permute-start.13 = (bf16[1,384,256]{2,1,0:T(8,128)(2,1)S(1)}, bf16[1,384,256]{2,1,0:T(8,128)(2,1)S(1)}, u32[]{:S(2)}, u32[]{:S(2)}) collective-permute-start(bf16[1,384,256]{2,1,0:T(8,128)(2,1)S(1)} %get-tuple-element.71.refs_0_), channel_id=1, source_target_pairs={{0,1},{1,0},{2,3},{3,2},{4,5},{5,4},{6,7},{7,6},{8,9},{9,8},{10,11... | collective-permute-start | bytes 589832 | tf_op jit(solution)/shard_map/ppermute | solution.py:358
  34.0 5.8 %collective-permute-start.12 = (bf16[1,128,256]{2,1,0:T(8,128)(2,1)S(1)}, bf16[1,128,256]{2,1,0:T(8,128)(2,1)S(1)}, u32[]{:S(2)}, u32[]{:S(2)}) collective-permute-start(bf16[1,128,256]{2,1,0:T(8,128)(2,1)S(1)} %get-tuple-element.79), channel_id=1, source_target_pairs={{4,0},{8,4},{12,8},{16,12},{20,16},{24,20},{28,24},{0,28},{5,1},{9... | collective-permute-start | bytes 196616 | tf_op jit(solution)/shard_map/ppermute | solution.py:367
  37.9 1.6 %collective-permute-start.11 = (bf16[1,640,256]{2,1,0:T(8,128)(2,1)S(1)}, bf16[1,640,256]{2,1,0:T(8,128)(2,1)S(1)}, u32[]{:S(2)}, u32[]{:S(2)}) collective-permute-start(bf16[1,640,256]{2,1,0:T(8,128)(2,1)S(1)} %collective-permute-done.10.refs_6_), channel_id=1, source_target_pairs={{0,1},{1,0},{2,3},{3,2},{4,5},{5,4},{6,7},{7,6},{8,9},{9,8},{10,11... | collective-permute-start | bytes 983048 | tf_op jit(solution)/shard_map/ppermute | solution.py:358
  39.9 1.6 %collective-permute-start.15 = (bf16[1,384,256]{2,1,0:T(8,128)(2,1)S(1)}, bf16[1,384,256]{2,1,0:T(8,128)(2,1)S(1)}, u32[]{:S(2)}, u32[]{:S(2)}) collective-permute-start(bf16[1,384,256]{2,1,0:T(8,128)(2,1)S(1)} %collective-permute-done.14.refs_2_), channel_id=1, source_target_pairs={{0,1},{1,0},{2,3},{3,2},{4,5},{5,4},{6,7},{7,6},{8,9},{9,8},{10,11... | collective-permute-start | bytes 589832 | tf_op jit(solution)/shard_map/ppermute | solution.py:358

commit v14 on v13

--- a/solution.py
+++ b/solution.py
@@ -148,19 +148,17 @@
             ]
         for copy in copies:
             copy.start()
-        first_ref, rest_ref = refs[:2] if new is None else refs[1:3]
+        part_ref, first_ref, rest_ref = refs[:3] if new is None else refs[1:4]
         me = lax.axis_index("trait")
         values = [r[...].reshape(2 * rows, owned) for r in block_refs]
-        compete, mutate = (blocks_dot(values, k_ref, k, [me ^ j for j in range(count)]) for k in range(2))
+        for k in range(2):
+            part_ref[k] = blocks_dot(values, k_ref, k, [me ^ j for j in range(count)])
         death = d_ref[...]
         inv_one = 1.0 / (1.0 + FIRST * death)
         inv_two = 1.0 / (1.0 + SECOND * death)
         for i, x in enumerate(cells):
             cores = (one_ref[i], two_ref[i])
-            e = []
-            for f in range(2):
-                at = slice(f * rows + i * ycount, f * rows + (i + 1) * ycount)
-                e.append(base_ref[f, i] - cores[f] * compete[at] + mutate[at])
+            e = (base_ref[0, i], base_ref[1, i])
             full_one = e[0] - death * cores[0]
             full_two = e[1] - death * cores[1]
             first = (
@@ -176,31 +174,32 @@
             copy.wait()
 
     args = [*blocks, base, one, two, initial, kernels, death]
-    outs = [pltpu.VMEM((len(cells), ycount, owned), F32)] * 2
+    outs = [pltpu.VMEM((2, 2 * rows, owned), F32)] + [pltpu.VMEM((len(cells), ycount, owned), F32)] * 2
     if new is None:
         return call(body, "early_part", args, outs, gflop=20.0)
     outs.append(jax.ShapeDtypeStruct((xcount, ycount, owned), F32))
     return call(
         body, "early_part", [*args, new], outs, scratch=[pltpu.SemaphoreType.DMA((len(runs_of(new_cells)),))],
-        out_specs=[SPEC, SPEC, ANYWHERE], gflop=20.0,
-    )
-
-
-def first_node(first, rest, last, one, two, kernels, death, cells, xcount, with_faces):
+        out_specs=[SPEC, SPEC, SPEC, ANYWHERE], gflop=20.0,
+    )
+
+
+def first_node(part, first, rest, last, one, two, kernels, death, cells, xcount, with_faces):
     _, ycount, owned = one.shape
     rows = len(cells) * ycount
 
-    def body(first_ref, begun_ref, last_ref, one_ref, two_ref, k_ref, d_ref, new_ref, rounded_ref, rest_ref, *face_refs):
+    def body(part_ref, first_ref, begun_ref, last_ref, one_ref, two_ref, k_ref, d_ref, *outs):
+        new_ref, rounded_ref, rest_ref, *face_refs = outs
         me = lax.axis_index("trait")
         values = [last_ref[...].reshape(2 * rows, owned)]
-        compete, mutate = (blocks_dot(values, k_ref, k, [me ^ 3]) for k in range(2))
+        compete, mutate = ((part_ref[k] + blocks_dot(values, k_ref, k, [me ^ 3])).astype(BF16) for k in range(2))
         inv_one = STEP_SIZE / (1.0 + FIRST * d_ref[...])
         inv_two = 1.0 / (1.0 + SECOND * d_ref[...])
         for i, x in enumerate(cells):
             e = []
             for f, ref in enumerate((one_ref, two_ref)):
                 at = slice(f * rows + i * ycount, f * rows + (i + 1) * ycount)
-                e.append(mutate[at] - ref[i] * compete[at])
+                e.append(mutate[at].astype(F32) - ref[i] * compete[at].astype(F32))
             more = (5.0 / 12.0 * e[0] - 1.0 / 12.0 * e[1]) * inv_one
             new = first_ref[i] + more
             new_ref[i] = new
@@ -219,7 +218,7 @@
     ]
     if with_faces:
         outs += [pltpu.VMEM((1, ycount, owned), BF16)] * 2
-    return call(body, "first_node", [first, rest, last, one, two, kernels, death], outs)
+    return call(body, "first_node", [part, first, rest, last, one, two, kernels, death], outs)
 
 
 def before_second(news, rests, growth, death, begun, blocks, kernels, chunks):
@@ -377,9 +376,9 @@
     sib_b = to_sibling(own_b)
     far_a = after(far_a, base_a)
     farsib_a = to_sibling(far_a)
-    first_a, rest_a = early_part([own_a, sib_a, far_a], base_a, one_a, two_a, initial, kernels, death, chunks[0])
+    part_a, first_a, rest_a = early_part([own_a, sib_a, far_a], base_a, one_a, two_a, initial, kernels, death, chunks[0])
     new_a, rounded_a, rest_a, new_head, new_tail = first_node(
-        first_a, rest_a, farsib_a, one_a, two_a, kernels, death, chunks[0], xcount, True
+        part_a, first_a, rest_a, farsib_a, one_a, two_a, kernels, death, chunks[0], xcount, True
     )
     nfar_a = to_far(rounded_a)
     nsib_a = to_sibling(rounded_a)
@@ -387,11 +386,11 @@
     new_lo = from_below(new_tail)
     far_b = after(far_b, rounded_a)
     farsib_b = to_sibling(far_b)
-    first_b, rest_b, new_one = early_part(
+    part_b, first_b, rest_b, new_one = early_part(
         [own_b, sib_b, far_b], base_b, one_b, two_b, initial, after(kernels, new_lo), death, chunks[1], new_a, chunks[0]
     )
     new_b, rounded_b, rest_b = first_node(
-        first_b, rest_b, farsib_b, one_b, two_b, kernels, death, chunks[1], xcount, False
+        part_b, first_b, rest_b, farsib_b, one_b, two_b, kernels, death, chunks[1], xcount, False
     )
     nfar_b = to_far(rounded_b)
     nsib_b = to_sibling(rounded_b)

time: 42.6 us -> 42.7 us (level)
  Pallas kernels: 11.1 us -> 11.6 us
    pallas_call x11, Pallas kernels: 11.1 us -> 11.6 us  [call(): pl.pallas_call(body, out_shape=outs, in_specs=specs, out_specs=out_specs...]
    ppermute x2, waiting for transfers between devices: 6.12 us -> 6.57 us  [from_below(): lax.ppermute(tail, 'gx', [(i, (i + 1) % gcount) for i in range(gcount)])]
  transfers between devices with their start and end apart: 16 -> 16, of which waited for: 8 -> 8; matrix products, arithmetic and copies ran while one was open for 0% -> 0% of each run, Pallas kernels for 21% -> 22%
where the time goes in v14:
time: 42.7 us; the launch traced here: 42.5 us
  starting transfers between devices  17.5 us (41%)
  waiting for transfers between devices  12.7 us (30%)
  Pallas kernels  11.6 us (27%)
  between operations  0.79 us (2%)
    pallas_call x11, Pallas kernels, call(): pl.pallas_call(body, out_shape=outs, in_specs=specs, out_specs=out_specs...  11.6 us
    ppermute x2, starting transfers between devices, from_above(): lax.ppermute(head, 'gx', [((i + 1) % gcount, i) for i in range(gcount)])  6.73 us
    ppermute x2, waiting for transfers between devices, from_below(): lax.ppermute(tail, 'gx', [(i, (i + 1) % gcount) for i in range(gcount)])  6.57 us
    ppermute x4, starting transfers between devices, to_far(): return lax.ppermute(v, 'trait', [(i, i ^ 2) for i in range(traits)])  6.53 us
    ppermute x4, waiting for transfers between devices, to_far(): return lax.ppermute(v, 'trait', [(i, i ^ 2) for i in range(traits)])  4.53 us
    ppermute x2, starting transfers between devices, from_below(): lax.ppermute(tail, 'gx', [(i, (i + 1) % gcount) for i in range(gcount)])  3.62 us
    ppermute x2, waiting for transfers between devices, from_above(): lax.ppermute(head, 'gx', [((i + 1) % gcount, i) for i in range(gcount)])  1.18 us
  transfers between devices with their start and end apart: 16, of which 8 were waited for; matrix products, arithmetic and copies ran while one was open for 0% of the time, Pallas kernels for 22%

profile of v14, /device:TPU:0, one launch (start us, length us, event | category | flops | bytes accessed | tf_op | source)
XLA Modules:
  0.0 42.5 jit_solution(15268974006132277381)
XLA Ops:
  0.6 1.3 %load_chunk.2 = (f32[5,128,256]{2,1,0:T(8,128)S(1)}, f32[5,128,256]{2,1,0:T(8,128)S(1)}, bf16[2,640,256]{2,1,0:T(8,128)(2,1)S(1)}, bf16[2,128,256]{2,1,0:T(8,128)(2,1)S(1)}, bf16[2,128,256]{2,1,0:T(8,128)(2,1)S(1)}) custom-call(f32[8,128,256]{2,1,0:T(8,128)} %refs_0_.2, f32[8,128,256]{2,1,0:T(8,128)} %refs_1_.3), custom_call_target="tpu_custom_call" | custom-call | tf_op jit(solution)/shard_map/load_chunk/pallas_call | solution.py:37
  2.0 0.0 copy-start.2
  2.0 3.0 %collective-permute-start.1 = (bf16[2,640,256]{2,1,0:T(8,128)(2,1)S(1)}, bf16[2,640,256]{2,1,0:T(8,128)(2,1)S(1)}, u32[]{:S(2)}, u32[]{:S(2)}) collective-permute-start(bf16[2,640,256]{2,1,0:T(8,128)(2,1)S(1)} %get-tuple-element.48.refs_0_), channel_id=1, source_target_pairs={{0,2},{1,3},{2,0},{3,1},{4,6},{5,7},{6,4},{7,5},{8,10},{9,11},{10,... | collective-permute-start | bytes 1966088 | tf_op jit(solution)/shard_map/ppermute | solution.py:360
  5.0 1.1 %load_chunk.3 = (f32[3,128,256]{2,1,0:T(8,128)S(1)}, f32[3,128,256]{2,1,0:T(8,128)S(1)}, bf16[2,384,256]{2,1,0:T(8,128)(2,1)S(1)}) custom-call(f32[8,128,256]{2,1,0:T(8,128)} %refs_0_.2, f32[8,128,256]{2,1,0:T(8,128)} %refs_1_.3), custom_call_target="tpu_custom_call" | custom-call | tf_op jit(solution)/shard_map/load_chunk/pallas_call | solution.py:37
  6.2 0.0 copy-start
  6.2 0.0 copy-start.1
  6.2 0.0 copy-start.3
  6.2 0.1 collective-permute-start
  6.3 1.5 %collective-permute-start.2 = (bf16[2,128,256]{2,1,0:T(8,128)(2,1)S(1)}, bf16[2,128,256]{2,1,0:T(8,128)(2,1)S(1)}, u32[]{:S(2)}, u32[]{:S(2)}) collective-permute-start(bf16[2,128,256]{2,1,0:T(8,128)(2,1)S(1)} %get-tuple-element.55), channel_id=1, source_target_pairs={{0,4},{4,8},{8,12},{12,16},{16,20},{20,24},{24,28},{28,0},{1,5},{5... | collective-permute-start | bytes 393224 | tf_op jit(solution)/shard_map/ppermute | solution.py:363
  7.8 3.2 %collective-permute-start.3 = (bf16[2,128,256]{2,1,0:T(8,128)(2,1)S(1)}, bf16[2,128,256]{2,1,0:T(8,128)(2,1)S(1)}, u32[]{:S(2)}, u32[]{:S(2)}) collective-permute-start(bf16[2,128,256]{2,1,0:T(8,128)(2,1)S(1)} %get-tuple-element.56), channel_id=1, source_target_pairs={{4,0},{8,4},{12,8},{16,12},{20,16},{24,20},{28,24},{0,28},{5,1},{9... | collective-permute-start | bytes 393224 | tf_op jit(solution)/shard_map/ppermute | solution.py:366
  11.1 0.4 collective-permute-start.6
  11.4 3.6 %collective-permute-done.2.refs_4_ = bf16[2,128,256]{2,1,0:T(8,128)(2,1)S(1)} collective-permute-done((bf16[2,128,256]{2,1,0:T(8,128)(2,1)S(1)}, bf16[2,128,256]{2,1,0:T(8,128)(2,1)S(1)}, u32[]{:S(2)}, u32[]{:S(2)}) %collective-permute-start.2) | collective-permute-done | bytes 131104 | tf_op jit(solution)/shard_map/ppermute | solution.py:363
  15.1 0.0 collective-permute-start.5
  15.1 1.1 %collective-permute-done.3.refs_5_ = bf16[2,128,256]{2,1,0:T(8,128)(2,1)S(1)} collective-permute-done((bf16[2,128,256]{2,1,0:T(8,128)(2,1)S(1)}, bf16[2,128,256]{2,1,0:T(8,128)(2,1)S(1)}, u32[]{:S(2)}, u32[]{:S(2)}) %collective-permute-start.3) | collective-permute-done | bytes 131104 | tf_op jit(solution)/shard_map/ppermute | solution.py:366
  16.2 0.0 copy-done.2
  16.2 0.9 %before_first.1 = (f32[2,5,128,256]{3,2,1,0:T(8,128)S(1)}, f32[2,3,128,256]{3,2,1,0:T(8,128)S(1)}) custom-call(f32[5,128,256]{2,1,0:T(8,128)S(1)} %get-tuple-element.49.refs_0_.refs_4_.one_ref, f32[3,128,256]{2,1,0:T(8,128)S(1)} %get-tuple-element.50.refs_1_.refs_4_.one_ref, f32[5,128,256]{2,1,0:T(8,128)S(1)} %get-tuple-element.51.refs_2_.refs_5_.two_ref, ...), custom_call_target="tpu_custom_call" | custom-call | tf_op jit(solution)/shard_map/before_first/pallas_call | solution.py:37
  17.1 3.4 %collective-permute-done.1.refs_2_ = bf16[2,640,256]{2,1,0:T(8,128)(2,1)S(1)} collective-permute-done((bf16[2,640,256]{2,1,0:T(8,128)(2,1)S(1)}, bf16[2,640,256]{2,1,0:T(8,128)(2,1)S(1)}, u32[]{:S(2)}, u32[]{:S(2)}) %collective-permute-start.1) | collective-permute-done | bytes 655392 | tf_op jit(solution)/shard_map/ppermute | solution.py:360
  20.6 0.0 collective-permute-start.4
  20.6 0.0 collective-permute-done.refs_1_
  20.6 1.8 %early_part.2 = (f32[2,1280,256]{2,1,0:T(8,128)S(1)}, f32[5,128,256]{2,1,0:T(8,128)S(1)}, f32[5,128,256]{2,1,0:T(8,128)S(1)}) custom-call(bf16[2,640,256]{2,1,0:T(8,128)(2,1)S(1)} %get-tuple-element.48.refs_0_, bf16[2,640,256]{2,1,0:T(8,128)(2,1)S(1)} %collective-permute-done.refs_1_, bf16[2,640,256]{2,1,0:T(8,128)(2,1)S(1)} %collective-permute-done.1.refs_2_, ...), custom_call_target="tpu_custom_call" | custom-call | flops 20000000000 | tf_op jit(solution)/shard_map/early_part/pallas_call | solution.py:37
  22.4 0.3 collective-permute-done.4.last_ref
  22.7 0.8 %first_node.2 = (f32[5,128,256]{2,1,0:T(8,128)S(1)}, bf16[1,640,256]{2,1,0:T(8,128)(2,1)S(1)}, f32[5,128,256]{2,1,0:T(8,128)S(1)}, bf16[1,128,256]{2,1,0:T(8,128)(2,1)S(1)}, bf16[1,128,256]{2,1,0:T(8,128)(2,1)S(1)}) custom-call(f32[2,1280,256]{2,1,0:T(8,128)S(1)} %get-tuple-element.60.part_ref, f32[5,128,256]{2,1,0:T(8,128)S(1)} %get-tuple-element.61.first_ref, ...), custom_call_target="tpu_custom_call" | custom-call | tf_op jit(solution)/shard_map/first_node/pallas_call | solution.py:37
  23.5 2.1 %collective-permute-start.7 = (bf16[1,128,256]{2,1,0:T(8,128)(2,1)S(1)}, bf16[1,128,256]{2,1,0:T(8,128)(2,1)S(1)}, u32[]{:S(2)}, u32[]{:S(2)}) collective-permute-start(bf16[1,128,256]{2,1,0:T(8,128)(2,1)S(1)} %get-tuple-element.67), channel_id=1, source_target_pairs={{0,4},{4,8},{8,12},{12,16},{16,20},{20,24},{24,28},{28,0},{1,5},{5... | collective-permute-start | bytes 196616 | tf_op jit(solution)/shard_map/ppermute | solution.py:363
  25.6 1.5 %collective-permute-start.10 = (bf16[1,640,256]{2,1,0:T(8,128)(2,1)S(1)}, bf16[1,640,256]{2,1,0:T(8,128)(2,1)S(1)}, u32[]{:S(2)}, u32[]{:S(2)}) collective-permute-start(bf16[1,640,256]{2,1,0:T(8,128)(2,1)S(1)} %get-tuple-element.64.refs_4_), channel_id=1, source_target_pairs={{0,2},{1,3},{2,0},{3,1},{4,6},{5,7},{6,4},{7,5},{8,10},{9,11},{10,... | collective-permute-start | bytes 983048 | tf_op jit(solution)/shard_map/ppermute | solution.py:360
  27.1 0.0 collective-permute-start.9
  27.1 1.1 %collective-permute-done.6.refs_2_ = bf16[2,384,256]{2,1,0:T(8,128)(2,1)S(1)} collective-permute-done((bf16[2,384,256]{2,1,0:T(8,128)(2,1)S(1)}, bf16[2,384,256]{2,1,0:T(8,128)(2,1)S(1)}, u32[]{:S(2)}, u32[]{:S(2)}) %collective-permute-start.6) | collective-permute-done | bytes 393248 | tf_op jit(solution)/shard_map/ppermute | solution.py:360
  28.2 0.0 collective-permute-start.8
  28.2 3.0 %collective-permute-done.7.lo_ref = bf16[1,128,256]{2,1,0:T(8,128)(2,1)S(1)} collective-permute-done((bf16[1,128,256]{2,1,0:T(8,128)(2,1)S(1)}, bf16[1,128,256]{2,1,0:T(8,128)(2,1)S(1)}, u32[]{:S(2)}, u32[]{:S(2)}) %collective-permute-start.7) | collective-permute-done | bytes 65568 | tf_op jit(solution)/shard_map/ppermute | solution.py:363
  31.1 0.0 collective-permute-done.5.refs_1_
  31.1 1.1 %early_part.3 = (f32[2,768,256]{2,1,0:T(8,128)S(1)}, f32[3,128,256]{2,1,0:T(8,128)S(1)}, f32[3,128,256]{2,1,0:T(8,128)S(1)}, f32[8,128,256]{2,1,0:T(8,128)}) custom-call(bf16[2,384,256]{2,1,0:T(8,128)(2,1)S(1)} %get-tuple-element.47.refs_0_, bf16[2,384,256]{2,1,0:T(8,128)(2,1)S(1)} %collective-permute-done.5.refs_1_, ...), custom_call_target="tpu_custom_call" | custom-call | flops 20000000000 | tf_op jit(solution)/shard_map/early_part/pallas_call | solution.py:37
  32.3 0.0 collective-permute-done.8.last_ref
  32.3 0.6 %first_node.3 = (f32[3,128,256]{2,1,0:T(8,128)S(1)}, bf16[1,384,256]{2,1,0:T(8,128)(2,1)S(1)}, f32[3,128,256]{2,1,0:T(8,128)S(1)}) custom-call(f32[2,768,256]{2,1,0:T(8,128)S(1)} %get-tuple-element.69.part_ref, f32[3,128,256]{2,1,0:T(8,128)S(1)} %get-tuple-element.70.first_ref, f32[3,128,256]{2,1,0:T(8,128)S(1)} %get-tuple-element.71.begun_ref, ...), custom_call_target="tpu_custom_call" | custom-call | tf_op jit(solution)/shard_map/first_node/pallas_call | solution.py:37
  32.8 1.6 %collective-permute-start.14 = (bf16[1,384,256]{2,1,0:T(8,128)(2,1)S(1)}, bf16[1,384,256]{2,1,0:T(8,128)(2,1)S(1)}, u32[]{:S(2)}, u32[]{:S(2)}) collective-permute-start(bf16[1,384,256]{2,1,0:T(8,128)(2,1)S(1)} %get-tuple-element.75.refs_0_), channel_id=1, source_target_pairs={{0,2},{1,3},{2,0},{3,1},{4,6},{5,7},{6,4},{7,5},{8,10},{9,11},{10,... | collective-permute-start | bytes 589832 | tf_op jit(solution)/shard_map/ppermute | solution.py:360
  34.4 0.0 collective-permute-start.13
  34.4 3.5 %collective-permute-start.12 = (bf16[1,128,256]{2,1,0:T(8,128)(2,1)S(1)}, bf16[1,128,256]{2,1,0:T(8,128)(2,1)S(1)}, u32[]{:S(2)}, u32[]{:S(2)}) collective-permute-start(bf16[1,128,256]{2,1,0:T(8,128)(2,1)S(1)} %get-tuple-element.83), channel_id=1, source_target_pairs={{4,0},{8,4},{12,8},{16,12},{20,16},{24,20},{28,24},{0,28},{5,1},{9... | collective-permute-start | bytes 196616 | tf_op jit(solution)/shard_map/ppermute | solution.py:366
  37.9 0.0 collective-permute-done.10.refs_6_
  37.9 0.2 collective-permute-start.11
  38.2 0.0 collective-permute-done.9.refs_5_
  38.2 1.3 %before_second.1 = (f32[8,128,256]{2,1,0:T(8,128)}, f32[2,640,256]{2,1,0:T(8,128)S(1)}, f32[5,128,256]{2,1,0:T(8,128)S(1)}, f32[3,128,256]{2,1,0:T(8,128)S(1)}) custom-call(f32[5,128,256]{2,1,0:T(8,128)S(1)} %get-tuple-element.63.refs_9_.refs_0_.new_ref, f32[3,128,256]{2,1,0:T(8,128)S(1)} %get-tuple-element.72.refs_1_.new_ref, ...), custom_call_target="tpu_custom_call", output_to_operand_aliasing={{0}: (10, {})} | custom-call | flops 20000000000 | tf_op jit(solution)/shard_map/before_second/pallas_call | solution.py:37
  39.5 0.1 collective-permute-done.11.last_ref
  39.6 0.3 whole_sums.1.sums_ref
  39.9 0.1 collective-permute-done.12.hi_ref
  40.0 0.0 collective-permute-done.14.refs_2_
  40.0 0.3 collective-permute-start.15
  40.2 0.0 collective-permute-done.13.refs_1_
  40.2 1.3 %second_first.1 = (f32[8,128,256]{2,1,0:T(8,128)}, f32[2,384,256]{2,1,0:T(8,128)S(1)}) custom-call(bf16[2,640,256]{2,1,0:T(8,128)(2,1)S(1)} %whole_sums.1.sums_ref, f32[5,128,256]{2,1,0:T(8,128)S(1)} %get-tuple-element.80.base_ref, f32[5,128,256]{2,1,0:T(8,128)S(1)} %get-tuple-element.63.refs_9_.refs_0_.new_ref, f32[1,256]{1,0:T(1,128)S(1)} %bitcast.7, ...), custom_call_target="tpu_custom_call" | custom-call | tf_op jit(solution)/shard_map/second_first/pallas_call | solution.py:37
  41.5 0.0 collective-permute-done.15.last_ref
  41.6 1.0 %second_last.1 = f32[8,128,256]{2,1,0:T(8,128)} custom-call(f32[2,384,256]{2,1,0:T(8,128)S(1)} %get-tuple-element.85.part_ref, bf16[1,384,256]{2,1,0:T(8,128)(2,1)S(1)} %collective-permute-done.15.last_ref, f32[3,128,256]{2,1,0:T(8,128)S(1)} %get-tuple-element.86.base_ref, ...), custom_call_target="tpu_custom_call", output_to_operand_aliasing={{}: (6, {})} | custom-call | tf_op jit(solution)/shard_map/second_last/pallas_call | solution.py:37
  (3 shorter events, 0.0 us)
Async XLA Ops:
  2.0 14.2 %copy-start.2 = (f32[256]{0:T(256)S(1)}, f32[256]{0:T(256)}, u32[]{:S(2)}) copy-start(f32[256]{0:T(256)} %param.10) | copy-start | bytes 3076
  2.0 18.6 %collective-permute-start.1 = (bf16[2,640,256]{2,1,0:T(8,128)(2,1)S(1)}, bf16[2,640,256]{2,1,0:T(8,128)(2,1)S(1)}, u32[]{:S(2)}, u32[]{:S(2)}) collective-permute-start(bf16[2,640,256]{2,1,0:T(8,128)(2,1)S(1)} %get-tuple-element.48.refs_0_), channel_id=1, source_target_pairs={{0,2},{1,3},{2,0},{3,1},{4,6},{5,7},{6,4},{7,5},{8,10},{9,11},{10,... | collective-permute-start | bytes 1966088 | tf_op jit(solution)/shard_map/ppermute | solution.py:360
  6.2 14.4 %copy-start = (bf16[2,1024,256]{2,1,0:T(8,128)(2,1)S(1)}, bf16[2,1024,256]{2,1,0:T(8,128)(2,1)}, u32[]{:S(2)}) copy-start(bf16[2,1024,256]{2,1,0:T(8,128)(2,1)} %k_ref.4) | copy-start | bytes 3145732
  6.2 14.4 %copy-start.1 = (f32[256]{0:T(256)S(1)}, f32[256]{0:T(256)}, u32[]{:S(2)}) copy-start(f32[256]{0:T(256)} %param.11) | copy-start | bytes 3076
  6.2 14.4 %copy-start.3 = (f32[8,128,256]{2,1,0:T(8,128)S(1)}, f32[8,128,256]{2,1,0:T(8,128)}, u32[]{:S(2)}) copy-start(f32[8,128,256]{2,1,0:T(8,128)} %refs_6_.3) | copy-start | bytes 3145732
  6.2 14.4 %collective-permute-start = (bf16[2,640,256]{2,1,0:T(8,128)(2,1)S(1)}, bf16[2,640,256]{2,1,0:T(8,128)(2,1)S(1)}, u32[]{:S(2)}, u32[]{:S(2)}) collective-permute-start(bf16[2,640,256]{2,1,0:T(8,128)(2,1)S(1)} %get-tuple-element.48.refs_0_), channel_id=1, source_target_pairs={{0,1},{1,0},{2,3},{3,2},{4,5},{5,4},{6,7},{7,6},{8,9},{9,8},{10,11... | collective-permute-start | bytes 1966088 | tf_op jit(solution)/shard_map/ppermute | solution.py:357
  6.3 8.8 %collective-permute-start.2 = (bf16[2,128,256]{2,1,0:T(8,128)(2,1)S(1)}, bf16[2,128,256]{2,1,0:T(8,128)(2,1)S(1)}, u32[]{:S(2)}, u32[]{:S(2)}) collective-permute-start(bf16[2,128,256]{2,1,0:T(8,128)(2,1)S(1)} %get-tuple-element.55), channel_id=1, source_target_pairs={{0,4},{4,8},{8,12},{12,16},{16,20},{20,24},{24,28},{28,0},{1,5},{5... | collective-permute-start | bytes 393224 | tf_op jit(solution)/shard_map/ppermute | solution.py:363
  7.8 8.4 %collective-permute-start.3 = (bf16[2,128,256]{2,1,0:T(8,128)(2,1)S(1)}, bf16[2,128,256]{2,1,0:T(8,128)(2,1)S(1)}, u32[]{:S(2)}, u32[]{:S(2)}) collective-permute-start(bf16[2,128,256]{2,1,0:T(8,128)(2,1)S(1)} %get-tuple-element.56), channel_id=1, source_target_pairs={{4,0},{8,4},{12,8},{16,12},{20,16},{24,20},{28,24},{0,28},{5,1},{9... | collective-permute-start | bytes 393224 | tf_op jit(solution)/shard_map/ppermute | solution.py:366
  11.1 17.1 %collective-permute-start.6 = (bf16[2,384,256]{2,1,0:T(8,128)(2,1)S(1)}, bf16[2,384,256]{2,1,0:T(8,128)(2,1)S(1)}, u32[]{:S(2)}, u32[]{:S(2)}) collective-permute-start(bf16[2,384,256]{2,1,0:T(8,128)(2,1)S(1)} %get-tuple-element.47.refs_0_), channel_id=1, source_target_pairs={{0,2},{1,3},{2,0},{3,1},{4,6},{5,7},{6,4},{7,5},{8,10},{9,11},{10,... | collective-permute-start | bytes 1179656 | tf_op jit(solution)/shard_map/ppermute | solution.py:360
  15.1 16.1 %collective-permute-start.5 = (bf16[2,384,256]{2,1,0:T(8,128)(2,1)S(1)}, bf16[2,384,256]{2,1,0:T(8,128)(2,1)S(1)}, u32[]{:S(2)}, u32[]{:S(2)}) collective-permute-start(bf16[2,384,256]{2,1,0:T(8,128)(2,1)S(1)} %get-tuple-element.47.refs_0_), channel_id=1, source_target_pairs={{0,1},{1,0},{2,3},{3,2},{4,5},{5,4},{6,7},{7,6},{8,9},{9,8},{10,11... | collective-permute-start | bytes 1179656 | tf_op jit(solution)/shard_map/ppermute | solution.py:357
  20.6 2.1 %collective-permute-start.4 = (bf16[2,640,256]{2,1,0:T(8,128)(2,1)S(1)}, bf16[2,640,256]{2,1,0:T(8,128)(2,1)S(1)}, u32[]{:S(2)}, u32[]{:S(2)}) collective-permute-start(bf16[2,640,256]{2,1,0:T(8,128)(2,1)S(1)} %collective-permute-done.1.refs_2_), channel_id=1, source_target_pairs={{0,1},{1,0},{2,3},{3,2},{4,5},{5,4},{6,7},{7,6},{8,9},{9,8},{10,11... | collective-permute-start | bytes 1966088 | tf_op jit(solution)/shard_map/ppermute | solution.py:357
  23.5 7.6 %collective-permute-start.7 = (bf16[1,128,256]{2,1,0:T(8,128)(2,1)S(1)}, bf16[1,128,256]{2,1,0:T(8,128)(2,1)S(1)}, u32[]{:S(2)}, u32[]{:S(2)}) collective-permute-start(bf16[1,128,256]{2,1,0:T(8,128)(2,1)S(1)} %get-tuple-element.67), channel_id=1, source_target_pairs={{0,4},{4,8},{8,12},{12,16},{16,20},{20,24},{24,28},{28,0},{1,5},{5... | collective-permute-start | bytes 196616 | tf_op jit(solution)/shard_map/ppermute | solution.py:363
  25.6 12.4 %collective-permute-start.10 = (bf16[1,640,256]{2,1,0:T(8,128)(2,1)S(1)}, bf16[1,640,256]{2,1,0:T(8,128)(2,1)S(1)}, u32[]{:S(2)}, u32[]{:S(2)}) collective-permute-start(bf16[1,640,256]{2,1,0:T(8,128)(2,1)S(1)} %get-tuple-element.64.refs_4_), channel_id=1, source_target_pairs={{0,2},{1,3},{2,0},{3,1},{4,6},{5,7},{6,4},{7,5},{8,10},{9,11},{10,... | collective-permute-start | bytes 983048 | tf_op jit(solution)/shard_map/ppermute | solution.py:360
  27.1 11.1 %collective-permute-start.9 = (bf16[1,640,256]{2,1,0:T(8,128)(2,1)S(1)}, bf16[1,640,256]{2,1,0:T(8,128)(2,1)S(1)}, u32[]{:S(2)}, u32[]{:S(2)}) collective-permute-start(bf16[1,640,256]{2,1,0:T(8,128)(2,1)S(1)} %get-tuple-element.64.refs_4_), channel_id=1, source_target_pairs={{0,1},{1,0},{2,3},{3,2},{4,5},{5,4},{6,7},{7,6},{8,9},{9,8},{10,11... | collective-permute-start | bytes 983048 | tf_op jit(solution)/shard_map/ppermute | solution.py:357
  28.2 4.1 %collective-permute-start.8 = (bf16[2,384,256]{2,1,0:T(8,128)(2,1)S(1)}, bf16[2,384,256]{2,1,0:T(8,128)(2,1)S(1)}, u32[]{:S(2)}, u32[]{:S(2)}) collective-permute-start(bf16[2,384,256]{2,1,0:T(8,128)(2,1)S(1)} %collective-permute-done.6.refs_2_), channel_id=1, source_target_pairs={{0,1},{1,0},{2,3},{3,2},{4,5},{5,4},{6,7},{7,6},{8,9},{9,8},{10,11... | collective-permute-start | bytes 1179656 | tf_op jit(solution)/shard_map/ppermute | solution.py:357
  32.8 7.1 %collective-permute-start.14 = (bf16[1,384,256]{2,1,0:T(8,128)(2,1)S(1)}, bf16[1,384,256]{2,1,0:T(8,128)(2,1)S(1)}, u32[]{:S(2)}, u32[]{:S(2)}) collective-permute-start(bf16[1,384,256]{2,1,0:T(8,128)(2,1)S(1)} %get-tuple-element.75.refs_0_), channel_id=1, source_target_pairs={{0,2},{1,3},{2,0},{3,1},{4,6},{5,7},{6,4},{7,5},{8,10},{9,11},{10,... | collective-permute-start | bytes 589832 | tf_op jit(solution)/shard_map/ppermute | solution.py:360
  34.4 5.8 %collective-permute-start.13 = (bf16[1,384,256]{2,1,0:T(8,128)(2,1)S(1)}, bf16[1,384,256]{2,1,0:T(8,128)(2,1)S(1)}, u32[]{:S(2)}, u32[]{:S(2)}) collective-permute-start(bf16[1,384,256]{2,1,0:T(8,128)(2,1)S(1)} %get-tuple-element.75.refs_0_), channel_id=1, source_target_pairs={{0,1},{1,0},{2,3},{3,2},{4,5},{5,4},{6,7},{7,6},{8,9},{9,8},{10,11... | collective-permute-start | bytes 589832 | tf_op jit(solution)/shard_map/ppermute | solution.py:357
  34.4 5.5 %collective-permute-start.12 = (bf16[1,128,256]{2,1,0:T(8,128)(2,1)S(1)}, bf16[1,128,256]{2,1,0:T(8,128)(2,1)S(1)}, u32[]{:S(2)}, u32[]{:S(2)}) collective-permute-start(bf16[1,128,256]{2,1,0:T(8,128)(2,1)S(1)} %get-tuple-element.83), channel_id=1, source_target_pairs={{4,0},{8,4},{12,8},{16,12},{20,16},{24,20},{28,24},{0,28},{5,1},{9... | collective-permute-start | bytes 196616 | tf_op jit(solution)/shard_map/ppermute | solution.py:366
  37.9 1.6 %collective-permute-start.11 = (bf16[1,640,256]{2,1,0:T(8,128)(2,1)S(1)}, bf16[1,640,256]{2,1,0:T(8,128)(2,1)S(1)}, u32[]{:S(2)}, u32[]{:S(2)}) collective-permute-start(bf16[1,640,256]{2,1,0:T(8,128)(2,1)S(1)} %collective-permute-done.10.refs_6_), channel_id=1, source_target_pairs={{0,1},{1,0},{2,3},{3,2},{4,5},{5,4},{6,7},{7,6},{8,9},{9,8},{10,11... | collective-permute-start | bytes 983048 | tf_op jit(solution)/shard_map/ppermute | solution.py:357
  40.0 1.6 %collective-permute-start.15 = (bf16[1,384,256]{2,1,0:T(8,128)(2,1)S(1)}, bf16[1,384,256]{2,1,0:T(8,128)(2,1)S(1)}, u32[]{:S(2)}, u32[]{:S(2)}) collective-permute-start(bf16[1,384,256]{2,1,0:T(8,128)(2,1)S(1)} %collective-permute-done.14.refs_2_), channel_id=1, source_target_pairs={{0,1},{1,0},{2,3},{3,2},{4,5},{5,4},{6,7},{7,6},{8,9},{9,8},{10,11... | collective-permute-start | bytes 589832 | tf_op jit(solution)/shard_map/ppermute | solution.py:357

commit v15 on v14

--- a/solution.py
+++ b/solution.py
@@ -277,35 +277,34 @@
     return call(body, "whole_sums", [part, last, kernels], [pltpu.VMEM((2, rows, owned), BF16)])[0]
 
 
-def finish(cells, pieces, ycount, sums, base_ref, new_ref, factor, faces, held, out_ref, sems):
+def finish(cells, sums_at, base_ref, new_ref, factor, faces, held, out_ref, sems, offset=0):
     copies = []
-    size = ycount // pieces
-    for i, x in enumerate(cells):
-        for p in range(pieces):
-            rows = pl.ds(p * size, size)
-            at = pl.ds(i * ycount + p * size, size)
-            e = sums[1, at, :].astype(F32) - new_ref[i, rows, :] * sums[0, at, :].astype(F32)
-            if x in faces:
-                e = e + DIFFUSION * faces[x][0, rows, :].astype(F32)
-            held[i, rows, :] = base_ref[i, rows, :] + factor * e
-            copies.append(
-                pltpu.make_async_copy(held.at[i, rows], out_ref.at[x, rows], sems.at[i * pieces + p])
-            )
-            copies[-1].start()
+    for j, (i, x) in enumerate(cells, offset):
+        e = sums_at(1, i) - new_ref[i] * sums_at(0, i)
+        if x in faces:
+            e = e + DIFFUSION * faces[x][0].astype(F32)
+        held[j] = base_ref[i] + factor * e
+        copies.append(pltpu.make_async_copy(held.at[j], out_ref.at[x], sems.at[j]))
+        copies[-1].start()
     return copies
 
 
-def second_first(sums, base, new, death, lo, hi, blocks, kernels, cells, xcount):
+def rounded_at(sums, ycount):
+    return lambda k, i: sums[k, pl.ds(i * ycount, ycount), :].astype(F32)
+
+
+def second_first(sums, base, new, death, blocks, kernels, cells, xcount):
     _, ycount, owned = new.shape
     rows = blocks[0].shape[1]
     count = len(blocks)
 
-    def body(sums_ref, base_ref, new_ref, d_ref, lo_ref, hi_ref, k_ref, *refs):
+    def body(sums_ref, base_ref, new_ref, d_ref, k_ref, *refs):
         block_refs = refs[:count]
         out_ref, part_ref, held, sems = refs[count:]
         factor = SECOND / (1.0 + SECOND * d_ref[...])
-        faces = {0: lo_ref, xcount - 1: hi_ref}
-        copies = finish(cells, 1, ycount, sums_ref, base_ref, new_ref, factor, faces, held, out_ref, sems)
+        copies = finish(
+            cells, rounded_at(sums_ref, ycount), base_ref, new_ref, factor, {}, held, out_ref, sems
+        )
         me = lax.axis_index("trait")
         values = [r[...].reshape(rows, owned) for r in block_refs]
         for k in range(2):
@@ -314,34 +313,45 @@
             copy.wait()
 
     return call(
-        body, "second_first", [sums, base, new, death, lo, hi, kernels, *blocks],
+        body, "second_first", [sums, base, new, death, kernels, *blocks],
         [jax.ShapeDtypeStruct((xcount, ycount, owned), F32), pltpu.VMEM((2, rows, owned), F32)],
         scratch=[pltpu.VMEM((len(cells), ycount, owned), F32), pltpu.SemaphoreType.DMA((len(cells),))],
         out_specs=[ANYWHERE, SPEC],
     )
 
 
-def second_last(part, last, base, new, death, kernels, begun, cells, xcount):
+def second_last(sums_a, base_a, new_a, lo, hi, part, last, base, new, death, kernels, begun, ends, cells, xcount):
     _, ycount, owned = new.shape
     rows = len(cells) * ycount
-
-    def body(part_ref, last_ref, base_ref, new_ref, d_ref, k_ref, begun_ref, out_ref, sums, held, sems):
+    total = len(ends) + len(cells)
+
+    def body(*refs):
+        sums_a_ref, base_a_ref, new_a_ref, lo_ref, hi_ref, part_ref, last_ref, base_ref, new_ref, d_ref, k_ref = refs[:11]
+        _, out_ref, sums, held, sems = refs[11:]
+        factor = SECOND / (1.0 + SECOND * d_ref[...])
+        faces = {0: lo_ref, xcount - 1: hi_ref}
+        copies = finish(
+            ends, rounded_at(sums_a_ref, ycount), base_a_ref, new_a_ref, factor, faces, held, out_ref, sems
+        )
         me = lax.axis_index("trait")
         for k in range(2):
             sums[k] = (part_ref[k] + blocks_dot([last_ref[...].reshape(rows, owned)], k_ref, k, [me ^ 3])).astype(BF16)
-        factor = SECOND / (1.0 + SECOND * d_ref[...])
-        for copy in finish(cells, 2, ycount, sums, base_ref, new_ref, factor, {}, held, out_ref, sems):
+        copies += finish(
+            list(enumerate(cells)), rounded_at(sums, ycount), base_ref, new_ref, factor, {}, held, out_ref, sems,
+            len(ends),
+        )
+        for copy in copies:
             copy.wait()
 
+    args = [sums_a, base_a, new_a, lo, hi, part, last, base, new, death, kernels, begun]
     return call(
-        body, "second_last", [part, last, base, new, death, kernels, begun],
-        [jax.ShapeDtypeStruct((xcount, ycount, owned), F32)],
+        body, "second_last", args, [jax.ShapeDtypeStruct((xcount, ycount, owned), F32)],
         scratch=[
             pltpu.VMEM((2, rows, owned), BF16),
-            pltpu.VMEM((len(cells), ycount, owned), F32),
-            pltpu.SemaphoreType.DMA((2 * len(cells),)),
+            pltpu.VMEM((total, ycount, owned), F32),
+            pltpu.SemaphoreType.DMA((total,)),
         ],
-        specs=[SPEC] * 6 + [FROM_HBM], out_specs=[ANYWHERE], alias={6: 0},
+        specs=[SPEC] * 11 + [FROM_HBM], out_specs=[ANYWHERE], alias={11: 0},
     )[0]
 
 
@@ -403,10 +413,15 @@
     sums_a = whole_sums(npart_a, nfarsib_a, after(kernels, nbase_a))
     nfar_b = after(nfar_b, sums_a, new_hi)
     nfarsib_b = to_sibling(nfar_b)
+    placed = list(enumerate(chunks[0]))
+    ends = [p for p in placed if p[1] in (0, xcount - 1)]
     begun, npart_b = second_first(
-        sums_a, nbase_a, new_a, death, new_lo, new_hi, [rounded_b, nsib_b, nfar_b], kernels, chunks[0], xcount
-    )
-    new_two = second_last(npart_b, nfarsib_b, nbase_b, new_b, death, kernels, begun, chunks[1], xcount)
+        sums_a, nbase_a, new_a, death, [rounded_b, nsib_b, nfar_b], kernels, [p for p in placed if p not in ends], xcount
+    )
+    new_two = second_last(
+        sums_a, nbase_a, new_a, new_lo, new_hi, npart_b, nfarsib_b, nbase_b, new_b, death, kernels, begun, ends,
+        chunks[1], xcount,
+    )
     return new_one, new_two
 
 

time: 42.7 us -> 42.7 us (level)
  transfers between devices with their start and end apart: 16 -> 16, of which waited for: 8 -> 7; matrix products, arithmetic and copies ran while one was open for 0% -> 0% of each run, Pallas kernels for 22% -> 22%
where the time goes in v15:
time: 42.7 us; the launch traced here: 42.5 us
  starting transfers between devices  17.5 us (41%)
  waiting for transfers between devices  12.7 us (30%)
  Pallas kernels  11.6 us (27%)
  between operations  0.79 us (2%)
    pallas_call x11, Pallas kernels, call(): pl.pallas_call(body, out_shape=outs, in_specs=specs, out_specs=out_specs...  11.6 us
    ppermute x2, starting transfers between devices, from_above(): lax.ppermute(head, 'gx', [((i + 1) % gcount, i) for i in range(gcount)])  6.72 us
    ppermute x2, waiting for transfers between devices, from_below(): lax.ppermute(tail, 'gx', [(i, (i + 1) % gcount) for i in range(gcount)])  6.57 us
    ppermute x4, starting transfers between devices, to_far(): return lax.ppermute(v, 'trait', [(i, i ^ 2) for i in range(traits)])  6.54 us
    ppermute x4, waiting for transfers between devices, to_far(): return lax.ppermute(v, 'trait', [(i, i ^ 2) for i in range(traits)])  4.53 us
    ppermute x2, starting transfers between devices, from_below(): lax.ppermute(tail, 'gx', [(i, (i + 1) % gcount) for i in range(gcount)])  3.62 us
    ppermute x2, waiting for transfers between devices, from_above(): lax.ppermute(head, 'gx', [((i + 1) % gcount, i) for i in range(gcount)])  1.18 us
  transfers between devices with their start and end apart: 16, of which 7 were waited for; matrix products, arithmetic and copies ran while one was open for 0% of the time, Pallas kernels for 22%

profile of v15, /device:TPU:0, one launch (start us, length us, event | category | flops | bytes accessed | tf_op | source)
XLA Modules:
  0.0 42.5 jit_solution(8696603482469033284)
XLA Ops:
  0.6 1.3 %load_chunk.2 = (f32[5,128,256]{2,1,0:T(8,128)S(1)}, f32[5,128,256]{2,1,0:T(8,128)S(1)}, bf16[2,640,256]{2,1,0:T(8,128)(2,1)S(1)}, bf16[2,128,256]{2,1,0:T(8,128)(2,1)S(1)}, bf16[2,128,256]{2,1,0:T(8,128)(2,1)S(1)}) custom-call(f32[8,128,256]{2,1,0:T(8,128)} %refs_0_.2, f32[8,128,256]{2,1,0:T(8,128)} %refs_1_.3), custom_call_target="tpu_custom_call" | custom-call | tf_op jit(solution)/shard_map/load_chunk/pallas_call | solution.py:37
  2.0 0.0 copy-start.2
  2.0 3.0 %collective-permute-start.1 = (bf16[2,640,256]{2,1,0:T(8,128)(2,1)S(1)}, bf16[2,640,256]{2,1,0:T(8,128)(2,1)S(1)}, u32[]{:S(2)}, u32[]{:S(2)}) collective-permute-start(bf16[2,640,256]{2,1,0:T(8,128)(2,1)S(1)} %get-tuple-element.48.refs_0_), channel_id=1, source_target_pairs={{0,2},{1,3},{2,0},{3,1},{4,6},{5,7},{6,4},{7,5},{8,10},{9,11},{10,... | collective-permute-start | bytes 1966088 | tf_op jit(solution)/shard_map/ppermute | solution.py:370
  5.0 1.1 %load_chunk.3 = (f32[3,128,256]{2,1,0:T(8,128)S(1)}, f32[3,128,256]{2,1,0:T(8,128)S(1)}, bf16[2,384,256]{2,1,0:T(8,128)(2,1)S(1)}) custom-call(f32[8,128,256]{2,1,0:T(8,128)} %refs_0_.2, f32[8,128,256]{2,1,0:T(8,128)} %refs_1_.3), custom_call_target="tpu_custom_call" | custom-call | tf_op jit(solution)/shard_map/load_chunk/pallas_call | solution.py:37
  6.2 0.0 copy-start
  6.2 0.0 copy-start.1
  6.2 0.0 copy-start.3
  6.2 0.1 collective-permute-start
  6.3 1.5 %collective-permute-start.2 = (bf16[2,128,256]{2,1,0:T(8,128)(2,1)S(1)}, bf16[2,128,256]{2,1,0:T(8,128)(2,1)S(1)}, u32[]{:S(2)}, u32[]{:S(2)}) collective-permute-start(bf16[2,128,256]{2,1,0:T(8,128)(2,1)S(1)} %get-tuple-element.55), channel_id=1, source_target_pairs={{0,4},{4,8},{8,12},{12,16},{16,20},{20,24},{24,28},{28,0},{1,5},{5... | collective-permute-start | bytes 393224 | tf_op jit(solution)/shard_map/ppermute | solution.py:373
  7.8 3.2 %collective-permute-start.3 = (bf16[2,128,256]{2,1,0:T(8,128)(2,1)S(1)}, bf16[2,128,256]{2,1,0:T(8,128)(2,1)S(1)}, u32[]{:S(2)}, u32[]{:S(2)}) collective-permute-start(bf16[2,128,256]{2,1,0:T(8,128)(2,1)S(1)} %get-tuple-element.56), channel_id=1, source_target_pairs={{4,0},{8,4},{12,8},{16,12},{20,16},{24,20},{28,24},{0,28},{5,1},{9... | collective-permute-start | bytes 393224 | tf_op jit(solution)/shard_map/ppermute | solution.py:376
  11.1 0.4 collective-permute-start.6
  11.4 3.6 %collective-permute-done.2.refs_4_ = bf16[2,128,256]{2,1,0:T(8,128)(2,1)S(1)} collective-permute-done((bf16[2,128,256]{2,1,0:T(8,128)(2,1)S(1)}, bf16[2,128,256]{2,1,0:T(8,128)(2,1)S(1)}, u32[]{:S(2)}, u32[]{:S(2)}) %collective-permute-start.2) | collective-permute-done | bytes 131104 | tf_op jit(solution)/shard_map/ppermute | solution.py:373
  15.1 0.0 collective-permute-start.5
  15.1 1.1 %collective-permute-done.3.refs_5_ = bf16[2,128,256]{2,1,0:T(8,128)(2,1)S(1)} collective-permute-done((bf16[2,128,256]{2,1,0:T(8,128)(2,1)S(1)}, bf16[2,128,256]{2,1,0:T(8,128)(2,1)S(1)}, u32[]{:S(2)}, u32[]{:S(2)}) %collective-permute-start.3) | collective-permute-done | bytes 131104 | tf_op jit(solution)/shard_map/ppermute | solution.py:376
  16.2 0.9 %before_first.1 = (f32[2,5,128,256]{3,2,1,0:T(8,128)S(1)}, f32[2,3,128,256]{3,2,1,0:T(8,128)S(1)}) custom-call(f32[5,128,256]{2,1,0:T(8,128)S(1)} %get-tuple-element.49.refs_0_.refs_4_.one_ref, f32[3,128,256]{2,1,0:T(8,128)S(1)} %get-tuple-element.50.refs_1_.refs_4_.one_ref, f32[5,128,256]{2,1,0:T(8,128)S(1)} %get-tuple-element.51.refs_2_.refs_5_.two_ref, ...), custom_call_target="tpu_custom_call" | custom-call | tf_op jit(solution)/shard_map/before_first/pallas_call | solution.py:37
  17.1 3.5 %collective-permute-done.1.refs_2_ = bf16[2,640,256]{2,1,0:T(8,128)(2,1)S(1)} collective-permute-done((bf16[2,640,256]{2,1,0:T(8,128)(2,1)S(1)}, bf16[2,640,256]{2,1,0:T(8,128)(2,1)S(1)}, u32[]{:S(2)}, u32[]{:S(2)}) %collective-permute-start.1) | collective-permute-done | bytes 655392 | tf_op jit(solution)/shard_map/ppermute | solution.py:370
  20.6 0.0 collective-permute-start.4
  20.6 0.0 collective-permute-done.refs_1_
  20.6 0.0 copy-done
  20.6 1.8 %early_part.2 = (f32[2,1280,256]{2,1,0:T(8,128)S(1)}, f32[5,128,256]{2,1,0:T(8,128)S(1)}, f32[5,128,256]{2,1,0:T(8,128)S(1)}) custom-call(bf16[2,640,256]{2,1,0:T(8,128)(2,1)S(1)} %get-tuple-element.48.refs_0_, bf16[2,640,256]{2,1,0:T(8,128)(2,1)S(1)} %collective-permute-done.refs_1_, bf16[2,640,256]{2,1,0:T(8,128)(2,1)S(1)} %collective-permute-done.1.refs_2_, ...), custom_call_target="tpu_custom_call" | custom-call | flops 20000000000 | tf_op jit(solution)/shard_map/early_part/pallas_call | solution.py:37
  22.4 0.3 collective-permute-done.4.last_ref
  22.7 0.8 %first_node.2 = (f32[5,128,256]{2,1,0:T(8,128)S(1)}, bf16[1,640,256]{2,1,0:T(8,128)(2,1)S(1)}, f32[5,128,256]{2,1,0:T(8,128)S(1)}, bf16[1,128,256]{2,1,0:T(8,128)(2,1)S(1)}, bf16[1,128,256]{2,1,0:T(8,128)(2,1)S(1)}) custom-call(f32[2,1280,256]{2,1,0:T(8,128)S(1)} %get-tuple-element.60.part_ref, f32[5,128,256]{2,1,0:T(8,128)S(1)} %get-tuple-element.61.first_ref, ...), custom_call_target="tpu_custom_call" | custom-call | tf_op jit(solution)/shard_map/first_node/pallas_call | solution.py:37
  23.5 2.1 %collective-permute-start.7 = (bf16[1,128,256]{2,1,0:T(8,128)(2,1)S(1)}, bf16[1,128,256]{2,1,0:T(8,128)(2,1)S(1)}, u32[]{:S(2)}, u32[]{:S(2)}) collective-permute-start(bf16[1,128,256]{2,1,0:T(8,128)(2,1)S(1)} %get-tuple-element.67), channel_id=1, source_target_pairs={{0,4},{4,8},{8,12},{12,16},{16,20},{20,24},{24,28},{28,0},{1,5},{5... | collective-permute-start | bytes 196616 | tf_op jit(solution)/shard_map/ppermute | solution.py:373
  25.6 1.5 %collective-permute-start.10 = (bf16[1,640,256]{2,1,0:T(8,128)(2,1)S(1)}, bf16[1,640,256]{2,1,0:T(8,128)(2,1)S(1)}, u32[]{:S(2)}, u32[]{:S(2)}) collective-permute-start(bf16[1,640,256]{2,1,0:T(8,128)(2,1)S(1)} %get-tuple-element.64.refs_4_), channel_id=1, source_target_pairs={{0,2},{1,3},{2,0},{3,1},{4,6},{5,7},{6,4},{7,5},{8,10},{9,11},{10,... | collective-permute-start | bytes 983048 | tf_op jit(solution)/shard_map/ppermute | solution.py:370
  27.1 0.0 collective-permute-start.9
  27.1 1.1 %collective-permute-done.6.refs_2_ = bf16[2,384,256]{2,1,0:T(8,128)(2,1)S(1)} collective-permute-done((bf16[2,384,256]{2,1,0:T(8,128)(2,1)S(1)}, bf16[2,384,256]{2,1,0:T(8,128)(2,1)S(1)}, u32[]{:S(2)}, u32[]{:S(2)}) %collective-permute-start.6) | collective-permute-done | bytes 393248 | tf_op jit(solution)/shard_map/ppermute | solution.py:370
  28.2 0.0 collective-permute-start.8
  28.2 3.0 %collective-permute-done.7.refs_3_ = bf16[1,128,256]{2,1,0:T(8,128)(2,1)S(1)} collective-permute-done((bf16[1,128,256]{2,1,0:T(8,128)(2,1)S(1)}, bf16[1,128,256]{2,1,0:T(8,128)(2,1)S(1)}, u32[]{:S(2)}, u32[]{:S(2)}) %collective-permute-start.7) | collective-permute-done | bytes 65568 | tf_op jit(solution)/shard_map/ppermute | solution.py:373
  31.1 0.0 collective-permute-done.5.refs_1_
  31.1 1.1 %early_part.3 = (f32[2,768,256]{2,1,0:T(8,128)S(1)}, f32[3,128,256]{2,1,0:T(8,128)S(1)}, f32[3,128,256]{2,1,0:T(8,128)S(1)}, f32[8,128,256]{2,1,0:T(8,128)}) custom-call(bf16[2,384,256]{2,1,0:T(8,128)(2,1)S(1)} %get-tuple-element.47.refs_0_, bf16[2,384,256]{2,1,0:T(8,128)(2,1)S(1)} %collective-permute-done.5.refs_1_, ...), custom_call_target="tpu_custom_call" | custom-call | flops 20000000000 | tf_op jit(solution)/shard_map/early_part/pallas_call | solution.py:37
  32.3 0.0 collective-permute-done.8.last_ref
  32.3 0.6 %first_node.3 = (f32[3,128,256]{2,1,0:T(8,128)S(1)}, bf16[1,384,256]{2,1,0:T(8,128)(2,1)S(1)}, f32[3,128,256]{2,1,0:T(8,128)S(1)}) custom-call(f32[2,768,256]{2,1,0:T(8,128)S(1)} %get-tuple-element.69.part_ref, f32[3,128,256]{2,1,0:T(8,128)S(1)} %get-tuple-element.70.first_ref, f32[3,128,256]{2,1,0:T(8,128)S(1)} %get-tuple-element.71.begun_ref, ...), custom_call_target="tpu_custom_call" | custom-call | tf_op jit(solution)/shard_map/first_node/pallas_call | solution.py:37
  32.8 1.6 %collective-permute-start.14 = (bf16[1,384,256]{2,1,0:T(8,128)(2,1)S(1)}, bf16[1,384,256]{2,1,0:T(8,128)(2,1)S(1)}, u32[]{:S(2)}, u32[]{:S(2)}) collective-permute-start(bf16[1,384,256]{2,1,0:T(8,128)(2,1)S(1)} %get-tuple-element.75.refs_0_), channel_id=1, source_target_pairs={{0,2},{1,3},{2,0},{3,1},{4,6},{5,7},{6,4},{7,5},{8,10},{9,11},{10,... | collective-permute-start | bytes 589832 | tf_op jit(solution)/shard_map/ppermute | solution.py:370
  34.4 0.0 collective-permute-start.13
  34.4 3.5 %collective-permute-start.12 = (bf16[1,128,256]{2,1,0:T(8,128)(2,1)S(1)}, bf16[1,128,256]{2,1,0:T(8,128)(2,1)S(1)}, u32[]{:S(2)}, u32[]{:S(2)}) collective-permute-start(bf16[1,128,256]{2,1,0:T(8,128)(2,1)S(1)} %get-tuple-element.83), channel_id=1, source_target_pairs={{4,0},{8,4},{12,8},{16,12},{20,16},{24,20},{28,24},{0,28},{5,1},{9... | collective-permute-start | bytes 196616 | tf_op jit(solution)/shard_map/ppermute | solution.py:376
  37.9 0.0 collective-permute-done.10.refs_6_
  37.9 0.2 collective-permute-start.11
  38.2 0.0 collective-permute-done.9.refs_5_
  38.2 1.3 %before_second.1 = (f32[8,128,256]{2,1,0:T(8,128)}, f32[2,640,256]{2,1,0:T(8,128)S(1)}, f32[5,128,256]{2,1,0:T(8,128)S(1)}, f32[3,128,256]{2,1,0:T(8,128)S(1)}) custom-call(f32[5,128,256]{2,1,0:T(8,128)S(1)} %get-tuple-element.63.refs_9_.refs_0_.new_ref.refs_2_, ...), custom_call_target="tpu_custom_call", output_to_operand_aliasing={{0}: (10, {})} | custom-call | flops 20000000000 | tf_op jit(solution)/shard_map/before_second/pallas_call | solution.py:37
  39.5 0.1 collective-permute-done.11.last_ref
  39.6 0.3 whole_sums.1.sums_ref.refs_0_
  39.9 0.1 collective-permute-done.12.refs_4_
  40.0 0.0 collective-permute-done.14.refs_2_
  40.0 0.3 collective-permute-start.15
  40.2 0.0 collective-permute-done.13.refs_1_
  40.2 1.2 %second_first.1 = (f32[8,128,256]{2,1,0:T(8,128)}, f32[2,384,256]{2,1,0:T(8,128)S(1)}) custom-call(bf16[2,640,256]{2,1,0:T(8,128)(2,1)S(1)} %whole_sums.1.sums_ref.refs_0_, f32[5,128,256]{2,1,0:T(8,128)S(1)} %get-tuple-element.80.base_ref.refs_1_, f32[5,128,256]{2,1,0:T(8,128)S(1)} %get-tuple-element.63.refs_9_.refs_0_.new_ref.refs_2_, ...), custom_call_target="tpu_custom_call" | custom-call | tf_op jit(solution)/shard_map/second_first/pallas_call | solution.py:37
  41.4 0.0 collective-permute-done.15.refs_6_
  41.4 1.1 %second_last.1 = f32[8,128,256]{2,1,0:T(8,128)} custom-call(bf16[2,640,256]{2,1,0:T(8,128)(2,1)S(1)} %whole_sums.1.sums_ref.refs_0_, f32[5,128,256]{2,1,0:T(8,128)S(1)} %get-tuple-element.80.base_ref.refs_1_, f32[5,128,256]{2,1,0:T(8,128)S(1)} %get-tuple-element.63.refs_9_.refs_0_.new_ref.refs_2_, ...), custom_call_target="tpu_custom_call", output_to_operand_aliasing={{}: (11, {})} | custom-call | tf_op jit(solution)/shard_map/second_last/pallas_call | solution.py:37
  (3 shorter events, 0.0 us)
Async XLA Ops:
  2.0 14.2 %copy-start.2 = (f32[256]{0:T(256)S(1)}, f32[256]{0:T(256)}, u32[]{:S(2)}) copy-start(f32[256]{0:T(256)} %param.10) | copy-start | bytes 3076
  2.0 18.6 %collective-permute-start.1 = (bf16[2,640,256]{2,1,0:T(8,128)(2,1)S(1)}, bf16[2,640,256]{2,1,0:T(8,128)(2,1)S(1)}, u32[]{:S(2)}, u32[]{:S(2)}) collective-permute-start(bf16[2,640,256]{2,1,0:T(8,128)(2,1)S(1)} %get-tuple-element.48.refs_0_), channel_id=1, source_target_pairs={{0,2},{1,3},{2,0},{3,1},{4,6},{5,7},{6,4},{7,5},{8,10},{9,11},{10,... | collective-permute-start | bytes 1966088 | tf_op jit(solution)/shard_map/ppermute | solution.py:370
  6.2 14.4 %copy-start = (bf16[2,1024,256]{2,1,0:T(8,128)(2,1)S(1)}, bf16[2,1024,256]{2,1,0:T(8,128)(2,1)}, u32[]{:S(2)}) copy-start(bf16[2,1024,256]{2,1,0:T(8,128)(2,1)} %refs_10_) | copy-start | bytes 3145732
  6.2 14.4 %copy-start.1 = (f32[256]{0:T(256)S(1)}, f32[256]{0:T(256)}, u32[]{:S(2)}) copy-start(f32[256]{0:T(256)} %param.11) | copy-start | bytes 3076
  6.2 14.4 %copy-start.3 = (f32[8,128,256]{2,1,0:T(8,128)S(1)}, f32[8,128,256]{2,1,0:T(8,128)}, u32[]{:S(2)}) copy-start(f32[8,128,256]{2,1,0:T(8,128)} %refs_6_.3) | copy-start | bytes 3145732
  6.2 14.4 %collective-permute-start = (bf16[2,640,256]{2,1,0:T(8,128)(2,1)S(1)}, bf16[2,640,256]{2,1,0:T(8,128)(2,1)S(1)}, u32[]{:S(2)}, u32[]{:S(2)}) collective-permute-start(bf16[2,640,256]{2,1,0:T(8,128)(2,1)S(1)} %get-tuple-element.48.refs_0_), channel_id=1, source_target_pairs={{0,1},{1,0},{2,3},{3,2},{4,5},{5,4},{6,7},{7,6},{8,9},{9,8},{10,11... | collective-permute-start | bytes 1966088 | tf_op jit(solution)/shard_map/ppermute | solution.py:367
  6.3 8.8 %collective-permute-start.2 = (bf16[2,128,256]{2,1,0:T(8,128)(2,1)S(1)}, bf16[2,128,256]{2,1,0:T(8,128)(2,1)S(1)}, u32[]{:S(2)}, u32[]{:S(2)}) collective-permute-start(bf16[2,128,256]{2,1,0:T(8,128)(2,1)S(1)} %get-tuple-element.55), channel_id=1, source_target_pairs={{0,4},{4,8},{8,12},{12,16},{16,20},{20,24},{24,28},{28,0},{1,5},{5... | collective-permute-start | bytes 393224 | tf_op jit(solution)/shard_map/ppermute | solution.py:373
  7.8 8.4 %collective-permute-start.3 = (bf16[2,128,256]{2,1,0:T(8,128)(2,1)S(1)}, bf16[2,128,256]{2,1,0:T(8,128)(2,1)S(1)}, u32[]{:S(2)}, u32[]{:S(2)}) collective-permute-start(bf16[2,128,256]{2,1,0:T(8,128)(2,1)S(1)} %get-tuple-element.56), channel_id=1, source_target_pairs={{4,0},{8,4},{12,8},{16,12},{20,16},{24,20},{28,24},{0,28},{5,1},{9... | collective-permute-start | bytes 393224 | tf_op jit(solution)/shard_map/ppermute | solution.py:376
  11.1 17.1 %collective-permute-start.6 = (bf16[2,384,256]{2,1,0:T(8,128)(2,1)S(1)}, bf16[2,384,256]{2,1,0:T(8,128)(2,1)S(1)}, u32[]{:S(2)}, u32[]{:S(2)}) collective-permute-start(bf16[2,384,256]{2,1,0:T(8,128)(2,1)S(1)} %get-tuple-element.47.refs_0_), channel_id=1, source_target_pairs={{0,2},{1,3},{2,0},{3,1},{4,6},{5,7},{6,4},{7,5},{8,10},{9,11},{10,... | collective-permute-start | bytes 1179656 | tf_op jit(solution)/shard_map/ppermute | solution.py:370
  15.1 16.1 %collective-permute-start.5 = (bf16[2,384,256]{2,1,0:T(8,128)(2,1)S(1)}, bf16[2,384,256]{2,1,0:T(8,128)(2,1)S(1)}, u32[]{:S(2)}, u32[]{:S(2)}) collective-permute-start(bf16[2,384,256]{2,1,0:T(8,128)(2,1)S(1)} %get-tuple-element.47.refs_0_), channel_id=1, source_target_pairs={{0,1},{1,0},{2,3},{3,2},{4,5},{5,4},{6,7},{7,6},{8,9},{9,8},{10,11... | collective-permute-start | bytes 1179656 | tf_op jit(solution)/shard_map/ppermute | solution.py:367
  20.6 2.1 %collective-permute-start.4 = (bf16[2,640,256]{2,1,0:T(8,128)(2,1)S(1)}, bf16[2,640,256]{2,1,0:T(8,128)(2,1)S(1)}, u32[]{:S(2)}, u32[]{:S(2)}) collective-permute-start(bf16[2,640,256]{2,1,0:T(8,128)(2,1)S(1)} %collective-permute-done.1.refs_2_), channel_id=1, source_target_pairs={{0,1},{1,0},{2,3},{3,2},{4,5},{5,4},{6,7},{7,6},{8,9},{9,8},{10,11... | collective-permute-start | bytes 1966088 | tf_op jit(solution)/shard_map/ppermute | solution.py:367
  23.5 7.6 %collective-permute-start.7 = (bf16[1,128,256]{2,1,0:T(8,128)(2,1)S(1)}, bf16[1,128,256]{2,1,0:T(8,128)(2,1)S(1)}, u32[]{:S(2)}, u32[]{:S(2)}) collective-permute-start(bf16[1,128,256]{2,1,0:T(8,128)(2,1)S(1)} %get-tuple-element.67), channel_id=1, source_target_pairs={{0,4},{4,8},{8,12},{12,16},{16,20},{20,24},{24,28},{28,0},{1,5},{5... | collective-permute-start | bytes 196616 | tf_op jit(solution)/shard_map/ppermute | solution.py:373
  25.6 12.4 %collective-permute-start.10 = (bf16[1,640,256]{2,1,0:T(8,128)(2,1)S(1)}, bf16[1,640,256]{2,1,0:T(8,128)(2,1)S(1)}, u32[]{:S(2)}, u32[]{:S(2)}) collective-permute-start(bf16[1,640,256]{2,1,0:T(8,128)(2,1)S(1)} %get-tuple-element.64.refs_4_), channel_id=1, source_target_pairs={{0,2},{1,3},{2,0},{3,1},{4,6},{5,7},{6,4},{7,5},{8,10},{9,11},{10,... | collective-permute-start | bytes 983048 | tf_op jit(solution)/shard_map/ppermute | solution.py:370
  27.1 11.1 %collective-permute-start.9 = (bf16[1,640,256]{2,1,0:T(8,128)(2,1)S(1)}, bf16[1,640,256]{2,1,0:T(8,128)(2,1)S(1)}, u32[]{:S(2)}, u32[]{:S(2)}) collective-permute-start(bf16[1,640,256]{2,1,0:T(8,128)(2,1)S(1)} %get-tuple-element.64.refs_4_), channel_id=1, source_target_pairs={{0,1},{1,0},{2,3},{3,2},{4,5},{5,4},{6,7},{7,6},{8,9},{9,8},{10,11... | collective-permute-start | bytes 983048 | tf_op jit(solution)/shard_map/ppermute | solution.py:367
  28.2 4.1 %collective-permute-start.8 = (bf16[2,384,256]{2,1,0:T(8,128)(2,1)S(1)}, bf16[2,384,256]{2,1,0:T(8,128)(2,1)S(1)}, u32[]{:S(2)}, u32[]{:S(2)}) collective-permute-start(bf16[2,384,256]{2,1,0:T(8,128)(2,1)S(1)} %collective-permute-done.6.refs_2_), channel_id=1, source_target_pairs={{0,1},{1,0},{2,3},{3,2},{4,5},{5,4},{6,7},{7,6},{8,9},{9,8},{10,11... | collective-permute-start | bytes 1179656 | tf_op jit(solution)/shard_map/ppermute | solution.py:367
  32.8 7.1 %collective-permute-start.14 = (bf16[1,384,256]{2,1,0:T(8,128)(2,1)S(1)}, bf16[1,384,256]{2,1,0:T(8,128)(2,1)S(1)}, u32[]{:S(2)}, u32[]{:S(2)}) collective-permute-start(bf16[1,384,256]{2,1,0:T(8,128)(2,1)S(1)} %get-tuple-element.75.refs_0_), channel_id=1, source_target_pairs={{0,2},{1,3},{2,0},{3,1},{4,6},{5,7},{6,4},{7,5},{8,10},{9,11},{10,... | collective-permute-start | bytes 589832 | tf_op jit(solution)/shard_map/ppermute | solution.py:370
  34.4 5.8 %collective-permute-start.13 = (bf16[1,384,256]{2,1,0:T(8,128)(2,1)S(1)}, bf16[1,384,256]{2,1,0:T(8,128)(2,1)S(1)}, u32[]{:S(2)}, u32[]{:S(2)}) collective-permute-start(bf16[1,384,256]{2,1,0:T(8,128)(2,1)S(1)} %get-tuple-element.75.refs_0_), channel_id=1, source_target_pairs={{0,1},{1,0},{2,3},{3,2},{4,5},{5,4},{6,7},{7,6},{8,9},{9,8},{10,11... | collective-permute-start | bytes 589832 | tf_op jit(solution)/shard_map/ppermute | solution.py:367
  34.4 5.5 %collective-permute-start.12 = (bf16[1,128,256]{2,1,0:T(8,128)(2,1)S(1)}, bf16[1,128,256]{2,1,0:T(8,128)(2,1)S(1)}, u32[]{:S(2)}, u32[]{:S(2)}) collective-permute-start(bf16[1,128,256]{2,1,0:T(8,128)(2,1)S(1)} %get-tuple-element.83), channel_id=1, source_target_pairs={{4,0},{8,4},{12,8},{16,12},{20,16},{24,20},{28,24},{0,28},{5,1},{9... | collective-permute-start | bytes 196616 | tf_op jit(solution)/shard_map/ppermute | solution.py:376
  37.9 1.6 %collective-permute-start.11 = (bf16[1,640,256]{2,1,0:T(8,128)(2,1)S(1)}, bf16[1,640,256]{2,1,0:T(8,128)(2,1)S(1)}, u32[]{:S(2)}, u32[]{:S(2)}) collective-permute-start(bf16[1,640,256]{2,1,0:T(8,128)(2,1)S(1)} %collective-permute-done.10.refs_6_), channel_id=1, source_target_pairs={{0,1},{1,0},{2,3},{3,2},{4,5},{5,4},{6,7},{7,6},{8,9},{9,8},{10,11... | collective-permute-start | bytes 983048 | tf_op jit(solution)/shard_map/ppermute | solution.py:367
  40.0 1.5 %collective-permute-start.15 = (bf16[1,384,256]{2,1,0:T(8,128)(2,1)S(1)}, bf16[1,384,256]{2,1,0:T(8,128)(2,1)S(1)}, u32[]{:S(2)}, u32[]{:S(2)}) collective-permute-start(bf16[1,384,256]{2,1,0:T(8,128)(2,1)S(1)} %collective-permute-done.14.refs_2_), channel_id=1, source_target_pairs={{0,1},{1,0},{2,3},{3,2},{4,5},{5,4},{6,7},{7,6},{8,9},{9,8},{10,11... | collective-permute-start | bytes 589832 | tf_op jit(solution)/shard_map/ppermute | solution.py:367

commit v16 on v15

--- a/solution.py
+++ b/solution.py
@@ -57,7 +57,7 @@
     return runs
 
 
-def load_chunk(fields, cells, with_faces):
+def load_chunk(fields, cells, with_faces, split=False):
     xcount, ycount, owned = fields[0].shape
     count = len(fields)
     runs = runs_of(cells)
@@ -78,6 +78,8 @@
                 for i in range(start, start + size):
                     value = held_refs[f][i].astype(BF16)
                     out_ref[f, i * ycount:(i + 1) * ycount, :] = value
+                    if split:
+                        refs[2 * count + 1 + f][0, i * ycount:(i + 1) * ycount, :] = value
                     if with_faces and cells[i] == 0:
                         refs[2 * count + 1][f] = value
                     if with_faces and cells[i] == xcount - 1:
@@ -85,6 +87,8 @@
 
     outs = [pltpu.VMEM((len(cells), ycount, owned), F32)] * count
     outs.append(pltpu.VMEM((count, len(cells) * ycount, owned), BF16))
+    if split:
+        outs += [pltpu.VMEM((1, len(cells) * ycount, owned), BF16)] * count
     if with_faces:
         outs += [pltpu.VMEM((count, ycount, owned), BF16)] * 2
     return call(
@@ -131,10 +135,15 @@
     return call(body, "before_first", [*ones, *twos, lo, hi, growth], outs)
 
 
+def rows_of(refs):
+    return jnp.concatenate([r[...].reshape(-1, r.shape[-1]) for r in refs], axis=0)
+
+
 def early_part(blocks, base, one, two, initial, kernels, death, cells, new=None, new_cells=()):
     xcount, ycount, owned = initial.shape
     rows = len(cells) * ycount
-    count = len(blocks)
+    owners = [j for j, block in enumerate(blocks) for _ in block]
+    count = len(owners)
 
     def body(*refs):
         block_refs = refs[:count]
@@ -150,9 +159,9 @@
             copy.start()
         part_ref, first_ref, rest_ref = refs[:3] if new is None else refs[1:4]
         me = lax.axis_index("trait")
-        values = [r[...].reshape(2 * rows, owned) for r in block_refs]
+        values = [rows_of([r for j, r in zip(owners, block_refs) if j == n]) for n in range(len(blocks))]
         for k in range(2):
-            part_ref[k] = blocks_dot(values, k_ref, k, [me ^ j for j in range(count)])
+            part_ref[k] = blocks_dot(values, k_ref, k, [me ^ j for j in range(len(blocks))])
         death = d_ref[...]
         inv_one = 1.0 / (1.0 + FIRST * death)
         inv_two = 1.0 / (1.0 + SECOND * death)
@@ -173,7 +182,7 @@
         for copy in copies:
             copy.wait()
 
-    args = [*blocks, base, one, two, initial, kernels, death]
+    args = [*sum(blocks, []), base, one, two, initial, kernels, death]
     outs = [pltpu.VMEM((2, 2 * rows, owned), F32)] + [pltpu.VMEM((len(cells), ycount, owned), F32)] * 2
     if new is None:
         return call(body, "early_part", args, outs, gflop=20.0)
@@ -188,10 +197,13 @@
     _, ycount, owned = one.shape
     rows = len(cells) * ycount
 
-    def body(part_ref, first_ref, begun_ref, last_ref, one_ref, two_ref, k_ref, d_ref, *outs):
+    count = len(last)
+
+    def body(*refs):
+        last_refs, (part_ref, first_ref, begun_ref, one_ref, two_ref, k_ref, d_ref, *outs) = refs[:count], refs[count:]
         new_ref, rounded_ref, rest_ref, *face_refs = outs
         me = lax.axis_index("trait")
-        values = [last_ref[...].reshape(2 * rows, owned)]
+        values = [rows_of(last_refs)]
         compete, mutate = ((part_ref[k] + blocks_dot(values, k_ref, k, [me ^ 3])).astype(BF16) for k in range(2))
         inv_one = STEP_SIZE / (1.0 + FIRST * d_ref[...])
         inv_two = 1.0 / (1.0 + SECOND * d_ref[...])
@@ -218,7 +230,7 @@
     ]
     if with_faces:
         outs += [pltpu.VMEM((1, ycount, owned), BF16)] * 2
-    return call(body, "first_node", [part, first, rest, last, one, two, kernels, death], outs)
+    return call(body, "first_node", [*last, part, first, rest, one, two, kernels, death], outs)
 
 
 def before_second(news, rests, growth, death, begun, blocks, kernels, chunks):
@@ -377,8 +389,8 @@
 
     one_a, two_a, own_a, head, tail = load_chunk((section_one, section_two), chunks[0], True)
     far_a = to_far(own_a)
-    one_b, two_b, own_b = load_chunk((after(section_one, own_a), section_two), chunks[1], False)
-    far_b = to_far(own_b)
+    one_b, two_b, own_b, *own_fields = load_chunk((after(section_one, own_a), section_two), chunks[1], False, True)
+    far_b = [to_far(v) for v in own_fields]
     head, tail, kernels = lax.optimization_barrier((head, tail, kernels, own_b))[:3]
     lo, hi = from_below(tail), from_above(head)
     base_a, base_b = before_first((one_a, one_b), (two_a, two_b), lo, hi, growth, chunks)
@@ -386,18 +398,20 @@
     sib_b = to_sibling(own_b)
     far_a = after(far_a, base_a)
     farsib_a = to_sibling(far_a)
-    part_a, first_a, rest_a = early_part([own_a, sib_a, far_a], base_a, one_a, two_a, initial, kernels, death, chunks[0])
+    part_a, first_a, rest_a = early_part([[own_a], [sib_a], [far_a]], base_a, one_a, two_a, initial, kernels, death, chunks[0])
     new_a, rounded_a, rest_a, new_head, new_tail = first_node(
-        part_a, first_a, rest_a, farsib_a, one_a, two_a, kernels, death, chunks[0], xcount, True
+        part_a, first_a, rest_a, [farsib_a], one_a, two_a, kernels, death, chunks[0], xcount, True
     )
     nfar_a = to_far(rounded_a)
     nsib_a = to_sibling(rounded_a)
 
     new_lo = from_below(new_tail)
-    far_b = after(far_b, rounded_a)
-    farsib_b = to_sibling(far_b)
+    far_b = [after(far_b[0], rounded_a), far_b[1]]
+    farsib_b = [to_sibling(far_b[0])]
+    far_b[1] = after(far_b[1], farsib_b[0])
+    farsib_b.append(to_sibling(far_b[1]))
     part_b, first_b, rest_b, new_one = early_part(
-        [own_b, sib_b, far_b], base_b, one_b, two_b, initial, after(kernels, new_lo), death, chunks[1], new_a, chunks[0]
+        [[own_b], [sib_b], far_b], base_b, one_b, two_b, initial, after(kernels, new_lo), death, chunks[1], new_a, chunks[0]
     )
     new_b, rounded_b, rest_b = first_node(
         part_b, first_b, rest_b, farsib_b, one_b, two_b, kernels, death, chunks[1], xcount, False

time: 42.7 us -> 44.8 us (1.049)
  waiting for transfers between devices: 12.7 us -> 15.3 us
  starting transfers between devices: 17.5 us -> 16.9 us
    ppermute x2, starting transfers between devices: 6.72 us -> 4.98 us  [from_above(): lax.ppermute(head, 'gx', [((i + 1) % gcount, i) for i in range(gcount)])]
    ppermute x2, waiting for transfers between devices: 6.57 us -> 8.29 us  [from_below(): lax.ppermute(tail, 'gx', [(i, (i + 1) % gcount) for i in range(gcount)])]
    ppermute x4 -> x5, starting transfers between devices: 6.54 us -> 7.54 us  [to_far(): return lax.ppermute(v, 'trait', [(i, i ^ 2) for i in range(traits)])]
    ppermute x8 -> x9, waiting for transfers between devices: 0.37 us -> 0.83 us  [to_sibling(): return lax.ppermute(v, 'trait', [(i, i ^ 1) for i in range(traits)])]
    ppermute x4 -> x5, waiting for transfers between devices: 4.53 us -> 4.76 us  [to_far(): return lax.ppermute(v, 'trait', [(i, i ^ 2) for i in range(traits)])]
  transfers between devices with their start and end apart: 16 -> 18, of which waited for: 7 -> 11; matrix products, arithmetic and copies ran while one was open for 0% -> 0% of each run, Pallas kernels for 22% -> 21%
where the time goes in v16:
time: 44.8 us; the launch traced here: 44.6 us
  starting transfers between devices  16.9 us (38%)
  waiting for transfers between devices  15.3 us (34%)
  Pallas kernels  11.6 us (26%)
  between operations  0.78 us (2%)
    pallas_call x11, Pallas kernels, call(): pl.pallas_call(body, out_shape=outs, in_specs=specs, out_specs=out_specs...  11.6 us
    ppermute x2, waiting for transfers between devices, from_below(): lax.ppermute(tail, 'gx', [(i, (i + 1) % gcount) for i in range(gcount)])  8.29 us
    ppermute x5, starting transfers between devices, to_far(): return lax.ppermute(v, 'trait', [(i, i ^ 2) for i in range(traits)])  7.54 us
    ppermute x2, starting transfers between devices, from_above(): lax.ppermute(head, 'gx', [((i + 1) % gcount, i) for i in range(gcount)])  4.98 us
    ppermute x5, waiting for transfers between devices, to_far(): return lax.ppermute(v, 'trait', [(i, i ^ 2) for i in range(traits)])  4.76 us
    ppermute x2, starting transfers between devices, from_below(): lax.ppermute(tail, 'gx', [(i, (i + 1) % gcount) for i in range(gcount)])  3.57 us
    ppermute x2, waiting for transfers between devices, from_above(): lax.ppermute(head, 'gx', [((i + 1) % gcount, i) for i in range(gcount)])  1.41 us
  transfers between devices with their start and end apart: 18, of which 11 were waited for; matrix products, arithmetic and copies ran while one was open for 0% of the time, Pallas kernels for 21%

profile of v16, /device:TPU:0, one launch (start us, length us, event | category | flops | bytes accessed | tf_op | source)
XLA Modules:
  0.0 44.6 jit_solution(14285913852800704058)
XLA Ops:
  0.6 1.3 %load_chunk.2 = (f32[5,128,256]{2,1,0:T(8,128)S(1)}, f32[5,128,256]{2,1,0:T(8,128)S(1)}, bf16[2,640,256]{2,1,0:T(8,128)(2,1)S(1)}, bf16[2,128,256]{2,1,0:T(8,128)(2,1)S(1)}, bf16[2,128,256]{2,1,0:T(8,128)(2,1)S(1)}) custom-call(f32[8,128,256]{2,1,0:T(8,128)} %refs_0_.2, f32[8,128,256]{2,1,0:T(8,128)} %refs_1_.3), custom_call_target="tpu_custom_call" | custom-call | tf_op jit(solution)/shard_map/load_chunk/pallas_call | solution.py:37
  2.0 0.0 copy-start.2
  2.0 3.0 %collective-permute-start = (bf16[2,640,256]{2,1,0:T(8,128)(2,1)S(1)}, bf16[2,640,256]{2,1,0:T(8,128)(2,1)S(1)}, u32[]{:S(2)}, u32[]{:S(2)}) collective-permute-start(bf16[2,640,256]{2,1,0:T(8,128)(2,1)S(1)} %get-tuple-element.61.refs_0_), channel_id=1, source_target_pairs={{0,2},{1,3},{2,0},{3,1},{4,6},{5,7},{6,4},{7,5},{8,10},{9,11},{10,... | collective-permute-start | bytes 1966088 | tf_op jit(solution)/shard_map/ppermute | solution.py:382
  5.0 1.2 %load_chunk.3 = (f32[3,128,256]{2,1,0:T(8,128)S(1)}, f32[3,128,256]{2,1,0:T(8,128)S(1)}, bf16[2,384,256]{2,1,0:T(8,128)(2,1)S(1)}, bf16[1,384,256]{2,1,0:T(8,128)(2,1)S(1)}, bf16[1,384,256]{2,1,0:T(8,128)(2,1)S(1)}) custom-call(f32[8,128,256]{2,1,0:T(8,128)} %refs_0_.2, f32[8,128,256]{2,1,0:T(8,128)} %refs_1_.3), custom_call_target="tpu_custom_call" | custom-call | tf_op jit(solution)/shard_map/load_chunk/pallas_call | solution.py:37
  6.2 0.0 copy-start
  6.2 0.0 copy-start.1
  6.2 0.0 copy-start.3
  6.2 0.1 collective-permute-start.4
  6.3 1.5 %collective-permute-start.1 = (bf16[2,128,256]{2,1,0:T(8,128)(2,1)S(1)}, bf16[2,128,256]{2,1,0:T(8,128)(2,1)S(1)}, u32[]{:S(2)}, u32[]{:S(2)}) collective-permute-start(bf16[2,128,256]{2,1,0:T(8,128)(2,1)S(1)} %get-tuple-element.57), channel_id=1, source_target_pairs={{0,4},{4,8},{8,12},{12,16},{16,20},{20,24},{24,28},{28,0},{1,5},{5... | collective-permute-start | bytes 393224 | tf_op jit(solution)/shard_map/ppermute | solution.py:385
  7.8 3.2 %collective-permute-start.2 = (bf16[2,128,256]{2,1,0:T(8,128)(2,1)S(1)}, bf16[2,128,256]{2,1,0:T(8,128)(2,1)S(1)}, u32[]{:S(2)}, u32[]{:S(2)}) collective-permute-start(bf16[2,128,256]{2,1,0:T(8,128)(2,1)S(1)} %get-tuple-element.58), channel_id=1, source_target_pairs={{4,0},{8,4},{12,8},{16,12},{20,16},{24,20},{28,24},{0,28},{5,1},{9... | collective-permute-start | bytes 393224 | tf_op jit(solution)/shard_map/ppermute | solution.py:388
  11.1 0.0 collective-permute-start.9
  11.1 4.0 %collective-permute-done.1.refs_4_ = bf16[2,128,256]{2,1,0:T(8,128)(2,1)S(1)} collective-permute-done((bf16[2,128,256]{2,1,0:T(8,128)(2,1)S(1)}, bf16[2,128,256]{2,1,0:T(8,128)(2,1)S(1)}, u32[]{:S(2)}, u32[]{:S(2)}) %collective-permute-start.1) | collective-permute-done | bytes 131104 | tf_op jit(solution)/shard_map/ppermute | solution.py:385
  15.1 0.5 %collective-permute-start.5 = (bf16[1,384,256]{2,1,0:T(8,128)(2,1)S(1)}, bf16[1,384,256]{2,1,0:T(8,128)(2,1)S(1)}, u32[]{:S(2)}, u32[]{:S(2)}) collective-permute-start(bf16[1,384,256]{2,1,0:T(8,128)(2,1)S(1)} %get-tuple-element.67), channel_id=1, source_target_pairs={{0,2},{1,3},{2,0},{3,1},{4,6},{5,7},{6,4},{7,5},{8,10},{9,11},{10,... | collective-permute-start | bytes 589832 | tf_op jit(solution)/shard_map/ppermute | solution.py:382
  15.6 0.6 %collective-permute-done.2.refs_5_ = bf16[2,128,256]{2,1,0:T(8,128)(2,1)S(1)} collective-permute-done((bf16[2,128,256]{2,1,0:T(8,128)(2,1)S(1)}, bf16[2,128,256]{2,1,0:T(8,128)(2,1)S(1)}, u32[]{:S(2)}, u32[]{:S(2)}) %collective-permute-start.2) | collective-permute-done | bytes 131104 | tf_op jit(solution)/shard_map/ppermute | solution.py:388
  16.2 0.9 %collective-permute-start.7 = (bf16[1,384,256]{2,1,0:T(8,128)(2,1)S(1)}, bf16[1,384,256]{2,1,0:T(8,128)(2,1)S(1)}, u32[]{:S(2)}, u32[]{:S(2)}) collective-permute-start(bf16[1,384,256]{2,1,0:T(8,128)(2,1)S(1)} %get-tuple-element.70), channel_id=1, source_target_pairs={{0,2},{1,3},{2,0},{3,1},{4,6},{5,7},{6,4},{7,5},{8,10},{9,11},{10,... | collective-permute-start | bytes 589832 | tf_op jit(solution)/shard_map/ppermute | solution.py:382
  17.1 0.9 %before_first.1 = (f32[2,5,128,256]{3,2,1,0:T(8,128)S(1)}, f32[2,3,128,256]{3,2,1,0:T(8,128)S(1)}) custom-call(f32[5,128,256]{2,1,0:T(8,128)S(1)} %get-tuple-element.49.refs_0_.refs_4_, f32[3,128,256]{2,1,0:T(8,128)S(1)} %get-tuple-element.51.refs_1_.refs_5_, f32[5,128,256]{2,1,0:T(8,128)S(1)} %get-tuple-element.52.refs_2_.refs_5_, ...), custom_call_target="tpu_custom_call" | custom-call | tf_op jit(solution)/shard_map/before_first/pallas_call | solution.py:37
  18.0 2.5 %collective-permute-done.refs_2_ = bf16[2,640,256]{2,1,0:T(8,128)(2,1)S(1)} collective-permute-done((bf16[2,640,256]{2,1,0:T(8,128)(2,1)S(1)}, bf16[2,640,256]{2,1,0:T(8,128)(2,1)S(1)}, u32[]{:S(2)}, u32[]{:S(2)}) %collective-permute-start) | collective-permute-done | bytes 655392 | tf_op jit(solution)/shard_map/ppermute | solution.py:382
  20.6 0.0 collective-permute-start.3
  20.6 0.0 collective-permute-done.4.refs_1_
  20.6 1.8 %early_part.2 = (f32[2,1280,256]{2,1,0:T(8,128)S(1)}, f32[5,128,256]{2,1,0:T(8,128)S(1)}, f32[5,128,256]{2,1,0:T(8,128)S(1)}) custom-call(bf16[2,640,256]{2,1,0:T(8,128)(2,1)S(1)} %get-tuple-element.61.refs_0_, bf16[2,640,256]{2,1,0:T(8,128)(2,1)S(1)} %collective-permute-done.4.refs_1_, bf16[2,640,256]{2,1,0:T(8,128)(2,1)S(1)} %collective-permute-done.refs_2_, ...), custom_call_target="tpu_custom_call" | custom-call | flops 20000000000 | tf_op jit(solution)/shard_map/early_part/pallas_call | solution.py:37
  22.4 0.3 collective-permute-done.3.refs_0_
  22.7 0.8 %first_node.2 = (f32[5,128,256]{2,1,0:T(8,128)S(1)}, bf16[1,640,256]{2,1,0:T(8,128)(2,1)S(1)}, f32[5,128,256]{2,1,0:T(8,128)S(1)}, bf16[1,128,256]{2,1,0:T(8,128)(2,1)S(1)}, bf16[1,128,256]{2,1,0:T(8,128)(2,1)S(1)}) custom-call(bf16[2,640,256]{2,1,0:T(8,128)(2,1)S(1)} %collective-permute-done.3.refs_0_, f32[2,1280,256]{2,1,0:T(8,128)S(1)} %get-tuple-element.63.refs_1_, ...), custom_call_target="tpu_custom_call" | custom-call | tf_op jit(solution)/shard_map/first_node/pallas_call | solution.py:37
  23.5 1.3 %collective-permute-done.5.refs_2_ = bf16[1,384,256]{2,1,0:T(8,128)(2,1)S(1)} collective-permute-done((bf16[1,384,256]{2,1,0:T(8,128)(2,1)S(1)}, bf16[1,384,256]{2,1,0:T(8,128)(2,1)S(1)}, u32[]{:S(2)}, u32[]{:S(2)}) %collective-permute-start.5) | collective-permute-done | bytes 196640 | tf_op jit(solution)/shard_map/ppermute | solution.py:382
  24.8 0.0 collective-permute-start.6
  24.8 2.0 %collective-permute-start.10 = (bf16[1,128,256]{2,1,0:T(8,128)(2,1)S(1)}, bf16[1,128,256]{2,1,0:T(8,128)(2,1)S(1)}, u32[]{:S(2)}, u32[]{:S(2)}) collective-permute-start(bf16[1,128,256]{2,1,0:T(8,128)(2,1)S(1)} %get-tuple-element.73), channel_id=1, source_target_pairs={{0,4},{4,8},{8,12},{12,16},{16,20},{20,24},{24,28},{28,0},{1,5},{5... | collective-permute-start | bytes 196616 | tf_op jit(solution)/shard_map/ppermute | solution.py:385
  26.8 1.5 %collective-permute-start.12 = (bf16[1,640,256]{2,1,0:T(8,128)(2,1)S(1)}, bf16[1,640,256]{2,1,0:T(8,128)(2,1)S(1)}, u32[]{:S(2)}, u32[]{:S(2)}) collective-permute-start(bf16[1,640,256]{2,1,0:T(8,128)(2,1)S(1)} %get-tuple-element.68.refs_4_), channel_id=1, source_target_pairs={{0,2},{1,3},{2,0},{3,1},{4,6},{5,7},{6,4},{7,5},{8,10},{9,11},{10,... | collective-permute-start | bytes 983048 | tf_op jit(solution)/shard_map/ppermute | solution.py:382
  28.3 4.3 %collective-permute-done.10.refs_3_ = bf16[1,128,256]{2,1,0:T(8,128)(2,1)S(1)} collective-permute-done((bf16[1,128,256]{2,1,0:T(8,128)(2,1)S(1)}, bf16[1,128,256]{2,1,0:T(8,128)(2,1)S(1)}, u32[]{:S(2)}, u32[]{:S(2)}) %collective-permute-start.10) | collective-permute-done | bytes 65568 | tf_op jit(solution)/shard_map/ppermute | solution.py:385
  32.6 0.0 collective-permute-start.11
  32.6 0.0 collective-permute-done.7.refs_3_
  32.6 0.0 collective-permute-done.6.refs_0_
  32.6 0.5 %collective-permute-start.8 = (bf16[1,384,256]{2,1,0:T(8,128)(2,1)S(1)}, bf16[1,384,256]{2,1,0:T(8,128)(2,1)S(1)}, u32[]{:S(2)}, u32[]{:S(2)}) collective-permute-start(bf16[1,384,256]{2,1,0:T(8,128)(2,1)S(1)} %collective-permute-done.7.refs_3_), channel_id=1, source_target_pairs={{0,1},{1,0},{2,3},{3,2},{4,5},{5,4},{6,7},{7,6},{8,9},{9,8},{10,11... | collective-permute-start | bytes 589832 | tf_op jit(solution)/shard_map/ppermute | solution.py:379
  33.1 0.0 collective-permute-done.9.refs_1_
  33.1 1.1 %early_part.3 = (f32[2,768,256]{2,1,0:T(8,128)S(1)}, f32[3,128,256]{2,1,0:T(8,128)S(1)}, f32[3,128,256]{2,1,0:T(8,128)S(1)}, f32[8,128,256]{2,1,0:T(8,128)}) custom-call(bf16[2,384,256]{2,1,0:T(8,128)(2,1)S(1)} %get-tuple-element.56.refs_0_, bf16[2,384,256]{2,1,0:T(8,128)(2,1)S(1)} %collective-permute-done.9.refs_1_, ...), custom_call_target="tpu_custom_call" | custom-call | flops 20000000000 | tf_op jit(solution)/shard_map/early_part/pallas_call | solution.py:37
  34.3 0.2 collective-permute-done.8.refs_1_
  34.5 0.6 %first_node.3 = (f32[3,128,256]{2,1,0:T(8,128)S(1)}, bf16[1,384,256]{2,1,0:T(8,128)(2,1)S(1)}, f32[3,128,256]{2,1,0:T(8,128)S(1)}) custom-call(bf16[1,384,256]{2,1,0:T(8,128)(2,1)S(1)} %collective-permute-done.6.refs_0_, bf16[1,384,256]{2,1,0:T(8,128)(2,1)S(1)} %collective-permute-done.8.refs_1_, f32[2,768,256]{2,1,0:T(8,128)S(1)} %get-tuple-element.75.refs_2_, ...), custom_call_target="tpu_custom_call" | custom-call | tf_op jit(solution)/shard_map/first_node/pallas_call | solution.py:37
  35.1 1.6 %collective-permute-start.16 = (bf16[1,384,256]{2,1,0:T(8,128)(2,1)S(1)}, bf16[1,384,256]{2,1,0:T(8,128)(2,1)S(1)}, u32[]{:S(2)}, u32[]{:S(2)}) collective-permute-start(bf16[1,384,256]{2,1,0:T(8,128)(2,1)S(1)} %get-tuple-element.81.refs_0_), channel_id=1, source_target_pairs={{0,2},{1,3},{2,0},{3,1},{4,6},{5,7},{6,4},{7,5},{8,10},{9,11},{10,... | collective-permute-start | bytes 589832 | tf_op jit(solution)/shard_map/ppermute | solution.py:382
  36.7 1.7 %collective-permute-start.14 = (bf16[1,128,256]{2,1,0:T(8,128)(2,1)S(1)}, bf16[1,128,256]{2,1,0:T(8,128)(2,1)S(1)}, u32[]{:S(2)}, u32[]{:S(2)}) collective-permute-start(bf16[1,128,256]{2,1,0:T(8,128)(2,1)S(1)} %get-tuple-element.89), channel_id=1, source_target_pairs={{4,0},{8,4},{12,8},{16,12},{20,16},{24,20},{28,24},{0,28},{5,1},{9... | collective-permute-start | bytes 196616 | tf_op jit(solution)/shard_map/ppermute | solution.py:388
  38.4 0.2 collective-permute-start.13
  38.7 1.3 %before_second.1 = (f32[8,128,256]{2,1,0:T(8,128)}, f32[2,640,256]{2,1,0:T(8,128)S(1)}, f32[5,128,256]{2,1,0:T(8,128)S(1)}, f32[3,128,256]{2,1,0:T(8,128)S(1)}) custom-call(f32[5,128,256]{2,1,0:T(8,128)S(1)} %get-tuple-element.66.refs_10_.refs_0_.new_ref.refs_2_, ...), custom_call_target="tpu_custom_call", output_to_operand_aliasing={{0}: (10, {})} | custom-call | flops 20000000000 | tf_op jit(solution)/shard_map/before_second/pallas_call | solution.py:37
  40.0 0.1 collective-permute-done.13.last_ref
  40.1 0.3 whole_sums.1.sums_ref.refs_0_
  40.4 0.8 %collective-permute-done.14.refs_4_ = bf16[1,128,256]{2,1,0:T(8,128)(2,1)S(1)} collective-permute-done((bf16[1,128,256]{2,1,0:T(8,128)(2,1)S(1)}, bf16[1,128,256]{2,1,0:T(8,128)(2,1)S(1)}, u32[]{:S(2)}, u32[]{:S(2)}) %collective-permute-start.14) | collective-permute-done | bytes 65568 | tf_op jit(solution)/shard_map/ppermute | solution.py:388
  41.2 0.9 %collective-permute-done.16.refs_2_ = bf16[1,384,256]{2,1,0:T(8,128)(2,1)S(1)} collective-permute-done((bf16[1,384,256]{2,1,0:T(8,128)(2,1)S(1)}, bf16[1,384,256]{2,1,0:T(8,128)(2,1)S(1)}, u32[]{:S(2)}, u32[]{:S(2)}) %collective-permute-start.16) | collective-permute-done | bytes 196640 | tf_op jit(solution)/shard_map/ppermute | solution.py:382
  42.1 0.0 collective-permute-start.17
  42.1 0.0 collective-permute-done.15.refs_1_
  42.1 1.2 %second_first.1 = (f32[8,128,256]{2,1,0:T(8,128)}, f32[2,384,256]{2,1,0:T(8,128)S(1)}) custom-call(bf16[2,640,256]{2,1,0:T(8,128)(2,1)S(1)} %whole_sums.1.sums_ref.refs_0_, f32[5,128,256]{2,1,0:T(8,128)S(1)} %get-tuple-element.86.base_ref.refs_1_, f32[5,128,256]{2,1,0:T(8,128)S(1)} %get-tuple-element.66.refs_10_.refs_0_.new_ref.refs_2_, ...), custom_call_target="tpu_custom_call" | custom-call | tf_op jit(solution)/shard_map/second_first/pallas_call | solution.py:37
  43.3 0.2 collective-permute-done.17.refs_6_
  43.5 1.1 %second_last.1 = f32[8,128,256]{2,1,0:T(8,128)} custom-call(bf16[2,640,256]{2,1,0:T(8,128)(2,1)S(1)} %whole_sums.1.sums_ref.refs_0_, f32[5,128,256]{2,1,0:T(8,128)S(1)} %get-tuple-element.86.base_ref.refs_1_, f32[5,128,256]{2,1,0:T(8,128)S(1)} %get-tuple-element.66.refs_10_.refs_0_.new_ref.refs_2_, ...), custom_call_target="tpu_custom_call", output_to_operand_aliasing={{}: (11, {})} | custom-call | tf_op jit(solution)/shard_map/second_last/pallas_call | solution.py:37
  (7 shorter events, 0.0 us)
Async XLA Ops:
  2.0 15.1 %copy-start.2 = (f32[256]{0:T(256)S(1)}, f32[256]{0:T(256)}, u32[]{:S(2)}) copy-start(f32[256]{0:T(256)} %param.10) | copy-start | bytes 3076
  2.0 18.6 %collective-permute-start = (bf16[2,640,256]{2,1,0:T(8,128)(2,1)S(1)}, bf16[2,640,256]{2,1,0:T(8,128)(2,1)S(1)}, u32[]{:S(2)}, u32[]{:S(2)}) collective-permute-start(bf16[2,640,256]{2,1,0:T(8,128)(2,1)S(1)} %get-tuple-element.61.refs_0_), channel_id=1, source_target_pairs={{0,2},{1,3},{2,0},{3,1},{4,6},{5,7},{6,4},{7,5},{8,10},{9,11},{10,... | collective-permute-start | bytes 1966088 | tf_op jit(solution)/shard_map/ppermute | solution.py:382
  6.2 14.4 %copy-start = (bf16[2,1024,256]{2,1,0:T(8,128)(2,1)S(1)}, bf16[2,1024,256]{2,1,0:T(8,128)(2,1)}, u32[]{:S(2)}) copy-start(bf16[2,1024,256]{2,1,0:T(8,128)(2,1)} %refs_10_) | copy-start | bytes 3145732
  6.2 14.4 %copy-start.1 = (f32[256]{0:T(256)S(1)}, f32[256]{0:T(256)}, u32[]{:S(2)}) copy-start(f32[256]{0:T(256)} %param.11) | copy-start | bytes 3076
  6.2 14.4 %copy-start.3 = (f32[8,128,256]{2,1,0:T(8,128)S(1)}, f32[8,128,256]{2,1,0:T(8,128)}, u32[]{:S(2)}) copy-start(f32[8,128,256]{2,1,0:T(8,128)} %refs_7_.2) | copy-start | bytes 3145732
  6.2 14.4 %collective-permute-start.4 = (bf16[2,640,256]{2,1,0:T(8,128)(2,1)S(1)}, bf16[2,640,256]{2,1,0:T(8,128)(2,1)S(1)}, u32[]{:S(2)}, u32[]{:S(2)}) collective-permute-start(bf16[2,640,256]{2,1,0:T(8,128)(2,1)S(1)} %get-tuple-element.61.refs_0_), channel_id=1, source_target_pairs={{0,1},{1,0},{2,3},{3,2},{4,5},{5,4},{6,7},{7,6},{8,9},{9,8},{10,11... | collective-permute-start | bytes 1966088 | tf_op jit(solution)/shard_map/ppermute | solution.py:379
  6.3 8.8 %collective-permute-start.1 = (bf16[2,128,256]{2,1,0:T(8,128)(2,1)S(1)}, bf16[2,128,256]{2,1,0:T(8,128)(2,1)S(1)}, u32[]{:S(2)}, u32[]{:S(2)}) collective-permute-start(bf16[2,128,256]{2,1,0:T(8,128)(2,1)S(1)} %get-tuple-element.57), channel_id=1, source_target_pairs={{0,4},{4,8},{8,12},{12,16},{16,20},{20,24},{24,28},{28,0},{1,5},{5... | collective-permute-start | bytes 393224 | tf_op jit(solution)/shard_map/ppermute | solution.py:385
  7.8 8.4 %collective-permute-start.2 = (bf16[2,128,256]{2,1,0:T(8,128)(2,1)S(1)}, bf16[2,128,256]{2,1,0:T(8,128)(2,1)S(1)}, u32[]{:S(2)}, u32[]{:S(2)}) collective-permute-start(bf16[2,128,256]{2,1,0:T(8,128)(2,1)S(1)} %get-tuple-element.58), channel_id=1, source_target_pairs={{4,0},{8,4},{12,8},{16,12},{20,16},{24,20},{28,24},{0,28},{5,1},{9... | collective-permute-start | bytes 393224 | tf_op jit(solution)/shard_map/ppermute | solution.py:388
  11.1 22.1 %collective-permute-start.9 = (bf16[2,384,256]{2,1,0:T(8,128)(2,1)S(1)}, bf16[2,384,256]{2,1,0:T(8,128)(2,1)S(1)}, u32[]{:S(2)}, u32[]{:S(2)}) collective-permute-start(bf16[2,384,256]{2,1,0:T(8,128)(2,1)S(1)} %get-tuple-element.56.refs_0_), channel_id=1, source_target_pairs={{0,1},{1,0},{2,3},{3,2},{4,5},{5,4},{6,7},{7,6},{8,9},{9,8},{10,11... | collective-permute-start | bytes 1179656 | tf_op jit(solution)/shard_map/ppermute | solution.py:379
  15.1 9.7 %collective-permute-start.5 = (bf16[1,384,256]{2,1,0:T(8,128)(2,1)S(1)}, bf16[1,384,256]{2,1,0:T(8,128)(2,1)S(1)}, u32[]{:S(2)}, u32[]{:S(2)}) collective-permute-start(bf16[1,384,256]{2,1,0:T(8,128)(2,1)S(1)} %get-tuple-element.67), channel_id=1, source_target_pairs={{0,2},{1,3},{2,0},{3,1},{4,6},{5,7},{6,4},{7,5},{8,10},{9,11},{10,... | collective-permute-start | bytes 589832 | tf_op jit(solution)/shard_map/ppermute | solution.py:382
  16.2 16.4 %collective-permute-start.7 = (bf16[1,384,256]{2,1,0:T(8,128)(2,1)S(1)}, bf16[1,384,256]{2,1,0:T(8,128)(2,1)S(1)}, u32[]{:S(2)}, u32[]{:S(2)}) collective-permute-start(bf16[1,384,256]{2,1,0:T(8,128)(2,1)S(1)} %get-tuple-element.70), channel_id=1, source_target_pairs={{0,2},{1,3},{2,0},{3,1},{4,6},{5,7},{6,4},{7,5},{8,10},{9,11},{10,... | collective-permute-start | bytes 589832 | tf_op jit(solution)/shard_map/ppermute | solution.py:382
  20.6 2.1 %collective-permute-start.3 = (bf16[2,640,256]{2,1,0:T(8,128)(2,1)S(1)}, bf16[2,640,256]{2,1,0:T(8,128)(2,1)S(1)}, u32[]{:S(2)}, u32[]{:S(2)}) collective-permute-start(bf16[2,640,256]{2,1,0:T(8,128)(2,1)S(1)} %collective-permute-done.refs_2_), channel_id=1, source_target_pairs={{0,1},{1,0},{2,3},{3,2},{4,5},{5,4},{6,7},{7,6},{8,9},{9,8},{10,11... | collective-permute-start | bytes 1966088 | tf_op jit(solution)/shard_map/ppermute | solution.py:379
  24.8 7.8 %collective-permute-start.6 = (bf16[1,384,256]{2,1,0:T(8,128)(2,1)S(1)}, bf16[1,384,256]{2,1,0:T(8,128)(2,1)S(1)}, u32[]{:S(2)}, u32[]{:S(2)}) collective-permute-start(bf16[1,384,256]{2,1,0:T(8,128)(2,1)S(1)} %collective-permute-done.5.refs_2_), channel_id=1, source_target_pairs={{0,1},{1,0},{2,3},{3,2},{4,5},{5,4},{6,7},{7,6},{8,9},{9,8},{10,11... | collective-permute-start | bytes 589832 | tf_op jit(solution)/shard_map/ppermute | solution.py:379
  24.8 7.8 %collective-permute-start.10 = (bf16[1,128,256]{2,1,0:T(8,128)(2,1)S(1)}, bf16[1,128,256]{2,1,0:T(8,128)(2,1)S(1)}, u32[]{:S(2)}, u32[]{:S(2)}) collective-permute-start(bf16[1,128,256]{2,1,0:T(8,128)(2,1)S(1)} %get-tuple-element.73), channel_id=1, source_target_pairs={{0,4},{4,8},{8,12},{12,16},{16,20},{20,24},{24,28},{28,0},{1,5},{5... | collective-permute-start | bytes 196616 | tf_op jit(solution)/shard_map/ppermute | solution.py:385
  26.8 11.6 %collective-permute-start.12 = (bf16[1,640,256]{2,1,0:T(8,128)(2,1)S(1)}, bf16[1,640,256]{2,1,0:T(8,128)(2,1)S(1)}, u32[]{:S(2)}, u32[]{:S(2)}) collective-permute-start(bf16[1,640,256]{2,1,0:T(8,128)(2,1)S(1)} %get-tuple-element.68.refs_4_), channel_id=1, source_target_pairs={{0,2},{1,3},{2,0},{3,1},{4,6},{5,7},{6,4},{7,5},{8,10},{9,11},{10,... | collective-permute-start | bytes 983048 | tf_op jit(solution)/shard_map/ppermute | solution.py:382
  32.6 6.0 %collective-permute-start.11 = (bf16[1,640,256]{2,1,0:T(8,128)(2,1)S(1)}, bf16[1,640,256]{2,1,0:T(8,128)(2,1)S(1)}, u32[]{:S(2)}, u32[]{:S(2)}) collective-permute-start(bf16[1,640,256]{2,1,0:T(8,128)(2,1)S(1)} %get-tuple-element.68.refs_4_), channel_id=1, source_target_pairs={{0,1},{1,0},{2,3},{3,2},{4,5},{5,4},{6,7},{7,6},{8,9},{9,8},{10,11... | collective-permute-start | bytes 983048 | tf_op jit(solution)/shard_map/ppermute | solution.py:379
  32.6 1.9 %collective-permute-start.8 = (bf16[1,384,256]{2,1,0:T(8,128)(2,1)S(1)}, bf16[1,384,256]{2,1,0:T(8,128)(2,1)S(1)}, u32[]{:S(2)}, u32[]{:S(2)}) collective-permute-start(bf16[1,384,256]{2,1,0:T(8,128)(2,1)S(1)} %collective-permute-done.7.refs_3_), channel_id=1, source_target_pairs={{0,1},{1,0},{2,3},{3,2},{4,5},{5,4},{6,7},{7,6},{8,9},{9,8},{10,11... | collective-permute-start | bytes 589832 | tf_op jit(solution)/shard_map/ppermute | solution.py:379
  35.1 7.0 %collective-permute-start.16 = (bf16[1,384,256]{2,1,0:T(8,128)(2,1)S(1)}, bf16[1,384,256]{2,1,0:T(8,128)(2,1)S(1)}, u32[]{:S(2)}, u32[]{:S(2)}) collective-permute-start(bf16[1,384,256]{2,1,0:T(8,128)(2,1)S(1)} %get-tuple-element.81.refs_0_), channel_id=1, source_target_pairs={{0,2},{1,3},{2,0},{3,1},{4,6},{5,7},{6,4},{7,5},{8,10},{9,11},{10,... | collective-permute-start | bytes 589832 | tf_op jit(solution)/shard_map/ppermute | solution.py:382
  36.7 5.4 %collective-permute-start.15 = (bf16[1,384,256]{2,1,0:T(8,128)(2,1)S(1)}, bf16[1,384,256]{2,1,0:T(8,128)(2,1)S(1)}, u32[]{:S(2)}, u32[]{:S(2)}) collective-permute-start(bf16[1,384,256]{2,1,0:T(8,128)(2,1)S(1)} %get-tuple-element.81.refs_0_), channel_id=1, source_target_pairs={{0,1},{1,0},{2,3},{3,2},{4,5},{5,4},{6,7},{7,6},{8,9},{9,8},{10,11... | collective-permute-start | bytes 589832 | tf_op jit(solution)/shard_map/ppermute | solution.py:379
  36.7 4.5 %collective-permute-start.14 = (bf16[1,128,256]{2,1,0:T(8,128)(2,1)S(1)}, bf16[1,128,256]{2,1,0:T(8,128)(2,1)S(1)}, u32[]{:S(2)}, u32[]{:S(2)}) collective-permute-start(bf16[1,128,256]{2,1,0:T(8,128)(2,1)S(1)} %get-tuple-element.89), channel_id=1, source_target_pairs={{4,0},{8,4},{12,8},{16,12},{20,16},{24,20},{28,24},{0,28},{5,1},{9... | collective-permute-start | bytes 196616 | tf_op jit(solution)/shard_map/ppermute | solution.py:388
  38.4 1.6 %collective-permute-start.13 = (bf16[1,640,256]{2,1,0:T(8,128)(2,1)S(1)}, bf16[1,640,256]{2,1,0:T(8,128)(2,1)S(1)}, u32[]{:S(2)}, u32[]{:S(2)}) collective-permute-start(bf16[1,640,256]{2,1,0:T(8,128)(2,1)S(1)} %collective-permute-done.12.refs_6_), channel_id=1, source_target_pairs={{0,1},{1,0},{2,3},{3,2},{4,5},{5,4},{6,7},{7,6},{8,9},{9,8},{10,11... | collective-permute-start | bytes 983048 | tf_op jit(solution)/shard_map/ppermute | solution.py:379
  42.1 1.4 %collective-permute-start.17 = (bf16[1,384,256]{2,1,0:T(8,128)(2,1)S(1)}, bf16[1,384,256]{2,1,0:T(8,128)(2,1)S(1)}, u32[]{:S(2)}, u32[]{:S(2)}) collective-permute-start(bf16[1,384,256]{2,1,0:T(8,128)(2,1)S(1)} %collective-permute-done.16.refs_2_), channel_id=1, source_target_pairs={{0,1},{1,0},{2,3},{3,2},{4,5},{5,4},{6,7},{7,6},{8,9},{9,8},{10,11... | collective-permute-start | bytes 589832 | tf_op jit(solution)/shard_map/ppermute | solution.py:379

commit v17 on v15

--- a/solution.py
+++ b/solution.py
@@ -221,7 +221,7 @@
     return call(body, "first_node", [part, first, rest, last, one, two, kernels, death], outs)
 
 
-def before_second(news, rests, growth, death, begun, blocks, kernels, chunks):
+def before_second(news, rests, growth, death, begun, blocks, own_b, kernels, chunks):
     _, ycount, owned = news[0].shape
     rows = blocks[0].shape[1]
     xcount = sum(len(cells) for cells in chunks)
@@ -231,8 +231,8 @@
 
     def body(*refs):
         new_refs, rest_refs, block_refs = refs[:count], refs[count:2 * count], refs[2 * count:2 * count + size]
-        k_ref, g_ref, d_ref, _, whole_ref, part_ref = refs[2 * count + size:2 * count + size + 6]
-        base_refs, sems = refs[2 * count + size + 6:-1], refs[-1]
+        own_b_ref, k_ref, g_ref, d_ref, _, whole_ref, part_ref, part_b_ref = refs[2 * count + size:2 * count + size + 8]
+        base_refs, sems = refs[2 * count + size + 8:-1], refs[-1]
         copies = [
             pltpu.make_async_copy(new_refs[-1].at[pl.ds(i, size)], whole_ref.at[pl.ds(x, size)], sems.at[r])
             for r, (i, x, size) in enumerate(runs_of(chunks[-1]))
@@ -243,6 +243,7 @@
         values = [r[...].reshape(rows, owned) for r in block_refs]
         for k in range(2):
             part_ref[k] = blocks_dot(values, k_ref, k, [me ^ j for j in range(size)])
+            part_b_ref[k] = blocks_dot([own_b_ref[...].reshape(-1, owned)], k_ref, k, [me])
         growth = g_ref[...]
         factor = SECOND / (1.0 + SECOND * d_ref[...])
         for x, (c, i) in place.items():
@@ -256,8 +257,9 @@
             copy.wait()
 
     outs = [jax.ShapeDtypeStruct((xcount, ycount, owned), F32), pltpu.VMEM((2, rows, owned), F32)]
+    outs.append(pltpu.VMEM((2, own_b.shape[1], owned), F32))
     outs += [pltpu.VMEM((len(cells), ycount, owned), F32) for cells in chunks]
-    args = [*news, *rests, *blocks, kernels, growth, death, begun]
+    args = [*news, *rests, *blocks, own_b, kernels, growth, death, begun]
     return call(
         body, "before_second", args, outs, scratch=[pltpu.SemaphoreType.DMA((len(runs_of(chunks[-1])),))],
         specs=[SPEC] * (len(args) - 1) + [FROM_HBM], out_specs=[ANYWHERE] + [SPEC] * (len(outs) - 1), gflop=20.0,
@@ -293,12 +295,12 @@
     return lambda k, i: sums[k, pl.ds(i * ycount, ycount), :].astype(F32)
 
 
-def second_first(sums, base, new, death, blocks, kernels, cells, xcount):
+def second_first(sums, base, new, death, part, blocks, kernels, cells, xcount):
     _, ycount, owned = new.shape
     rows = blocks[0].shape[1]
     count = len(blocks)
 
-    def body(sums_ref, base_ref, new_ref, d_ref, k_ref, *refs):
+    def body(sums_ref, base_ref, new_ref, d_ref, begun_ref, k_ref, *refs):
         block_refs = refs[:count]
         out_ref, part_ref, held, sems = refs[count:]
         factor = SECOND / (1.0 + SECOND * d_ref[...])
@@ -308,12 +310,12 @@
         me = lax.axis_index("trait")
         values = [r[...].reshape(rows, owned) for r in block_refs]
         for k in range(2):
-            part_ref[k] = blocks_dot(values, k_ref, k, [me ^ j for j in range(count)])
+            part_ref[k] = begun_ref[k] + blocks_dot(values, k_ref, k, [me ^ (j + 1) for j in range(count)])
         for copy in copies:
             copy.wait()
 
     return call(
-        body, "second_first", [sums, base, new, death, kernels, *blocks],
+        body, "second_first", [sums, base, new, death, part, kernels, *blocks],
         [jax.ShapeDtypeStruct((xcount, ycount, owned), F32), pltpu.VMEM((2, rows, owned), F32)],
         scratch=[pltpu.VMEM((len(cells), ycount, owned), F32), pltpu.SemaphoreType.DMA((len(cells),))],
         out_specs=[ANYWHERE, SPEC],
@@ -407,8 +409,8 @@
     new_hi = from_above(after(new_head, rounded_b))
     nfar_a = after(nfar_a, rounded_b)
     nfarsib_a = to_sibling(nfar_a)
-    new_one, npart_a, nbase_a, nbase_b = before_second(
-        (new_a, new_b), (rest_a, rest_b), growth, death, new_one, [rounded_a, nsib_a, nfar_a], kernels, chunks
+    new_one, npart_a, npart_b, nbase_a, nbase_b = before_second(
+        (new_a, new_b), (rest_a, rest_b), growth, death, new_one, [rounded_a, nsib_a, nfar_a], rounded_b, kernels, chunks
     )
     sums_a = whole_sums(npart_a, nfarsib_a, after(kernels, nbase_a))
     nfar_b = after(nfar_b, sums_a, new_hi)
@@ -416,7 +418,7 @@
     placed = list(enumerate(chunks[0]))
     ends = [p for p in placed if p[1] in (0, xcount - 1)]
     begun, npart_b = second_first(
-        sums_a, nbase_a, new_a, death, [rounded_b, nsib_b, nfar_b], kernels, [p for p in placed if p not in ends], xcount
+        sums_a, nbase_a, new_a, death, npart_b, [nsib_b, nfar_b], kernels, [p for p in placed if p not in ends], xcount
     )
     new_two = second_last(
         sums_a, nbase_a, new_a, new_lo, new_hi, npart_b, nfarsib_b, nbase_b, new_b, death, kernels, begun, ends,

time: 42.7 us -> 42.7 us (level)
  transfers between devices with their start and end apart: 16 -> 16, of which waited for: 7 -> 6; matrix products, arithmetic and copies ran while one was open for 0% -> 0% of each run, Pallas kernels for 22% -> 22%
where the time goes in v17:
time: 42.7 us; the launch traced here: 42.5 us
  starting transfers between devices  17.5 us (41%)
  waiting for transfers between devices  12.6 us (30%)
  Pallas kernels  11.6 us (27%)
  between operations  0.79 us (2%)
    pallas_call x11, Pallas kernels, call(): pl.pallas_call(body, out_shape=outs, in_specs=specs, out_specs=out_specs...  11.6 us
    ppermute x2, starting transfers between devices, from_above(): lax.ppermute(head, 'gx', [((i + 1) % gcount, i) for i in range(gcount)])  6.73 us
    ppermute x2, waiting for transfers between devices, from_below(): lax.ppermute(tail, 'gx', [(i, (i + 1) % gcount) for i in range(gcount)])  6.57 us
    ppermute x4, starting transfers between devices, to_far(): return lax.ppermute(v, 'trait', [(i, i ^ 2) for i in range(traits)])  6.53 us
    ppermute x4, waiting for transfers between devices, to_far(): return lax.ppermute(v, 'trait', [(i, i ^ 2) for i in range(traits)])  4.53 us
    ppermute x2, starting transfers between devices, from_below(): lax.ppermute(tail, 'gx', [(i, (i + 1) % gcount) for i in range(gcount)])  3.62 us
    ppermute x2, waiting for transfers between devices, from_above(): lax.ppermute(head, 'gx', [((i + 1) % gcount, i) for i in range(gcount)])  1.17 us
  transfers between devices with their start and end apart: 16, of which 6 were waited for; matrix products, arithmetic and copies ran while one was open for 0% of the time, Pallas kernels for 22%

profile of v17, /device:TPU:0, one launch (start us, length us, event | category | flops | bytes accessed | tf_op | source)
XLA Modules:
  0.0 42.5 jit_solution(843052451115090401)
XLA Ops:
  0.6 1.3 %load_chunk.2 = (f32[5,128,256]{2,1,0:T(8,128)S(1)}, f32[5,128,256]{2,1,0:T(8,128)S(1)}, bf16[2,640,256]{2,1,0:T(8,128)(2,1)S(1)}, bf16[2,128,256]{2,1,0:T(8,128)(2,1)S(1)}, bf16[2,128,256]{2,1,0:T(8,128)(2,1)S(1)}) custom-call(f32[8,128,256]{2,1,0:T(8,128)} %refs_0_.2, f32[8,128,256]{2,1,0:T(8,128)} %refs_1_.3), custom_call_target="tpu_custom_call" | custom-call | tf_op jit(solution)/shard_map/load_chunk/pallas_call | solution.py:37
  2.0 0.0 copy-start.2
  2.0 3.0 %collective-permute-start.1 = (bf16[2,640,256]{2,1,0:T(8,128)(2,1)S(1)}, bf16[2,640,256]{2,1,0:T(8,128)(2,1)S(1)}, u32[]{:S(2)}, u32[]{:S(2)}) collective-permute-start(bf16[2,640,256]{2,1,0:T(8,128)(2,1)S(1)} %get-tuple-element.49.refs_0_), channel_id=1, source_target_pairs={{0,2},{1,3},{2,0},{3,1},{4,6},{5,7},{6,4},{7,5},{8,10},{9,11},{10,... | collective-permute-start | bytes 1966088 | tf_op jit(solution)/shard_map/ppermute | solution.py:372
  5.0 1.1 %load_chunk.3 = (f32[3,128,256]{2,1,0:T(8,128)S(1)}, f32[3,128,256]{2,1,0:T(8,128)S(1)}, bf16[2,384,256]{2,1,0:T(8,128)(2,1)S(1)}) custom-call(f32[8,128,256]{2,1,0:T(8,128)} %refs_0_.2, f32[8,128,256]{2,1,0:T(8,128)} %refs_1_.3), custom_call_target="tpu_custom_call" | custom-call | tf_op jit(solution)/shard_map/load_chunk/pallas_call | solution.py:37
  6.2 0.0 copy-start
  6.2 0.0 copy-start.1
  6.2 0.0 copy-start.3
  6.2 0.1 collective-permute-start
  6.3 1.5 %collective-permute-start.2 = (bf16[2,128,256]{2,1,0:T(8,128)(2,1)S(1)}, bf16[2,128,256]{2,1,0:T(8,128)(2,1)S(1)}, u32[]{:S(2)}, u32[]{:S(2)}) collective-permute-start(bf16[2,128,256]{2,1,0:T(8,128)(2,1)S(1)} %get-tuple-element.56), channel_id=1, source_target_pairs={{0,4},{4,8},{8,12},{12,16},{16,20},{20,24},{24,28},{28,0},{1,5},{5... | collective-permute-start | bytes 393224 | tf_op jit(solution)/shard_map/ppermute | solution.py:375
  7.8 3.2 %collective-permute-start.3 = (bf16[2,128,256]{2,1,0:T(8,128)(2,1)S(1)}, bf16[2,128,256]{2,1,0:T(8,128)(2,1)S(1)}, u32[]{:S(2)}, u32[]{:S(2)}) collective-permute-start(bf16[2,128,256]{2,1,0:T(8,128)(2,1)S(1)} %get-tuple-element.57), channel_id=1, source_target_pairs={{4,0},{8,4},{12,8},{16,12},{20,16},{24,20},{28,24},{0,28},{5,1},{9... | collective-permute-start | bytes 393224 | tf_op jit(solution)/shard_map/ppermute | solution.py:378
  11.1 0.4 collective-permute-start.6
  11.4 3.6 %collective-permute-done.2.refs_4_ = bf16[2,128,256]{2,1,0:T(8,128)(2,1)S(1)} collective-permute-done((bf16[2,128,256]{2,1,0:T(8,128)(2,1)S(1)}, bf16[2,128,256]{2,1,0:T(8,128)(2,1)S(1)}, u32[]{:S(2)}, u32[]{:S(2)}) %collective-permute-start.2) | collective-permute-done | bytes 131104 | tf_op jit(solution)/shard_map/ppermute | solution.py:375
  15.1 0.0 collective-permute-start.5
  15.1 1.1 %collective-permute-done.3.refs_5_ = bf16[2,128,256]{2,1,0:T(8,128)(2,1)S(1)} collective-permute-done((bf16[2,128,256]{2,1,0:T(8,128)(2,1)S(1)}, bf16[2,128,256]{2,1,0:T(8,128)(2,1)S(1)}, u32[]{:S(2)}, u32[]{:S(2)}) %collective-permute-start.3) | collective-permute-done | bytes 131104 | tf_op jit(solution)/shard_map/ppermute | solution.py:378
  16.2 0.0 copy-done.2
  16.2 0.9 %before_first.1 = (f32[2,5,128,256]{3,2,1,0:T(8,128)S(1)}, f32[2,3,128,256]{3,2,1,0:T(8,128)S(1)}) custom-call(f32[5,128,256]{2,1,0:T(8,128)S(1)} %get-tuple-element.50.refs_0_.refs_4_.one_ref, f32[3,128,256]{2,1,0:T(8,128)S(1)} %get-tuple-element.51.refs_1_.refs_4_.one_ref, f32[5,128,256]{2,1,0:T(8,128)S(1)} %get-tuple-element.52.refs_2_.refs_5_.two_ref, ...), custom_call_target="tpu_custom_call" | custom-call | tf_op jit(solution)/shard_map/before_first/pallas_call | solution.py:37
  17.1 3.5 %collective-permute-done.1.refs_2_ = bf16[2,640,256]{2,1,0:T(8,128)(2,1)S(1)} collective-permute-done((bf16[2,640,256]{2,1,0:T(8,128)(2,1)S(1)}, bf16[2,640,256]{2,1,0:T(8,128)(2,1)S(1)}, u32[]{:S(2)}, u32[]{:S(2)}) %collective-permute-start.1) | collective-permute-done | bytes 655392 | tf_op jit(solution)/shard_map/ppermute | solution.py:372
  20.6 0.0 collective-permute-start.4
  20.6 0.0 collective-permute-done.refs_1_
  20.6 1.8 %early_part.2 = (f32[2,1280,256]{2,1,0:T(8,128)S(1)}, f32[5,128,256]{2,1,0:T(8,128)S(1)}, f32[5,128,256]{2,1,0:T(8,128)S(1)}) custom-call(bf16[2,640,256]{2,1,0:T(8,128)(2,1)S(1)} %get-tuple-element.49.refs_0_, bf16[2,640,256]{2,1,0:T(8,128)(2,1)S(1)} %collective-permute-done.refs_1_, bf16[2,640,256]{2,1,0:T(8,128)(2,1)S(1)} %collective-permute-done.1.refs_2_, ...), custom_call_target="tpu_custom_call" | custom-call | flops 20000000000 | tf_op jit(solution)/shard_map/early_part/pallas_call | solution.py:37
  22.4 0.3 collective-permute-done.4.last_ref
  22.7 0.8 %first_node.2 = (f32[5,128,256]{2,1,0:T(8,128)S(1)}, bf16[1,640,256]{2,1,0:T(8,128)(2,1)S(1)}, f32[5,128,256]{2,1,0:T(8,128)S(1)}, bf16[1,128,256]{2,1,0:T(8,128)(2,1)S(1)}, bf16[1,128,256]{2,1,0:T(8,128)(2,1)S(1)}) custom-call(f32[2,1280,256]{2,1,0:T(8,128)S(1)} %get-tuple-element.61.part_ref, f32[5,128,256]{2,1,0:T(8,128)S(1)} %get-tuple-element.62.first_ref, ...), custom_call_target="tpu_custom_call" | custom-call | tf_op jit(solution)/shard_map/first_node/pallas_call | solution.py:37
  23.5 2.1 %collective-permute-start.7 = (bf16[1,128,256]{2,1,0:T(8,128)(2,1)S(1)}, bf16[1,128,256]{2,1,0:T(8,128)(2,1)S(1)}, u32[]{:S(2)}, u32[]{:S(2)}) collective-permute-start(bf16[1,128,256]{2,1,0:T(8,128)(2,1)S(1)} %get-tuple-element.68), channel_id=1, source_target_pairs={{0,4},{4,8},{8,12},{12,16},{16,20},{20,24},{24,28},{28,0},{1,5},{5... | collective-permute-start | bytes 196616 | tf_op jit(solution)/shard_map/ppermute | solution.py:375
  25.6 1.5 %collective-permute-start.10 = (bf16[1,640,256]{2,1,0:T(8,128)(2,1)S(1)}, bf16[1,640,256]{2,1,0:T(8,128)(2,1)S(1)}, u32[]{:S(2)}, u32[]{:S(2)}) collective-permute-start(bf16[1,640,256]{2,1,0:T(8,128)(2,1)S(1)} %get-tuple-element.65.refs_4_), channel_id=1, source_target_pairs={{0,2},{1,3},{2,0},{3,1},{4,6},{5,7},{6,4},{7,5},{8,10},{9,11},{10,... | collective-permute-start | bytes 983048 | tf_op jit(solution)/shard_map/ppermute | solution.py:372
  27.1 0.0 collective-permute-start.9
  27.1 1.1 %collective-permute-done.6.refs_2_ = bf16[2,384,256]{2,1,0:T(8,128)(2,1)S(1)} collective-permute-done((bf16[2,384,256]{2,1,0:T(8,128)(2,1)S(1)}, bf16[2,384,256]{2,1,0:T(8,128)(2,1)S(1)}, u32[]{:S(2)}, u32[]{:S(2)}) %collective-permute-start.6) | collective-permute-done | bytes 393248 | tf_op jit(solution)/shard_map/ppermute | solution.py:372
  28.2 0.0 collective-permute-start.8
  28.2 3.0 %collective-permute-done.7.refs_3_ = bf16[1,128,256]{2,1,0:T(8,128)(2,1)S(1)} collective-permute-done((bf16[1,128,256]{2,1,0:T(8,128)(2,1)S(1)}, bf16[1,128,256]{2,1,0:T(8,128)(2,1)S(1)}, u32[]{:S(2)}, u32[]{:S(2)}) %collective-permute-start.7) | collective-permute-done | bytes 65568 | tf_op jit(solution)/shard_map/ppermute | solution.py:375
  31.1 0.0 collective-permute-done.5.refs_1_
  31.1 1.1 %early_part.3 = (f32[2,768,256]{2,1,0:T(8,128)S(1)}, f32[3,128,256]{2,1,0:T(8,128)S(1)}, f32[3,128,256]{2,1,0:T(8,128)S(1)}, f32[8,128,256]{2,1,0:T(8,128)}) custom-call(bf16[2,384,256]{2,1,0:T(8,128)(2,1)S(1)} %get-tuple-element.48.refs_0_, bf16[2,384,256]{2,1,0:T(8,128)(2,1)S(1)} %collective-permute-done.5.refs_1_, ...), custom_call_target="tpu_custom_call" | custom-call | flops 20000000000 | tf_op jit(solution)/shard_map/early_part/pallas_call | solution.py:37
  32.3 0.0 collective-permute-done.8.last_ref
  32.3 0.6 %first_node.3 = (f32[3,128,256]{2,1,0:T(8,128)S(1)}, bf16[1,384,256]{2,1,0:T(8,128)(2,1)S(1)}, f32[3,128,256]{2,1,0:T(8,128)S(1)}) custom-call(f32[2,768,256]{2,1,0:T(8,128)S(1)} %get-tuple-element.70.part_ref, f32[3,128,256]{2,1,0:T(8,128)S(1)} %get-tuple-element.71.first_ref, f32[3,128,256]{2,1,0:T(8,128)S(1)} %get-tuple-element.72.begun_ref, ...), custom_call_target="tpu_custom_call" | custom-call | tf_op jit(solution)/shard_map/first_node/pallas_call | solution.py:37
  32.8 1.6 %collective-permute-start.14 = (bf16[1,384,256]{2,1,0:T(8,128)(2,1)S(1)}, bf16[1,384,256]{2,1,0:T(8,128)(2,1)S(1)}, u32[]{:S(2)}, u32[]{:S(2)}) collective-permute-start(bf16[1,384,256]{2,1,0:T(8,128)(2,1)S(1)} %get-tuple-element.76.refs_7_), channel_id=1, source_target_pairs={{0,2},{1,3},{2,0},{3,1},{4,6},{5,7},{6,4},{7,5},{8,10},{9,11},{10,... | collective-permute-start | bytes 589832 | tf_op jit(solution)/shard_map/ppermute | solution.py:372
  34.4 0.0 collective-permute-start.13
  34.4 3.5 %collective-permute-start.12 = (bf16[1,128,256]{2,1,0:T(8,128)(2,1)S(1)}, bf16[1,128,256]{2,1,0:T(8,128)(2,1)S(1)}, u32[]{:S(2)}, u32[]{:S(2)}) collective-permute-start(bf16[1,128,256]{2,1,0:T(8,128)(2,1)S(1)} %get-tuple-element.84), channel_id=1, source_target_pairs={{4,0},{8,4},{12,8},{16,12},{20,16},{24,20},{28,24},{0,28},{5,1},{9... | collective-permute-start | bytes 196616 | tf_op jit(solution)/shard_map/ppermute | solution.py:378
  37.9 0.0 collective-permute-done.10.refs_6_
  37.9 0.2 collective-permute-start.11
  38.2 0.0 collective-permute-done.9.refs_5_
  38.2 1.4 %before_second.1 = (f32[8,128,256]{2,1,0:T(8,128)}, f32[2,640,256]{2,1,0:T(8,128)S(1)}, f32[2,384,256]{2,1,0:T(8,128)S(1)}, f32[5,128,256]{2,1,0:T(8,128)S(1)}, f32[3,128,256]{2,1,0:T(8,128)S(1)}) custom-call(f32[5,128,256]{2,1,0:T(8,128)S(1)} %get-tuple-element.64.refs_9_.refs_0_.new_ref.refs_2_, ...), custom_call_target="tpu_custom_call", output_to_operand_aliasing={{0}: (11, {})} | custom-call | flops 20000000000 | tf_op jit(solution)/shard_map/before_second/pallas_call | solution.py:37
  39.6 0.0 collective-permute-done.11.last_ref
  39.6 0.3 whole_sums.1.sums_ref.refs_0_
  39.9 0.0 collective-permute-done.12.refs_4_
  40.0 0.0 collective-permute-done.14.refs_1_
  40.0 0.3 collective-permute-start.15
  40.3 0.0 collective-permute-done.13.refs_0_
  40.3 1.1 %second_first.1 = (f32[8,128,256]{2,1,0:T(8,128)}, f32[2,384,256]{2,1,0:T(8,128)S(1)}) custom-call(bf16[2,640,256]{2,1,0:T(8,128)(2,1)S(1)} %whole_sums.1.sums_ref.refs_0_, f32[5,128,256]{2,1,0:T(8,128)S(1)} %get-tuple-element.81.base_ref.refs_1_, f32[5,128,256]{2,1,0:T(8,128)S(1)} %get-tuple-element.64.refs_9_.refs_0_.new_ref.refs_2_, ...), custom_call_target="tpu_custom_call" | custom-call | tf_op jit(solution)/shard_map/second_first/pallas_call | solution.py:37
  41.4 0.0 collective-permute-done.15.refs_6_
  41.4 1.1 %second_last.1 = f32[8,128,256]{2,1,0:T(8,128)} custom-call(bf16[2,640,256]{2,1,0:T(8,128)(2,1)S(1)} %whole_sums.1.sums_ref.refs_0_, f32[5,128,256]{2,1,0:T(8,128)S(1)} %get-tuple-element.81.base_ref.refs_1_, f32[5,128,256]{2,1,0:T(8,128)S(1)} %get-tuple-element.64.refs_9_.refs_0_.new_ref.refs_2_, ...), custom_call_target="tpu_custom_call", output_to_operand_aliasing={{}: (11, {})} | custom-call | tf_op jit(solution)/shard_map/second_last/pallas_call | solution.py:37
  (3 shorter events, 0.0 us)
Async XLA Ops:
  2.0 14.2 %copy-start.2 = (f32[256]{0:T(256)S(1)}, f32[256]{0:T(256)}, u32[]{:S(2)}) copy-start(f32[256]{0:T(256)} %param.10) | copy-start | bytes 3076
  2.0 18.6 %collective-permute-start.1 = (bf16[2,640,256]{2,1,0:T(8,128)(2,1)S(1)}, bf16[2,640,256]{2,1,0:T(8,128)(2,1)S(1)}, u32[]{:S(2)}, u32[]{:S(2)}) collective-permute-start(bf16[2,640,256]{2,1,0:T(8,128)(2,1)S(1)} %get-tuple-element.49.refs_0_), channel_id=1, source_target_pairs={{0,2},{1,3},{2,0},{3,1},{4,6},{5,7},{6,4},{7,5},{8,10},{9,11},{10,... | collective-permute-start | bytes 1966088 | tf_op jit(solution)/shard_map/ppermute | solution.py:372
  6.2 14.4 %copy-start = (bf16[2,1024,256]{2,1,0:T(8,128)(2,1)S(1)}, bf16[2,1024,256]{2,1,0:T(8,128)(2,1)}, u32[]{:S(2)}) copy-start(bf16[2,1024,256]{2,1,0:T(8,128)(2,1)} %refs_10_) | copy-start | bytes 3145732
  6.2 14.4 %copy-start.1 = (f32[256]{0:T(256)S(1)}, f32[256]{0:T(256)}, u32[]{:S(2)}) copy-start(f32[256]{0:T(256)} %param.11) | copy-start | bytes 3076
  6.2 14.4 %copy-start.3 = (f32[8,128,256]{2,1,0:T(8,128)S(1)}, f32[8,128,256]{2,1,0:T(8,128)}, u32[]{:S(2)}) copy-start(f32[8,128,256]{2,1,0:T(8,128)} %refs_6_.3) | copy-start | bytes 3145732
  6.2 14.4 %collective-permute-start = (bf16[2,640,256]{2,1,0:T(8,128)(2,1)S(1)}, bf16[2,640,256]{2,1,0:T(8,128)(2,1)S(1)}, u32[]{:S(2)}, u32[]{:S(2)}) collective-permute-start(bf16[2,640,256]{2,1,0:T(8,128)(2,1)S(1)} %get-tuple-element.49.refs_0_), channel_id=1, source_target_pairs={{0,1},{1,0},{2,3},{3,2},{4,5},{5,4},{6,7},{7,6},{8,9},{9,8},{10,11... | collective-permute-start | bytes 1966088 | tf_op jit(solution)/shard_map/ppermute | solution.py:369
  6.3 8.8 %collective-permute-start.2 = (bf16[2,128,256]{2,1,0:T(8,128)(2,1)S(1)}, bf16[2,128,256]{2,1,0:T(8,128)(2,1)S(1)}, u32[]{:S(2)}, u32[]{:S(2)}) collective-permute-start(bf16[2,128,256]{2,1,0:T(8,128)(2,1)S(1)} %get-tuple-element.56), channel_id=1, source_target_pairs={{0,4},{4,8},{8,12},{12,16},{16,20},{20,24},{24,28},{28,0},{1,5},{5... | collective-permute-start | bytes 393224 | tf_op jit(solution)/shard_map/ppermute | solution.py:375
  7.8 8.4 %collective-permute-start.3 = (bf16[2,128,256]{2,1,0:T(8,128)(2,1)S(1)}, bf16[2,128,256]{2,1,0:T(8,128)(2,1)S(1)}, u32[]{:S(2)}, u32[]{:S(2)}) collective-permute-start(bf16[2,128,256]{2,1,0:T(8,128)(2,1)S(1)} %get-tuple-element.57), channel_id=1, source_target_pairs={{4,0},{8,4},{12,8},{16,12},{20,16},{24,20},{28,24},{0,28},{5,1},{9... | collective-permute-start | bytes 393224 | tf_op jit(solution)/shard_map/ppermute | solution.py:378
  11.1 17.1 %collective-permute-start.6 = (bf16[2,384,256]{2,1,0:T(8,128)(2,1)S(1)}, bf16[2,384,256]{2,1,0:T(8,128)(2,1)S(1)}, u32[]{:S(2)}, u32[]{:S(2)}) collective-permute-start(bf16[2,384,256]{2,1,0:T(8,128)(2,1)S(1)} %get-tuple-element.48.refs_0_), channel_id=1, source_target_pairs={{0,2},{1,3},{2,0},{3,1},{4,6},{5,7},{6,4},{7,5},{8,10},{9,11},{10,... | collective-permute-start | bytes 1179656 | tf_op jit(solution)/shard_map/ppermute | solution.py:372
  15.1 16.1 %collective-permute-start.5 = (bf16[2,384,256]{2,1,0:T(8,128)(2,1)S(1)}, bf16[2,384,256]{2,1,0:T(8,128)(2,1)S(1)}, u32[]{:S(2)}, u32[]{:S(2)}) collective-permute-start(bf16[2,384,256]{2,1,0:T(8,128)(2,1)S(1)} %get-tuple-element.48.refs_0_), channel_id=1, source_target_pairs={{0,1},{1,0},{2,3},{3,2},{4,5},{5,4},{6,7},{7,6},{8,9},{9,8},{10,11... | collective-permute-start | bytes 1179656 | tf_op jit(solution)/shard_map/ppermute | solution.py:369
  20.6 2.1 %collective-permute-start.4 = (bf16[2,640,256]{2,1,0:T(8,128)(2,1)S(1)}, bf16[2,640,256]{2,1,0:T(8,128)(2,1)S(1)}, u32[]{:S(2)}, u32[]{:S(2)}) collective-permute-start(bf16[2,640,256]{2,1,0:T(8,128)(2,1)S(1)} %collective-permute-done.1.refs_2_), channel_id=1, source_target_pairs={{0,1},{1,0},{2,3},{3,2},{4,5},{5,4},{6,7},{7,6},{8,9},{9,8},{10,11... | collective-permute-start | bytes 1966088 | tf_op jit(solution)/shard_map/ppermute | solution.py:369
  23.5 7.6 %collective-permute-start.7 = (bf16[1,128,256]{2,1,0:T(8,128)(2,1)S(1)}, bf16[1,128,256]{2,1,0:T(8,128)(2,1)S(1)}, u32[]{:S(2)}, u32[]{:S(2)}) collective-permute-start(bf16[1,128,256]{2,1,0:T(8,128)(2,1)S(1)} %get-tuple-element.68), channel_id=1, source_target_pairs={{0,4},{4,8},{8,12},{12,16},{16,20},{20,24},{24,28},{28,0},{1,5},{5... | collective-permute-start | bytes 196616 | tf_op jit(solution)/shard_map/ppermute | solution.py:375
  25.6 12.4 %collective-permute-start.10 = (bf16[1,640,256]{2,1,0:T(8,128)(2,1)S(1)}, bf16[1,640,256]{2,1,0:T(8,128)(2,1)S(1)}, u32[]{:S(2)}, u32[]{:S(2)}) collective-permute-start(bf16[1,640,256]{2,1,0:T(8,128)(2,1)S(1)} %get-tuple-element.65.refs_4_), channel_id=1, source_target_pairs={{0,2},{1,3},{2,0},{3,1},{4,6},{5,7},{6,4},{7,5},{8,10},{9,11},{10,... | collective-permute-start | bytes 983048 | tf_op jit(solution)/shard_map/ppermute | solution.py:372
  27.1 11.1 %collective-permute-start.9 = (bf16[1,640,256]{2,1,0:T(8,128)(2,1)S(1)}, bf16[1,640,256]{2,1,0:T(8,128)(2,1)S(1)}, u32[]{:S(2)}, u32[]{:S(2)}) collective-permute-start(bf16[1,640,256]{2,1,0:T(8,128)(2,1)S(1)} %get-tuple-element.65.refs_4_), channel_id=1, source_target_pairs={{0,1},{1,0},{2,3},{3,2},{4,5},{5,4},{6,7},{7,6},{8,9},{9,8},{10,11... | collective-permute-start | bytes 983048 | tf_op jit(solution)/shard_map/ppermute | solution.py:369
  28.2 4.1 %collective-permute-start.8 = (bf16[2,384,256]{2,1,0:T(8,128)(2,1)S(1)}, bf16[2,384,256]{2,1,0:T(8,128)(2,1)S(1)}, u32[]{:S(2)}, u32[]{:S(2)}) collective-permute-start(bf16[2,384,256]{2,1,0:T(8,128)(2,1)S(1)} %collective-permute-done.6.refs_2_), channel_id=1, source_target_pairs={{0,1},{1,0},{2,3},{3,2},{4,5},{5,4},{6,7},{7,6},{8,9},{9,8},{10,11... | collective-permute-start | bytes 1179656 | tf_op jit(solution)/shard_map/ppermute | solution.py:369
  32.8 7.1 %collective-permute-start.14 = (bf16[1,384,256]{2,1,0:T(8,128)(2,1)S(1)}, bf16[1,384,256]{2,1,0:T(8,128)(2,1)S(1)}, u32[]{:S(2)}, u32[]{:S(2)}) collective-permute-start(bf16[1,384,256]{2,1,0:T(8,128)(2,1)S(1)} %get-tuple-element.76.refs_7_), channel_id=1, source_target_pairs={{0,2},{1,3},{2,0},{3,1},{4,6},{5,7},{6,4},{7,5},{8,10},{9,11},{10,... | collective-permute-start | bytes 589832 | tf_op jit(solution)/shard_map/ppermute | solution.py:372
  34.4 5.9 %collective-permute-start.13 = (bf16[1,384,256]{2,1,0:T(8,128)(2,1)S(1)}, bf16[1,384,256]{2,1,0:T(8,128)(2,1)S(1)}, u32[]{:S(2)}, u32[]{:S(2)}) collective-permute-start(bf16[1,384,256]{2,1,0:T(8,128)(2,1)S(1)} %get-tuple-element.76.refs_7_), channel_id=1, source_target_pairs={{0,1},{1,0},{2,3},{3,2},{4,5},{5,4},{6,7},{7,6},{8,9},{9,8},{10,11... | collective-permute-start | bytes 589832 | tf_op jit(solution)/shard_map/ppermute | solution.py:369
  34.4 5.5 %collective-permute-start.12 = (bf16[1,128,256]{2,1,0:T(8,128)(2,1)S(1)}, bf16[1,128,256]{2,1,0:T(8,128)(2,1)S(1)}, u32[]{:S(2)}, u32[]{:S(2)}) collective-permute-start(bf16[1,128,256]{2,1,0:T(8,128)(2,1)S(1)} %get-tuple-element.84), channel_id=1, source_target_pairs={{4,0},{8,4},{12,8},{16,12},{20,16},{24,20},{28,24},{0,28},{5,1},{9... | collective-permute-start | bytes 196616 | tf_op jit(solution)/shard_map/ppermute | solution.py:378
  37.9 1.6 %collective-permute-start.11 = (bf16[1,640,256]{2,1,0:T(8,128)(2,1)S(1)}, bf16[1,640,256]{2,1,0:T(8,128)(2,1)S(1)}, u32[]{:S(2)}, u32[]{:S(2)}) collective-permute-start(bf16[1,640,256]{2,1,0:T(8,128)(2,1)S(1)} %collective-permute-done.10.refs_6_), channel_id=1, source_target_pairs={{0,1},{1,0},{2,3},{3,2},{4,5},{5,4},{6,7},{7,6},{8,9},{9,8},{10,11... | collective-permute-start | bytes 983048 | tf_op jit(solution)/shard_map/ppermute | solution.py:369
  40.0 1.5 %collective-permute-start.15 = (bf16[1,384,256]{2,1,0:T(8,128)(2,1)S(1)}, bf16[1,384,256]{2,1,0:T(8,128)(2,1)S(1)}, u32[]{:S(2)}, u32[]{:S(2)}) collective-permute-start(bf16[1,384,256]{2,1,0:T(8,128)(2,1)S(1)} %collective-permute-done.14.refs_1_), channel_id=1, source_target_pairs={{0,1},{1,0},{2,3},{3,2},{4,5},{5,4},{6,7},{7,6},{8,9},{9,8},{10,11... | collective-permute-start | bytes 589832 | tf_op jit(solution)/shard_map/ppermute | solution.py:369

commit v18 on v15

--- a/solution.py
+++ b/solution.py
@@ -18,7 +18,7 @@
 
 
 def chunks_of(xcount):
-    last = max(1, 3 * xcount // 8)
+    last = max(1, xcount // 2)
     start = (xcount - last + 1) // 2
     middle = list(range(start, start + last))
     return [x for x in range(xcount) if x not in middle], middle

time: 42.7 us -> 43.1 us (level)
  starting transfers between devices: 17.5 us -> 18.9 us
  waiting for transfers between devices: 12.7 us -> 11.7 us
    ppermute x2, waiting for transfers between devices: 6.57 us -> 3.58 us  [from_below(): lax.ppermute(tail, 'gx', [(i, (i + 1) % gcount) for i in range(gcount)])]
    ppermute x4, waiting for transfers between devices: 4.53 us -> 5.67 us  [to_far(): return lax.ppermute(v, 'trait', [(i, i ^ 2) for i in range(traits)])]
    ppermute x2, starting transfers between devices: 6.72 us -> 7.76 us  [from_above(): lax.ppermute(head, 'gx', [((i + 1) % gcount, i) for i in range(gcount)])]
    ppermute x8, waiting for transfers between devices: 0.37 us -> 1.14 us  [to_sibling(): return lax.ppermute(v, 'trait', [(i, i ^ 1) for i in range(traits)])]
    ppermute x4, starting transfers between devices: 6.54 us -> 7.11 us  [to_far(): return lax.ppermute(v, 'trait', [(i, i ^ 2) for i in range(traits)])]
  transfers between devices with their start and end apart: 16 -> 16, of which waited for: 7 -> 10; matrix products, arithmetic and copies ran while one was open for 0% -> 0% of each run, Pallas kernels for 22% -> 21%
where the time goes in v18:
time: 43.1 us; the launch traced here: 42.9 us
  starting transfers between devices  18.9 us (44%)
  waiting for transfers between devices  11.7 us (27%)
  Pallas kernels  11.6 us (27%)
  between operations  0.78 us (2%)
    pallas_call x11, Pallas kernels, call(): pl.pallas_call(body, out_shape=outs, in_specs=specs, out_specs=out_specs...  11.6 us
    ppermute x2, starting transfers between devices, from_above(): lax.ppermute(head, 'gx', [((i + 1) % gcount, i) for i in range(gcount)])  7.76 us
    ppermute x4, starting transfers between devices, to_far(): return lax.ppermute(v, 'trait', [(i, i ^ 2) for i in range(traits)])  7.11 us
    ppermute x4, waiting for transfers between devices, to_far(): return lax.ppermute(v, 'trait', [(i, i ^ 2) for i in range(traits)])  5.67 us
    ppermute x2, starting transfers between devices, from_below(): lax.ppermute(tail, 'gx', [(i, (i + 1) % gcount) for i in range(gcount)])  3.62 us
    ppermute x2, waiting for transfers between devices, from_below(): lax.ppermute(tail, 'gx', [(i, (i + 1) % gcount) for i in range(gcount)])  3.58 us
    ppermute x2, waiting for transfers between devices, from_above(): lax.ppermute(head, 'gx', [((i + 1) % gcount, i) for i in range(gcount)])  1.3 us
    ppermute x8, waiting for transfers between devices, to_sibling(): return lax.ppermute(v, 'trait', [(i, i ^ 1) for i in range(traits)])  1.14 us
  transfers between devices with their start and end apart: 16, of which 10 were waited for; matrix products, arithmetic and copies ran while one was open for 0% of the time, Pallas kernels for 21%

profile of v18, /device:TPU:0, one launch (start us, length us, event | category | flops | bytes accessed | tf_op | source)
XLA Modules:
  0.0 42.9 jit_solution(8345132049242531185)
XLA Ops:
  0.6 1.2 %load_chunk.2 = (f32[4,128,256]{2,1,0:T(8,128)S(1)}, f32[4,128,256]{2,1,0:T(8,128)S(1)}, bf16[2,512,256]{2,1,0:T(8,128)(2,1)S(1)}, bf16[2,128,256]{2,1,0:T(8,128)(2,1)S(1)}, bf16[2,128,256]{2,1,0:T(8,128)(2,1)S(1)}) custom-call(f32[8,128,256]{2,1,0:T(8,128)} %refs_0_.2, f32[8,128,256]{2,1,0:T(8,128)} %refs_1_.3), custom_call_target="tpu_custom_call" | custom-call | tf_op jit(solution)/shard_map/load_chunk/pallas_call | solution.py:37
  1.9 0.0 copy-start
  1.9 0.0 copy-start.1
  1.9 0.0 copy-start.3
  1.9 3.0 %collective-permute-start.1 = (bf16[2,512,256]{2,1,0:T(8,128)(2,1)S(1)}, bf16[2,512,256]{2,1,0:T(8,128)(2,1)S(1)}, u32[]{:S(2)}, u32[]{:S(2)}) collective-permute-start(bf16[2,512,256]{2,1,0:T(8,128)(2,1)S(1)} %get-tuple-element.48.refs_0_), channel_id=1, source_target_pairs={{0,2},{1,3},{2,0},{3,1},{4,6},{5,7},{6,4},{7,5},{8,10},{9,11},{10,... | collective-permute-start | bytes 1572872 | tf_op jit(solution)/shard_map/ppermute | solution.py:370
  5.0 1.2 %load_chunk.3 = (f32[4,128,256]{2,1,0:T(8,128)S(1)}, f32[4,128,256]{2,1,0:T(8,128)S(1)}, bf16[2,512,256]{2,1,0:T(8,128)(2,1)S(1)}) custom-call(f32[8,128,256]{2,1,0:T(8,128)} %refs_0_.2, f32[8,128,256]{2,1,0:T(8,128)} %refs_1_.3), custom_call_target="tpu_custom_call" | custom-call | tf_op jit(solution)/shard_map/load_chunk/pallas_call | solution.py:37
  6.2 0.1 collective-permute-start
  6.3 1.5 %collective-permute-start.2 = (bf16[2,128,256]{2,1,0:T(8,128)(2,1)S(1)}, bf16[2,128,256]{2,1,0:T(8,128)(2,1)S(1)}, u32[]{:S(2)}, u32[]{:S(2)}) collective-permute-start(bf16[2,128,256]{2,1,0:T(8,128)(2,1)S(1)} %get-tuple-element.55), channel_id=1, source_target_pairs={{0,4},{4,8},{8,12},{12,16},{16,20},{20,24},{24,28},{28,0},{1,5},{5... | collective-permute-start | bytes 393224 | tf_op jit(solution)/shard_map/ppermute | solution.py:373
  7.8 3.2 %collective-permute-start.3 = (bf16[2,128,256]{2,1,0:T(8,128)(2,1)S(1)}, bf16[2,128,256]{2,1,0:T(8,128)(2,1)S(1)}, u32[]{:S(2)}, u32[]{:S(2)}) collective-permute-start(bf16[2,128,256]{2,1,0:T(8,128)(2,1)S(1)} %get-tuple-element.56), channel_id=1, source_target_pairs={{4,0},{8,4},{12,8},{16,12},{20,16},{24,20},{28,24},{0,28},{5,1},{9... | collective-permute-start | bytes 393224 | tf_op jit(solution)/shard_map/ppermute | solution.py:376
  11.1 0.4 %collective-permute-start.6 = (bf16[2,512,256]{2,1,0:T(8,128)(2,1)S(1)}, bf16[2,512,256]{2,1,0:T(8,128)(2,1)S(1)}, u32[]{:S(2)}, u32[]{:S(2)}) collective-permute-start(bf16[2,512,256]{2,1,0:T(8,128)(2,1)S(1)} %get-tuple-element.47.refs_0_), channel_id=1, source_target_pairs={{0,2},{1,3},{2,0},{3,1},{4,6},{5,7},{6,4},{7,5},{8,10},{9,11},{10,... | collective-permute-start | bytes 1572872 | tf_op jit(solution)/shard_map/ppermute | solution.py:370
  11.5 3.6 %collective-permute-done.2.refs_4_ = bf16[2,128,256]{2,1,0:T(8,128)(2,1)S(1)} collective-permute-done((bf16[2,128,256]{2,1,0:T(8,128)(2,1)S(1)}, bf16[2,128,256]{2,1,0:T(8,128)(2,1)S(1)}, u32[]{:S(2)}, u32[]{:S(2)}) %collective-permute-start.2) | collective-permute-done | bytes 131104 | tf_op jit(solution)/shard_map/ppermute | solution.py:373
  15.1 0.0 collective-permute-start.5
  15.1 1.1 %collective-permute-done.3.refs_5_ = bf16[2,128,256]{2,1,0:T(8,128)(2,1)S(1)} collective-permute-done((bf16[2,128,256]{2,1,0:T(8,128)(2,1)S(1)}, bf16[2,128,256]{2,1,0:T(8,128)(2,1)S(1)}, u32[]{:S(2)}, u32[]{:S(2)}) %collective-permute-start.3) | collective-permute-done | bytes 131104 | tf_op jit(solution)/shard_map/ppermute | solution.py:376
  16.2 0.9 %before_first.1 = (f32[2,4,128,256]{3,2,1,0:T(8,128)S(1)}, f32[2,4,128,256]{3,2,1,0:T(8,128)S(1)}) custom-call(f32[4,128,256]{2,1,0:T(8,128)S(1)} %get-tuple-element.49.refs_0_.refs_4_.one_ref, f32[4,128,256]{2,1,0:T(8,128)S(1)} %get-tuple-element.50.refs_1_.refs_4_.one_ref, f32[4,128,256]{2,1,0:T(8,128)S(1)} %get-tuple-element.51.refs_2_.refs_5_.two_ref, ...), custom_call_target="tpu_custom_call" | custom-call | tf_op jit(solution)/shard_map/before_first/pallas_call | solution.py:37
  17.1 0.6 %collective-permute-done.1.refs_2_ = bf16[2,512,256]{2,1,0:T(8,128)(2,1)S(1)} collective-permute-done((bf16[2,512,256]{2,1,0:T(8,128)(2,1)S(1)}, bf16[2,512,256]{2,1,0:T(8,128)(2,1)S(1)}, u32[]{:S(2)}, u32[]{:S(2)}) %collective-permute-start.1) | collective-permute-done | bytes 524320 | tf_op jit(solution)/shard_map/ppermute | solution.py:370
  17.7 0.0 collective-permute-start.4
  17.7 0.0 collective-permute-done.refs_1_
  17.7 0.0 copy-done.1
  17.7 0.0 copy-done.3
  17.7 1.4 %early_part.2 = (f32[2,1024,256]{2,1,0:T(8,128)S(1)}, f32[4,128,256]{2,1,0:T(8,128)S(1)}, f32[4,128,256]{2,1,0:T(8,128)S(1)}) custom-call(bf16[2,512,256]{2,1,0:T(8,128)(2,1)S(1)} %get-tuple-element.48.refs_0_, bf16[2,512,256]{2,1,0:T(8,128)(2,1)S(1)} %collective-permute-done.refs_1_, bf16[2,512,256]{2,1,0:T(8,128)(2,1)S(1)} %collective-permute-done.1.refs_2_, ...), custom_call_target="tpu_custom_call" | custom-call | flops 20000000000 | tf_op jit(solution)/shard_map/early_part/pallas_call | solution.py:37
  19.2 0.4 collective-permute-done.4.last_ref
  19.6 0.7 %first_node.2 = (f32[4,128,256]{2,1,0:T(8,128)S(1)}, bf16[1,512,256]{2,1,0:T(8,128)(2,1)S(1)}, f32[4,128,256]{2,1,0:T(8,128)S(1)}, bf16[1,128,256]{2,1,0:T(8,128)(2,1)S(1)}, bf16[1,128,256]{2,1,0:T(8,128)(2,1)S(1)}) custom-call(f32[2,1024,256]{2,1,0:T(8,128)S(1)} %get-tuple-element.60.part_ref, f32[4,128,256]{2,1,0:T(8,128)S(1)} %get-tuple-element.61.first_ref, ...), custom_call_target="tpu_custom_call" | custom-call | tf_op jit(solution)/shard_map/first_node/pallas_call | solution.py:37
  20.3 2.1 %collective-permute-start.7 = (bf16[1,128,256]{2,1,0:T(8,128)(2,1)S(1)}, bf16[1,128,256]{2,1,0:T(8,128)(2,1)S(1)}, u32[]{:S(2)}, u32[]{:S(2)}) collective-permute-start(bf16[1,128,256]{2,1,0:T(8,128)(2,1)S(1)} %get-tuple-element.67), channel_id=1, source_target_pairs={{0,4},{4,8},{8,12},{12,16},{16,20},{20,24},{24,28},{28,0},{1,5},{5... | collective-permute-start | bytes 196616 | tf_op jit(solution)/shard_map/ppermute | solution.py:373
  22.4 1.5 %collective-permute-start.10 = (bf16[1,512,256]{2,1,0:T(8,128)(2,1)S(1)}, bf16[1,512,256]{2,1,0:T(8,128)(2,1)S(1)}, u32[]{:S(2)}, u32[]{:S(2)}) collective-permute-start(bf16[1,512,256]{2,1,0:T(8,128)(2,1)S(1)} %get-tuple-element.64.refs_4_), channel_id=1, source_target_pairs={{0,2},{1,3},{2,0},{3,1},{4,6},{5,7},{6,4},{7,5},{8,10},{9,11},{10,... | collective-permute-start | bytes 786440 | tf_op jit(solution)/shard_map/ppermute | solution.py:370
  23.9 0.0 collective-permute-start.9
  23.9 5.0 %collective-permute-done.6.refs_2_ = bf16[2,512,256]{2,1,0:T(8,128)(2,1)S(1)} collective-permute-done((bf16[2,512,256]{2,1,0:T(8,128)(2,1)S(1)}, bf16[2,512,256]{2,1,0:T(8,128)(2,1)S(1)}, u32[]{:S(2)}, u32[]{:S(2)}) %collective-permute-start.6) | collective-permute-done | bytes 524320 | tf_op jit(solution)/shard_map/ppermute | solution.py:370
  28.9 0.0 collective-permute-start.8
  28.9 0.0 collective-permute-done.7.refs_3_
  29.0 0.0 collective-permute-done.5.refs_1_
  29.0 1.5 %early_part.3 = (f32[2,1024,256]{2,1,0:T(8,128)S(1)}, f32[4,128,256]{2,1,0:T(8,128)S(1)}, f32[4,128,256]{2,1,0:T(8,128)S(1)}, f32[8,128,256]{2,1,0:T(8,128)}) custom-call(bf16[2,512,256]{2,1,0:T(8,128)(2,1)S(1)} %get-tuple-element.47.refs_0_, bf16[2,512,256]{2,1,0:T(8,128)(2,1)S(1)} %collective-permute-done.5.refs_1_, ...), custom_call_target="tpu_custom_call" | custom-call | flops 20000000000 | tf_op jit(solution)/shard_map/early_part/pallas_call | solution.py:37
  30.4 0.4 collective-permute-done.8.last_ref
  30.9 0.7 %first_node.3 = (f32[4,128,256]{2,1,0:T(8,128)S(1)}, bf16[1,512,256]{2,1,0:T(8,128)(2,1)S(1)}, f32[4,128,256]{2,1,0:T(8,128)S(1)}) custom-call(f32[2,1024,256]{2,1,0:T(8,128)S(1)} %get-tuple-element.69.part_ref, f32[4,128,256]{2,1,0:T(8,128)S(1)} %get-tuple-element.70.first_ref, f32[4,128,256]{2,1,0:T(8,128)S(1)} %get-tuple-element.71.begun_ref, ...), custom_call_target="tpu_custom_call" | custom-call | tf_op jit(solution)/shard_map/first_node/pallas_call | solution.py:37
  31.6 2.1 %collective-permute-start.14 = (bf16[1,512,256]{2,1,0:T(8,128)(2,1)S(1)}, bf16[1,512,256]{2,1,0:T(8,128)(2,1)S(1)}, u32[]{:S(2)}, u32[]{:S(2)}) collective-permute-start(bf16[1,512,256]{2,1,0:T(8,128)(2,1)S(1)} %get-tuple-element.75.refs_0_), channel_id=1, source_target_pairs={{0,2},{1,3},{2,0},{3,1},{4,6},{5,7},{6,4},{7,5},{8,10},{9,11},{10,... | collective-permute-start | bytes 786440 | tf_op jit(solution)/shard_map/ppermute | solution.py:370
  33.7 0.0 collective-permute-start.13
  33.7 4.5 %collective-permute-start.12 = (bf16[1,128,256]{2,1,0:T(8,128)(2,1)S(1)}, bf16[1,128,256]{2,1,0:T(8,128)(2,1)S(1)}, u32[]{:S(2)}, u32[]{:S(2)}) collective-permute-start(bf16[1,128,256]{2,1,0:T(8,128)(2,1)S(1)} %get-tuple-element.83), channel_id=1, source_target_pairs={{4,0},{8,4},{12,8},{16,12},{20,16},{24,20},{28,24},{0,28},{5,1},{9... | collective-permute-start | bytes 196616 | tf_op jit(solution)/shard_map/ppermute | solution.py:376
  38.2 0.0 collective-permute-done.10.refs_6_
  38.2 0.2 collective-permute-start.11
  38.4 0.0 collective-permute-done.9.refs_5_
  38.4 1.2 %before_second.1 = (f32[8,128,256]{2,1,0:T(8,128)}, f32[2,512,256]{2,1,0:T(8,128)S(1)}, f32[4,128,256]{2,1,0:T(8,128)S(1)}, f32[4,128,256]{2,1,0:T(8,128)S(1)}) custom-call(f32[4,128,256]{2,1,0:T(8,128)S(1)} %get-tuple-element.63.refs_9_.refs_0_.new_ref.refs_2_, ...), custom_call_target="tpu_custom_call", output_to_operand_aliasing={{0}: (10, {})} | custom-call | flops 20000000000 | tf_op jit(solution)/shard_map/before_second/pallas_call | solution.py:37
  39.7 0.1 collective-permute-done.11.last_ref
  39.8 0.3 whole_sums.1.sums_ref.refs_0_
  40.1 0.2 collective-permute-done.12.refs_4_
  40.2 0.1 collective-permute-done.14.refs_2_
  40.3 0.1 collective-permute-start.15
  40.4 0.0 collective-permute-done.13.refs_1_
  40.4 1.2 %second_first.1 = (f32[8,128,256]{2,1,0:T(8,128)}, f32[2,512,256]{2,1,0:T(8,128)S(1)}) custom-call(bf16[2,512,256]{2,1,0:T(8,128)(2,1)S(1)} %whole_sums.1.sums_ref.refs_0_, f32[4,128,256]{2,1,0:T(8,128)S(1)} %get-tuple-element.80.base_ref.refs_1_, f32[4,128,256]{2,1,0:T(8,128)S(1)} %get-tuple-element.63.refs_9_.refs_0_.new_ref.refs_2_, ...), custom_call_target="tpu_custom_call" | custom-call | tf_op jit(solution)/shard_map/second_first/pallas_call | solution.py:37
  41.6 0.2 collective-permute-done.15.refs_6_
  41.8 1.1 %second_last.1 = f32[8,128,256]{2,1,0:T(8,128)} custom-call(bf16[2,512,256]{2,1,0:T(8,128)(2,1)S(1)} %whole_sums.1.sums_ref.refs_0_, f32[4,128,256]{2,1,0:T(8,128)S(1)} %get-tuple-element.80.base_ref.refs_1_, f32[4,128,256]{2,1,0:T(8,128)S(1)} %get-tuple-element.63.refs_9_.refs_0_.new_ref.refs_2_, ...), custom_call_target="tpu_custom_call", output_to_operand_aliasing={{}: (11, {})} | custom-call | tf_op jit(solution)/shard_map/second_last/pallas_call | solution.py:37
  (3 shorter events, 0.0 us)
Async XLA Ops:
  0.6 15.6 %copy-start.2 = (f32[256]{0:T(256)S(1)}, f32[256]{0:T(256)}, u32[]{:S(2)}) copy-start(f32[256]{0:T(256)} %param.10) | copy-start | bytes 3076
  1.9 15.8 %copy-start = (bf16[2,1024,256]{2,1,0:T(8,128)(2,1)S(1)}, bf16[2,1024,256]{2,1,0:T(8,128)(2,1)}, u32[]{:S(2)}) copy-start(bf16[2,1024,256]{2,1,0:T(8,128)(2,1)} %refs_10_) | copy-start | bytes 3145732
  1.9 15.8 %copy-start.1 = (f32[256]{0:T(256)S(1)}, f32[256]{0:T(256)}, u32[]{:S(2)}) copy-start(f32[256]{0:T(256)} %param.11) | copy-start | bytes 3076
  1.9 15.8 %copy-start.3 = (f32[8,128,256]{2,1,0:T(8,128)S(1)}, f32[8,128,256]{2,1,0:T(8,128)}, u32[]{:S(2)}) copy-start(f32[8,128,256]{2,1,0:T(8,128)} %refs_6_.3) | copy-start | bytes 3145732
  1.9 15.8 %collective-permute-start.1 = (bf16[2,512,256]{2,1,0:T(8,128)(2,1)S(1)}, bf16[2,512,256]{2,1,0:T(8,128)(2,1)S(1)}, u32[]{:S(2)}, u32[]{:S(2)}) collective-permute-start(bf16[2,512,256]{2,1,0:T(8,128)(2,1)S(1)} %get-tuple-element.48.refs_0_), channel_id=1, source_target_pairs={{0,2},{1,3},{2,0},{3,1},{4,6},{5,7},{6,4},{7,5},{8,10},{9,11},{10,... | collective-permute-start | bytes 1572872 | tf_op jit(solution)/shard_map/ppermute | solution.py:370
  6.2 11.5 %collective-permute-start = (bf16[2,512,256]{2,1,0:T(8,128)(2,1)S(1)}, bf16[2,512,256]{2,1,0:T(8,128)(2,1)S(1)}, u32[]{:S(2)}, u32[]{:S(2)}) collective-permute-start(bf16[2,512,256]{2,1,0:T(8,128)(2,1)S(1)} %get-tuple-element.48.refs_0_), channel_id=1, source_target_pairs={{0,1},{1,0},{2,3},{3,2},{4,5},{5,4},{6,7},{7,6},{8,9},{9,8},{10,11... | collective-permute-start | bytes 1572872 | tf_op jit(solution)/shard_map/ppermute | solution.py:367
  6.3 8.8 %collective-permute-start.2 = (bf16[2,128,256]{2,1,0:T(8,128)(2,1)S(1)}, bf16[2,128,256]{2,1,0:T(8,128)(2,1)S(1)}, u32[]{:S(2)}, u32[]{:S(2)}) collective-permute-start(bf16[2,128,256]{2,1,0:T(8,128)(2,1)S(1)} %get-tuple-element.55), channel_id=1, source_target_pairs={{0,4},{4,8},{8,12},{12,16},{16,20},{20,24},{24,28},{28,0},{1,5},{5... | collective-permute-start | bytes 393224 | tf_op jit(solution)/shard_map/ppermute | solution.py:373
  7.8 8.4 %collective-permute-start.3 = (bf16[2,128,256]{2,1,0:T(8,128)(2,1)S(1)}, bf16[2,128,256]{2,1,0:T(8,128)(2,1)S(1)}, u32[]{:S(2)}, u32[]{:S(2)}) collective-permute-start(bf16[2,128,256]{2,1,0:T(8,128)(2,1)S(1)} %get-tuple-element.56), channel_id=1, source_target_pairs={{4,0},{8,4},{12,8},{16,12},{20,16},{24,20},{28,24},{0,28},{5,1},{9... | collective-permute-start | bytes 393224 | tf_op jit(solution)/shard_map/ppermute | solution.py:376
  11.1 17.9 %collective-permute-start.6 = (bf16[2,512,256]{2,1,0:T(8,128)(2,1)S(1)}, bf16[2,512,256]{2,1,0:T(8,128)(2,1)S(1)}, u32[]{:S(2)}, u32[]{:S(2)}) collective-permute-start(bf16[2,512,256]{2,1,0:T(8,128)(2,1)S(1)} %get-tuple-element.47.refs_0_), channel_id=1, source_target_pairs={{0,2},{1,3},{2,0},{3,1},{4,6},{5,7},{6,4},{7,5},{8,10},{9,11},{10,... | collective-permute-start | bytes 1572872 | tf_op jit(solution)/shard_map/ppermute | solution.py:370
  15.1 13.9 %collective-permute-start.5 = (bf16[2,512,256]{2,1,0:T(8,128)(2,1)S(1)}, bf16[2,512,256]{2,1,0:T(8,128)(2,1)S(1)}, u32[]{:S(2)}, u32[]{:S(2)}) collective-permute-start(bf16[2,512,256]{2,1,0:T(8,128)(2,1)S(1)} %get-tuple-element.47.refs_0_), channel_id=1, source_target_pairs={{0,1},{1,0},{2,3},{3,2},{4,5},{5,4},{6,7},{7,6},{8,9},{9,8},{10,11... | collective-permute-start | bytes 1572872 | tf_op jit(solution)/shard_map/ppermute | solution.py:367
  17.7 1.9 %collective-permute-start.4 = (bf16[2,512,256]{2,1,0:T(8,128)(2,1)S(1)}, bf16[2,512,256]{2,1,0:T(8,128)(2,1)S(1)}, u32[]{:S(2)}, u32[]{:S(2)}) collective-permute-start(bf16[2,512,256]{2,1,0:T(8,128)(2,1)S(1)} %collective-permute-done.1.refs_2_), channel_id=1, source_target_pairs={{0,1},{1,0},{2,3},{3,2},{4,5},{5,4},{6,7},{7,6},{8,9},{9,8},{10,11... | collective-permute-start | bytes 1572872 | tf_op jit(solution)/shard_map/ppermute | solution.py:367
  20.3 8.6 %collective-permute-start.7 = (bf16[1,128,256]{2,1,0:T(8,128)(2,1)S(1)}, bf16[1,128,256]{2,1,0:T(8,128)(2,1)S(1)}, u32[]{:S(2)}, u32[]{:S(2)}) collective-permute-start(bf16[1,128,256]{2,1,0:T(8,128)(2,1)S(1)} %get-tuple-element.67), channel_id=1, source_target_pairs={{0,4},{4,8},{8,12},{12,16},{16,20},{20,24},{24,28},{28,0},{1,5},{5... | collective-permute-start | bytes 196616 | tf_op jit(solution)/shard_map/ppermute | solution.py:373
  22.4 15.8 %collective-permute-start.10 = (bf16[1,512,256]{2,1,0:T(8,128)(2,1)S(1)}, bf16[1,512,256]{2,1,0:T(8,128)(2,1)S(1)}, u32[]{:S(2)}, u32[]{:S(2)}) collective-permute-start(bf16[1,512,256]{2,1,0:T(8,128)(2,1)S(1)} %get-tuple-element.64.refs_4_), channel_id=1, source_target_pairs={{0,2},{1,3},{2,0},{3,1},{4,6},{5,7},{6,4},{7,5},{8,10},{9,11},{10,... | collective-permute-start | bytes 786440 | tf_op jit(solution)/shard_map/ppermute | solution.py:370
  23.9 14.5 %collective-permute-start.9 = (bf16[1,512,256]{2,1,0:T(8,128)(2,1)S(1)}, bf16[1,512,256]{2,1,0:T(8,128)(2,1)S(1)}, u32[]{:S(2)}, u32[]{:S(2)}) collective-permute-start(bf16[1,512,256]{2,1,0:T(8,128)(2,1)S(1)} %get-tuple-element.64.refs_4_), channel_id=1, source_target_pairs={{0,1},{1,0},{2,3},{3,2},{4,5},{5,4},{6,7},{7,6},{8,9},{9,8},{10,11... | collective-permute-start | bytes 786440 | tf_op jit(solution)/shard_map/ppermute | solution.py:367
  28.9 1.9 %collective-permute-start.8 = (bf16[2,512,256]{2,1,0:T(8,128)(2,1)S(1)}, bf16[2,512,256]{2,1,0:T(8,128)(2,1)S(1)}, u32[]{:S(2)}, u32[]{:S(2)}) collective-permute-start(bf16[2,512,256]{2,1,0:T(8,128)(2,1)S(1)} %collective-permute-done.6.refs_2_), channel_id=1, source_target_pairs={{0,1},{1,0},{2,3},{3,2},{4,5},{5,4},{6,7},{7,6},{8,9},{9,8},{10,11... | collective-permute-start | bytes 1572872 | tf_op jit(solution)/shard_map/ppermute | solution.py:367
  31.6 8.7 %collective-permute-start.14 = (bf16[1,512,256]{2,1,0:T(8,128)(2,1)S(1)}, bf16[1,512,256]{2,1,0:T(8,128)(2,1)S(1)}, u32[]{:S(2)}, u32[]{:S(2)}) collective-permute-start(bf16[1,512,256]{2,1,0:T(8,128)(2,1)S(1)} %get-tuple-element.75.refs_0_), channel_id=1, source_target_pairs={{0,2},{1,3},{2,0},{3,1},{4,6},{5,7},{6,4},{7,5},{8,10},{9,11},{10,... | collective-permute-start | bytes 786440 | tf_op jit(solution)/shard_map/ppermute | solution.py:370
  33.7 6.7 %collective-permute-start.13 = (bf16[1,512,256]{2,1,0:T(8,128)(2,1)S(1)}, bf16[1,512,256]{2,1,0:T(8,128)(2,1)S(1)}, u32[]{:S(2)}, u32[]{:S(2)}) collective-permute-start(bf16[1,512,256]{2,1,0:T(8,128)(2,1)S(1)} %get-tuple-element.75.refs_0_), channel_id=1, source_target_pairs={{0,1},{1,0},{2,3},{3,2},{4,5},{5,4},{6,7},{7,6},{8,9},{9,8},{10,11... | collective-permute-start | bytes 786440 | tf_op jit(solution)/shard_map/ppermute | solution.py:367
  33.7 6.6 %collective-permute-start.12 = (bf16[1,128,256]{2,1,0:T(8,128)(2,1)S(1)}, bf16[1,128,256]{2,1,0:T(8,128)(2,1)S(1)}, u32[]{:S(2)}, u32[]{:S(2)}) collective-permute-start(bf16[1,128,256]{2,1,0:T(8,128)(2,1)S(1)} %get-tuple-element.83), channel_id=1, source_target_pairs={{4,0},{8,4},{12,8},{16,12},{20,16},{24,20},{28,24},{0,28},{5,1},{9... | collective-permute-start | bytes 196616 | tf_op jit(solution)/shard_map/ppermute | solution.py:376
  38.2 1.5 %collective-permute-start.11 = (bf16[1,512,256]{2,1,0:T(8,128)(2,1)S(1)}, bf16[1,512,256]{2,1,0:T(8,128)(2,1)S(1)}, u32[]{:S(2)}, u32[]{:S(2)}) collective-permute-start(bf16[1,512,256]{2,1,0:T(8,128)(2,1)S(1)} %collective-permute-done.10.refs_6_), channel_id=1, source_target_pairs={{0,1},{1,0},{2,3},{3,2},{4,5},{5,4},{6,7},{7,6},{8,9},{9,8},{10,11... | collective-permute-start | bytes 786440 | tf_op jit(solution)/shard_map/ppermute | solution.py:367
  40.3 1.5 %collective-permute-start.15 = (bf16[1,512,256]{2,1,0:T(8,128)(2,1)S(1)}, bf16[1,512,256]{2,1,0:T(8,128)(2,1)S(1)}, u32[]{:S(2)}, u32[]{:S(2)}) collective-permute-start(bf16[1,512,256]{2,1,0:T(8,128)(2,1)S(1)} %collective-permute-done.14.refs_2_), channel_id=1, source_target_pairs={{0,1},{1,0},{2,3},{3,2},{4,5},{5,4},{6,7},{7,6},{8,9},{9,8},{10,11... | collective-permute-start | bytes 786440 | tf_op jit(solution)/shard_map/ppermute | solution.py:367

commit v19 on v15

--- a/solution.py
+++ b/solution.py
@@ -414,7 +414,7 @@
     nfar_b = after(nfar_b, sums_a, new_hi)
     nfarsib_b = to_sibling(nfar_b)
     placed = list(enumerate(chunks[0]))
-    ends = [p for p in placed if p[1] in (0, xcount - 1)]
+    ends = [p for p in placed if p[1] in (0, 1, xcount - 1)]
     begun, npart_b = second_first(
         sums_a, nbase_a, new_a, death, [rounded_b, nsib_b, nfar_b], kernels, [p for p in placed if p not in ends], xcount
     )

time: 42.7 us -> 42.7 us (level)
  transfers between devices with their start and end apart: 16 -> 16, of which waited for: 7 -> 8; matrix products, arithmetic and copies ran while one was open for 0% -> 0% of each run, Pallas kernels for 22% -> 22%
where the time goes in v19:
time: 42.7 us; the launch traced here: 42.5 us
  starting transfers between devices  17.5 us (41%)
  waiting for transfers between devices  12.7 us (30%)
  Pallas kernels  11.6 us (27%)
  between operations  0.79 us (2%)
    pallas_call x11, Pallas kernels, call(): pl.pallas_call(body, out_shape=outs, in_specs=specs, out_specs=out_specs...  11.6 us
    ppermute x2, starting transfers between devices, from_above(): lax.ppermute(head, 'gx', [((i + 1) % gcount, i) for i in range(gcount)])  6.72 us
    ppermute x2, waiting for transfers between devices, from_below(): lax.ppermute(tail, 'gx', [(i, (i + 1) % gcount) for i in range(gcount)])  6.57 us
    ppermute x4, starting transfers between devices, to_far(): return lax.ppermute(v, 'trait', [(i, i ^ 2) for i in range(traits)])  6.54 us
    ppermute x4, waiting for transfers between devices, to_far(): return lax.ppermute(v, 'trait', [(i, i ^ 2) for i in range(traits)])  4.53 us
    ppermute x2, starting transfers between devices, from_below(): lax.ppermute(tail, 'gx', [(i, (i + 1) % gcount) for i in range(gcount)])  3.62 us
    ppermute x2, waiting for transfers between devices, from_above(): lax.ppermute(head, 'gx', [((i + 1) % gcount, i) for i in range(gcount)])  1.18 us
  transfers between devices with their start and end apart: 16, of which 8 were waited for; matrix products, arithmetic and copies ran while one was open for 0% of the time, Pallas kernels for 22%

profile of v19, /device:TPU:0, one launch (start us, length us, event | category | flops | bytes accessed | tf_op | source)
XLA Modules:
  0.0 42.5 jit_solution(15920121486530788587)
XLA Ops:
  0.6 1.3 %load_chunk.2 = (f32[5,128,256]{2,1,0:T(8,128)S(1)}, f32[5,128,256]{2,1,0:T(8,128)S(1)}, bf16[2,640,256]{2,1,0:T(8,128)(2,1)S(1)}, bf16[2,128,256]{2,1,0:T(8,128)(2,1)S(1)}, bf16[2,128,256]{2,1,0:T(8,128)(2,1)S(1)}) custom-call(f32[8,128,256]{2,1,0:T(8,128)} %refs_0_.2, f32[8,128,256]{2,1,0:T(8,128)} %refs_1_.3), custom_call_target="tpu_custom_call" | custom-call | tf_op jit(solution)/shard_map/load_chunk/pallas_call | solution.py:37
  2.0 0.0 copy-start.2
  2.0 3.0 %collective-permute-start.1 = (bf16[2,640,256]{2,1,0:T(8,128)(2,1)S(1)}, bf16[2,640,256]{2,1,0:T(8,128)(2,1)S(1)}, u32[]{:S(2)}, u32[]{:S(2)}) collective-permute-start(bf16[2,640,256]{2,1,0:T(8,128)(2,1)S(1)} %get-tuple-element.48.refs_0_), channel_id=1, source_target_pairs={{0,2},{1,3},{2,0},{3,1},{4,6},{5,7},{6,4},{7,5},{8,10},{9,11},{10,... | collective-permute-start | bytes 1966088 | tf_op jit(solution)/shard_map/ppermute | solution.py:370
  5.0 1.1 %load_chunk.3 = (f32[3,128,256]{2,1,0:T(8,128)S(1)}, f32[3,128,256]{2,1,0:T(8,128)S(1)}, bf16[2,384,256]{2,1,0:T(8,128)(2,1)S(1)}) custom-call(f32[8,128,256]{2,1,0:T(8,128)} %refs_0_.2, f32[8,128,256]{2,1,0:T(8,128)} %refs_1_.3), custom_call_target="tpu_custom_call" | custom-call | tf_op jit(solution)/shard_map/load_chunk/pallas_call | solution.py:37
  6.2 0.0 copy-start
  6.2 0.0 copy-start.1
  6.2 0.0 copy-start.3
  6.2 0.1 collective-permute-start
  6.3 1.5 %collective-permute-start.2 = (bf16[2,128,256]{2,1,0:T(8,128)(2,1)S(1)}, bf16[2,128,256]{2,1,0:T(8,128)(2,1)S(1)}, u32[]{:S(2)}, u32[]{:S(2)}) collective-permute-start(bf16[2,128,256]{2,1,0:T(8,128)(2,1)S(1)} %get-tuple-element.55), channel_id=1, source_target_pairs={{0,4},{4,8},{8,12},{12,16},{16,20},{20,24},{24,28},{28,0},{1,5},{5... | collective-permute-start | bytes 393224 | tf_op jit(solution)/shard_map/ppermute | solution.py:373
  7.8 3.2 %collective-permute-start.3 = (bf16[2,128,256]{2,1,0:T(8,128)(2,1)S(1)}, bf16[2,128,256]{2,1,0:T(8,128)(2,1)S(1)}, u32[]{:S(2)}, u32[]{:S(2)}) collective-permute-start(bf16[2,128,256]{2,1,0:T(8,128)(2,1)S(1)} %get-tuple-element.56), channel_id=1, source_target_pairs={{4,0},{8,4},{12,8},{16,12},{20,16},{24,20},{28,24},{0,28},{5,1},{9... | collective-permute-start | bytes 393224 | tf_op jit(solution)/shard_map/ppermute | solution.py:376
  11.1 0.4 collective-permute-start.6
  11.4 3.6 %collective-permute-done.2.refs_4_ = bf16[2,128,256]{2,1,0:T(8,128)(2,1)S(1)} collective-permute-done((bf16[2,128,256]{2,1,0:T(8,128)(2,1)S(1)}, bf16[2,128,256]{2,1,0:T(8,128)(2,1)S(1)}, u32[]{:S(2)}, u32[]{:S(2)}) %collective-permute-start.2) | collective-permute-done | bytes 131104 | tf_op jit(solution)/shard_map/ppermute | solution.py:373
  15.1 0.0 collective-permute-start.5
  15.1 1.1 %collective-permute-done.3.refs_5_ = bf16[2,128,256]{2,1,0:T(8,128)(2,1)S(1)} collective-permute-done((bf16[2,128,256]{2,1,0:T(8,128)(2,1)S(1)}, bf16[2,128,256]{2,1,0:T(8,128)(2,1)S(1)}, u32[]{:S(2)}, u32[]{:S(2)}) %collective-permute-start.3) | collective-permute-done | bytes 131104 | tf_op jit(solution)/shard_map/ppermute | solution.py:376
  16.2 0.9 %before_first.1 = (f32[2,5,128,256]{3,2,1,0:T(8,128)S(1)}, f32[2,3,128,256]{3,2,1,0:T(8,128)S(1)}) custom-call(f32[5,128,256]{2,1,0:T(8,128)S(1)} %get-tuple-element.49.refs_0_.refs_4_.one_ref, f32[3,128,256]{2,1,0:T(8,128)S(1)} %get-tuple-element.50.refs_1_.refs_4_.one_ref, f32[5,128,256]{2,1,0:T(8,128)S(1)} %get-tuple-element.51.refs_2_.refs_5_.two_ref, ...), custom_call_target="tpu_custom_call" | custom-call | tf_op jit(solution)/shard_map/before_first/pallas_call | solution.py:37
  17.1 3.5 %collective-permute-done.1.refs_2_ = bf16[2,640,256]{2,1,0:T(8,128)(2,1)S(1)} collective-permute-done((bf16[2,640,256]{2,1,0:T(8,128)(2,1)S(1)}, bf16[2,640,256]{2,1,0:T(8,128)(2,1)S(1)}, u32[]{:S(2)}, u32[]{:S(2)}) %collective-permute-start.1) | collective-permute-done | bytes 655392 | tf_op jit(solution)/shard_map/ppermute | solution.py:370
  20.6 0.0 collective-permute-start.4
  20.6 0.0 collective-permute-done.refs_1_
  20.6 0.0 copy-done
  20.6 1.8 %early_part.2 = (f32[2,1280,256]{2,1,0:T(8,128)S(1)}, f32[5,128,256]{2,1,0:T(8,128)S(1)}, f32[5,128,256]{2,1,0:T(8,128)S(1)}) custom-call(bf16[2,640,256]{2,1,0:T(8,128)(2,1)S(1)} %get-tuple-element.48.refs_0_, bf16[2,640,256]{2,1,0:T(8,128)(2,1)S(1)} %collective-permute-done.refs_1_, bf16[2,640,256]{2,1,0:T(8,128)(2,1)S(1)} %collective-permute-done.1.refs_2_, ...), custom_call_target="tpu_custom_call" | custom-call | flops 20000000000 | tf_op jit(solution)/shard_map/early_part/pallas_call | solution.py:37
  22.4 0.3 collective-permute-done.4.last_ref
  22.7 0.8 %first_node.2 = (f32[5,128,256]{2,1,0:T(8,128)S(1)}, bf16[1,640,256]{2,1,0:T(8,128)(2,1)S(1)}, f32[5,128,256]{2,1,0:T(8,128)S(1)}, bf16[1,128,256]{2,1,0:T(8,128)(2,1)S(1)}, bf16[1,128,256]{2,1,0:T(8,128)(2,1)S(1)}) custom-call(f32[2,1280,256]{2,1,0:T(8,128)S(1)} %get-tuple-element.60.part_ref, f32[5,128,256]{2,1,0:T(8,128)S(1)} %get-tuple-element.61.first_ref, ...), custom_call_target="tpu_custom_call" | custom-call | tf_op jit(solution)/shard_map/first_node/pallas_call | solution.py:37
  23.5 2.1 %collective-permute-start.7 = (bf16[1,128,256]{2,1,0:T(8,128)(2,1)S(1)}, bf16[1,128,256]{2,1,0:T(8,128)(2,1)S(1)}, u32[]{:S(2)}, u32[]{:S(2)}) collective-permute-start(bf16[1,128,256]{2,1,0:T(8,128)(2,1)S(1)} %get-tuple-element.67), channel_id=1, source_target_pairs={{0,4},{4,8},{8,12},{12,16},{16,20},{20,24},{24,28},{28,0},{1,5},{5... | collective-permute-start | bytes 196616 | tf_op jit(solution)/shard_map/ppermute | solution.py:373
  25.6 1.5 %collective-permute-start.10 = (bf16[1,640,256]{2,1,0:T(8,128)(2,1)S(1)}, bf16[1,640,256]{2,1,0:T(8,128)(2,1)S(1)}, u32[]{:S(2)}, u32[]{:S(2)}) collective-permute-start(bf16[1,640,256]{2,1,0:T(8,128)(2,1)S(1)} %get-tuple-element.64.refs_4_), channel_id=1, source_target_pairs={{0,2},{1,3},{2,0},{3,1},{4,6},{5,7},{6,4},{7,5},{8,10},{9,11},{10,... | collective-permute-start | bytes 983048 | tf_op jit(solution)/shard_map/ppermute | solution.py:370
  27.1 0.0 collective-permute-start.9
  27.1 1.1 %collective-permute-done.6.refs_2_ = bf16[2,384,256]{2,1,0:T(8,128)(2,1)S(1)} collective-permute-done((bf16[2,384,256]{2,1,0:T(8,128)(2,1)S(1)}, bf16[2,384,256]{2,1,0:T(8,128)(2,1)S(1)}, u32[]{:S(2)}, u32[]{:S(2)}) %collective-permute-start.6) | collective-permute-done | bytes 393248 | tf_op jit(solution)/shard_map/ppermute | solution.py:370
  28.2 0.0 collective-permute-start.8
  28.2 3.0 %collective-permute-done.7.refs_3_ = bf16[1,128,256]{2,1,0:T(8,128)(2,1)S(1)} collective-permute-done((bf16[1,128,256]{2,1,0:T(8,128)(2,1)S(1)}, bf16[1,128,256]{2,1,0:T(8,128)(2,1)S(1)}, u32[]{:S(2)}, u32[]{:S(2)}) %collective-permute-start.7) | collective-permute-done | bytes 65568 | tf_op jit(solution)/shard_map/ppermute | solution.py:373
  31.1 0.0 collective-permute-done.5.refs_1_
  31.1 1.1 %early_part.3 = (f32[2,768,256]{2,1,0:T(8,128)S(1)}, f32[3,128,256]{2,1,0:T(8,128)S(1)}, f32[3,128,256]{2,1,0:T(8,128)S(1)}, f32[8,128,256]{2,1,0:T(8,128)}) custom-call(bf16[2,384,256]{2,1,0:T(8,128)(2,1)S(1)} %get-tuple-element.47.refs_0_, bf16[2,384,256]{2,1,0:T(8,128)(2,1)S(1)} %collective-permute-done.5.refs_1_, ...), custom_call_target="tpu_custom_call" | custom-call | flops 20000000000 | tf_op jit(solution)/shard_map/early_part/pallas_call | solution.py:37
  32.3 0.0 collective-permute-done.8.last_ref
  32.3 0.6 %first_node.3 = (f32[3,128,256]{2,1,0:T(8,128)S(1)}, bf16[1,384,256]{2,1,0:T(8,128)(2,1)S(1)}, f32[3,128,256]{2,1,0:T(8,128)S(1)}) custom-call(f32[2,768,256]{2,1,0:T(8,128)S(1)} %get-tuple-element.69.part_ref, f32[3,128,256]{2,1,0:T(8,128)S(1)} %get-tuple-element.70.first_ref, f32[3,128,256]{2,1,0:T(8,128)S(1)} %get-tuple-element.71.begun_ref, ...), custom_call_target="tpu_custom_call" | custom-call | tf_op jit(solution)/shard_map/first_node/pallas_call | solution.py:37
  32.8 1.6 %collective-permute-start.14 = (bf16[1,384,256]{2,1,0:T(8,128)(2,1)S(1)}, bf16[1,384,256]{2,1,0:T(8,128)(2,1)S(1)}, u32[]{:S(2)}, u32[]{:S(2)}) collective-permute-start(bf16[1,384,256]{2,1,0:T(8,128)(2,1)S(1)} %get-tuple-element.75.refs_0_), channel_id=1, source_target_pairs={{0,2},{1,3},{2,0},{3,1},{4,6},{5,7},{6,4},{7,5},{8,10},{9,11},{10,... | collective-permute-start | bytes 589832 | tf_op jit(solution)/shard_map/ppermute | solution.py:370
  34.4 0.0 collective-permute-start.13
  34.4 3.5 %collective-permute-start.12 = (bf16[1,128,256]{2,1,0:T(8,128)(2,1)S(1)}, bf16[1,128,256]{2,1,0:T(8,128)(2,1)S(1)}, u32[]{:S(2)}, u32[]{:S(2)}) collective-permute-start(bf16[1,128,256]{2,1,0:T(8,128)(2,1)S(1)} %get-tuple-element.83), channel_id=1, source_target_pairs={{4,0},{8,4},{12,8},{16,12},{20,16},{24,20},{28,24},{0,28},{5,1},{9... | collective-permute-start | bytes 196616 | tf_op jit(solution)/shard_map/ppermute | solution.py:376
  37.9 0.0 collective-permute-done.10.refs_6_
  37.9 0.2 collective-permute-start.11
  38.2 0.0 collective-permute-done.9.refs_5_
  38.2 1.3 %before_second.1 = (f32[8,128,256]{2,1,0:T(8,128)}, f32[2,640,256]{2,1,0:T(8,128)S(1)}, f32[5,128,256]{2,1,0:T(8,128)S(1)}, f32[3,128,256]{2,1,0:T(8,128)S(1)}) custom-call(f32[5,128,256]{2,1,0:T(8,128)S(1)} %get-tuple-element.63.refs_9_.refs_0_.new_ref.refs_2_, ...), custom_call_target="tpu_custom_call", output_to_operand_aliasing={{0}: (10, {})} | custom-call | flops 20000000000 | tf_op jit(solution)/shard_map/before_second/pallas_call | solution.py:37
  39.5 0.1 collective-permute-done.11.last_ref
  39.6 0.3 whole_sums.1.sums_ref.refs_0_
  39.9 0.1 collective-permute-done.12.refs_4_
  40.0 0.0 collective-permute-done.14.refs_2_
  40.0 0.3 collective-permute-start.15
  40.2 0.0 collective-permute-done.13.refs_1_
  40.2 1.2 %second_first.1 = (f32[8,128,256]{2,1,0:T(8,128)}, f32[2,384,256]{2,1,0:T(8,128)S(1)}) custom-call(bf16[2,640,256]{2,1,0:T(8,128)(2,1)S(1)} %whole_sums.1.sums_ref.refs_0_, f32[5,128,256]{2,1,0:T(8,128)S(1)} %get-tuple-element.80.base_ref.refs_1_, f32[5,128,256]{2,1,0:T(8,128)S(1)} %get-tuple-element.63.refs_9_.refs_0_.new_ref.refs_2_, ...), custom_call_target="tpu_custom_call" | custom-call | tf_op jit(solution)/shard_map/second_first/pallas_call | solution.py:37
  41.4 0.1 collective-permute-done.15.refs_6_
  41.4 1.1 %second_last.1 = f32[8,128,256]{2,1,0:T(8,128)} custom-call(bf16[2,640,256]{2,1,0:T(8,128)(2,1)S(1)} %whole_sums.1.sums_ref.refs_0_, f32[5,128,256]{2,1,0:T(8,128)S(1)} %get-tuple-element.80.base_ref.refs_1_, f32[5,128,256]{2,1,0:T(8,128)S(1)} %get-tuple-element.63.refs_9_.refs_0_.new_ref.refs_2_, ...), custom_call_target="tpu_custom_call", output_to_operand_aliasing={{}: (11, {})} | custom-call | tf_op jit(solution)/shard_map/second_last/pallas_call | solution.py:37
  (3 shorter events, 0.0 us)
Async XLA Ops:
  2.0 14.2 %copy-start.2 = (f32[256]{0:T(256)S(1)}, f32[256]{0:T(256)}, u32[]{:S(2)}) copy-start(f32[256]{0:T(256)} %param.10) | copy-start | bytes 3076
  2.0 18.6 %collective-permute-start.1 = (bf16[2,640,256]{2,1,0:T(8,128)(2,1)S(1)}, bf16[2,640,256]{2,1,0:T(8,128)(2,1)S(1)}, u32[]{:S(2)}, u32[]{:S(2)}) collective-permute-start(bf16[2,640,256]{2,1,0:T(8,128)(2,1)S(1)} %get-tuple-element.48.refs_0_), channel_id=1, source_target_pairs={{0,2},{1,3},{2,0},{3,1},{4,6},{5,7},{6,4},{7,5},{8,10},{9,11},{10,... | collective-permute-start | bytes 1966088 | tf_op jit(solution)/shard_map/ppermute | solution.py:370
  6.2 14.4 %copy-start = (bf16[2,1024,256]{2,1,0:T(8,128)(2,1)S(1)}, bf16[2,1024,256]{2,1,0:T(8,128)(2,1)}, u32[]{:S(2)}) copy-start(bf16[2,1024,256]{2,1,0:T(8,128)(2,1)} %refs_10_) | copy-start | bytes 3145732
  6.2 14.4 %copy-start.1 = (f32[256]{0:T(256)S(1)}, f32[256]{0:T(256)}, u32[]{:S(2)}) copy-start(f32[256]{0:T(256)} %param.11) | copy-start | bytes 3076
  6.2 14.4 %copy-start.3 = (f32[8,128,256]{2,1,0:T(8,128)S(1)}, f32[8,128,256]{2,1,0:T(8,128)}, u32[]{:S(2)}) copy-start(f32[8,128,256]{2,1,0:T(8,128)} %refs_6_.3) | copy-start | bytes 3145732
  6.2 14.4 %collective-permute-start = (bf16[2,640,256]{2,1,0:T(8,128)(2,1)S(1)}, bf16[2,640,256]{2,1,0:T(8,128)(2,1)S(1)}, u32[]{:S(2)}, u32[]{:S(2)}) collective-permute-start(bf16[2,640,256]{2,1,0:T(8,128)(2,1)S(1)} %get-tuple-element.48.refs_0_), channel_id=1, source_target_pairs={{0,1},{1,0},{2,3},{3,2},{4,5},{5,4},{6,7},{7,6},{8,9},{9,8},{10,11... | collective-permute-start | bytes 1966088 | tf_op jit(solution)/shard_map/ppermute | solution.py:367
  6.3 8.8 %collective-permute-start.2 = (bf16[2,128,256]{2,1,0:T(8,128)(2,1)S(1)}, bf16[2,128,256]{2,1,0:T(8,128)(2,1)S(1)}, u32[]{:S(2)}, u32[]{:S(2)}) collective-permute-start(bf16[2,128,256]{2,1,0:T(8,128)(2,1)S(1)} %get-tuple-element.55), channel_id=1, source_target_pairs={{0,4},{4,8},{8,12},{12,16},{16,20},{20,24},{24,28},{28,0},{1,5},{5... | collective-permute-start | bytes 393224 | tf_op jit(solution)/shard_map/ppermute | solution.py:373
  7.8 8.4 %collective-permute-start.3 = (bf16[2,128,256]{2,1,0:T(8,128)(2,1)S(1)}, bf16[2,128,256]{2,1,0:T(8,128)(2,1)S(1)}, u32[]{:S(2)}, u32[]{:S(2)}) collective-permute-start(bf16[2,128,256]{2,1,0:T(8,128)(2,1)S(1)} %get-tuple-element.56), channel_id=1, source_target_pairs={{4,0},{8,4},{12,8},{16,12},{20,16},{24,20},{28,24},{0,28},{5,1},{9... | collective-permute-start | bytes 393224 | tf_op jit(solution)/shard_map/ppermute | solution.py:376
  11.1 17.1 %collective-permute-start.6 = (bf16[2,384,256]{2,1,0:T(8,128)(2,1)S(1)}, bf16[2,384,256]{2,1,0:T(8,128)(2,1)S(1)}, u32[]{:S(2)}, u32[]{:S(2)}) collective-permute-start(bf16[2,384,256]{2,1,0:T(8,128)(2,1)S(1)} %get-tuple-element.47.refs_0_), channel_id=1, source_target_pairs={{0,2},{1,3},{2,0},{3,1},{4,6},{5,7},{6,4},{7,5},{8,10},{9,11},{10,... | collective-permute-start | bytes 1179656 | tf_op jit(solution)/shard_map/ppermute | solution.py:370
  15.1 16.1 %collective-permute-start.5 = (bf16[2,384,256]{2,1,0:T(8,128)(2,1)S(1)}, bf16[2,384,256]{2,1,0:T(8,128)(2,1)S(1)}, u32[]{:S(2)}, u32[]{:S(2)}) collective-permute-start(bf16[2,384,256]{2,1,0:T(8,128)(2,1)S(1)} %get-tuple-element.47.refs_0_), channel_id=1, source_target_pairs={{0,1},{1,0},{2,3},{3,2},{4,5},{5,4},{6,7},{7,6},{8,9},{9,8},{10,11... | collective-permute-start | bytes 1179656 | tf_op jit(solution)/shard_map/ppermute | solution.py:367
  20.6 2.1 %collective-permute-start.4 = (bf16[2,640,256]{2,1,0:T(8,128)(2,1)S(1)}, bf16[2,640,256]{2,1,0:T(8,128)(2,1)S(1)}, u32[]{:S(2)}, u32[]{:S(2)}) collective-permute-start(bf16[2,640,256]{2,1,0:T(8,128)(2,1)S(1)} %collective-permute-done.1.refs_2_), channel_id=1, source_target_pairs={{0,1},{1,0},{2,3},{3,2},{4,5},{5,4},{6,7},{7,6},{8,9},{9,8},{10,11... | collective-permute-start | bytes 1966088 | tf_op jit(solution)/shard_map/ppermute | solution.py:367
  23.5 7.6 %collective-permute-start.7 = (bf16[1,128,256]{2,1,0:T(8,128)(2,1)S(1)}, bf16[1,128,256]{2,1,0:T(8,128)(2,1)S(1)}, u32[]{:S(2)}, u32[]{:S(2)}) collective-permute-start(bf16[1,128,256]{2,1,0:T(8,128)(2,1)S(1)} %get-tuple-element.67), channel_id=1, source_target_pairs={{0,4},{4,8},{8,12},{12,16},{16,20},{20,24},{24,28},{28,0},{1,5},{5... | collective-permute-start | bytes 196616 | tf_op jit(solution)/shard_map/ppermute | solution.py:373
  25.6 12.4 %collective-permute-start.10 = (bf16[1,640,256]{2,1,0:T(8,128)(2,1)S(1)}, bf16[1,640,256]{2,1,0:T(8,128)(2,1)S(1)}, u32[]{:S(2)}, u32[]{:S(2)}) collective-permute-start(bf16[1,640,256]{2,1,0:T(8,128)(2,1)S(1)} %get-tuple-element.64.refs_4_), channel_id=1, source_target_pairs={{0,2},{1,3},{2,0},{3,1},{4,6},{5,7},{6,4},{7,5},{8,10},{9,11},{10,... | collective-permute-start | bytes 983048 | tf_op jit(solution)/shard_map/ppermute | solution.py:370
  27.1 11.1 %collective-permute-start.9 = (bf16[1,640,256]{2,1,0:T(8,128)(2,1)S(1)}, bf16[1,640,256]{2,1,0:T(8,128)(2,1)S(1)}, u32[]{:S(2)}, u32[]{:S(2)}) collective-permute-start(bf16[1,640,256]{2,1,0:T(8,128)(2,1)S(1)} %get-tuple-element.64.refs_4_), channel_id=1, source_target_pairs={{0,1},{1,0},{2,3},{3,2},{4,5},{5,4},{6,7},{7,6},{8,9},{9,8},{10,11... | collective-permute-start | bytes 983048 | tf_op jit(solution)/shard_map/ppermute | solution.py:367
  28.2 4.1 %collective-permute-start.8 = (bf16[2,384,256]{2,1,0:T(8,128)(2,1)S(1)}, bf16[2,384,256]{2,1,0:T(8,128)(2,1)S(1)}, u32[]{:S(2)}, u32[]{:S(2)}) collective-permute-start(bf16[2,384,256]{2,1,0:T(8,128)(2,1)S(1)} %collective-permute-done.6.refs_2_), channel_id=1, source_target_pairs={{0,1},{1,0},{2,3},{3,2},{4,5},{5,4},{6,7},{7,6},{8,9},{9,8},{10,11... | collective-permute-start | bytes 1179656 | tf_op jit(solution)/shard_map/ppermute | solution.py:367
  32.8 7.1 %collective-permute-start.14 = (bf16[1,384,256]{2,1,0:T(8,128)(2,1)S(1)}, bf16[1,384,256]{2,1,0:T(8,128)(2,1)S(1)}, u32[]{:S(2)}, u32[]{:S(2)}) collective-permute-start(bf16[1,384,256]{2,1,0:T(8,128)(2,1)S(1)} %get-tuple-element.75.refs_0_), channel_id=1, source_target_pairs={{0,2},{1,3},{2,0},{3,1},{4,6},{5,7},{6,4},{7,5},{8,10},{9,11},{10,... | collective-permute-start | bytes 589832 | tf_op jit(solution)/shard_map/ppermute | solution.py:370
  34.4 5.8 %collective-permute-start.13 = (bf16[1,384,256]{2,1,0:T(8,128)(2,1)S(1)}, bf16[1,384,256]{2,1,0:T(8,128)(2,1)S(1)}, u32[]{:S(2)}, u32[]{:S(2)}) collective-permute-start(bf16[1,384,256]{2,1,0:T(8,128)(2,1)S(1)} %get-tuple-element.75.refs_0_), channel_id=1, source_target_pairs={{0,1},{1,0},{2,3},{3,2},{4,5},{5,4},{6,7},{7,6},{8,9},{9,8},{10,11... | collective-permute-start | bytes 589832 | tf_op jit(solution)/shard_map/ppermute | solution.py:367
  34.4 5.5 %collective-permute-start.12 = (bf16[1,128,256]{2,1,0:T(8,128)(2,1)S(1)}, bf16[1,128,256]{2,1,0:T(8,128)(2,1)S(1)}, u32[]{:S(2)}, u32[]{:S(2)}) collective-permute-start(bf16[1,128,256]{2,1,0:T(8,128)(2,1)S(1)} %get-tuple-element.83), channel_id=1, source_target_pairs={{4,0},{8,4},{12,8},{16,12},{20,16},{24,20},{28,24},{0,28},{5,1},{9... | collective-permute-start | bytes 196616 | tf_op jit(solution)/shard_map/ppermute | solution.py:376
  37.9 1.6 %collective-permute-start.11 = (bf16[1,640,256]{2,1,0:T(8,128)(2,1)S(1)}, bf16[1,640,256]{2,1,0:T(8,128)(2,1)S(1)}, u32[]{:S(2)}, u32[]{:S(2)}) collective-permute-start(bf16[1,640,256]{2,1,0:T(8,128)(2,1)S(1)} %collective-permute-done.10.refs_6_), channel_id=1, source_target_pairs={{0,1},{1,0},{2,3},{3,2},{4,5},{5,4},{6,7},{7,6},{8,9},{9,8},{10,11... | collective-permute-start | bytes 983048 | tf_op jit(solution)/shard_map/ppermute | solution.py:367
  40.0 1.5 %collective-permute-start.15 = (bf16[1,384,256]{2,1,0:T(8,128)(2,1)S(1)}, bf16[1,384,256]{2,1,0:T(8,128)(2,1)S(1)}, u32[]{:S(2)}, u32[]{:S(2)}) collective-permute-start(bf16[1,384,256]{2,1,0:T(8,128)(2,1)S(1)} %collective-permute-done.14.refs_2_), channel_id=1, source_target_pairs={{0,1},{1,0},{2,3},{3,2},{4,5},{5,4},{6,7},{7,6},{8,9},{9,8},{10,11... | collective-permute-start | bytes 589832 | tf_op jit(solution)/shard_map/ppermute | solution.py:367

commit v20 on v15

--- a/solution.py
+++ b/solution.py
@@ -379,7 +379,7 @@
     far_a = to_far(own_a)
     one_b, two_b, own_b = load_chunk((after(section_one, own_a), section_two), chunks[1], False)
     far_b = to_far(own_b)
-    head, tail, kernels = lax.optimization_barrier((head, tail, kernels, own_b))[:3]
+    kernels = after(kernels, own_b)
     lo, hi = from_below(tail), from_above(head)
     base_a, base_b = before_first((one_a, one_b), (two_a, two_b), lo, hi, growth, chunks)
     sib_a = to_sibling(after(own_a, own_b))

time: 42.7 us -> 42.7 us (level)
  no operation moved by 1% of the time
where the time goes in v20:
time: 42.7 us; the launch traced here: 42.5 us
  starting transfers between devices  17.5 us (41%)
  waiting for transfers between devices  12.7 us (30%)
  Pallas kernels  11.6 us (27%)
  between operations  0.79 us (2%)
    pallas_call x11, Pallas kernels, call(): pl.pallas_call(body, out_shape=outs, in_specs=specs, out_specs=out_specs...  11.6 us
    ppermute x2, starting transfers between devices, from_above(): lax.ppermute(head, 'gx', [((i + 1) % gcount, i) for i in range(gcount)])  6.72 us
    ppermute x2, waiting for transfers between devices, from_below(): lax.ppermute(tail, 'gx', [(i, (i + 1) % gcount) for i in range(gcount)])  6.57 us
    ppermute x4, starting transfers between devices, to_far(): return lax.ppermute(v, 'trait', [(i, i ^ 2) for i in range(traits)])  6.54 us
    ppermute x4, waiting for transfers between devices, to_far(): return lax.ppermute(v, 'trait', [(i, i ^ 2) for i in range(traits)])  4.53 us
    ppermute x2, starting transfers between devices, from_below(): lax.ppermute(tail, 'gx', [(i, (i + 1) % gcount) for i in range(gcount)])  3.62 us
    ppermute x2, waiting for transfers between devices, from_above(): lax.ppermute(head, 'gx', [((i + 1) % gcount, i) for i in range(gcount)])  1.18 us
  transfers between devices with their start and end apart: 16, of which 7 were waited for; matrix products, arithmetic and copies ran while one was open for 0% of the time, Pallas kernels for 22%

profile of v20, /device:TPU:0, one launch (start us, length us, event | category | flops | bytes accessed | tf_op | source)
XLA Modules:
  0.0 42.5 jit_solution(16238985129217659130)
XLA Ops:
  0.6 1.3 %load_chunk.2 = (f32[5,128,256]{2,1,0:T(8,128)S(1)}, f32[5,128,256]{2,1,0:T(8,128)S(1)}, bf16[2,640,256]{2,1,0:T(8,128)(2,1)S(1)}, bf16[2,128,256]{2,1,0:T(8,128)(2,1)S(1)}, bf16[2,128,256]{2,1,0:T(8,128)(2,1)S(1)}) custom-call(f32[8,128,256]{2,1,0:T(8,128)} %refs_0_.2, f32[8,128,256]{2,1,0:T(8,128)} %refs_1_.3), custom_call_target="tpu_custom_call" | custom-call | tf_op jit(solution)/shard_map/load_chunk/pallas_call | solution.py:37
  2.0 0.0 copy-start.2
  2.0 3.0 %collective-permute-start.1 = (bf16[2,640,256]{2,1,0:T(8,128)(2,1)S(1)}, bf16[2,640,256]{2,1,0:T(8,128)(2,1)S(1)}, u32[]{:S(2)}, u32[]{:S(2)}) collective-permute-start(bf16[2,640,256]{2,1,0:T(8,128)(2,1)S(1)} %get-tuple-element.46.refs_0_), channel_id=1, source_target_pairs={{0,2},{1,3},{2,0},{3,1},{4,6},{5,7},{6,4},{7,5},{8,10},{9,11},{10,... | collective-permute-start | bytes 1966088 | tf_op jit(solution)/shard_map/ppermute | solution.py:370
  5.0 1.1 %load_chunk.3 = (f32[3,128,256]{2,1,0:T(8,128)S(1)}, f32[3,128,256]{2,1,0:T(8,128)S(1)}, bf16[2,384,256]{2,1,0:T(8,128)(2,1)S(1)}) custom-call(f32[8,128,256]{2,1,0:T(8,128)} %refs_0_.2, f32[8,128,256]{2,1,0:T(8,128)} %refs_1_.3), custom_call_target="tpu_custom_call" | custom-call | tf_op jit(solution)/shard_map/load_chunk/pallas_call | solution.py:37
  6.2 0.0 copy-start
  6.2 0.0 copy-start.1
  6.2 0.0 copy-start.3
  6.2 0.1 collective-permute-start
  6.3 1.5 %collective-permute-start.2 = (bf16[2,128,256]{2,1,0:T(8,128)(2,1)S(1)}, bf16[2,128,256]{2,1,0:T(8,128)(2,1)S(1)}, u32[]{:S(2)}, u32[]{:S(2)}) collective-permute-start(bf16[2,128,256]{2,1,0:T(8,128)(2,1)S(1)} %get-tuple-element.51), channel_id=1, source_target_pairs={{0,4},{4,8},{8,12},{12,16},{16,20},{20,24},{24,28},{28,0},{1,5},{5... | collective-permute-start | bytes 393224 | tf_op jit(solution)/shard_map/ppermute | solution.py:373
  7.8 3.2 %collective-permute-start.3 = (bf16[2,128,256]{2,1,0:T(8,128)(2,1)S(1)}, bf16[2,128,256]{2,1,0:T(8,128)(2,1)S(1)}, u32[]{:S(2)}, u32[]{:S(2)}) collective-permute-start(bf16[2,128,256]{2,1,0:T(8,128)(2,1)S(1)} %get-tuple-element.52), channel_id=1, source_target_pairs={{4,0},{8,4},{12,8},{16,12},{20,16},{24,20},{28,24},{0,28},{5,1},{9... | collective-permute-start | bytes 393224 | tf_op jit(solution)/shard_map/ppermute | solution.py:376
  11.1 0.4 collective-permute-start.6
  11.4 3.6 %collective-permute-done.2.refs_4_ = bf16[2,128,256]{2,1,0:T(8,128)(2,1)S(1)} collective-permute-done((bf16[2,128,256]{2,1,0:T(8,128)(2,1)S(1)}, bf16[2,128,256]{2,1,0:T(8,128)(2,1)S(1)}, u32[]{:S(2)}, u32[]{:S(2)}) %collective-permute-start.2) | collective-permute-done | bytes 131104 | tf_op jit(solution)/shard_map/ppermute | solution.py:373
  15.1 0.0 collective-permute-start.5
  15.1 1.1 %collective-permute-done.3.refs_5_ = bf16[2,128,256]{2,1,0:T(8,128)(2,1)S(1)} collective-permute-done((bf16[2,128,256]{2,1,0:T(8,128)(2,1)S(1)}, bf16[2,128,256]{2,1,0:T(8,128)(2,1)S(1)}, u32[]{:S(2)}, u32[]{:S(2)}) %collective-permute-start.3) | collective-permute-done | bytes 131104 | tf_op jit(solution)/shard_map/ppermute | solution.py:376
  16.2 0.9 %before_first.1 = (f32[2,5,128,256]{3,2,1,0:T(8,128)S(1)}, f32[2,3,128,256]{3,2,1,0:T(8,128)S(1)}) custom-call(f32[5,128,256]{2,1,0:T(8,128)S(1)} %get-tuple-element.47.refs_0_.refs_4_.one_ref, f32[3,128,256]{2,1,0:T(8,128)S(1)} %get-tuple-element.48.refs_1_.refs_4_.one_ref, f32[5,128,256]{2,1,0:T(8,128)S(1)} %get-tuple-element.49.refs_2_.refs_5_.two_ref, ...), custom_call_target="tpu_custom_call" | custom-call | tf_op jit(solution)/shard_map/before_first/pallas_call | solution.py:37
  17.1 3.5 %collective-permute-done.1.refs_2_ = bf16[2,640,256]{2,1,0:T(8,128)(2,1)S(1)} collective-permute-done((bf16[2,640,256]{2,1,0:T(8,128)(2,1)S(1)}, bf16[2,640,256]{2,1,0:T(8,128)(2,1)S(1)}, u32[]{:S(2)}, u32[]{:S(2)}) %collective-permute-start.1) | collective-permute-done | bytes 655392 | tf_op jit(solution)/shard_map/ppermute | solution.py:370
  20.6 0.0 collective-permute-start.4
  20.6 0.0 collective-permute-done.refs_1_
  20.6 0.0 copy-done
  20.6 1.8 %early_part.2 = (f32[2,1280,256]{2,1,0:T(8,128)S(1)}, f32[5,128,256]{2,1,0:T(8,128)S(1)}, f32[5,128,256]{2,1,0:T(8,128)S(1)}) custom-call(bf16[2,640,256]{2,1,0:T(8,128)(2,1)S(1)} %get-tuple-element.46.refs_0_, bf16[2,640,256]{2,1,0:T(8,128)(2,1)S(1)} %collective-permute-done.refs_1_, bf16[2,640,256]{2,1,0:T(8,128)(2,1)S(1)} %collective-permute-done.1.refs_2_, ...), custom_call_target="tpu_custom_call" | custom-call | flops 20000000000 | tf_op jit(solution)/shard_map/early_part/pallas_call | solution.py:37
  22.4 0.3 collective-permute-done.4.last_ref
  22.7 0.8 %first_node.2 = (f32[5,128,256]{2,1,0:T(8,128)S(1)}, bf16[1,640,256]{2,1,0:T(8,128)(2,1)S(1)}, f32[5,128,256]{2,1,0:T(8,128)S(1)}, bf16[1,128,256]{2,1,0:T(8,128)(2,1)S(1)}, bf16[1,128,256]{2,1,0:T(8,128)(2,1)S(1)}) custom-call(f32[2,1280,256]{2,1,0:T(8,128)S(1)} %get-tuple-element.56.part_ref, f32[5,128,256]{2,1,0:T(8,128)S(1)} %get-tuple-element.57.first_ref, ...), custom_call_target="tpu_custom_call" | custom-call | tf_op jit(solution)/shard_map/first_node/pallas_call | solution.py:37
  23.5 2.1 %collective-permute-start.7 = (bf16[1,128,256]{2,1,0:T(8,128)(2,1)S(1)}, bf16[1,128,256]{2,1,0:T(8,128)(2,1)S(1)}, u32[]{:S(2)}, u32[]{:S(2)}) collective-permute-start(bf16[1,128,256]{2,1,0:T(8,128)(2,1)S(1)} %get-tuple-element.63), channel_id=1, source_target_pairs={{0,4},{4,8},{8,12},{12,16},{16,20},{20,24},{24,28},{28,0},{1,5},{5... | collective-permute-start | bytes 196616 | tf_op jit(solution)/shard_map/ppermute | solution.py:373
  25.6 1.5 %collective-permute-start.10 = (bf16[1,640,256]{2,1,0:T(8,128)(2,1)S(1)}, bf16[1,640,256]{2,1,0:T(8,128)(2,1)S(1)}, u32[]{:S(2)}, u32[]{:S(2)}) collective-permute-start(bf16[1,640,256]{2,1,0:T(8,128)(2,1)S(1)} %get-tuple-element.60.refs_4_), channel_id=1, source_target_pairs={{0,2},{1,3},{2,0},{3,1},{4,6},{5,7},{6,4},{7,5},{8,10},{9,11},{10,... | collective-permute-start | bytes 983048 | tf_op jit(solution)/shard_map/ppermute | solution.py:370
  27.1 0.0 collective-permute-start.9
  27.1 1.1 %collective-permute-done.6.refs_2_ = bf16[2,384,256]{2,1,0:T(8,128)(2,1)S(1)} collective-permute-done((bf16[2,384,256]{2,1,0:T(8,128)(2,1)S(1)}, bf16[2,384,256]{2,1,0:T(8,128)(2,1)S(1)}, u32[]{:S(2)}, u32[]{:S(2)}) %collective-permute-start.6) | collective-permute-done | bytes 393248 | tf_op jit(solution)/shard_map/ppermute | solution.py:370
  28.2 0.0 collective-permute-start.8
  28.2 3.0 %collective-permute-done.7.refs_3_ = bf16[1,128,256]{2,1,0:T(8,128)(2,1)S(1)} collective-permute-done((bf16[1,128,256]{2,1,0:T(8,128)(2,1)S(1)}, bf16[1,128,256]{2,1,0:T(8,128)(2,1)S(1)}, u32[]{:S(2)}, u32[]{:S(2)}) %collective-permute-start.7) | collective-permute-done | bytes 65568 | tf_op jit(solution)/shard_map/ppermute | solution.py:373
  31.1 0.0 collective-permute-done.5.refs_1_
  31.1 1.1 %early_part.3 = (f32[2,768,256]{2,1,0:T(8,128)S(1)}, f32[3,128,256]{2,1,0:T(8,128)S(1)}, f32[3,128,256]{2,1,0:T(8,128)S(1)}, f32[8,128,256]{2,1,0:T(8,128)}) custom-call(bf16[2,384,256]{2,1,0:T(8,128)(2,1)S(1)} %get-tuple-element.45.refs_0_, bf16[2,384,256]{2,1,0:T(8,128)(2,1)S(1)} %collective-permute-done.5.refs_1_, ...), custom_call_target="tpu_custom_call" | custom-call | flops 20000000000 | tf_op jit(solution)/shard_map/early_part/pallas_call | solution.py:37
  32.3 0.0 collective-permute-done.8.last_ref
  32.3 0.6 %first_node.3 = (f32[3,128,256]{2,1,0:T(8,128)S(1)}, bf16[1,384,256]{2,1,0:T(8,128)(2,1)S(1)}, f32[3,128,256]{2,1,0:T(8,128)S(1)}) custom-call(f32[2,768,256]{2,1,0:T(8,128)S(1)} %get-tuple-element.65.part_ref, f32[3,128,256]{2,1,0:T(8,128)S(1)} %get-tuple-element.66.first_ref, f32[3,128,256]{2,1,0:T(8,128)S(1)} %get-tuple-element.67.begun_ref, ...), custom_call_target="tpu_custom_call" | custom-call | tf_op jit(solution)/shard_map/first_node/pallas_call | solution.py:37
  32.8 1.6 %collective-permute-start.14 = (bf16[1,384,256]{2,1,0:T(8,128)(2,1)S(1)}, bf16[1,384,256]{2,1,0:T(8,128)(2,1)S(1)}, u32[]{:S(2)}, u32[]{:S(2)}) collective-permute-start(bf16[1,384,256]{2,1,0:T(8,128)(2,1)S(1)} %get-tuple-element.71.refs_0_), channel_id=1, source_target_pairs={{0,2},{1,3},{2,0},{3,1},{4,6},{5,7},{6,4},{7,5},{8,10},{9,11},{10,... | collective-permute-start | bytes 589832 | tf_op jit(solution)/shard_map/ppermute | solution.py:370
  34.4 0.0 collective-permute-start.13
  34.4 3.5 %collective-permute-start.12 = (bf16[1,128,256]{2,1,0:T(8,128)(2,1)S(1)}, bf16[1,128,256]{2,1,0:T(8,128)(2,1)S(1)}, u32[]{:S(2)}, u32[]{:S(2)}) collective-permute-start(bf16[1,128,256]{2,1,0:T(8,128)(2,1)S(1)} %get-tuple-element.79), channel_id=1, source_target_pairs={{4,0},{8,4},{12,8},{16,12},{20,16},{24,20},{28,24},{0,28},{5,1},{9... | collective-permute-start | bytes 196616 | tf_op jit(solution)/shard_map/ppermute | solution.py:376
  37.9 0.0 collective-permute-done.10.refs_6_
  37.9 0.2 collective-permute-start.11
  38.2 0.0 collective-permute-done.9.refs_5_
  38.2 1.3 %before_second.1 = (f32[8,128,256]{2,1,0:T(8,128)}, f32[2,640,256]{2,1,0:T(8,128)S(1)}, f32[5,128,256]{2,1,0:T(8,128)S(1)}, f32[3,128,256]{2,1,0:T(8,128)S(1)}) custom-call(f32[5,128,256]{2,1,0:T(8,128)S(1)} %get-tuple-element.59.refs_9_.refs_0_.new_ref.refs_2_, ...), custom_call_target="tpu_custom_call", output_to_operand_aliasing={{0}: (10, {})} | custom-call | flops 20000000000 | tf_op jit(solution)/shard_map/before_second/pallas_call | solution.py:37
  39.5 0.1 collective-permute-done.11.last_ref
  39.6 0.3 whole_sums.1.sums_ref.refs_0_
  39.9 0.1 collective-permute-done.12.refs_4_
  40.0 0.0 collective-permute-done.14.refs_2_
  40.0 0.3 collective-permute-start.15
  40.2 0.0 collective-permute-done.13.refs_1_
  40.2 1.2 %second_first.1 = (f32[8,128,256]{2,1,0:T(8,128)}, f32[2,384,256]{2,1,0:T(8,128)S(1)}) custom-call(bf16[2,640,256]{2,1,0:T(8,128)(2,1)S(1)} %whole_sums.1.sums_ref.refs_0_, f32[5,128,256]{2,1,0:T(8,128)S(1)} %get-tuple-element.76.base_ref.refs_1_, f32[5,128,256]{2,1,0:T(8,128)S(1)} %get-tuple-element.59.refs_9_.refs_0_.new_ref.refs_2_, ...), custom_call_target="tpu_custom_call" | custom-call | tf_op jit(solution)/shard_map/second_first/pallas_call | solution.py:37
  41.4 0.0 collective-permute-done.15.refs_6_
  41.4 1.1 %second_last.1 = f32[8,128,256]{2,1,0:T(8,128)} custom-call(bf16[2,640,256]{2,1,0:T(8,128)(2,1)S(1)} %whole_sums.1.sums_ref.refs_0_, f32[5,128,256]{2,1,0:T(8,128)S(1)} %get-tuple-element.76.base_ref.refs_1_, f32[5,128,256]{2,1,0:T(8,128)S(1)} %get-tuple-element.59.refs_9_.refs_0_.new_ref.refs_2_, ...), custom_call_target="tpu_custom_call", output_to_operand_aliasing={{}: (11, {})} | custom-call | tf_op jit(solution)/shard_map/second_last/pallas_call | solution.py:37
  (3 shorter events, 0.0 us)
Async XLA Ops:
  2.0 14.2 %copy-start.2 = (f32[256]{0:T(256)S(1)}, f32[256]{0:T(256)}, u32[]{:S(2)}) copy-start(f32[256]{0:T(256)} %param.10) | copy-start | bytes 3076
  2.0 18.6 %collective-permute-start.1 = (bf16[2,640,256]{2,1,0:T(8,128)(2,1)S(1)}, bf16[2,640,256]{2,1,0:T(8,128)(2,1)S(1)}, u32[]{:S(2)}, u32[]{:S(2)}) collective-permute-start(bf16[2,640,256]{2,1,0:T(8,128)(2,1)S(1)} %get-tuple-element.46.refs_0_), channel_id=1, source_target_pairs={{0,2},{1,3},{2,0},{3,1},{4,6},{5,7},{6,4},{7,5},{8,10},{9,11},{10,... | collective-permute-start | bytes 1966088 | tf_op jit(solution)/shard_map/ppermute | solution.py:370
  6.2 14.4 %copy-start = (bf16[2,1024,256]{2,1,0:T(8,128)(2,1)S(1)}, bf16[2,1024,256]{2,1,0:T(8,128)(2,1)}, u32[]{:S(2)}) copy-start(bf16[2,1024,256]{2,1,0:T(8,128)(2,1)} %refs_10_) | copy-start | bytes 3145732
  6.2 14.4 %copy-start.1 = (f32[256]{0:T(256)S(1)}, f32[256]{0:T(256)}, u32[]{:S(2)}) copy-start(f32[256]{0:T(256)} %param.11) | copy-start | bytes 3076
  6.2 14.4 %copy-start.3 = (f32[8,128,256]{2,1,0:T(8,128)S(1)}, f32[8,128,256]{2,1,0:T(8,128)}, u32[]{:S(2)}) copy-start(f32[8,128,256]{2,1,0:T(8,128)} %refs_6_.3) | copy-start | bytes 3145732
  6.2 14.4 %collective-permute-start = (bf16[2,640,256]{2,1,0:T(8,128)(2,1)S(1)}, bf16[2,640,256]{2,1,0:T(8,128)(2,1)S(1)}, u32[]{:S(2)}, u32[]{:S(2)}) collective-permute-start(bf16[2,640,256]{2,1,0:T(8,128)(2,1)S(1)} %get-tuple-element.46.refs_0_), channel_id=1, source_target_pairs={{0,1},{1,0},{2,3},{3,2},{4,5},{5,4},{6,7},{7,6},{8,9},{9,8},{10,11... | collective-permute-start | bytes 1966088 | tf_op jit(solution)/shard_map/ppermute | solution.py:367
  6.3 8.8 %collective-permute-start.2 = (bf16[2,128,256]{2,1,0:T(8,128)(2,1)S(1)}, bf16[2,128,256]{2,1,0:T(8,128)(2,1)S(1)}, u32[]{:S(2)}, u32[]{:S(2)}) collective-permute-start(bf16[2,128,256]{2,1,0:T(8,128)(2,1)S(1)} %get-tuple-element.51), channel_id=1, source_target_pairs={{0,4},{4,8},{8,12},{12,16},{16,20},{20,24},{24,28},{28,0},{1,5},{5... | collective-permute-start | bytes 393224 | tf_op jit(solution)/shard_map/ppermute | solution.py:373
  7.8 8.4 %collective-permute-start.3 = (bf16[2,128,256]{2,1,0:T(8,128)(2,1)S(1)}, bf16[2,128,256]{2,1,0:T(8,128)(2,1)S(1)}, u32[]{:S(2)}, u32[]{:S(2)}) collective-permute-start(bf16[2,128,256]{2,1,0:T(8,128)(2,1)S(1)} %get-tuple-element.52), channel_id=1, source_target_pairs={{4,0},{8,4},{12,8},{16,12},{20,16},{24,20},{28,24},{0,28},{5,1},{9... | collective-permute-start | bytes 393224 | tf_op jit(solution)/shard_map/ppermute | solution.py:376
  11.1 17.1 %collective-permute-start.6 = (bf16[2,384,256]{2,1,0:T(8,128)(2,1)S(1)}, bf16[2,384,256]{2,1,0:T(8,128)(2,1)S(1)}, u32[]{:S(2)}, u32[]{:S(2)}) collective-permute-start(bf16[2,384,256]{2,1,0:T(8,128)(2,1)S(1)} %get-tuple-element.45.refs_0_), channel_id=1, source_target_pairs={{0,2},{1,3},{2,0},{3,1},{4,6},{5,7},{6,4},{7,5},{8,10},{9,11},{10,... | collective-permute-start | bytes 1179656 | tf_op jit(solution)/shard_map/ppermute | solution.py:370
  15.1 16.1 %collective-permute-start.5 = (bf16[2,384,256]{2,1,0:T(8,128)(2,1)S(1)}, bf16[2,384,256]{2,1,0:T(8,128)(2,1)S(1)}, u32[]{:S(2)}, u32[]{:S(2)}) collective-permute-start(bf16[2,384,256]{2,1,0:T(8,128)(2,1)S(1)} %get-tuple-element.45.refs_0_), channel_id=1, source_target_pairs={{0,1},{1,0},{2,3},{3,2},{4,5},{5,4},{6,7},{7,6},{8,9},{9,8},{10,11... | collective-permute-start | bytes 1179656 | tf_op jit(solution)/shard_map/ppermute | solution.py:367
  20.6 2.1 %collective-permute-start.4 = (bf16[2,640,256]{2,1,0:T(8,128)(2,1)S(1)}, bf16[2,640,256]{2,1,0:T(8,128)(2,1)S(1)}, u32[]{:S(2)}, u32[]{:S(2)}) collective-permute-start(bf16[2,640,256]{2,1,0:T(8,128)(2,1)S(1)} %collective-permute-done.1.refs_2_), channel_id=1, source_target_pairs={{0,1},{1,0},{2,3},{3,2},{4,5},{5,4},{6,7},{7,6},{8,9},{9,8},{10,11... | collective-permute-start | bytes 1966088 | tf_op jit(solution)/shard_map/ppermute | solution.py:367
  23.5 7.6 %collective-permute-start.7 = (bf16[1,128,256]{2,1,0:T(8,128)(2,1)S(1)}, bf16[1,128,256]{2,1,0:T(8,128)(2,1)S(1)}, u32[]{:S(2)}, u32[]{:S(2)}) collective-permute-start(bf16[1,128,256]{2,1,0:T(8,128)(2,1)S(1)} %get-tuple-element.63), channel_id=1, source_target_pairs={{0,4},{4,8},{8,12},{12,16},{16,20},{20,24},{24,28},{28,0},{1,5},{5... | collective-permute-start | bytes 196616 | tf_op jit(solution)/shard_map/ppermute | solution.py:373
  25.6 12.4 %collective-permute-start.10 = (bf16[1,640,256]{2,1,0:T(8,128)(2,1)S(1)}, bf16[1,640,256]{2,1,0:T(8,128)(2,1)S(1)}, u32[]{:S(2)}, u32[]{:S(2)}) collective-permute-start(bf16[1,640,256]{2,1,0:T(8,128)(2,1)S(1)} %get-tuple-element.60.refs_4_), channel_id=1, source_target_pairs={{0,2},{1,3},{2,0},{3,1},{4,6},{5,7},{6,4},{7,5},{8,10},{9,11},{10,... | collective-permute-start | bytes 983048 | tf_op jit(solution)/shard_map/ppermute | solution.py:370
  27.1 11.1 %collective-permute-start.9 = (bf16[1,640,256]{2,1,0:T(8,128)(2,1)S(1)}, bf16[1,640,256]{2,1,0:T(8,128)(2,1)S(1)}, u32[]{:S(2)}, u32[]{:S(2)}) collective-permute-start(bf16[1,640,256]{2,1,0:T(8,128)(2,1)S(1)} %get-tuple-element.60.refs_4_), channel_id=1, source_target_pairs={{0,1},{1,0},{2,3},{3,2},{4,5},{5,4},{6,7},{7,6},{8,9},{9,8},{10,11... | collective-permute-start | bytes 983048 | tf_op jit(solution)/shard_map/ppermute | solution.py:367
  28.2 4.1 %collective-permute-start.8 = (bf16[2,384,256]{2,1,0:T(8,128)(2,1)S(1)}, bf16[2,384,256]{2,1,0:T(8,128)(2,1)S(1)}, u32[]{:S(2)}, u32[]{:S(2)}) collective-permute-start(bf16[2,384,256]{2,1,0:T(8,128)(2,1)S(1)} %collective-permute-done.6.refs_2_), channel_id=1, source_target_pairs={{0,1},{1,0},{2,3},{3,2},{4,5},{5,4},{6,7},{7,6},{8,9},{9,8},{10,11... | collective-permute-start | bytes 1179656 | tf_op jit(solution)/shard_map/ppermute | solution.py:367
  32.8 7.1 %collective-permute-start.14 = (bf16[1,384,256]{2,1,0:T(8,128)(2,1)S(1)}, bf16[1,384,256]{2,1,0:T(8,128)(2,1)S(1)}, u32[]{:S(2)}, u32[]{:S(2)}) collective-permute-start(bf16[1,384,256]{2,1,0:T(8,128)(2,1)S(1)} %get-tuple-element.71.refs_0_), channel_id=1, source_target_pairs={{0,2},{1,3},{2,0},{3,1},{4,6},{5,7},{6,4},{7,5},{8,10},{9,11},{10,... | collective-permute-start | bytes 589832 | tf_op jit(solution)/shard_map/ppermute | solution.py:370
  34.4 5.8 %collective-permute-start.13 = (bf16[1,384,256]{2,1,0:T(8,128)(2,1)S(1)}, bf16[1,384,256]{2,1,0:T(8,128)(2,1)S(1)}, u32[]{:S(2)}, u32[]{:S(2)}) collective-permute-start(bf16[1,384,256]{2,1,0:T(8,128)(2,1)S(1)} %get-tuple-element.71.refs_0_), channel_id=1, source_target_pairs={{0,1},{1,0},{2,3},{3,2},{4,5},{5,4},{6,7},{7,6},{8,9},{9,8},{10,11... | collective-permute-start | bytes 589832 | tf_op jit(solution)/shard_map/ppermute | solution.py:367
  34.4 5.5 %collective-permute-start.12 = (bf16[1,128,256]{2,1,0:T(8,128)(2,1)S(1)}, bf16[1,128,256]{2,1,0:T(8,128)(2,1)S(1)}, u32[]{:S(2)}, u32[]{:S(2)}) collective-permute-start(bf16[1,128,256]{2,1,0:T(8,128)(2,1)S(1)} %get-tuple-element.79), channel_id=1, source_target_pairs={{4,0},{8,4},{12,8},{16,12},{20,16},{24,20},{28,24},{0,28},{5,1},{9... | collective-permute-start | bytes 196616 | tf_op jit(solution)/shard_map/ppermute | solution.py:376
  37.9 1.6 %collective-permute-start.11 = (bf16[1,640,256]{2,1,0:T(8,128)(2,1)S(1)}, bf16[1,640,256]{2,1,0:T(8,128)(2,1)S(1)}, u32[]{:S(2)}, u32[]{:S(2)}) collective-permute-start(bf16[1,640,256]{2,1,0:T(8,128)(2,1)S(1)} %collective-permute-done.10.refs_6_), channel_id=1, source_target_pairs={{0,1},{1,0},{2,3},{3,2},{4,5},{5,4},{6,7},{7,6},{8,9},{9,8},{10,11... | collective-permute-start | bytes 983048 | tf_op jit(solution)/shard_map/ppermute | solution.py:367
  40.0 1.5 %collective-permute-start.15 = (bf16[1,384,256]{2,1,0:T(8,128)(2,1)S(1)}, bf16[1,384,256]{2,1,0:T(8,128)(2,1)S(1)}, u32[]{:S(2)}, u32[]{:S(2)}) collective-permute-start(bf16[1,384,256]{2,1,0:T(8,128)(2,1)S(1)} %collective-permute-done.14.refs_2_), channel_id=1, source_target_pairs={{0,1},{1,0},{2,3},{3,2},{4,5},{5,4},{6,7},{7,6},{8,9},{9,8},{10,11... | collective-permute-start | bytes 589832 | tf_op jit(solution)/shard_map/ppermute | solution.py:367
